TPU v7x, 32 devices: a whole 2x2x4 slice. The times are simulated.
32 devices in a mesh: parts: 2 (over y), node: 4 (over x, core), local: 4 (over z).
Axes of the slice: x: 2, y: 2, z: 4, core: 2. Of those that a mesh axis runs over, the one named last changes fastest.
Arguments:
- tokens: bfloat16 [256, 7168], P(('parts', 'node', 'local')), parts along dimension 0, may hold values from -6 to 6
- expert_ids: int32 [256, 4], P(('parts', 'node', 'local')), parts along dimension 0, may hold values from 0 to 7, all different within a row; in each aligned block of 8 rows (0 to 7, 8 to 15, ...) at most 8 rows name the same one
- route_weights: float32 [256, 4], P(('parts', 'node', 'local')), parts along dimension 0, may hold values from 0.05 to 1
- expert_slot: int32 [8], replicated, may hold values from 0 to 7, each once
- w_gate: bfloat16 [8, 7168, 2048], P('node', None, 'local'), may hold values from -0.0625 to 0.0625
- w_up: bfloat16 [8, 7168, 2048], P('node', None, 'local'), may hold values from -0.0625 to 0.0625
- w_down: bfloat16 [8, 2048, 7168], P('node', 'local'), may hold values from -0.125 to 0.125
Outputs:
- combined: bfloat16 [256, 7168], P(('parts', 'node', 'local')), parts along dimension 0
There are 2 independent parts, one for each index of `parts`. A program takes and returns all parts, laid end to end along the dimension named above; an argument that names none is the same for every part. Nothing has to cross between parts.
Inputs may be any that keep to these rules, and one draw needn't show every extreme that they name: `expert_ids`: each row names 4 different experts. Among the 8 rows of one device at most 8 name any one expert, a bound that some block reaches. Every expert is named somewhere. `expert_slot`: each slot holds exactly one expert.
All inputs are finite; a program needn't handle non-finite values.
Results may differ from a plain program's by a relative error of at most 0.013.
Values may be sent and summed in bfloat16 or wider, within the bound.
No kernel may reach another device: no remote copies, remote signals or barrier semaphores. Data moves between devices by JAX's collectives and lax.ppermute only.
A program may use at most 128 MiB of HBM per device.

v0:
```python
import jax
import jax.numpy as jnp
from jax import lax
from jax.sharding import PartitionSpec as P


def slot_hits(id_rows, expert_slot, members, groups, capacity):
    slot_total = members * groups
    lookup = id_rows[..., None] == jnp.arange(slot_total, dtype=jnp.int32)
    slot_ids = jnp.sum(jnp.where(lookup, expert_slot, 0), axis=-1)
    onehot = (slot_ids[..., None] == jnp.arange(slot_total, dtype=jnp.int32)).astype(jnp.int32)
    per_token = jnp.sum(onehot, axis=-2)
    earlier = jnp.cumsum(per_token, axis=-2) - per_token
    position = jnp.sum(onehot * earlier[..., None, :], axis=-1)
    member_hit = ((slot_ids % members)[..., None] == jnp.arange(members)).astype(jnp.float32)
    group_hit = ((slot_ids // members)[..., None] == jnp.arange(groups)).astype(jnp.float32)
    place_hit = (position[..., None] == jnp.arange(capacity)).astype(jnp.float32)
    return (member_hit, group_hit, place_hit)


def per_device(tokens, expert_ids, route_weights, expert_slot, w_gate, w_up, w_down):
    groups = lax.axis_size("node")
    members = w_gate.shape[0]
    token_count = tokens.shape[0]
    model_width = tokens.shape[1]
    chosen = expert_ids.shape[1]
    capacity = 2 * token_count * chosen // (members * groups)
    member_hit, group_hit, place_hit = slot_hits(
        expert_ids[None], expert_slot, members, groups, capacity
    )
    dispatch = jnp.einsum("stke,stkg,stkc->segct", member_hit, group_hit, place_hit).astype(
        jnp.bfloat16
    )
    outgoing = jnp.einsum(
        "segct,std->segcd", dispatch, tokens[None], preferred_element_type=jnp.float32
    ).astype(jnp.bfloat16)[0]
    arrived = lax.all_to_all(outgoing, "node", split_axis=1, concat_axis=1, tiled=True)
    gathered = lax.all_gather(arrived.reshape(-1, model_width), "local", axis=0, tiled=True)
    rows_here = members * groups * capacity
    row_block = gathered
    row_block = row_block.reshape(
        lax.axis_size("local") * rows_here // rows_here, members, groups * capacity, model_width
    )
    gate_act = jnp.einsum("mecd,edh->mech", row_block, w_gate, preferred_element_type=jnp.float32)
    up_act = jnp.einsum("mecd,edh->mech", row_block, w_up, preferred_element_type=jnp.float32)
    hidden = (jax.nn.silu(gate_act) * up_act).astype(jnp.bfloat16)
    result = jnp.einsum("mech,ehd->mecd", hidden, w_down, preferred_element_type=jnp.float32)
    summed = lax.psum_scatter(
        result.reshape(lax.axis_size("local") * rows_here, model_width).astype(jnp.bfloat16),
        "local",
        scatter_dimension=0,
        tiled=True,
    )
    results = summed.reshape(members, groups, capacity, model_width)
    returned = lax.all_to_all(results, "node", split_axis=1, concat_axis=1, tiled=True)
    weighted = jnp.einsum(
        "tke,tkg,tkc,tk->tegc", member_hit[0], group_hit[0], place_hit[0], route_weights
    )
    combined = jnp.dot(
        weighted.reshape(token_count, -1),
        returned.reshape(-1, model_width).astype(jnp.float32),
        precision=lax.Precision.HIGHEST,
    )
    return combined.astype(jnp.bfloat16)


def solution(mesh):
    in_specs = (
        P(("parts", "node", "local"), None),
        P(("parts", "node", "local"), None),
        P(("parts", "node", "local"), None),
        P(),
        P("node", None, "local"),
        P("node", None, "local"),
        P("node", "local", None),
    )
    out_specs = P(("parts", "node", "local"), None)
    return jax.shard_map(
        per_device, mesh=mesh, in_specs=in_specs, out_specs=out_specs, check_vma=False
    )
```

profile of v0, /device:TPU:0, one launch (start us, length us, event | category | flops | bytes accessed | tf_op | source)
XLA Modules:
  0.0 215.0 jit_solution(8652136130535063563)
XLA Ops:
  6.5 0.0 copy-start
  6.5 0.0 all-gather.2.cloned.1.call-start
  6.5 0.9 select_reduce_fusion.1
  7.5 0.1 convert_reduce_fusion
  7.6 0.2 select_reduce_fusion
  7.8 0.1 copy.34
  7.9 0.1 copy.33
  8.0 0.1 copy.31
  8.1 0.2 fusion.35
  8.3 0.0 copy-done
  8.3 0.4 convolution_convert_fusion
  8.7 0.1 copy.36
  8.8 17.1 %all_to_all.10 = bf16[2,4,8,7168]{3,2,0,1:T(8,128)(2,1)S(1)} all-to-all(bf16[2,4,8,7168]{3,2,0,1:T(8,128)(2,1)S(1)} %copy.36), channel_id=1, replica_groups=mesh['parts'=2,'node'=4,'local'=4] {'node'}, dimensions={1} | all-to-all | bytes 1835008 | tf_op jit(solution)/shard_map/all_to_all | solution.py:37
  25.9 1.0 copy.37
  26.9 0.0 all-gather.2.cloned.1.call-update
  26.9 0.0 reduce-scatter.2.cloned.1.call-start
  26.9 72.5 %all-gather.2.cloned.1.call-done = bf16[256,7168]{1,0:T(8,128)(2,1)} async-done(((bf16[64,7168]{1,0:T(8,128)(2,1)}), bf16[256,7168]{1,0:T(8,128)(2,1)}) %all-gather.2.cloned.1.call-update) | async-done | bytes 3670032 | tf_op jit(solution)/shard_map/all_gather | solution.py:38
  99.5 0.0 copy-start.2
  99.5 0.0 slice-start
  99.5 0.0 slice-start.1
  99.5 8.5 %fusion.15 = f32[4,2,32,512]{3,2,0,1:T(8,128)S(1)} fusion(bf16[2,7168,512]{2,1,0:T(8,128)(2,1)} %param.11, bf16[4,2,32,7168]{3,2,1,0:T(8,128)(2,1)} %bitcast.70), kind=kOutput, calls=%fused_computation.13 | convolution fusion | flops 1879048192 | bytes 18874368 | tf_op jit(solution)/shard_map/mecd,edh->mech/dot_general | solution.py:44
  108.0 0.0 copy-done.2
  108.0 0.0 slice-start.2
  108.0 0.0 slice-start.3
  108.0 7.6 %fusion.30 = bf16[4,2,32,512]{3,2,0,1:T(8,128)(2,1)S(1)} fusion(bf16[2,7168,512]{2,1,0:T(8,128)(2,1)} %param.12, bf16[4,2,32,7168]{3,2,1,0:T(8,128)(2,1)S(1)} %bitcast.71, f32[4,2,32,512]{3,2,0,1:T(8,128)S(1)} %fusion.15), kind=kOutput, calls=%fused_computation.16 | convolution fusion | flops 1879834624 | bytes 19136512 | tf_op jit(solution)/shard_map/mecd,edh->mech/dot_general | solution.py:45
  115.6 0.0 slice-done
  115.6 0.0 slice-done.1
  115.6 0.0 slice-done.2
  115.6 0.0 slice-done.3
  115.6 2.1 fusion.9
  117.7 0.0 copy-start.1
  117.7 2.2 %copy.40 = bf16[4,2,32,7168]{3,2,1,0:T(8,128)(2,1)} copy(bf16[4,2,32,7168]{3,2,0,1:T(8,128)(2,1)S(1)} %fusion.9) | data formatting | bytes 7340032 | tf_op jit(solution)/shard_map/convert_element_type | solution.py:49
  119.9 0.0 reduce-scatter.2.cloned.1.call-update
  119.9 67.2 %reduce-scatter.2.cloned.1.call-done = bf16[64,7168]{1,0:T(8,128)(2,1)} async-done(((bf16[256,7168]{1,0:T(8,128)(2,1)}), bf16[64,7168]{1,0:T(8,128)(2,1)}) %reduce-scatter.2.cloned.1.call-update) | async-done | bytes 917520 | tf_op jit(solution)/shard_map/reduce_scatter | solution.py:48
  187.1 2.2 %copy.41 = bf16[2,4,8,7168]{3,2,0,1:T(8,128)(2,1)} copy(bf16[2,4,8,7168]{3,2,1,0:T(8,128)(2,1)} %bitcast.69) | data formatting | bytes 1835008 | tf_op jit(solution)/shard_map/reshape | solution.py:54
  189.2 3.5 %all-to-all-start.1 = ((bf16[2,4,8,7168]{3,2,0,1:T(8,128)(2,1)}), bf16[2,4,8,7168]{3,2,0,1:T(8,128)(2,1)S(1)}, u32[]{:S(2)}, u32[]{:S(2)}) async-start(bf16[2,4,8,7168]{3,2,0,1:T(8,128)(2,1)} %copy.41), calls=%async_computation.2 | async-start | bytes 1835008 | tf_op jit(solution)/shard_map/all_to_all | solution.py:55
  192.7 0.0 copy-done.1
  192.8 0.1 copy.32
  192.8 0.2 fusion.40
  193.0 12.7 %all-to-all-done.1 = bf16[2,4,8,7168]{3,2,0,1:T(8,128)(2,1)S(1)} async-done(((bf16[2,4,8,7168]{3,2,0,1:T(8,128)(2,1)}), bf16[2,4,8,7168]{3,2,0,1:T(8,128)(2,1)S(1)}, u32[]{:S(2)}, u32[]{:S(2)}) %all-to-all-start.1) | async-done | bytes 917536 | tf_op jit(solution)/shard_map/all_to_all | solution.py:55
  205.8 2.4 %fusion.12 = bf16[8,7168]{1,0:T(8,128)(2,1)} fusion(bf16[2,4,8,7168]{3,2,0,1:T(8,128)(2,1)S(1)} %all-to-all-done.1, f32[8,2,4,8]{3,2,1,0:T(4,128)S(1)} %fusion.40), kind=kOutput, calls=%fused_computation.10 | convolution fusion | flops 44097536 | bytes 1034240 | tf_op jit(solution)/shard_map/dot_general | solution.py:59
  (7 shorter events, 0.1 us)
Async XLA Ops:
  6.5 1.8 copy-start
  6.5 92.9 %all-gather.2.cloned.1.call-start = ((), (), s32[]{:S(2)}) async-start(), calls=%async_computation.3 | async-start | bytes 4587520 | tf_op jit(solution)/shard_map/all_gather | solution.py:38
  26.9 160.2 %reduce-scatter.2.cloned.1.call-start = ((), (), s32[]{:S(2)}) async-start(), calls=%async_computation.4 | async-start | bytes 4587520 | tf_op jit(solution)/shard_map/reduce_scatter | solution.py:48
  99.5 8.5 %copy-start.2 = (bf16[256,7168]{1,0:T(8,128)(2,1)S(1)}, bf16[256,7168]{1,0:T(8,128)(2,1)}, u32[]{:S(2)}) copy-start(bf16[256,7168]{1,0:T(8,128)(2,1)} %all-gather.2.cloned.1.call-done) | copy-start | bytes 11010052
  99.5 16.1 %slice-start = ((s8[14680064]{0:T(1024)(128)(4,1)}), s8[4194304]{0:T(1024)(128)(4,1)S(1)}, s32[]{:S(2)}) async-start(s8[14680064]{0:T(1024)(128)(4,1)} %bitcast.66), calls=%async_computation.5 | async-start | bytes 8388608
  99.5 16.1 %slice-start.1 = ((s8[14680064]{0:T(1024)(128)(4,1)}), s8[4194304]{0:T(1024)(128)(4,1)S(1)}, s32[]{:S(2)}) async-start(s8[14680064]{0:T(1024)(128)(4,1)} %bitcast.66), calls=%async_computation.6 | async-start | bytes 8388608
  108.0 7.6 %slice-start.2 = ((s8[14680064]{0:T(1024)(128)(4,1)}), s8[4194304]{0:T(1024)(128)(4,1)S(1)}, s32[]{:S(2)}) async-start(s8[14680064]{0:T(1024)(128)(4,1)} %bitcast.66), calls=%async_computation.7 | async-start | bytes 8388608
  108.0 7.6 %slice-start.3 = ((s8[14680064]{0:T(1024)(128)(4,1)}), s8[2097152]{0:T(1024)(128)(4,1)S(1)}, s32[]{:S(2)}) async-start(s8[14680064]{0:T(1024)(128)(4,1)} %bitcast.66), calls=%async_computation.8 | async-start | bytes 4194304
  117.7 75.0 %copy-start.1 = (f32[8,4]{0,1:T(4,128)S(1)}, f32[8,4]{0,1:T(4,128)}, u32[]{:S(2)}) copy-start(f32[8,4]{0,1:T(4,128)} %param.9) | copy-start | bytes 388
  189.2 16.5 %all-to-all-start.1 = ((bf16[2,4,8,7168]{3,2,0,1:T(8,128)(2,1)}), bf16[2,4,8,7168]{3,2,0,1:T(8,128)(2,1)S(1)}, u32[]{:S(2)}, u32[]{:S(2)}) async-start(bf16[2,4,8,7168]{3,2,0,1:T(8,128)(2,1)} %copy.41), calls=%async_computation.2 | async-start | bytes 1835008 | tf_op jit(solution)/shard_map/all_to_all | solution.py:55
Sparse Core Ops, SparseCore 0:
  27.0 72.4 all-gather.1
  120.0 66.9 reduce-scatter.1
where the time goes:
time: 215 us
  waiting for transfers between devices  152 us (71%)
  matrix products  21.4 us (10%)
  blocking collectives  17.1 us (8%)
  between operations  13.6 us (6%)
  local copies, waits for them, and re-layouts  5.73 us (3%)
  starting transfers between devices  3.55 us (2%)
    all_gather x1, waiting for transfers between devices, per_device(): lax.all_gather(arrived.reshape(-1, model_width), 'local', axis=0, tiled=T...  72.5 us
    reduce_scatter x1, waiting for transfers between devices, per_device(): lax.psum_scatter(result.reshape(lax.axis_size('local') * rows_here, model...  67.2 us
    all_to_all x1, blocking collectives, per_device(): lax.all_to_all(outgoing, 'node', split_axis=1, concat_axis=1, tiled=True)  17.1 us
    all_to_all x1, waiting for transfers between devices, per_device(): lax.all_to_all(results, 'node', split_axis=1, concat_axis=1, tiled=True)  12.7 us
    dot_general x1, matrix products, per_device(): jnp.einsum('mecd,edh->mech', row_block, w_gate, preferred_element_type=jn...  8.49 us
    dot_general x1, matrix products, per_device(): jnp.einsum('mecd,edh->mech', row_block, w_up, preferred_element_type=jnp....  7.55 us
  transfers between devices with their start and end apart: 3, of which 3 were waited for; matrix products, arithmetic and copies ran while one was open for 0% of the time, Pallas kernels for 0%

commit v1 on v0

v1 whole, which is shorter than its diff:
```python
import jax
import jax.numpy as jnp
from jax import lax
from jax.sharding import PartitionSpec as P

LANES = 128


def slot_weights(expert_ids, route_weights, expert_slot):
    experts = expert_slot.shape[0]
    slots = jnp.arange(experts, dtype=jnp.int32)
    lookup = expert_ids[..., None] == slots
    slot_ids = jnp.sum(jnp.where(lookup, expert_slot, 0), axis=-1)
    hit = slot_ids[..., None] == slots
    return jnp.sum(jnp.where(hit, route_weights[..., None], 0.0), axis=1)


def three_pieces(values):
    first = lax.reduce_precision(values, 8, 7)
    rest = values - first
    second = lax.reduce_precision(rest, 8, 7)
    third = rest - second
    return [piece.astype(jnp.bfloat16) for piece in (first, second, third)]


def per_device(tokens, expert_ids, route_weights, expert_slot, w_gate, w_up, w_down):
    members, width, hid = w_gate.shape
    slots = expert_slot.shape[0]
    weights = slot_weights(expert_ids, route_weights, expert_slot)
    pieces = three_pieces(weights)
    packed = jnp.concatenate([tokens] + pieces, axis=1)
    packed = jnp.pad(packed, ((0, 0), (0, -packed.shape[1] % LANES)))
    gathered = lax.all_gather(packed, ("node", "local"), axis=0, tiled=True)
    rows = gathered[:, :width]
    tail = gathered[:, width : width + 3 * slots].astype(jnp.float32)
    mine = tail[:, :slots] + tail[:, slots : 2 * slots] + tail[:, 2 * slots :]
    mine = lax.dynamic_slice_in_dim(mine, lax.axis_index("node") * members, members, axis=1)
    gate = jnp.einsum("td,edh->eth", rows, w_gate, preferred_element_type=jnp.float32)
    up = jnp.einsum("td,edh->eth", rows, w_up, preferred_element_type=jnp.float32)
    hidden = (jax.nn.silu(gate) * up * mine.T[..., None]).astype(jnp.bfloat16)
    result = jnp.einsum("eth,ehd->td", hidden, w_down, preferred_element_type=jnp.float32)
    return lax.psum_scatter(
        result.astype(jnp.bfloat16), ("node", "local"), scatter_dimension=0, tiled=True
    )


def solution(mesh):
    rows = P(("parts", "node", "local"), None)
    in_specs = (
        rows,
        rows,
        rows,
        P(),
        P("node", None, "local"),
        P("node", None, "local"),
        P("node", "local", None),
    )
    return jax.shard_map(
        per_device, mesh=mesh, in_specs=in_specs, out_specs=rows, check_vma=False
    )
```

time: 215 us -> 140 us (0.65)
  waiting for transfers between devices: 152 us -> 103 us
  blocking collectives: 17.1 us -> 0 us
  local copies, waits for them, and re-layouts: 5.73 us -> 1.82 us
  starting transfers between devices: 3.55 us -> 0.04 us
  matrix products: 21.4 us -> 18.7 us
    all_gather x1, waiting for transfers between devices: 72.5 us -> 43.6 us  [per_device(): gathered = lax.all_gather(packed, ('node', 'local'), axis=0, tiled=True)]
    all_to_all x1 -> x0, blocking collectives: 17.1 us -> none  [per_device(): lax.all_to_all(outgoing, 'node', split_axis=1, concat_axis=1, tiled=True)]
    all_to_all x1 -> x0, waiting for transfers between devices: 12.7 us -> none  [per_device(): lax.all_to_all(results, 'node', split_axis=1, concat_axis=1, tiled=True)]
    reduce_scatter x1, waiting for transfers between devices: 67.2 us -> 59.3 us  [per_device(): lax.psum_scatter(result.astype(jnp.bfloat16), ('node', 'local'), scatter_...]
    all_to_all x1 -> x0, starting transfers between devices: 3.5 us -> none  [per_device(): lax.all_to_all(results, 'node', split_axis=1, concat_axis=1, tiled=True)]
    dot_general x7 -> x3, matrix products: 21.4 us -> 18.7 us  [the longest x1 7.95 us: per_device(): jnp.einsum('td,edh->eth', rows, w_gate, preferred_element_type=jnp.float32)]
    convert_element_type x2 -> x0, local copies, waits for them, and re-layouts: 2.22 us -> none  [the longest x1 2.16 us: per_device(): result.reshape(lax.axis_size('local') * rows_here, model_width)]
    reshape x1 -> x0, local copies, waits for them, and re-layouts: 2.18 us -> none  [per_device(): results = summed.reshape(members, groups, capacity, model_width)]
  transfers between devices with their start and end apart: 3 -> 2, of which waited for: 3 -> 2; matrix products, arithmetic and copies ran while one was open for 0% -> 0% of each run, Pallas kernels for 0% -> 0%
where the time goes in v1:
time: 140 us
  waiting for transfers between devices  103 us (74%)
  matrix products  18.7 us (13%)
  between operations  13.5 us (10%)
  other arithmetic  2.57 us (2%)
  local copies, waits for them, and re-layouts  1.82 us (1%)
    reduce_scatter x1, waiting for transfers between devices, per_device(): lax.psum_scatter(result.astype(jnp.bfloat16), ('node', 'local'), scatter_...  59.3 us
    all_gather x1, waiting for transfers between devices, per_device(): gathered = lax.all_gather(packed, ('node', 'local'), axis=0, tiled=True)  43.6 us
    dot_general x1, matrix products, per_device(): jnp.einsum('td,edh->eth', rows, w_gate, preferred_element_type=jnp.float32)  7.95 us
    dot_general x1, matrix products, per_device(): jnp.einsum('td,edh->eth', rows, w_up, preferred_element_type=jnp.float32)  7.46 us
    dot_general x1, matrix products, per_device(): jnp.einsum('eth,ehd->td', hidden, w_down, preferred_element_type=jnp.floa...  3.32 us
  transfers between devices with their start and end apart: 2, of which 2 were waited for; matrix products, arithmetic and copies ran while one was open for 0% of the time, Pallas kernels for 0%

profile of v1, /device:TPU:0, one launch (start us, length us, event | category | flops | bytes accessed | tf_op | source)
XLA Modules:
  0.0 139.6 jit_solution(13439523027285225321)
XLA Ops:
  6.5 0.0 all-gather.2.cloned.1.call-start
  6.5 0.9 select_reduce_fusion.1
  7.4 0.8 select_reduce_fusion
  8.2 1.0 concatenate.3
  9.2 0.7 pad.4
  9.9 0.0 all-gather.2.cloned.1.call-update
  9.9 0.0 reduce-scatter.2.cloned.1.call-start
  10.0 43.6 %all-gather.2.cloned.1.call-done = bf16[128,7296]{1,0:T(8,128)(2,1)} async-done(((bf16[8,7296]{1,0:T(8,128)(2,1)}), bf16[128,7296]{1,0:T(8,128)(2,1)}) %all-gather.2.cloned.1.call-update) | async-done | bytes 1867792 | tf_op jit(solution)/shard_map/all_gather | solution.py:33
  53.5 0.8 slice_convert_fusion
  54.3 0.1 fusion.10
  54.4 0.1 fusion.8
  54.5 0.1 copy.11
  54.6 0.0 copy-start
  54.6 0.0 slice-start
  54.6 0.0 slice-start.1
  54.6 7.9 %fusion.3 = f32[2,128,512]{2,1,0:T(8,128)S(1)} fusion(bf16[2,7168,512]{2,1,0:T(8,128)(2,1)} %param.11, bf16[128,7296]{1,0:T(8,128)(2,1)} %all-gather.2.cloned.1.call-done), kind=kOutput, calls=%fused_computation.5 | convolution fusion | flops 1879048192 | bytes 17039360 | tf_op jit(solution)/shard_map/td,edh->eth/dot_general | solution.py:38
  62.6 0.0 copy-done
  62.6 0.0 slice-start.2
  62.6 0.0 slice-start.3
  62.6 7.5 %fusion.7 = bf16[2,128,512]{2,1,0:T(8,128)(2,1)S(1)} fusion(bf16[2,7168,512]{2,1,0:T(8,128)(2,1)} %param.12, bf16[128,7296]{1,0:T(8,128)(2,1)S(1)} %copy-done, f32[2,128,512]{2,1,0:T(8,128)S(1)} %fusion.3, f32[2,128]{1,0:T(2,128)S(1)} %copy.11), kind=kOutput, calls=%fused_computation.9 | convolution fusion | flops 1879965696 | bytes 17302528 | tf_op jit(solution)/shard_map/td,edh->eth/dot_general | solution.py:39
  70.1 0.0 slice-done
  70.1 0.0 slice-done.1
  70.1 0.0 slice-done.2
  70.1 0.0 slice-done.3
  70.1 3.3 %fusion = bf16[128,7168]{1,0:T(8,128)(2,1)} fusion(bf16[2,128,512]{2,1,0:T(8,128)(2,1)S(1)} %fusion.7, bf16[2,512,7168]{2,1,0:T(8,128)(2,1)S(1)} %bitcast.35), kind=kOutput, calls=%fused_computation.1 | convolution fusion | flops 1879965696 | bytes 16777216 | tf_op jit(solution)/shard_map/eth,ehd->td/dot_general | solution.py:41
  73.4 0.0 reduce-scatter.2.cloned.1.call-update
  73.5 59.3 %reduce-scatter.2.cloned.1.call-done = bf16[8,7168]{1,0:T(8,128)(2,1)} async-done(((bf16[128,7168]{1,0:T(8,128)(2,1)}), bf16[8,7168]{1,0:T(8,128)(2,1)}) %reduce-scatter.2.cloned.1.call-update) | async-done | bytes 114704 | tf_op jit(solution)/shard_map/reduce_scatter | solution.py:42
  (2 shorter events, 0.0 us)
Async XLA Ops:
  6.5 47.0 %all-gather.2.cloned.1.call-start = ((), (), s32[]{:S(2)}) async-start(), calls=%async_computation.1 | async-start | bytes 1984512 | tf_op jit(solution)/shard_map/all_gather | solution.py:33
  9.9 122.9 %reduce-scatter.2.cloned.1.call-start = ((), (), s32[]{:S(2)}) async-start(), calls=%async_computation.2 | async-start | bytes 1949696 | tf_op jit(solution)/shard_map/reduce_scatter | solution.py:42
  54.6 8.0 %copy-start = (bf16[128,7296]{1,0:T(8,128)(2,1)S(1)}, bf16[128,7296]{1,0:T(8,128)(2,1)}, u32[]{:S(2)}) copy-start(bf16[128,7296]{1,0:T(8,128)(2,1)} %all-gather.2.cloned.1.call-done) | copy-start | bytes 5603332
  54.6 15.5 %slice-start = ((s8[14680064]{0:T(1024)(128)(4,1)}), s8[4194304]{0:T(1024)(128)(4,1)S(1)}, s32[]{:S(2)}) async-start(s8[14680064]{0:T(1024)(128)(4,1)} %bitcast.34), calls=%async_computation.3 | async-start | bytes 8388608
  54.6 15.5 %slice-start.1 = ((s8[14680064]{0:T(1024)(128)(4,1)}), s8[4194304]{0:T(1024)(128)(4,1)S(1)}, s32[]{:S(2)}) async-start(s8[14680064]{0:T(1024)(128)(4,1)} %bitcast.34), calls=%async_computation.4 | async-start | bytes 8388608
  62.6 7.5 %slice-start.2 = ((s8[14680064]{0:T(1024)(128)(4,1)}), s8[4194304]{0:T(1024)(128)(4,1)S(1)}, s32[]{:S(2)}) async-start(s8[14680064]{0:T(1024)(128)(4,1)} %bitcast.34), calls=%async_computation.5 | async-start | bytes 8388608
  62.6 7.5 %slice-start.3 = ((s8[14680064]{0:T(1024)(128)(4,1)}), s8[2097152]{0:T(1024)(128)(4,1)S(1)}, s32[]{:S(2)}) async-start(s8[14680064]{0:T(1024)(128)(4,1)} %bitcast.34), calls=%async_computation.6 | async-start | bytes 4194304
Sparse Core Ops, SparseCore 0:
  10.0 43.4 all-gather.1
  73.6 59.1 reduce-scatter.1

commit v2 on v1

v2 whole, which is shorter than its diff:
```python
import functools

import jax
import jax.numpy as jnp
from jax import lax
from jax.experimental import pallas as pl
from jax.experimental.pallas import tpu as pltpu
from jax.sharding import PartitionSpec as P

LANES = 128
MAX_BLOCKS = 16
K_TILE = 512
N_TILE = 512
OUT_CHUNKS = 2
VMEM_LIMIT = 30 * 2**20


def pack_kernel(slot_ref, tokens_ref, ids_ref, route_ref, out_ref):
    rows, width = tokens_ref.shape
    experts = slot_ref.shape[0]
    column = lax.broadcasted_iota(jnp.int32, (rows, LANES), 1)
    weights = jnp.zeros((rows, LANES), jnp.float32)
    for expert in range(experts):
        at_slot = lax.rem(column, experts) == slot_ref[expert]
        for k in range(ids_ref.shape[1]):
            named = ids_ref[:, k : k + 1] == expert
            weights += jnp.where(at_slot & named, route_ref[:, k : k + 1], 0.0)
    first = weights.astype(jnp.bfloat16).astype(jnp.float32)
    second = (weights - first).astype(jnp.bfloat16).astype(jnp.float32)
    third = weights - first - second
    tail = jnp.where(column < experts, first, jnp.where(column < 2 * experts, second, third))
    out_ref[:, :width] = tokens_ref[...]
    out_ref[:, width:] = jnp.where(column < 3 * experts, tail, 0.0).astype(jnp.bfloat16)


def pack(tokens, expert_ids, route_weights, expert_slot):
    rows, width = tokens.shape
    vmem = pl.BlockSpec(memory_space=pltpu.VMEM)
    return pl.pallas_call(
        pack_kernel,
        out_shape=jax.ShapeDtypeStruct((rows, width + LANES), jnp.bfloat16),
        in_specs=[pl.BlockSpec(memory_space=pltpu.SMEM), vmem, vmem, vmem],
        out_specs=vmem,
        name="pack",
    )(expert_slot, tokens, expert_ids, route_weights)


def hidden_kernel(experts, *refs):
    *pieces, gate_ref, up_ref, out_ref, gate_acc, up_acc = refs
    step = pl.program_id(0)
    members, k_tile, hid = gate_ref.shape
    width = pieces[0].shape[1] - LANES
    columns = pl.ds(pl.multiple_of(step * k_tile, LANES), k_tile)
    x = jnp.concatenate([piece[:, columns] for piece in pieces], axis=0)

    @pl.when(step == 0)
    def _():
        gate_acc[...] = jnp.zeros_like(gate_acc)
        up_acc[...] = jnp.zeros_like(up_acc)

    for member in range(members):
        for ref, acc in ((gate_ref, gate_acc), (up_ref, up_acc)):
            acc[member] += jnp.dot(x, ref[member], preferred_element_type=jnp.float32)

    @pl.when(step == pl.num_programs(0) - 1)
    def _():
        tail = jnp.concatenate([piece[:, width:] for piece in pieces], axis=0)
        tail = tail.astype(jnp.float32)
        column = lax.broadcasted_iota(jnp.int32, tail.shape, 1)
        for member in range(members):
            slot = lax.axis_index("node") * members + member
            mine = (lax.rem(column, experts) == slot) & (column < 3 * experts)
            weight = jnp.sum(jnp.where(mine, tail, 0.0), axis=1, keepdims=True)
            gate = gate_acc[member]
            hidden = gate / (1.0 + jnp.exp(-gate)) * up_acc[member] * weight
            out_ref[:, member * hid : (member + 1) * hid] = hidden.astype(jnp.bfloat16)


def hidden_units(pieces, w_gate, w_up, experts):
    members, width, hid = w_gate.shape
    rows = sum(piece.shape[0] for piece in pieces)
    whole = pl.BlockSpec(memory_space=pltpu.VMEM)
    weights = pl.BlockSpec((members, K_TILE, hid), lambda k: (0, k, 0))
    return pl.pallas_call(
        functools.partial(hidden_kernel, experts),
        grid=(width // K_TILE,),
        out_shape=jax.ShapeDtypeStruct((rows, members * hid), jnp.bfloat16),
        in_specs=[whole] * len(pieces) + [weights, weights],
        out_specs=pl.BlockSpec((rows, members * hid), lambda k: (0, 0)),
        scratch_shapes=[pltpu.VMEM((members, rows, hid), jnp.float32)] * 2,
        compiler_params=pltpu.CompilerParams(vmem_limit_bytes=VMEM_LIMIT),
        cost_estimate=pl.CostEstimate(
            flops=4 * rows * members * width * hid,
            bytes_accessed=4 * members * width * hid,
            transcendentals=rows * members * hid,
        ),
        name="hidden",
    )(*pieces, w_gate, w_up)


def down_kernel(hidden_ref, down_ref, keep_ref, send_ref):
    members, hid, _ = down_ref.shape
    half = keep_ref.shape[0]
    total = sum(
        jnp.dot(
            hidden_ref[:, member * hid : (member + 1) * hid],
            down_ref[member],
            preferred_element_type=jnp.float32,
        )
        for member in range(members)
    ).astype(jnp.bfloat16)
    keep_ref[...] = total[:half]
    send_ref[...] = total[half:]


def down(hidden, w_down, chunk, chunks):
    members, hid, width = w_down.shape
    rows = hidden.shape[0]
    steps = width // chunks // N_TILE
    half = pl.BlockSpec((rows // 2, N_TILE), lambda j: (0, j))
    return pl.pallas_call(
        down_kernel,
        grid=(steps,),
        out_shape=[jax.ShapeDtypeStruct((rows // 2, width // chunks), jnp.bfloat16)] * 2,
        in_specs=[
            pl.BlockSpec((rows, members * hid), lambda j: (0, 0)),
            pl.BlockSpec((members, hid, N_TILE), lambda j: (0, 0, chunk * steps + j)),
        ],
        out_specs=[half, half],
        compiler_params=pltpu.CompilerParams(vmem_limit_bytes=VMEM_LIMIT),
        cost_estimate=pl.CostEstimate(
            flops=2 * rows * members * hid * width // chunks,
            bytes_accessed=2 * members * hid * width // chunks,
            transcendentals=0,
        ),
        name="down",
    )(hidden, w_down)


def swap(value, axis, bits):
    size = lax.axis_size(axis)
    return lax.ppermute(value, axis, [(i, i ^ bits) for i in range(size)])


def gather_blocks(own):
    chips = lax.axis_size("node") // 2
    along = [own] + [swap(own, "local", dz) for dz in range(1, lax.axis_size("local"))]
    chip = along + [swap(piece, "node", 2 * dx) for dx in range(1, chips) for piece in along]
    return chip + [swap(piece, "node", 1) for piece in chip]


def add(*terms):
    return sum(term.astype(jnp.float32) for term in terms).astype(jnp.bfloat16)


def reduce_blocks(keep, send, rows):
    places = lax.axis_size("local")
    chips = lax.axis_size("node") // 2
    chip = add(keep, swap(send, "node", 1)).reshape(chips, places * rows, -1)
    along = add(chip[0], *[swap(chip[dx], "node", 2 * dx) for dx in range(1, chips)])
    along = along.reshape(places, rows, -1)
    return add(along[0], *[swap(along[dz], "local", dz) for dz in range(1, places)])


def by_permutes(tokens, expert_ids, route_weights, expert_slot, w_gate, w_up, w_down):
    rows = tokens.shape[0]
    pieces = gather_blocks(pack(tokens, expert_ids, route_weights, expert_slot))
    hidden = hidden_units(pieces, w_gate, w_up, expert_slot.shape[0])
    outs = []
    for chunk in range(OUT_CHUNKS):
        keep, send = down(hidden, w_down, chunk, OUT_CHUNKS)
        outs.append(reduce_blocks(keep, send, rows))
    return jnp.concatenate(outs, axis=1)


def by_collectives(tokens, expert_ids, route_weights, expert_slot, w_gate, w_up, w_down):
    members, width, _ = w_gate.shape
    experts = expert_slot.shape[0]
    packed = pack(tokens, expert_ids, route_weights, expert_slot)
    gathered = lax.all_gather(packed, ("node", "local"), axis=0, tiled=True)
    rows = gathered[:, :width]
    tail = gathered[:, width : width + 3 * experts].astype(jnp.float32)
    weights = tail.reshape(-1, 3, experts).sum(axis=1)
    mine = lax.dynamic_slice_in_dim(weights, lax.axis_index("node") * members, members, axis=1)
    gate = jnp.einsum("td,edh->eth", rows, w_gate, preferred_element_type=jnp.float32)
    up = jnp.einsum("td,edh->eth", rows, w_up, preferred_element_type=jnp.float32)
    hidden = (jax.nn.silu(gate) * up * mine.T[..., None]).astype(jnp.bfloat16)
    result = jnp.einsum("eth,ehd->td", hidden, w_down, preferred_element_type=jnp.float32)
    return lax.psum_scatter(
        result.astype(jnp.bfloat16), ("node", "local"), scatter_dimension=0, tiled=True
    )


def per_device(*args):
    blocks = lax.axis_size("node") * lax.axis_size("local")
    return (by_permutes if blocks <= MAX_BLOCKS else by_collectives)(*args)


def solution(mesh):
    rows = P(("parts", "node", "local"), None)
    in_specs = (
        rows,
        rows,
        rows,
        P(),
        P("node", None, "local"),
        P("node", None, "local"),
        P("node", "local", None),
    )
    return jax.shard_map(
        per_device, mesh=mesh, in_specs=in_specs, out_specs=rows, check_vma=False
    )
```

time: 140 us -> 80.3 us (0.57)
  waiting for transfers between devices: 103 us -> 26 us
  starting transfers between devices: 0.04 us -> 22.4 us
  Pallas kernels: 0 us -> 21.3 us
  matrix products: 18.7 us -> 0 us
  between operations: 13.5 us -> 0.17 us
  local copies, waits for them, and re-layouts: 1.82 us -> 8.84 us
  other arithmetic: 2.57 us -> 1.04 us
    reduce_scatter x1 -> x0, waiting for transfers between devices: 59.3 us -> none  [per_device(): lax.psum_scatter(result.astype(jnp.bfloat16), ('node', 'local'), scatter_...]
    all_gather x1 -> x0, waiting for transfers between devices: 43.6 us -> none  [per_device(): gathered = lax.all_gather(packed, ('node', 'local'), axis=0, tiled=True)]
    ppermute x0 -> x25, waiting for transfers between devices: none -> 26 us  [swap(): return lax.ppermute(value, axis, [(i, i ^ bits) for i in range(size)])]
    ppermute x0 -> x25, starting transfers between devices: none -> 22.4 us  [swap(): return lax.ppermute(value, axis, [(i, i ^ bits) for i in range(size)])]
    pallas_call x0 -> x4, Pallas kernels: none -> 21.3 us  [the longest x1 13.7 us: hidden_units(): pl.pallas_call(functools.partial(hidden_kernel, experts), grid=(width //...]
    dot_general x3 -> x0, matrix products: 18.7 us -> none  [the longest x1 7.95 us: per_device(): jnp.einsum('td,edh->eth', rows, w_gate, preferred_element_type=jnp.float32)]
    unnamed x10 -> x14, local copies, waits for them, and re-layouts: 0.02 us -> 8.78 us
    reduce_sum x2 -> x0, other arithmetic: 1.67 us -> none  [the longest x1 0.91 us: slot_weights(): slot_ids = jnp.sum(jnp.where(lookup, expert_slot, 0), axis=-1)]
  transfers between devices with their start and end apart: 2 -> 25, of which waited for: 2 -> 11; matrix products, arithmetic and copies ran while one was open for 0% -> 1% of each run, Pallas kernels for 0% -> 4%
where the time goes in v2:
time: 80.3 us; the launch traced here: 79.8 us
  waiting for transfers between devices  26 us (32%)
  starting transfers between devices  22.4 us (28%)
  Pallas kernels  21.3 us (27%)
  local copies, waits for them, and re-layouts  8.84 us (11%)
  other arithmetic  1.04 us (1%)
    ppermute x25, waiting for transfers between devices, swap(): return lax.ppermute(value, axis, [(i, i ^ bits) for i in range(size)])  26 us
    ppermute x25, starting transfers between devices, swap(): return lax.ppermute(value, axis, [(i, i ^ bits) for i in range(size)])  22.4 us
    pallas_call x1, Pallas kernels, hidden_units(): pl.pallas_call(functools.partial(hidden_kernel, experts), grid=(width //...  13.7 us
    unnamed x14, local copies, waits for them, and re-layouts  8.78 us
    pallas_call x2, Pallas kernels, down(): pl.pallas_call(down_kernel, grid=(steps,), out_shape=[jax.ShapeDtypeStruc...  5.72 us
    pallas_call x1, Pallas kernels, pack(): pl.pallas_call(pack_kernel, out_shape=jax.ShapeDtypeStruct((rows, width +...  1.85 us
  transfers between devices with their start and end apart: 25, of which 11 were waited for; matrix products, arithmetic and copies ran while one was open for 1% of the time, Pallas kernels for 4%

profile of v2, /device:TPU:0, one launch (start us, length us, event | category | flops | bytes accessed | tf_op | source)
XLA Modules:
  0.0 79.8 jit_solution(9711850412546222486)
XLA Ops:
  0.0 1.3 %copy.8.ids_ref = s32[8,4]{1,0:T(8,128)} copy(s32[8,4]{0,1:T(4,128)} %param.8) | data formatting | bytes 256 | tf_op args[1]
  1.3 1.3 %copy.9.route_ref = f32[8,4]{1,0:T(8,128)} copy(f32[8,4]{0,1:T(4,128)} %param.9) | data formatting | bytes 256 | tf_op args[2]
  2.7 1.9 %pack.1.refs_0_ = bf16[8,7296]{1,0:T(8,128)(2,1)} custom-call(s32[8]{0:T(128)} %slot_ref.1, bf16[8,7168]{1,0:T(8,128)(2,1)} %tokens_ref.1, s32[8,4]{1,0:T(8,128)} %copy.8.ids_ref, f32[8,4]{1,0:T(8,128)} %copy.9.route_ref), custom_call_target="tpu_custom_call" | custom-call | tf_op jit(solution)/shard_map/pack/pallas_call | solution.py:39
  4.6 3.0 %collective-permute-start.3 = (bf16[8,7296]{1,0:T(8,128)(2,1)}, bf16[8,7296]{1,0:T(8,128)(2,1)S(1)}, u32[]{:S(2)}, u32[]{:S(2)}) collective-permute-start(bf16[8,7296]{1,0:T(8,128)(2,1)} %pack.1.refs_0_), channel_id=1, source_target_pairs={{0,8},{4,12},{8,0},{12,4},{1,9},{5,13},{9,1},{13,5},{2,10},{6,14},... | collective-permute-start | bytes 350216 | tf_op jit(solution)/shard_map/ppermute | solution.py:142
  7.6 3.6 %collective-permute-start.2 = (bf16[8,7296]{1,0:T(8,128)(2,1)}, bf16[8,7296]{1,0:T(8,128)(2,1)S(1)}, u32[]{:S(2)}, u32[]{:S(2)}) collective-permute-start(bf16[8,7296]{1,0:T(8,128)(2,1)} %pack.1.refs_0_), channel_id=1, source_target_pairs={{0,3},{1,2},{2,1},{3,0},{4,7},{5,6},{6,5},{7,4},{8,11},{9,10},{10,... | collective-permute-start | bytes 350216 | tf_op jit(solution)/shard_map/ppermute | solution.py:142
  11.2 0.0 collective-permute-start.7
  11.2 0.0 collective-permute-start.1
  11.2 0.8 collective-permute-start
  11.9 0.0 collective-permute-done.3.refs_4_
  11.9 0.0 collective-permute-start.11
  12.0 3.2 %collective-permute-done.2.refs_3_ = bf16[8,7296]{1,0:T(8,128)(2,1)S(1)} collective-permute-done((bf16[8,7296]{1,0:T(8,128)(2,1)}, bf16[8,7296]{1,0:T(8,128)(2,1)S(1)}, u32[]{:S(2)}, u32[]{:S(2)}) %collective-permute-start.2) | collective-permute-done | bytes 116768 | tf_op jit(solution)/shard_map/ppermute | solution.py:142
  15.1 0.0 collective-permute-start.10
  15.1 0.0 collective-permute-done.7.refs_8_
  15.1 0.5 collective-permute-start.6
  15.7 5.3 %collective-permute-done.1.refs_2_ = bf16[8,7296]{1,0:T(8,128)(2,1)S(1)} collective-permute-done((bf16[8,7296]{1,0:T(8,128)(2,1)}, bf16[8,7296]{1,0:T(8,128)(2,1)S(1)}, u32[]{:S(2)}, u32[]{:S(2)}) %collective-permute-start.1) | collective-permute-done | bytes 116768 | tf_op jit(solution)/shard_map/ppermute | solution.py:142
  20.9 0.5 collective-permute-start.5
  21.5 0.0 collective-permute-done.refs_1_
  21.5 1.5 %collective-permute-start.4 = (bf16[8,7296]{1,0:T(8,128)(2,1)S(1)}, bf16[8,7296]{1,0:T(8,128)(2,1)S(1)}, u32[]{:S(2)}, u32[]{:S(2)}) collective-permute-start(bf16[8,7296]{1,0:T(8,128)(2,1)S(1)} %collective-permute-done.refs_1_), channel_id=1, source_target_pairs={{0,8},{4,12},{8,0},{12,4},{1,9},{5,13},{9,1},{13,5},{2,10},{6,14},... | collective-permute-start | bytes 350216 | tf_op jit(solution)/shard_map/ppermute | solution.py:142
  23.0 0.0 collective-permute-done.11.refs_12_
  23.0 0.0 collective-permute-start.9
  23.0 0.0 collective-permute-done.10.refs_11_
  23.0 0.5 collective-permute-start.8
  23.5 0.0 collective-permute-done.6.refs_7_
  23.5 0.1 collective-permute-start.14
  23.6 2.8 %collective-permute-done.5.refs_6_ = bf16[8,7296]{1,0:T(8,128)(2,1)S(1)} collective-permute-done((bf16[8,7296]{1,0:T(8,128)(2,1)S(1)}, bf16[8,7296]{1,0:T(8,128)(2,1)S(1)}, u32[]{:S(2)}, u32[]{:S(2)}) %collective-permute-start.5) | collective-permute-done | bytes 116768 | tf_op jit(solution)/shard_map/ppermute | solution.py:142
  26.4 0.0 collective-permute-start.13
  26.4 1.2 %collective-permute-done.4.refs_5_ = bf16[8,7296]{1,0:T(8,128)(2,1)S(1)} collective-permute-done((bf16[8,7296]{1,0:T(8,128)(2,1)S(1)}, bf16[8,7296]{1,0:T(8,128)(2,1)S(1)}, u32[]{:S(2)}, u32[]{:S(2)}) %collective-permute-start.4) | collective-permute-done | bytes 116768 | tf_op jit(solution)/shard_map/ppermute | solution.py:142
  27.6 0.0 collective-permute-start.12
  27.6 0.0 collective-permute-done.9.refs_10_
  27.6 0.0 collective-permute-done.8.refs_9_
  27.6 0.0 collective-permute-done.14.refs_15_
  27.6 0.1 collective-permute-done.13.refs_14_
  27.7 1.3 %collective-permute-done.12.refs_13_ = bf16[8,7296]{1,0:T(8,128)(2,1)S(1)} collective-permute-done((bf16[8,7296]{1,0:T(8,128)(2,1)S(1)}, bf16[8,7296]{1,0:T(8,128)(2,1)S(1)}, u32[]{:S(2)}, u32[]{:S(2)}) %collective-permute-start.12) | collective-permute-done | bytes 116768 | tf_op jit(solution)/shard_map/ppermute | solution.py:142
  28.9 5.2 %copy-done = bf16[2,7168,512]{2,1,0:T(8,128)(2,1)S(1)} copy-done((bf16[2,7168,512]{2,1,0:T(8,128)(2,1)S(1)}, bf16[2,7168,512]{2,1,0:T(8,128)(2,1)}, u32[]{:S(2)}) %copy-start) | copy-done | bytes 14680088
  34.1 0.9 %copy-done.1 = bf16[8,7296]{1,0:T(8,128)(2,1)S(1)} copy-done((bf16[8,7296]{1,0:T(8,128)(2,1)S(1)}, bf16[8,7296]{1,0:T(8,128)(2,1)}, u32[]{:S(2)}) %copy-start.1) | copy-done | bytes 116760
  35.0 13.7 %hidden.1.hidden_ref = bf16[128,1024]{1,0:T(8,128)(2,1)S(1)} custom-call(bf16[8,7296]{1,0:T(8,128)(2,1)S(1)} %copy-done.1, bf16[8,7296]{1,0:T(8,128)(2,1)S(1)} %collective-permute-done.refs_1_, bf16[8,7296]{1,0:T(8,128)(2,1)S(1)} %collective-permute-done.1.refs_2_, bf16[8,7296]{1,0:T(8,128)(2,1)S(1)} %collective-permute-done.2.refs_3_, ...), custom_call_target="tpu_custom_call" | custom-call | flops 3758096384 | bytes 29360128 | tf_op jit(solution)/shard_map/hidden/pallas_call | solution.py:84
  48.7 0.0 slice-done
  48.8 2.9 %down.3 = (bf16[64,3584]{1,0:T(8,128)(2,1)S(1)}, bf16[64,3584]{1,0:T(8,128)(2,1)S(1)}) custom-call(bf16[128,1024]{1,0:T(8,128)(2,1)S(1)} %hidden.1.hidden_ref, bf16[2,512,7168]{2,1,0:T(8,128)(2,1)S(1)} %bitcast.1), custom_call_target="tpu_custom_call" | custom-call | flops 939524096 | bytes 7340032 | tf_op jit(solution)/shard_map/down/pallas_call | solution.py:121
  51.6 0.2 collective-permute-start.20
  51.9 2.9 %down.2 = (bf16[64,3584]{1,0:T(8,128)(2,1)S(1)}, bf16[64,3584]{1,0:T(8,128)(2,1)S(1)}) custom-call(bf16[128,1024]{1,0:T(8,128)(2,1)S(1)} %hidden.1.hidden_ref, bf16[2,512,7168]{2,1,0:T(8,128)(2,1)S(1)} %bitcast.1), custom_call_target="tpu_custom_call" | custom-call | flops 939524096 | bytes 7340032 | tf_op jit(solution)/shard_map/down/pallas_call | solution.py:121
  54.7 0.4 collective-permute-start.15
  55.1 0.0 collective-permute-done.20
  55.1 0.1 add_convert_fusion
  55.3 0.6 collective-permute-start.21
  55.9 0.7 collective-permute-done.15
  56.6 0.1 add_convert_fusion.1
  56.7 0.8 %collective-permute-start.16 = (bf16[32,3584]{1,0:T(8,128)(2,1)S(1)}, bf16[32,3584]{1,0:T(8,128)(2,1)S(1)}, u32[]{:S(2)}, u32[]{:S(2)}) collective-permute-start(bf16[32,3584]{1,0:T(8,128)(2,1)S(1)} %slice.61), channel_id=1, source_target_pairs={{0,8},{4,12},{8,0},{12,4},{1,9},{5,13},{9,1},{13,5},{2,10},{6,14},... | collective-permute-start | bytes 688136 | tf_op jit(solution)/shard_map/ppermute | solution.py:142
  57.6 6.2 %collective-permute-done.21 = bf16[32,3584]{1,0:T(8,128)(2,1)S(1)} collective-permute-done((bf16[32,3584]{1,0:T(8,128)(2,1)S(1)}, bf16[32,3584]{1,0:T(8,128)(2,1)S(1)}, u32[]{:S(2)}, u32[]{:S(2)}) %collective-permute-start.21) | collective-permute-done | bytes 229408 | tf_op jit(solution)/shard_map/ppermute | solution.py:142
  63.8 0.1 add_convert_fusion.2
  63.9 3.1 %collective-permute-start.22 = (bf16[8,3584]{1,0:T(8,128)(2,1)S(1)}, bf16[8,3584]{1,0:T(8,128)(2,1)S(1)}, u32[]{:S(2)}, u32[]{:S(2)}) collective-permute-start(bf16[8,3584]{1,0:T(8,128)(2,1)S(1)} %get-tuple-element.16), channel_id=1, source_target_pairs={{0,1},{1,0},{2,3},{3,2},{4,5},{5,4},{6,7},{7,6},{8,9},{9,8},{10,11... | collective-permute-start | bytes 172040 | tf_op jit(solution)/shard_map/ppermute | solution.py:142
  67.0 2.3 %collective-permute-start.24 = (bf16[8,3584]{1,0:T(8,128)(2,1)S(1)}, bf16[8,3584]{1,0:T(8,128)(2,1)S(1)}, u32[]{:S(2)}, u32[]{:S(2)}) collective-permute-start(bf16[8,3584]{1,0:T(8,128)(2,1)S(1)} %get-tuple-element.17), channel_id=1, source_target_pairs={{0,3},{1,2},{2,1},{3,0},{4,7},{5,6},{6,5},{7,4},{8,11},{9,10},{10,... | collective-permute-start | bytes 172040 | tf_op jit(solution)/shard_map/ppermute | solution.py:142
  69.2 0.0 collective-permute-start.23
  69.2 0.0 collective-permute-done.16
  69.2 0.1 add_convert_fusion.3
  69.3 2.2 %collective-permute-start.17 = (bf16[8,3584]{1,0:T(8,128)(2,1)S(1)}, bf16[8,3584]{1,0:T(8,128)(2,1)S(1)}, u32[]{:S(2)}, u32[]{:S(2)}) collective-permute-start(bf16[8,3584]{1,0:T(8,128)(2,1)S(1)} %get-tuple-element.13), channel_id=1, source_target_pairs={{0,1},{1,0},{2,3},{3,2},{4,5},{5,4},{6,7},{7,6},{8,9},{9,8},{10,11... | collective-permute-start | bytes 172040 | tf_op jit(solution)/shard_map/ppermute | solution.py:142
  71.5 2.3 %collective-permute-start.19 = (bf16[8,3584]{1,0:T(8,128)(2,1)S(1)}, bf16[8,3584]{1,0:T(8,128)(2,1)S(1)}, u32[]{:S(2)}, u32[]{:S(2)}) collective-permute-start(bf16[8,3584]{1,0:T(8,128)(2,1)S(1)} %get-tuple-element.14), channel_id=1, source_target_pairs={{0,3},{1,2},{2,1},{3,0},{4,7},{5,6},{6,5},{7,4},{8,11},{9,10},{10,... | collective-permute-start | bytes 172040 | tf_op jit(solution)/shard_map/ppermute | solution.py:142
  73.8 0.0 collective-permute-done.22
  73.8 0.0 collective-permute-start.18
  73.8 0.0 collective-permute-done.24
  73.8 2.0 %collective-permute-done.23 = bf16[8,3584]{1,0:T(8,128)(2,1)S(1)} collective-permute-done((bf16[8,3584]{1,0:T(8,128)(2,1)S(1)}, bf16[8,3584]{1,0:T(8,128)(2,1)S(1)}, u32[]{:S(2)}, u32[]{:S(2)}) %collective-permute-start.23) | collective-permute-done | bytes 57376 | tf_op jit(solution)/shard_map/ppermute | solution.py:142
  75.8 0.0 collective-permute-done.17
  75.8 1.8 %collective-permute-done.19 = bf16[8,3584]{1,0:T(8,128)(2,1)S(1)} collective-permute-done((bf16[8,3584]{1,0:T(8,128)(2,1)S(1)}, bf16[8,3584]{1,0:T(8,128)(2,1)S(1)}, u32[]{:S(2)}, u32[]{:S(2)}) %collective-permute-start.19) | collective-permute-done | bytes 57376 | tf_op jit(solution)/shard_map/ppermute | solution.py:142
  77.6 1.5 %collective-permute-done.18 = bf16[8,3584]{1,0:T(8,128)(2,1)S(1)} collective-permute-done((bf16[8,3584]{1,0:T(8,128)(2,1)S(1)}, bf16[8,3584]{1,0:T(8,128)(2,1)S(1)}, u32[]{:S(2)}, u32[]{:S(2)}) %collective-permute-start.18) | collective-permute-done | bytes 57376 | tf_op jit(solution)/shard_map/ppermute | solution.py:142
  79.1 0.7 pad_maximum_fusion
  (16 shorter events, 0.1 us)
Async XLA Ops:
  2.7 46.0 %slice-start = ((s8[14680064]{0:T(1024)(128)(4,1)}), s8[2097152]{0:T(1024)(128)(4,1)S(1)}, s32[]{:S(2)}) async-start(s8[14680064]{0:T(1024)(128)(4,1)} %bitcast), calls=%async_computation | async-start | bytes 4194304
  4.5 44.2 %slice-start.1 = ((s8[14680064]{0:T(1024)(128)(4,1)}), s8[4194304]{0:T(1024)(128)(4,1)S(1)}, s32[]{:S(2)}) async-start(s8[14680064]{0:T(1024)(128)(4,1)} %bitcast), calls=%async_computation.1 | async-start | bytes 8388608
  4.6 44.2 %slice-start.2 = ((s8[14680064]{0:T(1024)(128)(4,1)}), s8[4194304]{0:T(1024)(128)(4,1)S(1)}, s32[]{:S(2)}) async-start(s8[14680064]{0:T(1024)(128)(4,1)} %bitcast), calls=%async_computation.2 | async-start | bytes 8388608
  4.6 44.2 %slice-start.3 = ((s8[14680064]{0:T(1024)(128)(4,1)}), s8[4194304]{0:T(1024)(128)(4,1)S(1)}, s32[]{:S(2)}) async-start(s8[14680064]{0:T(1024)(128)(4,1)} %bitcast), calls=%async_computation.3 | async-start | bytes 8388608
  4.6 7.4 %collective-permute-start.3 = (bf16[8,7296]{1,0:T(8,128)(2,1)}, bf16[8,7296]{1,0:T(8,128)(2,1)S(1)}, u32[]{:S(2)}, u32[]{:S(2)}) collective-permute-start(bf16[8,7296]{1,0:T(8,128)(2,1)} %pack.1.refs_0_), channel_id=1, source_target_pairs={{0,8},{4,12},{8,0},{12,4},{1,9},{5,13},{9,1},{13,5},{2,10},{6,14},... | collective-permute-start | bytes 350216 | tf_op jit(solution)/shard_map/ppermute | solution.py:142
  7.6 7.6 %collective-permute-start.2 = (bf16[8,7296]{1,0:T(8,128)(2,1)}, bf16[8,7296]{1,0:T(8,128)(2,1)S(1)}, u32[]{:S(2)}, u32[]{:S(2)}) collective-permute-start(bf16[8,7296]{1,0:T(8,128)(2,1)} %pack.1.refs_0_), channel_id=1, source_target_pairs={{0,3},{1,2},{2,1},{3,0},{4,7},{5,6},{6,5},{7,4},{8,11},{9,10},{10,... | collective-permute-start | bytes 350216 | tf_op jit(solution)/shard_map/ppermute | solution.py:142
  11.2 4.0 %collective-permute-start.7 = (bf16[8,7296]{1,0:T(8,128)(2,1)}, bf16[8,7296]{1,0:T(8,128)(2,1)S(1)}, u32[]{:S(2)}, u32[]{:S(2)}) collective-permute-start(bf16[8,7296]{1,0:T(8,128)(2,1)} %pack.1.refs_0_), channel_id=1, source_target_pairs={{0,4},{4,0},{8,12},{12,8},{1,5},{5,1},{9,13},{13,9},{2,6},{6,2},{1... | collective-permute-start | bytes 350216 | tf_op jit(solution)/shard_map/ppermute | solution.py:142
  11.2 9.8 %collective-permute-start.1 = (bf16[8,7296]{1,0:T(8,128)(2,1)}, bf16[8,7296]{1,0:T(8,128)(2,1)S(1)}, u32[]{:S(2)}, u32[]{:S(2)}) collective-permute-start(bf16[8,7296]{1,0:T(8,128)(2,1)} %pack.1.refs_0_), channel_id=1, source_target_pairs={{0,2},{1,3},{2,0},{3,1},{4,6},{5,7},{6,4},{7,5},{8,10},{9,11},{10,... | collective-permute-start | bytes 350216 | tf_op jit(solution)/shard_map/ppermute | solution.py:142
  11.2 10.3 %collective-permute-start = (bf16[8,7296]{1,0:T(8,128)(2,1)}, bf16[8,7296]{1,0:T(8,128)(2,1)S(1)}, u32[]{:S(2)}, u32[]{:S(2)}) collective-permute-start(bf16[8,7296]{1,0:T(8,128)(2,1)} %pack.1.refs_0_), channel_id=1, source_target_pairs={{0,1},{1,0},{2,3},{3,2},{4,5},{5,4},{6,7},{7,6},{8,9},{9,8},{10,11... | collective-permute-start | bytes 350216 | tf_op jit(solution)/shard_map/ppermute | solution.py:142
  11.9 11.0 %collective-permute-start.11 = (bf16[8,7296]{1,0:T(8,128)(2,1)S(1)}, bf16[8,7296]{1,0:T(8,128)(2,1)S(1)}, u32[]{:S(2)}, u32[]{:S(2)}) collective-permute-start(bf16[8,7296]{1,0:T(8,128)(2,1)S(1)} %collective-permute-done.3.refs_4_), channel_id=1, source_target_pairs={{0,4},{4,0},{8,12},{12,8},{1,5},{5,1},{9,13},{13,9},{2,6},{6,2},{1... | collective-permute-start | bytes 350216 | tf_op jit(solution)/shard_map/ppermute | solution.py:142
  15.1 7.9 %collective-permute-start.10 = (bf16[8,7296]{1,0:T(8,128)(2,1)S(1)}, bf16[8,7296]{1,0:T(8,128)(2,1)S(1)}, u32[]{:S(2)}, u32[]{:S(2)}) collective-permute-start(bf16[8,7296]{1,0:T(8,128)(2,1)S(1)} %collective-permute-done.2.refs_3_), channel_id=1, source_target_pairs={{0,4},{4,0},{8,12},{12,8},{1,5},{5,1},{9,13},{13,9},{2,6},{6,2},{1... | collective-permute-start | bytes 350216 | tf_op jit(solution)/shard_map/ppermute | solution.py:142
  15.1 8.4 %collective-permute-start.6 = (bf16[8,7296]{1,0:T(8,128)(2,1)S(1)}, bf16[8,7296]{1,0:T(8,128)(2,1)S(1)}, u32[]{:S(2)}, u32[]{:S(2)}) collective-permute-start(bf16[8,7296]{1,0:T(8,128)(2,1)S(1)} %collective-permute-done.2.refs_3_), channel_id=1, source_target_pairs={{0,8},{4,12},{8,0},{12,4},{1,9},{5,13},{9,1},{13,5},{2,10},{6,14},... | collective-permute-start | bytes 350216 | tf_op jit(solution)/shard_map/ppermute | solution.py:142
  20.9 5.4 %collective-permute-start.5 = (bf16[8,7296]{1,0:T(8,128)(2,1)S(1)}, bf16[8,7296]{1,0:T(8,128)(2,1)S(1)}, u32[]{:S(2)}, u32[]{:S(2)}) collective-permute-start(bf16[8,7296]{1,0:T(8,128)(2,1)S(1)} %collective-permute-done.1.refs_2_), channel_id=1, source_target_pairs={{0,8},{4,12},{8,0},{12,4},{1,9},{5,13},{9,1},{13,5},{2,10},{6,14},... | collective-permute-start | bytes 350216 | tf_op jit(solution)/shard_map/ppermute | solution.py:142
  21.5 6.1 %collective-permute-start.4 = (bf16[8,7296]{1,0:T(8,128)(2,1)S(1)}, bf16[8,7296]{1,0:T(8,128)(2,1)S(1)}, u32[]{:S(2)}, u32[]{:S(2)}) collective-permute-start(bf16[8,7296]{1,0:T(8,128)(2,1)S(1)} %collective-permute-done.refs_1_), channel_id=1, source_target_pairs={{0,8},{4,12},{8,0},{12,4},{1,9},{5,13},{9,1},{13,5},{2,10},{6,14},... | collective-permute-start | bytes 350216 | tf_op jit(solution)/shard_map/ppermute | solution.py:142
  23.0 4.6 %collective-permute-start.9 = (bf16[8,7296]{1,0:T(8,128)(2,1)S(1)}, bf16[8,7296]{1,0:T(8,128)(2,1)S(1)}, u32[]{:S(2)}, u32[]{:S(2)}) collective-permute-start(bf16[8,7296]{1,0:T(8,128)(2,1)S(1)} %collective-permute-done.1.refs_2_), channel_id=1, source_target_pairs={{0,4},{4,0},{8,12},{12,8},{1,5},{5,1},{9,13},{13,9},{2,6},{6,2},{1... | collective-permute-start | bytes 350216 | tf_op jit(solution)/shard_map/ppermute | solution.py:142
  23.0 4.6 %collective-permute-start.8 = (bf16[8,7296]{1,0:T(8,128)(2,1)S(1)}, bf16[8,7296]{1,0:T(8,128)(2,1)S(1)}, u32[]{:S(2)}, u32[]{:S(2)}) collective-permute-start(bf16[8,7296]{1,0:T(8,128)(2,1)S(1)} %collective-permute-done.refs_1_), channel_id=1, source_target_pairs={{0,4},{4,0},{8,12},{12,8},{1,5},{5,1},{9,13},{13,9},{2,6},{6,2},{1... | collective-permute-start | bytes 350216 | tf_op jit(solution)/shard_map/ppermute | solution.py:142
  23.5 4.1 %collective-permute-start.14 = (bf16[8,7296]{1,0:T(8,128)(2,1)S(1)}, bf16[8,7296]{1,0:T(8,128)(2,1)S(1)}, u32[]{:S(2)}, u32[]{:S(2)}) collective-permute-start(bf16[8,7296]{1,0:T(8,128)(2,1)S(1)} %collective-permute-done.6.refs_7_), channel_id=1, source_target_pairs={{0,4},{4,0},{8,12},{12,8},{1,5},{5,1},{9,13},{13,9},{2,6},{6,2},{1... | collective-permute-start | bytes 350216 | tf_op jit(solution)/shard_map/ppermute | solution.py:142
  26.4 1.3 %collective-permute-start.13 = (bf16[8,7296]{1,0:T(8,128)(2,1)S(1)}, bf16[8,7296]{1,0:T(8,128)(2,1)S(1)}, u32[]{:S(2)}, u32[]{:S(2)}) collective-permute-start(bf16[8,7296]{1,0:T(8,128)(2,1)S(1)} %collective-permute-done.5.refs_6_), channel_id=1, source_target_pairs={{0,4},{4,0},{8,12},{12,8},{1,5},{5,1},{9,13},{13,9},{2,6},{6,2},{1... | collective-permute-start | bytes 350216 | tf_op jit(solution)/shard_map/ppermute | solution.py:142
  27.6 1.3 %collective-permute-start.12 = (bf16[8,7296]{1,0:T(8,128)(2,1)S(1)}, bf16[8,7296]{1,0:T(8,128)(2,1)S(1)}, u32[]{:S(2)}, u32[]{:S(2)}) collective-permute-start(bf16[8,7296]{1,0:T(8,128)(2,1)S(1)} %collective-permute-done.4.refs_5_), channel_id=1, source_target_pairs={{0,4},{4,0},{8,12},{12,8},{1,5},{5,1},{9,13},{13,9},{2,6},{6,2},{1... | collective-permute-start | bytes 350216 | tf_op jit(solution)/shard_map/ppermute | solution.py:142
  28.9 5.2 %copy-start = (bf16[2,7168,512]{2,1,0:T(8,128)(2,1)S(1)}, bf16[2,7168,512]{2,1,0:T(8,128)(2,1)}, u32[]{:S(2)}) copy-start(bf16[2,7168,512]{2,1,0:T(8,128)(2,1)} %refs_16_.1) | copy-start | bytes 44040196
  34.1 0.9 %copy-start.1 = (bf16[8,7296]{1,0:T(8,128)(2,1)S(1)}, bf16[8,7296]{1,0:T(8,128)(2,1)}, u32[]{:S(2)}) copy-start(bf16[8,7296]{1,0:T(8,128)(2,1)} %pack.1.refs_0_) | copy-start | bytes 350212
  51.6 3.5 %collective-permute-start.20 = (bf16[64,3584]{1,0:T(8,128)(2,1)S(1)}, bf16[64,3584]{1,0:T(8,128)(2,1)S(1)}, u32[]{:S(2)}, u32[]{:S(2)}) collective-permute-start(bf16[64,3584]{1,0:T(8,128)(2,1)S(1)} %get-tuple-element.12), channel_id=1, source_target_pairs={{0,4},{4,0},{8,12},{12,8},{1,5},{5,1},{9,13},{13,9},{2,6},{6,2},{1... | collective-permute-start | bytes 1376264 | tf_op jit(solution)/shard_map/ppermute | solution.py:142
  54.7 1.9 %collective-permute-start.15 = (bf16[64,3584]{1,0:T(8,128)(2,1)S(1)}, bf16[64,3584]{1,0:T(8,128)(2,1)S(1)}, u32[]{:S(2)}, u32[]{:S(2)}) collective-permute-start(bf16[64,3584]{1,0:T(8,128)(2,1)S(1)} %get-tuple-element.10), channel_id=1, source_target_pairs={{0,4},{4,0},{8,12},{12,8},{1,5},{5,1},{9,13},{13,9},{2,6},{6,2},{1... | collective-permute-start | bytes 1376264 | tf_op jit(solution)/shard_map/ppermute | solution.py:142
  55.3 8.5 %collective-permute-start.21 = (bf16[32,3584]{1,0:T(8,128)(2,1)S(1)}, bf16[32,3584]{1,0:T(8,128)(2,1)S(1)}, u32[]{:S(2)}, u32[]{:S(2)}) collective-permute-start(bf16[32,3584]{1,0:T(8,128)(2,1)S(1)} %slice.67), channel_id=1, source_target_pairs={{0,8},{4,12},{8,0},{12,4},{1,9},{5,13},{9,1},{13,5},{2,10},{6,14},... | collective-permute-start | bytes 688136 | tf_op jit(solution)/shard_map/ppermute | solution.py:142
  56.7 12.5 %collective-permute-start.16 = (bf16[32,3584]{1,0:T(8,128)(2,1)S(1)}, bf16[32,3584]{1,0:T(8,128)(2,1)S(1)}, u32[]{:S(2)}, u32[]{:S(2)}) collective-permute-start(bf16[32,3584]{1,0:T(8,128)(2,1)S(1)} %slice.61), channel_id=1, source_target_pairs={{0,8},{4,12},{8,0},{12,4},{1,9},{5,13},{9,1},{13,5},{2,10},{6,14},... | collective-permute-start | bytes 688136 | tf_op jit(solution)/shard_map/ppermute | solution.py:142
  63.9 9.9 %collective-permute-start.22 = (bf16[8,3584]{1,0:T(8,128)(2,1)S(1)}, bf16[8,3584]{1,0:T(8,128)(2,1)S(1)}, u32[]{:S(2)}, u32[]{:S(2)}) collective-permute-start(bf16[8,3584]{1,0:T(8,128)(2,1)S(1)} %get-tuple-element.16), channel_id=1, source_target_pairs={{0,1},{1,0},{2,3},{3,2},{4,5},{5,4},{6,7},{7,6},{8,9},{9,8},{10,11... | collective-permute-start | bytes 172040 | tf_op jit(solution)/shard_map/ppermute | solution.py:142
  67.0 6.8 %collective-permute-start.24 = (bf16[8,3584]{1,0:T(8,128)(2,1)S(1)}, bf16[8,3584]{1,0:T(8,128)(2,1)S(1)}, u32[]{:S(2)}, u32[]{:S(2)}) collective-permute-start(bf16[8,3584]{1,0:T(8,128)(2,1)S(1)} %get-tuple-element.17), channel_id=1, source_target_pairs={{0,3},{1,2},{2,1},{3,0},{4,7},{5,6},{6,5},{7,4},{8,11},{9,10},{10,... | collective-permute-start | bytes 172040 | tf_op jit(solution)/shard_map/ppermute | solution.py:142
  69.2 6.5 %collective-permute-start.23 = (bf16[8,3584]{1,0:T(8,128)(2,1)S(1)}, bf16[8,3584]{1,0:T(8,128)(2,1)S(1)}, u32[]{:S(2)}, u32[]{:S(2)}) collective-permute-start(bf16[8,3584]{1,0:T(8,128)(2,1)S(1)} %get-tuple-element.18), channel_id=1, source_target_pairs={{0,2},{1,3},{2,0},{3,1},{4,6},{5,7},{6,4},{7,5},{8,10},{9,11},{10,... | collective-permute-start | bytes 172040 | tf_op jit(solution)/shard_map/ppermute | solution.py:142
  69.3 6.5 %collective-permute-start.17 = (bf16[8,3584]{1,0:T(8,128)(2,1)S(1)}, bf16[8,3584]{1,0:T(8,128)(2,1)S(1)}, u32[]{:S(2)}, u32[]{:S(2)}) collective-permute-start(bf16[8,3584]{1,0:T(8,128)(2,1)S(1)} %get-tuple-element.13), channel_id=1, source_target_pairs={{0,1},{1,0},{2,3},{3,2},{4,5},{5,4},{6,7},{7,6},{8,9},{9,8},{10,11... | collective-permute-start | bytes 172040 | tf_op jit(solution)/shard_map/ppermute | solution.py:142
  71.5 6.1 %collective-permute-start.19 = (bf16[8,3584]{1,0:T(8,128)(2,1)S(1)}, bf16[8,3584]{1,0:T(8,128)(2,1)S(1)}, u32[]{:S(2)}, u32[]{:S(2)}) collective-permute-start(bf16[8,3584]{1,0:T(8,128)(2,1)S(1)} %get-tuple-element.14), channel_id=1, source_target_pairs={{0,3},{1,2},{2,1},{3,0},{4,7},{5,6},{6,5},{7,4},{8,11},{9,10},{10,... | collective-permute-start | bytes 172040 | tf_op jit(solution)/shard_map/ppermute | solution.py:142
  73.8 5.3 %collective-permute-start.18 = (bf16[8,3584]{1,0:T(8,128)(2,1)S(1)}, bf16[8,3584]{1,0:T(8,128)(2,1)S(1)}, u32[]{:S(2)}, u32[]{:S(2)}) collective-permute-start(bf16[8,3584]{1,0:T(8,128)(2,1)S(1)} %get-tuple-element.15), channel_id=1, source_target_pairs={{0,2},{1,3},{2,0},{3,1},{4,6},{5,7},{6,4},{7,5},{8,10},{9,11},{10,... | collective-permute-start | bytes 172040 | tf_op jit(solution)/shard_map/ppermute | solution.py:142

commit v3 on v2

v3 whole, which is shorter than its diff:
```python
import functools

import jax
import jax.numpy as jnp
from jax import lax
from jax.experimental import pallas as pl
from jax.experimental.pallas import tpu as pltpu
from jax.sharding import PartitionSpec as P

LANES = 128
K_TILE = 1024
N_TILE = 512
OUT_CHUNKS = 1
VMEM_LIMIT = 8 * 2**20


def pack_kernel(slot_ref, ids_ref, route_ref, tokens_ref, out_ref):
    rows, width = tokens_ref.shape
    experts = slot_ref.shape[0]
    row = lax.broadcasted_iota(jnp.int32, (rows, LANES), 0)
    column = lax.broadcasted_iota(jnp.int32, (rows, LANES), 1)
    slot = lax.rem(column, experts)
    weights = jnp.zeros((rows, LANES), jnp.float32)
    for k in range(ids_ref.shape[0]):
        for token in range(rows):
            named = (row == token) & (slot == slot_ref[ids_ref[k, token]])
            weights = jnp.where(named, route_ref[k, token], weights)
    first = weights.astype(jnp.bfloat16).astype(jnp.float32)
    second = (weights - first).astype(jnp.bfloat16).astype(jnp.float32)
    third = weights - first - second
    tail = jnp.where(column < experts, first, jnp.where(column < 2 * experts, second, third))
    out_ref[:, :width] = tokens_ref[...]
    out_ref[:, width:] = jnp.where(column < 3 * experts, tail, 0.0).astype(jnp.bfloat16)


def pack(tokens, expert_ids, route_weights, expert_slot):
    rows, width = tokens.shape
    vmem = pl.BlockSpec(memory_space=pltpu.VMEM)
    smem = pl.BlockSpec(memory_space=pltpu.SMEM)
    return pl.pallas_call(
        pack_kernel,
        out_shape=jax.ShapeDtypeStruct((rows, width + LANES), jnp.bfloat16),
        in_specs=[smem, smem, smem, vmem],
        out_specs=vmem,
        compiler_params=pltpu.CompilerParams(vmem_limit_bytes=VMEM_LIMIT),
        name="pack",
    )(expert_slot, expert_ids.T, route_weights.T, tokens)


def fetch_kernel(weights_ref, out_ref):
    del weights_ref
    out_ref[...] = jnp.zeros_like(out_ref)


def fetch(weights):
    return pl.pallas_call(
        fetch_kernel,
        out_shape=jax.ShapeDtypeStruct((8, LANES), jnp.float32),
        in_specs=[pl.BlockSpec(memory_space=pl.ANY)],
        out_specs=pl.BlockSpec(memory_space=pltpu.VMEM),
        compiler_params=pltpu.CompilerParams(vmem_limit_bytes=VMEM_LIMIT, has_side_effects=True),
        name="fetch",
    )(weights)


def hidden_kernel(experts, *refs):
    *pieces, gate_ref, up_ref, out_ref, x_ref, gate_acc, up_acc = refs
    members, width, hid = gate_ref.shape
    steps = width // K_TILE

    def add_product(step, ref, acc):
        at = pl.ds(pl.multiple_of(step * K_TILE, K_TILE), K_TILE)
        for member in range(members):
            acc[member] += jnp.dot(
                x_ref[:, at], ref[member, at], preferred_element_type=jnp.float32
            )

    gate_acc[...] = jnp.zeros_like(gate_acc)
    up_acc[...] = jnp.zeros_like(up_acc)

    @pl.loop(0, steps)
    def _(step):
        at = pl.ds(pl.multiple_of(step * K_TILE, K_TILE), K_TILE)
        x_ref[:, at] = jnp.concatenate([piece[:, at] for piece in pieces], axis=0)
        add_product(step, gate_ref, gate_acc)

    @pl.loop(0, steps)
    def _(step):
        add_product(step, up_ref, up_acc)

    tail = jnp.concatenate([piece[:, width:] for piece in pieces], axis=0)
    tail = tail.astype(jnp.float32)
    column = lax.broadcasted_iota(jnp.int32, tail.shape, 1)
    for member in range(members):
        slot = lax.axis_index("node") * members + member
        mine = (lax.rem(column, experts) == slot) & (column < 3 * experts)
        weight = jnp.sum(jnp.where(mine, tail, 0.0), axis=1, keepdims=True)
        gate = gate_acc[member]
        hidden = gate / (1.0 + jnp.exp(-gate)) * up_acc[member] * weight
        out_ref[:, member * hid : (member + 1) * hid] = hidden.astype(jnp.bfloat16)


def hidden_units(pieces, w_gate, w_up, experts):
    members, width, hid = w_gate.shape
    rows = sum(piece.shape[0] for piece in pieces)
    vmem = pl.BlockSpec(memory_space=pltpu.VMEM)
    return pl.pallas_call(
        functools.partial(hidden_kernel, experts),
        out_shape=jax.ShapeDtypeStruct((rows, members * hid), jnp.bfloat16),
        in_specs=[vmem] * (len(pieces) + 2),
        out_specs=vmem,
        scratch_shapes=[
            pltpu.VMEM((rows, width), jnp.bfloat16),
            pltpu.VMEM((members, rows, hid), jnp.float32),
            pltpu.VMEM((members, rows, hid), jnp.float32),
        ],
        compiler_params=pltpu.CompilerParams(vmem_limit_bytes=VMEM_LIMIT),
        cost_estimate=pl.CostEstimate(
            flops=4 * rows * members * width * hid,
            bytes_accessed=4 * members * width * hid,
            transcendentals=rows * members * hid,
        ),
        name="hidden",
    )(*pieces, w_gate, w_up)


def down_kernel(chunk, hidden_ref, down_ref, keep_ref, send_ref):
    members, hid, _ = down_ref.shape
    half, width = keep_ref.shape

    @pl.loop(0, width // N_TILE)
    def _(step):
        here = pl.ds(pl.multiple_of(step * N_TILE, N_TILE), N_TILE)
        there = pl.ds(pl.multiple_of(chunk * width + step * N_TILE, N_TILE), N_TILE)
        total = sum(
            jnp.dot(
                hidden_ref[:, member * hid : (member + 1) * hid],
                down_ref[member, :, there],
                preferred_element_type=jnp.float32,
            )
            for member in range(members)
        ).astype(jnp.bfloat16)
        keep_ref[:, here] = total[:half]
        send_ref[:, here] = total[half:]


def down(hidden, w_down, chunk, chunks):
    members, hid, width = w_down.shape
    rows = hidden.shape[0]
    vmem = pl.BlockSpec(memory_space=pltpu.VMEM)
    return pl.pallas_call(
        functools.partial(down_kernel, chunk),
        out_shape=[jax.ShapeDtypeStruct((rows // 2, width // chunks), jnp.bfloat16)] * 2,
        in_specs=[vmem, vmem],
        out_specs=[vmem, vmem],
        compiler_params=pltpu.CompilerParams(vmem_limit_bytes=VMEM_LIMIT),
        cost_estimate=pl.CostEstimate(
            flops=2 * rows * members * hid * width // chunks,
            bytes_accessed=2 * members * hid * width // chunks,
            transcendentals=0,
        ),
        name="down",
    )(hidden, w_down)


CHIPS, PLACES = 2, 4


def to_core(value):
    return lax.ppermute(value, "node", [(i, i ^ 1) for i in range(2 * CHIPS)])


def to_chip(value):
    return lax.ppermute(value, "node", [(i, i ^ 2) for i in range(2 * CHIPS)])


def to_place(value, bits):
    return lax.ppermute(value, "local", [(i, i ^ bits) for i in range(PLACES)])


def gather_blocks(own, meanwhile):
    third = to_place(own, 3)
    first = to_place(own, 1)
    third, _ = lax.optimization_barrier((third, meanwhile()))
    along = [own, first, to_place(third, 1), third]
    chip = along + [to_chip(piece) for piece in along]
    return chip + [to_core(piece) for piece in chip]


def add(*terms):
    return sum(term.astype(jnp.float32) for term in terms).astype(jnp.bfloat16)


def reduce_blocks(keep, send, rows):
    half = PLACES * rows
    far = add(keep[half:], to_core(send[half:])).reshape(PLACES, rows, -1)
    near = add(keep[:half], to_core(send[:half])).reshape(PLACES, rows, -1)
    own, first, second, third = [
        add(near[place], to_chip(far[place])) for place in range(PLACES)
    ]
    third = add(third, to_place(second, 1))
    return add(own, to_place(first, 1), to_place(third, 3))


def by_permutes(tokens, expert_ids, route_weights, expert_slot, w_gate, w_up, w_down):
    rows = tokens.shape[0]
    own = pack(tokens, expert_ids, route_weights, expert_slot)
    pieces = gather_blocks(own, lambda: fetch(w_gate))
    hidden = hidden_units(pieces, w_gate, w_up, expert_slot.shape[0])
    outs = []
    for chunk in range(OUT_CHUNKS):
        keep, send = down(hidden, w_down, chunk, OUT_CHUNKS)
        outs.append(reduce_blocks(keep, send, rows))
    return jnp.concatenate(outs, axis=1)


def by_collectives(tokens, expert_ids, route_weights, expert_slot, w_gate, w_up, w_down):
    members, width, _ = w_gate.shape
    experts = expert_slot.shape[0]
    packed = pack(tokens, expert_ids, route_weights, expert_slot)
    gathered = lax.all_gather(packed, ("node", "local"), axis=0, tiled=True)
    rows = gathered[:, :width]
    tail = gathered[:, width : width + 3 * experts].astype(jnp.float32)
    weights = tail.reshape(-1, 3, experts).sum(axis=1)
    mine = lax.dynamic_slice_in_dim(weights, lax.axis_index("node") * members, members, axis=1)
    gate = jnp.einsum("td,edh->eth", rows, w_gate, preferred_element_type=jnp.float32)
    up = jnp.einsum("td,edh->eth", rows, w_up, preferred_element_type=jnp.float32)
    hidden = (jax.nn.silu(gate) * up * mine.T[..., None]).astype(jnp.bfloat16)
    result = jnp.einsum("eth,ehd->td", hidden, w_down, preferred_element_type=jnp.float32)
    return lax.psum_scatter(
        result.astype(jnp.bfloat16), ("node", "local"), scatter_dimension=0, tiled=True
    )


def per_device(*args):
    small = (lax.axis_size("node"), lax.axis_size("local")) == (2 * CHIPS, PLACES)
    return (by_permutes if small else by_collectives)(*args)


def solution(mesh):
    rows = P(("parts", "node", "local"), None)
    in_specs = (
        rows,
        rows,
        rows,
        P(),
        P("node", None, "local"),
        P("node", None, "local"),
        P("node", "local", None),
    )
    return jax.shard_map(
        per_device, mesh=mesh, in_specs=in_specs, out_specs=rows, check_vma=False
    )
```

time: 80.3 us -> 65.1 us (0.81)
  Pallas kernels: 21.3 us -> 12.4 us
  starting transfers between devices: 22.4 us -> 18.4 us
  waiting for transfers between devices: 26 us -> 24.7 us
    pallas_call x3, Pallas kernels: 19.4 us -> 11.7 us  [the longest x1 6.57 us: hidden_units(): pl.pallas_call(functools.partial(hidden_kernel, experts), out_shape=jax.S...]
    ppermute x25 -> x24, starting transfers between devices: 22.4 us -> 18.4 us  [the longest x6 9.61 us: to_place(): return lax.ppermute(value, 'local', [(i, i ^ bits) for i in range(PLACES)])]
    ppermute x25 -> x24, waiting for transfers between devices: 26 us -> 24.7 us  [the longest x8 12.1 us: to_chip(): return lax.ppermute(value, 'node', [(i, i ^ 2) for i in range(2 * CHIPS)])]
    pallas_call x1, Pallas kernels: 1.85 us -> 0.65 us  [pack(): pl.pallas_call(pack_kernel, out_shape=jax.ShapeDtypeStruct((rows, width +...]
    unnamed x14 -> x20, local copies, waits for them, and re-layouts: 8.78 us -> 8.11 us
  transfers between devices with their start and end apart: 25 -> 24, of which waited for: 11 -> 12; matrix products, arithmetic and copies ran while one was open for 1% -> 0% of each run, Pallas kernels for 4% -> 1%
where the time goes in v3:
time: 65.1 us; the launch traced here: 64.9 us
  waiting for transfers between devices  24.7 us (38%)
  starting transfers between devices  18.4 us (28%)
  Pallas kernels  12.4 us (19%)
  local copies, waits for them, and re-layouts  8.2 us (13%)
  other arithmetic  1.02 us (2%)
    ppermute x8, waiting for transfers between devices, to_chip(): return lax.ppermute(value, 'node', [(i, i ^ 2) for i in range(2 * CHIPS)])  12.1 us
    ppermute x6, starting transfers between devices, to_place(): return lax.ppermute(value, 'local', [(i, i ^ bits) for i in range(PLACES)])  9.61 us
    ppermute x6, waiting for transfers between devices, to_place(): return lax.ppermute(value, 'local', [(i, i ^ bits) for i in range(PLACES)])  9.3 us
    unnamed x20, local copies, waits for them, and re-layouts  8.11 us
    ppermute x8, starting transfers between devices, to_chip(): return lax.ppermute(value, 'node', [(i, i ^ 2) for i in range(2 * CHIPS)])  7.23 us
    pallas_call x1, Pallas kernels, hidden_units(): pl.pallas_call(functools.partial(hidden_kernel, experts), out_shape=jax.S...  6.57 us
    pallas_call x1, Pallas kernels, down(): pl.pallas_call(functools.partial(down_kernel, chunk), out_shape=[jax.Shap...  4.56 us
    ppermute x10, waiting for transfers between devices, to_core(): return lax.ppermute(value, 'node', [(i, i ^ 1) for i in range(2 * CHIPS)])  3.27 us
  transfers between devices with their start and end apart: 24, of which 12 were waited for; matrix products, arithmetic and copies ran while one was open for 0% of the time, Pallas kernels for 1%

profile of v3, /device:TPU:0, one launch (start us, length us, event | category | flops | bytes accessed | tf_op | source)
XLA Modules:
  0.0 64.9 jit_solution(2142922242510197158)
XLA Ops:
  0.0 0.9 %copy-done.2 = bf16[8,7168]{1,0:T(8,128)(2,1)S(1)} copy-done((bf16[8,7168]{1,0:T(8,128)(2,1)S(1)}, bf16[8,7168]{1,0:T(8,128)(2,1)}, u32[]{:S(2)}) %copy-start.2) | copy-done | bytes 114712
  0.9 0.7 %copy-done.3 = s32[8,4]{0,1:T(4,128)S(1)} copy-done((s32[8,4]{0,1:T(4,128)S(1)}, s32[8,4]{0,1:T(4,128)}, u32[]{:S(2)}) %copy-start.3) | copy-done | bytes 152
  1.6 0.7 %copy-done.4 = f32[8,4]{0,1:T(4,128)S(1)} copy-done((f32[8,4]{0,1:T(4,128)S(1)}, f32[8,4]{0,1:T(4,128)}, u32[]{:S(2)}) %copy-start.4) | copy-done | bytes 152
  2.3 0.7 %copy-done.5 = s32[8]{0:T(128)S(1)} copy-done((s32[8]{0:T(128)S(1)}, s32[8]{0:T(128)}, u32[]{:S(2)}) %copy-start.5) | copy-done | bytes 56
  2.9 0.7 %pack.1.refs_0_ = bf16[8,7296]{1,0:T(8,128)(2,1)S(1)} custom-call(s32[8]{0:T(128)S(1)} %copy-done.5, s32[4,8]{1,0:T(4,128)S(1)} %bitcast.4, f32[4,8]{1,0:T(4,128)S(1)} %bitcast.5, bf16[8,7168]{1,0:T(8,128)(2,1)S(1)} %copy-done.2), custom_call_target="tpu_custom_call" | custom-call | tf_op jit(solution)/shard_map/pack/pallas_call | solution.py:40
  3.6 5.1 %collective-permute-start.1 = (bf16[8,7296]{1,0:T(8,128)(2,1)S(1)}, bf16[8,7296]{1,0:T(8,128)(2,1)S(1)}, u32[]{:S(2)}, u32[]{:S(2)}) collective-permute-start(bf16[8,7296]{1,0:T(8,128)(2,1)S(1)} %pack.1.refs_0_), channel_id=1, source_target_pairs={{0,3},{1,2},{2,1},{3,0},{4,7},{5,6},{6,5},{7,4},{8,11},{9,10},{10,... | collective-permute-start | bytes 350216 | tf_op jit(solution)/shard_map/ppermute | solution.py:178
  8.7 0.0 collective-permute-start.7
  8.7 1.5 %collective-permute-start.3 = (bf16[8,7296]{1,0:T(8,128)(2,1)S(1)}, bf16[8,7296]{1,0:T(8,128)(2,1)S(1)}, u32[]{:S(2)}, u32[]{:S(2)}) collective-permute-start(bf16[8,7296]{1,0:T(8,128)(2,1)S(1)} %pack.1.refs_0_), channel_id=1, source_target_pairs={{0,8},{4,12},{8,0},{12,4},{1,9},{5,13},{9,1},{13,5},{2,10},{6,14},... | collective-permute-start | bytes 350216 | tf_op jit(solution)/shard_map/ppermute | solution.py:174
  10.2 0.0 collective-permute-start
  10.2 5.2 %copy-done = bf16[2,7168,512]{2,1,0:T(8,128)(2,1)S(1)} copy-done((bf16[2,7168,512]{2,1,0:T(8,128)(2,1)S(1)}, bf16[2,7168,512]{2,1,0:T(8,128)(2,1)}, u32[]{:S(2)}) %copy-start) | copy-done | bytes 14680088
  15.4 0.6 fetch.1
  16.0 0.0 collective-permute-done.1.refs_3_
  16.0 2.0 %collective-permute-start.2 = (bf16[8,7296]{1,0:T(8,128)(2,1)S(1)}, bf16[8,7296]{1,0:T(8,128)(2,1)S(1)}, u32[]{:S(2)}, u32[]{:S(2)}) collective-permute-start(bf16[8,7296]{1,0:T(8,128)(2,1)S(1)} %collective-permute-done.1.refs_3_), channel_id=1, source_target_pairs={{0,1},{1,0},{2,3},{3,2},{4,5},{5,4},{6,7},{7,6},{8,9},{9,8},{10,11... | collective-permute-start | bytes 350216 | tf_op jit(solution)/shard_map/ppermute | solution.py:178
  18.0 0.0 collective-permute-done.3.refs_4_
  18.0 0.0 collective-permute-start.11
  18.0 0.5 collective-permute-start.10
  18.5 0.0 collective-permute-done.7.refs_8_
  18.5 0.5 collective-permute-start.6
  19.0 0.0 collective-permute-done.refs_1_
  19.1 1.5 %collective-permute-start.4 = (bf16[8,7296]{1,0:T(8,128)(2,1)S(1)}, bf16[8,7296]{1,0:T(8,128)(2,1)S(1)}, u32[]{:S(2)}, u32[]{:S(2)}) collective-permute-start(bf16[8,7296]{1,0:T(8,128)(2,1)S(1)} %collective-permute-done.refs_1_), channel_id=1, source_target_pairs={{0,8},{4,12},{8,0},{12,4},{1,9},{5,13},{9,1},{13,5},{2,10},{6,14},... | collective-permute-start | bytes 350216 | tf_op jit(solution)/shard_map/ppermute | solution.py:174
  20.5 0.8 %collective-permute-done.2.refs_2_ = bf16[8,7296]{1,0:T(8,128)(2,1)S(1)} collective-permute-done((bf16[8,7296]{1,0:T(8,128)(2,1)S(1)}, bf16[8,7296]{1,0:T(8,128)(2,1)S(1)}, u32[]{:S(2)}, u32[]{:S(2)}) %collective-permute-start.2) | collective-permute-done | bytes 116768 | tf_op jit(solution)/shard_map/ppermute | solution.py:178
  21.3 0.5 collective-permute-start.5
  21.8 0.0 collective-permute-done.11.refs_12_
  21.8 0.0 collective-permute-start.8
  21.8 0.0 collective-permute-done.10.refs_11_
  21.8 0.5 collective-permute-start.9
  22.3 2.2 %collective-permute-done.6.refs_7_ = bf16[8,7296]{1,0:T(8,128)(2,1)S(1)} collective-permute-done((bf16[8,7296]{1,0:T(8,128)(2,1)S(1)}, bf16[8,7296]{1,0:T(8,128)(2,1)S(1)}, u32[]{:S(2)}, u32[]{:S(2)}) %collective-permute-start.6) | collective-permute-done | bytes 116768 | tf_op jit(solution)/shard_map/ppermute | solution.py:174
  24.6 0.0 collective-permute-start.14
  24.6 2.5 %collective-permute-done.4.refs_5_ = bf16[8,7296]{1,0:T(8,128)(2,1)S(1)} collective-permute-done((bf16[8,7296]{1,0:T(8,128)(2,1)S(1)}, bf16[8,7296]{1,0:T(8,128)(2,1)S(1)}, u32[]{:S(2)}, u32[]{:S(2)}) %collective-permute-start.4) | collective-permute-done | bytes 116768 | tf_op jit(solution)/shard_map/ppermute | solution.py:174
  27.1 0.0 collective-permute-start.12
  27.1 1.5 %collective-permute-done.5.refs_6_ = bf16[8,7296]{1,0:T(8,128)(2,1)S(1)} collective-permute-done((bf16[8,7296]{1,0:T(8,128)(2,1)S(1)}, bf16[8,7296]{1,0:T(8,128)(2,1)S(1)}, u32[]{:S(2)}, u32[]{:S(2)}) %collective-permute-start.5) | collective-permute-done | bytes 116768 | tf_op jit(solution)/shard_map/ppermute | solution.py:174
  28.6 0.0 collective-permute-start.13
  28.6 0.0 collective-permute-done.8.refs_9_
  28.6 0.0 collective-permute-done.14.refs_15_
  28.6 0.0 collective-permute-done.9.refs_10_
  28.6 0.0 collective-permute-done.12.refs_13_
  28.6 1.3 %collective-permute-done.13.refs_14_ = bf16[8,7296]{1,0:T(8,128)(2,1)S(1)} collective-permute-done((bf16[8,7296]{1,0:T(8,128)(2,1)S(1)}, bf16[8,7296]{1,0:T(8,128)(2,1)S(1)}, u32[]{:S(2)}, u32[]{:S(2)}) %collective-permute-start.13) | collective-permute-done | bytes 116768 | tf_op jit(solution)/shard_map/ppermute | solution.py:170
  29.9 0.0 copy-done.1
  29.9 6.6 %hidden.1.hidden_ref = bf16[128,1024]{1,0:T(8,128)(2,1)S(1)} custom-call(bf16[8,7296]{1,0:T(8,128)(2,1)S(1)} %pack.1.refs_0_, bf16[8,7296]{1,0:T(8,128)(2,1)S(1)} %collective-permute-done.refs_1_, bf16[8,7296]{1,0:T(8,128)(2,1)S(1)} %collective-permute-done.2.refs_2_, bf16[8,7296]{1,0:T(8,128)(2,1)S(1)} %collective-permute-done.1.refs_3_, ...), custom_call_target="tpu_custom_call" | custom-call | flops 3758096384 | bytes 29360128 | tf_op jit(solution)/shard_map/hidden/pallas_call | solution.py:107
  36.5 0.0 slice-done
  36.5 0.0 slice-done.1
  36.6 4.6 %down.1 = (bf16[64,7168]{1,0:T(8,128)(2,1)S(1)}, bf16[64,7168]{1,0:T(8,128)(2,1)S(1)}) custom-call(bf16[128,1024]{1,0:T(8,128)(2,1)S(1)} %hidden.1.hidden_ref, bf16[2,512,7168]{2,1,0:T(8,128)(2,1)S(1)} %bitcast.3), custom_call_target="tpu_custom_call" | custom-call | flops 1879048192 | bytes 14680064 | tf_op jit(solution)/shard_map/down/pallas_call | solution.py:151
  41.1 0.1 fusion
  41.2 0.2 collective-permute-start.15
  41.4 0.4 collective-permute-start.16
  41.8 1.3 %collective-permute-done.15 = bf16[32,7168]{1,0:T(8,128)(2,1)S(1)} collective-permute-done((bf16[32,7168]{1,0:T(8,128)(2,1)S(1)}, bf16[32,7168]{1,0:T(8,128)(2,1)S(1)}, u32[]{:S(2)}, u32[]{:S(2)}) %collective-permute-start.15) | collective-permute-done | bytes 458784 | tf_op jit(solution)/shard_map/ppermute | solution.py:170
  43.1 0.7 %collective-permute-done.16 = bf16[32,7168]{1,0:T(8,128)(2,1)S(1)} collective-permute-done((bf16[32,7168]{1,0:T(8,128)(2,1)S(1)}, bf16[32,7168]{1,0:T(8,128)(2,1)S(1)}, u32[]{:S(2)}, u32[]{:S(2)}) %collective-permute-start.16) | collective-permute-done | bytes 458784 | tf_op jit(solution)/shard_map/ppermute | solution.py:170
  43.7 0.2 add_convert_fusion.1
  44.0 0.6 collective-permute-start.21
  44.6 1.5 %collective-permute-start.18 = (bf16[8,7168]{1,0:T(8,128)(2,1)S(1)}, bf16[8,7168]{1,0:T(8,128)(2,1)S(1)}, u32[]{:S(2)}, u32[]{:S(2)}) collective-permute-start(bf16[8,7168]{1,0:T(8,128)(2,1)S(1)} %get-tuple-element.18), channel_id=1, source_target_pairs={{0,8},{4,12},{8,0},{12,4},{1,9},{5,13},{9,1},{13,5},{2,10},{6,14},... | collective-permute-start | bytes 344072 | tf_op jit(solution)/shard_map/ppermute | solution.py:174
  46.1 0.5 collective-permute-start.20
  46.6 3.4 %collective-permute-done.21 = bf16[8,7168]{1,0:T(8,128)(2,1)S(1)} collective-permute-done((bf16[8,7168]{1,0:T(8,128)(2,1)S(1)}, bf16[8,7168]{1,0:T(8,128)(2,1)S(1)}, u32[]{:S(2)}, u32[]{:S(2)}) %collective-permute-start.21) | collective-permute-done | bytes 114720 | tf_op jit(solution)/shard_map/ppermute | solution.py:174
  50.1 2.5 %collective-permute-done.18 = bf16[8,7168]{1,0:T(8,128)(2,1)S(1)} collective-permute-done((bf16[8,7168]{1,0:T(8,128)(2,1)S(1)}, bf16[8,7168]{1,0:T(8,128)(2,1)S(1)}, u32[]{:S(2)}, u32[]{:S(2)}) %collective-permute-start.18) | collective-permute-done | bytes 114720 | tf_op jit(solution)/shard_map/ppermute | solution.py:174
  52.5 0.1 add_convert_fusion.6
  52.6 0.2 collective-permute-start.22
  52.8 0.5 collective-permute-start.17
  53.3 1.9 %collective-permute-start.19 = (bf16[8,7168]{1,0:T(8,128)(2,1)S(1)}, bf16[8,7168]{1,0:T(8,128)(2,1)S(1)}, u32[]{:S(2)}, u32[]{:S(2)}) collective-permute-start(bf16[8,7168]{1,0:T(8,128)(2,1)S(1)} %get-tuple-element.19), channel_id=1, source_target_pairs={{0,1},{1,0},{2,3},{3,2},{4,5},{5,4},{6,7},{7,6},{8,9},{9,8},{10,11... | collective-permute-start | bytes 344072 | tf_op jit(solution)/shard_map/ppermute | solution.py:178
  55.2 0.0 collective-permute-done.20
  55.2 2.3 %collective-permute-done.22 = bf16[8,7168]{1,0:T(8,128)(2,1)S(1)} collective-permute-done((bf16[8,7168]{1,0:T(8,128)(2,1)S(1)}, bf16[8,7168]{1,0:T(8,128)(2,1)S(1)}, u32[]{:S(2)}, u32[]{:S(2)}) %collective-permute-start.22) | collective-permute-done | bytes 114720 | tf_op jit(solution)/shard_map/ppermute | solution.py:178
  57.5 0.4 collective-permute-start.23
  57.9 0.0 collective-permute-done.17
  57.9 0.8 %collective-permute-done.19 = bf16[8,7168]{1,0:T(8,128)(2,1)S(1)} collective-permute-done((bf16[8,7168]{1,0:T(8,128)(2,1)S(1)}, bf16[8,7168]{1,0:T(8,128)(2,1)S(1)}, u32[]{:S(2)}, u32[]{:S(2)}) %collective-permute-start.19) | collective-permute-done | bytes 114720 | tf_op jit(solution)/shard_map/ppermute | solution.py:178
  58.7 5.5 %collective-permute-done.23 = bf16[8,7168]{1,0:T(8,128)(2,1)S(1)} collective-permute-done((bf16[8,7168]{1,0:T(8,128)(2,1)S(1)}, bf16[8,7168]{1,0:T(8,128)(2,1)S(1)}, u32[]{:S(2)}, u32[]{:S(2)}) %collective-permute-start.23) | collective-permute-done | bytes 114720 | tf_op jit(solution)/shard_map/ppermute | solution.py:178
  64.2 0.7 %add_convert_fusion.2 = bf16[8,7168]{1,0:T(8,128)(2,1)} fusion(bf16[8,7168]{1,0:T(8,128)(2,1)S(1)} %collective-permute-done.23, bf16[8,7168]{1,0:T(8,128)(2,1)S(1)} %collective-permute-done.19, bf16[8,7168]{1,0:T(8,128)(2,1)S(1)} %collective-permute-done.17, bf16[32,7168]{1,0:T(8,128)(2,1)S(1)} %get-tuple-element.11), kind=kLoop, calls=%fused_computation.2 | loop fusion | flops 573440 | bytes 573440 | tf_op jit(solution)/shard_map/convert_element_type | solution.py:191
  (15 shorter events, 0.1 us)
Async XLA Ops:
  0.0 0.9 %copy-start.2 = (bf16[8,7168]{1,0:T(8,128)(2,1)S(1)}, bf16[8,7168]{1,0:T(8,128)(2,1)}, u32[]{:S(2)}) copy-start(bf16[8,7168]{1,0:T(8,128)(2,1)} %tokens_ref.1) | copy-start | bytes 344068
  0.9 0.7 %copy-start.3 = (s32[8,4]{0,1:T(4,128)S(1)}, s32[8,4]{0,1:T(4,128)}, u32[]{:S(2)}) copy-start(s32[8,4]{0,1:T(4,128)} %param.8) | copy-start | bytes 388
  1.6 0.7 %copy-start.4 = (f32[8,4]{0,1:T(4,128)S(1)}, f32[8,4]{0,1:T(4,128)}, u32[]{:S(2)}) copy-start(f32[8,4]{0,1:T(4,128)} %param.9) | copy-start | bytes 388
  2.3 0.7 %copy-start.5 = (s32[8]{0:T(128)S(1)}, s32[8]{0:T(128)}, u32[]{:S(2)}) copy-start(s32[8]{0:T(128)} %slot_ref.1) | copy-start | bytes 100
  3.6 12.4 %collective-permute-start.1 = (bf16[8,7296]{1,0:T(8,128)(2,1)S(1)}, bf16[8,7296]{1,0:T(8,128)(2,1)S(1)}, u32[]{:S(2)}, u32[]{:S(2)}) collective-permute-start(bf16[8,7296]{1,0:T(8,128)(2,1)S(1)} %pack.1.refs_0_), channel_id=1, source_target_pairs={{0,3},{1,2},{2,1},{3,0},{4,7},{5,6},{6,5},{7,4},{8,11},{9,10},{10,... | collective-permute-start | bytes 350216 | tf_op jit(solution)/shard_map/ppermute | solution.py:178
  8.7 9.8 %collective-permute-start.7 = (bf16[8,7296]{1,0:T(8,128)(2,1)S(1)}, bf16[8,7296]{1,0:T(8,128)(2,1)S(1)}, u32[]{:S(2)}, u32[]{:S(2)}) collective-permute-start(bf16[8,7296]{1,0:T(8,128)(2,1)S(1)} %pack.1.refs_0_), channel_id=1, source_target_pairs={{0,4},{4,0},{8,12},{12,8},{1,5},{5,1},{9,13},{13,9},{2,6},{6,2},{1... | collective-permute-start | bytes 350216 | tf_op jit(solution)/shard_map/ppermute | solution.py:170
  8.7 9.3 %collective-permute-start.3 = (bf16[8,7296]{1,0:T(8,128)(2,1)S(1)}, bf16[8,7296]{1,0:T(8,128)(2,1)S(1)}, u32[]{:S(2)}, u32[]{:S(2)}) collective-permute-start(bf16[8,7296]{1,0:T(8,128)(2,1)S(1)} %pack.1.refs_0_), channel_id=1, source_target_pairs={{0,8},{4,12},{8,0},{12,4},{1,9},{5,13},{9,1},{13,5},{2,10},{6,14},... | collective-permute-start | bytes 350216 | tf_op jit(solution)/shard_map/ppermute | solution.py:174
  10.2 8.9 %collective-permute-start = (bf16[8,7296]{1,0:T(8,128)(2,1)S(1)}, bf16[8,7296]{1,0:T(8,128)(2,1)S(1)}, u32[]{:S(2)}, u32[]{:S(2)}) collective-permute-start(bf16[8,7296]{1,0:T(8,128)(2,1)S(1)} %pack.1.refs_0_), channel_id=1, source_target_pairs={{0,1},{1,0},{2,3},{3,2},{4,5},{5,4},{6,7},{7,6},{8,9},{9,8},{10,11... | collective-permute-start | bytes 350216 | tf_op jit(solution)/shard_map/ppermute | solution.py:178
  10.2 5.2 %copy-start = (bf16[2,7168,512]{2,1,0:T(8,128)(2,1)S(1)}, bf16[2,7168,512]{2,1,0:T(8,128)(2,1)}, u32[]{:S(2)}) copy-start(bf16[2,7168,512]{2,1,0:T(8,128)(2,1)} %refs_16_.1) | copy-start | bytes 44040196
  15.4 14.6 %copy-start.1 = (bf16[2,7168,512]{2,1,0:T(8,128)(2,1)S(1)}, bf16[2,7168,512]{2,1,0:T(8,128)(2,1)}, u32[]{:S(2)}) copy-start(bf16[2,7168,512]{2,1,0:T(8,128)(2,1)} %refs_17_.1) | copy-start | bytes 44040196
  15.4 21.2 %slice-start = ((s8[14680064]{0:T(1024)(128)(4,1)}), s8[4194304]{0:T(1024)(128)(4,1)S(1)}, s32[]{:S(2)}) async-start(s8[14680064]{0:T(1024)(128)(4,1)} %bitcast.2), calls=%async_computation | async-start | bytes 8388608
  15.4 21.2 %slice-start.1 = ((s8[14680064]{0:T(1024)(128)(4,1)}), s8[4194304]{0:T(1024)(128)(4,1)S(1)}, s32[]{:S(2)}) async-start(s8[14680064]{0:T(1024)(128)(4,1)} %bitcast.2), calls=%async_computation.1 | async-start | bytes 8388608
  16.0 20.6 %slice-start.2 = ((s8[14680064]{0:T(1024)(128)(4,1)}), s8[4194304]{0:T(1024)(128)(4,1)S(1)}, s32[]{:S(2)}) async-start(s8[14680064]{0:T(1024)(128)(4,1)} %bitcast.2), calls=%async_computation.2 | async-start | bytes 8388608
  16.0 20.6 %slice-start.3 = ((s8[14680064]{0:T(1024)(128)(4,1)}), s8[2097152]{0:T(1024)(128)(4,1)S(1)}, s32[]{:S(2)}) async-start(s8[14680064]{0:T(1024)(128)(4,1)} %bitcast.2), calls=%async_computation.3 | async-start | bytes 4194304
  16.0 5.3 %collective-permute-start.2 = (bf16[8,7296]{1,0:T(8,128)(2,1)S(1)}, bf16[8,7296]{1,0:T(8,128)(2,1)S(1)}, u32[]{:S(2)}, u32[]{:S(2)}) collective-permute-start(bf16[8,7296]{1,0:T(8,128)(2,1)S(1)} %collective-permute-done.1.refs_3_), channel_id=1, source_target_pairs={{0,1},{1,0},{2,3},{3,2},{4,5},{5,4},{6,7},{7,6},{8,9},{9,8},{10,11... | collective-permute-start | bytes 350216 | tf_op jit(solution)/shard_map/ppermute | solution.py:178
  18.0 3.8 %collective-permute-start.11 = (bf16[8,7296]{1,0:T(8,128)(2,1)S(1)}, bf16[8,7296]{1,0:T(8,128)(2,1)S(1)}, u32[]{:S(2)}, u32[]{:S(2)}) collective-permute-start(bf16[8,7296]{1,0:T(8,128)(2,1)S(1)} %collective-permute-done.3.refs_4_), channel_id=1, source_target_pairs={{0,4},{4,0},{8,12},{12,8},{1,5},{5,1},{9,13},{13,9},{2,6},{6,2},{1... | collective-permute-start | bytes 350216 | tf_op jit(solution)/shard_map/ppermute | solution.py:170
  18.0 3.8 %collective-permute-start.10 = (bf16[8,7296]{1,0:T(8,128)(2,1)S(1)}, bf16[8,7296]{1,0:T(8,128)(2,1)S(1)}, u32[]{:S(2)}, u32[]{:S(2)}) collective-permute-start(bf16[8,7296]{1,0:T(8,128)(2,1)S(1)} %collective-permute-done.1.refs_3_), channel_id=1, source_target_pairs={{0,4},{4,0},{8,12},{12,8},{1,5},{5,1},{9,13},{13,9},{2,6},{6,2},{1... | collective-permute-start | bytes 350216 | tf_op jit(solution)/shard_map/ppermute | solution.py:170
  18.5 6.1 %collective-permute-start.6 = (bf16[8,7296]{1,0:T(8,128)(2,1)S(1)}, bf16[8,7296]{1,0:T(8,128)(2,1)S(1)}, u32[]{:S(2)}, u32[]{:S(2)}) collective-permute-start(bf16[8,7296]{1,0:T(8,128)(2,1)S(1)} %collective-permute-done.1.refs_3_), channel_id=1, source_target_pairs={{0,8},{4,12},{8,0},{12,4},{1,9},{5,13},{9,1},{13,5},{2,10},{6,14},... | collective-permute-start | bytes 350216 | tf_op jit(solution)/shard_map/ppermute | solution.py:174
  19.1 8.0 %collective-permute-start.4 = (bf16[8,7296]{1,0:T(8,128)(2,1)S(1)}, bf16[8,7296]{1,0:T(8,128)(2,1)S(1)}, u32[]{:S(2)}, u32[]{:S(2)}) collective-permute-start(bf16[8,7296]{1,0:T(8,128)(2,1)S(1)} %collective-permute-done.refs_1_), channel_id=1, source_target_pairs={{0,8},{4,12},{8,0},{12,4},{1,9},{5,13},{9,1},{13,5},{2,10},{6,14},... | collective-permute-start | bytes 350216 | tf_op jit(solution)/shard_map/ppermute | solution.py:174
  21.3 7.3 %collective-permute-start.5 = (bf16[8,7296]{1,0:T(8,128)(2,1)S(1)}, bf16[8,7296]{1,0:T(8,128)(2,1)S(1)}, u32[]{:S(2)}, u32[]{:S(2)}) collective-permute-start(bf16[8,7296]{1,0:T(8,128)(2,1)S(1)} %collective-permute-done.2.refs_2_), channel_id=1, source_target_pairs={{0,8},{4,12},{8,0},{12,4},{1,9},{5,13},{9,1},{13,5},{2,10},{6,14},... | collective-permute-start | bytes 350216 | tf_op jit(solution)/shard_map/ppermute | solution.py:174
  21.8 6.8 %collective-permute-start.8 = (bf16[8,7296]{1,0:T(8,128)(2,1)S(1)}, bf16[8,7296]{1,0:T(8,128)(2,1)S(1)}, u32[]{:S(2)}, u32[]{:S(2)}) collective-permute-start(bf16[8,7296]{1,0:T(8,128)(2,1)S(1)} %collective-permute-done.refs_1_), channel_id=1, source_target_pairs={{0,4},{4,0},{8,12},{12,8},{1,5},{5,1},{9,13},{13,9},{2,6},{6,2},{1... | collective-permute-start | bytes 350216 | tf_op jit(solution)/shard_map/ppermute | solution.py:170
  21.8 6.8 %collective-permute-start.9 = (bf16[8,7296]{1,0:T(8,128)(2,1)S(1)}, bf16[8,7296]{1,0:T(8,128)(2,1)S(1)}, u32[]{:S(2)}, u32[]{:S(2)}) collective-permute-start(bf16[8,7296]{1,0:T(8,128)(2,1)S(1)} %collective-permute-done.2.refs_2_), channel_id=1, source_target_pairs={{0,4},{4,0},{8,12},{12,8},{1,5},{5,1},{9,13},{13,9},{2,6},{6,2},{1... | collective-permute-start | bytes 350216 | tf_op jit(solution)/shard_map/ppermute | solution.py:170
  24.6 4.1 %collective-permute-start.14 = (bf16[8,7296]{1,0:T(8,128)(2,1)S(1)}, bf16[8,7296]{1,0:T(8,128)(2,1)S(1)}, u32[]{:S(2)}, u32[]{:S(2)}) collective-permute-start(bf16[8,7296]{1,0:T(8,128)(2,1)S(1)} %collective-permute-done.6.refs_7_), channel_id=1, source_target_pairs={{0,4},{4,0},{8,12},{12,8},{1,5},{5,1},{9,13},{13,9},{2,6},{6,2},{1... | collective-permute-start | bytes 350216 | tf_op jit(solution)/shard_map/ppermute | solution.py:170
  27.1 1.6 %collective-permute-start.12 = (bf16[8,7296]{1,0:T(8,128)(2,1)S(1)}, bf16[8,7296]{1,0:T(8,128)(2,1)S(1)}, u32[]{:S(2)}, u32[]{:S(2)}) collective-permute-start(bf16[8,7296]{1,0:T(8,128)(2,1)S(1)} %collective-permute-done.4.refs_5_), channel_id=1, source_target_pairs={{0,4},{4,0},{8,12},{12,8},{1,5},{5,1},{9,13},{13,9},{2,6},{6,2},{1... | collective-permute-start | bytes 350216 | tf_op jit(solution)/shard_map/ppermute | solution.py:170
  28.6 1.3 %collective-permute-start.13 = (bf16[8,7296]{1,0:T(8,128)(2,1)S(1)}, bf16[8,7296]{1,0:T(8,128)(2,1)S(1)}, u32[]{:S(2)}, u32[]{:S(2)}) collective-permute-start(bf16[8,7296]{1,0:T(8,128)(2,1)S(1)} %collective-permute-done.5.refs_6_), channel_id=1, source_target_pairs={{0,4},{4,0},{8,12},{12,8},{1,5},{5,1},{9,13},{13,9},{2,6},{6,2},{1... | collective-permute-start | bytes 350216 | tf_op jit(solution)/shard_map/ppermute | solution.py:170
  41.2 1.9 %collective-permute-start.15 = (bf16[32,7168]{1,0:T(8,128)(2,1)S(1)}, bf16[32,7168]{1,0:T(8,128)(2,1)S(1)}, u32[]{:S(2)}, u32[]{:S(2)}) collective-permute-start(bf16[32,7168]{1,0:T(8,128)(2,1)S(1)} %get-tuple-element.13), channel_id=1, source_target_pairs={{0,4},{4,0},{8,12},{12,8},{1,5},{5,1},{9,13},{13,9},{2,6},{6,2},{1... | collective-permute-start | bytes 1376264 | tf_op jit(solution)/shard_map/ppermute | solution.py:170
  41.4 2.3 %collective-permute-start.16 = (bf16[32,7168]{1,0:T(8,128)(2,1)S(1)}, bf16[32,7168]{1,0:T(8,128)(2,1)S(1)}, u32[]{:S(2)}, u32[]{:S(2)}) collective-permute-start(bf16[32,7168]{1,0:T(8,128)(2,1)S(1)} %get-tuple-element.14), channel_id=1, source_target_pairs={{0,4},{4,0},{8,12},{12,8},{1,5},{5,1},{9,13},{13,9},{2,6},{6,2},{1... | collective-permute-start | bytes 1376264 | tf_op jit(solution)/shard_map/ppermute | solution.py:170
  44.0 6.1 %collective-permute-start.21 = (bf16[8,7168]{1,0:T(8,128)(2,1)S(1)}, bf16[8,7168]{1,0:T(8,128)(2,1)S(1)}, u32[]{:S(2)}, u32[]{:S(2)}) collective-permute-start(bf16[8,7168]{1,0:T(8,128)(2,1)S(1)} %get-tuple-element.16), channel_id=1, source_target_pairs={{0,8},{4,12},{8,0},{12,4},{1,9},{5,13},{9,1},{13,5},{2,10},{6,14},... | collective-permute-start | bytes 344072 | tf_op jit(solution)/shard_map/ppermute | solution.py:174
  44.6 7.9 %collective-permute-start.18 = (bf16[8,7168]{1,0:T(8,128)(2,1)S(1)}, bf16[8,7168]{1,0:T(8,128)(2,1)S(1)}, u32[]{:S(2)}, u32[]{:S(2)}) collective-permute-start(bf16[8,7168]{1,0:T(8,128)(2,1)S(1)} %get-tuple-element.18), channel_id=1, source_target_pairs={{0,8},{4,12},{8,0},{12,4},{1,9},{5,13},{9,1},{13,5},{2,10},{6,14},... | collective-permute-start | bytes 344072 | tf_op jit(solution)/shard_map/ppermute | solution.py:174
  46.1 9.1 %collective-permute-start.20 = (bf16[8,7168]{1,0:T(8,128)(2,1)S(1)}, bf16[8,7168]{1,0:T(8,128)(2,1)S(1)}, u32[]{:S(2)}, u32[]{:S(2)}) collective-permute-start(bf16[8,7168]{1,0:T(8,128)(2,1)S(1)} %get-tuple-element.17), channel_id=1, source_target_pairs={{0,8},{4,12},{8,0},{12,4},{1,9},{5,13},{9,1},{13,5},{2,10},{6,14},... | collective-permute-start | bytes 344072 | tf_op jit(solution)/shard_map/ppermute | solution.py:174
  52.6 4.9 %collective-permute-start.22 = (bf16[8,7168]{1,0:T(8,128)(2,1)S(1)}, bf16[8,7168]{1,0:T(8,128)(2,1)S(1)}, u32[]{:S(2)}, u32[]{:S(2)}) collective-permute-start(bf16[8,7168]{1,0:T(8,128)(2,1)S(1)} %get-tuple-element.20), channel_id=1, source_target_pairs={{0,1},{1,0},{2,3},{3,2},{4,5},{5,4},{6,7},{7,6},{8,9},{9,8},{10,11... | collective-permute-start | bytes 344072 | tf_op jit(solution)/shard_map/ppermute | solution.py:178
  52.8 5.1 %collective-permute-start.17 = (bf16[8,7168]{1,0:T(8,128)(2,1)S(1)}, bf16[8,7168]{1,0:T(8,128)(2,1)S(1)}, u32[]{:S(2)}, u32[]{:S(2)}) collective-permute-start(bf16[8,7168]{1,0:T(8,128)(2,1)S(1)} %get-tuple-element.15), channel_id=1, source_target_pairs={{0,8},{4,12},{8,0},{12,4},{1,9},{5,13},{9,1},{13,5},{2,10},{6,14},... | collective-permute-start | bytes 344072 | tf_op jit(solution)/shard_map/ppermute | solution.py:174
  53.3 5.4 %collective-permute-start.19 = (bf16[8,7168]{1,0:T(8,128)(2,1)S(1)}, bf16[8,7168]{1,0:T(8,128)(2,1)S(1)}, u32[]{:S(2)}, u32[]{:S(2)}) collective-permute-start(bf16[8,7168]{1,0:T(8,128)(2,1)S(1)} %get-tuple-element.19), channel_id=1, source_target_pairs={{0,1},{1,0},{2,3},{3,2},{4,5},{5,4},{6,7},{7,6},{8,9},{9,8},{10,11... | collective-permute-start | bytes 344072 | tf_op jit(solution)/shard_map/ppermute | solution.py:178
  57.5 6.7 %collective-permute-start.23 = (bf16[8,7168]{1,0:T(8,128)(2,1)S(1)}, bf16[8,7168]{1,0:T(8,128)(2,1)S(1)}, u32[]{:S(2)}, u32[]{:S(2)}) collective-permute-start(bf16[8,7168]{1,0:T(8,128)(2,1)S(1)} %add_convert_fusion.3), channel_id=1, source_target_pairs={{0,3},{1,2},{2,1},{3,0},{4,7},{5,6},{6,5},{7,4},{8,11},{9,10},{10,... | collective-permute-start | bytes 344072 | tf_op jit(solution)/shard_map/ppermute | solution.py:178

commit v4 on v3

v4 whole, which is shorter than its diff:
```python
import functools

import jax
import jax.numpy as jnp
from jax import lax
from jax.experimental import pallas as pl
from jax.experimental.pallas import tpu as pltpu
from jax.sharding import PartitionSpec as P

LANES = 128
N_TILE = 256
OUT_CHUNKS = 1
VMEM_LIMIT = 4 * 2**20


def pack_kernel(*refs):
    inputs, out_ref, local, sems = refs[:4], refs[-6], refs[-5:-1], refs[-1]
    copies = [
        pltpu.make_async_copy(here, there, sems.at[i])
        for i, (here, there) in enumerate(zip(inputs, local))
    ]
    for copy in copies:
        copy.start()
    for copy in copies:
        copy.wait()
    tokens_ref, ids_ref, route_ref, slot_ref = local
    rows, width = tokens_ref.shape
    experts = slot_ref.shape[0]
    row = lax.broadcasted_iota(jnp.int32, (rows, LANES), 0)
    column = lax.broadcasted_iota(jnp.int32, (rows, LANES), 1)
    slot = lax.rem(column, experts)
    weights = jnp.zeros((rows, LANES), jnp.float32)
    for k in range(ids_ref.shape[0]):
        for token in range(rows):
            named = (row == token) & (slot == slot_ref[ids_ref[k, token]])
            weights = jnp.where(named, route_ref[k, token], weights)
    first = weights.astype(jnp.bfloat16).astype(jnp.float32)
    second = (weights - first).astype(jnp.bfloat16).astype(jnp.float32)
    third = weights - first - second
    tail = jnp.where(column < experts, first, jnp.where(column < 2 * experts, second, third))
    out_ref[:, :width] = tokens_ref[...]
    out_ref[:, width:] = jnp.where(column < 3 * experts, tail, 0.0).astype(jnp.bfloat16)


def pack(tokens, expert_ids, route_weights, expert_slot, *weights):
    rows, width = tokens.shape
    inputs = (tokens, expert_ids.T, route_weights.T, expert_slot)
    held = [pltpu.with_memory_space_constraint(each, pltpu.HBM) for each in inputs + weights]
    return pl.pallas_call(
        pack_kernel,
        out_shape=jax.ShapeDtypeStruct((rows, width + LANES), jnp.bfloat16),
        in_specs=[pl.BlockSpec(memory_space=pl.ANY)] * len(held),
        out_specs=pl.BlockSpec(memory_space=pltpu.VMEM),
        scratch_shapes=[
            pltpu.VMEM(tokens.shape, tokens.dtype),
            *[pltpu.SMEM(each.shape, each.dtype) for each in inputs[1:]],
            pltpu.SemaphoreType.DMA((len(inputs),)),
        ],
        compiler_params=pltpu.CompilerParams(vmem_limit_bytes=VMEM_LIMIT),
        name="pack",
    )(*held)


def hidden_kernel(experts, *refs):
    *pieces, gate_ref, up_ref, out_ref, x_ref, weight_ref = refs
    members, width, hid = gate_ref.shape
    x_ref[...] = jnp.concatenate([piece[:, :width] for piece in pieces], axis=0)
    tail = jnp.concatenate([piece[:, width:] for piece in pieces], axis=0)
    tail = tail.astype(jnp.float32)
    column = lax.broadcasted_iota(jnp.int32, tail.shape, 1)
    for member in range(members):
        slot = lax.axis_index("node") * members + member
        mine = (lax.rem(column, experts) == slot) & (column < 3 * experts)
        weight_ref[member] = jnp.sum(jnp.where(mine, tail, 0.0), axis=1, keepdims=True)
    tiles = hid // N_TILE

    @pl.loop(0, members * tiles)
    def _(step):
        member = step // tiles
        at = pl.ds(pl.multiple_of(lax.rem(step, tiles) * N_TILE, N_TILE), N_TILE)
        gate, up = [
            jnp.dot(x_ref[...], ref[member, :, at], preferred_element_type=jnp.float32)
            for ref in (gate_ref, up_ref)
        ]
        hidden = gate / (1.0 + jnp.exp(-gate)) * up * weight_ref[member]
        to = pl.ds(pl.multiple_of(step * N_TILE, N_TILE), N_TILE)
        out_ref[:, to] = hidden.astype(jnp.bfloat16)


def hidden_units(pieces, w_gate, w_up, experts):
    members, width, hid = w_gate.shape
    rows = sum(piece.shape[0] for piece in pieces)
    vmem = pl.BlockSpec(memory_space=pltpu.VMEM)
    return pl.pallas_call(
        functools.partial(hidden_kernel, experts),
        out_shape=jax.ShapeDtypeStruct((rows, members * hid), jnp.bfloat16),
        in_specs=[vmem] * (len(pieces) + 2),
        out_specs=vmem,
        scratch_shapes=[
            pltpu.VMEM((rows, width), jnp.bfloat16),
            pltpu.VMEM((members, rows, 1), jnp.float32),
        ],
        compiler_params=pltpu.CompilerParams(vmem_limit_bytes=VMEM_LIMIT),
        cost_estimate=pl.CostEstimate(
            flops=4 * rows * members * width * hid,
            bytes_accessed=4 * members * width * hid,
            transcendentals=rows * members * hid,
        ),
        name="hidden",
    )(*pieces, w_gate, w_up)


def down_kernel(chunk, hidden_ref, down_ref, far_ref, near_ref, *keep_refs):
    members, hid, _ = down_ref.shape
    width = far_ref.shape[1]
    part = far_ref.shape[0]
    outs = (*keep_refs, near_ref, far_ref)

    @pl.loop(0, width // N_TILE)
    def _(step):
        here = pl.ds(pl.multiple_of(step * N_TILE, N_TILE), N_TILE)
        there = pl.ds(pl.multiple_of(chunk * width + step * N_TILE, N_TILE), N_TILE)
        total = jnp.dot(
            hidden_ref[...],
            down_ref[:, :, there].reshape(members * hid, N_TILE),
            preferred_element_type=jnp.float32,
        ).astype(jnp.bfloat16)
        for i, ref in enumerate(outs):
            ref[:, here] = total[i * part : (i + 1) * part]


def down(hidden, w_down, chunk, chunks):
    members, hid, width = w_down.shape
    rows = hidden.shape[0]
    vmem = pl.BlockSpec(memory_space=pltpu.VMEM)
    return pl.pallas_call(
        functools.partial(down_kernel, chunk),
        out_shape=[jax.ShapeDtypeStruct((rows // 4, width // chunks), jnp.bfloat16)] * 4,
        in_specs=[vmem, vmem],
        out_specs=[vmem] * 4,
        compiler_params=pltpu.CompilerParams(vmem_limit_bytes=VMEM_LIMIT),
        cost_estimate=pl.CostEstimate(
            flops=2 * rows * members * hid * width // chunks,
            bytes_accessed=2 * members * hid * width // chunks,
            transcendentals=0,
        ),
        name="down",
    )(hidden, w_down)


CHIPS, PLACES = 2, 4


def to_core(value):
    return lax.ppermute(value, "node", [(i, i ^ 1) for i in range(2 * CHIPS)])


def to_chip(value):
    return lax.ppermute(value, "node", [(i, i ^ 2) for i in range(2 * CHIPS)])


def to_place(value, bits):
    return lax.ppermute(value, "local", [(i, i ^ bits) for i in range(PLACES)])


def gather_blocks(own):
    third = to_place(own, 3)
    first = to_place(own, 1)
    along = [own, first, to_place(third, 1), third]
    chip = along + [to_chip(piece) for piece in along]
    return chip + [to_core(piece) for piece in chip]


def add(*terms):
    return sum(term.astype(jnp.float32) for term in terms).astype(jnp.bfloat16)


def after(value, *others):
    return lax.optimization_barrier((value, *others))[0]


def reduce_blocks(other_far, other_near, near, far, rows):
    far = add(far, to_core(other_far)).reshape(PLACES, rows, -1)
    near = add(near, to_core(other_near)).reshape(PLACES, rows, -1)
    far_second = to_place(far[2], 1)
    first = add(near[1], to_chip(far[1]))
    far_third = add(far[3], far_second)
    near_second = to_place(after(near[2], far_second), 1)
    third = add(near[3], near_second, to_chip(far_third))
    third_here = to_place(third, 3)
    own = add(near[0], to_chip(after(far[0], third)))
    return add(own, to_place(after(first, third), 1), third_here)


def by_permutes(tokens, expert_ids, route_weights, expert_slot, w_gate, w_up, w_down):
    rows = tokens.shape[0]
    own = pack(tokens, expert_ids, route_weights, expert_slot, w_gate, w_up, w_down)
    hidden = hidden_units(gather_blocks(own), w_gate, w_up, expert_slot.shape[0])
    outs = []
    for chunk in range(OUT_CHUNKS):
        outs.append(reduce_blocks(*down(hidden, w_down, chunk, OUT_CHUNKS), rows))
    return jnp.concatenate(outs, axis=1)


def by_collectives(tokens, expert_ids, route_weights, expert_slot, w_gate, w_up, w_down):
    members, width, _ = w_gate.shape
    experts = expert_slot.shape[0]
    packed = pack(tokens, expert_ids, route_weights, expert_slot)
    gathered = lax.all_gather(packed, ("node", "local"), axis=0, tiled=True)
    rows = gathered[:, :width]
    tail = gathered[:, width : width + 3 * experts].astype(jnp.float32)
    weights = tail.reshape(-1, 3, experts).sum(axis=1)
    mine = lax.dynamic_slice_in_dim(weights, lax.axis_index("node") * members, members, axis=1)
    gate = jnp.einsum("td,edh->eth", rows, w_gate, preferred_element_type=jnp.float32)
    up = jnp.einsum("td,edh->eth", rows, w_up, preferred_element_type=jnp.float32)
    hidden = (jax.nn.silu(gate) * up * mine.T[..., None]).astype(jnp.bfloat16)
    result = jnp.einsum("eth,ehd->td", hidden, w_down, preferred_element_type=jnp.float32)
    return lax.psum_scatter(
        result.astype(jnp.bfloat16), ("node", "local"), scatter_dimension=0, tiled=True
    )


def per_device(*args):
    small = (lax.axis_size("node"), lax.axis_size("local")) == (2 * CHIPS, PLACES)
    return (by_permutes if small else by_collectives)(*args)


def solution(mesh):
    rows = P(("parts", "node", "local"), None)
    in_specs = (
        rows,
        rows,
        rows,
        P(),
        P("node", None, "local"),
        P("node", None, "local"),
        P("node", "local", None),
    )
    return jax.shard_map(
        per_device, mesh=mesh, in_specs=in_specs, out_specs=rows, check_vma=False
    )
```

time: 65.1 us -> 59.7 us (0.917)
  local copies, waits for them, and re-layouts: 8.2 us -> 0.06 us
  starting transfers between devices: 18.4 us -> 23.4 us
  waiting for transfers between devices: 24.7 us -> 21.3 us
  Pallas kernels: 12.4 us -> 13.6 us
    unnamed x20 -> x12, local copies, waits for them, and re-layouts: 8.11 us -> 0.03 us
    ppermute x8 -> x7, waiting for transfers between devices: 12.1 us -> 5.66 us  [to_chip(): return lax.ppermute(value, 'node', [(i, i ^ 2) for i in range(2 * CHIPS)])]
    ppermute x6 -> x7, waiting for transfers between devices: 9.3 us -> 12.9 us  [to_place(): return lax.ppermute(value, 'local', [(i, i ^ bits) for i in range(PLACES)])]
    pallas_call x1, Pallas kernels: 4.56 us -> 7.13 us  [down(): pl.pallas_call(functools.partial(down_kernel, chunk), out_shape=[jax.Shap...]
    ppermute x6 -> x7, starting transfers between devices: 9.61 us -> 12.1 us  [to_place(): return lax.ppermute(value, 'local', [(i, i ^ bits) for i in range(PLACES)])]
    ppermute x8 -> x7, starting transfers between devices: 7.23 us -> 9.65 us  [to_chip(): return lax.ppermute(value, 'node', [(i, i ^ 2) for i in range(2 * CHIPS)])]
    pallas_call x1, Pallas kernels: 6.57 us -> 5.3 us  [hidden_units(): pl.pallas_call(functools.partial(hidden_kernel, experts), out_shape=jax.S...]
  transfers between devices with their start and end apart: 24 -> 24, of which waited for: 12 -> 14; matrix products, arithmetic and copies ran while one was open for 0% -> 0% of each run, Pallas kernels for 1% -> 0%
where the time goes in v4:
time: 59.7 us; the launch traced here: 59.5 us
  starting transfers between devices  23.4 us (39%)
  waiting for transfers between devices  21.3 us (36%)
  Pallas kernels  13.6 us (23%)
  other arithmetic  1.03 us (2%)
    ppermute x7, waiting for transfers between devices, to_place(): return lax.ppermute(value, 'local', [(i, i ^ bits) for i in range(PLACES)])  12.9 us
    ppermute x7, starting transfers between devices, to_place(): return lax.ppermute(value, 'local', [(i, i ^ bits) for i in range(PLACES)])  12.1 us
    ppermute x7, starting transfers between devices, to_chip(): return lax.ppermute(value, 'node', [(i, i ^ 2) for i in range(2 * CHIPS)])  9.65 us
    pallas_call x1, Pallas kernels, down(): pl.pallas_call(functools.partial(down_kernel, chunk), out_shape=[jax.Shap...  7.13 us
    ppermute x7, waiting for transfers between devices, to_chip(): return lax.ppermute(value, 'node', [(i, i ^ 2) for i in range(2 * CHIPS)])  5.66 us
    pallas_call x1, Pallas kernels, hidden_units(): pl.pallas_call(functools.partial(hidden_kernel, experts), out_shape=jax.S...  5.3 us
    ppermute x10, waiting for transfers between devices, to_core(): return lax.ppermute(value, 'node', [(i, i ^ 1) for i in range(2 * CHIPS)])  2.71 us
    ppermute x10, starting transfers between devices, to_core(): return lax.ppermute(value, 'node', [(i, i ^ 1) for i in range(2 * CHIPS)])  1.6 us
  transfers between devices with their start and end apart: 24, of which 14 were waited for; matrix products, arithmetic and copies ran while one was open for 0% of the time, Pallas kernels for 0%

profile of v4, /device:TPU:0, one launch (start us, length us, event | category | flops | bytes accessed | tf_op | source)
XLA Modules:
  0.0 59.5 jit_solution(7853860934460067835)
XLA Ops:
  0.0 0.0 copy-start
  0.0 0.0 copy-start.1
  0.0 1.2 %pack.1.refs_0_ = bf16[8,7296]{1,0:T(8,128)(2,1)S(1)} custom-call(bf16[8,7168]{1,0:T(8,128)(2,1)} %refs_0_.1, s32[4,8]{1,0:T(4,128)} %bitcast.4, f32[4,8]{1,0:T(4,128)} %bitcast.5, s32[8]{0:T(128)} %refs_3_.1, bf16[2,7168,512]{2,1,0:T(8,128)(2,1)} %refs_16_.1, bf16[2,7168,512]{2,1,0:T(8,128)(2,1)} %refs_17_.1, bf16[2,512,7168]{2,1,0:T(8,128)(2,1)} %down_ref.1), custom_call_target="tpu_custom_call" | custom-call | tf_op jit(solution)/shard_map/pack/pallas_call | solution.py:49
  1.2 0.0 slice-start.3
  1.2 5.1 %collective-permute-start.1 = (bf16[8,7296]{1,0:T(8,128)(2,1)S(1)}, bf16[8,7296]{1,0:T(8,128)(2,1)S(1)}, u32[]{:S(2)}, u32[]{:S(2)}) collective-permute-start(bf16[8,7296]{1,0:T(8,128)(2,1)S(1)} %pack.1.refs_0_), channel_id=1, source_target_pairs={{0,3},{1,2},{2,1},{3,0},{4,7},{5,6},{6,5},{7,4},{8,11},{9,10},{10,... | collective-permute-start | bytes 350216 | tf_op jit(solution)/shard_map/ppermute | solution.py:163
  6.3 1.5 %collective-permute-start.3 = (bf16[8,7296]{1,0:T(8,128)(2,1)S(1)}, bf16[8,7296]{1,0:T(8,128)(2,1)S(1)}, u32[]{:S(2)}, u32[]{:S(2)}) collective-permute-start(bf16[8,7296]{1,0:T(8,128)(2,1)S(1)} %pack.1.refs_0_), channel_id=1, source_target_pairs={{0,8},{4,12},{8,0},{12,4},{1,9},{5,13},{9,1},{13,5},{2,10},{6,14},... | collective-permute-start | bytes 350216 | tf_op jit(solution)/shard_map/ppermute | solution.py:159
  7.8 0.0 collective-permute-start.7
  7.8 0.0 collective-permute-start
  7.8 1.8 %collective-permute-done.1.refs_3_ = bf16[8,7296]{1,0:T(8,128)(2,1)S(1)} collective-permute-done((bf16[8,7296]{1,0:T(8,128)(2,1)S(1)}, bf16[8,7296]{1,0:T(8,128)(2,1)S(1)}, u32[]{:S(2)}, u32[]{:S(2)}) %collective-permute-start.1) | collective-permute-done | bytes 116768 | tf_op jit(solution)/shard_map/ppermute | solution.py:163
  9.6 2.1 %collective-permute-start.2 = (bf16[8,7296]{1,0:T(8,128)(2,1)S(1)}, bf16[8,7296]{1,0:T(8,128)(2,1)S(1)}, u32[]{:S(2)}, u32[]{:S(2)}) collective-permute-start(bf16[8,7296]{1,0:T(8,128)(2,1)S(1)} %collective-permute-done.1.refs_3_), channel_id=1, source_target_pairs={{0,1},{1,0},{2,3},{3,2},{4,5},{5,4},{6,7},{7,6},{8,9},{9,8},{10,11... | collective-permute-start | bytes 350216 | tf_op jit(solution)/shard_map/ppermute | solution.py:163
  11.7 0.0 collective-permute-done.3.refs_4_
  11.7 0.0 collective-permute-start.11
  11.7 0.5 collective-permute-start.10
  12.3 0.0 collective-permute-done.7.refs_8_
  12.3 1.5 %collective-permute-start.6 = (bf16[8,7296]{1,0:T(8,128)(2,1)S(1)}, bf16[8,7296]{1,0:T(8,128)(2,1)S(1)}, u32[]{:S(2)}, u32[]{:S(2)}) collective-permute-start(bf16[8,7296]{1,0:T(8,128)(2,1)S(1)} %collective-permute-done.1.refs_3_), channel_id=1, source_target_pairs={{0,8},{4,12},{8,0},{12,4},{1,9},{5,13},{9,1},{13,5},{2,10},{6,14},... | collective-permute-start | bytes 350216 | tf_op jit(solution)/shard_map/ppermute | solution.py:159
  13.7 0.1 collective-permute-done.refs_1_
  13.8 0.6 %collective-permute-start.4 = (bf16[8,7296]{1,0:T(8,128)(2,1)S(1)}, bf16[8,7296]{1,0:T(8,128)(2,1)S(1)}, u32[]{:S(2)}, u32[]{:S(2)}) collective-permute-start(bf16[8,7296]{1,0:T(8,128)(2,1)S(1)} %collective-permute-done.refs_1_), channel_id=1, source_target_pairs={{0,8},{4,12},{8,0},{12,4},{1,9},{5,13},{9,1},{13,5},{2,10},{6,14},... | collective-permute-start | bytes 350216 | tf_op jit(solution)/shard_map/ppermute | solution.py:159
  14.4 1.5 %collective-permute-done.2.refs_2_ = bf16[8,7296]{1,0:T(8,128)(2,1)S(1)} collective-permute-done((bf16[8,7296]{1,0:T(8,128)(2,1)S(1)}, bf16[8,7296]{1,0:T(8,128)(2,1)S(1)}, u32[]{:S(2)}, u32[]{:S(2)}) %collective-permute-start.2) | collective-permute-done | bytes 116768 | tf_op jit(solution)/shard_map/ppermute | solution.py:163
  15.9 0.7 %collective-permute-start.5 = (bf16[8,7296]{1,0:T(8,128)(2,1)S(1)}, bf16[8,7296]{1,0:T(8,128)(2,1)S(1)}, u32[]{:S(2)}, u32[]{:S(2)}) collective-permute-start(bf16[8,7296]{1,0:T(8,128)(2,1)S(1)} %collective-permute-done.2.refs_2_), channel_id=1, source_target_pairs={{0,8},{4,12},{8,0},{12,4},{1,9},{5,13},{9,1},{13,5},{2,10},{6,14},... | collective-permute-start | bytes 350216 | tf_op jit(solution)/shard_map/ppermute | solution.py:159
  16.6 0.0 collective-permute-done.11.refs_12_
  16.6 0.0 collective-permute-start.8
  16.6 0.0 collective-permute-done.10.refs_11_
  16.7 0.5 collective-permute-start.9
  17.2 1.2 %collective-permute-done.6.refs_7_ = bf16[8,7296]{1,0:T(8,128)(2,1)S(1)} collective-permute-done((bf16[8,7296]{1,0:T(8,128)(2,1)S(1)}, bf16[8,7296]{1,0:T(8,128)(2,1)S(1)}, u32[]{:S(2)}, u32[]{:S(2)}) %collective-permute-start.6) | collective-permute-done | bytes 116768 | tf_op jit(solution)/shard_map/ppermute | solution.py:159
  18.3 0.0 collective-permute-start.14
  18.3 2.5 %collective-permute-done.4.refs_5_ = bf16[8,7296]{1,0:T(8,128)(2,1)S(1)} collective-permute-done((bf16[8,7296]{1,0:T(8,128)(2,1)S(1)}, bf16[8,7296]{1,0:T(8,128)(2,1)S(1)}, u32[]{:S(2)}, u32[]{:S(2)}) %collective-permute-start.4) | collective-permute-done | bytes 116768 | tf_op jit(solution)/shard_map/ppermute | solution.py:159
  20.8 0.0 collective-permute-start.12
  20.8 1.5 %collective-permute-done.5.refs_6_ = bf16[8,7296]{1,0:T(8,128)(2,1)S(1)} collective-permute-done((bf16[8,7296]{1,0:T(8,128)(2,1)S(1)}, bf16[8,7296]{1,0:T(8,128)(2,1)S(1)}, u32[]{:S(2)}, u32[]{:S(2)}) %collective-permute-start.5) | collective-permute-done | bytes 116768 | tf_op jit(solution)/shard_map/ppermute | solution.py:159
  22.4 0.0 collective-permute-start.13
  22.4 0.0 collective-permute-done.8.refs_9_
  22.4 0.0 collective-permute-done.14.refs_15_
  22.4 0.0 collective-permute-done.9.refs_10_
  22.4 0.0 collective-permute-done.12.refs_13_
  22.4 1.3 %collective-permute-done.13.refs_14_ = bf16[8,7296]{1,0:T(8,128)(2,1)S(1)} collective-permute-done((bf16[8,7296]{1,0:T(8,128)(2,1)S(1)}, bf16[8,7296]{1,0:T(8,128)(2,1)S(1)}, u32[]{:S(2)}, u32[]{:S(2)}) %collective-permute-start.13) | collective-permute-done | bytes 116768 | tf_op jit(solution)/shard_map/ppermute | solution.py:155
  23.7 0.0 copy-done
  23.7 0.0 copy-done.1
  23.7 5.3 %hidden.1.hidden_ref = bf16[128,1024]{1,0:T(8,128)(2,1)S(1)} custom-call(bf16[8,7296]{1,0:T(8,128)(2,1)S(1)} %pack.1.refs_0_, bf16[8,7296]{1,0:T(8,128)(2,1)S(1)} %collective-permute-done.refs_1_, bf16[8,7296]{1,0:T(8,128)(2,1)S(1)} %collective-permute-done.2.refs_2_, bf16[8,7296]{1,0:T(8,128)(2,1)S(1)} %collective-permute-done.1.refs_3_, ...), custom_call_target="tpu_custom_call" | custom-call | flops 3758096384 | bytes 29360128 | tf_op jit(solution)/shard_map/hidden/pallas_call | solution.py:94
  29.0 0.0 slice-done
  29.0 0.0 slice-done.1
  29.0 0.0 slice-done.2
  29.0 0.0 slice-done.3
  29.0 7.1 %down.1 = (bf16[32,7168]{1,0:T(8,128)(2,1)S(1)}, bf16[32,7168]{1,0:T(8,128)(2,1)S(1)}, bf16[32,7168]{1,0:T(8,128)(2,1)S(1)}, bf16[32,7168]{1,0:T(8,128)(2,1)S(1)}) custom-call(bf16[128,1024]{1,0:T(8,128)(2,1)S(1)} %hidden.1.hidden_ref, bf16[2,512,7168]{2,1,0:T(8,128)(2,1)S(1)} %bitcast.3), custom_call_target="tpu_custom_call" | custom-call | flops 1879048192 | bytes 14680064 | tf_op jit(solution)/shard_map/down/pallas_call | solution.py:136
  36.2 0.2 collective-permute-start.16
  36.4 0.4 collective-permute-start.15
  36.8 1.3 %collective-permute-done.16 = bf16[32,7168]{1,0:T(8,128)(2,1)S(1)} collective-permute-done((bf16[32,7168]{1,0:T(8,128)(2,1)S(1)}, bf16[32,7168]{1,0:T(8,128)(2,1)S(1)}, u32[]{:S(2)}, u32[]{:S(2)}) %collective-permute-start.16) | collective-permute-done | bytes 458784 | tf_op jit(solution)/shard_map/ppermute | solution.py:155
  38.1 0.1 add_convert_fusion
  38.2 0.4 collective-permute-start.17
  38.6 0.1 collective-permute-done.15
  38.7 0.1 add_convert_fusion.1
  38.9 1.7 %collective-permute-start.21 = (bf16[8,7168]{1,0:T(8,128)(2,1)S(1)}, bf16[8,7168]{1,0:T(8,128)(2,1)S(1)}, u32[]{:S(2)}, u32[]{:S(2)}) collective-permute-start(bf16[8,7168]{1,0:T(8,128)(2,1)S(1)} %get-tuple-element.20), channel_id=1, source_target_pairs={{0,8},{4,12},{8,0},{12,4},{1,9},{5,13},{9,1},{13,5},{2,10},{6,14},... | collective-permute-start | bytes 344072 | tf_op jit(solution)/shard_map/ppermute | solution.py:159
  40.6 2.9 %collective-permute-done.17 = bf16[8,7168]{1,0:T(8,128)(2,1)S(1)} collective-permute-done((bf16[8,7168]{1,0:T(8,128)(2,1)S(1)}, bf16[8,7168]{1,0:T(8,128)(2,1)S(1)}, u32[]{:S(2)}, u32[]{:S(2)}) %collective-permute-start.17) | collective-permute-done | bytes 114720 | tf_op jit(solution)/shard_map/ppermute | solution.py:163
  43.5 0.4 collective-permute-start.18
  43.9 1.8 %collective-permute-start.19 = (bf16[8,7168]{1,0:T(8,128)(2,1)S(1)}, bf16[8,7168]{1,0:T(8,128)(2,1)S(1)}, u32[]{:S(2)}, u32[]{:S(2)}) collective-permute-start(bf16[8,7168]{1,0:T(8,128)(2,1)S(1)} %add_convert_fusion.6), channel_id=1, source_target_pairs={{0,8},{4,12},{8,0},{12,4},{1,9},{5,13},{9,1},{13,5},{2,10},{6,14},... | collective-permute-start | bytes 344072 | tf_op jit(solution)/shard_map/ppermute | solution.py:159
  45.7 0.0 collective-permute-done.21
  45.7 2.6 %collective-permute-done.18 = bf16[8,7168]{1,0:T(8,128)(2,1)S(1)} collective-permute-done((bf16[8,7168]{1,0:T(8,128)(2,1)S(1)}, bf16[8,7168]{1,0:T(8,128)(2,1)S(1)}, u32[]{:S(2)}, u32[]{:S(2)}) %collective-permute-start.18) | collective-permute-done | bytes 114720 | tf_op jit(solution)/shard_map/ppermute | solution.py:163
  48.3 0.5 collective-permute-done.19
  48.7 0.1 add_convert_fusion.3
  48.8 1.8 %collective-permute-start.20 = (bf16[8,7168]{1,0:T(8,128)(2,1)S(1)}, bf16[8,7168]{1,0:T(8,128)(2,1)S(1)}, u32[]{:S(2)}, u32[]{:S(2)}) collective-permute-start(bf16[8,7168]{1,0:T(8,128)(2,1)S(1)} %get-tuple-element.17), channel_id=1, source_target_pairs={{0,8},{4,12},{8,0},{12,4},{1,9},{5,13},{9,1},{13,5},{2,10},{6,14},... | collective-permute-start | bytes 344072 | tf_op jit(solution)/shard_map/ppermute | solution.py:159
  50.6 1.4 %collective-permute-start.22 = (bf16[8,7168]{1,0:T(8,128)(2,1)S(1)}, bf16[8,7168]{1,0:T(8,128)(2,1)S(1)}, u32[]{:S(2)}, u32[]{:S(2)}) collective-permute-start(bf16[8,7168]{1,0:T(8,128)(2,1)S(1)} %get-tuple-element.18), channel_id=1, source_target_pairs={{0,1},{1,0},{2,3},{3,2},{4,5},{5,4},{6,7},{7,6},{8,9},{9,8},{10,11... | collective-permute-start | bytes 344072 | tf_op jit(solution)/shard_map/ppermute | solution.py:163
  52.0 2.7 %collective-permute-start.23 = (bf16[8,7168]{1,0:T(8,128)(2,1)S(1)}, bf16[8,7168]{1,0:T(8,128)(2,1)S(1)}, u32[]{:S(2)}, u32[]{:S(2)}) collective-permute-start(bf16[8,7168]{1,0:T(8,128)(2,1)S(1)} %get-tuple-element.23), channel_id=1, source_target_pairs={{0,3},{1,2},{2,1},{3,0},{4,7},{5,6},{6,5},{7,4},{8,11},{9,10},{10,... | collective-permute-start | bytes 344072 | tf_op jit(solution)/shard_map/ppermute | solution.py:163
  54.7 0.0 collective-permute-done.20
  54.7 1.9 %collective-permute-done.22 = bf16[8,7168]{1,0:T(8,128)(2,1)S(1)} collective-permute-done((bf16[8,7168]{1,0:T(8,128)(2,1)S(1)}, bf16[8,7168]{1,0:T(8,128)(2,1)S(1)}, u32[]{:S(2)}, u32[]{:S(2)}) %collective-permute-start.22) | collective-permute-done | bytes 114720 | tf_op jit(solution)/shard_map/ppermute | solution.py:163
  56.6 2.2 %collective-permute-done.23 = bf16[8,7168]{1,0:T(8,128)(2,1)S(1)} collective-permute-done((bf16[8,7168]{1,0:T(8,128)(2,1)S(1)}, bf16[8,7168]{1,0:T(8,128)(2,1)S(1)}, u32[]{:S(2)}, u32[]{:S(2)}) %collective-permute-start.23) | collective-permute-done | bytes 114720 | tf_op jit(solution)/shard_map/ppermute | solution.py:163
  58.8 0.7 %add_convert_fusion.2 = bf16[8,7168]{1,0:T(8,128)(2,1)} fusion(bf16[8,7168]{1,0:T(8,128)(2,1)S(1)} %collective-permute-done.23, bf16[8,7168]{1,0:T(8,128)(2,1)S(1)} %collective-permute-done.22, bf16[8,7168]{1,0:T(8,128)(2,1)S(1)} %collective-permute-done.20, bf16[32,7168]{1,0:T(8,128)(2,1)S(1)} %add_convert_fusion.1), kind=kLoop, calls=%fused_computation.2 | loop fusion | flops 573440 | bytes 573440 | tf_op jit(solution)/shard_map/convert_element_type | solution.py:175
  (7 shorter events, 0.1 us)
Async XLA Ops:
  0.0 23.7 %copy-start = (bf16[2,7168,512]{2,1,0:T(8,128)(2,1)S(1)}, bf16[2,7168,512]{2,1,0:T(8,128)(2,1)}, u32[]{:S(2)}) copy-start(bf16[2,7168,512]{2,1,0:T(8,128)(2,1)} %refs_16_.1) | copy-start | bytes 44040196
  0.0 23.7 %copy-start.1 = (bf16[2,7168,512]{2,1,0:T(8,128)(2,1)S(1)}, bf16[2,7168,512]{2,1,0:T(8,128)(2,1)}, u32[]{:S(2)}) copy-start(bf16[2,7168,512]{2,1,0:T(8,128)(2,1)} %refs_17_.1) | copy-start | bytes 44040196
  0.0 29.0 %slice-start = ((s8[14680064]{0:T(1024)(128)(4,1)}), s8[4194304]{0:T(1024)(128)(4,1)S(1)}, s32[]{:S(2)}) async-start(s8[14680064]{0:T(1024)(128)(4,1)} %bitcast.2), calls=%async_computation | async-start | bytes 8388608
  0.0 29.0 %slice-start.1 = ((s8[14680064]{0:T(1024)(128)(4,1)}), s8[4194304]{0:T(1024)(128)(4,1)S(1)}, s32[]{:S(2)}) async-start(s8[14680064]{0:T(1024)(128)(4,1)} %bitcast.2), calls=%async_computation.1 | async-start | bytes 8388608
  0.0 29.0 %slice-start.2 = ((s8[14680064]{0:T(1024)(128)(4,1)}), s8[4194304]{0:T(1024)(128)(4,1)S(1)}, s32[]{:S(2)}) async-start(s8[14680064]{0:T(1024)(128)(4,1)} %bitcast.2), calls=%async_computation.2 | async-start | bytes 8388608
  1.2 27.8 %slice-start.3 = ((s8[14680064]{0:T(1024)(128)(4,1)}), s8[2097152]{0:T(1024)(128)(4,1)S(1)}, s32[]{:S(2)}) async-start(s8[14680064]{0:T(1024)(128)(4,1)} %bitcast.2), calls=%async_computation.3 | async-start | bytes 4194304
  1.2 8.4 %collective-permute-start.1 = (bf16[8,7296]{1,0:T(8,128)(2,1)S(1)}, bf16[8,7296]{1,0:T(8,128)(2,1)S(1)}, u32[]{:S(2)}, u32[]{:S(2)}) collective-permute-start(bf16[8,7296]{1,0:T(8,128)(2,1)S(1)} %pack.1.refs_0_), channel_id=1, source_target_pairs={{0,3},{1,2},{2,1},{3,0},{4,7},{5,6},{6,5},{7,4},{8,11},{9,10},{10,... | collective-permute-start | bytes 350216 | tf_op jit(solution)/shard_map/ppermute | solution.py:163
  6.3 5.4 %collective-permute-start.3 = (bf16[8,7296]{1,0:T(8,128)(2,1)S(1)}, bf16[8,7296]{1,0:T(8,128)(2,1)S(1)}, u32[]{:S(2)}, u32[]{:S(2)}) collective-permute-start(bf16[8,7296]{1,0:T(8,128)(2,1)S(1)} %pack.1.refs_0_), channel_id=1, source_target_pairs={{0,8},{4,12},{8,0},{12,4},{1,9},{5,13},{9,1},{13,5},{2,10},{6,14},... | collective-permute-start | bytes 350216 | tf_op jit(solution)/shard_map/ppermute | solution.py:159
  7.8 4.4 %collective-permute-start.7 = (bf16[8,7296]{1,0:T(8,128)(2,1)S(1)}, bf16[8,7296]{1,0:T(8,128)(2,1)S(1)}, u32[]{:S(2)}, u32[]{:S(2)}) collective-permute-start(bf16[8,7296]{1,0:T(8,128)(2,1)S(1)} %pack.1.refs_0_), channel_id=1, source_target_pairs={{0,4},{4,0},{8,12},{12,8},{1,5},{5,1},{9,13},{13,9},{2,6},{6,2},{1... | collective-permute-start | bytes 350216 | tf_op jit(solution)/shard_map/ppermute | solution.py:155
  7.8 6.0 %collective-permute-start = (bf16[8,7296]{1,0:T(8,128)(2,1)S(1)}, bf16[8,7296]{1,0:T(8,128)(2,1)S(1)}, u32[]{:S(2)}, u32[]{:S(2)}) collective-permute-start(bf16[8,7296]{1,0:T(8,128)(2,1)S(1)} %pack.1.refs_0_), channel_id=1, source_target_pairs={{0,1},{1,0},{2,3},{3,2},{4,5},{5,4},{6,7},{7,6},{8,9},{9,8},{10,11... | collective-permute-start | bytes 350216 | tf_op jit(solution)/shard_map/ppermute | solution.py:163
  9.6 6.3 %collective-permute-start.2 = (bf16[8,7296]{1,0:T(8,128)(2,1)S(1)}, bf16[8,7296]{1,0:T(8,128)(2,1)S(1)}, u32[]{:S(2)}, u32[]{:S(2)}) collective-permute-start(bf16[8,7296]{1,0:T(8,128)(2,1)S(1)} %collective-permute-done.1.refs_3_), channel_id=1, source_target_pairs={{0,1},{1,0},{2,3},{3,2},{4,5},{5,4},{6,7},{7,6},{8,9},{9,8},{10,11... | collective-permute-start | bytes 350216 | tf_op jit(solution)/shard_map/ppermute | solution.py:163
  11.7 4.9 %collective-permute-start.11 = (bf16[8,7296]{1,0:T(8,128)(2,1)S(1)}, bf16[8,7296]{1,0:T(8,128)(2,1)S(1)}, u32[]{:S(2)}, u32[]{:S(2)}) collective-permute-start(bf16[8,7296]{1,0:T(8,128)(2,1)S(1)} %collective-permute-done.3.refs_4_), channel_id=1, source_target_pairs={{0,4},{4,0},{8,12},{12,8},{1,5},{5,1},{9,13},{13,9},{2,6},{6,2},{1... | collective-permute-start | bytes 350216 | tf_op jit(solution)/shard_map/ppermute | solution.py:155
  11.7 4.9 %collective-permute-start.10 = (bf16[8,7296]{1,0:T(8,128)(2,1)S(1)}, bf16[8,7296]{1,0:T(8,128)(2,1)S(1)}, u32[]{:S(2)}, u32[]{:S(2)}) collective-permute-start(bf16[8,7296]{1,0:T(8,128)(2,1)S(1)} %collective-permute-done.1.refs_3_), channel_id=1, source_target_pairs={{0,4},{4,0},{8,12},{12,8},{1,5},{5,1},{9,13},{13,9},{2,6},{6,2},{1... | collective-permute-start | bytes 350216 | tf_op jit(solution)/shard_map/ppermute | solution.py:155
  12.3 6.1 %collective-permute-start.6 = (bf16[8,7296]{1,0:T(8,128)(2,1)S(1)}, bf16[8,7296]{1,0:T(8,128)(2,1)S(1)}, u32[]{:S(2)}, u32[]{:S(2)}) collective-permute-start(bf16[8,7296]{1,0:T(8,128)(2,1)S(1)} %collective-permute-done.1.refs_3_), channel_id=1, source_target_pairs={{0,8},{4,12},{8,0},{12,4},{1,9},{5,13},{9,1},{13,5},{2,10},{6,14},... | collective-permute-start | bytes 350216 | tf_op jit(solution)/shard_map/ppermute | solution.py:159
  13.8 7.0 %collective-permute-start.4 = (bf16[8,7296]{1,0:T(8,128)(2,1)S(1)}, bf16[8,7296]{1,0:T(8,128)(2,1)S(1)}, u32[]{:S(2)}, u32[]{:S(2)}) collective-permute-start(bf16[8,7296]{1,0:T(8,128)(2,1)S(1)} %collective-permute-done.refs_1_), channel_id=1, source_target_pairs={{0,8},{4,12},{8,0},{12,4},{1,9},{5,13},{9,1},{13,5},{2,10},{6,14},... | collective-permute-start | bytes 350216 | tf_op jit(solution)/shard_map/ppermute | solution.py:159
  15.9 6.4 %collective-permute-start.5 = (bf16[8,7296]{1,0:T(8,128)(2,1)S(1)}, bf16[8,7296]{1,0:T(8,128)(2,1)S(1)}, u32[]{:S(2)}, u32[]{:S(2)}) collective-permute-start(bf16[8,7296]{1,0:T(8,128)(2,1)S(1)} %collective-permute-done.2.refs_2_), channel_id=1, source_target_pairs={{0,8},{4,12},{8,0},{12,4},{1,9},{5,13},{9,1},{13,5},{2,10},{6,14},... | collective-permute-start | bytes 350216 | tf_op jit(solution)/shard_map/ppermute | solution.py:159
  16.6 5.7 %collective-permute-start.8 = (bf16[8,7296]{1,0:T(8,128)(2,1)S(1)}, bf16[8,7296]{1,0:T(8,128)(2,1)S(1)}, u32[]{:S(2)}, u32[]{:S(2)}) collective-permute-start(bf16[8,7296]{1,0:T(8,128)(2,1)S(1)} %collective-permute-done.refs_1_), channel_id=1, source_target_pairs={{0,4},{4,0},{8,12},{12,8},{1,5},{5,1},{9,13},{13,9},{2,6},{6,2},{1... | collective-permute-start | bytes 350216 | tf_op jit(solution)/shard_map/ppermute | solution.py:155
  16.7 5.7 %collective-permute-start.9 = (bf16[8,7296]{1,0:T(8,128)(2,1)S(1)}, bf16[8,7296]{1,0:T(8,128)(2,1)S(1)}, u32[]{:S(2)}, u32[]{:S(2)}) collective-permute-start(bf16[8,7296]{1,0:T(8,128)(2,1)S(1)} %collective-permute-done.2.refs_2_), channel_id=1, source_target_pairs={{0,4},{4,0},{8,12},{12,8},{1,5},{5,1},{9,13},{13,9},{2,6},{6,2},{1... | collective-permute-start | bytes 350216 | tf_op jit(solution)/shard_map/ppermute | solution.py:155
  18.3 4.1 %collective-permute-start.14 = (bf16[8,7296]{1,0:T(8,128)(2,1)S(1)}, bf16[8,7296]{1,0:T(8,128)(2,1)S(1)}, u32[]{:S(2)}, u32[]{:S(2)}) collective-permute-start(bf16[8,7296]{1,0:T(8,128)(2,1)S(1)} %collective-permute-done.6.refs_7_), channel_id=1, source_target_pairs={{0,4},{4,0},{8,12},{12,8},{1,5},{5,1},{9,13},{13,9},{2,6},{6,2},{1... | collective-permute-start | bytes 350216 | tf_op jit(solution)/shard_map/ppermute | solution.py:155
  20.8 1.6 %collective-permute-start.12 = (bf16[8,7296]{1,0:T(8,128)(2,1)S(1)}, bf16[8,7296]{1,0:T(8,128)(2,1)S(1)}, u32[]{:S(2)}, u32[]{:S(2)}) collective-permute-start(bf16[8,7296]{1,0:T(8,128)(2,1)S(1)} %collective-permute-done.4.refs_5_), channel_id=1, source_target_pairs={{0,4},{4,0},{8,12},{12,8},{1,5},{5,1},{9,13},{13,9},{2,6},{6,2},{1... | collective-permute-start | bytes 350216 | tf_op jit(solution)/shard_map/ppermute | solution.py:155
  22.4 1.3 %collective-permute-start.13 = (bf16[8,7296]{1,0:T(8,128)(2,1)S(1)}, bf16[8,7296]{1,0:T(8,128)(2,1)S(1)}, u32[]{:S(2)}, u32[]{:S(2)}) collective-permute-start(bf16[8,7296]{1,0:T(8,128)(2,1)S(1)} %collective-permute-done.5.refs_6_), channel_id=1, source_target_pairs={{0,4},{4,0},{8,12},{12,8},{1,5},{5,1},{9,13},{13,9},{2,6},{6,2},{1... | collective-permute-start | bytes 350216 | tf_op jit(solution)/shard_map/ppermute | solution.py:155
  36.2 1.9 %collective-permute-start.16 = (bf16[32,7168]{1,0:T(8,128)(2,1)S(1)}, bf16[32,7168]{1,0:T(8,128)(2,1)S(1)}, u32[]{:S(2)}, u32[]{:S(2)}) collective-permute-start(bf16[32,7168]{1,0:T(8,128)(2,1)S(1)} %get-tuple-element.15), channel_id=1, source_target_pairs={{0,4},{4,0},{8,12},{12,8},{1,5},{5,1},{9,13},{13,9},{2,6},{6,2},{1... | collective-permute-start | bytes 1376264 | tf_op jit(solution)/shard_map/ppermute | solution.py:155
  36.4 2.3 %collective-permute-start.15 = (bf16[32,7168]{1,0:T(8,128)(2,1)S(1)}, bf16[32,7168]{1,0:T(8,128)(2,1)S(1)}, u32[]{:S(2)}, u32[]{:S(2)}) collective-permute-start(bf16[32,7168]{1,0:T(8,128)(2,1)S(1)} %get-tuple-element.13), channel_id=1, source_target_pairs={{0,4},{4,0},{8,12},{12,8},{1,5},{5,1},{9,13},{13,9},{2,6},{6,2},{1... | collective-permute-start | bytes 1376264 | tf_op jit(solution)/shard_map/ppermute | solution.py:155
  38.2 5.3 %collective-permute-start.17 = (bf16[8,7168]{1,0:T(8,128)(2,1)S(1)}, bf16[8,7168]{1,0:T(8,128)(2,1)S(1)}, u32[]{:S(2)}, u32[]{:S(2)}) collective-permute-start(bf16[8,7168]{1,0:T(8,128)(2,1)S(1)} %get-tuple-element.21), channel_id=1, source_target_pairs={{0,1},{1,0},{2,3},{3,2},{4,5},{5,4},{6,7},{7,6},{8,9},{9,8},{10,11... | collective-permute-start | bytes 344072 | tf_op jit(solution)/shard_map/ppermute | solution.py:163
  38.9 6.8 %collective-permute-start.21 = (bf16[8,7168]{1,0:T(8,128)(2,1)S(1)}, bf16[8,7168]{1,0:T(8,128)(2,1)S(1)}, u32[]{:S(2)}, u32[]{:S(2)}) collective-permute-start(bf16[8,7168]{1,0:T(8,128)(2,1)S(1)} %get-tuple-element.20), channel_id=1, source_target_pairs={{0,8},{4,12},{8,0},{12,4},{1,9},{5,13},{9,1},{13,5},{2,10},{6,14},... | collective-permute-start | bytes 344072 | tf_op jit(solution)/shard_map/ppermute | solution.py:159
  43.5 4.8 %collective-permute-start.18 = (bf16[8,7168]{1,0:T(8,128)(2,1)S(1)}, bf16[8,7168]{1,0:T(8,128)(2,1)S(1)}, u32[]{:S(2)}, u32[]{:S(2)}) collective-permute-start(bf16[8,7168]{1,0:T(8,128)(2,1)S(1)} %slice.43), channel_id=1, source_target_pairs={{0,1},{1,0},{2,3},{3,2},{4,5},{5,4},{6,7},{7,6},{8,9},{9,8},{10,11... | collective-permute-start | bytes 344072 | tf_op jit(solution)/shard_map/ppermute | solution.py:163
  43.9 4.9 %collective-permute-start.19 = (bf16[8,7168]{1,0:T(8,128)(2,1)S(1)}, bf16[8,7168]{1,0:T(8,128)(2,1)S(1)}, u32[]{:S(2)}, u32[]{:S(2)}) collective-permute-start(bf16[8,7168]{1,0:T(8,128)(2,1)S(1)} %add_convert_fusion.6), channel_id=1, source_target_pairs={{0,8},{4,12},{8,0},{12,4},{1,9},{5,13},{9,1},{13,5},{2,10},{6,14},... | collective-permute-start | bytes 344072 | tf_op jit(solution)/shard_map/ppermute | solution.py:159
  48.8 5.9 %collective-permute-start.20 = (bf16[8,7168]{1,0:T(8,128)(2,1)S(1)}, bf16[8,7168]{1,0:T(8,128)(2,1)S(1)}, u32[]{:S(2)}, u32[]{:S(2)}) collective-permute-start(bf16[8,7168]{1,0:T(8,128)(2,1)S(1)} %get-tuple-element.17), channel_id=1, source_target_pairs={{0,8},{4,12},{8,0},{12,4},{1,9},{5,13},{9,1},{13,5},{2,10},{6,14},... | collective-permute-start | bytes 344072 | tf_op jit(solution)/shard_map/ppermute | solution.py:159
  50.6 6.0 %collective-permute-start.22 = (bf16[8,7168]{1,0:T(8,128)(2,1)S(1)}, bf16[8,7168]{1,0:T(8,128)(2,1)S(1)}, u32[]{:S(2)}, u32[]{:S(2)}) collective-permute-start(bf16[8,7168]{1,0:T(8,128)(2,1)S(1)} %get-tuple-element.18), channel_id=1, source_target_pairs={{0,1},{1,0},{2,3},{3,2},{4,5},{5,4},{6,7},{7,6},{8,9},{9,8},{10,11... | collective-permute-start | bytes 344072 | tf_op jit(solution)/shard_map/ppermute | solution.py:163
  52.0 6.8 %collective-permute-start.23 = (bf16[8,7168]{1,0:T(8,128)(2,1)S(1)}, bf16[8,7168]{1,0:T(8,128)(2,1)S(1)}, u32[]{:S(2)}, u32[]{:S(2)}) collective-permute-start(bf16[8,7168]{1,0:T(8,128)(2,1)S(1)} %get-tuple-element.23), channel_id=1, source_target_pairs={{0,3},{1,2},{2,1},{3,0},{4,7},{5,6},{6,5},{7,4},{8,11},{9,10},{10,... | collective-permute-start | bytes 344072 | tf_op jit(solution)/shard_map/ppermute | solution.py:163

commit v5 on v4

--- a/solution.py
+++ b/solution.py
@@ -9,6 +9,7 @@
 
 LANES = 128
 N_TILE = 256
+DOWN_TILE = 1792
 OUT_CHUNKS = 1
 VMEM_LIMIT = 4 * 2**20
 
@@ -111,26 +112,22 @@
 
 
 def down_kernel(chunk, hidden_ref, down_ref, far_ref, near_ref, *keep_refs):
-    members, hid, _ = down_ref.shape
-    width = far_ref.shape[1]
-    part = far_ref.shape[0]
+    part, width = far_ref.shape
     outs = (*keep_refs, near_ref, far_ref)
 
-    @pl.loop(0, width // N_TILE)
+    @pl.loop(0, width // DOWN_TILE)
     def _(step):
-        here = pl.ds(pl.multiple_of(step * N_TILE, N_TILE), N_TILE)
-        there = pl.ds(pl.multiple_of(chunk * width + step * N_TILE, N_TILE), N_TILE)
+        here = pl.ds(pl.multiple_of(step * DOWN_TILE, DOWN_TILE), DOWN_TILE)
+        there = pl.ds(pl.multiple_of(chunk * width + step * DOWN_TILE, DOWN_TILE), DOWN_TILE)
         total = jnp.dot(
-            hidden_ref[...],
-            down_ref[:, :, there].reshape(members * hid, N_TILE),
-            preferred_element_type=jnp.float32,
+            hidden_ref[...], down_ref[:, there], preferred_element_type=jnp.float32
         ).astype(jnp.bfloat16)
         for i, ref in enumerate(outs):
             ref[:, here] = total[i * part : (i + 1) * part]
 
 
 def down(hidden, w_down, chunk, chunks):
-    members, hid, width = w_down.shape
+    units, width = w_down.shape
     rows = hidden.shape[0]
     vmem = pl.BlockSpec(memory_space=pltpu.VMEM)
     return pl.pallas_call(
@@ -140,8 +137,8 @@
         out_specs=[vmem] * 4,
         compiler_params=pltpu.CompilerParams(vmem_limit_bytes=VMEM_LIMIT),
         cost_estimate=pl.CostEstimate(
-            flops=2 * rows * members * hid * width // chunks,
-            bytes_accessed=2 * members * hid * width // chunks,
+            flops=2 * rows * units * width // chunks,
+            bytes_accessed=2 * units * width // chunks,
             transcendentals=0,
         ),
         name="down",
@@ -163,12 +160,10 @@
     return lax.ppermute(value, "local", [(i, i ^ bits) for i in range(PLACES)])
 
 
-def gather_blocks(own):
-    third = to_place(own, 3)
-    first = to_place(own, 1)
-    along = [own, first, to_place(third, 1), third]
-    chip = along + [to_chip(piece) for piece in along]
-    return chip + [to_core(piece) for piece in chip]
+def to_both(value, bits):
+    count = 2 * CHIPS * PLACES
+    perm = [(i, i ^ (2 * PLACES + bits)) for i in range(count)]
+    return lax.ppermute(value, ("node", "local"), perm)
 
 
 def add(*terms):
@@ -177,28 +172,37 @@
 
 def after(value, *others):
     return lax.optimization_barrier((value, *others))[0]
+
+
+def gather_blocks(own):
+    second = to_place(own, 2)
+    first = to_place(own, 1)
+    far_own = to_chip(own)
+    far_second, far_third, third = to_chip(second), to_both(second, 1), to_place(second, 1)
+    far_first = to_chip(after(first, second))
+    chip = [own, first, second, third, far_own, far_first, far_second, far_third]
+    ready = [own, first, after(second, third), third, *chip[PLACES:]]
+    return chip + [to_core(piece) for piece in ready]
 
 
 def reduce_blocks(other_far, other_near, near, far, rows):
     far = add(far, to_core(other_far)).reshape(PLACES, rows, -1)
     near = add(near, to_core(other_near)).reshape(PLACES, rows, -1)
-    far_second = to_place(far[2], 1)
-    first = add(near[1], to_chip(far[1]))
-    far_third = add(far[3], far_second)
-    near_second = to_place(after(near[2], far_second), 1)
-    third = add(near[3], near_second, to_chip(far_third))
-    third_here = to_place(third, 3)
-    own = add(near[0], to_chip(after(far[0], third)))
-    return add(own, to_place(after(first, third), 1), third_here)
+    second = add(near[2], to_both(far[3], 1), to_chip(far[2]), to_place(near[3], 1))
+    second_here = to_place(second, 2)
+    first = add(near[1], to_chip(after(far[1], second)))
+    own = add(near[0], to_chip(after(far[0], second)))
+    return add(own, to_place(first, 1), second_here)
 
 
 def by_permutes(tokens, expert_ids, route_weights, expert_slot, w_gate, w_up, w_down):
     rows = tokens.shape[0]
     own = pack(tokens, expert_ids, route_weights, expert_slot, w_gate, w_up, w_down)
     hidden = hidden_units(gather_blocks(own), w_gate, w_up, expert_slot.shape[0])
+    matrix = w_down.reshape(-1, w_down.shape[-1])
     outs = []
     for chunk in range(OUT_CHUNKS):
-        outs.append(reduce_blocks(*down(hidden, w_down, chunk, OUT_CHUNKS), rows))
+        outs.append(reduce_blocks(*down(hidden, matrix, chunk, OUT_CHUNKS), rows))
     return jnp.concatenate(outs, axis=1)
 
 

time: 59.7 us -> 55.4 us (0.928)
  Pallas kernels: 13.6 us -> 9.14 us
  waiting for transfers between devices: 21.3 us -> 21.9 us
    ppermute x7 -> x6, waiting for transfers between devices: 12.9 us -> 7.01 us  [to_place(): return lax.ppermute(value, 'local', [(i, i ^ bits) for i in range(PLACES)])]
    pallas_call x1, Pallas kernels: 7.13 us -> 2.68 us  [down(): pl.pallas_call(functools.partial(down_kernel, chunk), out_shape=[jax.Shap...]
    ppermute x7 -> x6, waiting for transfers between devices: 5.66 us -> 9.88 us  [to_chip(): return lax.ppermute(value, 'node', [(i, i ^ 2) for i in range(2 * CHIPS)])]
    ppermute x0 -> x2, starting transfers between devices: none -> 3.45 us  [to_both(): return lax.ppermute(value, ('node', 'local'), perm)]
    ppermute x7 -> x6, starting transfers between devices: 9.65 us -> 6.67 us  [to_chip(): return lax.ppermute(value, 'node', [(i, i ^ 2) for i in range(2 * CHIPS)])]
    ppermute x0 -> x2, waiting for transfers between devices: none -> 2.76 us  [to_both(): return lax.ppermute(value, ('node', 'local'), perm)]
    ppermute x7 -> x6, starting transfers between devices: 12.1 us -> 11.2 us  [to_place(): return lax.ppermute(value, 'local', [(i, i ^ bits) for i in range(PLACES)])]
  transfers between devices with their start and end apart: 24 -> 24, of which waited for: 14 -> 12; matrix products, arithmetic and copies ran while one was open for 0% -> 1% of each run, Pallas kernels for 0% -> 0%
where the time goes in v5:
time: 55.4 us; the launch traced here: 55.2 us
  starting transfers between devices  23 us (42%)
  waiting for transfers between devices  21.9 us (40%)
  Pallas kernels  9.14 us (16%)
  other arithmetic  1.01 us (2%)
    ppermute x6, starting transfers between devices, to_place(): return lax.ppermute(value, 'local', [(i, i ^ bits) for i in range(PLACES)])  11.2 us
    ppermute x6, waiting for transfers between devices, to_chip(): return lax.ppermute(value, 'node', [(i, i ^ 2) for i in range(2 * CHIPS)])  9.88 us
    ppermute x6, waiting for transfers between devices, to_place(): return lax.ppermute(value, 'local', [(i, i ^ bits) for i in range(PLACES)])  7.01 us
    ppermute x6, starting transfers between devices, to_chip(): return lax.ppermute(value, 'node', [(i, i ^ 2) for i in range(2 * CHIPS)])  6.67 us
    pallas_call x1, Pallas kernels, hidden_units(): pl.pallas_call(functools.partial(hidden_kernel, experts), out_shape=jax.S...  5.3 us
    ppermute x2, starting transfers between devices, to_both(): return lax.ppermute(value, ('node', 'local'), perm)  3.45 us
    ppermute x2, waiting for transfers between devices, to_both(): return lax.ppermute(value, ('node', 'local'), perm)  2.76 us
    pallas_call x1, Pallas kernels, down(): pl.pallas_call(functools.partial(down_kernel, chunk), out_shape=[jax.Shap...  2.68 us
  transfers between devices with their start and end apart: 24, of which 12 were waited for; matrix products, arithmetic and copies ran while one was open for 1% of the time, Pallas kernels for 0%

profile of v5, /device:TPU:0, one launch (start us, length us, event | category | flops | bytes accessed | tf_op | source)
XLA Modules:
  0.0 55.2 jit_solution(12982247211254145761)
XLA Ops:
  0.0 0.0 copy-start
  0.0 0.0 copy-start.1
  0.0 1.2 %pack.1.refs_0_ = bf16[8,7296]{1,0:T(8,128)(2,1)S(1)} custom-call(bf16[8,7168]{1,0:T(8,128)(2,1)} %refs_0_.1, s32[4,8]{1,0:T(4,128)} %bitcast.6, f32[4,8]{1,0:T(4,128)} %bitcast.7, s32[8]{0:T(128)} %refs_3_.1, bf16[2,7168,512]{2,1,0:T(8,128)(2,1)} %refs_16_.1, bf16[2,7168,512]{2,1,0:T(8,128)(2,1)} %refs_17_.1, bf16[2,512,7168]{2,1,0:T(8,128)(2,1)} %refs_6_.1), custom_call_target="tpu_custom_call" | custom-call | tf_op jit(solution)/shard_map/pack/pallas_call | solution.py:50
  1.2 0.0 slice-start.3
  1.2 4.1 %collective-permute-start.1 = (bf16[8,7296]{1,0:T(8,128)(2,1)S(1)}, bf16[8,7296]{1,0:T(8,128)(2,1)S(1)}, u32[]{:S(2)}, u32[]{:S(2)}) collective-permute-start(bf16[8,7296]{1,0:T(8,128)(2,1)S(1)} %pack.1.refs_0_), channel_id=1, source_target_pairs={{0,2},{1,3},{2,0},{3,1},{4,6},{5,7},{6,4},{7,5},{8,10},{9,11},{10,... | collective-permute-start | bytes 350216 | tf_op jit(solution)/shard_map/ppermute | solution.py:160
  5.3 1.5 %collective-permute-start.3 = (bf16[8,7296]{1,0:T(8,128)(2,1)S(1)}, bf16[8,7296]{1,0:T(8,128)(2,1)S(1)}, u32[]{:S(2)}, u32[]{:S(2)}) collective-permute-start(bf16[8,7296]{1,0:T(8,128)(2,1)S(1)} %pack.1.refs_0_), channel_id=1, source_target_pairs={{0,8},{4,12},{8,0},{12,4},{1,9},{5,13},{9,1},{13,5},{2,10},{6,14},... | collective-permute-start | bytes 350216 | tf_op jit(solution)/shard_map/ppermute | solution.py:156
  6.8 1.6 %collective-permute-start = (bf16[8,7296]{1,0:T(8,128)(2,1)S(1)}, bf16[8,7296]{1,0:T(8,128)(2,1)S(1)}, u32[]{:S(2)}, u32[]{:S(2)}) collective-permute-start(bf16[8,7296]{1,0:T(8,128)(2,1)S(1)} %pack.1.refs_0_), channel_id=1, source_target_pairs={{0,1},{1,0},{2,3},{3,2},{4,5},{5,4},{6,7},{7,6},{8,9},{9,8},{10,11... | collective-permute-start | bytes 350216 | tf_op jit(solution)/shard_map/ppermute | solution.py:160
  8.4 0.0 collective-permute-start.7
  8.4 2.7 %collective-permute-done.1.refs_2_ = bf16[8,7296]{1,0:T(8,128)(2,1)S(1)} collective-permute-done((bf16[8,7296]{1,0:T(8,128)(2,1)S(1)}, bf16[8,7296]{1,0:T(8,128)(2,1)S(1)}, u32[]{:S(2)}, u32[]{:S(2)}) %collective-permute-start.1) | collective-permute-done | bytes 116768 | tf_op jit(solution)/shard_map/ppermute | solution.py:160
  11.1 0.7 %collective-permute-start.2 = (bf16[8,7296]{1,0:T(8,128)(2,1)S(1)}, bf16[8,7296]{1,0:T(8,128)(2,1)S(1)}, u32[]{:S(2)}, u32[]{:S(2)}) collective-permute-start(bf16[8,7296]{1,0:T(8,128)(2,1)S(1)} %collective-permute-done.1.refs_2_), channel_id=1, source_target_pairs={{0,1},{1,0},{2,3},{3,2},{4,5},{5,4},{6,7},{7,6},{8,9},{9,8},{10,11... | collective-permute-start | bytes 350216 | tf_op jit(solution)/shard_map/ppermute | solution.py:160
  11.8 0.0 collective-permute-done.3.refs_4_
  11.8 0.0 collective-permute-start.11
  11.8 0.7 %collective-permute-done.refs_1_ = bf16[8,7296]{1,0:T(8,128)(2,1)S(1)} collective-permute-done((bf16[8,7296]{1,0:T(8,128)(2,1)S(1)}, bf16[8,7296]{1,0:T(8,128)(2,1)S(1)}, u32[]{:S(2)}, u32[]{:S(2)}) %collective-permute-start) | collective-permute-done | bytes 116768 | tf_op jit(solution)/shard_map/ppermute | solution.py:160
  12.5 1.7 %collective-permute-start.6 = (bf16[8,7296]{1,0:T(8,128)(2,1)S(1)}, bf16[8,7296]{1,0:T(8,128)(2,1)S(1)}, u32[]{:S(2)}, u32[]{:S(2)}) collective-permute-start(bf16[8,7296]{1,0:T(8,128)(2,1)S(1)} %collective-permute-done.1.refs_2_), channel_id=1, source_target_pairs={{0,9},{1,8},{2,11},{3,10},{4,13},{5,12},{6,15},{7,14},{8,1},{9,0},... | collective-permute-start | bytes 350216 | tf_op jit(solution)/shard_map/ppermute | solution.py:166
  14.2 0.5 collective-permute-start.5
  14.7 0.0 collective-permute-done.7.refs_8_
  14.7 1.6 %collective-permute-start.4 = (bf16[8,7296]{1,0:T(8,128)(2,1)S(1)}, bf16[8,7296]{1,0:T(8,128)(2,1)S(1)}, u32[]{:S(2)}, u32[]{:S(2)}) collective-permute-start(bf16[8,7296]{1,0:T(8,128)(2,1)S(1)} %collective-permute-done.refs_1_), channel_id=1, source_target_pairs={{0,8},{4,12},{8,0},{12,4},{1,9},{5,13},{9,1},{13,5},{2,10},{6,14},... | collective-permute-start | bytes 350216 | tf_op jit(solution)/shard_map/ppermute | solution.py:156
  16.2 0.0 collective-permute-done.2.refs_3_
  16.2 0.0 collective-permute-start.8
  16.2 0.0 collective-permute-done.11.refs_12_
  16.3 0.5 collective-permute-start.9
  16.8 2.8 %collective-permute-done.6.refs_7_ = bf16[8,7296]{1,0:T(8,128)(2,1)S(1)} collective-permute-done((bf16[8,7296]{1,0:T(8,128)(2,1)S(1)}, bf16[8,7296]{1,0:T(8,128)(2,1)S(1)}, u32[]{:S(2)}, u32[]{:S(2)}) %collective-permute-start.6) | collective-permute-done | bytes 116768 | tf_op jit(solution)/shard_map/ppermute | solution.py:166
  19.5 0.0 collective-permute-start.14
  19.5 2.2 %collective-permute-done.5.refs_6_ = bf16[8,7296]{1,0:T(8,128)(2,1)S(1)} collective-permute-done((bf16[8,7296]{1,0:T(8,128)(2,1)S(1)}, bf16[8,7296]{1,0:T(8,128)(2,1)S(1)}, u32[]{:S(2)}, u32[]{:S(2)}) %collective-permute-start.5) | collective-permute-done | bytes 116768 | tf_op jit(solution)/shard_map/ppermute | solution.py:156
  21.8 0.0 collective-permute-start.13
  21.8 2.1 %collective-permute-done.4.refs_5_ = bf16[8,7296]{1,0:T(8,128)(2,1)S(1)} collective-permute-done((bf16[8,7296]{1,0:T(8,128)(2,1)S(1)}, bf16[8,7296]{1,0:T(8,128)(2,1)S(1)}, u32[]{:S(2)}, u32[]{:S(2)}) %collective-permute-start.4) | collective-permute-done | bytes 116768 | tf_op jit(solution)/shard_map/ppermute | solution.py:156
  23.9 0.0 collective-permute-start.10
  23.9 0.0 collective-permute-done.8.refs_9_
  23.9 0.5 collective-permute-start.12
  24.4 0.0 collective-permute-done.14.refs_15_
  24.4 0.0 collective-permute-done.13.refs_14_
  24.4 0.0 collective-permute-done.9.refs_10_
  24.4 0.8 %collective-permute-done.10.refs_11_ = bf16[8,7296]{1,0:T(8,128)(2,1)S(1)} collective-permute-done((bf16[8,7296]{1,0:T(8,128)(2,1)S(1)}, bf16[8,7296]{1,0:T(8,128)(2,1)S(1)}, u32[]{:S(2)}, u32[]{:S(2)}) %collective-permute-start.10) | collective-permute-done | bytes 116768 | tf_op jit(solution)/shard_map/ppermute | solution.py:152
  25.2 0.2 collective-permute-done.12.refs_13_
  25.4 0.0 copy-done
  25.4 0.0 copy-done.1
  25.4 5.3 %hidden.1.hidden_ref = bf16[128,1024]{1,0:T(8,128)(2,1)S(1)} custom-call(bf16[8,7296]{1,0:T(8,128)(2,1)S(1)} %pack.1.refs_0_, bf16[8,7296]{1,0:T(8,128)(2,1)S(1)} %collective-permute-done.refs_1_, bf16[8,7296]{1,0:T(8,128)(2,1)S(1)} %collective-permute-done.1.refs_2_, bf16[8,7296]{1,0:T(8,128)(2,1)S(1)} %collective-permute-done.2.refs_3_, ...), custom_call_target="tpu_custom_call" | custom-call | flops 3758096384 | bytes 29360128 | tf_op jit(solution)/shard_map/hidden/pallas_call | solution.py:95
  30.7 0.0 slice-done
  30.7 0.0 slice-done.1
  30.7 0.0 slice-done.2
  30.7 0.0 slice-done.3
  30.7 2.7 %down.1 = (bf16[32,7168]{1,0:T(8,128)(2,1)S(1)}, bf16[32,7168]{1,0:T(8,128)(2,1)S(1)}, bf16[32,7168]{1,0:T(8,128)(2,1)S(1)}, bf16[32,7168]{1,0:T(8,128)(2,1)S(1)}) custom-call(bf16[128,1024]{1,0:T(8,128)(2,1)S(1)} %hidden.1.hidden_ref, bf16[1024,7168]{1,0:T(8,128)(2,1)S(1)} %bitcast.5), custom_call_target="tpu_custom_call" | custom-call | flops 1879048192 | bytes 14680064 | tf_op jit(solution)/shard_map/down/pallas_call | solution.py:133
  33.4 0.4 collective-permute-start.15
  33.8 0.2 collective-permute-start.16
  34.0 1.3 %collective-permute-done.15 = bf16[32,7168]{1,0:T(8,128)(2,1)S(1)} collective-permute-done((bf16[32,7168]{1,0:T(8,128)(2,1)S(1)}, bf16[32,7168]{1,0:T(8,128)(2,1)S(1)}, u32[]{:S(2)}, u32[]{:S(2)}) %collective-permute-start.15) | collective-permute-done | bytes 458784 | tf_op jit(solution)/shard_map/ppermute | solution.py:152
  35.3 0.1 add_convert_fusion.1
  35.4 1.0 %collective-permute-start.19 = (bf16[8,7168]{1,0:T(8,128)(2,1)S(1)}, bf16[8,7168]{1,0:T(8,128)(2,1)S(1)}, u32[]{:S(2)}, u32[]{:S(2)}) collective-permute-start(bf16[8,7168]{1,0:T(8,128)(2,1)S(1)} %slice.45), channel_id=1, source_target_pairs={{0,1},{1,0},{2,3},{3,2},{4,5},{5,4},{6,7},{7,6},{8,9},{9,8},{10,11... | collective-permute-start | bytes 344072 | tf_op jit(solution)/shard_map/ppermute | solution.py:160
  36.5 0.0 collective-permute-done.16
  36.5 0.1 add_convert_fusion
  36.6 0.8 %collective-permute-start.18 = (bf16[8,7168]{1,0:T(8,128)(2,1)S(1)}, bf16[8,7168]{1,0:T(8,128)(2,1)S(1)}, u32[]{:S(2)}, u32[]{:S(2)}) collective-permute-start(bf16[8,7168]{1,0:T(8,128)(2,1)S(1)} %get-tuple-element.23), channel_id=1, source_target_pairs={{0,8},{4,12},{8,0},{12,4},{1,9},{5,13},{9,1},{13,5},{2,10},{6,14},... | collective-permute-start | bytes 344072 | tf_op jit(solution)/shard_map/ppermute | solution.py:156
  37.5 1.7 %collective-permute-start.17 = (bf16[8,7168]{1,0:T(8,128)(2,1)S(1)}, bf16[8,7168]{1,0:T(8,128)(2,1)S(1)}, u32[]{:S(2)}, u32[]{:S(2)}) collective-permute-start(bf16[8,7168]{1,0:T(8,128)(2,1)S(1)} %get-tuple-element.24), channel_id=1, source_target_pairs={{0,9},{1,8},{2,11},{3,10},{4,13},{5,12},{6,15},{7,14},{8,1},{9,0},... | collective-permute-start | bytes 344072 | tf_op jit(solution)/shard_map/ppermute | solution.py:166
  39.2 2.0 %collective-permute-done.19 = bf16[8,7168]{1,0:T(8,128)(2,1)S(1)} collective-permute-done((bf16[8,7168]{1,0:T(8,128)(2,1)S(1)}, bf16[8,7168]{1,0:T(8,128)(2,1)S(1)}, u32[]{:S(2)}, u32[]{:S(2)}) %collective-permute-start.19) | collective-permute-done | bytes 114720 | tf_op jit(solution)/shard_map/ppermute | solution.py:160
  41.2 3.0 %collective-permute-done.18 = bf16[8,7168]{1,0:T(8,128)(2,1)S(1)} collective-permute-done((bf16[8,7168]{1,0:T(8,128)(2,1)S(1)}, bf16[8,7168]{1,0:T(8,128)(2,1)S(1)}, u32[]{:S(2)}, u32[]{:S(2)}) %collective-permute-start.18) | collective-permute-done | bytes 114720 | tf_op jit(solution)/shard_map/ppermute | solution.py:156
  44.2 0.0 collective-permute-done.17
  44.2 0.1 add_convert_fusion.5
  44.3 0.8 %collective-permute-start.21 = (bf16[8,7168]{1,0:T(8,128)(2,1)S(1)}, bf16[8,7168]{1,0:T(8,128)(2,1)S(1)}, u32[]{:S(2)}, u32[]{:S(2)}) collective-permute-start(bf16[8,7168]{1,0:T(8,128)(2,1)S(1)} %get-tuple-element.20), channel_id=1, source_target_pairs={{0,8},{4,12},{8,0},{12,4},{1,9},{5,13},{9,1},{13,5},{2,10},{6,14},... | collective-permute-start | bytes 344072 | tf_op jit(solution)/shard_map/ppermute | solution.py:156
  45.2 3.0 %collective-permute-start.23 = (bf16[8,7168]{1,0:T(8,128)(2,1)S(1)}, bf16[8,7168]{1,0:T(8,128)(2,1)S(1)}, u32[]{:S(2)}, u32[]{:S(2)}) collective-permute-start(bf16[8,7168]{1,0:T(8,128)(2,1)S(1)} %add_convert_fusion.5), channel_id=1, source_target_pairs={{0,2},{1,3},{2,0},{3,1},{4,6},{5,7},{6,4},{7,5},{8,10},{9,11},{10,... | collective-permute-start | bytes 344072 | tf_op jit(solution)/shard_map/ppermute | solution.py:160
  48.2 1.5 %collective-permute-start.20 = (bf16[8,7168]{1,0:T(8,128)(2,1)S(1)}, bf16[8,7168]{1,0:T(8,128)(2,1)S(1)}, u32[]{:S(2)}, u32[]{:S(2)}) collective-permute-start(bf16[8,7168]{1,0:T(8,128)(2,1)S(1)} %get-tuple-element.19), channel_id=1, source_target_pairs={{0,8},{4,12},{8,0},{12,4},{1,9},{5,13},{9,1},{13,5},{2,10},{6,14},... | collective-permute-start | bytes 344072 | tf_op jit(solution)/shard_map/ppermute | solution.py:156
  49.6 0.0 collective-permute-done.21
  49.7 0.8 %collective-permute-start.22 = (bf16[8,7168]{1,0:T(8,128)(2,1)S(1)}, bf16[8,7168]{1,0:T(8,128)(2,1)S(1)}, u32[]{:S(2)}, u32[]{:S(2)}) collective-permute-start(bf16[8,7168]{1,0:T(8,128)(2,1)S(1)} %add_convert_fusion.3), channel_id=1, source_target_pairs={{0,1},{1,0},{2,3},{3,2},{4,5},{5,4},{6,7},{7,6},{8,9},{9,8},{10,11... | collective-permute-start | bytes 344072 | tf_op jit(solution)/shard_map/ppermute | solution.py:160
  50.5 2.5 %collective-permute-done.20 = bf16[8,7168]{1,0:T(8,128)(2,1)S(1)} collective-permute-done((bf16[8,7168]{1,0:T(8,128)(2,1)S(1)}, bf16[8,7168]{1,0:T(8,128)(2,1)S(1)}, u32[]{:S(2)}, u32[]{:S(2)}) %collective-permute-start.20) | collective-permute-done | bytes 114720 | tf_op jit(solution)/shard_map/ppermute | solution.py:156
  53.0 0.0 collective-permute-done.23
  53.0 1.6 %collective-permute-done.22 = bf16[8,7168]{1,0:T(8,128)(2,1)S(1)} collective-permute-done((bf16[8,7168]{1,0:T(8,128)(2,1)S(1)}, bf16[8,7168]{1,0:T(8,128)(2,1)S(1)}, u32[]{:S(2)}, u32[]{:S(2)}) %collective-permute-start.22) | collective-permute-done | bytes 114720 | tf_op jit(solution)/shard_map/ppermute | solution.py:160
  54.5 0.7 %add_convert_fusion.2 = bf16[8,7168]{1,0:T(8,128)(2,1)} fusion(bf16[8,7168]{1,0:T(8,128)(2,1)S(1)} %collective-permute-done.23, bf16[8,7168]{1,0:T(8,128)(2,1)S(1)} %collective-permute-done.22, bf16[8,7168]{1,0:T(8,128)(2,1)S(1)} %collective-permute-done.20, bf16[32,7168]{1,0:T(8,128)(2,1)S(1)} %add_convert_fusion.1), kind=kLoop, calls=%fused_computation.2 | loop fusion | flops 573440 | bytes 573440 | tf_op jit(solution)/shard_map/convert_element_type | solution.py:170
  (7 shorter events, 0.1 us)
Async XLA Ops:
  0.0 25.4 %copy-start = (bf16[2,7168,512]{2,1,0:T(8,128)(2,1)S(1)}, bf16[2,7168,512]{2,1,0:T(8,128)(2,1)}, u32[]{:S(2)}) copy-start(bf16[2,7168,512]{2,1,0:T(8,128)(2,1)} %refs_16_.1) | copy-start | bytes 44040196
  0.0 25.4 %copy-start.1 = (bf16[2,7168,512]{2,1,0:T(8,128)(2,1)S(1)}, bf16[2,7168,512]{2,1,0:T(8,128)(2,1)}, u32[]{:S(2)}) copy-start(bf16[2,7168,512]{2,1,0:T(8,128)(2,1)} %refs_17_.1) | copy-start | bytes 44040196
  0.0 30.7 %slice-start = ((s8[14680064]{0:T(1024)(128)(4,1)}), s8[4194304]{0:T(1024)(128)(4,1)S(1)}, s32[]{:S(2)}) async-start(s8[14680064]{0:T(1024)(128)(4,1)} %bitcast.3), calls=%async_computation | async-start | bytes 8388608
  0.0 30.7 %slice-start.1 = ((s8[14680064]{0:T(1024)(128)(4,1)}), s8[4194304]{0:T(1024)(128)(4,1)S(1)}, s32[]{:S(2)}) async-start(s8[14680064]{0:T(1024)(128)(4,1)} %bitcast.3), calls=%async_computation.1 | async-start | bytes 8388608
  0.0 30.7 %slice-start.2 = ((s8[14680064]{0:T(1024)(128)(4,1)}), s8[4194304]{0:T(1024)(128)(4,1)S(1)}, s32[]{:S(2)}) async-start(s8[14680064]{0:T(1024)(128)(4,1)} %bitcast.3), calls=%async_computation.2 | async-start | bytes 8388608
  1.2 29.5 %slice-start.3 = ((s8[14680064]{0:T(1024)(128)(4,1)}), s8[2097152]{0:T(1024)(128)(4,1)S(1)}, s32[]{:S(2)}) async-start(s8[14680064]{0:T(1024)(128)(4,1)} %bitcast.3), calls=%async_computation.3 | async-start | bytes 4194304
  1.2 9.9 %collective-permute-start.1 = (bf16[8,7296]{1,0:T(8,128)(2,1)S(1)}, bf16[8,7296]{1,0:T(8,128)(2,1)S(1)}, u32[]{:S(2)}, u32[]{:S(2)}) collective-permute-start(bf16[8,7296]{1,0:T(8,128)(2,1)S(1)} %pack.1.refs_0_), channel_id=1, source_target_pairs={{0,2},{1,3},{2,0},{3,1},{4,6},{5,7},{6,4},{7,5},{8,10},{9,11},{10,... | collective-permute-start | bytes 350216 | tf_op jit(solution)/shard_map/ppermute | solution.py:160
  5.3 6.5 %collective-permute-start.3 = (bf16[8,7296]{1,0:T(8,128)(2,1)S(1)}, bf16[8,7296]{1,0:T(8,128)(2,1)S(1)}, u32[]{:S(2)}, u32[]{:S(2)}) collective-permute-start(bf16[8,7296]{1,0:T(8,128)(2,1)S(1)} %pack.1.refs_0_), channel_id=1, source_target_pairs={{0,8},{4,12},{8,0},{12,4},{1,9},{5,13},{9,1},{13,5},{2,10},{6,14},... | collective-permute-start | bytes 350216 | tf_op jit(solution)/shard_map/ppermute | solution.py:156
  6.8 5.7 %collective-permute-start = (bf16[8,7296]{1,0:T(8,128)(2,1)S(1)}, bf16[8,7296]{1,0:T(8,128)(2,1)S(1)}, u32[]{:S(2)}, u32[]{:S(2)}) collective-permute-start(bf16[8,7296]{1,0:T(8,128)(2,1)S(1)} %pack.1.refs_0_), channel_id=1, source_target_pairs={{0,1},{1,0},{2,3},{3,2},{4,5},{5,4},{6,7},{7,6},{8,9},{9,8},{10,11... | collective-permute-start | bytes 350216 | tf_op jit(solution)/shard_map/ppermute | solution.py:160
  8.4 6.3 %collective-permute-start.7 = (bf16[8,7296]{1,0:T(8,128)(2,1)S(1)}, bf16[8,7296]{1,0:T(8,128)(2,1)S(1)}, u32[]{:S(2)}, u32[]{:S(2)}) collective-permute-start(bf16[8,7296]{1,0:T(8,128)(2,1)S(1)} %pack.1.refs_0_), channel_id=1, source_target_pairs={{0,4},{4,0},{8,12},{12,8},{1,5},{5,1},{9,13},{13,9},{2,6},{6,2},{1... | collective-permute-start | bytes 350216 | tf_op jit(solution)/shard_map/ppermute | solution.py:152
  11.1 5.1 %collective-permute-start.2 = (bf16[8,7296]{1,0:T(8,128)(2,1)S(1)}, bf16[8,7296]{1,0:T(8,128)(2,1)S(1)}, u32[]{:S(2)}, u32[]{:S(2)}) collective-permute-start(bf16[8,7296]{1,0:T(8,128)(2,1)S(1)} %collective-permute-done.1.refs_2_), channel_id=1, source_target_pairs={{0,1},{1,0},{2,3},{3,2},{4,5},{5,4},{6,7},{7,6},{8,9},{9,8},{10,11... | collective-permute-start | bytes 350216 | tf_op jit(solution)/shard_map/ppermute | solution.py:160
  11.8 4.5 %collective-permute-start.11 = (bf16[8,7296]{1,0:T(8,128)(2,1)S(1)}, bf16[8,7296]{1,0:T(8,128)(2,1)S(1)}, u32[]{:S(2)}, u32[]{:S(2)}) collective-permute-start(bf16[8,7296]{1,0:T(8,128)(2,1)S(1)} %collective-permute-done.3.refs_4_), channel_id=1, source_target_pairs={{0,4},{4,0},{8,12},{12,8},{1,5},{5,1},{9,13},{13,9},{2,6},{6,2},{1... | collective-permute-start | bytes 350216 | tf_op jit(solution)/shard_map/ppermute | solution.py:152
  12.5 7.0 %collective-permute-start.6 = (bf16[8,7296]{1,0:T(8,128)(2,1)S(1)}, bf16[8,7296]{1,0:T(8,128)(2,1)S(1)}, u32[]{:S(2)}, u32[]{:S(2)}) collective-permute-start(bf16[8,7296]{1,0:T(8,128)(2,1)S(1)} %collective-permute-done.1.refs_2_), channel_id=1, source_target_pairs={{0,9},{1,8},{2,11},{3,10},{4,13},{5,12},{6,15},{7,14},{8,1},{9,0},... | collective-permute-start | bytes 350216 | tf_op jit(solution)/shard_map/ppermute | solution.py:166
  14.2 7.6 %collective-permute-start.5 = (bf16[8,7296]{1,0:T(8,128)(2,1)S(1)}, bf16[8,7296]{1,0:T(8,128)(2,1)S(1)}, u32[]{:S(2)}, u32[]{:S(2)}) collective-permute-start(bf16[8,7296]{1,0:T(8,128)(2,1)S(1)} %collective-permute-done.1.refs_2_), channel_id=1, source_target_pairs={{0,8},{4,12},{8,0},{12,4},{1,9},{5,13},{9,1},{13,5},{2,10},{6,14},... | collective-permute-start | bytes 350216 | tf_op jit(solution)/shard_map/ppermute | solution.py:156
  14.7 9.2 %collective-permute-start.4 = (bf16[8,7296]{1,0:T(8,128)(2,1)S(1)}, bf16[8,7296]{1,0:T(8,128)(2,1)S(1)}, u32[]{:S(2)}, u32[]{:S(2)}) collective-permute-start(bf16[8,7296]{1,0:T(8,128)(2,1)S(1)} %collective-permute-done.refs_1_), channel_id=1, source_target_pairs={{0,8},{4,12},{8,0},{12,4},{1,9},{5,13},{9,1},{13,5},{2,10},{6,14},... | collective-permute-start | bytes 350216 | tf_op jit(solution)/shard_map/ppermute | solution.py:156
  16.2 7.6 %collective-permute-start.8 = (bf16[8,7296]{1,0:T(8,128)(2,1)S(1)}, bf16[8,7296]{1,0:T(8,128)(2,1)S(1)}, u32[]{:S(2)}, u32[]{:S(2)}) collective-permute-start(bf16[8,7296]{1,0:T(8,128)(2,1)S(1)} %collective-permute-done.refs_1_), channel_id=1, source_target_pairs={{0,4},{4,0},{8,12},{12,8},{1,5},{5,1},{9,13},{13,9},{2,6},{6,2},{1... | collective-permute-start | bytes 350216 | tf_op jit(solution)/shard_map/ppermute | solution.py:152
  16.3 8.1 %collective-permute-start.9 = (bf16[8,7296]{1,0:T(8,128)(2,1)S(1)}, bf16[8,7296]{1,0:T(8,128)(2,1)S(1)}, u32[]{:S(2)}, u32[]{:S(2)}) collective-permute-start(bf16[8,7296]{1,0:T(8,128)(2,1)S(1)} %collective-permute-done.1.refs_2_), channel_id=1, source_target_pairs={{0,4},{4,0},{8,12},{12,8},{1,5},{5,1},{9,13},{13,9},{2,6},{6,2},{1... | collective-permute-start | bytes 350216 | tf_op jit(solution)/shard_map/ppermute | solution.py:152
  19.5 4.9 %collective-permute-start.14 = (bf16[8,7296]{1,0:T(8,128)(2,1)S(1)}, bf16[8,7296]{1,0:T(8,128)(2,1)S(1)}, u32[]{:S(2)}, u32[]{:S(2)}) collective-permute-start(bf16[8,7296]{1,0:T(8,128)(2,1)S(1)} %collective-permute-done.6.refs_7_), channel_id=1, source_target_pairs={{0,4},{4,0},{8,12},{12,8},{1,5},{5,1},{9,13},{13,9},{2,6},{6,2},{1... | collective-permute-start | bytes 350216 | tf_op jit(solution)/shard_map/ppermute | solution.py:152
  21.8 2.6 %collective-permute-start.13 = (bf16[8,7296]{1,0:T(8,128)(2,1)S(1)}, bf16[8,7296]{1,0:T(8,128)(2,1)S(1)}, u32[]{:S(2)}, u32[]{:S(2)}) collective-permute-start(bf16[8,7296]{1,0:T(8,128)(2,1)S(1)} %collective-permute-done.5.refs_6_), channel_id=1, source_target_pairs={{0,4},{4,0},{8,12},{12,8},{1,5},{5,1},{9,13},{13,9},{2,6},{6,2},{1... | collective-permute-start | bytes 350216 | tf_op jit(solution)/shard_map/ppermute | solution.py:152
  23.9 1.3 %collective-permute-start.10 = (bf16[8,7296]{1,0:T(8,128)(2,1)S(1)}, bf16[8,7296]{1,0:T(8,128)(2,1)S(1)}, u32[]{:S(2)}, u32[]{:S(2)}) collective-permute-start(bf16[8,7296]{1,0:T(8,128)(2,1)S(1)} %collective-permute-done.2.refs_3_), channel_id=1, source_target_pairs={{0,4},{4,0},{8,12},{12,8},{1,5},{5,1},{9,13},{13,9},{2,6},{6,2},{1... | collective-permute-start | bytes 350216 | tf_op jit(solution)/shard_map/ppermute | solution.py:152
  23.9 1.5 %collective-permute-start.12 = (bf16[8,7296]{1,0:T(8,128)(2,1)S(1)}, bf16[8,7296]{1,0:T(8,128)(2,1)S(1)}, u32[]{:S(2)}, u32[]{:S(2)}) collective-permute-start(bf16[8,7296]{1,0:T(8,128)(2,1)S(1)} %collective-permute-done.4.refs_5_), channel_id=1, source_target_pairs={{0,4},{4,0},{8,12},{12,8},{1,5},{5,1},{9,13},{13,9},{2,6},{6,2},{1... | collective-permute-start | bytes 350216 | tf_op jit(solution)/shard_map/ppermute | solution.py:152
  33.4 1.9 %collective-permute-start.15 = (bf16[32,7168]{1,0:T(8,128)(2,1)S(1)}, bf16[32,7168]{1,0:T(8,128)(2,1)S(1)}, u32[]{:S(2)}, u32[]{:S(2)}) collective-permute-start(bf16[32,7168]{1,0:T(8,128)(2,1)S(1)} %get-tuple-element.16), channel_id=1, source_target_pairs={{0,4},{4,0},{8,12},{12,8},{1,5},{5,1},{9,13},{13,9},{2,6},{6,2},{1... | collective-permute-start | bytes 1376264 | tf_op jit(solution)/shard_map/ppermute | solution.py:152
  33.8 2.6 %collective-permute-start.16 = (bf16[32,7168]{1,0:T(8,128)(2,1)S(1)}, bf16[32,7168]{1,0:T(8,128)(2,1)S(1)}, u32[]{:S(2)}, u32[]{:S(2)}) collective-permute-start(bf16[32,7168]{1,0:T(8,128)(2,1)S(1)} %get-tuple-element.18), channel_id=1, source_target_pairs={{0,4},{4,0},{8,12},{12,8},{1,5},{5,1},{9,13},{13,9},{2,6},{6,2},{1... | collective-permute-start | bytes 1376264 | tf_op jit(solution)/shard_map/ppermute | solution.py:152
  35.4 5.8 %collective-permute-start.19 = (bf16[8,7168]{1,0:T(8,128)(2,1)S(1)}, bf16[8,7168]{1,0:T(8,128)(2,1)S(1)}, u32[]{:S(2)}, u32[]{:S(2)}) collective-permute-start(bf16[8,7168]{1,0:T(8,128)(2,1)S(1)} %slice.45), channel_id=1, source_target_pairs={{0,1},{1,0},{2,3},{3,2},{4,5},{5,4},{6,7},{7,6},{8,9},{9,8},{10,11... | collective-permute-start | bytes 344072 | tf_op jit(solution)/shard_map/ppermute | solution.py:160
  36.6 7.6 %collective-permute-start.18 = (bf16[8,7168]{1,0:T(8,128)(2,1)S(1)}, bf16[8,7168]{1,0:T(8,128)(2,1)S(1)}, u32[]{:S(2)}, u32[]{:S(2)}) collective-permute-start(bf16[8,7168]{1,0:T(8,128)(2,1)S(1)} %get-tuple-element.23), channel_id=1, source_target_pairs={{0,8},{4,12},{8,0},{12,4},{1,9},{5,13},{9,1},{13,5},{2,10},{6,14},... | collective-permute-start | bytes 344072 | tf_op jit(solution)/shard_map/ppermute | solution.py:156
  37.5 6.8 %collective-permute-start.17 = (bf16[8,7168]{1,0:T(8,128)(2,1)S(1)}, bf16[8,7168]{1,0:T(8,128)(2,1)S(1)}, u32[]{:S(2)}, u32[]{:S(2)}) collective-permute-start(bf16[8,7168]{1,0:T(8,128)(2,1)S(1)} %get-tuple-element.24), channel_id=1, source_target_pairs={{0,9},{1,8},{2,11},{3,10},{4,13},{5,12},{6,15},{7,14},{8,1},{9,0},... | collective-permute-start | bytes 344072 | tf_op jit(solution)/shard_map/ppermute | solution.py:166
  44.3 5.3 %collective-permute-start.21 = (bf16[8,7168]{1,0:T(8,128)(2,1)S(1)}, bf16[8,7168]{1,0:T(8,128)(2,1)S(1)}, u32[]{:S(2)}, u32[]{:S(2)}) collective-permute-start(bf16[8,7168]{1,0:T(8,128)(2,1)S(1)} %get-tuple-element.20), channel_id=1, source_target_pairs={{0,8},{4,12},{8,0},{12,4},{1,9},{5,13},{9,1},{13,5},{2,10},{6,14},... | collective-permute-start | bytes 344072 | tf_op jit(solution)/shard_map/ppermute | solution.py:156
  45.2 7.8 %collective-permute-start.23 = (bf16[8,7168]{1,0:T(8,128)(2,1)S(1)}, bf16[8,7168]{1,0:T(8,128)(2,1)S(1)}, u32[]{:S(2)}, u32[]{:S(2)}) collective-permute-start(bf16[8,7168]{1,0:T(8,128)(2,1)S(1)} %add_convert_fusion.5), channel_id=1, source_target_pairs={{0,2},{1,3},{2,0},{3,1},{4,6},{5,7},{6,4},{7,5},{8,10},{9,11},{10,... | collective-permute-start | bytes 344072 | tf_op jit(solution)/shard_map/ppermute | solution.py:160
  48.2 4.8 %collective-permute-start.20 = (bf16[8,7168]{1,0:T(8,128)(2,1)S(1)}, bf16[8,7168]{1,0:T(8,128)(2,1)S(1)}, u32[]{:S(2)}, u32[]{:S(2)}) collective-permute-start(bf16[8,7168]{1,0:T(8,128)(2,1)S(1)} %get-tuple-element.19), channel_id=1, source_target_pairs={{0,8},{4,12},{8,0},{12,4},{1,9},{5,13},{9,1},{13,5},{2,10},{6,14},... | collective-permute-start | bytes 344072 | tf_op jit(solution)/shard_map/ppermute | solution.py:156
  49.7 4.9 %collective-permute-start.22 = (bf16[8,7168]{1,0:T(8,128)(2,1)S(1)}, bf16[8,7168]{1,0:T(8,128)(2,1)S(1)}, u32[]{:S(2)}, u32[]{:S(2)}) collective-permute-start(bf16[8,7168]{1,0:T(8,128)(2,1)S(1)} %add_convert_fusion.3), channel_id=1, source_target_pairs={{0,1},{1,0},{2,3},{3,2},{4,5},{5,4},{6,7},{7,6},{8,9},{9,8},{10,11... | collective-permute-start | bytes 344072 | tf_op jit(solution)/shard_map/ppermute | solution.py:160

commit v6 on v5

--- a/solution.py
+++ b/solution.py
@@ -111,19 +111,18 @@
     )(*pieces, w_gate, w_up)
 
 
-def down_kernel(chunk, hidden_ref, down_ref, far_ref, near_ref, *keep_refs):
-    part, width = far_ref.shape
-    outs = (*keep_refs, near_ref, far_ref)
+def down_kernel(chunk, hidden_ref, down_ref, other_ref, here_ref):
+    half, width = here_ref.shape
 
     @pl.loop(0, width // DOWN_TILE)
     def _(step):
-        here = pl.ds(pl.multiple_of(step * DOWN_TILE, DOWN_TILE), DOWN_TILE)
+        at = pl.ds(pl.multiple_of(step * DOWN_TILE, DOWN_TILE), DOWN_TILE)
         there = pl.ds(pl.multiple_of(chunk * width + step * DOWN_TILE, DOWN_TILE), DOWN_TILE)
         total = jnp.dot(
             hidden_ref[...], down_ref[:, there], preferred_element_type=jnp.float32
         ).astype(jnp.bfloat16)
-        for i, ref in enumerate(outs):
-            ref[:, here] = total[i * part : (i + 1) * part]
+        here_ref[:, at] = total[:half]
+        other_ref[:, at] = total[half:]
 
 
 def down(hidden, w_down, chunk, chunks):
@@ -132,9 +131,9 @@
     vmem = pl.BlockSpec(memory_space=pltpu.VMEM)
     return pl.pallas_call(
         functools.partial(down_kernel, chunk),
-        out_shape=[jax.ShapeDtypeStruct((rows // 4, width // chunks), jnp.bfloat16)] * 4,
+        out_shape=[jax.ShapeDtypeStruct((rows // 2, width // chunks), jnp.bfloat16)] * 2,
         in_specs=[vmem, vmem],
-        out_specs=[vmem] * 4,
+        out_specs=[vmem, vmem],
         compiler_params=pltpu.CompilerParams(vmem_limit_bytes=VMEM_LIMIT),
         cost_estimate=pl.CostEstimate(
             flops=2 * rows * units * width // chunks,
@@ -146,6 +145,7 @@
 
 
 CHIPS, PLACES = 2, 4
+GATHER_ORDER = (0, 2, 4, 5, 1, 3, 6, 7)
 
 
 def to_core(value):
@@ -166,33 +166,33 @@
     return lax.ppermute(value, ("node", "local"), perm)
 
 
-def add(*terms):
-    return sum(term.astype(jnp.float32) for term in terms).astype(jnp.bfloat16)
-
-
 def after(value, *others):
     return lax.optimization_barrier((value, *others))[0]
 
 
 def gather_blocks(own):
-    second = to_place(own, 2)
-    first = to_place(own, 1)
-    far_own = to_chip(own)
+    second, far_own = to_place(own, 2), to_chip(own)
+    far_first, first = to_both(own, 1), to_place(own, 1)
+    other = [to_core(own), to_core(far_own), to_core(first)]
     far_second, far_third, third = to_chip(second), to_both(second, 1), to_place(second, 1)
-    far_first = to_chip(after(first, second))
-    chip = [own, first, second, third, far_own, far_first, far_second, far_third]
-    ready = [own, first, after(second, third), third, *chip[PLACES:]]
-    return chip + [to_core(piece) for piece in ready]
-
-
-def reduce_blocks(other_far, other_near, near, far, rows):
-    far = add(far, to_core(other_far)).reshape(PLACES, rows, -1)
-    near = add(near, to_core(other_near)).reshape(PLACES, rows, -1)
-    second = add(near[2], to_both(far[3], 1), to_chip(far[2]), to_place(near[3], 1))
-    second_here = to_place(second, 2)
-    first = add(near[1], to_chip(after(far[1], second)))
-    own = add(near[0], to_chip(after(far[0], second)))
-    return add(own, to_place(first, 1), second_here)
+    other += [to_core(after(piece, third)) for piece in (far_first, second)]
+    other += [to_core(piece) for piece in (third, far_second, far_third)]
+    chip = [own, far_own, first, far_first, second, third, far_second, far_third]
+    return [chip[i] for i in GATHER_ORDER] + [other[i] for i in GATHER_ORDER]
+
+
+def total(*terms):
+    return sum(term.astype(jnp.float32) for term in terms)
+
+
+def reduce_blocks(other, here, rows):
+    sums = total(here, to_core(other)).astype(jnp.bfloat16).reshape(2 * PLACES, rows, -1)
+    near, far = sums[:PLACES], sums[PLACES:]
+    second = total(near[2], to_chip(far[2]), to_both(far[3], 1), to_place(near[3], 1))
+    second = second.astype(jnp.bfloat16)
+    own = total(near[0], after(to_place(near[1], 1), second))
+    far_own, far_first = to_chip(after(far[0], own)), to_both(after(far[1], own), 1)
+    return total(own, to_place(second, 2), far_own, far_first).astype(jnp.bfloat16)
 
 
 def by_permutes(tokens, expert_ids, route_weights, expert_slot, w_gate, w_up, w_down):

time: 55.4 us -> 54.8 us (0.989)
    ppermute x6 -> x4, waiting for transfers between devices: 9.88 us -> 3.58 us  [to_chip(): return lax.ppermute(value, 'node', [(i, i ^ 2) for i in range(2 * CHIPS)])]
    ppermute x2 -> x4, starting transfers between devices: 3.45 us -> 7.91 us  [to_both(): return lax.ppermute(value, ('node', 'local'), perm)]
    ppermute x2 -> x4, waiting for transfers between devices: 2.76 us -> 6.56 us  [to_both(): return lax.ppermute(value, ('node', 'local'), perm)]
    ppermute x6 -> x4, starting transfers between devices: 6.67 us -> 3.77 us  [to_chip(): return lax.ppermute(value, 'node', [(i, i ^ 2) for i in range(2 * CHIPS)])]
    ppermute x6, starting transfers between devices: 11.2 us -> 9.6 us  [to_place(): return lax.ppermute(value, 'local', [(i, i ^ bits) for i in range(PLACES)])]
    ppermute x10 -> x9, waiting for transfers between devices: 2.29 us -> 3.56 us  [to_core(): return lax.ppermute(value, 'node', [(i, i ^ 1) for i in range(2 * CHIPS)])]
    ppermute x6, waiting for transfers between devices: 7.01 us -> 8.03 us  [to_place(): return lax.ppermute(value, 'local', [(i, i ^ bits) for i in range(PLACES)])]
    ppermute x10 -> x9, starting transfers between devices: 1.6 us -> 1.34 us  [to_core(): return lax.ppermute(value, 'node', [(i, i ^ 1) for i in range(2 * CHIPS)])]
  transfers between devices with their start and end apart: 24 -> 23, of which waited for: 12 -> 15; matrix products, arithmetic and copies ran while one was open for 1% -> 0% of each run, Pallas kernels for 0% -> 0%
where the time goes in v6:
time: 54.8 us; the launch traced here: 54.7 us
  starting transfers between devices  22.6 us (41%)
  waiting for transfers between devices  21.7 us (40%)
  Pallas kernels  9.14 us (17%)
  other arithmetic  0.99 us (2%)
    ppermute x6, starting transfers between devices, to_place(): return lax.ppermute(value, 'local', [(i, i ^ bits) for i in range(PLACES)])  9.6 us
    ppermute x6, waiting for transfers between devices, to_place(): return lax.ppermute(value, 'local', [(i, i ^ bits) for i in range(PLACES)])  8.03 us
    ppermute x4, starting transfers between devices, to_both(): return lax.ppermute(value, ('node', 'local'), perm)  7.91 us
    ppermute x4, waiting for transfers between devices, to_both(): return lax.ppermute(value, ('node', 'local'), perm)  6.56 us
    pallas_call x1, Pallas kernels, hidden_units(): pl.pallas_call(functools.partial(hidden_kernel, experts), out_shape=jax.S...  5.29 us
    ppermute x4, starting transfers between devices, to_chip(): return lax.ppermute(value, 'node', [(i, i ^ 2) for i in range(2 * CHIPS)])  3.77 us
    ppermute x4, waiting for transfers between devices, to_chip(): return lax.ppermute(value, 'node', [(i, i ^ 2) for i in range(2 * CHIPS)])  3.58 us
    ppermute x9, waiting for transfers between devices, to_core(): return lax.ppermute(value, 'node', [(i, i ^ 1) for i in range(2 * CHIPS)])  3.56 us
  transfers between devices with their start and end apart: 23, of which 15 were waited for; matrix products, arithmetic and copies ran while one was open for 0% of the time, Pallas kernels for 0%

profile of v6, /device:TPU:0, one launch (start us, length us, event | category | flops | bytes accessed | tf_op | source)
XLA Modules:
  0.0 54.7 jit_solution(8156011559272188881)
XLA Ops:
  0.0 0.0 copy-start
  0.0 0.0 copy-start.1
  0.0 0.0 slice-start
  0.0 0.0 slice-start.1
  0.0 0.0 slice-start.2
  0.0 1.2 %pack.1.refs_0_ = bf16[8,7296]{1,0:T(8,128)(2,1)S(1)} custom-call(bf16[8,7168]{1,0:T(8,128)(2,1)} %refs_0_.1, s32[4,8]{1,0:T(4,128)} %bitcast.6, f32[4,8]{1,0:T(4,128)} %bitcast.7, s32[8]{0:T(128)} %refs_3_.1, bf16[2,7168,512]{2,1,0:T(8,128)(2,1)} %refs_16_.1, bf16[2,7168,512]{2,1,0:T(8,128)(2,1)} %refs_17_.1, bf16[2,512,7168]{2,1,0:T(8,128)(2,1)} %refs_6_.1), custom_call_target="tpu_custom_call" | custom-call | tf_op jit(solution)/shard_map/pack/pallas_call | solution.py:50
  1.2 0.0 slice-start.3
  1.2 4.1 %collective-permute-start.1 = (bf16[8,7296]{1,0:T(8,128)(2,1)S(1)}, bf16[8,7296]{1,0:T(8,128)(2,1)S(1)}, u32[]{:S(2)}, u32[]{:S(2)}) collective-permute-start(bf16[8,7296]{1,0:T(8,128)(2,1)S(1)} %pack.1.refs_0_), channel_id=1, source_target_pairs={{0,2},{1,3},{2,0},{3,1},{4,6},{5,7},{6,4},{7,5},{8,10},{9,11},{10,... | collective-permute-start | bytes 350216 | tf_op jit(solution)/shard_map/ppermute | solution.py:160
  5.3 2.5 %collective-permute-start.4 = (bf16[8,7296]{1,0:T(8,128)(2,1)S(1)}, bf16[8,7296]{1,0:T(8,128)(2,1)S(1)}, u32[]{:S(2)}, u32[]{:S(2)}) collective-permute-start(bf16[8,7296]{1,0:T(8,128)(2,1)S(1)} %pack.1.refs_0_), channel_id=1, source_target_pairs={{0,9},{1,8},{2,11},{3,10},{4,13},{5,12},{6,15},{7,14},{8,1},{9,0},... | collective-permute-start | bytes 350216 | tf_op jit(solution)/shard_map/ppermute | solution.py:166
  7.8 0.5 collective-permute-start.3
  8.4 0.4 collective-permute-start
  8.8 2.3 %collective-permute-done.1.refs_2_ = bf16[8,7296]{1,0:T(8,128)(2,1)S(1)} collective-permute-done((bf16[8,7296]{1,0:T(8,128)(2,1)S(1)}, bf16[8,7296]{1,0:T(8,128)(2,1)S(1)}, u32[]{:S(2)}, u32[]{:S(2)}) %collective-permute-start.1) | collective-permute-done | bytes 116768 | tf_op jit(solution)/shard_map/ppermute | solution.py:160
  11.1 0.7 %collective-permute-start.2 = (bf16[8,7296]{1,0:T(8,128)(2,1)S(1)}, bf16[8,7296]{1,0:T(8,128)(2,1)S(1)}, u32[]{:S(2)}, u32[]{:S(2)}) collective-permute-start(bf16[8,7296]{1,0:T(8,128)(2,1)S(1)} %collective-permute-done.1.refs_2_), channel_id=1, source_target_pairs={{0,1},{1,0},{2,3},{3,2},{4,5},{5,4},{6,7},{7,6},{8,9},{9,8},{10,11... | collective-permute-start | bytes 350216 | tf_op jit(solution)/shard_map/ppermute | solution.py:160
  11.8 0.0 collective-permute-start.7
  11.8 1.2 %collective-permute-done.4.refs_5_ = bf16[8,7296]{1,0:T(8,128)(2,1)S(1)} collective-permute-done((bf16[8,7296]{1,0:T(8,128)(2,1)S(1)}, bf16[8,7296]{1,0:T(8,128)(2,1)S(1)}, u32[]{:S(2)}, u32[]{:S(2)}) %collective-permute-start.4) | collective-permute-done | bytes 116768 | tf_op jit(solution)/shard_map/ppermute | solution.py:166
  13.0 1.9 %collective-permute-start.6 = (bf16[8,7296]{1,0:T(8,128)(2,1)S(1)}, bf16[8,7296]{1,0:T(8,128)(2,1)S(1)}, u32[]{:S(2)}, u32[]{:S(2)}) collective-permute-start(bf16[8,7296]{1,0:T(8,128)(2,1)S(1)} %collective-permute-done.1.refs_2_), channel_id=1, source_target_pairs={{0,9},{1,8},{2,11},{3,10},{4,13},{5,12},{6,15},{7,14},{8,1},{9,0},... | collective-permute-start | bytes 350216 | tf_op jit(solution)/shard_map/ppermute | solution.py:166
  14.9 0.0 collective-permute-done.3.refs_4_
  14.9 1.4 %collective-permute-start.5 = (bf16[8,7296]{1,0:T(8,128)(2,1)S(1)}, bf16[8,7296]{1,0:T(8,128)(2,1)S(1)}, u32[]{:S(2)}, u32[]{:S(2)}) collective-permute-start(bf16[8,7296]{1,0:T(8,128)(2,1)S(1)} %collective-permute-done.1.refs_2_), channel_id=1, source_target_pairs={{0,8},{4,12},{8,0},{12,4},{1,9},{5,13},{9,1},{13,5},{2,10},{6,14},... | collective-permute-start | bytes 350216 | tf_op jit(solution)/shard_map/ppermute | solution.py:156
  16.3 0.0 collective-permute-done.refs_1_
  16.3 0.0 collective-permute-start.11
  16.3 1.8 %collective-permute-done.2.refs_3_ = bf16[8,7296]{1,0:T(8,128)(2,1)S(1)} collective-permute-done((bf16[8,7296]{1,0:T(8,128)(2,1)S(1)}, bf16[8,7296]{1,0:T(8,128)(2,1)S(1)}, u32[]{:S(2)}, u32[]{:S(2)}) %collective-permute-start.2) | collective-permute-done | bytes 116768 | tf_op jit(solution)/shard_map/ppermute | solution.py:160
  18.1 0.0 collective-permute-start.8
  18.1 0.0 collective-permute-done.7.refs_8_
  18.1 0.5 collective-permute-start.9
  18.6 1.3 %collective-permute-done.6.refs_7_ = bf16[8,7296]{1,0:T(8,128)(2,1)S(1)} collective-permute-done((bf16[8,7296]{1,0:T(8,128)(2,1)S(1)}, bf16[8,7296]{1,0:T(8,128)(2,1)S(1)}, u32[]{:S(2)}, u32[]{:S(2)}) %collective-permute-start.6) | collective-permute-done | bytes 116768 | tf_op jit(solution)/shard_map/ppermute | solution.py:166
  19.9 0.0 collective-permute-start.14
  19.9 1.8 %collective-permute-done.5.refs_6_ = bf16[8,7296]{1,0:T(8,128)(2,1)S(1)} collective-permute-done((bf16[8,7296]{1,0:T(8,128)(2,1)S(1)}, bf16[8,7296]{1,0:T(8,128)(2,1)S(1)}, u32[]{:S(2)}, u32[]{:S(2)}) %collective-permute-start.5) | collective-permute-done | bytes 116768 | tf_op jit(solution)/shard_map/ppermute | solution.py:156
  21.7 0.0 collective-permute-start.13
  21.7 0.0 collective-permute-done.11.refs_12_
  21.7 0.5 collective-permute-start.12
  22.2 0.0 collective-permute-done.8.refs_9_
  22.2 0.1 collective-permute-start.10
  22.3 0.0 collective-permute-done.14.refs_15_
  22.3 0.7 %collective-permute-done.13.refs_14_ = bf16[8,7296]{1,0:T(8,128)(2,1)S(1)} collective-permute-done((bf16[8,7296]{1,0:T(8,128)(2,1)S(1)}, bf16[8,7296]{1,0:T(8,128)(2,1)S(1)}, u32[]{:S(2)}, u32[]{:S(2)}) %collective-permute-start.13) | collective-permute-done | bytes 116768 | tf_op jit(solution)/shard_map/ppermute | solution.py:152
  23.0 0.0 collective-permute-done.9.refs_10_
  23.0 0.2 collective-permute-done.12.refs_13_
  23.2 0.4 collective-permute-done.10.refs_11_
  23.5 0.0 copy-done
  23.5 0.0 copy-done.1
  23.5 5.3 %hidden.1.hidden_ref = bf16[128,1024]{1,0:T(8,128)(2,1)S(1)} custom-call(bf16[8,7296]{1,0:T(8,128)(2,1)S(1)} %pack.1.refs_0_, bf16[8,7296]{1,0:T(8,128)(2,1)S(1)} %collective-permute-done.refs_1_, bf16[8,7296]{1,0:T(8,128)(2,1)S(1)} %collective-permute-done.1.refs_2_, bf16[8,7296]{1,0:T(8,128)(2,1)S(1)} %collective-permute-done.2.refs_3_, ...), custom_call_target="tpu_custom_call" | custom-call | flops 3758096384 | bytes 29360128 | tf_op jit(solution)/shard_map/hidden/pallas_call | solution.py:95
  28.8 0.0 slice-done
  28.8 0.0 slice-done.1
  28.8 0.0 slice-done.2
  28.9 0.0 slice-done.3
  28.9 2.7 %down.1 = (bf16[64,7168]{1,0:T(8,128)(2,1)S(1)}, bf16[64,7168]{1,0:T(8,128)(2,1)S(1)}) custom-call(bf16[128,1024]{1,0:T(8,128)(2,1)S(1)} %hidden.1.hidden_ref, bf16[1024,7168]{1,0:T(8,128)(2,1)S(1)} %bitcast.5), custom_call_target="tpu_custom_call" | custom-call | flops 1879048192 | bytes 14680064 | tf_op jit(solution)/shard_map/down/pallas_call | solution.py:132
  31.6 0.2 collective-permute-start.15
  31.8 2.3 %collective-permute-done.15 = bf16[64,7168]{1,0:T(8,128)(2,1)S(1)} collective-permute-done((bf16[64,7168]{1,0:T(8,128)(2,1)S(1)}, bf16[64,7168]{1,0:T(8,128)(2,1)S(1)}, u32[]{:S(2)}, u32[]{:S(2)}) %collective-permute-start.15) | collective-permute-done | bytes 917536 | tf_op jit(solution)/shard_map/ppermute | solution.py:152
  34.1 0.2 add_convert_fusion
  34.4 1.0 %collective-permute-start.19 = (bf16[8,7168]{1,0:T(8,128)(2,1)S(1)}, bf16[8,7168]{1,0:T(8,128)(2,1)S(1)}, u32[]{:S(2)}, u32[]{:S(2)}) collective-permute-start(bf16[8,7168]{1,0:T(8,128)(2,1)S(1)} %get-tuple-element.21), channel_id=1, source_target_pairs={{0,1},{1,0},{2,3},{3,2},{4,5},{5,4},{6,7},{7,6},{8,9},{9,8},{10,11... | collective-permute-start | bytes 344072 | tf_op jit(solution)/shard_map/ppermute | solution.py:160
  35.3 1.3 %collective-permute-start.18 = (bf16[8,7168]{1,0:T(8,128)(2,1)S(1)}, bf16[8,7168]{1,0:T(8,128)(2,1)S(1)}, u32[]{:S(2)}, u32[]{:S(2)}) collective-permute-start(bf16[8,7168]{1,0:T(8,128)(2,1)S(1)} %get-tuple-element.22), channel_id=1, source_target_pairs={{0,9},{1,8},{2,11},{3,10},{4,13},{5,12},{6,15},{7,14},{8,1},{9,0},... | collective-permute-start | bytes 344072 | tf_op jit(solution)/shard_map/ppermute | solution.py:166
  36.7 1.2 %collective-permute-start.17 = (bf16[8,7168]{1,0:T(8,128)(2,1)S(1)}, bf16[8,7168]{1,0:T(8,128)(2,1)S(1)}, u32[]{:S(2)}, u32[]{:S(2)}) collective-permute-start(bf16[8,7168]{1,0:T(8,128)(2,1)S(1)} %get-tuple-element.23), channel_id=1, source_target_pairs={{0,8},{4,12},{8,0},{12,4},{1,9},{5,13},{9,1},{13,5},{2,10},{6,14},... | collective-permute-start | bytes 344072 | tf_op jit(solution)/shard_map/ppermute | solution.py:156
  37.9 0.9 %collective-permute-start.16 = (bf16[8,7168]{1,0:T(8,128)(2,1)S(1)}, bf16[8,7168]{1,0:T(8,128)(2,1)S(1)}, u32[]{:S(2)}, u32[]{:S(2)}) collective-permute-start(bf16[8,7168]{1,0:T(8,128)(2,1)S(1)} %get-tuple-element.24), channel_id=1, source_target_pairs={{0,1},{1,0},{2,3},{3,2},{4,5},{5,4},{6,7},{7,6},{8,9},{9,8},{10,11... | collective-permute-start | bytes 344072 | tf_op jit(solution)/shard_map/ppermute | solution.py:160
  38.8 1.6 %collective-permute-done.19 = bf16[8,7168]{1,0:T(8,128)(2,1)S(1)} collective-permute-done((bf16[8,7168]{1,0:T(8,128)(2,1)S(1)}, bf16[8,7168]{1,0:T(8,128)(2,1)S(1)}, u32[]{:S(2)}, u32[]{:S(2)}) %collective-permute-start.19) | collective-permute-done | bytes 114720 | tf_op jit(solution)/shard_map/ppermute | solution.py:160
  40.4 2.7 %collective-permute-done.18 = bf16[8,7168]{1,0:T(8,128)(2,1)S(1)} collective-permute-done((bf16[8,7168]{1,0:T(8,128)(2,1)S(1)}, bf16[8,7168]{1,0:T(8,128)(2,1)S(1)}, u32[]{:S(2)}, u32[]{:S(2)}) %collective-permute-start.18) | collective-permute-done | bytes 114720 | tf_op jit(solution)/shard_map/ppermute | solution.py:166
  43.1 0.7 %collective-permute-done.17 = bf16[8,7168]{1,0:T(8,128)(2,1)S(1)} collective-permute-done((bf16[8,7168]{1,0:T(8,128)(2,1)S(1)}, bf16[8,7168]{1,0:T(8,128)(2,1)S(1)}, u32[]{:S(2)}, u32[]{:S(2)}) %collective-permute-start.17) | collective-permute-done | bytes 114720 | tf_op jit(solution)/shard_map/ppermute | solution.py:156
  43.8 0.1 add_convert_fusion.2
  43.9 2.5 %collective-permute-start.20 = (bf16[8,7168]{1,0:T(8,128)(2,1)S(1)}, bf16[8,7168]{1,0:T(8,128)(2,1)S(1)}, u32[]{:S(2)}, u32[]{:S(2)}) collective-permute-start(bf16[8,7168]{1,0:T(8,128)(2,1)S(1)} %add_convert_fusion.2), channel_id=1, source_target_pairs={{0,2},{1,3},{2,0},{3,1},{4,6},{5,7},{6,4},{7,5},{8,10},{9,11},{10,... | collective-permute-start | bytes 344072 | tf_op jit(solution)/shard_map/ppermute | solution.py:160
  46.4 0.0 collective-permute-done.16
  46.4 2.2 %collective-permute-start.22 = (bf16[8,7168]{1,0:T(8,128)(2,1)S(1)}, bf16[8,7168]{1,0:T(8,128)(2,1)S(1)}, u32[]{:S(2)}, u32[]{:S(2)}) collective-permute-start(bf16[8,7168]{1,0:T(8,128)(2,1)S(1)} %get-tuple-element.18), channel_id=1, source_target_pairs={{0,9},{1,8},{2,11},{3,10},{4,13},{5,12},{6,15},{7,14},{8,1},{9,0},... | collective-permute-start | bytes 344072 | tf_op jit(solution)/shard_map/ppermute | solution.py:166
  48.5 0.6 %collective-permute-start.21 = (bf16[8,7168]{1,0:T(8,128)(2,1)S(1)}, bf16[8,7168]{1,0:T(8,128)(2,1)S(1)}, u32[]{:S(2)}, u32[]{:S(2)}) collective-permute-start(bf16[8,7168]{1,0:T(8,128)(2,1)S(1)} %get-tuple-element.17), channel_id=1, source_target_pairs={{0,8},{4,12},{8,0},{12,4},{1,9},{5,13},{9,1},{13,5},{2,10},{6,14},... | collective-permute-start | bytes 344072 | tf_op jit(solution)/shard_map/ppermute | solution.py:156
  49.1 2.3 %collective-permute-done.20 = bf16[8,7168]{1,0:T(8,128)(2,1)S(1)} collective-permute-done((bf16[8,7168]{1,0:T(8,128)(2,1)S(1)}, bf16[8,7168]{1,0:T(8,128)(2,1)S(1)}, u32[]{:S(2)}, u32[]{:S(2)}) %collective-permute-start.20) | collective-permute-done | bytes 114720 | tf_op jit(solution)/shard_map/ppermute | solution.py:160
  51.5 1.4 %collective-permute-done.22 = bf16[8,7168]{1,0:T(8,128)(2,1)S(1)} collective-permute-done((bf16[8,7168]{1,0:T(8,128)(2,1)S(1)}, bf16[8,7168]{1,0:T(8,128)(2,1)S(1)}, u32[]{:S(2)}, u32[]{:S(2)}) %collective-permute-start.22) | collective-permute-done | bytes 114720 | tf_op jit(solution)/shard_map/ppermute | solution.py:166
  52.8 1.1 %collective-permute-done.21 = bf16[8,7168]{1,0:T(8,128)(2,1)S(1)} collective-permute-done((bf16[8,7168]{1,0:T(8,128)(2,1)S(1)}, bf16[8,7168]{1,0:T(8,128)(2,1)S(1)}, u32[]{:S(2)}, u32[]{:S(2)}) %collective-permute-start.21) | collective-permute-done | bytes 114720 | tf_op jit(solution)/shard_map/ppermute | solution.py:156
  54.0 0.7 %add_convert_fusion.1 = bf16[8,7168]{1,0:T(8,128)(2,1)} fusion(bf16[8,7168]{1,0:T(8,128)(2,1)S(1)} %collective-permute-done.22, bf16[8,7168]{1,0:T(8,128)(2,1)S(1)} %collective-permute-done.21, bf16[8,7168]{1,0:T(8,128)(2,1)S(1)} %collective-permute-done.20, bf16[8,7168]{1,0:T(8,128)(2,1)S(1)} %collective-permute-done.16, bf16[64,7168]{1,0:T(8,128)(2,1)S(1)} %add_convert_fusion), kind=kLoop, calls=%fused_computation.1 | loop fusion | flops 573440 | bytes 688128 | tf_op jit(solution)/shard_map/convert_element_type | solution.py:195
  (2 shorter events, 0.0 us)
Async XLA Ops:
  0.0 23.5 %copy-start = (bf16[2,7168,512]{2,1,0:T(8,128)(2,1)S(1)}, bf16[2,7168,512]{2,1,0:T(8,128)(2,1)}, u32[]{:S(2)}) copy-start(bf16[2,7168,512]{2,1,0:T(8,128)(2,1)} %refs_16_.1) | copy-start | bytes 44040196
  0.0 23.5 %copy-start.1 = (bf16[2,7168,512]{2,1,0:T(8,128)(2,1)S(1)}, bf16[2,7168,512]{2,1,0:T(8,128)(2,1)}, u32[]{:S(2)}) copy-start(bf16[2,7168,512]{2,1,0:T(8,128)(2,1)} %refs_17_.1) | copy-start | bytes 44040196
  0.0 28.8 %slice-start = ((s8[14680064]{0:T(1024)(128)(4,1)}), s8[4194304]{0:T(1024)(128)(4,1)S(1)}, s32[]{:S(2)}) async-start(s8[14680064]{0:T(1024)(128)(4,1)} %bitcast.3), calls=%async_computation | async-start | bytes 8388608
  0.0 28.8 %slice-start.1 = ((s8[14680064]{0:T(1024)(128)(4,1)}), s8[4194304]{0:T(1024)(128)(4,1)S(1)}, s32[]{:S(2)}) async-start(s8[14680064]{0:T(1024)(128)(4,1)} %bitcast.3), calls=%async_computation.1 | async-start | bytes 8388608
  0.0 28.8 %slice-start.2 = ((s8[14680064]{0:T(1024)(128)(4,1)}), s8[4194304]{0:T(1024)(128)(4,1)S(1)}, s32[]{:S(2)}) async-start(s8[14680064]{0:T(1024)(128)(4,1)} %bitcast.3), calls=%async_computation.2 | async-start | bytes 8388608
  1.2 27.7 %slice-start.3 = ((s8[14680064]{0:T(1024)(128)(4,1)}), s8[2097152]{0:T(1024)(128)(4,1)S(1)}, s32[]{:S(2)}) async-start(s8[14680064]{0:T(1024)(128)(4,1)} %bitcast.3), calls=%async_computation.3 | async-start | bytes 4194304
  1.2 9.9 %collective-permute-start.1 = (bf16[8,7296]{1,0:T(8,128)(2,1)S(1)}, bf16[8,7296]{1,0:T(8,128)(2,1)S(1)}, u32[]{:S(2)}, u32[]{:S(2)}) collective-permute-start(bf16[8,7296]{1,0:T(8,128)(2,1)S(1)} %pack.1.refs_0_), channel_id=1, source_target_pairs={{0,2},{1,3},{2,0},{3,1},{4,6},{5,7},{6,4},{7,5},{8,10},{9,11},{10,... | collective-permute-start | bytes 350216 | tf_op jit(solution)/shard_map/ppermute | solution.py:160
  5.3 7.7 %collective-permute-start.4 = (bf16[8,7296]{1,0:T(8,128)(2,1)S(1)}, bf16[8,7296]{1,0:T(8,128)(2,1)S(1)}, u32[]{:S(2)}, u32[]{:S(2)}) collective-permute-start(bf16[8,7296]{1,0:T(8,128)(2,1)S(1)} %pack.1.refs_0_), channel_id=1, source_target_pairs={{0,9},{1,8},{2,11},{3,10},{4,13},{5,12},{6,15},{7,14},{8,1},{9,0},... | collective-permute-start | bytes 350216 | tf_op jit(solution)/shard_map/ppermute | solution.py:166
  7.8 7.1 %collective-permute-start.3 = (bf16[8,7296]{1,0:T(8,128)(2,1)S(1)}, bf16[8,7296]{1,0:T(8,128)(2,1)S(1)}, u32[]{:S(2)}, u32[]{:S(2)}) collective-permute-start(bf16[8,7296]{1,0:T(8,128)(2,1)S(1)} %pack.1.refs_0_), channel_id=1, source_target_pairs={{0,8},{4,12},{8,0},{12,4},{1,9},{5,13},{9,1},{13,5},{2,10},{6,14},... | collective-permute-start | bytes 350216 | tf_op jit(solution)/shard_map/ppermute | solution.py:156
  8.4 7.9 %collective-permute-start = (bf16[8,7296]{1,0:T(8,128)(2,1)S(1)}, bf16[8,7296]{1,0:T(8,128)(2,1)S(1)}, u32[]{:S(2)}, u32[]{:S(2)}) collective-permute-start(bf16[8,7296]{1,0:T(8,128)(2,1)S(1)} %pack.1.refs_0_), channel_id=1, source_target_pairs={{0,1},{1,0},{2,3},{3,2},{4,5},{5,4},{6,7},{7,6},{8,9},{9,8},{10,11... | collective-permute-start | bytes 350216 | tf_op jit(solution)/shard_map/ppermute | solution.py:160
  11.1 7.0 %collective-permute-start.2 = (bf16[8,7296]{1,0:T(8,128)(2,1)S(1)}, bf16[8,7296]{1,0:T(8,128)(2,1)S(1)}, u32[]{:S(2)}, u32[]{:S(2)}) collective-permute-start(bf16[8,7296]{1,0:T(8,128)(2,1)S(1)} %collective-permute-done.1.refs_2_), channel_id=1, source_target_pairs={{0,1},{1,0},{2,3},{3,2},{4,5},{5,4},{6,7},{7,6},{8,9},{9,8},{10,11... | collective-permute-start | bytes 350216 | tf_op jit(solution)/shard_map/ppermute | solution.py:160
  11.8 6.3 %collective-permute-start.7 = (bf16[8,7296]{1,0:T(8,128)(2,1)S(1)}, bf16[8,7296]{1,0:T(8,128)(2,1)S(1)}, u32[]{:S(2)}, u32[]{:S(2)}) collective-permute-start(bf16[8,7296]{1,0:T(8,128)(2,1)S(1)} %pack.1.refs_0_), channel_id=1, source_target_pairs={{0,4},{4,0},{8,12},{12,8},{1,5},{5,1},{9,13},{13,9},{2,6},{6,2},{1... | collective-permute-start | bytes 350216 | tf_op jit(solution)/shard_map/ppermute | solution.py:152
  13.0 6.9 %collective-permute-start.6 = (bf16[8,7296]{1,0:T(8,128)(2,1)S(1)}, bf16[8,7296]{1,0:T(8,128)(2,1)S(1)}, u32[]{:S(2)}, u32[]{:S(2)}) collective-permute-start(bf16[8,7296]{1,0:T(8,128)(2,1)S(1)} %collective-permute-done.1.refs_2_), channel_id=1, source_target_pairs={{0,9},{1,8},{2,11},{3,10},{4,13},{5,12},{6,15},{7,14},{8,1},{9,0},... | collective-permute-start | bytes 350216 | tf_op jit(solution)/shard_map/ppermute | solution.py:166
  14.9 6.8 %collective-permute-start.5 = (bf16[8,7296]{1,0:T(8,128)(2,1)S(1)}, bf16[8,7296]{1,0:T(8,128)(2,1)S(1)}, u32[]{:S(2)}, u32[]{:S(2)}) collective-permute-start(bf16[8,7296]{1,0:T(8,128)(2,1)S(1)} %collective-permute-done.1.refs_2_), channel_id=1, source_target_pairs={{0,8},{4,12},{8,0},{12,4},{1,9},{5,13},{9,1},{13,5},{2,10},{6,14},... | collective-permute-start | bytes 350216 | tf_op jit(solution)/shard_map/ppermute | solution.py:156
  16.3 5.4 %collective-permute-start.11 = (bf16[8,7296]{1,0:T(8,128)(2,1)S(1)}, bf16[8,7296]{1,0:T(8,128)(2,1)S(1)}, u32[]{:S(2)}, u32[]{:S(2)}) collective-permute-start(bf16[8,7296]{1,0:T(8,128)(2,1)S(1)} %collective-permute-done.3.refs_4_), channel_id=1, source_target_pairs={{0,4},{4,0},{8,12},{12,8},{1,5},{5,1},{9,13},{13,9},{2,6},{6,2},{1... | collective-permute-start | bytes 350216 | tf_op jit(solution)/shard_map/ppermute | solution.py:152
  18.1 4.1 %collective-permute-start.8 = (bf16[8,7296]{1,0:T(8,128)(2,1)S(1)}, bf16[8,7296]{1,0:T(8,128)(2,1)S(1)}, u32[]{:S(2)}, u32[]{:S(2)}) collective-permute-start(bf16[8,7296]{1,0:T(8,128)(2,1)S(1)} %collective-permute-done.refs_1_), channel_id=1, source_target_pairs={{0,4},{4,0},{8,12},{12,8},{1,5},{5,1},{9,13},{13,9},{2,6},{6,2},{1... | collective-permute-start | bytes 350216 | tf_op jit(solution)/shard_map/ppermute | solution.py:152
  18.1 4.9 %collective-permute-start.9 = (bf16[8,7296]{1,0:T(8,128)(2,1)S(1)}, bf16[8,7296]{1,0:T(8,128)(2,1)S(1)}, u32[]{:S(2)}, u32[]{:S(2)}) collective-permute-start(bf16[8,7296]{1,0:T(8,128)(2,1)S(1)} %collective-permute-done.1.refs_2_), channel_id=1, source_target_pairs={{0,4},{4,0},{8,12},{12,8},{1,5},{5,1},{9,13},{13,9},{2,6},{6,2},{1... | collective-permute-start | bytes 350216 | tf_op jit(solution)/shard_map/ppermute | solution.py:152
  19.9 2.4 %collective-permute-start.14 = (bf16[8,7296]{1,0:T(8,128)(2,1)S(1)}, bf16[8,7296]{1,0:T(8,128)(2,1)S(1)}, u32[]{:S(2)}, u32[]{:S(2)}) collective-permute-start(bf16[8,7296]{1,0:T(8,128)(2,1)S(1)} %collective-permute-done.6.refs_7_), channel_id=1, source_target_pairs={{0,4},{4,0},{8,12},{12,8},{1,5},{5,1},{9,13},{13,9},{2,6},{6,2},{1... | collective-permute-start | bytes 350216 | tf_op jit(solution)/shard_map/ppermute | solution.py:152
  21.7 1.3 %collective-permute-start.13 = (bf16[8,7296]{1,0:T(8,128)(2,1)S(1)}, bf16[8,7296]{1,0:T(8,128)(2,1)S(1)}, u32[]{:S(2)}, u32[]{:S(2)}) collective-permute-start(bf16[8,7296]{1,0:T(8,128)(2,1)S(1)} %collective-permute-done.5.refs_6_), channel_id=1, source_target_pairs={{0,4},{4,0},{8,12},{12,8},{1,5},{5,1},{9,13},{13,9},{2,6},{6,2},{1... | collective-permute-start | bytes 350216 | tf_op jit(solution)/shard_map/ppermute | solution.py:152
  21.7 1.5 %collective-permute-start.12 = (bf16[8,7296]{1,0:T(8,128)(2,1)S(1)}, bf16[8,7296]{1,0:T(8,128)(2,1)S(1)}, u32[]{:S(2)}, u32[]{:S(2)}) collective-permute-start(bf16[8,7296]{1,0:T(8,128)(2,1)S(1)} %collective-permute-done.4.refs_5_), channel_id=1, source_target_pairs={{0,4},{4,0},{8,12},{12,8},{1,5},{5,1},{9,13},{13,9},{2,6},{6,2},{1... | collective-permute-start | bytes 350216 | tf_op jit(solution)/shard_map/ppermute | solution.py:152
  22.2 1.3 %collective-permute-start.10 = (bf16[8,7296]{1,0:T(8,128)(2,1)S(1)}, bf16[8,7296]{1,0:T(8,128)(2,1)S(1)}, u32[]{:S(2)}, u32[]{:S(2)}) collective-permute-start(bf16[8,7296]{1,0:T(8,128)(2,1)S(1)} %collective-permute-done.2.refs_3_), channel_id=1, source_target_pairs={{0,4},{4,0},{8,12},{12,8},{1,5},{5,1},{9,13},{13,9},{2,6},{6,2},{1... | collective-permute-start | bytes 350216 | tf_op jit(solution)/shard_map/ppermute | solution.py:152
  31.6 2.5 %collective-permute-start.15 = (bf16[64,7168]{1,0:T(8,128)(2,1)S(1)}, bf16[64,7168]{1,0:T(8,128)(2,1)S(1)}, u32[]{:S(2)}, u32[]{:S(2)}) collective-permute-start(bf16[64,7168]{1,0:T(8,128)(2,1)S(1)} %get-tuple-element.15), channel_id=1, source_target_pairs={{0,4},{4,0},{8,12},{12,8},{1,5},{5,1},{9,13},{13,9},{2,6},{6,2},{1... | collective-permute-start | bytes 2752520 | tf_op jit(solution)/shard_map/ppermute | solution.py:152
  34.4 6.1 %collective-permute-start.19 = (bf16[8,7168]{1,0:T(8,128)(2,1)S(1)}, bf16[8,7168]{1,0:T(8,128)(2,1)S(1)}, u32[]{:S(2)}, u32[]{:S(2)}) collective-permute-start(bf16[8,7168]{1,0:T(8,128)(2,1)S(1)} %get-tuple-element.21), channel_id=1, source_target_pairs={{0,1},{1,0},{2,3},{3,2},{4,5},{5,4},{6,7},{7,6},{8,9},{9,8},{10,11... | collective-permute-start | bytes 344072 | tf_op jit(solution)/shard_map/ppermute | solution.py:160
  35.3 7.8 %collective-permute-start.18 = (bf16[8,7168]{1,0:T(8,128)(2,1)S(1)}, bf16[8,7168]{1,0:T(8,128)(2,1)S(1)}, u32[]{:S(2)}, u32[]{:S(2)}) collective-permute-start(bf16[8,7168]{1,0:T(8,128)(2,1)S(1)} %get-tuple-element.22), channel_id=1, source_target_pairs={{0,9},{1,8},{2,11},{3,10},{4,13},{5,12},{6,15},{7,14},{8,1},{9,0},... | collective-permute-start | bytes 344072 | tf_op jit(solution)/shard_map/ppermute | solution.py:166
  36.7 7.1 %collective-permute-start.17 = (bf16[8,7168]{1,0:T(8,128)(2,1)S(1)}, bf16[8,7168]{1,0:T(8,128)(2,1)S(1)}, u32[]{:S(2)}, u32[]{:S(2)}) collective-permute-start(bf16[8,7168]{1,0:T(8,128)(2,1)S(1)} %get-tuple-element.23), channel_id=1, source_target_pairs={{0,8},{4,12},{8,0},{12,4},{1,9},{5,13},{9,1},{13,5},{2,10},{6,14},... | collective-permute-start | bytes 344072 | tf_op jit(solution)/shard_map/ppermute | solution.py:156
  37.9 8.4 %collective-permute-start.16 = (bf16[8,7168]{1,0:T(8,128)(2,1)S(1)}, bf16[8,7168]{1,0:T(8,128)(2,1)S(1)}, u32[]{:S(2)}, u32[]{:S(2)}) collective-permute-start(bf16[8,7168]{1,0:T(8,128)(2,1)S(1)} %get-tuple-element.24), channel_id=1, source_target_pairs={{0,1},{1,0},{2,3},{3,2},{4,5},{5,4},{6,7},{7,6},{8,9},{9,8},{10,11... | collective-permute-start | bytes 344072 | tf_op jit(solution)/shard_map/ppermute | solution.py:160
  43.9 7.6 %collective-permute-start.20 = (bf16[8,7168]{1,0:T(8,128)(2,1)S(1)}, bf16[8,7168]{1,0:T(8,128)(2,1)S(1)}, u32[]{:S(2)}, u32[]{:S(2)}) collective-permute-start(bf16[8,7168]{1,0:T(8,128)(2,1)S(1)} %add_convert_fusion.2), channel_id=1, source_target_pairs={{0,2},{1,3},{2,0},{3,1},{4,6},{5,7},{6,4},{7,5},{8,10},{9,11},{10,... | collective-permute-start | bytes 344072 | tf_op jit(solution)/shard_map/ppermute | solution.py:160
  46.4 6.5 %collective-permute-start.22 = (bf16[8,7168]{1,0:T(8,128)(2,1)S(1)}, bf16[8,7168]{1,0:T(8,128)(2,1)S(1)}, u32[]{:S(2)}, u32[]{:S(2)}) collective-permute-start(bf16[8,7168]{1,0:T(8,128)(2,1)S(1)} %get-tuple-element.18), channel_id=1, source_target_pairs={{0,9},{1,8},{2,11},{3,10},{4,13},{5,12},{6,15},{7,14},{8,1},{9,0},... | collective-permute-start | bytes 344072 | tf_op jit(solution)/shard_map/ppermute | solution.py:166
  48.5 5.4 %collective-permute-start.21 = (bf16[8,7168]{1,0:T(8,128)(2,1)S(1)}, bf16[8,7168]{1,0:T(8,128)(2,1)S(1)}, u32[]{:S(2)}, u32[]{:S(2)}) collective-permute-start(bf16[8,7168]{1,0:T(8,128)(2,1)S(1)} %get-tuple-element.17), channel_id=1, source_target_pairs={{0,8},{4,12},{8,0},{12,4},{1,9},{5,13},{9,1},{13,5},{2,10},{6,14},... | collective-permute-start | bytes 344072 | tf_op jit(solution)/shard_map/ppermute | solution.py:156

commit v7 on v6

--- a/solution.py
+++ b/solution.py
@@ -111,8 +111,8 @@
     )(*pieces, w_gate, w_up)
 
 
-def down_kernel(chunk, hidden_ref, down_ref, other_ref, here_ref):
-    half, width = here_ref.shape
+def down_kernel(chunk, hidden_ref, down_ref, *outs):
+    part, width = outs[0].shape
 
     @pl.loop(0, width // DOWN_TILE)
     def _(step):
@@ -121,8 +121,8 @@
         total = jnp.dot(
             hidden_ref[...], down_ref[:, there], preferred_element_type=jnp.float32
         ).astype(jnp.bfloat16)
-        here_ref[:, at] = total[:half]
-        other_ref[:, at] = total[half:]
+        for i, ref in enumerate(outs):
+            ref[:, at] = total[i * part : (i + 1) * part]
 
 
 def down(hidden, w_down, chunk, chunks):
@@ -131,9 +131,9 @@
     vmem = pl.BlockSpec(memory_space=pltpu.VMEM)
     return pl.pallas_call(
         functools.partial(down_kernel, chunk),
-        out_shape=[jax.ShapeDtypeStruct((rows // 2, width // chunks), jnp.bfloat16)] * 2,
+        out_shape=[jax.ShapeDtypeStruct((rows // 4, width // chunks), jnp.bfloat16)] * 4,
         in_specs=[vmem, vmem],
-        out_specs=[vmem, vmem],
+        out_specs=[vmem] * 4,
         compiler_params=pltpu.CompilerParams(vmem_limit_bytes=VMEM_LIMIT),
         cost_estimate=pl.CostEstimate(
             flops=2 * rows * units * width // chunks,
@@ -171,10 +171,11 @@
 
 
 def gather_blocks(own):
-    second, far_own = to_place(own, 2), to_chip(own)
-    far_first, first = to_both(own, 1), to_place(own, 1)
-    other = [to_core(own), to_core(far_own), to_core(first)]
-    far_second, far_third, third = to_chip(second), to_both(second, 1), to_place(second, 1)
+    second, first, far_own = to_place(own, 2), to_place(own, 1), to_chip(own)
+    far_first = to_chip(first)
+    other = [to_core(after(own, first)), to_core(after(far_own, first)), to_core(first)]
+    ready = after(second, far_first, far_own, other[0])
+    far_second, far_third, third = to_chip(ready), to_both(ready, 1), to_place(ready, 1)
     other += [to_core(after(piece, third)) for piece in (far_first, second)]
     other += [to_core(piece) for piece in (third, far_second, far_third)]
     chip = [own, far_own, first, far_first, second, third, far_second, far_third]
@@ -185,11 +186,13 @@
     return sum(term.astype(jnp.float32) for term in terms)
 
 
-def reduce_blocks(other, here, rows):
-    sums = total(here, to_core(other)).astype(jnp.bfloat16).reshape(2 * PLACES, rows, -1)
-    near, far = sums[:PLACES], sums[PLACES:]
-    second = total(near[2], to_chip(far[2]), to_both(far[3], 1), to_place(near[3], 1))
-    second = second.astype(jnp.bfloat16)
+def reduce_blocks(near, far, other_near, other_far, rows):
+    other_far = to_core(other_far)
+    other_near = to_core(after(other_near, other_far))
+    far = total(far, other_far).astype(jnp.bfloat16).reshape(PLACES, rows, -1)
+    second, third = to_chip(far[2]), to_both(far[3], 1)
+    near = total(near, other_near).astype(jnp.bfloat16).reshape(PLACES, rows, -1)
+    second = total(near[2], second, third, to_place(near[3], 1)).astype(jnp.bfloat16)
     own = total(near[0], after(to_place(near[1], 1), second))
     far_own, far_first = to_chip(after(far[0], own)), to_both(after(far[1], own), 1)
     return total(own, to_place(second, 2), far_own, far_first).astype(jnp.bfloat16)

time: 54.8 us -> 56.8 us (1.036)
  starting transfers between devices: 22.6 us -> 24 us
  waiting for transfers between devices: 21.7 us -> 22.3 us
    ppermute x4 -> x3, starting transfers between devices: 7.91 us -> 4.63 us  [to_both(): return lax.ppermute(value, ('node', 'local'), perm)]
    ppermute x6, starting transfers between devices: 9.6 us -> 12.3 us  [to_place(): return lax.ppermute(value, 'local', [(i, i ^ bits) for i in range(PLACES)])]
    ppermute x6, waiting for transfers between devices: 8.03 us -> 10 us  [to_place(): return lax.ppermute(value, 'local', [(i, i ^ bits) for i in range(PLACES)])]
    ppermute x4 -> x5, starting transfers between devices: 3.77 us -> 5.52 us  [to_chip(): return lax.ppermute(value, 'node', [(i, i ^ 2) for i in range(2 * CHIPS)])]
    ppermute x4 -> x3, waiting for transfers between devices: 6.56 us -> 4.9 us  [to_both(): return lax.ppermute(value, ('node', 'local'), perm)]
    ppermute x4 -> x5, waiting for transfers between devices: 3.58 us -> 4.48 us  [to_chip(): return lax.ppermute(value, 'node', [(i, i ^ 2) for i in range(2 * CHIPS)])]
    ppermute x9 -> x10, waiting for transfers between devices: 3.56 us -> 2.92 us  [to_core(): return lax.ppermute(value, 'node', [(i, i ^ 1) for i in range(2 * CHIPS)])]
    ppermute x9 -> x10, starting transfers between devices: 1.34 us -> 1.49 us  [to_core(): return lax.ppermute(value, 'node', [(i, i ^ 1) for i in range(2 * CHIPS)])]
  transfers between devices with their start and end apart: 23 -> 24, of which waited for: 15 -> 15; matrix products, arithmetic and copies ran while one was open for 0% -> 1% of each run, Pallas kernels for 0% -> 0%
where the time goes in v7:
time: 56.8 us; the launch traced here: 56.6 us
  starting transfers between devices  24 us (42%)
  waiting for transfers between devices  22.3 us (39%)
  Pallas kernels  9.14 us (16%)
  other arithmetic  0.99 us (2%)
    ppermute x6, starting transfers between devices, to_place(): return lax.ppermute(value, 'local', [(i, i ^ bits) for i in range(PLACES)])  12.3 us
    ppermute x6, waiting for transfers between devices, to_place(): return lax.ppermute(value, 'local', [(i, i ^ bits) for i in range(PLACES)])  10 us
    ppermute x5, starting transfers between devices, to_chip(): return lax.ppermute(value, 'node', [(i, i ^ 2) for i in range(2 * CHIPS)])  5.52 us
    pallas_call x1, Pallas kernels, hidden_units(): pl.pallas_call(functools.partial(hidden_kernel, experts), out_shape=jax.S...  5.3 us
    ppermute x3, waiting for transfers between devices, to_both(): return lax.ppermute(value, ('node', 'local'), perm)  4.9 us
    ppermute x3, starting transfers between devices, to_both(): return lax.ppermute(value, ('node', 'local'), perm)  4.63 us
    ppermute x5, waiting for transfers between devices, to_chip(): return lax.ppermute(value, 'node', [(i, i ^ 2) for i in range(2 * CHIPS)])  4.48 us
    ppermute x10, waiting for transfers between devices, to_core(): return lax.ppermute(value, 'node', [(i, i ^ 1) for i in range(2 * CHIPS)])  2.92 us
  transfers between devices with their start and end apart: 24, of which 15 were waited for; matrix products, arithmetic and copies ran while one was open for 1% of the time, Pallas kernels for 0%

profile of v7, /device:TPU:0, one launch (start us, length us, event | category | flops | bytes accessed | tf_op | source)
XLA Modules:
  0.0 56.6 jit_solution(889922115202299012)
XLA Ops:
  0.0 0.0 copy-start
  0.0 0.0 copy-start.1
  0.0 1.2 %pack.1.refs_0_ = bf16[8,7296]{1,0:T(8,128)(2,1)S(1)} custom-call(bf16[8,7168]{1,0:T(8,128)(2,1)} %refs_0_.1, s32[4,8]{1,0:T(4,128)} %bitcast.6, f32[4,8]{1,0:T(4,128)} %bitcast.7, s32[8]{0:T(128)} %refs_3_.1, bf16[2,7168,512]{2,1,0:T(8,128)(2,1)} %refs_16_.1, bf16[2,7168,512]{2,1,0:T(8,128)(2,1)} %refs_17_.1, bf16[2,512,7168]{2,1,0:T(8,128)(2,1)} %refs_6_.1), custom_call_target="tpu_custom_call" | custom-call | tf_op jit(solution)/shard_map/pack/pallas_call | solution.py:50
  1.2 0.0 slice-start.3
  1.2 3.1 %collective-permute-start = (bf16[8,7296]{1,0:T(8,128)(2,1)S(1)}, bf16[8,7296]{1,0:T(8,128)(2,1)S(1)}, u32[]{:S(2)}, u32[]{:S(2)}) collective-permute-start(bf16[8,7296]{1,0:T(8,128)(2,1)S(1)} %pack.1.refs_0_), channel_id=1, source_target_pairs={{0,1},{1,0},{2,3},{3,2},{4,5},{5,4},{6,7},{7,6},{8,9},{9,8},{10,11... | collective-permute-start | bytes 350216 | tf_op jit(solution)/shard_map/ppermute | solution.py:160
  4.3 1.5 %collective-permute-start.3 = (bf16[8,7296]{1,0:T(8,128)(2,1)S(1)}, bf16[8,7296]{1,0:T(8,128)(2,1)S(1)}, u32[]{:S(2)}, u32[]{:S(2)}) collective-permute-start(bf16[8,7296]{1,0:T(8,128)(2,1)S(1)} %pack.1.refs_0_), channel_id=1, source_target_pairs={{0,8},{4,12},{8,0},{12,4},{1,9},{5,13},{9,1},{13,5},{2,10},{6,14},... | collective-permute-start | bytes 350216 | tf_op jit(solution)/shard_map/ppermute | solution.py:156
  5.8 2.6 %collective-permute-start.1 = (bf16[8,7296]{1,0:T(8,128)(2,1)S(1)}, bf16[8,7296]{1,0:T(8,128)(2,1)S(1)}, u32[]{:S(2)}, u32[]{:S(2)}) collective-permute-start(bf16[8,7296]{1,0:T(8,128)(2,1)S(1)} %pack.1.refs_0_), channel_id=1, source_target_pairs={{0,2},{1,3},{2,0},{3,1},{4,6},{5,7},{6,4},{7,5},{8,10},{9,11},{10,... | collective-permute-start | bytes 350216 | tf_op jit(solution)/shard_map/ppermute | solution.py:160
  8.4 0.0 collective-permute-done.refs_1_
  8.4 0.0 collective-permute-start.4
  8.4 0.8 %collective-permute-start.2 = (bf16[8,7296]{1,0:T(8,128)(2,1)S(1)}, bf16[8,7296]{1,0:T(8,128)(2,1)S(1)}, u32[]{:S(2)}, u32[]{:S(2)}) collective-permute-start(bf16[8,7296]{1,0:T(8,128)(2,1)S(1)} %collective-permute-done.refs_1_), channel_id=1, source_target_pairs={{0,8},{4,12},{8,0},{12,4},{1,9},{5,13},{9,1},{13,5},{2,10},{6,14},... | collective-permute-start | bytes 350216 | tf_op jit(solution)/shard_map/ppermute | solution.py:156
  9.2 0.0 collective-permute-done.3.refs_4_
  9.2 4.4 %collective-permute-done.1.refs_2_ = bf16[8,7296]{1,0:T(8,128)(2,1)S(1)} collective-permute-done((bf16[8,7296]{1,0:T(8,128)(2,1)S(1)}, bf16[8,7296]{1,0:T(8,128)(2,1)S(1)}, u32[]{:S(2)}, u32[]{:S(2)}) %collective-permute-start.1) | collective-permute-done | bytes 116768 | tf_op jit(solution)/shard_map/ppermute | solution.py:160
  13.6 0.0 collective-permute-done.4.refs_8_
  13.6 0.4 collective-permute-done.2.refs_5_
  14.0 0.8 %collective-permute-start.5 = (bf16[8,7296]{1,0:T(8,128)(2,1)S(1)}, bf16[8,7296]{1,0:T(8,128)(2,1)S(1)}, u32[]{:S(2)}, u32[]{:S(2)}) collective-permute-start(bf16[8,7296]{1,0:T(8,128)(2,1)S(1)} %collective-permute-done.1.refs_2_), channel_id=1, source_target_pairs={{0,1},{1,0},{2,3},{3,2},{4,5},{5,4},{6,7},{7,6},{8,9},{9,8},{10,11... | collective-permute-start | bytes 350216 | tf_op jit(solution)/shard_map/ppermute | solution.py:160
  14.8 1.4 %collective-permute-start.7 = (bf16[8,7296]{1,0:T(8,128)(2,1)S(1)}, bf16[8,7296]{1,0:T(8,128)(2,1)S(1)}, u32[]{:S(2)}, u32[]{:S(2)}) collective-permute-start(bf16[8,7296]{1,0:T(8,128)(2,1)S(1)} %collective-permute-done.1.refs_2_), channel_id=1, source_target_pairs={{0,9},{1,8},{2,11},{3,10},{4,13},{5,12},{6,15},{7,14},{8,1},{9,0},... | collective-permute-start | bytes 350216 | tf_op jit(solution)/shard_map/ppermute | solution.py:166
  16.2 1.3 %collective-permute-start.6 = (bf16[8,7296]{1,0:T(8,128)(2,1)S(1)}, bf16[8,7296]{1,0:T(8,128)(2,1)S(1)}, u32[]{:S(2)}, u32[]{:S(2)}) collective-permute-start(bf16[8,7296]{1,0:T(8,128)(2,1)S(1)} %collective-permute-done.1.refs_2_), channel_id=1, source_target_pairs={{0,8},{4,12},{8,0},{12,4},{1,9},{5,13},{9,1},{13,5},{2,10},{6,14},... | collective-permute-start | bytes 350216 | tf_op jit(solution)/shard_map/ppermute | solution.py:156
  17.5 0.0 collective-permute-start.11
  17.5 0.5 collective-permute-start.8
  18.0 1.8 %collective-permute-done.5.refs_3_ = bf16[8,7296]{1,0:T(8,128)(2,1)S(1)} collective-permute-done((bf16[8,7296]{1,0:T(8,128)(2,1)S(1)}, bf16[8,7296]{1,0:T(8,128)(2,1)S(1)}, u32[]{:S(2)}, u32[]{:S(2)}) %collective-permute-start.5) | collective-permute-done | bytes 116768 | tf_op jit(solution)/shard_map/ppermute | solution.py:160
  19.8 0.0 collective-permute-start.9
  19.8 1.8 %collective-permute-done.7.refs_7_ = bf16[8,7296]{1,0:T(8,128)(2,1)S(1)} collective-permute-done((bf16[8,7296]{1,0:T(8,128)(2,1)S(1)}, bf16[8,7296]{1,0:T(8,128)(2,1)S(1)}, u32[]{:S(2)}, u32[]{:S(2)}) %collective-permute-start.7) | collective-permute-done | bytes 116768 | tf_op jit(solution)/shard_map/ppermute | solution.py:166
  21.6 0.0 collective-permute-start.14
  21.6 1.3 %collective-permute-done.6.refs_6_ = bf16[8,7296]{1,0:T(8,128)(2,1)S(1)} collective-permute-done((bf16[8,7296]{1,0:T(8,128)(2,1)S(1)}, bf16[8,7296]{1,0:T(8,128)(2,1)S(1)}, u32[]{:S(2)}, u32[]{:S(2)}) %collective-permute-start.6) | collective-permute-done | bytes 116768 | tf_op jit(solution)/shard_map/ppermute | solution.py:156
  22.9 0.0 collective-permute-start.13
  22.9 0.0 collective-permute-done.11.refs_12_
  22.9 0.5 collective-permute-start.12
  23.4 0.0 collective-permute-done.8.refs_9_
  23.4 0.1 collective-permute-start.10
  23.5 0.0 collective-permute-done.14.refs_15_
  23.5 0.7 %collective-permute-done.13.refs_14_ = bf16[8,7296]{1,0:T(8,128)(2,1)S(1)} collective-permute-done((bf16[8,7296]{1,0:T(8,128)(2,1)S(1)}, bf16[8,7296]{1,0:T(8,128)(2,1)S(1)}, u32[]{:S(2)}, u32[]{:S(2)}) %collective-permute-start.13) | collective-permute-done | bytes 116768 | tf_op jit(solution)/shard_map/ppermute | solution.py:152
  24.2 0.0 collective-permute-done.9.refs_10_
  24.2 0.2 collective-permute-done.12.refs_13_
  24.4 0.4 collective-permute-done.10.refs_11_
  24.7 0.0 copy-done
  24.7 0.0 copy-done.1
  24.7 5.3 %hidden.1.hidden_ref = bf16[128,1024]{1,0:T(8,128)(2,1)S(1)} custom-call(bf16[8,7296]{1,0:T(8,128)(2,1)S(1)} %pack.1.refs_0_, bf16[8,7296]{1,0:T(8,128)(2,1)S(1)} %collective-permute-done.refs_1_, bf16[8,7296]{1,0:T(8,128)(2,1)S(1)} %collective-permute-done.1.refs_2_, bf16[8,7296]{1,0:T(8,128)(2,1)S(1)} %collective-permute-done.5.refs_3_, ...), custom_call_target="tpu_custom_call" | custom-call | flops 3758096384 | bytes 29360128 | tf_op jit(solution)/shard_map/hidden/pallas_call | solution.py:95
  30.1 0.0 slice-done
  30.1 0.0 slice-done.1
  30.1 0.0 slice-done.2
  30.1 0.0 slice-done.3
  30.1 2.7 %down.1 = (bf16[32,7168]{1,0:T(8,128)(2,1)S(1)}, bf16[32,7168]{1,0:T(8,128)(2,1)S(1)}, bf16[32,7168]{1,0:T(8,128)(2,1)S(1)}, bf16[32,7168]{1,0:T(8,128)(2,1)S(1)}) custom-call(bf16[128,1024]{1,0:T(8,128)(2,1)S(1)} %hidden.1.hidden_ref, bf16[1024,7168]{1,0:T(8,128)(2,1)S(1)} %bitcast.5), custom_call_target="tpu_custom_call" | custom-call | flops 1879048192 | bytes 14680064 | tf_op jit(solution)/shard_map/down/pallas_call | solution.py:132
  32.8 0.2 collective-permute-start.15
  33.0 1.7 %collective-permute-done.15 = bf16[32,7168]{1,0:T(8,128)(2,1)S(1)} collective-permute-done((bf16[32,7168]{1,0:T(8,128)(2,1)S(1)}, bf16[32,7168]{1,0:T(8,128)(2,1)S(1)}, u32[]{:S(2)}, u32[]{:S(2)}) %collective-permute-start.15) | collective-permute-done | bytes 458784 | tf_op jit(solution)/shard_map/ppermute | solution.py:152
  34.7 0.2 collective-permute-start.16
  34.8 0.1 add_convert_fusion
  35.0 1.6 %collective-permute-start.19 = (bf16[8,7168]{1,0:T(8,128)(2,1)S(1)}, bf16[8,7168]{1,0:T(8,128)(2,1)S(1)}, u32[]{:S(2)}, u32[]{:S(2)}) collective-permute-start(bf16[8,7168]{1,0:T(8,128)(2,1)S(1)} %get-tuple-element.33), channel_id=1, source_target_pairs={{0,9},{1,8},{2,11},{3,10},{4,13},{5,12},{6,15},{7,14},{8,1},{9,0},... | collective-permute-start | bytes 344072 | tf_op jit(solution)/shard_map/ppermute | solution.py:166
  36.6 1.5 %collective-permute-start.18 = (bf16[8,7168]{1,0:T(8,128)(2,1)S(1)}, bf16[8,7168]{1,0:T(8,128)(2,1)S(1)}, u32[]{:S(2)}, u32[]{:S(2)}) collective-permute-start(bf16[8,7168]{1,0:T(8,128)(2,1)S(1)} %get-tuple-element.34), channel_id=1, source_target_pairs={{0,8},{4,12},{8,0},{12,4},{1,9},{5,13},{9,1},{13,5},{2,10},{6,14},... | collective-permute-start | bytes 344072 | tf_op jit(solution)/shard_map/ppermute | solution.py:156
  38.1 0.0 collective-permute-done.16
  38.1 0.1 add_convert_fusion.1
  38.2 0.5 collective-permute-start.20
  38.7 1.5 %collective-permute-start.17 = (bf16[8,7168]{1,0:T(8,128)(2,1)S(1)}, bf16[8,7168]{1,0:T(8,128)(2,1)S(1)}, u32[]{:S(2)}, u32[]{:S(2)}) collective-permute-start(bf16[8,7168]{1,0:T(8,128)(2,1)S(1)} %get-tuple-element.36), channel_id=1, source_target_pairs={{0,1},{1,0},{2,3},{3,2},{4,5},{5,4},{6,7},{7,6},{8,9},{9,8},{10,11... | collective-permute-start | bytes 344072 | tf_op jit(solution)/shard_map/ppermute | solution.py:160
  40.3 1.6 %collective-permute-done.19 = bf16[8,7168]{1,0:T(8,128)(2,1)S(1)} collective-permute-done((bf16[8,7168]{1,0:T(8,128)(2,1)S(1)}, bf16[8,7168]{1,0:T(8,128)(2,1)S(1)}, u32[]{:S(2)}, u32[]{:S(2)}) %collective-permute-start.19) | collective-permute-done | bytes 114720 | tf_op jit(solution)/shard_map/ppermute | solution.py:166
  41.9 1.9 %collective-permute-done.18 = bf16[8,7168]{1,0:T(8,128)(2,1)S(1)} collective-permute-done((bf16[8,7168]{1,0:T(8,128)(2,1)S(1)}, bf16[8,7168]{1,0:T(8,128)(2,1)S(1)}, u32[]{:S(2)}, u32[]{:S(2)}) %collective-permute-start.18) | collective-permute-done | bytes 114720 | tf_op jit(solution)/shard_map/ppermute | solution.py:156
  43.8 0.5 collective-permute-done.20
  44.3 0.1 add_convert_fusion.3
  44.4 3.7 %collective-permute-start.21 = (bf16[8,7168]{1,0:T(8,128)(2,1)S(1)}, bf16[8,7168]{1,0:T(8,128)(2,1)S(1)}, u32[]{:S(2)}, u32[]{:S(2)}) collective-permute-start(bf16[8,7168]{1,0:T(8,128)(2,1)S(1)} %add_convert_fusion.3), channel_id=1, source_target_pairs={{0,2},{1,3},{2,0},{3,1},{4,6},{5,7},{6,4},{7,5},{8,10},{9,11},{10,... | collective-permute-start | bytes 344072 | tf_op jit(solution)/shard_map/ppermute | solution.py:160
  48.1 0.0 collective-permute-done.17
  48.1 1.7 %collective-permute-start.23 = (bf16[8,7168]{1,0:T(8,128)(2,1)S(1)}, bf16[8,7168]{1,0:T(8,128)(2,1)S(1)}, u32[]{:S(2)}, u32[]{:S(2)}) collective-permute-start(bf16[8,7168]{1,0:T(8,128)(2,1)S(1)} %get-tuple-element.30), channel_id=1, source_target_pairs={{0,9},{1,8},{2,11},{3,10},{4,13},{5,12},{6,15},{7,14},{8,1},{9,0},... | collective-permute-start | bytes 344072 | tf_op jit(solution)/shard_map/ppermute | solution.py:166
  49.8 0.5 collective-permute-start.22
  50.3 3.3 %collective-permute-done.21 = bf16[8,7168]{1,0:T(8,128)(2,1)S(1)} collective-permute-done((bf16[8,7168]{1,0:T(8,128)(2,1)S(1)}, bf16[8,7168]{1,0:T(8,128)(2,1)S(1)}, u32[]{:S(2)}, u32[]{:S(2)}) %collective-permute-start.21) | collective-permute-done | bytes 114720 | tf_op jit(solution)/shard_map/ppermute | solution.py:160
  53.5 1.5 %collective-permute-done.23 = bf16[8,7168]{1,0:T(8,128)(2,1)S(1)} collective-permute-done((bf16[8,7168]{1,0:T(8,128)(2,1)S(1)}, bf16[8,7168]{1,0:T(8,128)(2,1)S(1)}, u32[]{:S(2)}, u32[]{:S(2)}) %collective-permute-start.23) | collective-permute-done | bytes 114720 | tf_op jit(solution)/shard_map/ppermute | solution.py:166
  55.0 0.9 %collective-permute-done.22 = bf16[8,7168]{1,0:T(8,128)(2,1)S(1)} collective-permute-done((bf16[8,7168]{1,0:T(8,128)(2,1)S(1)}, bf16[8,7168]{1,0:T(8,128)(2,1)S(1)}, u32[]{:S(2)}, u32[]{:S(2)}) %collective-permute-start.22) | collective-permute-done | bytes 114720 | tf_op jit(solution)/shard_map/ppermute | solution.py:156
  55.9 0.7 %add_convert_fusion.2 = bf16[8,7168]{1,0:T(8,128)(2,1)} fusion(bf16[8,7168]{1,0:T(8,128)(2,1)S(1)} %collective-permute-done.23, bf16[8,7168]{1,0:T(8,128)(2,1)S(1)} %collective-permute-done.22, bf16[8,7168]{1,0:T(8,128)(2,1)S(1)} %collective-permute-done.21, bf16[8,7168]{1,0:T(8,128)(2,1)S(1)} %collective-permute-done.17, ...), kind=kLoop, calls=%fused_computation.2 | loop fusion | flops 573440 | bytes 688128 | tf_op jit(solution)/shard_map/convert_element_type | solution.py:198
  (6 shorter events, 0.1 us)
Async XLA Ops:
  0.0 24.7 %copy-start = (bf16[2,7168,512]{2,1,0:T(8,128)(2,1)S(1)}, bf16[2,7168,512]{2,1,0:T(8,128)(2,1)}, u32[]{:S(2)}) copy-start(bf16[2,7168,512]{2,1,0:T(8,128)(2,1)} %refs_16_.1) | copy-start | bytes 44040196
  0.0 24.7 %copy-start.1 = (bf16[2,7168,512]{2,1,0:T(8,128)(2,1)S(1)}, bf16[2,7168,512]{2,1,0:T(8,128)(2,1)}, u32[]{:S(2)}) copy-start(bf16[2,7168,512]{2,1,0:T(8,128)(2,1)} %refs_17_.1) | copy-start | bytes 44040196
  0.0 30.0 %slice-start = ((s8[14680064]{0:T(1024)(128)(4,1)}), s8[4194304]{0:T(1024)(128)(4,1)S(1)}, s32[]{:S(2)}) async-start(s8[14680064]{0:T(1024)(128)(4,1)} %bitcast.3), calls=%async_computation | async-start | bytes 8388608
  0.0 30.1 %slice-start.1 = ((s8[14680064]{0:T(1024)(128)(4,1)}), s8[4194304]{0:T(1024)(128)(4,1)S(1)}, s32[]{:S(2)}) async-start(s8[14680064]{0:T(1024)(128)(4,1)} %bitcast.3), calls=%async_computation.1 | async-start | bytes 8388608
  0.0 30.1 %slice-start.2 = ((s8[14680064]{0:T(1024)(128)(4,1)}), s8[4194304]{0:T(1024)(128)(4,1)S(1)}, s32[]{:S(2)}) async-start(s8[14680064]{0:T(1024)(128)(4,1)} %bitcast.3), calls=%async_computation.2 | async-start | bytes 8388608
  1.2 28.9 %slice-start.3 = ((s8[14680064]{0:T(1024)(128)(4,1)}), s8[2097152]{0:T(1024)(128)(4,1)S(1)}, s32[]{:S(2)}) async-start(s8[14680064]{0:T(1024)(128)(4,1)} %bitcast.3), calls=%async_computation.3 | async-start | bytes 4194304
  1.2 7.2 %collective-permute-start = (bf16[8,7296]{1,0:T(8,128)(2,1)S(1)}, bf16[8,7296]{1,0:T(8,128)(2,1)S(1)}, u32[]{:S(2)}, u32[]{:S(2)}) collective-permute-start(bf16[8,7296]{1,0:T(8,128)(2,1)S(1)} %pack.1.refs_0_), channel_id=1, source_target_pairs={{0,1},{1,0},{2,3},{3,2},{4,5},{5,4},{6,7},{7,6},{8,9},{9,8},{10,11... | collective-permute-start | bytes 350216 | tf_op jit(solution)/shard_map/ppermute | solution.py:160
  4.3 4.9 %collective-permute-start.3 = (bf16[8,7296]{1,0:T(8,128)(2,1)S(1)}, bf16[8,7296]{1,0:T(8,128)(2,1)S(1)}, u32[]{:S(2)}, u32[]{:S(2)}) collective-permute-start(bf16[8,7296]{1,0:T(8,128)(2,1)S(1)} %pack.1.refs_0_), channel_id=1, source_target_pairs={{0,8},{4,12},{8,0},{12,4},{1,9},{5,13},{9,1},{13,5},{2,10},{6,14},... | collective-permute-start | bytes 350216 | tf_op jit(solution)/shard_map/ppermute | solution.py:156
  5.8 7.8 %collective-permute-start.1 = (bf16[8,7296]{1,0:T(8,128)(2,1)S(1)}, bf16[8,7296]{1,0:T(8,128)(2,1)S(1)}, u32[]{:S(2)}, u32[]{:S(2)}) collective-permute-start(bf16[8,7296]{1,0:T(8,128)(2,1)S(1)} %pack.1.refs_0_), channel_id=1, source_target_pairs={{0,2},{1,3},{2,0},{3,1},{4,6},{5,7},{6,4},{7,5},{8,10},{9,11},{10,... | collective-permute-start | bytes 350216 | tf_op jit(solution)/shard_map/ppermute | solution.py:160
  8.4 5.2 %collective-permute-start.4 = (bf16[8,7296]{1,0:T(8,128)(2,1)S(1)}, bf16[8,7296]{1,0:T(8,128)(2,1)S(1)}, u32[]{:S(2)}, u32[]{:S(2)}) collective-permute-start(bf16[8,7296]{1,0:T(8,128)(2,1)S(1)} %pack.1.refs_0_), channel_id=1, source_target_pairs={{0,4},{4,0},{8,12},{12,8},{1,5},{5,1},{9,13},{13,9},{2,6},{6,2},{1... | collective-permute-start | bytes 350216 | tf_op jit(solution)/shard_map/ppermute | solution.py:152
  8.4 5.6 %collective-permute-start.2 = (bf16[8,7296]{1,0:T(8,128)(2,1)S(1)}, bf16[8,7296]{1,0:T(8,128)(2,1)S(1)}, u32[]{:S(2)}, u32[]{:S(2)}) collective-permute-start(bf16[8,7296]{1,0:T(8,128)(2,1)S(1)} %collective-permute-done.refs_1_), channel_id=1, source_target_pairs={{0,8},{4,12},{8,0},{12,4},{1,9},{5,13},{9,1},{13,5},{2,10},{6,14},... | collective-permute-start | bytes 350216 | tf_op jit(solution)/shard_map/ppermute | solution.py:156
  14.0 5.8 %collective-permute-start.5 = (bf16[8,7296]{1,0:T(8,128)(2,1)S(1)}, bf16[8,7296]{1,0:T(8,128)(2,1)S(1)}, u32[]{:S(2)}, u32[]{:S(2)}) collective-permute-start(bf16[8,7296]{1,0:T(8,128)(2,1)S(1)} %collective-permute-done.1.refs_2_), channel_id=1, source_target_pairs={{0,1},{1,0},{2,3},{3,2},{4,5},{5,4},{6,7},{7,6},{8,9},{9,8},{10,11... | collective-permute-start | bytes 350216 | tf_op jit(solution)/shard_map/ppermute | solution.py:160
  14.8 6.8 %collective-permute-start.7 = (bf16[8,7296]{1,0:T(8,128)(2,1)S(1)}, bf16[8,7296]{1,0:T(8,128)(2,1)S(1)}, u32[]{:S(2)}, u32[]{:S(2)}) collective-permute-start(bf16[8,7296]{1,0:T(8,128)(2,1)S(1)} %collective-permute-done.1.refs_2_), channel_id=1, source_target_pairs={{0,9},{1,8},{2,11},{3,10},{4,13},{5,12},{6,15},{7,14},{8,1},{9,0},... | collective-permute-start | bytes 350216 | tf_op jit(solution)/shard_map/ppermute | solution.py:166
  16.2 6.7 %collective-permute-start.6 = (bf16[8,7296]{1,0:T(8,128)(2,1)S(1)}, bf16[8,7296]{1,0:T(8,128)(2,1)S(1)}, u32[]{:S(2)}, u32[]{:S(2)}) collective-permute-start(bf16[8,7296]{1,0:T(8,128)(2,1)S(1)} %collective-permute-done.1.refs_2_), channel_id=1, source_target_pairs={{0,8},{4,12},{8,0},{12,4},{1,9},{5,13},{9,1},{13,5},{2,10},{6,14},... | collective-permute-start | bytes 350216 | tf_op jit(solution)/shard_map/ppermute | solution.py:156
  17.5 5.4 %collective-permute-start.11 = (bf16[8,7296]{1,0:T(8,128)(2,1)S(1)}, bf16[8,7296]{1,0:T(8,128)(2,1)S(1)}, u32[]{:S(2)}, u32[]{:S(2)}) collective-permute-start(bf16[8,7296]{1,0:T(8,128)(2,1)S(1)} %collective-permute-done.3.refs_4_), channel_id=1, source_target_pairs={{0,4},{4,0},{8,12},{12,8},{1,5},{5,1},{9,13},{13,9},{2,6},{6,2},{1... | collective-permute-start | bytes 350216 | tf_op jit(solution)/shard_map/ppermute | solution.py:152
  17.5 5.9 %collective-permute-start.8 = (bf16[8,7296]{1,0:T(8,128)(2,1)S(1)}, bf16[8,7296]{1,0:T(8,128)(2,1)S(1)}, u32[]{:S(2)}, u32[]{:S(2)}) collective-permute-start(bf16[8,7296]{1,0:T(8,128)(2,1)S(1)} %collective-permute-done.refs_1_), channel_id=1, source_target_pairs={{0,4},{4,0},{8,12},{12,8},{1,5},{5,1},{9,13},{13,9},{2,6},{6,2},{1... | collective-permute-start | bytes 350216 | tf_op jit(solution)/shard_map/ppermute | solution.py:152
  19.8 4.4 %collective-permute-start.9 = (bf16[8,7296]{1,0:T(8,128)(2,1)S(1)}, bf16[8,7296]{1,0:T(8,128)(2,1)S(1)}, u32[]{:S(2)}, u32[]{:S(2)}) collective-permute-start(bf16[8,7296]{1,0:T(8,128)(2,1)S(1)} %collective-permute-done.1.refs_2_), channel_id=1, source_target_pairs={{0,4},{4,0},{8,12},{12,8},{1,5},{5,1},{9,13},{13,9},{2,6},{6,2},{1... | collective-permute-start | bytes 350216 | tf_op jit(solution)/shard_map/ppermute | solution.py:152
  21.6 1.8 %collective-permute-start.14 = (bf16[8,7296]{1,0:T(8,128)(2,1)S(1)}, bf16[8,7296]{1,0:T(8,128)(2,1)S(1)}, u32[]{:S(2)}, u32[]{:S(2)}) collective-permute-start(bf16[8,7296]{1,0:T(8,128)(2,1)S(1)} %collective-permute-done.7.refs_7_), channel_id=1, source_target_pairs={{0,4},{4,0},{8,12},{12,8},{1,5},{5,1},{9,13},{13,9},{2,6},{6,2},{1... | collective-permute-start | bytes 350216 | tf_op jit(solution)/shard_map/ppermute | solution.py:152
  22.9 1.3 %collective-permute-start.13 = (bf16[8,7296]{1,0:T(8,128)(2,1)S(1)}, bf16[8,7296]{1,0:T(8,128)(2,1)S(1)}, u32[]{:S(2)}, u32[]{:S(2)}) collective-permute-start(bf16[8,7296]{1,0:T(8,128)(2,1)S(1)} %collective-permute-done.6.refs_6_), channel_id=1, source_target_pairs={{0,4},{4,0},{8,12},{12,8},{1,5},{5,1},{9,13},{13,9},{2,6},{6,2},{1... | collective-permute-start | bytes 350216 | tf_op jit(solution)/shard_map/ppermute | solution.py:152
  22.9 1.5 %collective-permute-start.12 = (bf16[8,7296]{1,0:T(8,128)(2,1)S(1)}, bf16[8,7296]{1,0:T(8,128)(2,1)S(1)}, u32[]{:S(2)}, u32[]{:S(2)}) collective-permute-start(bf16[8,7296]{1,0:T(8,128)(2,1)S(1)} %collective-permute-done.2.refs_5_), channel_id=1, source_target_pairs={{0,4},{4,0},{8,12},{12,8},{1,5},{5,1},{9,13},{13,9},{2,6},{6,2},{1... | collective-permute-start | bytes 350216 | tf_op jit(solution)/shard_map/ppermute | solution.py:152
  23.4 1.3 %collective-permute-start.10 = (bf16[8,7296]{1,0:T(8,128)(2,1)S(1)}, bf16[8,7296]{1,0:T(8,128)(2,1)S(1)}, u32[]{:S(2)}, u32[]{:S(2)}) collective-permute-start(bf16[8,7296]{1,0:T(8,128)(2,1)S(1)} %collective-permute-done.5.refs_3_), channel_id=1, source_target_pairs={{0,4},{4,0},{8,12},{12,8},{1,5},{5,1},{9,13},{13,9},{2,6},{6,2},{1... | collective-permute-start | bytes 350216 | tf_op jit(solution)/shard_map/ppermute | solution.py:152
  32.8 1.9 %collective-permute-start.15 = (bf16[32,7168]{1,0:T(8,128)(2,1)S(1)}, bf16[32,7168]{1,0:T(8,128)(2,1)S(1)}, u32[]{:S(2)}, u32[]{:S(2)}) collective-permute-start(bf16[32,7168]{1,0:T(8,128)(2,1)S(1)} %get-tuple-element.25), channel_id=1, source_target_pairs={{0,4},{4,0},{8,12},{12,8},{1,5},{5,1},{9,13},{13,9},{2,6},{6,2},{1... | collective-permute-start | bytes 1376264 | tf_op jit(solution)/shard_map/ppermute | solution.py:152
  34.7 3.4 %collective-permute-start.16 = (bf16[32,7168]{1,0:T(8,128)(2,1)S(1)}, bf16[32,7168]{1,0:T(8,128)(2,1)S(1)}, u32[]{:S(2)}, u32[]{:S(2)}) collective-permute-start(bf16[32,7168]{1,0:T(8,128)(2,1)S(1)} %get-tuple-element.26), channel_id=1, source_target_pairs={{0,4},{4,0},{8,12},{12,8},{1,5},{5,1},{9,13},{13,9},{2,6},{6,2},{1... | collective-permute-start | bytes 1376264 | tf_op jit(solution)/shard_map/ppermute | solution.py:152
  35.0 6.9 %collective-permute-start.19 = (bf16[8,7168]{1,0:T(8,128)(2,1)S(1)}, bf16[8,7168]{1,0:T(8,128)(2,1)S(1)}, u32[]{:S(2)}, u32[]{:S(2)}) collective-permute-start(bf16[8,7168]{1,0:T(8,128)(2,1)S(1)} %get-tuple-element.33), channel_id=1, source_target_pairs={{0,9},{1,8},{2,11},{3,10},{4,13},{5,12},{6,15},{7,14},{8,1},{9,0},... | collective-permute-start | bytes 344072 | tf_op jit(solution)/shard_map/ppermute | solution.py:166
  36.6 7.2 %collective-permute-start.18 = (bf16[8,7168]{1,0:T(8,128)(2,1)S(1)}, bf16[8,7168]{1,0:T(8,128)(2,1)S(1)}, u32[]{:S(2)}, u32[]{:S(2)}) collective-permute-start(bf16[8,7168]{1,0:T(8,128)(2,1)S(1)} %get-tuple-element.34), channel_id=1, source_target_pairs={{0,8},{4,12},{8,0},{12,4},{1,9},{5,13},{9,1},{13,5},{2,10},{6,14},... | collective-permute-start | bytes 344072 | tf_op jit(solution)/shard_map/ppermute | solution.py:156
  38.2 6.2 %collective-permute-start.20 = (bf16[8,7168]{1,0:T(8,128)(2,1)S(1)}, bf16[8,7168]{1,0:T(8,128)(2,1)S(1)}, u32[]{:S(2)}, u32[]{:S(2)}) collective-permute-start(bf16[8,7168]{1,0:T(8,128)(2,1)S(1)} %get-tuple-element.35), channel_id=1, source_target_pairs={{0,1},{1,0},{2,3},{3,2},{4,5},{5,4},{6,7},{7,6},{8,9},{9,8},{10,11... | collective-permute-start | bytes 344072 | tf_op jit(solution)/shard_map/ppermute | solution.py:160
  38.7 9.3 %collective-permute-start.17 = (bf16[8,7168]{1,0:T(8,128)(2,1)S(1)}, bf16[8,7168]{1,0:T(8,128)(2,1)S(1)}, u32[]{:S(2)}, u32[]{:S(2)}) collective-permute-start(bf16[8,7168]{1,0:T(8,128)(2,1)S(1)} %get-tuple-element.36), channel_id=1, source_target_pairs={{0,1},{1,0},{2,3},{3,2},{4,5},{5,4},{6,7},{7,6},{8,9},{9,8},{10,11... | collective-permute-start | bytes 344072 | tf_op jit(solution)/shard_map/ppermute | solution.py:160
  44.4 9.1 %collective-permute-start.21 = (bf16[8,7168]{1,0:T(8,128)(2,1)S(1)}, bf16[8,7168]{1,0:T(8,128)(2,1)S(1)}, u32[]{:S(2)}, u32[]{:S(2)}) collective-permute-start(bf16[8,7168]{1,0:T(8,128)(2,1)S(1)} %add_convert_fusion.3), channel_id=1, source_target_pairs={{0,2},{1,3},{2,0},{3,1},{4,6},{5,7},{6,4},{7,5},{8,10},{9,11},{10,... | collective-permute-start | bytes 344072 | tf_op jit(solution)/shard_map/ppermute | solution.py:160
  48.1 6.9 %collective-permute-start.23 = (bf16[8,7168]{1,0:T(8,128)(2,1)S(1)}, bf16[8,7168]{1,0:T(8,128)(2,1)S(1)}, u32[]{:S(2)}, u32[]{:S(2)}) collective-permute-start(bf16[8,7168]{1,0:T(8,128)(2,1)S(1)} %get-tuple-element.30), channel_id=1, source_target_pairs={{0,9},{1,8},{2,11},{3,10},{4,13},{5,12},{6,15},{7,14},{8,1},{9,0},... | collective-permute-start | bytes 344072 | tf_op jit(solution)/shard_map/ppermute | solution.py:166
  49.8 6.1 %collective-permute-start.22 = (bf16[8,7168]{1,0:T(8,128)(2,1)S(1)}, bf16[8,7168]{1,0:T(8,128)(2,1)S(1)}, u32[]{:S(2)}, u32[]{:S(2)}) collective-permute-start(bf16[8,7168]{1,0:T(8,128)(2,1)S(1)} %get-tuple-element.29), channel_id=1, source_target_pairs={{0,8},{4,12},{8,0},{12,4},{1,9},{5,13},{9,1},{13,5},{2,10},{6,14},... | collective-permute-start | bytes 344072 | tf_op jit(solution)/shard_map/ppermute | solution.py:156

commit v8 on v6

--- a/solution.py
+++ b/solution.py
@@ -10,7 +10,6 @@
 LANES = 128
 N_TILE = 256
 DOWN_TILE = 1792
-OUT_CHUNKS = 1
 VMEM_LIMIT = 4 * 2**20
 
 
@@ -62,6 +61,24 @@
     )(*held)
 
 
+def stack_kernel(*refs):
+    *pieces, out_ref = refs
+    out_ref[...] = jnp.concatenate([piece[...] for piece in pieces], axis=0)
+
+
+def stack(*pieces):
+    rows = sum(piece.shape[0] for piece in pieces)
+    vmem = pl.BlockSpec(memory_space=pltpu.VMEM)
+    return pl.pallas_call(
+        stack_kernel,
+        out_shape=jax.ShapeDtypeStruct((rows, pieces[0].shape[1]), pieces[0].dtype),
+        in_specs=[vmem] * len(pieces),
+        out_specs=vmem,
+        compiler_params=pltpu.CompilerParams(vmem_limit_bytes=VMEM_LIMIT),
+        name="stack",
+    )(*pieces)
+
+
 def hidden_kernel(experts, *refs):
     *pieces, gate_ref, up_ref, out_ref, x_ref, weight_ref = refs
     members, width, hid = gate_ref.shape
@@ -104,48 +121,44 @@
         compiler_params=pltpu.CompilerParams(vmem_limit_bytes=VMEM_LIMIT),
         cost_estimate=pl.CostEstimate(
             flops=4 * rows * members * width * hid,
-            bytes_accessed=4 * members * width * hid,
+            bytes_accessed=0,
             transcendentals=rows * members * hid,
         ),
         name="hidden",
     )(*pieces, w_gate, w_up)
 
 
-def down_kernel(chunk, hidden_ref, down_ref, other_ref, here_ref):
+def down_kernel(hidden_ref, down_ref, here_ref, other_ref):
     half, width = here_ref.shape
 
     @pl.loop(0, width // DOWN_TILE)
     def _(step):
         at = pl.ds(pl.multiple_of(step * DOWN_TILE, DOWN_TILE), DOWN_TILE)
-        there = pl.ds(pl.multiple_of(chunk * width + step * DOWN_TILE, DOWN_TILE), DOWN_TILE)
         total = jnp.dot(
-            hidden_ref[...], down_ref[:, there], preferred_element_type=jnp.float32
+            hidden_ref[...], down_ref[:, at], preferred_element_type=jnp.float32
         ).astype(jnp.bfloat16)
         here_ref[:, at] = total[:half]
         other_ref[:, at] = total[half:]
 
 
-def down(hidden, w_down, chunk, chunks):
+def down(hidden, w_down):
     units, width = w_down.shape
     rows = hidden.shape[0]
     vmem = pl.BlockSpec(memory_space=pltpu.VMEM)
     return pl.pallas_call(
-        functools.partial(down_kernel, chunk),
-        out_shape=[jax.ShapeDtypeStruct((rows // 2, width // chunks), jnp.bfloat16)] * 2,
+        down_kernel,
+        out_shape=[jax.ShapeDtypeStruct((rows // 2, width), jnp.bfloat16)] * 2,
         in_specs=[vmem, vmem],
         out_specs=[vmem, vmem],
         compiler_params=pltpu.CompilerParams(vmem_limit_bytes=VMEM_LIMIT),
         cost_estimate=pl.CostEstimate(
-            flops=2 * rows * units * width // chunks,
-            bytes_accessed=2 * units * width // chunks,
-            transcendentals=0,
+            flops=2 * rows * units * width, bytes_accessed=0, transcendentals=0
         ),
         name="down",
     )(hidden, w_down)
 
 
 CHIPS, PLACES = 2, 4
-GATHER_ORDER = (0, 2, 4, 5, 1, 3, 6, 7)
 
 
 def to_core(value):
@@ -170,40 +183,45 @@
     return lax.optimization_barrier((value, *others))[0]
 
 
-def gather_blocks(own):
-    second, far_own = to_place(own, 2), to_chip(own)
-    far_first, first = to_both(own, 1), to_place(own, 1)
-    other = [to_core(own), to_core(far_own), to_core(first)]
+def hidden_groups(own, hidden_of):
+    second, first, far_own = to_place(own, 2), to_place(own, 1), to_chip(own)
+    far_first = to_both(own, 1)
+    group = [own, far_own, first, far_first]
+    early = hidden_of(group + [to_core(stack(after(own, second), *group[1:]))])
     far_second, far_third, third = to_chip(second), to_both(second, 1), to_place(second, 1)
-    other += [to_core(after(piece, third)) for piece in (far_first, second)]
-    other += [to_core(piece) for piece in (third, far_second, far_third)]
-    chip = [own, far_own, first, far_first, second, third, far_second, far_third]
-    return [chip[i] for i in GATHER_ORDER] + [other[i] for i in GATHER_ORDER]
+    group = [after(piece, early) for piece in (second, third, far_second, far_third)]
+    return early, hidden_of(group + [to_core(piece) for piece in group])
 
 
 def total(*terms):
     return sum(term.astype(jnp.float32) for term in terms)
 
 
-def reduce_blocks(other, here, rows):
-    sums = total(here, to_core(other)).astype(jnp.bfloat16).reshape(2 * PLACES, rows, -1)
-    near, far = sums[:PLACES], sums[PLACES:]
-    second = total(near[2], to_chip(far[2]), to_both(far[3], 1), to_place(near[3], 1))
+def reduce_blocks(hidden_early, hidden_late, matrix, rows):
+    def shares(hidden):
+        here, other = down(hidden, matrix)
+        return here, to_core(other), other
+
+    def blocks(here, other):
+        return total(here, other).astype(jnp.bfloat16).reshape(PLACES, rows, -1)
+
+    here, other, leaving = shares(hidden_late)
+    here_early, other_early, _ = shares(after(hidden_early, leaving))
+    second, third, far_second, far_third = blocks(here, other)
+    second = total(second, to_chip(far_second), to_both(far_third, 1), to_place(third, 1))
     second = second.astype(jnp.bfloat16)
-    own = total(near[0], after(to_place(near[1], 1), second))
-    far_own, far_first = to_chip(after(far[0], own)), to_both(after(far[1], own), 1)
+    own, far_own, first, far_first = blocks(here_early, other_early)
+    own = total(own, after(to_place(first, 1), second))
+    far_own, far_first = to_chip(after(far_own, own)), to_both(after(far_first, own), 1)
     return total(own, to_place(second, 2), far_own, far_first).astype(jnp.bfloat16)
 
 
 def by_permutes(tokens, expert_ids, route_weights, expert_slot, w_gate, w_up, w_down):
-    rows = tokens.shape[0]
     own = pack(tokens, expert_ids, route_weights, expert_slot, w_gate, w_up, w_down)
-    hidden = hidden_units(gather_blocks(own), w_gate, w_up, expert_slot.shape[0])
+    experts = expert_slot.shape[0]
+    early, late = hidden_groups(own, lambda rows: hidden_units(rows, w_gate, w_up, experts))
     matrix = w_down.reshape(-1, w_down.shape[-1])
-    outs = []
-    for chunk in range(OUT_CHUNKS):
-        outs.append(reduce_blocks(*down(hidden, matrix, chunk, OUT_CHUNKS), rows))
-    return jnp.concatenate(outs, axis=1)
+    return reduce_blocks(early, late, matrix, tokens.shape[0])
 
 
 def by_collectives(tokens, expert_ids, route_weights, expert_slot, w_gate, w_up, w_down):

time: 54.8 us -> 58.5 us (1.068)
  Pallas kernels: 9.14 us -> 19.2 us
  waiting for transfers between devices: 21.7 us -> 15.8 us
    pallas_call x1 -> x2, Pallas kernels: 5.29 us -> 11.9 us  [hidden_units(): pl.pallas_call(functools.partial(hidden_kernel, experts), out_shape=jax.S...]
    pallas_call x1 -> x3, Pallas kernels: 2.68 us -> 6.16 us  [the longest x2 6.09 us: down(): pl.pallas_call(down_kernel, out_shape=[jax.ShapeDtypeStruct((rows // 2, w...]
    ppermute x9 -> x7, waiting for transfers between devices: 3.56 us -> 0.99 us  [to_core(): return lax.ppermute(value, 'node', [(i, i ^ 1) for i in range(2 * CHIPS)])]
    ppermute x4, waiting for transfers between devices: 3.58 us -> 1.68 us  [to_chip(): return lax.ppermute(value, 'node', [(i, i ^ 2) for i in range(2 * CHIPS)])]
    ppermute x6, waiting for transfers between devices: 8.03 us -> 7.1 us  [to_place(): return lax.ppermute(value, 'local', [(i, i ^ bits) for i in range(PLACES)])]
    ppermute x9 -> x7, starting transfers between devices: 1.34 us -> 1.79 us  [to_core(): return lax.ppermute(value, 'node', [(i, i ^ 1) for i in range(2 * CHIPS)])]
  transfers between devices with their start and end apart: 23 -> 21, of which waited for: 15 -> 13; matrix products, arithmetic and copies ran while one was open for 0% -> 1% of each run, Pallas kernels for 0% -> 15%
where the time goes in v8:
time: 58.5 us; the launch traced here: 58.4 us
  starting transfers between devices  22.2 us (38%)
  Pallas kernels  19.2 us (33%)
  waiting for transfers between devices  15.8 us (27%)
  other arithmetic  0.99 us (2%)
    pallas_call x2, Pallas kernels, hidden_units(): pl.pallas_call(functools.partial(hidden_kernel, experts), out_shape=jax.S...  11.9 us
    ppermute x6, starting transfers between devices, to_place(): return lax.ppermute(value, 'local', [(i, i ^ bits) for i in range(PLACES)])  9.17 us
    ppermute x4, starting transfers between devices, to_both(): return lax.ppermute(value, ('node', 'local'), perm)  7.52 us
    ppermute x6, waiting for transfers between devices, to_place(): return lax.ppermute(value, 'local', [(i, i ^ bits) for i in range(PLACES)])  7.1 us
    pallas_call x2, Pallas kernels, down(): pl.pallas_call(down_kernel, out_shape=[jax.ShapeDtypeStruct((rows // 2, w...  6.09 us
    ppermute x4, waiting for transfers between devices, to_both(): return lax.ppermute(value, ('node', 'local'), perm)  5.99 us
    ppermute x4, starting transfers between devices, to_chip(): return lax.ppermute(value, 'node', [(i, i ^ 2) for i in range(2 * CHIPS)])  3.68 us
    ppermute x7, starting transfers between devices, to_core(): return lax.ppermute(value, 'node', [(i, i ^ 1) for i in range(2 * CHIPS)])  1.79 us
  transfers between devices with their start and end apart: 21, of which 13 were waited for; matrix products, arithmetic and copies ran while one was open for 1% of the time, Pallas kernels for 15%

profile of v8, /device:TPU:0, one launch (start us, length us, event | category | flops | bytes accessed | tf_op | source)
XLA Modules:
  0.0 58.4 jit_solution(1669289589587355287)
XLA Ops:
  0.0 0.0 copy-start
  0.0 0.0 copy-start.1
  0.0 1.2 %pack.1.refs_0_ = bf16[8,7296]{1,0:T(8,128)(2,1)S(1)} custom-call(bf16[8,7168]{1,0:T(8,128)(2,1)} %refs_0_.1, s32[4,8]{1,0:T(4,128)} %bitcast.7, f32[4,8]{1,0:T(4,128)} %bitcast.8, s32[8]{0:T(128)} %refs_3_.1, bf16[2,7168,512]{2,1,0:T(8,128)(2,1)} %refs_8_.1, bf16[2,7168,512]{2,1,0:T(8,128)(2,1)} %refs_9_.1, bf16[2,512,7168]{2,1,0:T(8,128)(2,1)} %refs_6_.2), custom_call_target="tpu_custom_call" | custom-call | tf_op jit(solution)/shard_map/pack/pallas_call | solution.py:49
  1.2 4.1 %collective-permute-start.3 = (bf16[8,7296]{1,0:T(8,128)(2,1)S(1)}, bf16[8,7296]{1,0:T(8,128)(2,1)S(1)}, u32[]{:S(2)}, u32[]{:S(2)}) collective-permute-start(bf16[8,7296]{1,0:T(8,128)(2,1)S(1)} %pack.1.refs_0_), channel_id=1, source_target_pairs={{0,2},{1,3},{2,0},{3,1},{4,6},{5,7},{6,4},{7,5},{8,10},{9,11},{10,... | collective-permute-start | bytes 350216 | tf_op jit(solution)/shard_map/ppermute | solution.py:173
  5.3 2.5 %collective-permute-start.2 = (bf16[8,7296]{1,0:T(8,128)(2,1)S(1)}, bf16[8,7296]{1,0:T(8,128)(2,1)S(1)}, u32[]{:S(2)}, u32[]{:S(2)}) collective-permute-start(bf16[8,7296]{1,0:T(8,128)(2,1)S(1)} %pack.1.refs_0_), channel_id=1, source_target_pairs={{0,9},{1,8},{2,11},{3,10},{4,13},{5,12},{6,15},{7,14},{8,1},{9,0},... | collective-permute-start | bytes 350216 | tf_op jit(solution)/shard_map/ppermute | solution.py:179
  7.8 0.4 collective-permute-start.1
  8.2 0.5 collective-permute-start
  8.8 2.3 %collective-permute-done.3.refs_0_ = bf16[8,7296]{1,0:T(8,128)(2,1)S(1)} collective-permute-done((bf16[8,7296]{1,0:T(8,128)(2,1)S(1)}, bf16[8,7296]{1,0:T(8,128)(2,1)S(1)}, u32[]{:S(2)}, u32[]{:S(2)}) %collective-permute-start.3) | collective-permute-done | bytes 116768 | tf_op jit(solution)/shard_map/ppermute | solution.py:173
  11.1 2.5 %collective-permute-done.2.refs_3_ = bf16[8,7296]{1,0:T(8,128)(2,1)S(1)} collective-permute-done((bf16[8,7296]{1,0:T(8,128)(2,1)S(1)}, bf16[8,7296]{1,0:T(8,128)(2,1)S(1)}, u32[]{:S(2)}, u32[]{:S(2)}) %collective-permute-start.2) | collective-permute-done | bytes 116768 | tf_op jit(solution)/shard_map/ppermute | solution.py:179
  13.6 1.1 %collective-permute-done.1.refs_2_ = bf16[8,7296]{1,0:T(8,128)(2,1)S(1)} collective-permute-done((bf16[8,7296]{1,0:T(8,128)(2,1)S(1)}, bf16[8,7296]{1,0:T(8,128)(2,1)S(1)}, u32[]{:S(2)}, u32[]{:S(2)}) %collective-permute-start.1) | collective-permute-done | bytes 116768 | tf_op jit(solution)/shard_map/ppermute | solution.py:173
  14.7 0.0 collective-permute-done.refs_1_
  14.7 0.1 stack.1
  14.8 0.1 collective-permute-start.4
  14.9 1.5 %collective-permute-start.7 = (bf16[8,7296]{1,0:T(8,128)(2,1)S(1)}, bf16[8,7296]{1,0:T(8,128)(2,1)S(1)}, u32[]{:S(2)}, u32[]{:S(2)}) collective-permute-start(bf16[8,7296]{1,0:T(8,128)(2,1)S(1)} %collective-permute-done.3.refs_0_), channel_id=1, source_target_pairs={{0,9},{1,8},{2,11},{3,10},{4,13},{5,12},{6,15},{7,14},{8,1},{9,0},... | collective-permute-start | bytes 350216 | tf_op jit(solution)/shard_map/ppermute | solution.py:179
  16.4 1.0 %collective-permute-start.6 = (bf16[8,7296]{1,0:T(8,128)(2,1)S(1)}, bf16[8,7296]{1,0:T(8,128)(2,1)S(1)}, u32[]{:S(2)}, u32[]{:S(2)}) collective-permute-start(bf16[8,7296]{1,0:T(8,128)(2,1)S(1)} %collective-permute-done.3.refs_0_), channel_id=1, source_target_pairs={{0,8},{4,12},{8,0},{12,4},{1,9},{5,13},{9,1},{13,5},{2,10},{6,14},... | collective-permute-start | bytes 350216 | tf_op jit(solution)/shard_map/ppermute | solution.py:169
  17.4 1.0 %collective-permute-start.5 = (bf16[8,7296]{1,0:T(8,128)(2,1)S(1)}, bf16[8,7296]{1,0:T(8,128)(2,1)S(1)}, u32[]{:S(2)}, u32[]{:S(2)}) collective-permute-start(bf16[8,7296]{1,0:T(8,128)(2,1)S(1)} %collective-permute-done.3.refs_0_), channel_id=1, source_target_pairs={{0,1},{1,0},{2,3},{3,2},{4,5},{5,4},{6,7},{7,6},{8,9},{9,8},{10,11... | collective-permute-start | bytes 350216 | tf_op jit(solution)/shard_map/ppermute | solution.py:173
  18.4 0.0 collective-permute-done.4.refs_4_
  18.4 0.0 copy-done
  18.4 0.0 copy-done.1
  18.4 0.0 slice-start
  18.4 0.0 slice-start.1
  18.4 5.9 %hidden.2.hidden_ref = bf16[64,1024]{1,0:T(8,128)(2,1)S(1)} custom-call(bf16[8,7296]{1,0:T(8,128)(2,1)S(1)} %pack.1.refs_0_, bf16[8,7296]{1,0:T(8,128)(2,1)S(1)} %collective-permute-done.refs_1_, bf16[8,7296]{1,0:T(8,128)(2,1)S(1)} %collective-permute-done.1.refs_2_, bf16[8,7296]{1,0:T(8,128)(2,1)S(1)} %collective-permute-done.2.refs_3_, ...), custom_call_target="tpu_custom_call" | custom-call | flops 1879048192 | tf_op jit(solution)/shard_map/hidden/pallas_call | solution.py:112
  24.4 0.0 slice-start.2
  24.4 0.0 slice-start.3
  24.4 0.0 collective-permute-done.7.refs_3_
  24.4 0.0 collective-permute-done.6.refs_2_
  24.4 0.0 collective-permute-done.5.refs_1_
  24.4 0.1 collective-permute-start.8
  24.5 0.5 collective-permute-start.9
  25.0 0.1 collective-permute-start.10
  25.1 0.4 collective-permute-start.11
  25.5 0.3 collective-permute-done.8.refs_4_
  25.8 0.2 collective-permute-done.9.refs_5_
  26.0 0.3 collective-permute-done.10.refs_6_
  26.3 0.2 collective-permute-done.11.refs_7_
  26.5 6.0 %hidden.3.hidden_ref = bf16[64,1024]{1,0:T(8,128)(2,1)S(1)} custom-call(bf16[8,7296]{1,0:T(8,128)(2,1)S(1)} %collective-permute-done.3.refs_0_, bf16[8,7296]{1,0:T(8,128)(2,1)S(1)} %collective-permute-done.5.refs_1_, bf16[8,7296]{1,0:T(8,128)(2,1)S(1)} %collective-permute-done.6.refs_2_, bf16[8,7296]{1,0:T(8,128)(2,1)S(1)} %collective-permute-done.7.refs_3_, ...), custom_call_target="tpu_custom_call" | custom-call | flops 1879048192 | tf_op jit(solution)/shard_map/hidden/pallas_call | solution.py:112
  32.4 0.0 slice-done
  32.5 0.0 slice-done.1
  32.5 0.0 slice-done.2
  32.5 0.0 slice-done.3
  32.5 3.0 %down.2 = (bf16[32,7168]{1,0:T(8,128)(2,1)S(1)}, bf16[32,7168]{1,0:T(8,128)(2,1)S(1)}) custom-call(bf16[64,1024]{1,0:T(8,128)(2,1)S(1)} %hidden.3.hidden_ref, bf16[1024,7168]{1,0:T(8,128)(2,1)S(1)} %bitcast.5), custom_call_target="tpu_custom_call" | custom-call | flops 939524096 | tf_op jit(solution)/shard_map/down/pallas_call | solution.py:148
  35.5 0.4 collective-permute-start.14
  36.0 3.0 %down.3 = (bf16[32,7168]{1,0:T(8,128)(2,1)S(1)}, bf16[32,7168]{1,0:T(8,128)(2,1)S(1)}) custom-call(bf16[64,1024]{1,0:T(8,128)(2,1)S(1)} %hidden.2.hidden_ref, bf16[1024,7168]{1,0:T(8,128)(2,1)S(1)} %bitcast.6), custom_call_target="tpu_custom_call" | custom-call | flops 939524096 | tf_op jit(solution)/shard_map/down/pallas_call | solution.py:148
  39.0 0.2 collective-permute-start.12
  39.2 0.0 collective-permute-done.14
  39.2 0.1 add_convert_fusion
  39.4 0.6 %collective-permute-start.15 = (bf16[8,7168]{1,0:T(8,128)(2,1)S(1)}, bf16[8,7168]{1,0:T(8,128)(2,1)S(1)}, u32[]{:S(2)}, u32[]{:S(2)}) collective-permute-start(bf16[8,7168]{1,0:T(8,128)(2,1)S(1)} %get-tuple-element.34), channel_id=1, source_target_pairs={{0,8},{4,12},{8,0},{12,4},{1,9},{5,13},{9,1},{13,5},{2,10},{6,14},... | collective-permute-start | bytes 344072 | tf_op jit(solution)/shard_map/ppermute | solution.py:169
  40.0 1.4 %collective-permute-start.17 = (bf16[8,7168]{1,0:T(8,128)(2,1)S(1)}, bf16[8,7168]{1,0:T(8,128)(2,1)S(1)}, u32[]{:S(2)}, u32[]{:S(2)}) collective-permute-start(bf16[8,7168]{1,0:T(8,128)(2,1)S(1)} %get-tuple-element.35), channel_id=1, source_target_pairs={{0,1},{1,0},{2,3},{3,2},{4,5},{5,4},{6,7},{7,6},{8,9},{9,8},{10,11... | collective-permute-start | bytes 344072 | tf_op jit(solution)/shard_map/ppermute | solution.py:173
  41.5 1.5 %collective-permute-start.16 = (bf16[8,7168]{1,0:T(8,128)(2,1)S(1)}, bf16[8,7168]{1,0:T(8,128)(2,1)S(1)}, u32[]{:S(2)}, u32[]{:S(2)}) collective-permute-start(bf16[8,7168]{1,0:T(8,128)(2,1)S(1)} %get-tuple-element.36), channel_id=1, source_target_pairs={{0,9},{1,8},{2,11},{3,10},{4,13},{5,12},{6,15},{7,14},{8,1},{9,0},... | collective-permute-start | bytes 344072 | tf_op jit(solution)/shard_map/ppermute | solution.py:179
  42.9 0.0 collective-permute-done.12
  42.9 0.1 add_convert_fusion.1
  43.1 1.1 %collective-permute-start.13 = (bf16[8,7168]{1,0:T(8,128)(2,1)S(1)}, bf16[8,7168]{1,0:T(8,128)(2,1)S(1)}, u32[]{:S(2)}, u32[]{:S(2)}) collective-permute-start(bf16[8,7168]{1,0:T(8,128)(2,1)S(1)} %get-tuple-element.33), channel_id=1, source_target_pairs={{0,1},{1,0},{2,3},{3,2},{4,5},{5,4},{6,7},{7,6},{8,9},{9,8},{10,11... | collective-permute-start | bytes 344072 | tf_op jit(solution)/shard_map/ppermute | solution.py:173
  44.1 0.7 %collective-permute-done.15 = bf16[8,7168]{1,0:T(8,128)(2,1)S(1)} collective-permute-done((bf16[8,7168]{1,0:T(8,128)(2,1)S(1)}, bf16[8,7168]{1,0:T(8,128)(2,1)S(1)}, u32[]{:S(2)}, u32[]{:S(2)}) %collective-permute-start.15) | collective-permute-done | bytes 114720 | tf_op jit(solution)/shard_map/ppermute | solution.py:169
  44.8 1.2 %collective-permute-done.17 = bf16[8,7168]{1,0:T(8,128)(2,1)S(1)} collective-permute-done((bf16[8,7168]{1,0:T(8,128)(2,1)S(1)}, bf16[8,7168]{1,0:T(8,128)(2,1)S(1)}, u32[]{:S(2)}, u32[]{:S(2)}) %collective-permute-start.17) | collective-permute-done | bytes 114720 | tf_op jit(solution)/shard_map/ppermute | solution.py:173
  46.1 3.3 %collective-permute-done.16 = bf16[8,7168]{1,0:T(8,128)(2,1)S(1)} collective-permute-done((bf16[8,7168]{1,0:T(8,128)(2,1)S(1)}, bf16[8,7168]{1,0:T(8,128)(2,1)S(1)}, u32[]{:S(2)}, u32[]{:S(2)}) %collective-permute-start.16) | collective-permute-done | bytes 114720 | tf_op jit(solution)/shard_map/ppermute | solution.py:179
  49.4 0.1 add_convert_fusion.3
  49.4 1.1 %collective-permute-start.18 = (bf16[8,7168]{1,0:T(8,128)(2,1)S(1)}, bf16[8,7168]{1,0:T(8,128)(2,1)S(1)}, u32[]{:S(2)}, u32[]{:S(2)}) collective-permute-start(bf16[8,7168]{1,0:T(8,128)(2,1)S(1)} %add_convert_fusion.3), channel_id=1, source_target_pairs={{0,2},{1,3},{2,0},{3,1},{4,6},{5,7},{6,4},{7,5},{8,10},{9,11},{10,... | collective-permute-start | bytes 344072 | tf_op jit(solution)/shard_map/ppermute | solution.py:173
  50.5 0.0 collective-permute-done.13
  50.5 2.0 %collective-permute-start.20 = (bf16[8,7168]{1,0:T(8,128)(2,1)S(1)}, bf16[8,7168]{1,0:T(8,128)(2,1)S(1)}, u32[]{:S(2)}, u32[]{:S(2)}) collective-permute-start(bf16[8,7168]{1,0:T(8,128)(2,1)S(1)} %get-tuple-element.30), channel_id=1, source_target_pairs={{0,9},{1,8},{2,11},{3,10},{4,13},{5,12},{6,15},{7,14},{8,1},{9,0},... | collective-permute-start | bytes 344072 | tf_op jit(solution)/shard_map/ppermute | solution.py:179
  52.6 1.5 %collective-permute-start.19 = (bf16[8,7168]{1,0:T(8,128)(2,1)S(1)}, bf16[8,7168]{1,0:T(8,128)(2,1)S(1)}, u32[]{:S(2)}, u32[]{:S(2)}) collective-permute-start(bf16[8,7168]{1,0:T(8,128)(2,1)S(1)} %get-tuple-element.29), channel_id=1, source_target_pairs={{0,8},{4,12},{8,0},{12,4},{1,9},{5,13},{9,1},{13,5},{2,10},{6,14},... | collective-permute-start | bytes 344072 | tf_op jit(solution)/shard_map/ppermute | solution.py:169
  54.1 2.5 %collective-permute-done.18 = bf16[8,7168]{1,0:T(8,128)(2,1)S(1)} collective-permute-done((bf16[8,7168]{1,0:T(8,128)(2,1)S(1)}, bf16[8,7168]{1,0:T(8,128)(2,1)S(1)}, u32[]{:S(2)}, u32[]{:S(2)}) %collective-permute-start.18) | collective-permute-done | bytes 114720 | tf_op jit(solution)/shard_map/ppermute | solution.py:173
  56.5 0.2 collective-permute-done.20
  56.7 1.0 %collective-permute-done.19 = bf16[8,7168]{1,0:T(8,128)(2,1)S(1)} collective-permute-done((bf16[8,7168]{1,0:T(8,128)(2,1)S(1)}, bf16[8,7168]{1,0:T(8,128)(2,1)S(1)}, u32[]{:S(2)}, u32[]{:S(2)}) %collective-permute-start.19) | collective-permute-done | bytes 114720 | tf_op jit(solution)/shard_map/ppermute | solution.py:169
  57.7 0.7 %add_convert_fusion.2 = bf16[8,7168]{1,0:T(8,128)(2,1)} fusion(bf16[8,7168]{1,0:T(8,128)(2,1)S(1)} %collective-permute-done.20, bf16[8,7168]{1,0:T(8,128)(2,1)S(1)} %collective-permute-done.19, bf16[8,7168]{1,0:T(8,128)(2,1)S(1)} %collective-permute-done.18, bf16[8,7168]{1,0:T(8,128)(2,1)S(1)} %collective-permute-done.13, ...), kind=kLoop, calls=%fused_computation.2 | loop fusion | flops 573440 | bytes 688128 | tf_op jit(solution)/shard_map/convert_element_type | solution.py:216
  (3 shorter events, 0.1 us)
Async XLA Ops:
  0.0 18.4 %copy-start = (bf16[2,7168,512]{2,1,0:T(8,128)(2,1)S(1)}, bf16[2,7168,512]{2,1,0:T(8,128)(2,1)}, u32[]{:S(2)}) copy-start(bf16[2,7168,512]{2,1,0:T(8,128)(2,1)} %refs_8_.1) | copy-start | bytes 44040196
  0.0 18.4 %copy-start.1 = (bf16[2,7168,512]{2,1,0:T(8,128)(2,1)S(1)}, bf16[2,7168,512]{2,1,0:T(8,128)(2,1)}, u32[]{:S(2)}) copy-start(bf16[2,7168,512]{2,1,0:T(8,128)(2,1)} %refs_9_.1) | copy-start | bytes 44040196
  1.2 9.9 %collective-permute-start.3 = (bf16[8,7296]{1,0:T(8,128)(2,1)S(1)}, bf16[8,7296]{1,0:T(8,128)(2,1)S(1)}, u32[]{:S(2)}, u32[]{:S(2)}) collective-permute-start(bf16[8,7296]{1,0:T(8,128)(2,1)S(1)} %pack.1.refs_0_), channel_id=1, source_target_pairs={{0,2},{1,3},{2,0},{3,1},{4,6},{5,7},{6,4},{7,5},{8,10},{9,11},{10,... | collective-permute-start | bytes 350216 | tf_op jit(solution)/shard_map/ppermute | solution.py:173
  5.3 8.3 %collective-permute-start.2 = (bf16[8,7296]{1,0:T(8,128)(2,1)S(1)}, bf16[8,7296]{1,0:T(8,128)(2,1)S(1)}, u32[]{:S(2)}, u32[]{:S(2)}) collective-permute-start(bf16[8,7296]{1,0:T(8,128)(2,1)S(1)} %pack.1.refs_0_), channel_id=1, source_target_pairs={{0,9},{1,8},{2,11},{3,10},{4,13},{5,12},{6,15},{7,14},{8,1},{9,0},... | collective-permute-start | bytes 350216 | tf_op jit(solution)/shard_map/ppermute | solution.py:179
  7.8 6.9 %collective-permute-start.1 = (bf16[8,7296]{1,0:T(8,128)(2,1)S(1)}, bf16[8,7296]{1,0:T(8,128)(2,1)S(1)}, u32[]{:S(2)}, u32[]{:S(2)}) collective-permute-start(bf16[8,7296]{1,0:T(8,128)(2,1)S(1)} %pack.1.refs_0_), channel_id=1, source_target_pairs={{0,1},{1,0},{2,3},{3,2},{4,5},{5,4},{6,7},{7,6},{8,9},{9,8},{10,11... | collective-permute-start | bytes 350216 | tf_op jit(solution)/shard_map/ppermute | solution.py:173
  8.2 6.5 %collective-permute-start = (bf16[8,7296]{1,0:T(8,128)(2,1)S(1)}, bf16[8,7296]{1,0:T(8,128)(2,1)S(1)}, u32[]{:S(2)}, u32[]{:S(2)}) collective-permute-start(bf16[8,7296]{1,0:T(8,128)(2,1)S(1)} %pack.1.refs_0_), channel_id=1, source_target_pairs={{0,8},{4,12},{8,0},{12,4},{1,9},{5,13},{9,1},{13,5},{2,10},{6,14},... | collective-permute-start | bytes 350216 | tf_op jit(solution)/shard_map/ppermute | solution.py:169
  14.8 3.6 %collective-permute-start.4 = (bf16[32,7296]{1,0:T(8,128)(2,1)S(1)}, bf16[32,7296]{1,0:T(8,128)(2,1)S(1)}, u32[]{:S(2)}, u32[]{:S(2)}) collective-permute-start(bf16[32,7296]{1,0:T(8,128)(2,1)S(1)} %stack.1), channel_id=1, source_target_pairs={{0,4},{4,0},{8,12},{12,8},{1,5},{5,1},{9,13},{13,9},{2,6},{6,2},{1... | collective-permute-start | bytes 1400840 | tf_op jit(solution)/shard_map/ppermute | solution.py:165
  14.9 9.5 %collective-permute-start.7 = (bf16[8,7296]{1,0:T(8,128)(2,1)S(1)}, bf16[8,7296]{1,0:T(8,128)(2,1)S(1)}, u32[]{:S(2)}, u32[]{:S(2)}) collective-permute-start(bf16[8,7296]{1,0:T(8,128)(2,1)S(1)} %collective-permute-done.3.refs_0_), channel_id=1, source_target_pairs={{0,9},{1,8},{2,11},{3,10},{4,13},{5,12},{6,15},{7,14},{8,1},{9,0},... | collective-permute-start | bytes 350216 | tf_op jit(solution)/shard_map/ppermute | solution.py:179
  16.4 8.0 %collective-permute-start.6 = (bf16[8,7296]{1,0:T(8,128)(2,1)S(1)}, bf16[8,7296]{1,0:T(8,128)(2,1)S(1)}, u32[]{:S(2)}, u32[]{:S(2)}) collective-permute-start(bf16[8,7296]{1,0:T(8,128)(2,1)S(1)} %collective-permute-done.3.refs_0_), channel_id=1, source_target_pairs={{0,8},{4,12},{8,0},{12,4},{1,9},{5,13},{9,1},{13,5},{2,10},{6,14},... | collective-permute-start | bytes 350216 | tf_op jit(solution)/shard_map/ppermute | solution.py:169
  17.4 7.0 %collective-permute-start.5 = (bf16[8,7296]{1,0:T(8,128)(2,1)S(1)}, bf16[8,7296]{1,0:T(8,128)(2,1)S(1)}, u32[]{:S(2)}, u32[]{:S(2)}) collective-permute-start(bf16[8,7296]{1,0:T(8,128)(2,1)S(1)} %collective-permute-done.3.refs_0_), channel_id=1, source_target_pairs={{0,1},{1,0},{2,3},{3,2},{4,5},{5,4},{6,7},{7,6},{8,9},{9,8},{10,11... | collective-permute-start | bytes 350216 | tf_op jit(solution)/shard_map/ppermute | solution.py:173
  18.4 14.0 %slice-start = ((s8[14680064]{0:T(1024)(128)(4,1)}), s8[4194304]{0:T(1024)(128)(4,1)S(1)}, s32[]{:S(2)}) async-start(s8[14680064]{0:T(1024)(128)(4,1)} %bitcast.3), calls=%async_computation | async-start | bytes 8388608
  18.4 14.0 %slice-start.1 = ((s8[14680064]{0:T(1024)(128)(4,1)}), s8[4194304]{0:T(1024)(128)(4,1)S(1)}, s32[]{:S(2)}) async-start(s8[14680064]{0:T(1024)(128)(4,1)} %bitcast.3), calls=%async_computation.1 | async-start | bytes 8388608
  24.4 8.1 %slice-start.2 = ((s8[14680064]{0:T(1024)(128)(4,1)}), s8[4194304]{0:T(1024)(128)(4,1)S(1)}, s32[]{:S(2)}) async-start(s8[14680064]{0:T(1024)(128)(4,1)} %bitcast.3), calls=%async_computation.2 | async-start | bytes 8388608
  24.4 8.1 %slice-start.3 = ((s8[14680064]{0:T(1024)(128)(4,1)}), s8[2097152]{0:T(1024)(128)(4,1)S(1)}, s32[]{:S(2)}) async-start(s8[14680064]{0:T(1024)(128)(4,1)} %bitcast.3), calls=%async_computation.3 | async-start | bytes 4194304
  24.4 1.4 %collective-permute-start.8 = (bf16[8,7296]{1,0:T(8,128)(2,1)S(1)}, bf16[8,7296]{1,0:T(8,128)(2,1)S(1)}, u32[]{:S(2)}, u32[]{:S(2)}) collective-permute-start(bf16[8,7296]{1,0:T(8,128)(2,1)S(1)} %collective-permute-done.3.refs_0_), channel_id=1, source_target_pairs={{0,4},{4,0},{8,12},{12,8},{1,5},{5,1},{9,13},{13,9},{2,6},{6,2},{1... | collective-permute-start | bytes 350216 | tf_op jit(solution)/shard_map/ppermute | solution.py:165
  24.5 1.5 %collective-permute-start.9 = (bf16[8,7296]{1,0:T(8,128)(2,1)S(1)}, bf16[8,7296]{1,0:T(8,128)(2,1)S(1)}, u32[]{:S(2)}, u32[]{:S(2)}) collective-permute-start(bf16[8,7296]{1,0:T(8,128)(2,1)S(1)} %collective-permute-done.5.refs_1_), channel_id=1, source_target_pairs={{0,4},{4,0},{8,12},{12,8},{1,5},{5,1},{9,13},{13,9},{2,6},{6,2},{1... | collective-permute-start | bytes 350216 | tf_op jit(solution)/shard_map/ppermute | solution.py:165
  25.0 1.3 %collective-permute-start.10 = (bf16[8,7296]{1,0:T(8,128)(2,1)S(1)}, bf16[8,7296]{1,0:T(8,128)(2,1)S(1)}, u32[]{:S(2)}, u32[]{:S(2)}) collective-permute-start(bf16[8,7296]{1,0:T(8,128)(2,1)S(1)} %collective-permute-done.6.refs_2_), channel_id=1, source_target_pairs={{0,4},{4,0},{8,12},{12,8},{1,5},{5,1},{9,13},{13,9},{2,6},{6,2},{1... | collective-permute-start | bytes 350216 | tf_op jit(solution)/shard_map/ppermute | solution.py:165
  25.1 1.4 %collective-permute-start.11 = (bf16[8,7296]{1,0:T(8,128)(2,1)S(1)}, bf16[8,7296]{1,0:T(8,128)(2,1)S(1)}, u32[]{:S(2)}, u32[]{:S(2)}) collective-permute-start(bf16[8,7296]{1,0:T(8,128)(2,1)S(1)} %collective-permute-done.7.refs_3_), channel_id=1, source_target_pairs={{0,4},{4,0},{8,12},{12,8},{1,5},{5,1},{9,13},{13,9},{2,6},{6,2},{1... | collective-permute-start | bytes 350216 | tf_op jit(solution)/shard_map/ppermute | solution.py:165
  35.5 3.7 %collective-permute-start.14 = (bf16[32,7168]{1,0:T(8,128)(2,1)S(1)}, bf16[32,7168]{1,0:T(8,128)(2,1)S(1)}, u32[]{:S(2)}, u32[]{:S(2)}) collective-permute-start(bf16[32,7168]{1,0:T(8,128)(2,1)S(1)} %get-tuple-element.23), channel_id=1, source_target_pairs={{0,4},{4,0},{8,12},{12,8},{1,5},{5,1},{9,13},{13,9},{2,6},{6,2},{1... | collective-permute-start | bytes 1376264 | tf_op jit(solution)/shard_map/ppermute | solution.py:165
  39.0 3.9 %collective-permute-start.12 = (bf16[32,7168]{1,0:T(8,128)(2,1)S(1)}, bf16[32,7168]{1,0:T(8,128)(2,1)S(1)}, u32[]{:S(2)}, u32[]{:S(2)}) collective-permute-start(bf16[32,7168]{1,0:T(8,128)(2,1)S(1)} %get-tuple-element.26), channel_id=1, source_target_pairs={{0,4},{4,0},{8,12},{12,8},{1,5},{5,1},{9,13},{13,9},{2,6},{6,2},{1... | collective-permute-start | bytes 1376264 | tf_op jit(solution)/shard_map/ppermute | solution.py:165
  39.4 5.5 %collective-permute-start.15 = (bf16[8,7168]{1,0:T(8,128)(2,1)S(1)}, bf16[8,7168]{1,0:T(8,128)(2,1)S(1)}, u32[]{:S(2)}, u32[]{:S(2)}) collective-permute-start(bf16[8,7168]{1,0:T(8,128)(2,1)S(1)} %get-tuple-element.34), channel_id=1, source_target_pairs={{0,8},{4,12},{8,0},{12,4},{1,9},{5,13},{9,1},{13,5},{2,10},{6,14},... | collective-permute-start | bytes 344072 | tf_op jit(solution)/shard_map/ppermute | solution.py:169
  40.0 6.0 %collective-permute-start.17 = (bf16[8,7168]{1,0:T(8,128)(2,1)S(1)}, bf16[8,7168]{1,0:T(8,128)(2,1)S(1)}, u32[]{:S(2)}, u32[]{:S(2)}) collective-permute-start(bf16[8,7168]{1,0:T(8,128)(2,1)S(1)} %get-tuple-element.35), channel_id=1, source_target_pairs={{0,1},{1,0},{2,3},{3,2},{4,5},{5,4},{6,7},{7,6},{8,9},{9,8},{10,11... | collective-permute-start | bytes 344072 | tf_op jit(solution)/shard_map/ppermute | solution.py:173
  41.5 7.9 %collective-permute-start.16 = (bf16[8,7168]{1,0:T(8,128)(2,1)S(1)}, bf16[8,7168]{1,0:T(8,128)(2,1)S(1)}, u32[]{:S(2)}, u32[]{:S(2)}) collective-permute-start(bf16[8,7168]{1,0:T(8,128)(2,1)S(1)} %get-tuple-element.36), channel_id=1, source_target_pairs={{0,9},{1,8},{2,11},{3,10},{4,13},{5,12},{6,15},{7,14},{8,1},{9,0},... | collective-permute-start | bytes 344072 | tf_op jit(solution)/shard_map/ppermute | solution.py:179
  43.1 7.5 %collective-permute-start.13 = (bf16[8,7168]{1,0:T(8,128)(2,1)S(1)}, bf16[8,7168]{1,0:T(8,128)(2,1)S(1)}, u32[]{:S(2)}, u32[]{:S(2)}) collective-permute-start(bf16[8,7168]{1,0:T(8,128)(2,1)S(1)} %get-tuple-element.33), channel_id=1, source_target_pairs={{0,1},{1,0},{2,3},{3,2},{4,5},{5,4},{6,7},{7,6},{8,9},{9,8},{10,11... | collective-permute-start | bytes 344072 | tf_op jit(solution)/shard_map/ppermute | solution.py:173
  49.4 7.1 %collective-permute-start.18 = (bf16[8,7168]{1,0:T(8,128)(2,1)S(1)}, bf16[8,7168]{1,0:T(8,128)(2,1)S(1)}, u32[]{:S(2)}, u32[]{:S(2)}) collective-permute-start(bf16[8,7168]{1,0:T(8,128)(2,1)S(1)} %add_convert_fusion.3), channel_id=1, source_target_pairs={{0,2},{1,3},{2,0},{3,1},{4,6},{5,7},{6,4},{7,5},{8,10},{9,11},{10,... | collective-permute-start | bytes 344072 | tf_op jit(solution)/shard_map/ppermute | solution.py:173
  50.5 6.1 %collective-permute-start.20 = (bf16[8,7168]{1,0:T(8,128)(2,1)S(1)}, bf16[8,7168]{1,0:T(8,128)(2,1)S(1)}, u32[]{:S(2)}, u32[]{:S(2)}) collective-permute-start(bf16[8,7168]{1,0:T(8,128)(2,1)S(1)} %get-tuple-element.30), channel_id=1, source_target_pairs={{0,9},{1,8},{2,11},{3,10},{4,13},{5,12},{6,15},{7,14},{8,1},{9,0},... | collective-permute-start | bytes 344072 | tf_op jit(solution)/shard_map/ppermute | solution.py:179
  52.6 5.1 %collective-permute-start.19 = (bf16[8,7168]{1,0:T(8,128)(2,1)S(1)}, bf16[8,7168]{1,0:T(8,128)(2,1)S(1)}, u32[]{:S(2)}, u32[]{:S(2)}) collective-permute-start(bf16[8,7168]{1,0:T(8,128)(2,1)S(1)} %get-tuple-element.29), channel_id=1, source_target_pairs={{0,8},{4,12},{8,0},{12,4},{1,9},{5,13},{9,1},{13,5},{2,10},{6,14},... | collective-permute-start | bytes 344072 | tf_op jit(solution)/shard_map/ppermute | solution.py:169

commit v9 on v7

--- a/solution.py
+++ b/solution.py
@@ -145,7 +145,6 @@
 
 
 CHIPS, PLACES = 2, 4
-GATHER_ORDER = (0, 2, 4, 5, 1, 3, 6, 7)
 
 
 def to_core(value):
@@ -173,29 +172,33 @@
 def gather_blocks(own):
     second, first, far_own = to_place(own, 2), to_place(own, 1), to_chip(own)
     far_first = to_chip(first)
-    other = [to_core(after(own, first)), to_core(after(far_own, first)), to_core(first)]
-    ready = after(second, far_first, far_own, other[0])
-    far_second, far_third, third = to_chip(ready), to_both(ready, 1), to_place(ready, 1)
-    other += [to_core(after(piece, third)) for piece in (far_first, second)]
-    other += [to_core(piece) for piece in (third, far_second, far_third)]
+    other = [to_core(own), to_core(far_own), to_core(first)]
+    ready = after(second, other[2], far_own)
+    far_second, third = to_chip(ready), to_place(ready, 1)
+    far_third = to_both(after(ready, far_first), 1)
+    other += [to_core(after(piece, far_second)) for piece in (far_first, second, third)]
+    other += [to_core(piece) for piece in (far_second, far_third)]
     chip = [own, far_own, first, far_first, second, third, far_second, far_third]
-    return [chip[i] for i in GATHER_ORDER] + [other[i] for i in GATHER_ORDER]
+    return chip + other
 
 
 def total(*terms):
     return sum(term.astype(jnp.float32) for term in terms)
 
 
-def reduce_blocks(near, far, other_near, other_far, rows):
-    other_far = to_core(other_far)
-    other_near = to_core(after(other_near, other_far))
-    far = total(far, other_far).astype(jnp.bfloat16).reshape(PLACES, rows, -1)
-    second, third = to_chip(far[2]), to_both(far[3], 1)
-    near = total(near, other_near).astype(jnp.bfloat16).reshape(PLACES, rows, -1)
-    second = total(near[2], second, third, to_place(near[3], 1)).astype(jnp.bfloat16)
-    own = total(near[0], after(to_place(near[1], 1), second))
-    far_own, far_first = to_chip(after(far[0], own)), to_both(after(far[1], own), 1)
-    return total(own, to_place(second, 2), far_own, far_first).astype(jnp.bfloat16)
+def reduce_blocks(early, late, other_early, other_late, rows):
+    def blocks(here, other):
+        return total(here, other).astype(jnp.bfloat16).reshape(PLACES, rows, -1)
+
+    other_late = to_core(other_late)
+    other_early = to_core(after(other_early, other_late))
+    second, third, far_second, far_third = blocks(late, other_late)
+    second = total(second, to_chip(far_second), to_both(far_third, 1), to_place(third, 1))
+    second = second.astype(jnp.bfloat16)
+    own, far_own, first, far_first = blocks(early, other_early)
+    first = total(first, to_chip(far_first)).astype(jnp.bfloat16)
+    far_own = to_chip(after(far_own, second))
+    return total(own, to_place(second, 2), far_own, to_place(first, 1)).astype(jnp.bfloat16)
 
 
 def by_permutes(tokens, expert_ids, route_weights, expert_slot, w_gate, w_up, w_down):

time: 56.8 us -> 52.3 us (0.921)
  waiting for transfers between devices: 22.3 us -> 17.4 us
    ppermute x5 -> x6, starting transfers between devices: 5.52 us -> 9.4 us  [to_chip(): return lax.ppermute(value, 'node', [(i, i ^ 2) for i in range(2 * CHIPS)])]
    ppermute x5 -> x6, waiting for transfers between devices: 4.48 us -> 0.97 us  [to_chip(): return lax.ppermute(value, 'node', [(i, i ^ 2) for i in range(2 * CHIPS)])]
    ppermute x6, starting transfers between devices: 12.3 us -> 10.3 us  [to_place(): return lax.ppermute(value, 'local', [(i, i ^ bits) for i in range(PLACES)])]
    ppermute x3 -> x2, waiting for transfers between devices: 4.9 us -> 3.22 us  [to_both(): return lax.ppermute(value, ('node', 'local'), perm)]
    ppermute x3 -> x2, starting transfers between devices: 4.63 us -> 3.18 us  [to_both(): return lax.ppermute(value, ('node', 'local'), perm)]
where the time goes in v9:
time: 52.3 us; the launch traced here: 52.2 us
  starting transfers between devices  24.4 us (47%)
  waiting for transfers between devices  17.4 us (33%)
  Pallas kernels  9.14 us (17%)
  other arithmetic  1.01 us (2%)
    ppermute x6, waiting for transfers between devices, to_place(): return lax.ppermute(value, 'local', [(i, i ^ bits) for i in range(PLACES)])  10.3 us
    ppermute x6, starting transfers between devices, to_place(): return lax.ppermute(value, 'local', [(i, i ^ bits) for i in range(PLACES)])  10.3 us
    ppermute x6, starting transfers between devices, to_chip(): return lax.ppermute(value, 'node', [(i, i ^ 2) for i in range(2 * CHIPS)])  9.4 us
    pallas_call x1, Pallas kernels, hidden_units(): pl.pallas_call(functools.partial(hidden_kernel, experts), out_shape=jax.S...  5.3 us
    ppermute x2, waiting for transfers between devices, to_both(): return lax.ppermute(value, ('node', 'local'), perm)  3.22 us
    ppermute x2, starting transfers between devices, to_both(): return lax.ppermute(value, ('node', 'local'), perm)  3.18 us
    ppermute x10, waiting for transfers between devices, to_core(): return lax.ppermute(value, 'node', [(i, i ^ 1) for i in range(2 * CHIPS)])  2.92 us
    pallas_call x1, Pallas kernels, down(): pl.pallas_call(functools.partial(down_kernel, chunk), out_shape=[jax.Shap...  2.68 us
  transfers between devices with their start and end apart: 24, of which 15 were waited for; matrix products, arithmetic and copies ran while one was open for 1% of the time, Pallas kernels for 0%

profile of v9, /device:TPU:0, one launch (start us, length us, event | category | flops | bytes accessed | tf_op | source)
XLA Modules:
  0.0 52.2 jit_solution(2724233951871022084)
XLA Ops:
  0.0 0.0 copy-start
  0.0 0.0 copy-start.1
  0.0 1.2 %pack.1.refs_0_ = bf16[8,7296]{1,0:T(8,128)(2,1)S(1)} custom-call(bf16[8,7168]{1,0:T(8,128)(2,1)} %refs_0_.1, s32[4,8]{1,0:T(4,128)} %bitcast.6, f32[4,8]{1,0:T(4,128)} %bitcast.7, s32[8]{0:T(128)} %refs_3_.1, bf16[2,7168,512]{2,1,0:T(8,128)(2,1)} %refs_16_.1, bf16[2,7168,512]{2,1,0:T(8,128)(2,1)} %refs_17_.1, bf16[2,512,7168]{2,1,0:T(8,128)(2,1)} %refs_6_.1), custom_call_target="tpu_custom_call" | custom-call | tf_op jit(solution)/shard_map/pack/pallas_call | solution.py:50
  1.2 0.0 slice-start.3
  1.2 3.1 %collective-permute-start.1 = (bf16[8,7296]{1,0:T(8,128)(2,1)S(1)}, bf16[8,7296]{1,0:T(8,128)(2,1)S(1)}, u32[]{:S(2)}, u32[]{:S(2)}) collective-permute-start(bf16[8,7296]{1,0:T(8,128)(2,1)S(1)} %pack.1.refs_0_), channel_id=1, source_target_pairs={{0,1},{1,0},{2,3},{3,2},{4,5},{5,4},{6,7},{7,6},{8,9},{9,8},{10,11... | collective-permute-start | bytes 350216 | tf_op jit(solution)/shard_map/ppermute | solution.py:159
  4.3 2.6 %collective-permute-start.3 = (bf16[8,7296]{1,0:T(8,128)(2,1)S(1)}, bf16[8,7296]{1,0:T(8,128)(2,1)S(1)}, u32[]{:S(2)}, u32[]{:S(2)}) collective-permute-start(bf16[8,7296]{1,0:T(8,128)(2,1)S(1)} %pack.1.refs_0_), channel_id=1, source_target_pairs={{0,2},{1,3},{2,0},{3,1},{4,6},{5,7},{6,4},{7,5},{8,10},{9,11},{10,... | collective-permute-start | bytes 350216 | tf_op jit(solution)/shard_map/ppermute | solution.py:159
  6.9 1.5 %collective-permute-start = (bf16[8,7296]{1,0:T(8,128)(2,1)S(1)}, bf16[8,7296]{1,0:T(8,128)(2,1)S(1)}, u32[]{:S(2)}, u32[]{:S(2)}) collective-permute-start(bf16[8,7296]{1,0:T(8,128)(2,1)S(1)} %pack.1.refs_0_), channel_id=1, source_target_pairs={{0,8},{4,12},{8,0},{12,4},{1,9},{5,13},{9,1},{13,5},{2,10},{6,14},... | collective-permute-start | bytes 350216 | tf_op jit(solution)/shard_map/ppermute | solution.py:155
  8.4 0.3 collective-permute-done.1.refs_2_
  8.7 0.0 collective-permute-start.4
  8.7 1.8 %collective-permute-start.2 = (bf16[8,7296]{1,0:T(8,128)(2,1)S(1)}, bf16[8,7296]{1,0:T(8,128)(2,1)S(1)}, u32[]{:S(2)}, u32[]{:S(2)}) collective-permute-start(bf16[8,7296]{1,0:T(8,128)(2,1)S(1)} %collective-permute-done.1.refs_2_), channel_id=1, source_target_pairs={{0,8},{4,12},{8,0},{12,4},{1,9},{5,13},{9,1},{13,5},{2,10},{6,14},... | collective-permute-start | bytes 350216 | tf_op jit(solution)/shard_map/ppermute | solution.py:155
  10.5 1.9 %collective-permute-done.3.refs_4_ = bf16[8,7296]{1,0:T(8,128)(2,1)S(1)} collective-permute-done((bf16[8,7296]{1,0:T(8,128)(2,1)S(1)}, bf16[8,7296]{1,0:T(8,128)(2,1)S(1)}, u32[]{:S(2)}, u32[]{:S(2)}) %collective-permute-start.3) | collective-permute-done | bytes 116768 | tf_op jit(solution)/shard_map/ppermute | solution.py:159
  12.4 0.0 collective-permute-done.refs_1_
  12.4 0.0 collective-permute-done.4.refs_10_
  12.4 1.5 %collective-permute-start.6 = (bf16[8,7296]{1,0:T(8,128)(2,1)S(1)}, bf16[8,7296]{1,0:T(8,128)(2,1)S(1)}, u32[]{:S(2)}, u32[]{:S(2)}) collective-permute-start(bf16[8,7296]{1,0:T(8,128)(2,1)S(1)} %collective-permute-done.3.refs_4_), channel_id=1, source_target_pairs={{0,8},{4,12},{8,0},{12,4},{1,9},{5,13},{9,1},{13,5},{2,10},{6,14},... | collective-permute-start | bytes 350216 | tf_op jit(solution)/shard_map/ppermute | solution.py:155
  13.9 0.4 collective-permute-start.5
  14.3 0.4 collective-permute-done.2.refs_3_
  14.7 1.6 %collective-permute-start.7 = (bf16[8,7296]{1,0:T(8,128)(2,1)S(1)}, bf16[8,7296]{1,0:T(8,128)(2,1)S(1)}, u32[]{:S(2)}, u32[]{:S(2)}) collective-permute-start(bf16[8,7296]{1,0:T(8,128)(2,1)S(1)} %collective-permute-done.3.refs_4_), channel_id=1, source_target_pairs={{0,9},{1,8},{2,11},{3,10},{4,13},{5,12},{6,15},{7,14},{8,1},{9,0},... | collective-permute-start | bytes 350216 | tf_op jit(solution)/shard_map/ppermute | solution.py:165
  16.3 0.0 collective-permute-start.8
  16.3 0.5 collective-permute-start.9
  16.8 0.4 collective-permute-done.6.refs_6_
  17.2 0.0 collective-permute-start.10
  17.2 2.4 %collective-permute-done.5.refs_5_ = bf16[8,7296]{1,0:T(8,128)(2,1)S(1)} collective-permute-done((bf16[8,7296]{1,0:T(8,128)(2,1)S(1)}, bf16[8,7296]{1,0:T(8,128)(2,1)S(1)}, u32[]{:S(2)}, u32[]{:S(2)}) %collective-permute-start.5) | collective-permute-done | bytes 116768 | tf_op jit(solution)/shard_map/ppermute | solution.py:159
  19.6 0.0 collective-permute-start.11
  19.6 1.6 %collective-permute-done.7.refs_7_ = bf16[8,7296]{1,0:T(8,128)(2,1)S(1)} collective-permute-done((bf16[8,7296]{1,0:T(8,128)(2,1)S(1)}, bf16[8,7296]{1,0:T(8,128)(2,1)S(1)}, u32[]{:S(2)}, u32[]{:S(2)}) %collective-permute-start.7) | collective-permute-done | bytes 116768 | tf_op jit(solution)/shard_map/ppermute | solution.py:165
  21.2 0.0 collective-permute-start.14
  21.2 0.0 collective-permute-done.8.refs_8_
  21.2 0.5 collective-permute-start.13
  21.7 0.0 collective-permute-done.9.refs_9_
  21.7 0.1 collective-permute-start.12
  21.8 0.7 %collective-permute-done.14.refs_15_ = bf16[8,7296]{1,0:T(8,128)(2,1)S(1)} collective-permute-done((bf16[8,7296]{1,0:T(8,128)(2,1)S(1)}, bf16[8,7296]{1,0:T(8,128)(2,1)S(1)}, u32[]{:S(2)}, u32[]{:S(2)}) %collective-permute-start.14) | collective-permute-done | bytes 116768 | tf_op jit(solution)/shard_map/ppermute | solution.py:151
  22.5 0.0 collective-permute-done.10.refs_11_
  22.5 0.0 collective-permute-done.11.refs_12_
  22.5 0.2 collective-permute-done.13.refs_14_
  22.7 0.4 collective-permute-done.12.refs_13_
  23.0 0.0 copy-done
  23.0 0.0 copy-done.1
  23.0 5.3 %hidden.1.hidden_ref = bf16[128,1024]{1,0:T(8,128)(2,1)S(1)} custom-call(bf16[8,7296]{1,0:T(8,128)(2,1)S(1)} %pack.1.refs_0_, bf16[8,7296]{1,0:T(8,128)(2,1)S(1)} %collective-permute-done.refs_1_, bf16[8,7296]{1,0:T(8,128)(2,1)S(1)} %collective-permute-done.1.refs_2_, bf16[8,7296]{1,0:T(8,128)(2,1)S(1)} %collective-permute-done.2.refs_3_, ...), custom_call_target="tpu_custom_call" | custom-call | flops 3758096384 | bytes 29360128 | tf_op jit(solution)/shard_map/hidden/pallas_call | solution.py:95
  28.3 0.0 slice-done
  28.4 0.0 slice-done.1
  28.4 0.0 slice-done.2
  28.4 0.0 slice-done.3
  28.4 2.7 %down.1 = (bf16[32,7168]{1,0:T(8,128)(2,1)S(1)}, bf16[32,7168]{1,0:T(8,128)(2,1)S(1)}, bf16[32,7168]{1,0:T(8,128)(2,1)S(1)}, bf16[32,7168]{1,0:T(8,128)(2,1)S(1)}) custom-call(bf16[128,1024]{1,0:T(8,128)(2,1)S(1)} %hidden.1.hidden_ref, bf16[1024,7168]{1,0:T(8,128)(2,1)S(1)} %bitcast.5), custom_call_target="tpu_custom_call" | custom-call | flops 1879048192 | bytes 14680064 | tf_op jit(solution)/shard_map/down/pallas_call | solution.py:132
  31.1 0.2 collective-permute-start.15
  31.3 1.7 %collective-permute-done.15 = bf16[32,7168]{1,0:T(8,128)(2,1)S(1)} collective-permute-done((bf16[32,7168]{1,0:T(8,128)(2,1)S(1)}, bf16[32,7168]{1,0:T(8,128)(2,1)S(1)}, u32[]{:S(2)}, u32[]{:S(2)}) %collective-permute-start.15) | collective-permute-done | bytes 458784 | tf_op jit(solution)/shard_map/ppermute | solution.py:151
  33.0 0.2 collective-permute-start.16
  33.1 0.1 add_convert_fusion
  33.3 1.6 %collective-permute-start.17 = (bf16[8,7168]{1,0:T(8,128)(2,1)S(1)}, bf16[8,7168]{1,0:T(8,128)(2,1)S(1)}, u32[]{:S(2)}, u32[]{:S(2)}) collective-permute-start(bf16[8,7168]{1,0:T(8,128)(2,1)S(1)} %get-tuple-element.27), channel_id=1, source_target_pairs={{0,8},{4,12},{8,0},{12,4},{1,9},{5,13},{9,1},{13,5},{2,10},{6,14},... | collective-permute-start | bytes 344072 | tf_op jit(solution)/shard_map/ppermute | solution.py:155
  34.8 0.4 collective-permute-start.19
  35.3 1.6 %collective-permute-start.18 = (bf16[8,7168]{1,0:T(8,128)(2,1)S(1)}, bf16[8,7168]{1,0:T(8,128)(2,1)S(1)}, u32[]{:S(2)}, u32[]{:S(2)}) collective-permute-start(bf16[8,7168]{1,0:T(8,128)(2,1)S(1)} %get-tuple-element.29), channel_id=1, source_target_pairs={{0,9},{1,8},{2,11},{3,10},{4,13},{5,12},{6,15},{7,14},{8,1},{9,0},... | collective-permute-start | bytes 344072 | tf_op jit(solution)/shard_map/ppermute | solution.py:165
  36.8 0.0 collective-permute-done.16
  36.8 0.1 add_convert_fusion.1
  37.0 1.6 %collective-permute-start.22 = (bf16[8,7168]{1,0:T(8,128)(2,1)S(1)}, bf16[8,7168]{1,0:T(8,128)(2,1)S(1)}, u32[]{:S(2)}, u32[]{:S(2)}) collective-permute-start(bf16[8,7168]{1,0:T(8,128)(2,1)S(1)} %get-tuple-element.31), channel_id=1, source_target_pairs={{0,8},{4,12},{8,0},{12,4},{1,9},{5,13},{9,1},{13,5},{2,10},{6,14},... | collective-permute-start | bytes 344072 | tf_op jit(solution)/shard_map/ppermute | solution.py:155
  38.5 0.2 collective-permute-done.17
  38.7 2.1 %collective-permute-done.19 = bf16[8,7168]{1,0:T(8,128)(2,1)S(1)} collective-permute-done((bf16[8,7168]{1,0:T(8,128)(2,1)S(1)}, bf16[8,7168]{1,0:T(8,128)(2,1)S(1)}, u32[]{:S(2)}, u32[]{:S(2)}) %collective-permute-start.19) | collective-permute-done | bytes 114720 | tf_op jit(solution)/shard_map/ppermute | solution.py:159
  40.8 1.7 %collective-permute-done.18 = bf16[8,7168]{1,0:T(8,128)(2,1)S(1)} collective-permute-done((bf16[8,7168]{1,0:T(8,128)(2,1)S(1)}, bf16[8,7168]{1,0:T(8,128)(2,1)S(1)}, u32[]{:S(2)}, u32[]{:S(2)}) %collective-permute-start.18) | collective-permute-done | bytes 114720 | tf_op jit(solution)/shard_map/ppermute | solution.py:165
  42.5 0.1 add_convert_fusion.4
  42.5 2.0 %collective-permute-start.20 = (bf16[8,7168]{1,0:T(8,128)(2,1)S(1)}, bf16[8,7168]{1,0:T(8,128)(2,1)S(1)}, u32[]{:S(2)}, u32[]{:S(2)}) collective-permute-start(bf16[8,7168]{1,0:T(8,128)(2,1)S(1)} %add_convert_fusion.4), channel_id=1, source_target_pairs={{0,2},{1,3},{2,0},{3,1},{4,6},{5,7},{6,4},{7,5},{8,10},{9,11},{10,... | collective-permute-start | bytes 344072 | tf_op jit(solution)/shard_map/ppermute | solution.py:159
  44.5 1.5 %collective-permute-start.21 = (bf16[8,7168]{1,0:T(8,128)(2,1)S(1)}, bf16[8,7168]{1,0:T(8,128)(2,1)S(1)}, u32[]{:S(2)}, u32[]{:S(2)}) collective-permute-start(bf16[8,7168]{1,0:T(8,128)(2,1)S(1)} %get-tuple-element.26), channel_id=1, source_target_pairs={{0,8},{4,12},{8,0},{12,4},{1,9},{5,13},{9,1},{13,5},{2,10},{6,14},... | collective-permute-start | bytes 344072 | tf_op jit(solution)/shard_map/ppermute | solution.py:155
  46.0 0.0 collective-permute-done.22
  46.1 1.7 %collective-permute-start.23 = (bf16[8,7168]{1,0:T(8,128)(2,1)S(1)}, bf16[8,7168]{1,0:T(8,128)(2,1)S(1)}, u32[]{:S(2)}, u32[]{:S(2)}) collective-permute-start(bf16[8,7168]{1,0:T(8,128)(2,1)S(1)} %add_convert_fusion.3), channel_id=1, source_target_pairs={{0,1},{1,0},{2,3},{3,2},{4,5},{5,4},{6,7},{7,6},{8,9},{9,8},{10,11... | collective-permute-start | bytes 344072 | tf_op jit(solution)/shard_map/ppermute | solution.py:159
  47.8 2.4 %collective-permute-done.20 = bf16[8,7168]{1,0:T(8,128)(2,1)S(1)} collective-permute-done((bf16[8,7168]{1,0:T(8,128)(2,1)S(1)}, bf16[8,7168]{1,0:T(8,128)(2,1)S(1)}, u32[]{:S(2)}, u32[]{:S(2)}) %collective-permute-start.20) | collective-permute-done | bytes 114720 | tf_op jit(solution)/shard_map/ppermute | solution.py:159
  50.2 0.0 collective-permute-done.21
  50.2 1.2 %collective-permute-done.23 = bf16[8,7168]{1,0:T(8,128)(2,1)S(1)} collective-permute-done((bf16[8,7168]{1,0:T(8,128)(2,1)S(1)}, bf16[8,7168]{1,0:T(8,128)(2,1)S(1)}, u32[]{:S(2)}, u32[]{:S(2)}) %collective-permute-start.23) | collective-permute-done | bytes 114720 | tf_op jit(solution)/shard_map/ppermute | solution.py:159
  51.4 0.7 %add_convert_fusion.2 = bf16[8,7168]{1,0:T(8,128)(2,1)} fusion(bf16[8,7168]{1,0:T(8,128)(2,1)S(1)} %collective-permute-done.23, bf16[8,7168]{1,0:T(8,128)(2,1)S(1)} %collective-permute-done.21, bf16[8,7168]{1,0:T(8,128)(2,1)S(1)} %collective-permute-done.20, bf16[32,7168]{1,0:T(8,128)(2,1)S(1)} %add_convert_fusion.1), kind=kLoop, calls=%fused_computation.2 | loop fusion | flops 458752 | bytes 573440 | tf_op jit(solution)/shard_map/convert_element_type | solution.py:201
  (7 shorter events, 0.1 us)
Async XLA Ops:
  0.0 23.0 %copy-start = (bf16[2,7168,512]{2,1,0:T(8,128)(2,1)S(1)}, bf16[2,7168,512]{2,1,0:T(8,128)(2,1)}, u32[]{:S(2)}) copy-start(bf16[2,7168,512]{2,1,0:T(8,128)(2,1)} %refs_16_.1) | copy-start | bytes 44040196
  0.0 23.0 %copy-start.1 = (bf16[2,7168,512]{2,1,0:T(8,128)(2,1)S(1)}, bf16[2,7168,512]{2,1,0:T(8,128)(2,1)}, u32[]{:S(2)}) copy-start(bf16[2,7168,512]{2,1,0:T(8,128)(2,1)} %refs_17_.1) | copy-start | bytes 44040196
  0.0 28.3 %slice-start = ((s8[14680064]{0:T(1024)(128)(4,1)}), s8[4194304]{0:T(1024)(128)(4,1)S(1)}, s32[]{:S(2)}) async-start(s8[14680064]{0:T(1024)(128)(4,1)} %bitcast.3), calls=%async_computation | async-start | bytes 8388608
  0.0 28.4 %slice-start.1 = ((s8[14680064]{0:T(1024)(128)(4,1)}), s8[4194304]{0:T(1024)(128)(4,1)S(1)}, s32[]{:S(2)}) async-start(s8[14680064]{0:T(1024)(128)(4,1)} %bitcast.3), calls=%async_computation.1 | async-start | bytes 8388608
  0.0 28.4 %slice-start.2 = ((s8[14680064]{0:T(1024)(128)(4,1)}), s8[4194304]{0:T(1024)(128)(4,1)S(1)}, s32[]{:S(2)}) async-start(s8[14680064]{0:T(1024)(128)(4,1)} %bitcast.3), calls=%async_computation.2 | async-start | bytes 8388608
  1.2 27.2 %slice-start.3 = ((s8[14680064]{0:T(1024)(128)(4,1)}), s8[2097152]{0:T(1024)(128)(4,1)S(1)}, s32[]{:S(2)}) async-start(s8[14680064]{0:T(1024)(128)(4,1)} %bitcast.3), calls=%async_computation.3 | async-start | bytes 4194304
  1.2 7.5 %collective-permute-start.1 = (bf16[8,7296]{1,0:T(8,128)(2,1)S(1)}, bf16[8,7296]{1,0:T(8,128)(2,1)S(1)}, u32[]{:S(2)}, u32[]{:S(2)}) collective-permute-start(bf16[8,7296]{1,0:T(8,128)(2,1)S(1)} %pack.1.refs_0_), channel_id=1, source_target_pairs={{0,1},{1,0},{2,3},{3,2},{4,5},{5,4},{6,7},{7,6},{8,9},{9,8},{10,11... | collective-permute-start | bytes 350216 | tf_op jit(solution)/shard_map/ppermute | solution.py:159
  4.3 8.1 %collective-permute-start.3 = (bf16[8,7296]{1,0:T(8,128)(2,1)S(1)}, bf16[8,7296]{1,0:T(8,128)(2,1)S(1)}, u32[]{:S(2)}, u32[]{:S(2)}) collective-permute-start(bf16[8,7296]{1,0:T(8,128)(2,1)S(1)} %pack.1.refs_0_), channel_id=1, source_target_pairs={{0,2},{1,3},{2,0},{3,1},{4,6},{5,7},{6,4},{7,5},{8,10},{9,11},{10,... | collective-permute-start | bytes 350216 | tf_op jit(solution)/shard_map/ppermute | solution.py:159
  6.9 5.5 %collective-permute-start = (bf16[8,7296]{1,0:T(8,128)(2,1)S(1)}, bf16[8,7296]{1,0:T(8,128)(2,1)S(1)}, u32[]{:S(2)}, u32[]{:S(2)}) collective-permute-start(bf16[8,7296]{1,0:T(8,128)(2,1)S(1)} %pack.1.refs_0_), channel_id=1, source_target_pairs={{0,8},{4,12},{8,0},{12,4},{1,9},{5,13},{9,1},{13,5},{2,10},{6,14},... | collective-permute-start | bytes 350216 | tf_op jit(solution)/shard_map/ppermute | solution.py:155
  8.7 3.7 %collective-permute-start.4 = (bf16[8,7296]{1,0:T(8,128)(2,1)S(1)}, bf16[8,7296]{1,0:T(8,128)(2,1)S(1)}, u32[]{:S(2)}, u32[]{:S(2)}) collective-permute-start(bf16[8,7296]{1,0:T(8,128)(2,1)S(1)} %collective-permute-done.1.refs_2_), channel_id=1, source_target_pairs={{0,4},{4,0},{8,12},{12,8},{1,5},{5,1},{9,13},{13,9},{2,6},{6,2},{1... | collective-permute-start | bytes 350216 | tf_op jit(solution)/shard_map/ppermute | solution.py:151
  8.7 6.0 %collective-permute-start.2 = (bf16[8,7296]{1,0:T(8,128)(2,1)S(1)}, bf16[8,7296]{1,0:T(8,128)(2,1)S(1)}, u32[]{:S(2)}, u32[]{:S(2)}) collective-permute-start(bf16[8,7296]{1,0:T(8,128)(2,1)S(1)} %collective-permute-done.1.refs_2_), channel_id=1, source_target_pairs={{0,8},{4,12},{8,0},{12,4},{1,9},{5,13},{9,1},{13,5},{2,10},{6,14},... | collective-permute-start | bytes 350216 | tf_op jit(solution)/shard_map/ppermute | solution.py:155
  12.4 4.8 %collective-permute-start.6 = (bf16[8,7296]{1,0:T(8,128)(2,1)S(1)}, bf16[8,7296]{1,0:T(8,128)(2,1)S(1)}, u32[]{:S(2)}, u32[]{:S(2)}) collective-permute-start(bf16[8,7296]{1,0:T(8,128)(2,1)S(1)} %collective-permute-done.3.refs_4_), channel_id=1, source_target_pairs={{0,8},{4,12},{8,0},{12,4},{1,9},{5,13},{9,1},{13,5},{2,10},{6,14},... | collective-permute-start | bytes 350216 | tf_op jit(solution)/shard_map/ppermute | solution.py:155
  13.9 5.7 %collective-permute-start.5 = (bf16[8,7296]{1,0:T(8,128)(2,1)S(1)}, bf16[8,7296]{1,0:T(8,128)(2,1)S(1)}, u32[]{:S(2)}, u32[]{:S(2)}) collective-permute-start(bf16[8,7296]{1,0:T(8,128)(2,1)S(1)} %collective-permute-done.3.refs_4_), channel_id=1, source_target_pairs={{0,1},{1,0},{2,3},{3,2},{4,5},{5,4},{6,7},{7,6},{8,9},{9,8},{10,11... | collective-permute-start | bytes 350216 | tf_op jit(solution)/shard_map/ppermute | solution.py:159
  14.7 6.5 %collective-permute-start.7 = (bf16[8,7296]{1,0:T(8,128)(2,1)S(1)}, bf16[8,7296]{1,0:T(8,128)(2,1)S(1)}, u32[]{:S(2)}, u32[]{:S(2)}) collective-permute-start(bf16[8,7296]{1,0:T(8,128)(2,1)S(1)} %collective-permute-done.3.refs_4_), channel_id=1, source_target_pairs={{0,9},{1,8},{2,11},{3,10},{4,13},{5,12},{6,15},{7,14},{8,1},{9,0},... | collective-permute-start | bytes 350216 | tf_op jit(solution)/shard_map/ppermute | solution.py:165
  16.3 4.9 %collective-permute-start.8 = (bf16[8,7296]{1,0:T(8,128)(2,1)S(1)}, bf16[8,7296]{1,0:T(8,128)(2,1)S(1)}, u32[]{:S(2)}, u32[]{:S(2)}) collective-permute-start(bf16[8,7296]{1,0:T(8,128)(2,1)S(1)} %pack.1.refs_0_), channel_id=1, source_target_pairs={{0,4},{4,0},{8,12},{12,8},{1,5},{5,1},{9,13},{13,9},{2,6},{6,2},{1... | collective-permute-start | bytes 350216 | tf_op jit(solution)/shard_map/ppermute | solution.py:151
  16.3 5.4 %collective-permute-start.9 = (bf16[8,7296]{1,0:T(8,128)(2,1)S(1)}, bf16[8,7296]{1,0:T(8,128)(2,1)S(1)}, u32[]{:S(2)}, u32[]{:S(2)}) collective-permute-start(bf16[8,7296]{1,0:T(8,128)(2,1)S(1)} %collective-permute-done.refs_1_), channel_id=1, source_target_pairs={{0,4},{4,0},{8,12},{12,8},{1,5},{5,1},{9,13},{13,9},{2,6},{6,2},{1... | collective-permute-start | bytes 350216 | tf_op jit(solution)/shard_map/ppermute | solution.py:151
  17.2 5.3 %collective-permute-start.10 = (bf16[8,7296]{1,0:T(8,128)(2,1)S(1)}, bf16[8,7296]{1,0:T(8,128)(2,1)S(1)}, u32[]{:S(2)}, u32[]{:S(2)}) collective-permute-start(bf16[8,7296]{1,0:T(8,128)(2,1)S(1)} %collective-permute-done.2.refs_3_), channel_id=1, source_target_pairs={{0,4},{4,0},{8,12},{12,8},{1,5},{5,1},{9,13},{13,9},{2,6},{6,2},{1... | collective-permute-start | bytes 350216 | tf_op jit(solution)/shard_map/ppermute | solution.py:151
  19.6 2.9 %collective-permute-start.11 = (bf16[8,7296]{1,0:T(8,128)(2,1)S(1)}, bf16[8,7296]{1,0:T(8,128)(2,1)S(1)}, u32[]{:S(2)}, u32[]{:S(2)}) collective-permute-start(bf16[8,7296]{1,0:T(8,128)(2,1)S(1)} %collective-permute-done.3.refs_4_), channel_id=1, source_target_pairs={{0,4},{4,0},{8,12},{12,8},{1,5},{5,1},{9,13},{13,9},{2,6},{6,2},{1... | collective-permute-start | bytes 350216 | tf_op jit(solution)/shard_map/ppermute | solution.py:151
  21.2 1.3 %collective-permute-start.14 = (bf16[8,7296]{1,0:T(8,128)(2,1)S(1)}, bf16[8,7296]{1,0:T(8,128)(2,1)S(1)}, u32[]{:S(2)}, u32[]{:S(2)}) collective-permute-start(bf16[8,7296]{1,0:T(8,128)(2,1)S(1)} %collective-permute-done.7.refs_7_), channel_id=1, source_target_pairs={{0,4},{4,0},{8,12},{12,8},{1,5},{5,1},{9,13},{13,9},{2,6},{6,2},{1... | collective-permute-start | bytes 350216 | tf_op jit(solution)/shard_map/ppermute | solution.py:151
  21.2 1.5 %collective-permute-start.13 = (bf16[8,7296]{1,0:T(8,128)(2,1)S(1)}, bf16[8,7296]{1,0:T(8,128)(2,1)S(1)}, u32[]{:S(2)}, u32[]{:S(2)}) collective-permute-start(bf16[8,7296]{1,0:T(8,128)(2,1)S(1)} %collective-permute-done.6.refs_6_), channel_id=1, source_target_pairs={{0,4},{4,0},{8,12},{12,8},{1,5},{5,1},{9,13},{13,9},{2,6},{6,2},{1... | collective-permute-start | bytes 350216 | tf_op jit(solution)/shard_map/ppermute | solution.py:151
  21.7 1.3 %collective-permute-start.12 = (bf16[8,7296]{1,0:T(8,128)(2,1)S(1)}, bf16[8,7296]{1,0:T(8,128)(2,1)S(1)}, u32[]{:S(2)}, u32[]{:S(2)}) collective-permute-start(bf16[8,7296]{1,0:T(8,128)(2,1)S(1)} %collective-permute-done.5.refs_5_), channel_id=1, source_target_pairs={{0,4},{4,0},{8,12},{12,8},{1,5},{5,1},{9,13},{13,9},{2,6},{6,2},{1... | collective-permute-start | bytes 350216 | tf_op jit(solution)/shard_map/ppermute | solution.py:151
  31.1 1.9 %collective-permute-start.15 = (bf16[32,7168]{1,0:T(8,128)(2,1)S(1)}, bf16[32,7168]{1,0:T(8,128)(2,1)S(1)}, u32[]{:S(2)}, u32[]{:S(2)}) collective-permute-start(bf16[32,7168]{1,0:T(8,128)(2,1)S(1)} %get-tuple-element.23), channel_id=1, source_target_pairs={{0,4},{4,0},{8,12},{12,8},{1,5},{5,1},{9,13},{13,9},{2,6},{6,2},{1... | collective-permute-start | bytes 1376264 | tf_op jit(solution)/shard_map/ppermute | solution.py:151
  33.0 3.9 %collective-permute-start.16 = (bf16[32,7168]{1,0:T(8,128)(2,1)S(1)}, bf16[32,7168]{1,0:T(8,128)(2,1)S(1)}, u32[]{:S(2)}, u32[]{:S(2)}) collective-permute-start(bf16[32,7168]{1,0:T(8,128)(2,1)S(1)} %get-tuple-element.24), channel_id=1, source_target_pairs={{0,4},{4,0},{8,12},{12,8},{1,5},{5,1},{9,13},{13,9},{2,6},{6,2},{1... | collective-permute-start | bytes 1376264 | tf_op jit(solution)/shard_map/ppermute | solution.py:151
  33.3 5.5 %collective-permute-start.17 = (bf16[8,7168]{1,0:T(8,128)(2,1)S(1)}, bf16[8,7168]{1,0:T(8,128)(2,1)S(1)}, u32[]{:S(2)}, u32[]{:S(2)}) collective-permute-start(bf16[8,7168]{1,0:T(8,128)(2,1)S(1)} %get-tuple-element.27), channel_id=1, source_target_pairs={{0,8},{4,12},{8,0},{12,4},{1,9},{5,13},{9,1},{13,5},{2,10},{6,14},... | collective-permute-start | bytes 344072 | tf_op jit(solution)/shard_map/ppermute | solution.py:155
  34.8 6.0 %collective-permute-start.19 = (bf16[8,7168]{1,0:T(8,128)(2,1)S(1)}, bf16[8,7168]{1,0:T(8,128)(2,1)S(1)}, u32[]{:S(2)}, u32[]{:S(2)}) collective-permute-start(bf16[8,7168]{1,0:T(8,128)(2,1)S(1)} %get-tuple-element.28), channel_id=1, source_target_pairs={{0,1},{1,0},{2,3},{3,2},{4,5},{5,4},{6,7},{7,6},{8,9},{9,8},{10,11... | collective-permute-start | bytes 344072 | tf_op jit(solution)/shard_map/ppermute | solution.py:159
  35.3 7.2 %collective-permute-start.18 = (bf16[8,7168]{1,0:T(8,128)(2,1)S(1)}, bf16[8,7168]{1,0:T(8,128)(2,1)S(1)}, u32[]{:S(2)}, u32[]{:S(2)}) collective-permute-start(bf16[8,7168]{1,0:T(8,128)(2,1)S(1)} %get-tuple-element.29), channel_id=1, source_target_pairs={{0,9},{1,8},{2,11},{3,10},{4,13},{5,12},{6,15},{7,14},{8,1},{9,0},... | collective-permute-start | bytes 344072 | tf_op jit(solution)/shard_map/ppermute | solution.py:165
  37.0 9.1 %collective-permute-start.22 = (bf16[8,7168]{1,0:T(8,128)(2,1)S(1)}, bf16[8,7168]{1,0:T(8,128)(2,1)S(1)}, u32[]{:S(2)}, u32[]{:S(2)}) collective-permute-start(bf16[8,7168]{1,0:T(8,128)(2,1)S(1)} %get-tuple-element.31), channel_id=1, source_target_pairs={{0,8},{4,12},{8,0},{12,4},{1,9},{5,13},{9,1},{13,5},{2,10},{6,14},... | collective-permute-start | bytes 344072 | tf_op jit(solution)/shard_map/ppermute | solution.py:155
  42.5 7.6 %collective-permute-start.20 = (bf16[8,7168]{1,0:T(8,128)(2,1)S(1)}, bf16[8,7168]{1,0:T(8,128)(2,1)S(1)}, u32[]{:S(2)}, u32[]{:S(2)}) collective-permute-start(bf16[8,7168]{1,0:T(8,128)(2,1)S(1)} %add_convert_fusion.4), channel_id=1, source_target_pairs={{0,2},{1,3},{2,0},{3,1},{4,6},{5,7},{6,4},{7,5},{8,10},{9,11},{10,... | collective-permute-start | bytes 344072 | tf_op jit(solution)/shard_map/ppermute | solution.py:159
  44.5 5.7 %collective-permute-start.21 = (bf16[8,7168]{1,0:T(8,128)(2,1)S(1)}, bf16[8,7168]{1,0:T(8,128)(2,1)S(1)}, u32[]{:S(2)}, u32[]{:S(2)}) collective-permute-start(bf16[8,7168]{1,0:T(8,128)(2,1)S(1)} %get-tuple-element.26), channel_id=1, source_target_pairs={{0,8},{4,12},{8,0},{12,4},{1,9},{5,13},{9,1},{13,5},{2,10},{6,14},... | collective-permute-start | bytes 344072 | tf_op jit(solution)/shard_map/ppermute | solution.py:155
  46.1 5.4 %collective-permute-start.23 = (bf16[8,7168]{1,0:T(8,128)(2,1)S(1)}, bf16[8,7168]{1,0:T(8,128)(2,1)S(1)}, u32[]{:S(2)}, u32[]{:S(2)}) collective-permute-start(bf16[8,7168]{1,0:T(8,128)(2,1)S(1)} %add_convert_fusion.3), channel_id=1, source_target_pairs={{0,1},{1,0},{2,3},{3,2},{4,5},{5,4},{6,7},{7,6},{8,9},{9,8},{10,11... | collective-permute-start | bytes 344072 | tf_op jit(solution)/shard_map/ppermute | solution.py:159

commit v10 on v9

--- a/solution.py
+++ b/solution.py
@@ -62,6 +62,24 @@
     )(*held)
 
 
+def stack_kernel(*refs):
+    *pieces, out_ref = refs
+    out_ref[...] = jnp.concatenate([piece[...] for piece in pieces], axis=0)
+
+
+def stack(*pieces):
+    rows = sum(piece.shape[0] for piece in pieces)
+    vmem = pl.BlockSpec(memory_space=pltpu.VMEM)
+    return pl.pallas_call(
+        stack_kernel,
+        out_shape=jax.ShapeDtypeStruct((rows, pieces[0].shape[1]), pieces[0].dtype),
+        in_specs=[vmem] * len(pieces),
+        out_specs=vmem,
+        compiler_params=pltpu.CompilerParams(vmem_limit_bytes=VMEM_LIMIT),
+        name="stack",
+    )(*pieces)
+
+
 def hidden_kernel(experts, *refs):
     *pieces, gate_ref, up_ref, out_ref, x_ref, weight_ref = refs
     members, width, hid = gate_ref.shape
@@ -172,14 +190,11 @@
 def gather_blocks(own):
     second, first, far_own = to_place(own, 2), to_place(own, 1), to_chip(own)
     far_first = to_chip(first)
-    other = [to_core(own), to_core(far_own), to_core(first)]
-    ready = after(second, other[2], far_own)
-    far_second, third = to_chip(ready), to_place(ready, 1)
-    far_third = to_both(after(ready, far_first), 1)
-    other += [to_core(after(piece, far_second)) for piece in (far_first, second, third)]
-    other += [to_core(piece) for piece in (far_second, far_third)]
-    chip = [own, far_own, first, far_first, second, third, far_second, far_third]
-    return chip + other
+    ready = after(second, far_own)
+    far_second, far_third = to_chip(ready), to_both(ready, 1)
+    third = to_place(after(ready, far_first), 1)
+    early, late = stack(own, far_own, first, far_first), stack(second, third, far_second, far_third)
+    return [early, late, to_core(early), to_core(late)]
 
 
 def total(*terms):

time: 52.3 us -> 53.9 us (1.031)
  waiting for transfers between devices: 17.4 us -> 19 us
    ppermute x6, starting transfers between devices: 10.3 us -> 12.4 us  [to_place(): return lax.ppermute(value, 'local', [(i, i ^ bits) for i in range(PLACES)])]
    ppermute x10 -> x4, starting transfers between devices: 1.49 us -> 0.46 us  [to_core(): return lax.ppermute(value, 'node', [(i, i ^ 1) for i in range(2 * CHIPS)])]
    ppermute x2, waiting for transfers between devices: 3.22 us -> 4.12 us  [to_both(): return lax.ppermute(value, ('node', 'local'), perm)]
    ppermute x6, waiting for transfers between devices: 0.97 us -> 1.59 us  [to_chip(): return lax.ppermute(value, 'node', [(i, i ^ 2) for i in range(2 * CHIPS)])]
    ppermute x10 -> x4, waiting for transfers between devices: 2.92 us -> 3.51 us  [to_core(): return lax.ppermute(value, 'node', [(i, i ^ 1) for i in range(2 * CHIPS)])]
    ppermute x6, waiting for transfers between devices: 10.3 us -> 9.78 us  [to_place(): return lax.ppermute(value, 'local', [(i, i ^ bits) for i in range(PLACES)])]
  transfers between devices with their start and end apart: 24 -> 18, of which waited for: 15 -> 13; matrix products, arithmetic and copies ran while one was open for 1% -> 1% of each run, Pallas kernels for 0% -> 0%
where the time goes in v10:
time: 53.9 us; the launch traced here: 53.8 us
  starting transfers between devices  24.5 us (45%)
  waiting for transfers between devices  19 us (35%)
  Pallas kernels  9.02 us (17%)
  other arithmetic  1.01 us (2%)
    ppermute x6, starting transfers between devices, to_place(): return lax.ppermute(value, 'local', [(i, i ^ bits) for i in range(PLACES)])  12.4 us
    ppermute x6, waiting for transfers between devices, to_place(): return lax.ppermute(value, 'local', [(i, i ^ bits) for i in range(PLACES)])  9.78 us
    ppermute x6, starting transfers between devices, to_chip(): return lax.ppermute(value, 'node', [(i, i ^ 2) for i in range(2 * CHIPS)])  8.88 us
    pallas_call x1, Pallas kernels, hidden_units(): pl.pallas_call(functools.partial(hidden_kernel, experts), out_shape=jax.S...  5.03 us
    ppermute x2, waiting for transfers between devices, to_both(): return lax.ppermute(value, ('node', 'local'), perm)  4.12 us
    ppermute x4, waiting for transfers between devices, to_core(): return lax.ppermute(value, 'node', [(i, i ^ 1) for i in range(2 * CHIPS)])  3.51 us
    ppermute x2, starting transfers between devices, to_both(): return lax.ppermute(value, ('node', 'local'), perm)  2.76 us
    pallas_call x1, Pallas kernels, down(): pl.pallas_call(functools.partial(down_kernel, chunk), out_shape=[jax.Shap...  2.69 us
  transfers between devices with their start and end apart: 18, of which 13 were waited for; matrix products, arithmetic and copies ran while one was open for 1% of the time, Pallas kernels for 0%

profile of v10, /device:TPU:0, one launch (start us, length us, event | category | flops | bytes accessed | tf_op | source)
XLA Modules:
  0.0 53.8 jit_solution(6414022046632994319)
XLA Ops:
  0.0 0.0 copy-start
  0.0 0.0 copy-start.1
  0.0 1.2 %pack.1.refs_0_ = bf16[8,7296]{1,0:T(8,128)(2,1)S(1)} custom-call(bf16[8,7168]{1,0:T(8,128)(2,1)} %refs_0_.1, s32[4,8]{1,0:T(4,128)} %bitcast.6, f32[4,8]{1,0:T(4,128)} %bitcast.7, s32[8]{0:T(128)} %refs_3_.1, bf16[2,7168,512]{2,1,0:T(8,128)(2,1)} %refs_4_.3, bf16[2,7168,512]{2,1,0:T(8,128)(2,1)} %refs_5_.3, bf16[2,512,7168]{2,1,0:T(8,128)(2,1)} %refs_6_.1), custom_call_target="tpu_custom_call" | custom-call | tf_op jit(solution)/shard_map/pack/pallas_call | solution.py:50
  1.2 3.1 %collective-permute-start.1 = (bf16[8,7296]{1,0:T(8,128)(2,1)S(1)}, bf16[8,7296]{1,0:T(8,128)(2,1)S(1)}, u32[]{:S(2)}, u32[]{:S(2)}) collective-permute-start(bf16[8,7296]{1,0:T(8,128)(2,1)S(1)} %pack.1.refs_0_), channel_id=1, source_target_pairs={{0,1},{1,0},{2,3},{3,2},{4,5},{5,4},{6,7},{7,6},{8,9},{9,8},{10,11... | collective-permute-start | bytes 350216 | tf_op jit(solution)/shard_map/ppermute | solution.py:177
  4.3 2.6 %collective-permute-start.3 = (bf16[8,7296]{1,0:T(8,128)(2,1)S(1)}, bf16[8,7296]{1,0:T(8,128)(2,1)S(1)}, u32[]{:S(2)}, u32[]{:S(2)}) collective-permute-start(bf16[8,7296]{1,0:T(8,128)(2,1)S(1)} %pack.1.refs_0_), channel_id=1, source_target_pairs={{0,2},{1,3},{2,0},{3,1},{4,6},{5,7},{6,4},{7,5},{8,10},{9,11},{10,... | collective-permute-start | bytes 350216 | tf_op jit(solution)/shard_map/ppermute | solution.py:177
  6.8 1.5 %collective-permute-start = (bf16[8,7296]{1,0:T(8,128)(2,1)S(1)}, bf16[8,7296]{1,0:T(8,128)(2,1)S(1)}, u32[]{:S(2)}, u32[]{:S(2)}) collective-permute-start(bf16[8,7296]{1,0:T(8,128)(2,1)S(1)} %pack.1.refs_0_), channel_id=1, source_target_pairs={{0,8},{4,12},{8,0},{12,4},{1,9},{5,13},{9,1},{13,5},{2,10},{6,14},... | collective-permute-start | bytes 350216 | tf_op jit(solution)/shard_map/ppermute | solution.py:173
  8.3 0.3 collective-permute-done.1.refs_2_
  8.7 1.8 %collective-permute-start.2 = (bf16[8,7296]{1,0:T(8,128)(2,1)S(1)}, bf16[8,7296]{1,0:T(8,128)(2,1)S(1)}, u32[]{:S(2)}, u32[]{:S(2)}) collective-permute-start(bf16[8,7296]{1,0:T(8,128)(2,1)S(1)} %collective-permute-done.1.refs_2_), channel_id=1, source_target_pairs={{0,8},{4,12},{8,0},{12,4},{1,9},{5,13},{9,1},{13,5},{2,10},{6,14},... | collective-permute-start | bytes 350216 | tf_op jit(solution)/shard_map/ppermute | solution.py:173
  10.5 1.9 %collective-permute-done.3.refs_0_ = bf16[8,7296]{1,0:T(8,128)(2,1)S(1)} collective-permute-done((bf16[8,7296]{1,0:T(8,128)(2,1)S(1)}, bf16[8,7296]{1,0:T(8,128)(2,1)S(1)}, u32[]{:S(2)}, u32[]{:S(2)}) %collective-permute-start.3) | collective-permute-done | bytes 116768 | tf_op jit(solution)/shard_map/ppermute | solution.py:177
  12.4 0.1 collective-permute-done.refs_1_
  12.5 1.7 %collective-permute-start.6 = (bf16[8,7296]{1,0:T(8,128)(2,1)S(1)}, bf16[8,7296]{1,0:T(8,128)(2,1)S(1)}, u32[]{:S(2)}, u32[]{:S(2)}) collective-permute-start(bf16[8,7296]{1,0:T(8,128)(2,1)S(1)} %collective-permute-done.3.refs_0_), channel_id=1, source_target_pairs={{0,9},{1,8},{2,11},{3,10},{4,13},{5,12},{6,15},{7,14},{8,1},{9,0},... | collective-permute-start | bytes 350216 | tf_op jit(solution)/shard_map/ppermute | solution.py:183
  14.2 0.5 collective-permute-start.5
  14.7 0.3 collective-permute-done.2.refs_3_
  15.0 1.0 %collective-permute-start.4 = (bf16[8,7296]{1,0:T(8,128)(2,1)S(1)}, bf16[8,7296]{1,0:T(8,128)(2,1)S(1)}, u32[]{:S(2)}, u32[]{:S(2)}) collective-permute-start(bf16[8,7296]{1,0:T(8,128)(2,1)S(1)} %collective-permute-done.3.refs_0_), channel_id=1, source_target_pairs={{0,1},{1,0},{2,3},{3,2},{4,5},{5,4},{6,7},{7,6},{8,9},{9,8},{10,11... | collective-permute-start | bytes 350216 | tf_op jit(solution)/shard_map/ppermute | solution.py:177
  16.0 0.1 stack.2.refs_0_
  16.0 0.1 collective-permute-start.7
  16.1 2.6 %collective-permute-done.6.refs_3_ = bf16[8,7296]{1,0:T(8,128)(2,1)S(1)} collective-permute-done((bf16[8,7296]{1,0:T(8,128)(2,1)S(1)}, bf16[8,7296]{1,0:T(8,128)(2,1)S(1)}, u32[]{:S(2)}, u32[]{:S(2)}) %collective-permute-start.6) | collective-permute-done | bytes 116768 | tf_op jit(solution)/shard_map/ppermute | solution.py:183
  18.7 1.1 %collective-permute-done.5.refs_2_ = bf16[8,7296]{1,0:T(8,128)(2,1)S(1)} collective-permute-done((bf16[8,7296]{1,0:T(8,128)(2,1)S(1)}, bf16[8,7296]{1,0:T(8,128)(2,1)S(1)}, u32[]{:S(2)}, u32[]{:S(2)}) %collective-permute-start.5) | collective-permute-done | bytes 116768 | tf_op jit(solution)/shard_map/ppermute | solution.py:173
  19.8 0.0 collective-permute-done.4.refs_1_
  19.8 0.0 slice-start
  19.8 0.1 stack.3.refs_1_
  19.9 0.0 slice-start.1
  19.9 0.0 slice-start.2
  19.9 0.0 slice-start.3
  19.9 0.1 collective-permute-start.8
  20.0 0.0 collective-permute-done.7.refs_2_
  20.0 1.8 %collective-permute-done.8.refs_3_ = bf16[32,7296]{1,0:T(8,128)(2,1)S(1)} collective-permute-done((bf16[32,7296]{1,0:T(8,128)(2,1)S(1)}, bf16[32,7296]{1,0:T(8,128)(2,1)S(1)}, u32[]{:S(2)}, u32[]{:S(2)}) %collective-permute-start.8) | collective-permute-done | bytes 466976 | tf_op jit(solution)/shard_map/ppermute | solution.py:169
  21.8 0.0 copy-done
  21.8 0.0 copy-done.1
  21.8 5.0 %hidden.1.hidden_ref = bf16[128,1024]{1,0:T(8,128)(2,1)S(1)} custom-call(bf16[32,7296]{1,0:T(8,128)(2,1)S(1)} %stack.2.refs_0_, bf16[32,7296]{1,0:T(8,128)(2,1)S(1)} %stack.3.refs_1_, bf16[32,7296]{1,0:T(8,128)(2,1)S(1)} %collective-permute-done.7.refs_2_, bf16[32,7296]{1,0:T(8,128)(2,1)S(1)} %collective-permute-done.8.refs_3_, ...), custom_call_target="tpu_custom_call" | custom-call | flops 3758096384 | bytes 29360128 | tf_op jit(solution)/shard_map/hidden/pallas_call | solution.py:113
  26.9 0.0 slice-done
  26.9 0.0 slice-done.1
  26.9 0.0 slice-done.2
  26.9 0.0 slice-done.3
  26.9 2.7 %down.1 = (bf16[32,7168]{1,0:T(8,128)(2,1)S(1)}, bf16[32,7168]{1,0:T(8,128)(2,1)S(1)}, bf16[32,7168]{1,0:T(8,128)(2,1)S(1)}, bf16[32,7168]{1,0:T(8,128)(2,1)S(1)}) custom-call(bf16[128,1024]{1,0:T(8,128)(2,1)S(1)} %hidden.1.hidden_ref, bf16[1024,7168]{1,0:T(8,128)(2,1)S(1)} %bitcast.5), custom_call_target="tpu_custom_call" | custom-call | flops 1879048192 | bytes 14680064 | tf_op jit(solution)/shard_map/down/pallas_call | solution.py:150
  29.6 0.2 collective-permute-start.9
  29.8 1.7 %collective-permute-done.9 = bf16[32,7168]{1,0:T(8,128)(2,1)S(1)} collective-permute-done((bf16[32,7168]{1,0:T(8,128)(2,1)S(1)}, bf16[32,7168]{1,0:T(8,128)(2,1)S(1)}, u32[]{:S(2)}, u32[]{:S(2)}) %collective-permute-start.9) | collective-permute-done | bytes 458784 | tf_op jit(solution)/shard_map/ppermute | solution.py:169
  31.5 0.1 collective-permute-start.10
  31.6 0.1 add_convert_fusion
  31.8 1.7 %collective-permute-start.11 = (bf16[8,7168]{1,0:T(8,128)(2,1)S(1)}, bf16[8,7168]{1,0:T(8,128)(2,1)S(1)}, u32[]{:S(2)}, u32[]{:S(2)}) collective-permute-start(bf16[8,7168]{1,0:T(8,128)(2,1)S(1)} %get-tuple-element.21), channel_id=1, source_target_pairs={{0,8},{4,12},{8,0},{12,4},{1,9},{5,13},{9,1},{13,5},{2,10},{6,14},... | collective-permute-start | bytes 344072 | tf_op jit(solution)/shard_map/ppermute | solution.py:173
  33.5 0.8 %collective-permute-start.13 = (bf16[8,7168]{1,0:T(8,128)(2,1)S(1)}, bf16[8,7168]{1,0:T(8,128)(2,1)S(1)}, u32[]{:S(2)}, u32[]{:S(2)}) collective-permute-start(bf16[8,7168]{1,0:T(8,128)(2,1)S(1)} %get-tuple-element.22), channel_id=1, source_target_pairs={{0,1},{1,0},{2,3},{3,2},{4,5},{5,4},{6,7},{7,6},{8,9},{9,8},{10,11... | collective-permute-start | bytes 344072 | tf_op jit(solution)/shard_map/ppermute | solution.py:177
  34.3 1.1 %collective-permute-start.12 = (bf16[8,7168]{1,0:T(8,128)(2,1)S(1)}, bf16[8,7168]{1,0:T(8,128)(2,1)S(1)}, u32[]{:S(2)}, u32[]{:S(2)}) collective-permute-start(bf16[8,7168]{1,0:T(8,128)(2,1)S(1)} %get-tuple-element.23), channel_id=1, source_target_pairs={{0,9},{1,8},{2,11},{3,10},{4,13},{5,12},{6,15},{7,14},{8,1},{9,0},... | collective-permute-start | bytes 344072 | tf_op jit(solution)/shard_map/ppermute | solution.py:183
  35.4 0.0 collective-permute-done.10
  35.4 0.1 add_convert_fusion.1
  35.5 1.7 %collective-permute-start.16 = (bf16[8,7168]{1,0:T(8,128)(2,1)S(1)}, bf16[8,7168]{1,0:T(8,128)(2,1)S(1)}, u32[]{:S(2)}, u32[]{:S(2)}) collective-permute-start(bf16[8,7168]{1,0:T(8,128)(2,1)S(1)} %get-tuple-element.25), channel_id=1, source_target_pairs={{0,8},{4,12},{8,0},{12,4},{1,9},{5,13},{9,1},{13,5},{2,10},{6,14},... | collective-permute-start | bytes 344072 | tf_op jit(solution)/shard_map/ppermute | solution.py:173
  37.2 0.1 collective-permute-done.11
  37.3 2.2 %collective-permute-done.13 = bf16[8,7168]{1,0:T(8,128)(2,1)S(1)} collective-permute-done((bf16[8,7168]{1,0:T(8,128)(2,1)S(1)}, bf16[8,7168]{1,0:T(8,128)(2,1)S(1)}, u32[]{:S(2)}, u32[]{:S(2)}) %collective-permute-start.13) | collective-permute-done | bytes 114720 | tf_op jit(solution)/shard_map/ppermute | solution.py:177
  39.5 1.5 %collective-permute-done.12 = bf16[8,7168]{1,0:T(8,128)(2,1)S(1)} collective-permute-done((bf16[8,7168]{1,0:T(8,128)(2,1)S(1)}, bf16[8,7168]{1,0:T(8,128)(2,1)S(1)}, u32[]{:S(2)}, u32[]{:S(2)}) %collective-permute-start.12) | collective-permute-done | bytes 114720 | tf_op jit(solution)/shard_map/ppermute | solution.py:183
  41.0 0.1 add_convert_fusion.4
  41.1 4.6 %collective-permute-start.14 = (bf16[8,7168]{1,0:T(8,128)(2,1)S(1)}, bf16[8,7168]{1,0:T(8,128)(2,1)S(1)}, u32[]{:S(2)}, u32[]{:S(2)}) collective-permute-start(bf16[8,7168]{1,0:T(8,128)(2,1)S(1)} %add_convert_fusion.4), channel_id=1, source_target_pairs={{0,2},{1,3},{2,0},{3,1},{4,6},{5,7},{6,4},{7,5},{8,10},{9,11},{10,... | collective-permute-start | bytes 344072 | tf_op jit(solution)/shard_map/ppermute | solution.py:177
  45.7 1.7 %collective-permute-start.15 = (bf16[8,7168]{1,0:T(8,128)(2,1)S(1)}, bf16[8,7168]{1,0:T(8,128)(2,1)S(1)}, u32[]{:S(2)}, u32[]{:S(2)}) collective-permute-start(bf16[8,7168]{1,0:T(8,128)(2,1)S(1)} %get-tuple-element.20), channel_id=1, source_target_pairs={{0,8},{4,12},{8,0},{12,4},{1,9},{5,13},{9,1},{13,5},{2,10},{6,14},... | collective-permute-start | bytes 344072 | tf_op jit(solution)/shard_map/ppermute | solution.py:173
  47.3 0.0 collective-permute-done.16
  47.4 0.3 collective-permute-start.17
  47.7 3.3 %collective-permute-done.14 = bf16[8,7168]{1,0:T(8,128)(2,1)S(1)} collective-permute-done((bf16[8,7168]{1,0:T(8,128)(2,1)S(1)}, bf16[8,7168]{1,0:T(8,128)(2,1)S(1)}, u32[]{:S(2)}, u32[]{:S(2)}) %collective-permute-start.14) | collective-permute-done | bytes 114720 | tf_op jit(solution)/shard_map/ppermute | solution.py:177
  51.0 0.0 collective-permute-done.15
  51.0 2.0 %collective-permute-done.17 = bf16[8,7168]{1,0:T(8,128)(2,1)S(1)} collective-permute-done((bf16[8,7168]{1,0:T(8,128)(2,1)S(1)}, bf16[8,7168]{1,0:T(8,128)(2,1)S(1)}, u32[]{:S(2)}, u32[]{:S(2)}) %collective-permute-start.17) | collective-permute-done | bytes 114720 | tf_op jit(solution)/shard_map/ppermute | solution.py:177
  53.1 0.7 %add_convert_fusion.2 = bf16[8,7168]{1,0:T(8,128)(2,1)} fusion(bf16[8,7168]{1,0:T(8,128)(2,1)S(1)} %collective-permute-done.17, bf16[8,7168]{1,0:T(8,128)(2,1)S(1)} %collective-permute-done.15, bf16[8,7168]{1,0:T(8,128)(2,1)S(1)} %collective-permute-done.14, bf16[32,7168]{1,0:T(8,128)(2,1)S(1)} %add_convert_fusion.1), kind=kLoop, calls=%fused_computation.2 | loop fusion | flops 458752 | bytes 573440 | tf_op jit(solution)/shard_map/convert_element_type | solution.py:216
  (4 shorter events, 0.1 us)
Async XLA Ops:
  0.0 21.8 %copy-start = (bf16[2,7168,512]{2,1,0:T(8,128)(2,1)S(1)}, bf16[2,7168,512]{2,1,0:T(8,128)(2,1)}, u32[]{:S(2)}) copy-start(bf16[2,7168,512]{2,1,0:T(8,128)(2,1)} %refs_4_.3) | copy-start | bytes 44040196
  0.0 21.8 %copy-start.1 = (bf16[2,7168,512]{2,1,0:T(8,128)(2,1)S(1)}, bf16[2,7168,512]{2,1,0:T(8,128)(2,1)}, u32[]{:S(2)}) copy-start(bf16[2,7168,512]{2,1,0:T(8,128)(2,1)} %refs_5_.3) | copy-start | bytes 44040196
  1.2 7.5 %collective-permute-start.1 = (bf16[8,7296]{1,0:T(8,128)(2,1)S(1)}, bf16[8,7296]{1,0:T(8,128)(2,1)S(1)}, u32[]{:S(2)}, u32[]{:S(2)}) collective-permute-start(bf16[8,7296]{1,0:T(8,128)(2,1)S(1)} %pack.1.refs_0_), channel_id=1, source_target_pairs={{0,1},{1,0},{2,3},{3,2},{4,5},{5,4},{6,7},{7,6},{8,9},{9,8},{10,11... | collective-permute-start | bytes 350216 | tf_op jit(solution)/shard_map/ppermute | solution.py:177
  4.3 8.1 %collective-permute-start.3 = (bf16[8,7296]{1,0:T(8,128)(2,1)S(1)}, bf16[8,7296]{1,0:T(8,128)(2,1)S(1)}, u32[]{:S(2)}, u32[]{:S(2)}) collective-permute-start(bf16[8,7296]{1,0:T(8,128)(2,1)S(1)} %pack.1.refs_0_), channel_id=1, source_target_pairs={{0,2},{1,3},{2,0},{3,1},{4,6},{5,7},{6,4},{7,5},{8,10},{9,11},{10,... | collective-permute-start | bytes 350216 | tf_op jit(solution)/shard_map/ppermute | solution.py:177
  6.8 5.6 %collective-permute-start = (bf16[8,7296]{1,0:T(8,128)(2,1)S(1)}, bf16[8,7296]{1,0:T(8,128)(2,1)S(1)}, u32[]{:S(2)}, u32[]{:S(2)}) collective-permute-start(bf16[8,7296]{1,0:T(8,128)(2,1)S(1)} %pack.1.refs_0_), channel_id=1, source_target_pairs={{0,8},{4,12},{8,0},{12,4},{1,9},{5,13},{9,1},{13,5},{2,10},{6,14},... | collective-permute-start | bytes 350216 | tf_op jit(solution)/shard_map/ppermute | solution.py:173
  8.7 6.3 %collective-permute-start.2 = (bf16[8,7296]{1,0:T(8,128)(2,1)S(1)}, bf16[8,7296]{1,0:T(8,128)(2,1)S(1)}, u32[]{:S(2)}, u32[]{:S(2)}) collective-permute-start(bf16[8,7296]{1,0:T(8,128)(2,1)S(1)} %collective-permute-done.1.refs_2_), channel_id=1, source_target_pairs={{0,8},{4,12},{8,0},{12,4},{1,9},{5,13},{9,1},{13,5},{2,10},{6,14},... | collective-permute-start | bytes 350216 | tf_op jit(solution)/shard_map/ppermute | solution.py:173
  12.5 6.2 %collective-permute-start.6 = (bf16[8,7296]{1,0:T(8,128)(2,1)S(1)}, bf16[8,7296]{1,0:T(8,128)(2,1)S(1)}, u32[]{:S(2)}, u32[]{:S(2)}) collective-permute-start(bf16[8,7296]{1,0:T(8,128)(2,1)S(1)} %collective-permute-done.3.refs_0_), channel_id=1, source_target_pairs={{0,9},{1,8},{2,11},{3,10},{4,13},{5,12},{6,15},{7,14},{8,1},{9,0},... | collective-permute-start | bytes 350216 | tf_op jit(solution)/shard_map/ppermute | solution.py:183
  14.2 5.6 %collective-permute-start.5 = (bf16[8,7296]{1,0:T(8,128)(2,1)S(1)}, bf16[8,7296]{1,0:T(8,128)(2,1)S(1)}, u32[]{:S(2)}, u32[]{:S(2)}) collective-permute-start(bf16[8,7296]{1,0:T(8,128)(2,1)S(1)} %collective-permute-done.3.refs_0_), channel_id=1, source_target_pairs={{0,8},{4,12},{8,0},{12,4},{1,9},{5,13},{9,1},{13,5},{2,10},{6,14},... | collective-permute-start | bytes 350216 | tf_op jit(solution)/shard_map/ppermute | solution.py:173
  15.0 4.9 %collective-permute-start.4 = (bf16[8,7296]{1,0:T(8,128)(2,1)S(1)}, bf16[8,7296]{1,0:T(8,128)(2,1)S(1)}, u32[]{:S(2)}, u32[]{:S(2)}) collective-permute-start(bf16[8,7296]{1,0:T(8,128)(2,1)S(1)} %collective-permute-done.3.refs_0_), channel_id=1, source_target_pairs={{0,1},{1,0},{2,3},{3,2},{4,5},{5,4},{6,7},{7,6},{8,9},{9,8},{10,11... | collective-permute-start | bytes 350216 | tf_op jit(solution)/shard_map/ppermute | solution.py:177
  16.0 4.0 %collective-permute-start.7 = (bf16[32,7296]{1,0:T(8,128)(2,1)S(1)}, bf16[32,7296]{1,0:T(8,128)(2,1)S(1)}, u32[]{:S(2)}, u32[]{:S(2)}) collective-permute-start(bf16[32,7296]{1,0:T(8,128)(2,1)S(1)} %stack.2.refs_0_), channel_id=1, source_target_pairs={{0,4},{4,0},{8,12},{12,8},{1,5},{5,1},{9,13},{13,9},{2,6},{6,2},{1... | collective-permute-start | bytes 1400840 | tf_op jit(solution)/shard_map/ppermute | solution.py:169
  19.8 7.1 %slice-start = ((s8[14680064]{0:T(1024)(128)(4,1)}), s8[4194304]{0:T(1024)(128)(4,1)S(1)}, s32[]{:S(2)}) async-start(s8[14680064]{0:T(1024)(128)(4,1)} %bitcast.3), calls=%async_computation | async-start | bytes 8388608
  19.9 7.0 %slice-start.1 = ((s8[14680064]{0:T(1024)(128)(4,1)}), s8[4194304]{0:T(1024)(128)(4,1)S(1)}, s32[]{:S(2)}) async-start(s8[14680064]{0:T(1024)(128)(4,1)} %bitcast.3), calls=%async_computation.1 | async-start | bytes 8388608
  19.9 7.0 %slice-start.2 = ((s8[14680064]{0:T(1024)(128)(4,1)}), s8[4194304]{0:T(1024)(128)(4,1)S(1)}, s32[]{:S(2)}) async-start(s8[14680064]{0:T(1024)(128)(4,1)} %bitcast.3), calls=%async_computation.2 | async-start | bytes 8388608
  19.9 7.0 %slice-start.3 = ((s8[14680064]{0:T(1024)(128)(4,1)}), s8[2097152]{0:T(1024)(128)(4,1)S(1)}, s32[]{:S(2)}) async-start(s8[14680064]{0:T(1024)(128)(4,1)} %bitcast.3), calls=%async_computation.3 | async-start | bytes 4194304
  19.9 1.9 %collective-permute-start.8 = (bf16[32,7296]{1,0:T(8,128)(2,1)S(1)}, bf16[32,7296]{1,0:T(8,128)(2,1)S(1)}, u32[]{:S(2)}, u32[]{:S(2)}) collective-permute-start(bf16[32,7296]{1,0:T(8,128)(2,1)S(1)} %stack.3.refs_1_), channel_id=1, source_target_pairs={{0,4},{4,0},{8,12},{12,8},{1,5},{5,1},{9,13},{13,9},{2,6},{6,2},{1... | collective-permute-start | bytes 1400840 | tf_op jit(solution)/shard_map/ppermute | solution.py:169
  29.6 1.9 %collective-permute-start.9 = (bf16[32,7168]{1,0:T(8,128)(2,1)S(1)}, bf16[32,7168]{1,0:T(8,128)(2,1)S(1)}, u32[]{:S(2)}, u32[]{:S(2)}) collective-permute-start(bf16[32,7168]{1,0:T(8,128)(2,1)S(1)} %get-tuple-element.17), channel_id=1, source_target_pairs={{0,4},{4,0},{8,12},{12,8},{1,5},{5,1},{9,13},{13,9},{2,6},{6,2},{1... | collective-permute-start | bytes 1376264 | tf_op jit(solution)/shard_map/ppermute | solution.py:169
  31.5 3.9 %collective-permute-start.10 = (bf16[32,7168]{1,0:T(8,128)(2,1)S(1)}, bf16[32,7168]{1,0:T(8,128)(2,1)S(1)}, u32[]{:S(2)}, u32[]{:S(2)}) collective-permute-start(bf16[32,7168]{1,0:T(8,128)(2,1)S(1)} %get-tuple-element.18), channel_id=1, source_target_pairs={{0,4},{4,0},{8,12},{12,8},{1,5},{5,1},{9,13},{13,9},{2,6},{6,2},{1... | collective-permute-start | bytes 1376264 | tf_op jit(solution)/shard_map/ppermute | solution.py:169
  31.8 5.5 %collective-permute-start.11 = (bf16[8,7168]{1,0:T(8,128)(2,1)S(1)}, bf16[8,7168]{1,0:T(8,128)(2,1)S(1)}, u32[]{:S(2)}, u32[]{:S(2)}) collective-permute-start(bf16[8,7168]{1,0:T(8,128)(2,1)S(1)} %get-tuple-element.21), channel_id=1, source_target_pairs={{0,8},{4,12},{8,0},{12,4},{1,9},{5,13},{9,1},{13,5},{2,10},{6,14},... | collective-permute-start | bytes 344072 | tf_op jit(solution)/shard_map/ppermute | solution.py:173
  33.5 6.0 %collective-permute-start.13 = (bf16[8,7168]{1,0:T(8,128)(2,1)S(1)}, bf16[8,7168]{1,0:T(8,128)(2,1)S(1)}, u32[]{:S(2)}, u32[]{:S(2)}) collective-permute-start(bf16[8,7168]{1,0:T(8,128)(2,1)S(1)} %get-tuple-element.22), channel_id=1, source_target_pairs={{0,1},{1,0},{2,3},{3,2},{4,5},{5,4},{6,7},{7,6},{8,9},{9,8},{10,11... | collective-permute-start | bytes 344072 | tf_op jit(solution)/shard_map/ppermute | solution.py:177
  34.3 6.7 %collective-permute-start.12 = (bf16[8,7168]{1,0:T(8,128)(2,1)S(1)}, bf16[8,7168]{1,0:T(8,128)(2,1)S(1)}, u32[]{:S(2)}, u32[]{:S(2)}) collective-permute-start(bf16[8,7168]{1,0:T(8,128)(2,1)S(1)} %get-tuple-element.23), channel_id=1, source_target_pairs={{0,9},{1,8},{2,11},{3,10},{4,13},{5,12},{6,15},{7,14},{8,1},{9,0},... | collective-permute-start | bytes 344072 | tf_op jit(solution)/shard_map/ppermute | solution.py:183
  35.5 11.9 %collective-permute-start.16 = (bf16[8,7168]{1,0:T(8,128)(2,1)S(1)}, bf16[8,7168]{1,0:T(8,128)(2,1)S(1)}, u32[]{:S(2)}, u32[]{:S(2)}) collective-permute-start(bf16[8,7168]{1,0:T(8,128)(2,1)S(1)} %get-tuple-element.25), channel_id=1, source_target_pairs={{0,8},{4,12},{8,0},{12,4},{1,9},{5,13},{9,1},{13,5},{2,10},{6,14},... | collective-permute-start | bytes 344072 | tf_op jit(solution)/shard_map/ppermute | solution.py:173
  41.1 10.0 %collective-permute-start.14 = (bf16[8,7168]{1,0:T(8,128)(2,1)S(1)}, bf16[8,7168]{1,0:T(8,128)(2,1)S(1)}, u32[]{:S(2)}, u32[]{:S(2)}) collective-permute-start(bf16[8,7168]{1,0:T(8,128)(2,1)S(1)} %add_convert_fusion.4), channel_id=1, source_target_pairs={{0,2},{1,3},{2,0},{3,1},{4,6},{5,7},{6,4},{7,5},{8,10},{9,11},{10,... | collective-permute-start | bytes 344072 | tf_op jit(solution)/shard_map/ppermute | solution.py:177
  45.7 5.4 %collective-permute-start.15 = (bf16[8,7168]{1,0:T(8,128)(2,1)S(1)}, bf16[8,7168]{1,0:T(8,128)(2,1)S(1)}, u32[]{:S(2)}, u32[]{:S(2)}) collective-permute-start(bf16[8,7168]{1,0:T(8,128)(2,1)S(1)} %get-tuple-element.20), channel_id=1, source_target_pairs={{0,8},{4,12},{8,0},{12,4},{1,9},{5,13},{9,1},{13,5},{2,10},{6,14},... | collective-permute-start | bytes 344072 | tf_op jit(solution)/shard_map/ppermute | solution.py:173
  47.4 5.7 %collective-permute-start.17 = (bf16[8,7168]{1,0:T(8,128)(2,1)S(1)}, bf16[8,7168]{1,0:T(8,128)(2,1)S(1)}, u32[]{:S(2)}, u32[]{:S(2)}) collective-permute-start(bf16[8,7168]{1,0:T(8,128)(2,1)S(1)} %add_convert_fusion.3), channel_id=1, source_target_pairs={{0,1},{1,0},{2,3},{3,2},{4,5},{5,4},{6,7},{7,6},{8,9},{9,8},{10,11... | collective-permute-start | bytes 344072 | tf_op jit(solution)/shard_map/ppermute | solution.py:177

commit v11 on v10

--- a/solution.py
+++ b/solution.py
@@ -191,9 +191,10 @@
     second, first, far_own = to_place(own, 2), to_place(own, 1), to_chip(own)
     far_first = to_chip(first)
     ready = after(second, far_own)
-    far_second, far_third = to_chip(ready), to_both(ready, 1)
-    third = to_place(after(ready, far_first), 1)
-    early, late = stack(own, far_own, first, far_first), stack(second, third, far_second, far_third)
+    far_second, third = to_chip(ready), to_place(ready, 1)
+    far_third = to_both(after(ready, far_first), 1)
+    early = stack(own, far_own, first, far_first)
+    late = stack(second, third, far_second, far_third)
     return [early, late, to_core(early), to_core(late)]
 
 

time: 53.9 us -> 51.4 us (0.954)
  waiting for transfers between devices: 19 us -> 17.6 us
  starting transfers between devices: 24.5 us -> 23.4 us
    ppermute x6, starting transfers between devices: 12.4 us -> 10.6 us  [to_place(): return lax.ppermute(value, 'local', [(i, i ^ bits) for i in range(PLACES)])]
    ppermute x6, waiting for transfers between devices: 9.78 us -> 8.28 us  [to_place(): return lax.ppermute(value, 'local', [(i, i ^ bits) for i in range(PLACES)])]
    ppermute x6, waiting for transfers between devices: 1.59 us -> 2.58 us  [to_chip(): return lax.ppermute(value, 'node', [(i, i ^ 2) for i in range(2 * CHIPS)])]
    ppermute x2, waiting for transfers between devices: 4.12 us -> 3.17 us  [to_both(): return lax.ppermute(value, ('node', 'local'), perm)]
    ppermute x6, starting transfers between devices: 8.88 us -> 9.48 us  [to_chip(): return lax.ppermute(value, 'node', [(i, i ^ 2) for i in range(2 * CHIPS)])]
  transfers between devices with their start and end apart: 18 -> 18, of which waited for: 13 -> 12; matrix products, arithmetic and copies ran while one was open for 1% -> 1% of each run, Pallas kernels for 0% -> 0%
where the time goes in v11:
time: 51.4 us; the launch traced here: 51.3 us
  starting transfers between devices  23.4 us (46%)
  waiting for transfers between devices  17.6 us (34%)
  Pallas kernels  9.03 us (18%)
  other arithmetic  1.01 us (2%)
    ppermute x6, starting transfers between devices, to_place(): return lax.ppermute(value, 'local', [(i, i ^ bits) for i in range(PLACES)])  10.6 us
    ppermute x6, starting transfers between devices, to_chip(): return lax.ppermute(value, 'node', [(i, i ^ 2) for i in range(2 * CHIPS)])  9.48 us
    ppermute x6, waiting for transfers between devices, to_place(): return lax.ppermute(value, 'local', [(i, i ^ bits) for i in range(PLACES)])  8.28 us
    pallas_call x1, Pallas kernels, hidden_units(): pl.pallas_call(functools.partial(hidden_kernel, experts), out_shape=jax.S...  5.04 us
    ppermute x4, waiting for transfers between devices, to_core(): return lax.ppermute(value, 'node', [(i, i ^ 1) for i in range(2 * CHIPS)])  3.52 us
    ppermute x2, waiting for transfers between devices, to_both(): return lax.ppermute(value, ('node', 'local'), perm)  3.17 us
    ppermute x2, starting transfers between devices, to_both(): return lax.ppermute(value, ('node', 'local'), perm)  2.91 us
    pallas_call x1, Pallas kernels, down(): pl.pallas_call(functools.partial(down_kernel, chunk), out_shape=[jax.Shap...  2.69 us
  transfers between devices with their start and end apart: 18, of which 12 were waited for; matrix products, arithmetic and copies ran while one was open for 1% of the time, Pallas kernels for 0%

profile of v11, /device:TPU:0, one launch (start us, length us, event | category | flops | bytes accessed | tf_op | source)
XLA Modules:
  0.0 51.3 jit_solution(17764867745351445652)
XLA Ops:
  0.0 0.0 copy-start
  0.0 0.0 copy-start.1
  0.0 1.2 %pack.1.refs_0_ = bf16[8,7296]{1,0:T(8,128)(2,1)S(1)} custom-call(bf16[8,7168]{1,0:T(8,128)(2,1)} %refs_0_.1, s32[4,8]{1,0:T(4,128)} %bitcast.6, f32[4,8]{1,0:T(4,128)} %bitcast.7, s32[8]{0:T(128)} %refs_3_.1, bf16[2,7168,512]{2,1,0:T(8,128)(2,1)} %refs_4_.3, bf16[2,7168,512]{2,1,0:T(8,128)(2,1)} %refs_5_.3, bf16[2,512,7168]{2,1,0:T(8,128)(2,1)} %refs_6_.1), custom_call_target="tpu_custom_call" | custom-call | tf_op jit(solution)/shard_map/pack/pallas_call | solution.py:50
  1.2 3.1 %collective-permute-start.1 = (bf16[8,7296]{1,0:T(8,128)(2,1)S(1)}, bf16[8,7296]{1,0:T(8,128)(2,1)S(1)}, u32[]{:S(2)}, u32[]{:S(2)}) collective-permute-start(bf16[8,7296]{1,0:T(8,128)(2,1)S(1)} %pack.1.refs_0_), channel_id=1, source_target_pairs={{0,1},{1,0},{2,3},{3,2},{4,5},{5,4},{6,7},{7,6},{8,9},{9,8},{10,11... | collective-permute-start | bytes 350216 | tf_op jit(solution)/shard_map/ppermute | solution.py:177
  4.3 2.6 %collective-permute-start.3 = (bf16[8,7296]{1,0:T(8,128)(2,1)S(1)}, bf16[8,7296]{1,0:T(8,128)(2,1)S(1)}, u32[]{:S(2)}, u32[]{:S(2)}) collective-permute-start(bf16[8,7296]{1,0:T(8,128)(2,1)S(1)} %pack.1.refs_0_), channel_id=1, source_target_pairs={{0,2},{1,3},{2,0},{3,1},{4,6},{5,7},{6,4},{7,5},{8,10},{9,11},{10,... | collective-permute-start | bytes 350216 | tf_op jit(solution)/shard_map/ppermute | solution.py:177
  6.8 1.5 %collective-permute-start = (bf16[8,7296]{1,0:T(8,128)(2,1)S(1)}, bf16[8,7296]{1,0:T(8,128)(2,1)S(1)}, u32[]{:S(2)}, u32[]{:S(2)}) collective-permute-start(bf16[8,7296]{1,0:T(8,128)(2,1)S(1)} %pack.1.refs_0_), channel_id=1, source_target_pairs={{0,8},{4,12},{8,0},{12,4},{1,9},{5,13},{9,1},{13,5},{2,10},{6,14},... | collective-permute-start | bytes 350216 | tf_op jit(solution)/shard_map/ppermute | solution.py:173
  8.3 0.3 collective-permute-done.1.refs_2_
  8.7 1.8 %collective-permute-start.2 = (bf16[8,7296]{1,0:T(8,128)(2,1)S(1)}, bf16[8,7296]{1,0:T(8,128)(2,1)S(1)}, u32[]{:S(2)}, u32[]{:S(2)}) collective-permute-start(bf16[8,7296]{1,0:T(8,128)(2,1)S(1)} %collective-permute-done.1.refs_2_), channel_id=1, source_target_pairs={{0,8},{4,12},{8,0},{12,4},{1,9},{5,13},{9,1},{13,5},{2,10},{6,14},... | collective-permute-start | bytes 350216 | tf_op jit(solution)/shard_map/ppermute | solution.py:173
  10.5 1.9 %collective-permute-done.3.refs_0_ = bf16[8,7296]{1,0:T(8,128)(2,1)S(1)} collective-permute-done((bf16[8,7296]{1,0:T(8,128)(2,1)S(1)}, bf16[8,7296]{1,0:T(8,128)(2,1)S(1)}, u32[]{:S(2)}, u32[]{:S(2)}) %collective-permute-start.3) | collective-permute-done | bytes 116768 | tf_op jit(solution)/shard_map/ppermute | solution.py:177
  12.4 0.1 collective-permute-done.refs_1_
  12.5 1.5 %collective-permute-start.5 = (bf16[8,7296]{1,0:T(8,128)(2,1)S(1)}, bf16[8,7296]{1,0:T(8,128)(2,1)S(1)}, u32[]{:S(2)}, u32[]{:S(2)}) collective-permute-start(bf16[8,7296]{1,0:T(8,128)(2,1)S(1)} %collective-permute-done.3.refs_0_), channel_id=1, source_target_pairs={{0,8},{4,12},{8,0},{12,4},{1,9},{5,13},{9,1},{13,5},{2,10},{6,14},... | collective-permute-start | bytes 350216 | tf_op jit(solution)/shard_map/ppermute | solution.py:173
  14.0 0.8 %collective-permute-start.4 = (bf16[8,7296]{1,0:T(8,128)(2,1)S(1)}, bf16[8,7296]{1,0:T(8,128)(2,1)S(1)}, u32[]{:S(2)}, u32[]{:S(2)}) collective-permute-start(bf16[8,7296]{1,0:T(8,128)(2,1)S(1)} %collective-permute-done.3.refs_0_), channel_id=1, source_target_pairs={{0,1},{1,0},{2,3},{3,2},{4,5},{5,4},{6,7},{7,6},{8,9},{9,8},{10,11... | collective-permute-start | bytes 350216 | tf_op jit(solution)/shard_map/ppermute | solution.py:177
  14.7 0.0 collective-permute-done.2.refs_3_
  14.7 1.2 %collective-permute-start.6 = (bf16[8,7296]{1,0:T(8,128)(2,1)S(1)}, bf16[8,7296]{1,0:T(8,128)(2,1)S(1)}, u32[]{:S(2)}, u32[]{:S(2)}) collective-permute-start(bf16[8,7296]{1,0:T(8,128)(2,1)S(1)} %collective-permute-done.3.refs_0_), channel_id=1, source_target_pairs={{0,9},{1,8},{2,11},{3,10},{4,13},{5,12},{6,15},{7,14},{8,1},{9,0},... | collective-permute-start | bytes 350216 | tf_op jit(solution)/shard_map/ppermute | solution.py:183
  16.0 0.1 stack.2.refs_0_
  16.0 0.1 collective-permute-start.7
  16.1 2.4 %collective-permute-done.5.refs_2_ = bf16[8,7296]{1,0:T(8,128)(2,1)S(1)} collective-permute-done((bf16[8,7296]{1,0:T(8,128)(2,1)S(1)}, bf16[8,7296]{1,0:T(8,128)(2,1)S(1)}, u32[]{:S(2)}, u32[]{:S(2)}) %collective-permute-start.5) | collective-permute-done | bytes 116768 | tf_op jit(solution)/shard_map/ppermute | solution.py:173
  18.5 0.2 collective-permute-done.4.refs_1_
  18.8 1.7 %collective-permute-done.6.refs_3_ = bf16[8,7296]{1,0:T(8,128)(2,1)S(1)} collective-permute-done((bf16[8,7296]{1,0:T(8,128)(2,1)S(1)}, bf16[8,7296]{1,0:T(8,128)(2,1)S(1)}, u32[]{:S(2)}, u32[]{:S(2)}) %collective-permute-start.6) | collective-permute-done | bytes 116768 | tf_op jit(solution)/shard_map/ppermute | solution.py:183
  20.5 0.0 slice-start
  20.5 0.1 stack.3.refs_1_
  20.5 0.0 slice-start.1
  20.5 0.0 slice-start.2
  20.6 0.0 slice-start.3
  20.6 0.1 collective-permute-start.8
  20.6 0.0 collective-permute-done.7.refs_2_
  20.7 1.8 %collective-permute-done.8.refs_3_ = bf16[32,7296]{1,0:T(8,128)(2,1)S(1)} collective-permute-done((bf16[32,7296]{1,0:T(8,128)(2,1)S(1)}, bf16[32,7296]{1,0:T(8,128)(2,1)S(1)}, u32[]{:S(2)}, u32[]{:S(2)}) %collective-permute-start.8) | collective-permute-done | bytes 466976 | tf_op jit(solution)/shard_map/ppermute | solution.py:169
  22.5 0.0 copy-done
  22.5 0.0 copy-done.1
  22.5 5.0 %hidden.1.hidden_ref = bf16[128,1024]{1,0:T(8,128)(2,1)S(1)} custom-call(bf16[32,7296]{1,0:T(8,128)(2,1)S(1)} %stack.2.refs_0_, bf16[32,7296]{1,0:T(8,128)(2,1)S(1)} %stack.3.refs_1_, bf16[32,7296]{1,0:T(8,128)(2,1)S(1)} %collective-permute-done.7.refs_2_, bf16[32,7296]{1,0:T(8,128)(2,1)S(1)} %collective-permute-done.8.refs_3_, ...), custom_call_target="tpu_custom_call" | custom-call | flops 3758096384 | bytes 29360128 | tf_op jit(solution)/shard_map/hidden/pallas_call | solution.py:113
  27.5 0.0 slice-done
  27.5 0.0 slice-done.1
  27.5 0.0 slice-done.2
  27.5 0.0 slice-done.3
  27.6 2.7 %down.1 = (bf16[32,7168]{1,0:T(8,128)(2,1)S(1)}, bf16[32,7168]{1,0:T(8,128)(2,1)S(1)}, bf16[32,7168]{1,0:T(8,128)(2,1)S(1)}, bf16[32,7168]{1,0:T(8,128)(2,1)S(1)}) custom-call(bf16[128,1024]{1,0:T(8,128)(2,1)S(1)} %hidden.1.hidden_ref, bf16[1024,7168]{1,0:T(8,128)(2,1)S(1)} %bitcast.5), custom_call_target="tpu_custom_call" | custom-call | flops 1879048192 | bytes 14680064 | tf_op jit(solution)/shard_map/down/pallas_call | solution.py:150
  30.3 0.2 collective-permute-start.9
  30.4 1.7 %collective-permute-done.9 = bf16[32,7168]{1,0:T(8,128)(2,1)S(1)} collective-permute-done((bf16[32,7168]{1,0:T(8,128)(2,1)S(1)}, bf16[32,7168]{1,0:T(8,128)(2,1)S(1)}, u32[]{:S(2)}, u32[]{:S(2)}) %collective-permute-start.9) | collective-permute-done | bytes 458784 | tf_op jit(solution)/shard_map/ppermute | solution.py:169
  32.1 0.1 collective-permute-start.10
  32.3 0.1 add_convert_fusion
  32.4 1.7 %collective-permute-start.11 = (bf16[8,7168]{1,0:T(8,128)(2,1)S(1)}, bf16[8,7168]{1,0:T(8,128)(2,1)S(1)}, u32[]{:S(2)}, u32[]{:S(2)}) collective-permute-start(bf16[8,7168]{1,0:T(8,128)(2,1)S(1)} %get-tuple-element.21), channel_id=1, source_target_pairs={{0,8},{4,12},{8,0},{12,4},{1,9},{5,13},{9,1},{13,5},{2,10},{6,14},... | collective-permute-start | bytes 344072 | tf_op jit(solution)/shard_map/ppermute | solution.py:173
  34.2 0.1 collective-permute-start.13
  34.3 1.7 %collective-permute-start.12 = (bf16[8,7168]{1,0:T(8,128)(2,1)S(1)}, bf16[8,7168]{1,0:T(8,128)(2,1)S(1)}, u32[]{:S(2)}, u32[]{:S(2)}) collective-permute-start(bf16[8,7168]{1,0:T(8,128)(2,1)S(1)} %get-tuple-element.23), channel_id=1, source_target_pairs={{0,9},{1,8},{2,11},{3,10},{4,13},{5,12},{6,15},{7,14},{8,1},{9,0},... | collective-permute-start | bytes 344072 | tf_op jit(solution)/shard_map/ppermute | solution.py:183
  36.0 0.0 collective-permute-done.10
  36.0 0.1 add_convert_fusion.1
  36.1 1.7 %collective-permute-start.16 = (bf16[8,7168]{1,0:T(8,128)(2,1)S(1)}, bf16[8,7168]{1,0:T(8,128)(2,1)S(1)}, u32[]{:S(2)}, u32[]{:S(2)}) collective-permute-start(bf16[8,7168]{1,0:T(8,128)(2,1)S(1)} %get-tuple-element.25), channel_id=1, source_target_pairs={{0,8},{4,12},{8,0},{12,4},{1,9},{5,13},{9,1},{13,5},{2,10},{6,14},... | collective-permute-start | bytes 344072 | tf_op jit(solution)/shard_map/ppermute | solution.py:173
  37.9 0.0 collective-permute-done.11
  37.9 2.3 %collective-permute-done.13 = bf16[8,7168]{1,0:T(8,128)(2,1)S(1)} collective-permute-done((bf16[8,7168]{1,0:T(8,128)(2,1)S(1)}, bf16[8,7168]{1,0:T(8,128)(2,1)S(1)}, u32[]{:S(2)}, u32[]{:S(2)}) %collective-permute-start.13) | collective-permute-done | bytes 114720 | tf_op jit(solution)/shard_map/ppermute | solution.py:177
  40.2 1.5 %collective-permute-done.12 = bf16[8,7168]{1,0:T(8,128)(2,1)S(1)} collective-permute-done((bf16[8,7168]{1,0:T(8,128)(2,1)S(1)}, bf16[8,7168]{1,0:T(8,128)(2,1)S(1)}, u32[]{:S(2)}, u32[]{:S(2)}) %collective-permute-start.12) | collective-permute-done | bytes 114720 | tf_op jit(solution)/shard_map/ppermute | solution.py:183
  41.7 0.1 add_convert_fusion.4
  41.7 2.2 %collective-permute-start.14 = (bf16[8,7168]{1,0:T(8,128)(2,1)S(1)}, bf16[8,7168]{1,0:T(8,128)(2,1)S(1)}, u32[]{:S(2)}, u32[]{:S(2)}) collective-permute-start(bf16[8,7168]{1,0:T(8,128)(2,1)S(1)} %add_convert_fusion.4), channel_id=1, source_target_pairs={{0,2},{1,3},{2,0},{3,1},{4,6},{5,7},{6,4},{7,5},{8,10},{9,11},{10,... | collective-permute-start | bytes 344072 | tf_op jit(solution)/shard_map/ppermute | solution.py:177
  43.9 1.2 %collective-permute-start.15 = (bf16[8,7168]{1,0:T(8,128)(2,1)S(1)}, bf16[8,7168]{1,0:T(8,128)(2,1)S(1)}, u32[]{:S(2)}, u32[]{:S(2)}) collective-permute-start(bf16[8,7168]{1,0:T(8,128)(2,1)S(1)} %get-tuple-element.20), channel_id=1, source_target_pairs={{0,8},{4,12},{8,0},{12,4},{1,9},{5,13},{9,1},{13,5},{2,10},{6,14},... | collective-permute-start | bytes 344072 | tf_op jit(solution)/shard_map/ppermute | solution.py:173
  45.1 0.0 collective-permute-done.16
  45.2 1.8 %collective-permute-start.17 = (bf16[8,7168]{1,0:T(8,128)(2,1)S(1)}, bf16[8,7168]{1,0:T(8,128)(2,1)S(1)}, u32[]{:S(2)}, u32[]{:S(2)}) collective-permute-start(bf16[8,7168]{1,0:T(8,128)(2,1)S(1)} %add_convert_fusion.3), channel_id=1, source_target_pairs={{0,1},{1,0},{2,3},{3,2},{4,5},{5,4},{6,7},{7,6},{8,9},{9,8},{10,11... | collective-permute-start | bytes 344072 | tf_op jit(solution)/shard_map/ppermute | solution.py:177
  47.0 2.4 %collective-permute-done.14 = bf16[8,7168]{1,0:T(8,128)(2,1)S(1)} collective-permute-done((bf16[8,7168]{1,0:T(8,128)(2,1)S(1)}, bf16[8,7168]{1,0:T(8,128)(2,1)S(1)}, u32[]{:S(2)}, u32[]{:S(2)}) %collective-permute-start.14) | collective-permute-done | bytes 114720 | tf_op jit(solution)/shard_map/ppermute | solution.py:177
  49.3 0.0 collective-permute-done.15
  49.3 1.2 %collective-permute-done.17 = bf16[8,7168]{1,0:T(8,128)(2,1)S(1)} collective-permute-done((bf16[8,7168]{1,0:T(8,128)(2,1)S(1)}, bf16[8,7168]{1,0:T(8,128)(2,1)S(1)}, u32[]{:S(2)}, u32[]{:S(2)}) %collective-permute-start.17) | collective-permute-done | bytes 114720 | tf_op jit(solution)/shard_map/ppermute | solution.py:177
  50.6 0.7 %add_convert_fusion.2 = bf16[8,7168]{1,0:T(8,128)(2,1)} fusion(bf16[8,7168]{1,0:T(8,128)(2,1)S(1)} %collective-permute-done.17, bf16[8,7168]{1,0:T(8,128)(2,1)S(1)} %collective-permute-done.15, bf16[8,7168]{1,0:T(8,128)(2,1)S(1)} %collective-permute-done.14, bf16[32,7168]{1,0:T(8,128)(2,1)S(1)} %add_convert_fusion.1), kind=kLoop, calls=%fused_computation.2 | loop fusion | flops 458752 | bytes 573440 | tf_op jit(solution)/shard_map/convert_element_type | solution.py:217
  (4 shorter events, 0.1 us)
Async XLA Ops:
  0.0 22.5 %copy-start = (bf16[2,7168,512]{2,1,0:T(8,128)(2,1)S(1)}, bf16[2,7168,512]{2,1,0:T(8,128)(2,1)}, u32[]{:S(2)}) copy-start(bf16[2,7168,512]{2,1,0:T(8,128)(2,1)} %refs_4_.3) | copy-start | bytes 44040196
  0.0 22.5 %copy-start.1 = (bf16[2,7168,512]{2,1,0:T(8,128)(2,1)S(1)}, bf16[2,7168,512]{2,1,0:T(8,128)(2,1)}, u32[]{:S(2)}) copy-start(bf16[2,7168,512]{2,1,0:T(8,128)(2,1)} %refs_5_.3) | copy-start | bytes 44040196
  1.2 7.5 %collective-permute-start.1 = (bf16[8,7296]{1,0:T(8,128)(2,1)S(1)}, bf16[8,7296]{1,0:T(8,128)(2,1)S(1)}, u32[]{:S(2)}, u32[]{:S(2)}) collective-permute-start(bf16[8,7296]{1,0:T(8,128)(2,1)S(1)} %pack.1.refs_0_), channel_id=1, source_target_pairs={{0,1},{1,0},{2,3},{3,2},{4,5},{5,4},{6,7},{7,6},{8,9},{9,8},{10,11... | collective-permute-start | bytes 350216 | tf_op jit(solution)/shard_map/ppermute | solution.py:177
  4.3 8.1 %collective-permute-start.3 = (bf16[8,7296]{1,0:T(8,128)(2,1)S(1)}, bf16[8,7296]{1,0:T(8,128)(2,1)S(1)}, u32[]{:S(2)}, u32[]{:S(2)}) collective-permute-start(bf16[8,7296]{1,0:T(8,128)(2,1)S(1)} %pack.1.refs_0_), channel_id=1, source_target_pairs={{0,2},{1,3},{2,0},{3,1},{4,6},{5,7},{6,4},{7,5},{8,10},{9,11},{10,... | collective-permute-start | bytes 350216 | tf_op jit(solution)/shard_map/ppermute | solution.py:177
  6.8 5.6 %collective-permute-start = (bf16[8,7296]{1,0:T(8,128)(2,1)S(1)}, bf16[8,7296]{1,0:T(8,128)(2,1)S(1)}, u32[]{:S(2)}, u32[]{:S(2)}) collective-permute-start(bf16[8,7296]{1,0:T(8,128)(2,1)S(1)} %pack.1.refs_0_), channel_id=1, source_target_pairs={{0,8},{4,12},{8,0},{12,4},{1,9},{5,13},{9,1},{13,5},{2,10},{6,14},... | collective-permute-start | bytes 350216 | tf_op jit(solution)/shard_map/ppermute | solution.py:173
  8.7 6.1 %collective-permute-start.2 = (bf16[8,7296]{1,0:T(8,128)(2,1)S(1)}, bf16[8,7296]{1,0:T(8,128)(2,1)S(1)}, u32[]{:S(2)}, u32[]{:S(2)}) collective-permute-start(bf16[8,7296]{1,0:T(8,128)(2,1)S(1)} %collective-permute-done.1.refs_2_), channel_id=1, source_target_pairs={{0,8},{4,12},{8,0},{12,4},{1,9},{5,13},{9,1},{13,5},{2,10},{6,14},... | collective-permute-start | bytes 350216 | tf_op jit(solution)/shard_map/ppermute | solution.py:173
  12.5 6.1 %collective-permute-start.5 = (bf16[8,7296]{1,0:T(8,128)(2,1)S(1)}, bf16[8,7296]{1,0:T(8,128)(2,1)S(1)}, u32[]{:S(2)}, u32[]{:S(2)}) collective-permute-start(bf16[8,7296]{1,0:T(8,128)(2,1)S(1)} %collective-permute-done.3.refs_0_), channel_id=1, source_target_pairs={{0,8},{4,12},{8,0},{12,4},{1,9},{5,13},{9,1},{13,5},{2,10},{6,14},... | collective-permute-start | bytes 350216 | tf_op jit(solution)/shard_map/ppermute | solution.py:173
  14.0 4.8 %collective-permute-start.4 = (bf16[8,7296]{1,0:T(8,128)(2,1)S(1)}, bf16[8,7296]{1,0:T(8,128)(2,1)S(1)}, u32[]{:S(2)}, u32[]{:S(2)}) collective-permute-start(bf16[8,7296]{1,0:T(8,128)(2,1)S(1)} %collective-permute-done.3.refs_0_), channel_id=1, source_target_pairs={{0,1},{1,0},{2,3},{3,2},{4,5},{5,4},{6,7},{7,6},{8,9},{9,8},{10,11... | collective-permute-start | bytes 350216 | tf_op jit(solution)/shard_map/ppermute | solution.py:177
  14.7 5.7 %collective-permute-start.6 = (bf16[8,7296]{1,0:T(8,128)(2,1)S(1)}, bf16[8,7296]{1,0:T(8,128)(2,1)S(1)}, u32[]{:S(2)}, u32[]{:S(2)}) collective-permute-start(bf16[8,7296]{1,0:T(8,128)(2,1)S(1)} %collective-permute-done.3.refs_0_), channel_id=1, source_target_pairs={{0,9},{1,8},{2,11},{3,10},{4,13},{5,12},{6,15},{7,14},{8,1},{9,0},... | collective-permute-start | bytes 350216 | tf_op jit(solution)/shard_map/ppermute | solution.py:183
  16.0 4.6 %collective-permute-start.7 = (bf16[32,7296]{1,0:T(8,128)(2,1)S(1)}, bf16[32,7296]{1,0:T(8,128)(2,1)S(1)}, u32[]{:S(2)}, u32[]{:S(2)}) collective-permute-start(bf16[32,7296]{1,0:T(8,128)(2,1)S(1)} %stack.2.refs_0_), channel_id=1, source_target_pairs={{0,4},{4,0},{8,12},{12,8},{1,5},{5,1},{9,13},{13,9},{2,6},{6,2},{1... | collective-permute-start | bytes 1400840 | tf_op jit(solution)/shard_map/ppermute | solution.py:169
  20.5 7.1 %slice-start = ((s8[14680064]{0:T(1024)(128)(4,1)}), s8[4194304]{0:T(1024)(128)(4,1)S(1)}, s32[]{:S(2)}) async-start(s8[14680064]{0:T(1024)(128)(4,1)} %bitcast.3), calls=%async_computation | async-start | bytes 8388608
  20.5 7.0 %slice-start.1 = ((s8[14680064]{0:T(1024)(128)(4,1)}), s8[4194304]{0:T(1024)(128)(4,1)S(1)}, s32[]{:S(2)}) async-start(s8[14680064]{0:T(1024)(128)(4,1)} %bitcast.3), calls=%async_computation.1 | async-start | bytes 8388608
  20.5 7.0 %slice-start.2 = ((s8[14680064]{0:T(1024)(128)(4,1)}), s8[4194304]{0:T(1024)(128)(4,1)S(1)}, s32[]{:S(2)}) async-start(s8[14680064]{0:T(1024)(128)(4,1)} %bitcast.3), calls=%async_computation.2 | async-start | bytes 8388608
  20.6 7.0 %slice-start.3 = ((s8[14680064]{0:T(1024)(128)(4,1)}), s8[2097152]{0:T(1024)(128)(4,1)S(1)}, s32[]{:S(2)}) async-start(s8[14680064]{0:T(1024)(128)(4,1)} %bitcast.3), calls=%async_computation.3 | async-start | bytes 4194304
  20.6 1.9 %collective-permute-start.8 = (bf16[32,7296]{1,0:T(8,128)(2,1)S(1)}, bf16[32,7296]{1,0:T(8,128)(2,1)S(1)}, u32[]{:S(2)}, u32[]{:S(2)}) collective-permute-start(bf16[32,7296]{1,0:T(8,128)(2,1)S(1)} %stack.3.refs_1_), channel_id=1, source_target_pairs={{0,4},{4,0},{8,12},{12,8},{1,5},{5,1},{9,13},{13,9},{2,6},{6,2},{1... | collective-permute-start | bytes 1400840 | tf_op jit(solution)/shard_map/ppermute | solution.py:169
  30.3 1.9 %collective-permute-start.9 = (bf16[32,7168]{1,0:T(8,128)(2,1)S(1)}, bf16[32,7168]{1,0:T(8,128)(2,1)S(1)}, u32[]{:S(2)}, u32[]{:S(2)}) collective-permute-start(bf16[32,7168]{1,0:T(8,128)(2,1)S(1)} %get-tuple-element.17), channel_id=1, source_target_pairs={{0,4},{4,0},{8,12},{12,8},{1,5},{5,1},{9,13},{13,9},{2,6},{6,2},{1... | collective-permute-start | bytes 1376264 | tf_op jit(solution)/shard_map/ppermute | solution.py:169
  32.1 3.9 %collective-permute-start.10 = (bf16[32,7168]{1,0:T(8,128)(2,1)S(1)}, bf16[32,7168]{1,0:T(8,128)(2,1)S(1)}, u32[]{:S(2)}, u32[]{:S(2)}) collective-permute-start(bf16[32,7168]{1,0:T(8,128)(2,1)S(1)} %get-tuple-element.18), channel_id=1, source_target_pairs={{0,4},{4,0},{8,12},{12,8},{1,5},{5,1},{9,13},{13,9},{2,6},{6,2},{1... | collective-permute-start | bytes 1376264 | tf_op jit(solution)/shard_map/ppermute | solution.py:169
  32.4 5.5 %collective-permute-start.11 = (bf16[8,7168]{1,0:T(8,128)(2,1)S(1)}, bf16[8,7168]{1,0:T(8,128)(2,1)S(1)}, u32[]{:S(2)}, u32[]{:S(2)}) collective-permute-start(bf16[8,7168]{1,0:T(8,128)(2,1)S(1)} %get-tuple-element.21), channel_id=1, source_target_pairs={{0,8},{4,12},{8,0},{12,4},{1,9},{5,13},{9,1},{13,5},{2,10},{6,14},... | collective-permute-start | bytes 344072 | tf_op jit(solution)/shard_map/ppermute | solution.py:173
  34.2 6.0 %collective-permute-start.13 = (bf16[8,7168]{1,0:T(8,128)(2,1)S(1)}, bf16[8,7168]{1,0:T(8,128)(2,1)S(1)}, u32[]{:S(2)}, u32[]{:S(2)}) collective-permute-start(bf16[8,7168]{1,0:T(8,128)(2,1)S(1)} %get-tuple-element.22), channel_id=1, source_target_pairs={{0,1},{1,0},{2,3},{3,2},{4,5},{5,4},{6,7},{7,6},{8,9},{9,8},{10,11... | collective-permute-start | bytes 344072 | tf_op jit(solution)/shard_map/ppermute | solution.py:177
  34.3 7.4 %collective-permute-start.12 = (bf16[8,7168]{1,0:T(8,128)(2,1)S(1)}, bf16[8,7168]{1,0:T(8,128)(2,1)S(1)}, u32[]{:S(2)}, u32[]{:S(2)}) collective-permute-start(bf16[8,7168]{1,0:T(8,128)(2,1)S(1)} %get-tuple-element.23), channel_id=1, source_target_pairs={{0,9},{1,8},{2,11},{3,10},{4,13},{5,12},{6,15},{7,14},{8,1},{9,0},... | collective-permute-start | bytes 344072 | tf_op jit(solution)/shard_map/ppermute | solution.py:183
  36.1 9.0 %collective-permute-start.16 = (bf16[8,7168]{1,0:T(8,128)(2,1)S(1)}, bf16[8,7168]{1,0:T(8,128)(2,1)S(1)}, u32[]{:S(2)}, u32[]{:S(2)}) collective-permute-start(bf16[8,7168]{1,0:T(8,128)(2,1)S(1)} %get-tuple-element.25), channel_id=1, source_target_pairs={{0,8},{4,12},{8,0},{12,4},{1,9},{5,13},{9,1},{13,5},{2,10},{6,14},... | collective-permute-start | bytes 344072 | tf_op jit(solution)/shard_map/ppermute | solution.py:173
  41.7 7.6 %collective-permute-start.14 = (bf16[8,7168]{1,0:T(8,128)(2,1)S(1)}, bf16[8,7168]{1,0:T(8,128)(2,1)S(1)}, u32[]{:S(2)}, u32[]{:S(2)}) collective-permute-start(bf16[8,7168]{1,0:T(8,128)(2,1)S(1)} %add_convert_fusion.4), channel_id=1, source_target_pairs={{0,2},{1,3},{2,0},{3,1},{4,6},{5,7},{6,4},{7,5},{8,10},{9,11},{10,... | collective-permute-start | bytes 344072 | tf_op jit(solution)/shard_map/ppermute | solution.py:177
  43.9 5.4 %collective-permute-start.15 = (bf16[8,7168]{1,0:T(8,128)(2,1)S(1)}, bf16[8,7168]{1,0:T(8,128)(2,1)S(1)}, u32[]{:S(2)}, u32[]{:S(2)}) collective-permute-start(bf16[8,7168]{1,0:T(8,128)(2,1)S(1)} %get-tuple-element.20), channel_id=1, source_target_pairs={{0,8},{4,12},{8,0},{12,4},{1,9},{5,13},{9,1},{13,5},{2,10},{6,14},... | collective-permute-start | bytes 344072 | tf_op jit(solution)/shard_map/ppermute | solution.py:173
  45.2 5.4 %collective-permute-start.17 = (bf16[8,7168]{1,0:T(8,128)(2,1)S(1)}, bf16[8,7168]{1,0:T(8,128)(2,1)S(1)}, u32[]{:S(2)}, u32[]{:S(2)}) collective-permute-start(bf16[8,7168]{1,0:T(8,128)(2,1)S(1)} %add_convert_fusion.3), channel_id=1, source_target_pairs={{0,1},{1,0},{2,3},{3,2},{4,5},{5,4},{6,7},{7,6},{8,9},{9,8},{10,11... | collective-permute-start | bytes 344072 | tf_op jit(solution)/shard_map/ppermute | solution.py:177

commit v12 on v11

--- a/solution.py
+++ b/solution.py
@@ -209,12 +209,15 @@
     other_late = to_core(other_late)
     other_early = to_core(after(other_early, other_late))
     second, third, far_second, far_third = blocks(late, other_late)
-    second = total(second, to_chip(far_second), to_both(far_third, 1), to_place(third, 1))
-    second = second.astype(jnp.bfloat16)
+    far_second = to_chip(far_second)
+    far_third = to_both(far_third, 1)
+    third = to_place(third, 1)
+    second = total(second, far_second, far_third, third).astype(jnp.bfloat16)
     own, far_own, first, far_first = blocks(early, other_early)
-    first = total(first, to_chip(far_first)).astype(jnp.bfloat16)
-    far_own = to_chip(after(far_own, second))
-    return total(own, to_place(second, 2), far_own, to_place(first, 1)).astype(jnp.bfloat16)
+    first = total(first, to_chip(after(far_first, third))).astype(jnp.bfloat16)
+    first, far_own = lax.optimization_barrier((first, far_own))
+    second_here, first_here, far_own = to_place(second, 2), to_place(first, 1), to_chip(far_own)
+    return total(own, second_here, first_here, far_own).astype(jnp.bfloat16)
 
 
 def by_permutes(tokens, expert_ids, route_weights, expert_slot, w_gate, w_up, w_down):

time: 51.4 us -> 51.1 us (level)
  starting transfers between devices: 23.4 us -> 21.1 us
  waiting for transfers between devices: 17.6 us -> 19.6 us
    ppermute x6, waiting for transfers between devices: 8.28 us -> 9.69 us  [to_place(): return lax.ppermute(value, 'local', [(i, i ^ bits) for i in range(PLACES)])]
    ppermute x6, starting transfers between devices: 10.6 us -> 9.27 us  [to_place(): return lax.ppermute(value, 'local', [(i, i ^ bits) for i in range(PLACES)])]
    ppermute x6, waiting for transfers between devices: 2.58 us -> 3.64 us  [to_chip(): return lax.ppermute(value, 'node', [(i, i ^ 2) for i in range(2 * CHIPS)])]
    ppermute x6, starting transfers between devices: 9.48 us -> 8.44 us  [to_chip(): return lax.ppermute(value, 'node', [(i, i ^ 2) for i in range(2 * CHIPS)])]
  transfers between devices with their start and end apart: 18 -> 18, of which waited for: 12 -> 13; matrix products, arithmetic and copies ran while one was open for 1% -> 1% of each run, Pallas kernels for 0% -> 0%
where the time goes in v12:
time: 51.1 us; the launch traced here: 50.9 us
  starting transfers between devices  21.1 us (41%)
  waiting for transfers between devices  19.6 us (38%)
  Pallas kernels  9.03 us (18%)
  other arithmetic  1.01 us (2%)
    ppermute x6, waiting for transfers between devices, to_place(): return lax.ppermute(value, 'local', [(i, i ^ bits) for i in range(PLACES)])  9.69 us
    ppermute x6, starting transfers between devices, to_place(): return lax.ppermute(value, 'local', [(i, i ^ bits) for i in range(PLACES)])  9.27 us
    ppermute x6, starting transfers between devices, to_chip(): return lax.ppermute(value, 'node', [(i, i ^ 2) for i in range(2 * CHIPS)])  8.44 us
    pallas_call x1, Pallas kernels, hidden_units(): pl.pallas_call(functools.partial(hidden_kernel, experts), out_shape=jax.S...  5.04 us
    ppermute x6, waiting for transfers between devices, to_chip(): return lax.ppermute(value, 'node', [(i, i ^ 2) for i in range(2 * CHIPS)])  3.64 us
    ppermute x4, waiting for transfers between devices, to_core(): return lax.ppermute(value, 'node', [(i, i ^ 1) for i in range(2 * CHIPS)])  3.52 us
    ppermute x2, starting transfers between devices, to_both(): return lax.ppermute(value, ('node', 'local'), perm)  2.91 us
    ppermute x2, waiting for transfers between devices, to_both(): return lax.ppermute(value, ('node', 'local'), perm)  2.74 us
  transfers between devices with their start and end apart: 18, of which 13 were waited for; matrix products, arithmetic and copies ran while one was open for 1% of the time, Pallas kernels for 0%

profile of v12, /device:TPU:0, one launch (start us, length us, event | category | flops | bytes accessed | tf_op | source)
XLA Modules:
  0.0 50.9 jit_solution(6719670385560443614)
XLA Ops:
  0.0 0.0 copy-start
  0.0 0.0 copy-start.1
  0.0 1.2 %pack.1.refs_0_ = bf16[8,7296]{1,0:T(8,128)(2,1)S(1)} custom-call(bf16[8,7168]{1,0:T(8,128)(2,1)} %refs_0_.1, s32[4,8]{1,0:T(4,128)} %bitcast.6, f32[4,8]{1,0:T(4,128)} %bitcast.7, s32[8]{0:T(128)} %refs_3_.1, bf16[2,7168,512]{2,1,0:T(8,128)(2,1)} %refs_4_.3, bf16[2,7168,512]{2,1,0:T(8,128)(2,1)} %refs_5_.3, bf16[2,512,7168]{2,1,0:T(8,128)(2,1)} %refs_6_.1), custom_call_target="tpu_custom_call" | custom-call | tf_op jit(solution)/shard_map/pack/pallas_call | solution.py:50
  1.2 3.1 %collective-permute-start.1 = (bf16[8,7296]{1,0:T(8,128)(2,1)S(1)}, bf16[8,7296]{1,0:T(8,128)(2,1)S(1)}, u32[]{:S(2)}, u32[]{:S(2)}) collective-permute-start(bf16[8,7296]{1,0:T(8,128)(2,1)S(1)} %pack.1.refs_0_), channel_id=1, source_target_pairs={{0,1},{1,0},{2,3},{3,2},{4,5},{5,4},{6,7},{7,6},{8,9},{9,8},{10,11... | collective-permute-start | bytes 350216 | tf_op jit(solution)/shard_map/ppermute | solution.py:177
  4.3 2.6 %collective-permute-start.3 = (bf16[8,7296]{1,0:T(8,128)(2,1)S(1)}, bf16[8,7296]{1,0:T(8,128)(2,1)S(1)}, u32[]{:S(2)}, u32[]{:S(2)}) collective-permute-start(bf16[8,7296]{1,0:T(8,128)(2,1)S(1)} %pack.1.refs_0_), channel_id=1, source_target_pairs={{0,2},{1,3},{2,0},{3,1},{4,6},{5,7},{6,4},{7,5},{8,10},{9,11},{10,... | collective-permute-start | bytes 350216 | tf_op jit(solution)/shard_map/ppermute | solution.py:177
  6.8 1.5 %collective-permute-start = (bf16[8,7296]{1,0:T(8,128)(2,1)S(1)}, bf16[8,7296]{1,0:T(8,128)(2,1)S(1)}, u32[]{:S(2)}, u32[]{:S(2)}) collective-permute-start(bf16[8,7296]{1,0:T(8,128)(2,1)S(1)} %pack.1.refs_0_), channel_id=1, source_target_pairs={{0,8},{4,12},{8,0},{12,4},{1,9},{5,13},{9,1},{13,5},{2,10},{6,14},... | collective-permute-start | bytes 350216 | tf_op jit(solution)/shard_map/ppermute | solution.py:173
  8.3 0.3 collective-permute-done.1.refs_2_
  8.7 1.8 %collective-permute-start.2 = (bf16[8,7296]{1,0:T(8,128)(2,1)S(1)}, bf16[8,7296]{1,0:T(8,128)(2,1)S(1)}, u32[]{:S(2)}, u32[]{:S(2)}) collective-permute-start(bf16[8,7296]{1,0:T(8,128)(2,1)S(1)} %collective-permute-done.1.refs_2_), channel_id=1, source_target_pairs={{0,8},{4,12},{8,0},{12,4},{1,9},{5,13},{9,1},{13,5},{2,10},{6,14},... | collective-permute-start | bytes 350216 | tf_op jit(solution)/shard_map/ppermute | solution.py:173
  10.5 1.9 %collective-permute-done.3.refs_0_ = bf16[8,7296]{1,0:T(8,128)(2,1)S(1)} collective-permute-done((bf16[8,7296]{1,0:T(8,128)(2,1)S(1)}, bf16[8,7296]{1,0:T(8,128)(2,1)S(1)}, u32[]{:S(2)}, u32[]{:S(2)}) %collective-permute-start.3) | collective-permute-done | bytes 116768 | tf_op jit(solution)/shard_map/ppermute | solution.py:177
  12.4 0.1 collective-permute-done.refs_1_
  12.5 1.5 %collective-permute-start.5 = (bf16[8,7296]{1,0:T(8,128)(2,1)S(1)}, bf16[8,7296]{1,0:T(8,128)(2,1)S(1)}, u32[]{:S(2)}, u32[]{:S(2)}) collective-permute-start(bf16[8,7296]{1,0:T(8,128)(2,1)S(1)} %collective-permute-done.3.refs_0_), channel_id=1, source_target_pairs={{0,8},{4,12},{8,0},{12,4},{1,9},{5,13},{9,1},{13,5},{2,10},{6,14},... | collective-permute-start | bytes 350216 | tf_op jit(solution)/shard_map/ppermute | solution.py:173
  14.0 0.8 %collective-permute-start.4 = (bf16[8,7296]{1,0:T(8,128)(2,1)S(1)}, bf16[8,7296]{1,0:T(8,128)(2,1)S(1)}, u32[]{:S(2)}, u32[]{:S(2)}) collective-permute-start(bf16[8,7296]{1,0:T(8,128)(2,1)S(1)} %collective-permute-done.3.refs_0_), channel_id=1, source_target_pairs={{0,1},{1,0},{2,3},{3,2},{4,5},{5,4},{6,7},{7,6},{8,9},{9,8},{10,11... | collective-permute-start | bytes 350216 | tf_op jit(solution)/shard_map/ppermute | solution.py:177
  14.7 0.0 collective-permute-done.2.refs_3_
  14.7 1.2 %collective-permute-start.6 = (bf16[8,7296]{1,0:T(8,128)(2,1)S(1)}, bf16[8,7296]{1,0:T(8,128)(2,1)S(1)}, u32[]{:S(2)}, u32[]{:S(2)}) collective-permute-start(bf16[8,7296]{1,0:T(8,128)(2,1)S(1)} %collective-permute-done.3.refs_0_), channel_id=1, source_target_pairs={{0,9},{1,8},{2,11},{3,10},{4,13},{5,12},{6,15},{7,14},{8,1},{9,0},... | collective-permute-start | bytes 350216 | tf_op jit(solution)/shard_map/ppermute | solution.py:183
  16.0 0.1 stack.2.refs_0_
  16.0 0.1 collective-permute-start.7
  16.1 2.4 %collective-permute-done.5.refs_2_ = bf16[8,7296]{1,0:T(8,128)(2,1)S(1)} collective-permute-done((bf16[8,7296]{1,0:T(8,128)(2,1)S(1)}, bf16[8,7296]{1,0:T(8,128)(2,1)S(1)}, u32[]{:S(2)}, u32[]{:S(2)}) %collective-permute-start.5) | collective-permute-done | bytes 116768 | tf_op jit(solution)/shard_map/ppermute | solution.py:173
  18.5 0.2 collective-permute-done.4.refs_1_
  18.8 1.7 %collective-permute-done.6.refs_3_ = bf16[8,7296]{1,0:T(8,128)(2,1)S(1)} collective-permute-done((bf16[8,7296]{1,0:T(8,128)(2,1)S(1)}, bf16[8,7296]{1,0:T(8,128)(2,1)S(1)}, u32[]{:S(2)}, u32[]{:S(2)}) %collective-permute-start.6) | collective-permute-done | bytes 116768 | tf_op jit(solution)/shard_map/ppermute | solution.py:183
  20.5 0.0 slice-start
  20.5 0.1 stack.3.refs_1_
  20.5 0.0 slice-start.1
  20.5 0.0 slice-start.2
  20.6 0.0 slice-start.3
  20.6 0.1 collective-permute-start.8
  20.6 0.0 collective-permute-done.7.refs_2_
  20.7 1.8 %collective-permute-done.8.refs_3_ = bf16[32,7296]{1,0:T(8,128)(2,1)S(1)} collective-permute-done((bf16[32,7296]{1,0:T(8,128)(2,1)S(1)}, bf16[32,7296]{1,0:T(8,128)(2,1)S(1)}, u32[]{:S(2)}, u32[]{:S(2)}) %collective-permute-start.8) | collective-permute-done | bytes 466976 | tf_op jit(solution)/shard_map/ppermute | solution.py:169
  22.5 0.0 copy-done
  22.5 0.0 copy-done.1
  22.5 5.0 %hidden.1.hidden_ref = bf16[128,1024]{1,0:T(8,128)(2,1)S(1)} custom-call(bf16[32,7296]{1,0:T(8,128)(2,1)S(1)} %stack.2.refs_0_, bf16[32,7296]{1,0:T(8,128)(2,1)S(1)} %stack.3.refs_1_, bf16[32,7296]{1,0:T(8,128)(2,1)S(1)} %collective-permute-done.7.refs_2_, bf16[32,7296]{1,0:T(8,128)(2,1)S(1)} %collective-permute-done.8.refs_3_, ...), custom_call_target="tpu_custom_call" | custom-call | flops 3758096384 | bytes 29360128 | tf_op jit(solution)/shard_map/hidden/pallas_call | solution.py:113
  27.5 0.0 slice-done
  27.5 0.0 slice-done.1
  27.5 0.0 slice-done.2
  27.5 0.0 slice-done.3
  27.6 2.7 %down.1 = (bf16[32,7168]{1,0:T(8,128)(2,1)S(1)}, bf16[32,7168]{1,0:T(8,128)(2,1)S(1)}, bf16[32,7168]{1,0:T(8,128)(2,1)S(1)}, bf16[32,7168]{1,0:T(8,128)(2,1)S(1)}) custom-call(bf16[128,1024]{1,0:T(8,128)(2,1)S(1)} %hidden.1.hidden_ref, bf16[1024,7168]{1,0:T(8,128)(2,1)S(1)} %bitcast.5), custom_call_target="tpu_custom_call" | custom-call | flops 1879048192 | bytes 14680064 | tf_op jit(solution)/shard_map/down/pallas_call | solution.py:150
  30.3 0.2 collective-permute-start.9
  30.4 1.7 %collective-permute-done.9 = bf16[32,7168]{1,0:T(8,128)(2,1)S(1)} collective-permute-done((bf16[32,7168]{1,0:T(8,128)(2,1)S(1)}, bf16[32,7168]{1,0:T(8,128)(2,1)S(1)}, u32[]{:S(2)}, u32[]{:S(2)}) %collective-permute-start.9) | collective-permute-done | bytes 458784 | tf_op jit(solution)/shard_map/ppermute | solution.py:169
  32.1 0.1 collective-permute-start.10
  32.3 0.1 add_convert_fusion
  32.4 1.7 %collective-permute-start.11 = (bf16[8,7168]{1,0:T(8,128)(2,1)S(1)}, bf16[8,7168]{1,0:T(8,128)(2,1)S(1)}, u32[]{:S(2)}, u32[]{:S(2)}) collective-permute-start(bf16[8,7168]{1,0:T(8,128)(2,1)S(1)} %get-tuple-element.25), channel_id=1, source_target_pairs={{0,8},{4,12},{8,0},{12,4},{1,9},{5,13},{9,1},{13,5},{2,10},{6,14},... | collective-permute-start | bytes 344072 | tf_op jit(solution)/shard_map/ppermute | solution.py:173
  34.2 0.1 collective-permute-start.13
  34.3 1.7 %collective-permute-start.12 = (bf16[8,7168]{1,0:T(8,128)(2,1)S(1)}, bf16[8,7168]{1,0:T(8,128)(2,1)S(1)}, u32[]{:S(2)}, u32[]{:S(2)}) collective-permute-start(bf16[8,7168]{1,0:T(8,128)(2,1)S(1)} %get-tuple-element.27), channel_id=1, source_target_pairs={{0,9},{1,8},{2,11},{3,10},{4,13},{5,12},{6,15},{7,14},{8,1},{9,0},... | collective-permute-start | bytes 344072 | tf_op jit(solution)/shard_map/ppermute | solution.py:183
  36.0 0.0 collective-permute-done.10
  36.0 0.1 add_convert_fusion.1
  36.1 4.0 %collective-permute-done.13 = bf16[8,7168]{1,0:T(8,128)(2,1)S(1)} collective-permute-done((bf16[8,7168]{1,0:T(8,128)(2,1)S(1)}, bf16[8,7168]{1,0:T(8,128)(2,1)S(1)}, u32[]{:S(2)}, u32[]{:S(2)}) %collective-permute-start.13) | collective-permute-done | bytes 114720 | tf_op jit(solution)/shard_map/ppermute | solution.py:177
  40.2 0.4 collective-permute-start.15
  40.5 0.0 collective-permute-done.11
  40.5 1.1 %collective-permute-done.12 = bf16[8,7168]{1,0:T(8,128)(2,1)S(1)} collective-permute-done((bf16[8,7168]{1,0:T(8,128)(2,1)S(1)}, bf16[8,7168]{1,0:T(8,128)(2,1)S(1)}, u32[]{:S(2)}, u32[]{:S(2)}) %collective-permute-start.12) | collective-permute-done | bytes 114720 | tf_op jit(solution)/shard_map/ppermute | solution.py:183
  41.6 0.1 add_convert_fusion.4
  41.7 2.2 %collective-permute-start.14 = (bf16[8,7168]{1,0:T(8,128)(2,1)S(1)}, bf16[8,7168]{1,0:T(8,128)(2,1)S(1)}, u32[]{:S(2)}, u32[]{:S(2)}) collective-permute-start(bf16[8,7168]{1,0:T(8,128)(2,1)S(1)} %add_convert_fusion.4), channel_id=1, source_target_pairs={{0,2},{1,3},{2,0},{3,1},{4,6},{5,7},{6,4},{7,5},{8,10},{9,11},{10,... | collective-permute-start | bytes 344072 | tf_op jit(solution)/shard_map/ppermute | solution.py:177
  43.9 1.1 %collective-permute-done.15 = bf16[8,7168]{1,0:T(8,128)(2,1)S(1)} collective-permute-done((bf16[8,7168]{1,0:T(8,128)(2,1)S(1)}, bf16[8,7168]{1,0:T(8,128)(2,1)S(1)}, u32[]{:S(2)}, u32[]{:S(2)}) %collective-permute-start.15) | collective-permute-done | bytes 114720 | tf_op jit(solution)/shard_map/ppermute | solution.py:173
  45.0 0.4 collective-permute-start.16
  45.4 1.5 %collective-permute-start.17 = (bf16[8,7168]{1,0:T(8,128)(2,1)S(1)}, bf16[8,7168]{1,0:T(8,128)(2,1)S(1)}, u32[]{:S(2)}, u32[]{:S(2)}) collective-permute-start(bf16[8,7168]{1,0:T(8,128)(2,1)S(1)} %get-tuple-element.24), channel_id=1, source_target_pairs={{0,8},{4,12},{8,0},{12,4},{1,9},{5,13},{9,1},{13,5},{2,10},{6,14},... | collective-permute-start | bytes 344072 | tf_op jit(solution)/shard_map/ppermute | solution.py:173
  47.0 2.3 %collective-permute-done.14 = bf16[8,7168]{1,0:T(8,128)(2,1)S(1)} collective-permute-done((bf16[8,7168]{1,0:T(8,128)(2,1)S(1)}, bf16[8,7168]{1,0:T(8,128)(2,1)S(1)}, u32[]{:S(2)}, u32[]{:S(2)}) %collective-permute-start.14) | collective-permute-done | bytes 114720 | tf_op jit(solution)/shard_map/ppermute | solution.py:177
  49.3 0.9 %collective-permute-done.16 = bf16[8,7168]{1,0:T(8,128)(2,1)S(1)} collective-permute-done((bf16[8,7168]{1,0:T(8,128)(2,1)S(1)}, bf16[8,7168]{1,0:T(8,128)(2,1)S(1)}, u32[]{:S(2)}, u32[]{:S(2)}) %collective-permute-start.16) | collective-permute-done | bytes 114720 | tf_op jit(solution)/shard_map/ppermute | solution.py:177
  50.2 0.0 collective-permute-done.17
  50.2 0.7 %add_convert_fusion.2 = bf16[8,7168]{1,0:T(8,128)(2,1)} fusion(bf16[8,7168]{1,0:T(8,128)(2,1)S(1)} %collective-permute-done.17, bf16[8,7168]{1,0:T(8,128)(2,1)S(1)} %collective-permute-done.16, bf16[8,7168]{1,0:T(8,128)(2,1)S(1)} %collective-permute-done.14, bf16[32,7168]{1,0:T(8,128)(2,1)S(1)} %add_convert_fusion.1), kind=kLoop, calls=%fused_computation.2 | loop fusion | flops 458752 | bytes 573440 | tf_op jit(solution)/shard_map/convert_element_type | solution.py:220
  (4 shorter events, 0.1 us)
Async XLA Ops:
  0.0 22.5 %copy-start = (bf16[2,7168,512]{2,1,0:T(8,128)(2,1)S(1)}, bf16[2,7168,512]{2,1,0:T(8,128)(2,1)}, u32[]{:S(2)}) copy-start(bf16[2,7168,512]{2,1,0:T(8,128)(2,1)} %refs_4_.3) | copy-start | bytes 44040196
  0.0 22.5 %copy-start.1 = (bf16[2,7168,512]{2,1,0:T(8,128)(2,1)S(1)}, bf16[2,7168,512]{2,1,0:T(8,128)(2,1)}, u32[]{:S(2)}) copy-start(bf16[2,7168,512]{2,1,0:T(8,128)(2,1)} %refs_5_.3) | copy-start | bytes 44040196
  1.2 7.5 %collective-permute-start.1 = (bf16[8,7296]{1,0:T(8,128)(2,1)S(1)}, bf16[8,7296]{1,0:T(8,128)(2,1)S(1)}, u32[]{:S(2)}, u32[]{:S(2)}) collective-permute-start(bf16[8,7296]{1,0:T(8,128)(2,1)S(1)} %pack.1.refs_0_), channel_id=1, source_target_pairs={{0,1},{1,0},{2,3},{3,2},{4,5},{5,4},{6,7},{7,6},{8,9},{9,8},{10,11... | collective-permute-start | bytes 350216 | tf_op jit(solution)/shard_map/ppermute | solution.py:177
  4.3 8.1 %collective-permute-start.3 = (bf16[8,7296]{1,0:T(8,128)(2,1)S(1)}, bf16[8,7296]{1,0:T(8,128)(2,1)S(1)}, u32[]{:S(2)}, u32[]{:S(2)}) collective-permute-start(bf16[8,7296]{1,0:T(8,128)(2,1)S(1)} %pack.1.refs_0_), channel_id=1, source_target_pairs={{0,2},{1,3},{2,0},{3,1},{4,6},{5,7},{6,4},{7,5},{8,10},{9,11},{10,... | collective-permute-start | bytes 350216 | tf_op jit(solution)/shard_map/ppermute | solution.py:177
  6.8 5.6 %collective-permute-start = (bf16[8,7296]{1,0:T(8,128)(2,1)S(1)}, bf16[8,7296]{1,0:T(8,128)(2,1)S(1)}, u32[]{:S(2)}, u32[]{:S(2)}) collective-permute-start(bf16[8,7296]{1,0:T(8,128)(2,1)S(1)} %pack.1.refs_0_), channel_id=1, source_target_pairs={{0,8},{4,12},{8,0},{12,4},{1,9},{5,13},{9,1},{13,5},{2,10},{6,14},... | collective-permute-start | bytes 350216 | tf_op jit(solution)/shard_map/ppermute | solution.py:173
  8.7 6.1 %collective-permute-start.2 = (bf16[8,7296]{1,0:T(8,128)(2,1)S(1)}, bf16[8,7296]{1,0:T(8,128)(2,1)S(1)}, u32[]{:S(2)}, u32[]{:S(2)}) collective-permute-start(bf16[8,7296]{1,0:T(8,128)(2,1)S(1)} %collective-permute-done.1.refs_2_), channel_id=1, source_target_pairs={{0,8},{4,12},{8,0},{12,4},{1,9},{5,13},{9,1},{13,5},{2,10},{6,14},... | collective-permute-start | bytes 350216 | tf_op jit(solution)/shard_map/ppermute | solution.py:173
  12.5 6.1 %collective-permute-start.5 = (bf16[8,7296]{1,0:T(8,128)(2,1)S(1)}, bf16[8,7296]{1,0:T(8,128)(2,1)S(1)}, u32[]{:S(2)}, u32[]{:S(2)}) collective-permute-start(bf16[8,7296]{1,0:T(8,128)(2,1)S(1)} %collective-permute-done.3.refs_0_), channel_id=1, source_target_pairs={{0,8},{4,12},{8,0},{12,4},{1,9},{5,13},{9,1},{13,5},{2,10},{6,14},... | collective-permute-start | bytes 350216 | tf_op jit(solution)/shard_map/ppermute | solution.py:173
  14.0 4.8 %collective-permute-start.4 = (bf16[8,7296]{1,0:T(8,128)(2,1)S(1)}, bf16[8,7296]{1,0:T(8,128)(2,1)S(1)}, u32[]{:S(2)}, u32[]{:S(2)}) collective-permute-start(bf16[8,7296]{1,0:T(8,128)(2,1)S(1)} %collective-permute-done.3.refs_0_), channel_id=1, source_target_pairs={{0,1},{1,0},{2,3},{3,2},{4,5},{5,4},{6,7},{7,6},{8,9},{9,8},{10,11... | collective-permute-start | bytes 350216 | tf_op jit(solution)/shard_map/ppermute | solution.py:177
  14.7 5.7 %collective-permute-start.6 = (bf16[8,7296]{1,0:T(8,128)(2,1)S(1)}, bf16[8,7296]{1,0:T(8,128)(2,1)S(1)}, u32[]{:S(2)}, u32[]{:S(2)}) collective-permute-start(bf16[8,7296]{1,0:T(8,128)(2,1)S(1)} %collective-permute-done.3.refs_0_), channel_id=1, source_target_pairs={{0,9},{1,8},{2,11},{3,10},{4,13},{5,12},{6,15},{7,14},{8,1},{9,0},... | collective-permute-start | bytes 350216 | tf_op jit(solution)/shard_map/ppermute | solution.py:183
  16.0 4.6 %collective-permute-start.7 = (bf16[32,7296]{1,0:T(8,128)(2,1)S(1)}, bf16[32,7296]{1,0:T(8,128)(2,1)S(1)}, u32[]{:S(2)}, u32[]{:S(2)}) collective-permute-start(bf16[32,7296]{1,0:T(8,128)(2,1)S(1)} %stack.2.refs_0_), channel_id=1, source_target_pairs={{0,4},{4,0},{8,12},{12,8},{1,5},{5,1},{9,13},{13,9},{2,6},{6,2},{1... | collective-permute-start | bytes 1400840 | tf_op jit(solution)/shard_map/ppermute | solution.py:169
  20.5 7.1 %slice-start = ((s8[14680064]{0:T(1024)(128)(4,1)}), s8[4194304]{0:T(1024)(128)(4,1)S(1)}, s32[]{:S(2)}) async-start(s8[14680064]{0:T(1024)(128)(4,1)} %bitcast.3), calls=%async_computation | async-start | bytes 8388608
  20.5 7.0 %slice-start.1 = ((s8[14680064]{0:T(1024)(128)(4,1)}), s8[4194304]{0:T(1024)(128)(4,1)S(1)}, s32[]{:S(2)}) async-start(s8[14680064]{0:T(1024)(128)(4,1)} %bitcast.3), calls=%async_computation.1 | async-start | bytes 8388608
  20.5 7.0 %slice-start.2 = ((s8[14680064]{0:T(1024)(128)(4,1)}), s8[4194304]{0:T(1024)(128)(4,1)S(1)}, s32[]{:S(2)}) async-start(s8[14680064]{0:T(1024)(128)(4,1)} %bitcast.3), calls=%async_computation.2 | async-start | bytes 8388608
  20.6 7.0 %slice-start.3 = ((s8[14680064]{0:T(1024)(128)(4,1)}), s8[2097152]{0:T(1024)(128)(4,1)S(1)}, s32[]{:S(2)}) async-start(s8[14680064]{0:T(1024)(128)(4,1)} %bitcast.3), calls=%async_computation.3 | async-start | bytes 4194304
  20.6 1.9 %collective-permute-start.8 = (bf16[32,7296]{1,0:T(8,128)(2,1)S(1)}, bf16[32,7296]{1,0:T(8,128)(2,1)S(1)}, u32[]{:S(2)}, u32[]{:S(2)}) collective-permute-start(bf16[32,7296]{1,0:T(8,128)(2,1)S(1)} %stack.3.refs_1_), channel_id=1, source_target_pairs={{0,4},{4,0},{8,12},{12,8},{1,5},{5,1},{9,13},{13,9},{2,6},{6,2},{1... | collective-permute-start | bytes 1400840 | tf_op jit(solution)/shard_map/ppermute | solution.py:169
  30.3 1.9 %collective-permute-start.9 = (bf16[32,7168]{1,0:T(8,128)(2,1)S(1)}, bf16[32,7168]{1,0:T(8,128)(2,1)S(1)}, u32[]{:S(2)}, u32[]{:S(2)}) collective-permute-start(bf16[32,7168]{1,0:T(8,128)(2,1)S(1)} %get-tuple-element.19), channel_id=1, source_target_pairs={{0,4},{4,0},{8,12},{12,8},{1,5},{5,1},{9,13},{13,9},{2,6},{6,2},{1... | collective-permute-start | bytes 1376264 | tf_op jit(solution)/shard_map/ppermute | solution.py:169
  32.1 3.9 %collective-permute-start.10 = (bf16[32,7168]{1,0:T(8,128)(2,1)S(1)}, bf16[32,7168]{1,0:T(8,128)(2,1)S(1)}, u32[]{:S(2)}, u32[]{:S(2)}) collective-permute-start(bf16[32,7168]{1,0:T(8,128)(2,1)S(1)} %get-tuple-element.20), channel_id=1, source_target_pairs={{0,4},{4,0},{8,12},{12,8},{1,5},{5,1},{9,13},{13,9},{2,6},{6,2},{1... | collective-permute-start | bytes 1376264 | tf_op jit(solution)/shard_map/ppermute | solution.py:169
  32.4 8.1 %collective-permute-start.11 = (bf16[8,7168]{1,0:T(8,128)(2,1)S(1)}, bf16[8,7168]{1,0:T(8,128)(2,1)S(1)}, u32[]{:S(2)}, u32[]{:S(2)}) collective-permute-start(bf16[8,7168]{1,0:T(8,128)(2,1)S(1)} %get-tuple-element.25), channel_id=1, source_target_pairs={{0,8},{4,12},{8,0},{12,4},{1,9},{5,13},{9,1},{13,5},{2,10},{6,14},... | collective-permute-start | bytes 344072 | tf_op jit(solution)/shard_map/ppermute | solution.py:173
  34.2 6.0 %collective-permute-start.13 = (bf16[8,7168]{1,0:T(8,128)(2,1)S(1)}, bf16[8,7168]{1,0:T(8,128)(2,1)S(1)}, u32[]{:S(2)}, u32[]{:S(2)}) collective-permute-start(bf16[8,7168]{1,0:T(8,128)(2,1)S(1)} %get-tuple-element.26), channel_id=1, source_target_pairs={{0,1},{1,0},{2,3},{3,2},{4,5},{5,4},{6,7},{7,6},{8,9},{9,8},{10,11... | collective-permute-start | bytes 344072 | tf_op jit(solution)/shard_map/ppermute | solution.py:177
  34.3 7.3 %collective-permute-start.12 = (bf16[8,7168]{1,0:T(8,128)(2,1)S(1)}, bf16[8,7168]{1,0:T(8,128)(2,1)S(1)}, u32[]{:S(2)}, u32[]{:S(2)}) collective-permute-start(bf16[8,7168]{1,0:T(8,128)(2,1)S(1)} %get-tuple-element.27), channel_id=1, source_target_pairs={{0,9},{1,8},{2,11},{3,10},{4,13},{5,12},{6,15},{7,14},{8,1},{9,0},... | collective-permute-start | bytes 344072 | tf_op jit(solution)/shard_map/ppermute | solution.py:183
  40.2 4.8 %collective-permute-start.15 = (bf16[8,7168]{1,0:T(8,128)(2,1)S(1)}, bf16[8,7168]{1,0:T(8,128)(2,1)S(1)}, u32[]{:S(2)}, u32[]{:S(2)}) collective-permute-start(bf16[8,7168]{1,0:T(8,128)(2,1)S(1)} %get-tuple-element.22), channel_id=1, source_target_pairs={{0,8},{4,12},{8,0},{12,4},{1,9},{5,13},{9,1},{13,5},{2,10},{6,14},... | collective-permute-start | bytes 344072 | tf_op jit(solution)/shard_map/ppermute | solution.py:173
  41.7 7.6 %collective-permute-start.14 = (bf16[8,7168]{1,0:T(8,128)(2,1)S(1)}, bf16[8,7168]{1,0:T(8,128)(2,1)S(1)}, u32[]{:S(2)}, u32[]{:S(2)}) collective-permute-start(bf16[8,7168]{1,0:T(8,128)(2,1)S(1)} %add_convert_fusion.4), channel_id=1, source_target_pairs={{0,2},{1,3},{2,0},{3,1},{4,6},{5,7},{6,4},{7,5},{8,10},{9,11},{10,... | collective-permute-start | bytes 344072 | tf_op jit(solution)/shard_map/ppermute | solution.py:177
  45.0 5.2 %collective-permute-start.16 = (bf16[8,7168]{1,0:T(8,128)(2,1)S(1)}, bf16[8,7168]{1,0:T(8,128)(2,1)S(1)}, u32[]{:S(2)}, u32[]{:S(2)}) collective-permute-start(bf16[8,7168]{1,0:T(8,128)(2,1)S(1)} %add_convert_fusion.3), channel_id=1, source_target_pairs={{0,1},{1,0},{2,3},{3,2},{4,5},{5,4},{6,7},{7,6},{8,9},{9,8},{10,11... | collective-permute-start | bytes 344072 | tf_op jit(solution)/shard_map/ppermute | solution.py:177
  45.4 4.8 %collective-permute-start.17 = (bf16[8,7168]{1,0:T(8,128)(2,1)S(1)}, bf16[8,7168]{1,0:T(8,128)(2,1)S(1)}, u32[]{:S(2)}, u32[]{:S(2)}) collective-permute-start(bf16[8,7168]{1,0:T(8,128)(2,1)S(1)} %get-tuple-element.24), channel_id=1, source_target_pairs={{0,8},{4,12},{8,0},{12,4},{1,9},{5,13},{9,1},{13,5},{2,10},{6,14},... | collective-permute-start | bytes 344072 | tf_op jit(solution)/shard_map/ppermute | solution.py:173

commit v13 on v12

--- a/solution.py
+++ b/solution.py
@@ -10,7 +10,7 @@
 LANES = 128
 N_TILE = 256
 DOWN_TILE = 1792
-OUT_CHUNKS = 1
+OUT_CHUNKS = 2
 VMEM_LIMIT = 4 * 2**20
 
 
@@ -198,22 +198,45 @@
     return [early, late, to_core(early), to_core(late)]
 
 
+def sums_kernel(*refs):
+    inputs, outs = refs[: -PLACES], refs[-PLACES:]
+    chunks = len(inputs) // 2
+    rows, width = outs[0].shape
+    for chunk in range(chunks):
+        at = pl.ds(chunk * (width // chunks), width // chunks)
+        here, other = [ref[...].astype(jnp.float32) for ref in inputs[chunk::chunks]]
+        total = here + other
+        for place, ref in enumerate(outs):
+            ref[:, at] = total[place * rows : (place + 1) * rows].astype(ref.dtype)
+
+
+def sums(here, other):
+    rows, width = here[0].shape[0] // PLACES, here[0].shape[1] * len(here)
+    vmem = pl.BlockSpec(memory_space=pltpu.VMEM)
+    return pl.pallas_call(
+        sums_kernel,
+        out_shape=[jax.ShapeDtypeStruct((rows, width), here[0].dtype)] * PLACES,
+        in_specs=[vmem] * (2 * len(here)),
+        out_specs=[vmem] * PLACES,
+        compiler_params=pltpu.CompilerParams(vmem_limit_bytes=VMEM_LIMIT),
+        name="sums",
+    )(*here, *other)
+
+
 def total(*terms):
     return sum(term.astype(jnp.float32) for term in terms)
 
 
-def reduce_blocks(early, late, other_early, other_late, rows):
-    def blocks(here, other):
-        return total(here, other).astype(jnp.bfloat16).reshape(PLACES, rows, -1)
-
-    other_late = to_core(other_late)
-    other_early = to_core(after(other_early, other_late))
-    second, third, far_second, far_third = blocks(late, other_late)
+def reduce_blocks(chunks):
+    early, late, other_early, other_late = zip(*chunks)
+    other_late = [to_core(each) for each in other_late]
+    other_early = [to_core(after(each, *other_late)) for each in other_early]
+    second, third, far_second, far_third = sums(late, other_late)
     far_second = to_chip(far_second)
     far_third = to_both(far_third, 1)
     third = to_place(third, 1)
     second = total(second, far_second, far_third, third).astype(jnp.bfloat16)
-    own, far_own, first, far_first = blocks(early, other_early)
+    own, far_own, first, far_first = sums(early, other_early)
     first = total(first, to_chip(after(far_first, third))).astype(jnp.bfloat16)
     first, far_own = lax.optimization_barrier((first, far_own))
     second_here, first_here, far_own = to_place(second, 2), to_place(first, 1), to_chip(far_own)
@@ -221,14 +244,14 @@
 
 
 def by_permutes(tokens, expert_ids, route_weights, expert_slot, w_gate, w_up, w_down):
-    rows = tokens.shape[0]
     own = pack(tokens, expert_ids, route_weights, expert_slot, w_gate, w_up, w_down)
     hidden = hidden_units(gather_blocks(own), w_gate, w_up, expert_slot.shape[0])
     matrix = w_down.reshape(-1, w_down.shape[-1])
-    outs = []
+    chunks = []
     for chunk in range(OUT_CHUNKS):
-        outs.append(reduce_blocks(*down(hidden, matrix, chunk, OUT_CHUNKS), rows))
-    return jnp.concatenate(outs, axis=1)
+        chunks.append(down(hidden, matrix, chunk, OUT_CHUNKS))
+        hidden = after(hidden, chunks[-1][-1])
+    return reduce_blocks(chunks)
 
 
 def by_collectives(tokens, expert_ids, route_weights, expert_slot, w_gate, w_up, w_down):

time: 51.1 us -> 52.1 us (1.020)
  starting transfers between devices: 21.1 us -> 24 us
  waiting for transfers between devices: 19.6 us -> 17.8 us
    ppermute x6, starting transfers between devices: 9.27 us -> 11.3 us  [to_place(): return lax.ppermute(value, 'local', [(i, i ^ bits) for i in range(PLACES)])]
    ppermute x6, waiting for transfers between devices: 3.64 us -> 2.54 us  [to_chip(): return lax.ppermute(value, 'node', [(i, i ^ 2) for i in range(2 * CHIPS)])]
    ppermute x4 -> x6, starting transfers between devices: 0.45 us -> 1.29 us  [to_core(): return lax.ppermute(value, 'node', [(i, i ^ 1) for i in range(2 * CHIPS)])]
    ppermute x4 -> x6, waiting for transfers between devices: 3.52 us -> 2.93 us  [to_core(): return lax.ppermute(value, 'node', [(i, i ^ 1) for i in range(2 * CHIPS)])]
    pallas_call x1 -> x2, Pallas kernels: 2.69 us -> 2.68 us  [down(): pl.pallas_call(functools.partial(down_kernel, chunk), out_shape=[jax.Shap...]
  transfers between devices with their start and end apart: 18 -> 20, of which waited for: 13 -> 12; matrix products, arithmetic and copies ran while one was open for 1% -> 0% of each run, Pallas kernels for 0% -> 3%
where the time goes in v13:
time: 52.1 us; the launch traced here: 52 us
  starting transfers between devices  24 us (46%)
  waiting for transfers between devices  17.8 us (34%)
  Pallas kernels  9.24 us (18%)
  other arithmetic  0.8 us (2%)
    ppermute x6, starting transfers between devices, to_place(): return lax.ppermute(value, 'local', [(i, i ^ bits) for i in range(PLACES)])  11.3 us
    ppermute x6, waiting for transfers between devices, to_place(): return lax.ppermute(value, 'local', [(i, i ^ bits) for i in range(PLACES)])  9.18 us
    ppermute x6, starting transfers between devices, to_chip(): return lax.ppermute(value, 'node', [(i, i ^ 2) for i in range(2 * CHIPS)])  8.46 us
    pallas_call x1, Pallas kernels, hidden_units(): pl.pallas_call(functools.partial(hidden_kernel, experts), out_shape=jax.S...  5.04 us
    ppermute x2, waiting for transfers between devices, to_both(): return lax.ppermute(value, ('node', 'local'), perm)  3.12 us
    ppermute x6, waiting for transfers between devices, to_core(): return lax.ppermute(value, 'node', [(i, i ^ 1) for i in range(2 * CHIPS)])  2.93 us
    ppermute x2, starting transfers between devices, to_both(): return lax.ppermute(value, ('node', 'local'), perm)  2.91 us
    pallas_call x2, Pallas kernels, down(): pl.pallas_call(functools.partial(down_kernel, chunk), out_shape=[jax.Shap...  2.68 us
  transfers between devices with their start and end apart: 20, of which 12 were waited for; matrix products, arithmetic and copies ran while one was open for 0% of the time, Pallas kernels for 3%

profile of v13, /device:TPU:0, one launch (start us, length us, event | category | flops | bytes accessed | tf_op | source)
XLA Modules:
  0.0 52.0 jit_solution(14456691536667444138)
XLA Ops:
  0.0 0.0 copy-start
  0.0 0.0 copy-start.1
  0.0 1.2 %pack.1.refs_0_ = bf16[8,7296]{1,0:T(8,128)(2,1)S(1)} custom-call(bf16[8,7168]{1,0:T(8,128)(2,1)} %refs_0_.1, s32[4,8]{1,0:T(4,128)} %bitcast.7, f32[4,8]{1,0:T(4,128)} %bitcast.8, s32[8]{0:T(128)} %refs_3_.1, bf16[2,7168,512]{2,1,0:T(8,128)(2,1)} %refs_4_.3, bf16[2,7168,512]{2,1,0:T(8,128)(2,1)} %refs_5_.3, bf16[2,512,7168]{2,1,0:T(8,128)(2,1)} %refs_6_.1), custom_call_target="tpu_custom_call" | custom-call | tf_op jit(solution)/shard_map/pack/pallas_call | solution.py:50
  1.2 3.1 %collective-permute-start.1 = (bf16[8,7296]{1,0:T(8,128)(2,1)S(1)}, bf16[8,7296]{1,0:T(8,128)(2,1)S(1)}, u32[]{:S(2)}, u32[]{:S(2)}) collective-permute-start(bf16[8,7296]{1,0:T(8,128)(2,1)S(1)} %pack.1.refs_0_), channel_id=1, source_target_pairs={{0,1},{1,0},{2,3},{3,2},{4,5},{5,4},{6,7},{7,6},{8,9},{9,8},{10,11... | collective-permute-start | bytes 350216 | tf_op jit(solution)/shard_map/ppermute | solution.py:177
  4.3 2.6 %collective-permute-start.3 = (bf16[8,7296]{1,0:T(8,128)(2,1)S(1)}, bf16[8,7296]{1,0:T(8,128)(2,1)S(1)}, u32[]{:S(2)}, u32[]{:S(2)}) collective-permute-start(bf16[8,7296]{1,0:T(8,128)(2,1)S(1)} %pack.1.refs_0_), channel_id=1, source_target_pairs={{0,2},{1,3},{2,0},{3,1},{4,6},{5,7},{6,4},{7,5},{8,10},{9,11},{10,... | collective-permute-start | bytes 350216 | tf_op jit(solution)/shard_map/ppermute | solution.py:177
  6.8 1.5 %collective-permute-start = (bf16[8,7296]{1,0:T(8,128)(2,1)S(1)}, bf16[8,7296]{1,0:T(8,128)(2,1)S(1)}, u32[]{:S(2)}, u32[]{:S(2)}) collective-permute-start(bf16[8,7296]{1,0:T(8,128)(2,1)S(1)} %pack.1.refs_0_), channel_id=1, source_target_pairs={{0,8},{4,12},{8,0},{12,4},{1,9},{5,13},{9,1},{13,5},{2,10},{6,14},... | collective-permute-start | bytes 350216 | tf_op jit(solution)/shard_map/ppermute | solution.py:173
  8.3 0.3 collective-permute-done.1.refs_2_
  8.7 1.8 %collective-permute-start.2 = (bf16[8,7296]{1,0:T(8,128)(2,1)S(1)}, bf16[8,7296]{1,0:T(8,128)(2,1)S(1)}, u32[]{:S(2)}, u32[]{:S(2)}) collective-permute-start(bf16[8,7296]{1,0:T(8,128)(2,1)S(1)} %collective-permute-done.1.refs_2_), channel_id=1, source_target_pairs={{0,8},{4,12},{8,0},{12,4},{1,9},{5,13},{9,1},{13,5},{2,10},{6,14},... | collective-permute-start | bytes 350216 | tf_op jit(solution)/shard_map/ppermute | solution.py:173
  10.5 1.9 %collective-permute-done.3.refs_0_ = bf16[8,7296]{1,0:T(8,128)(2,1)S(1)} collective-permute-done((bf16[8,7296]{1,0:T(8,128)(2,1)S(1)}, bf16[8,7296]{1,0:T(8,128)(2,1)S(1)}, u32[]{:S(2)}, u32[]{:S(2)}) %collective-permute-start.3) | collective-permute-done | bytes 116768 | tf_op jit(solution)/shard_map/ppermute | solution.py:177
  12.4 0.1 collective-permute-done.refs_1_
  12.5 1.5 %collective-permute-start.5 = (bf16[8,7296]{1,0:T(8,128)(2,1)S(1)}, bf16[8,7296]{1,0:T(8,128)(2,1)S(1)}, u32[]{:S(2)}, u32[]{:S(2)}) collective-permute-start(bf16[8,7296]{1,0:T(8,128)(2,1)S(1)} %collective-permute-done.3.refs_0_), channel_id=1, source_target_pairs={{0,8},{4,12},{8,0},{12,4},{1,9},{5,13},{9,1},{13,5},{2,10},{6,14},... | collective-permute-start | bytes 350216 | tf_op jit(solution)/shard_map/ppermute | solution.py:173
  14.0 0.8 %collective-permute-start.4 = (bf16[8,7296]{1,0:T(8,128)(2,1)S(1)}, bf16[8,7296]{1,0:T(8,128)(2,1)S(1)}, u32[]{:S(2)}, u32[]{:S(2)}) collective-permute-start(bf16[8,7296]{1,0:T(8,128)(2,1)S(1)} %collective-permute-done.3.refs_0_), channel_id=1, source_target_pairs={{0,1},{1,0},{2,3},{3,2},{4,5},{5,4},{6,7},{7,6},{8,9},{9,8},{10,11... | collective-permute-start | bytes 350216 | tf_op jit(solution)/shard_map/ppermute | solution.py:177
  14.7 0.0 collective-permute-done.2.refs_3_
  14.7 1.2 %collective-permute-start.6 = (bf16[8,7296]{1,0:T(8,128)(2,1)S(1)}, bf16[8,7296]{1,0:T(8,128)(2,1)S(1)}, u32[]{:S(2)}, u32[]{:S(2)}) collective-permute-start(bf16[8,7296]{1,0:T(8,128)(2,1)S(1)} %collective-permute-done.3.refs_0_), channel_id=1, source_target_pairs={{0,9},{1,8},{2,11},{3,10},{4,13},{5,12},{6,15},{7,14},{8,1},{9,0},... | collective-permute-start | bytes 350216 | tf_op jit(solution)/shard_map/ppermute | solution.py:183
  16.0 0.1 stack.2.refs_0_
  16.0 0.1 collective-permute-start.7
  16.1 2.4 %collective-permute-done.5.refs_2_ = bf16[8,7296]{1,0:T(8,128)(2,1)S(1)} collective-permute-done((bf16[8,7296]{1,0:T(8,128)(2,1)S(1)}, bf16[8,7296]{1,0:T(8,128)(2,1)S(1)}, u32[]{:S(2)}, u32[]{:S(2)}) %collective-permute-start.5) | collective-permute-done | bytes 116768 | tf_op jit(solution)/shard_map/ppermute | solution.py:173
  18.5 0.2 collective-permute-done.4.refs_1_
  18.8 1.7 %collective-permute-done.6.refs_3_ = bf16[8,7296]{1,0:T(8,128)(2,1)S(1)} collective-permute-done((bf16[8,7296]{1,0:T(8,128)(2,1)S(1)}, bf16[8,7296]{1,0:T(8,128)(2,1)S(1)}, u32[]{:S(2)}, u32[]{:S(2)}) %collective-permute-start.6) | collective-permute-done | bytes 116768 | tf_op jit(solution)/shard_map/ppermute | solution.py:183
  20.5 0.0 slice-start
  20.5 0.1 stack.3.refs_1_
  20.5 0.0 slice-start.1
  20.5 0.0 slice-start.2
  20.6 0.0 slice-start.3
  20.6 0.1 collective-permute-start.8
  20.6 0.0 collective-permute-done.7.refs_2_
  20.7 1.8 %collective-permute-done.8.refs_3_ = bf16[32,7296]{1,0:T(8,128)(2,1)S(1)} collective-permute-done((bf16[32,7296]{1,0:T(8,128)(2,1)S(1)}, bf16[32,7296]{1,0:T(8,128)(2,1)S(1)}, u32[]{:S(2)}, u32[]{:S(2)}) %collective-permute-start.8) | collective-permute-done | bytes 466976 | tf_op jit(solution)/shard_map/ppermute | solution.py:169
  22.5 0.0 copy-done
  22.5 0.0 copy-done.1
  22.5 5.0 %hidden.1.hidden_ref = bf16[128,1024]{1,0:T(8,128)(2,1)S(1)} custom-call(bf16[32,7296]{1,0:T(8,128)(2,1)S(1)} %stack.2.refs_0_, bf16[32,7296]{1,0:T(8,128)(2,1)S(1)} %stack.3.refs_1_, bf16[32,7296]{1,0:T(8,128)(2,1)S(1)} %collective-permute-done.7.refs_2_, bf16[32,7296]{1,0:T(8,128)(2,1)S(1)} %collective-permute-done.8.refs_3_, ...), custom_call_target="tpu_custom_call" | custom-call | flops 3758096384 | bytes 29360128 | tf_op jit(solution)/shard_map/hidden/pallas_call | solution.py:113
  27.5 0.0 slice-done
  27.5 0.0 slice-done.1
  27.5 0.0 slice-done.2
  27.5 0.0 slice-done.3
  27.6 1.3 %down.2 = (bf16[32,3584]{1,0:T(8,128)(2,1)S(1)}, bf16[32,3584]{1,0:T(8,128)(2,1)S(1)}, bf16[32,3584]{1,0:T(8,128)(2,1)S(1)}, bf16[32,3584]{1,0:T(8,128)(2,1)S(1)}) custom-call(bf16[128,1024]{1,0:T(8,128)(2,1)S(1)} %hidden.1.hidden_ref, bf16[1024,7168]{1,0:T(8,128)(2,1)S(1)} %bitcast.5), custom_call_target="tpu_custom_call" | custom-call | flops 939524096 | bytes 7340032 | tf_op jit(solution)/shard_map/down/pallas_call | solution.py:150
  28.9 0.2 collective-permute-start.9
  29.1 1.3 %down.3 = (bf16[32,3584]{1,0:T(8,128)(2,1)S(1)}, bf16[32,3584]{1,0:T(8,128)(2,1)S(1)}, bf16[32,3584]{1,0:T(8,128)(2,1)S(1)}, bf16[32,3584]{1,0:T(8,128)(2,1)S(1)}) custom-call(bf16[128,1024]{1,0:T(8,128)(2,1)S(1)} %hidden.1.hidden_ref, bf16[1024,7168]{1,0:T(8,128)(2,1)S(1)} %bitcast.6), custom_call_target="tpu_custom_call" | custom-call | flops 939524096 | bytes 7340032 | tf_op jit(solution)/shard_map/down/pallas_call | solution.py:150
  30.4 0.5 collective-permute-start.10
  30.9 0.0 collective-permute-done.9.refs_2_
  30.9 1.1 %collective-permute-done.10.refs_3_ = bf16[32,3584]{1,0:T(8,128)(2,1)S(1)} collective-permute-done((bf16[32,3584]{1,0:T(8,128)(2,1)S(1)}, bf16[32,3584]{1,0:T(8,128)(2,1)S(1)}, u32[]{:S(2)}, u32[]{:S(2)}) %collective-permute-start.10) | collective-permute-done | bytes 229408 | tf_op jit(solution)/shard_map/ppermute | solution.py:169
  32.0 0.4 collective-permute-start.11
  32.4 0.1 collective-permute-start.12
  32.5 0.1 sums.3
  32.6 1.3 %collective-permute-start.15 = (bf16[8,7168]{1,0:T(8,128)(2,1)S(1)}, bf16[8,7168]{1,0:T(8,128)(2,1)S(1)}, u32[]{:S(2)}, u32[]{:S(2)}) collective-permute-start(bf16[8,7168]{1,0:T(8,128)(2,1)S(1)} %get-tuple-element.46), channel_id=1, source_target_pairs={{0,1},{1,0},{2,3},{3,2},{4,5},{5,4},{6,7},{7,6},{8,9},{9,8},{10,11... | collective-permute-start | bytes 344072 | tf_op jit(solution)/shard_map/ppermute | solution.py:177
  34.0 0.6 %collective-permute-start.13 = (bf16[8,7168]{1,0:T(8,128)(2,1)S(1)}, bf16[8,7168]{1,0:T(8,128)(2,1)S(1)}, u32[]{:S(2)}, u32[]{:S(2)}) collective-permute-start(bf16[8,7168]{1,0:T(8,128)(2,1)S(1)} %get-tuple-element.44), channel_id=1, source_target_pairs={{0,8},{4,12},{8,0},{12,4},{1,9},{5,13},{9,1},{13,5},{2,10},{6,14},... | collective-permute-start | bytes 344072 | tf_op jit(solution)/shard_map/ppermute | solution.py:173
  34.5 1.7 %collective-permute-start.14 = (bf16[8,7168]{1,0:T(8,128)(2,1)S(1)}, bf16[8,7168]{1,0:T(8,128)(2,1)S(1)}, u32[]{:S(2)}, u32[]{:S(2)}) collective-permute-start(bf16[8,7168]{1,0:T(8,128)(2,1)S(1)} %get-tuple-element.45), channel_id=1, source_target_pairs={{0,9},{1,8},{2,11},{3,10},{4,13},{5,12},{6,15},{7,14},{8,1},{9,0},... | collective-permute-start | bytes 344072 | tf_op jit(solution)/shard_map/ppermute | solution.py:183
  36.2 0.0 collective-permute-done.11.refs_2_
  36.2 0.0 collective-permute-done.12.refs_3_
  36.2 0.1 sums.2
  36.3 2.1 %collective-permute-done.15 = bf16[8,7168]{1,0:T(8,128)(2,1)S(1)} collective-permute-done((bf16[8,7168]{1,0:T(8,128)(2,1)S(1)}, bf16[8,7168]{1,0:T(8,128)(2,1)S(1)}, u32[]{:S(2)}, u32[]{:S(2)}) %collective-permute-start.15) | collective-permute-done | bytes 114720 | tf_op jit(solution)/shard_map/ppermute | solution.py:177
  38.4 2.0 %collective-permute-start.17 = (bf16[8,7168]{1,0:T(8,128)(2,1)S(1)}, bf16[8,7168]{1,0:T(8,128)(2,1)S(1)}, u32[]{:S(2)}, u32[]{:S(2)}) collective-permute-start(bf16[8,7168]{1,0:T(8,128)(2,1)S(1)} %get-tuple-element.49), channel_id=1, source_target_pairs={{0,8},{4,12},{8,0},{12,4},{1,9},{5,13},{9,1},{13,5},{2,10},{6,14},... | collective-permute-start | bytes 344072 | tf_op jit(solution)/shard_map/ppermute | solution.py:173
  40.4 0.0 collective-permute-done.13
  40.4 1.4 %collective-permute-done.14 = bf16[8,7168]{1,0:T(8,128)(2,1)S(1)} collective-permute-done((bf16[8,7168]{1,0:T(8,128)(2,1)S(1)}, bf16[8,7168]{1,0:T(8,128)(2,1)S(1)}, u32[]{:S(2)}, u32[]{:S(2)}) %collective-permute-start.14) | collective-permute-done | bytes 114720 | tf_op jit(solution)/shard_map/ppermute | solution.py:183
  41.8 0.1 add_convert_fusion.2
  41.9 2.3 %collective-permute-start.16 = (bf16[8,7168]{1,0:T(8,128)(2,1)S(1)}, bf16[8,7168]{1,0:T(8,128)(2,1)S(1)}, u32[]{:S(2)}, u32[]{:S(2)}) collective-permute-start(bf16[8,7168]{1,0:T(8,128)(2,1)S(1)} %add_convert_fusion.2), channel_id=1, source_target_pairs={{0,2},{1,3},{2,0},{3,1},{4,6},{5,7},{6,4},{7,5},{8,10},{9,11},{10,... | collective-permute-start | bytes 344072 | tf_op jit(solution)/shard_map/ppermute | solution.py:177
  44.2 0.0 collective-permute-done.17
  44.2 1.2 %collective-permute-start.18 = (bf16[8,7168]{1,0:T(8,128)(2,1)S(1)}, bf16[8,7168]{1,0:T(8,128)(2,1)S(1)}, u32[]{:S(2)}, u32[]{:S(2)}) collective-permute-start(bf16[8,7168]{1,0:T(8,128)(2,1)S(1)} %add_convert_fusion.1), channel_id=1, source_target_pairs={{0,1},{1,0},{2,3},{3,2},{4,5},{5,4},{6,7},{7,6},{8,9},{9,8},{10,11... | collective-permute-start | bytes 344072 | tf_op jit(solution)/shard_map/ppermute | solution.py:177
  45.5 1.1 %collective-permute-start.19 = (bf16[8,7168]{1,0:T(8,128)(2,1)S(1)}, bf16[8,7168]{1,0:T(8,128)(2,1)S(1)}, u32[]{:S(2)}, u32[]{:S(2)}) collective-permute-start(bf16[8,7168]{1,0:T(8,128)(2,1)S(1)} %get-tuple-element.52), channel_id=1, source_target_pairs={{0,8},{4,12},{8,0},{12,4},{1,9},{5,13},{9,1},{13,5},{2,10},{6,14},... | collective-permute-start | bytes 344072 | tf_op jit(solution)/shard_map/ppermute | solution.py:173
  46.6 3.3 %collective-permute-done.16 = bf16[8,7168]{1,0:T(8,128)(2,1)S(1)} collective-permute-done((bf16[8,7168]{1,0:T(8,128)(2,1)S(1)}, bf16[8,7168]{1,0:T(8,128)(2,1)S(1)}, u32[]{:S(2)}, u32[]{:S(2)}) %collective-permute-start.16) | collective-permute-done | bytes 114720 | tf_op jit(solution)/shard_map/ppermute | solution.py:177
  49.9 1.4 %collective-permute-done.18 = bf16[8,7168]{1,0:T(8,128)(2,1)S(1)} collective-permute-done((bf16[8,7168]{1,0:T(8,128)(2,1)S(1)}, bf16[8,7168]{1,0:T(8,128)(2,1)S(1)}, u32[]{:S(2)}, u32[]{:S(2)}) %collective-permute-start.18) | collective-permute-done | bytes 114720 | tf_op jit(solution)/shard_map/ppermute | solution.py:177
  51.3 0.0 collective-permute-done.19
  51.3 0.7 %add_convert_fusion = bf16[8,7168]{1,0:T(8,128)(2,1)} fusion(bf16[8,7168]{1,0:T(8,128)(2,1)S(1)} %collective-permute-done.19, bf16[8,7168]{1,0:T(8,128)(2,1)S(1)} %collective-permute-done.18, bf16[8,7168]{1,0:T(8,128)(2,1)S(1)} %collective-permute-done.16, bf16[8,7168]{1,0:T(8,128)(2,1)S(1)} %get-tuple-element.40), kind=kLoop, calls=%fused_computation | loop fusion | flops 458752 | bytes 573440 | tf_op jit(solution)/shard_map/convert_element_type | solution.py:243
  (2 shorter events, 0.0 us)
Async XLA Ops:
  0.0 22.5 %copy-start = (bf16[2,7168,512]{2,1,0:T(8,128)(2,1)S(1)}, bf16[2,7168,512]{2,1,0:T(8,128)(2,1)}, u32[]{:S(2)}) copy-start(bf16[2,7168,512]{2,1,0:T(8,128)(2,1)} %refs_4_.3) | copy-start | bytes 44040196
  0.0 22.5 %copy-start.1 = (bf16[2,7168,512]{2,1,0:T(8,128)(2,1)S(1)}, bf16[2,7168,512]{2,1,0:T(8,128)(2,1)}, u32[]{:S(2)}) copy-start(bf16[2,7168,512]{2,1,0:T(8,128)(2,1)} %refs_5_.3) | copy-start | bytes 44040196
  1.2 7.5 %collective-permute-start.1 = (bf16[8,7296]{1,0:T(8,128)(2,1)S(1)}, bf16[8,7296]{1,0:T(8,128)(2,1)S(1)}, u32[]{:S(2)}, u32[]{:S(2)}) collective-permute-start(bf16[8,7296]{1,0:T(8,128)(2,1)S(1)} %pack.1.refs_0_), channel_id=1, source_target_pairs={{0,1},{1,0},{2,3},{3,2},{4,5},{5,4},{6,7},{7,6},{8,9},{9,8},{10,11... | collective-permute-start | bytes 350216 | tf_op jit(solution)/shard_map/ppermute | solution.py:177
  4.3 8.1 %collective-permute-start.3 = (bf16[8,7296]{1,0:T(8,128)(2,1)S(1)}, bf16[8,7296]{1,0:T(8,128)(2,1)S(1)}, u32[]{:S(2)}, u32[]{:S(2)}) collective-permute-start(bf16[8,7296]{1,0:T(8,128)(2,1)S(1)} %pack.1.refs_0_), channel_id=1, source_target_pairs={{0,2},{1,3},{2,0},{3,1},{4,6},{5,7},{6,4},{7,5},{8,10},{9,11},{10,... | collective-permute-start | bytes 350216 | tf_op jit(solution)/shard_map/ppermute | solution.py:177
  6.8 5.6 %collective-permute-start = (bf16[8,7296]{1,0:T(8,128)(2,1)S(1)}, bf16[8,7296]{1,0:T(8,128)(2,1)S(1)}, u32[]{:S(2)}, u32[]{:S(2)}) collective-permute-start(bf16[8,7296]{1,0:T(8,128)(2,1)S(1)} %pack.1.refs_0_), channel_id=1, source_target_pairs={{0,8},{4,12},{8,0},{12,4},{1,9},{5,13},{9,1},{13,5},{2,10},{6,14},... | collective-permute-start | bytes 350216 | tf_op jit(solution)/shard_map/ppermute | solution.py:173
  8.7 6.1 %collective-permute-start.2 = (bf16[8,7296]{1,0:T(8,128)(2,1)S(1)}, bf16[8,7296]{1,0:T(8,128)(2,1)S(1)}, u32[]{:S(2)}, u32[]{:S(2)}) collective-permute-start(bf16[8,7296]{1,0:T(8,128)(2,1)S(1)} %collective-permute-done.1.refs_2_), channel_id=1, source_target_pairs={{0,8},{4,12},{8,0},{12,4},{1,9},{5,13},{9,1},{13,5},{2,10},{6,14},... | collective-permute-start | bytes 350216 | tf_op jit(solution)/shard_map/ppermute | solution.py:173
  12.5 6.1 %collective-permute-start.5 = (bf16[8,7296]{1,0:T(8,128)(2,1)S(1)}, bf16[8,7296]{1,0:T(8,128)(2,1)S(1)}, u32[]{:S(2)}, u32[]{:S(2)}) collective-permute-start(bf16[8,7296]{1,0:T(8,128)(2,1)S(1)} %collective-permute-done.3.refs_0_), channel_id=1, source_target_pairs={{0,8},{4,12},{8,0},{12,4},{1,9},{5,13},{9,1},{13,5},{2,10},{6,14},... | collective-permute-start | bytes 350216 | tf_op jit(solution)/shard_map/ppermute | solution.py:173
  14.0 4.8 %collective-permute-start.4 = (bf16[8,7296]{1,0:T(8,128)(2,1)S(1)}, bf16[8,7296]{1,0:T(8,128)(2,1)S(1)}, u32[]{:S(2)}, u32[]{:S(2)}) collective-permute-start(bf16[8,7296]{1,0:T(8,128)(2,1)S(1)} %collective-permute-done.3.refs_0_), channel_id=1, source_target_pairs={{0,1},{1,0},{2,3},{3,2},{4,5},{5,4},{6,7},{7,6},{8,9},{9,8},{10,11... | collective-permute-start | bytes 350216 | tf_op jit(solution)/shard_map/ppermute | solution.py:177
  14.7 5.7 %collective-permute-start.6 = (bf16[8,7296]{1,0:T(8,128)(2,1)S(1)}, bf16[8,7296]{1,0:T(8,128)(2,1)S(1)}, u32[]{:S(2)}, u32[]{:S(2)}) collective-permute-start(bf16[8,7296]{1,0:T(8,128)(2,1)S(1)} %collective-permute-done.3.refs_0_), channel_id=1, source_target_pairs={{0,9},{1,8},{2,11},{3,10},{4,13},{5,12},{6,15},{7,14},{8,1},{9,0},... | collective-permute-start | bytes 350216 | tf_op jit(solution)/shard_map/ppermute | solution.py:183
  16.0 4.6 %collective-permute-start.7 = (bf16[32,7296]{1,0:T(8,128)(2,1)S(1)}, bf16[32,7296]{1,0:T(8,128)(2,1)S(1)}, u32[]{:S(2)}, u32[]{:S(2)}) collective-permute-start(bf16[32,7296]{1,0:T(8,128)(2,1)S(1)} %stack.2.refs_0_), channel_id=1, source_target_pairs={{0,4},{4,0},{8,12},{12,8},{1,5},{5,1},{9,13},{13,9},{2,6},{6,2},{1... | collective-permute-start | bytes 1400840 | tf_op jit(solution)/shard_map/ppermute | solution.py:169
  20.5 7.1 %slice-start = ((s8[14680064]{0:T(1024)(128)(4,1)}), s8[4194304]{0:T(1024)(128)(4,1)S(1)}, s32[]{:S(2)}) async-start(s8[14680064]{0:T(1024)(128)(4,1)} %bitcast.3), calls=%async_computation | async-start | bytes 8388608
  20.5 7.0 %slice-start.1 = ((s8[14680064]{0:T(1024)(128)(4,1)}), s8[4194304]{0:T(1024)(128)(4,1)S(1)}, s32[]{:S(2)}) async-start(s8[14680064]{0:T(1024)(128)(4,1)} %bitcast.3), calls=%async_computation.1 | async-start | bytes 8388608
  20.5 7.0 %slice-start.2 = ((s8[14680064]{0:T(1024)(128)(4,1)}), s8[4194304]{0:T(1024)(128)(4,1)S(1)}, s32[]{:S(2)}) async-start(s8[14680064]{0:T(1024)(128)(4,1)} %bitcast.3), calls=%async_computation.2 | async-start | bytes 8388608
  20.6 7.0 %slice-start.3 = ((s8[14680064]{0:T(1024)(128)(4,1)}), s8[2097152]{0:T(1024)(128)(4,1)S(1)}, s32[]{:S(2)}) async-start(s8[14680064]{0:T(1024)(128)(4,1)} %bitcast.3), calls=%async_computation.3 | async-start | bytes 4194304
  20.6 1.9 %collective-permute-start.8 = (bf16[32,7296]{1,0:T(8,128)(2,1)S(1)}, bf16[32,7296]{1,0:T(8,128)(2,1)S(1)}, u32[]{:S(2)}, u32[]{:S(2)}) collective-permute-start(bf16[32,7296]{1,0:T(8,128)(2,1)S(1)} %stack.3.refs_1_), channel_id=1, source_target_pairs={{0,4},{4,0},{8,12},{12,8},{1,5},{5,1},{9,13},{13,9},{2,6},{6,2},{1... | collective-permute-start | bytes 1400840 | tf_op jit(solution)/shard_map/ppermute | solution.py:169
  28.9 2.0 %collective-permute-start.9 = (bf16[32,3584]{1,0:T(8,128)(2,1)S(1)}, bf16[32,3584]{1,0:T(8,128)(2,1)S(1)}, u32[]{:S(2)}, u32[]{:S(2)}) collective-permute-start(bf16[32,3584]{1,0:T(8,128)(2,1)S(1)} %get-tuple-element.32), channel_id=1, source_target_pairs={{0,4},{4,0},{8,12},{12,8},{1,5},{5,1},{9,13},{13,9},{2,6},{6,2},{1... | collective-permute-start | bytes 688136 | tf_op jit(solution)/shard_map/ppermute | solution.py:169
  30.4 1.6 %collective-permute-start.10 = (bf16[32,3584]{1,0:T(8,128)(2,1)S(1)}, bf16[32,3584]{1,0:T(8,128)(2,1)S(1)}, u32[]{:S(2)}, u32[]{:S(2)}) collective-permute-start(bf16[32,3584]{1,0:T(8,128)(2,1)S(1)} %get-tuple-element.36), channel_id=1, source_target_pairs={{0,4},{4,0},{8,12},{12,8},{1,5},{5,1},{9,13},{13,9},{2,6},{6,2},{1... | collective-permute-start | bytes 688136 | tf_op jit(solution)/shard_map/ppermute | solution.py:169
  32.0 4.2 %collective-permute-start.11 = (bf16[32,3584]{1,0:T(8,128)(2,1)S(1)}, bf16[32,3584]{1,0:T(8,128)(2,1)S(1)}, u32[]{:S(2)}, u32[]{:S(2)}) collective-permute-start(bf16[32,3584]{1,0:T(8,128)(2,1)S(1)} %get-tuple-element.37), channel_id=1, source_target_pairs={{0,4},{4,0},{8,12},{12,8},{1,5},{5,1},{9,13},{13,9},{2,6},{6,2},{1... | collective-permute-start | bytes 688136 | tf_op jit(solution)/shard_map/ppermute | solution.py:169
  32.4 3.8 %collective-permute-start.12 = (bf16[32,3584]{1,0:T(8,128)(2,1)S(1)}, bf16[32,3584]{1,0:T(8,128)(2,1)S(1)}, u32[]{:S(2)}, u32[]{:S(2)}) collective-permute-start(bf16[32,3584]{1,0:T(8,128)(2,1)S(1)} %get-tuple-element.39), channel_id=1, source_target_pairs={{0,4},{4,0},{8,12},{12,8},{1,5},{5,1},{9,13},{13,9},{2,6},{6,2},{1... | collective-permute-start | bytes 688136 | tf_op jit(solution)/shard_map/ppermute | solution.py:169
  32.6 5.7 %collective-permute-start.15 = (bf16[8,7168]{1,0:T(8,128)(2,1)S(1)}, bf16[8,7168]{1,0:T(8,128)(2,1)S(1)}, u32[]{:S(2)}, u32[]{:S(2)}) collective-permute-start(bf16[8,7168]{1,0:T(8,128)(2,1)S(1)} %get-tuple-element.46), channel_id=1, source_target_pairs={{0,1},{1,0},{2,3},{3,2},{4,5},{5,4},{6,7},{7,6},{8,9},{9,8},{10,11... | collective-permute-start | bytes 344072 | tf_op jit(solution)/shard_map/ppermute | solution.py:177
  34.0 6.4 %collective-permute-start.13 = (bf16[8,7168]{1,0:T(8,128)(2,1)S(1)}, bf16[8,7168]{1,0:T(8,128)(2,1)S(1)}, u32[]{:S(2)}, u32[]{:S(2)}) collective-permute-start(bf16[8,7168]{1,0:T(8,128)(2,1)S(1)} %get-tuple-element.44), channel_id=1, source_target_pairs={{0,8},{4,12},{8,0},{12,4},{1,9},{5,13},{9,1},{13,5},{2,10},{6,14},... | collective-permute-start | bytes 344072 | tf_op jit(solution)/shard_map/ppermute | solution.py:173
  34.5 7.3 %collective-permute-start.14 = (bf16[8,7168]{1,0:T(8,128)(2,1)S(1)}, bf16[8,7168]{1,0:T(8,128)(2,1)S(1)}, u32[]{:S(2)}, u32[]{:S(2)}) collective-permute-start(bf16[8,7168]{1,0:T(8,128)(2,1)S(1)} %get-tuple-element.45), channel_id=1, source_target_pairs={{0,9},{1,8},{2,11},{3,10},{4,13},{5,12},{6,15},{7,14},{8,1},{9,0},... | collective-permute-start | bytes 344072 | tf_op jit(solution)/shard_map/ppermute | solution.py:183
  38.4 5.8 %collective-permute-start.17 = (bf16[8,7168]{1,0:T(8,128)(2,1)S(1)}, bf16[8,7168]{1,0:T(8,128)(2,1)S(1)}, u32[]{:S(2)}, u32[]{:S(2)}) collective-permute-start(bf16[8,7168]{1,0:T(8,128)(2,1)S(1)} %get-tuple-element.49), channel_id=1, source_target_pairs={{0,8},{4,12},{8,0},{12,4},{1,9},{5,13},{9,1},{13,5},{2,10},{6,14},... | collective-permute-start | bytes 344072 | tf_op jit(solution)/shard_map/ppermute | solution.py:173
  41.9 8.0 %collective-permute-start.16 = (bf16[8,7168]{1,0:T(8,128)(2,1)S(1)}, bf16[8,7168]{1,0:T(8,128)(2,1)S(1)}, u32[]{:S(2)}, u32[]{:S(2)}) collective-permute-start(bf16[8,7168]{1,0:T(8,128)(2,1)S(1)} %add_convert_fusion.2), channel_id=1, source_target_pairs={{0,2},{1,3},{2,0},{3,1},{4,6},{5,7},{6,4},{7,5},{8,10},{9,11},{10,... | collective-permute-start | bytes 344072 | tf_op jit(solution)/shard_map/ppermute | solution.py:177
  44.2 7.0 %collective-permute-start.18 = (bf16[8,7168]{1,0:T(8,128)(2,1)S(1)}, bf16[8,7168]{1,0:T(8,128)(2,1)S(1)}, u32[]{:S(2)}, u32[]{:S(2)}) collective-permute-start(bf16[8,7168]{1,0:T(8,128)(2,1)S(1)} %add_convert_fusion.1), channel_id=1, source_target_pairs={{0,1},{1,0},{2,3},{3,2},{4,5},{5,4},{6,7},{7,6},{8,9},{9,8},{10,11... | collective-permute-start | bytes 344072 | tf_op jit(solution)/shard_map/ppermute | solution.py:177
  45.5 5.8 %collective-permute-start.19 = (bf16[8,7168]{1,0:T(8,128)(2,1)S(1)}, bf16[8,7168]{1,0:T(8,128)(2,1)S(1)}, u32[]{:S(2)}, u32[]{:S(2)}) collective-permute-start(bf16[8,7168]{1,0:T(8,128)(2,1)S(1)} %get-tuple-element.52), channel_id=1, source_target_pairs={{0,8},{4,12},{8,0},{12,4},{1,9},{5,13},{9,1},{13,5},{2,10},{6,14},... | collective-permute-start | bytes 344072 | tf_op jit(solution)/shard_map/ppermute | solution.py:173

commit v14 on v13

--- a/solution.py
+++ b/solution.py
@@ -10,7 +10,7 @@
 LANES = 128
 N_TILE = 256
 DOWN_TILE = 1792
-OUT_CHUNKS = 2
+OUT_CHUNKS = 1
 VMEM_LIMIT = 4 * 2**20
 
 
@@ -93,7 +93,7 @@
         weight_ref[member] = jnp.sum(jnp.where(mine, tail, 0.0), axis=1, keepdims=True)
     tiles = hid // N_TILE
 
-    @pl.loop(0, members * tiles)
+    @pl.loop(0, members * tiles, unroll=True)
     def _(step):
         member = step // tiles
         at = pl.ds(pl.multiple_of(lax.rem(step, tiles) * N_TILE, N_TILE), N_TILE)
@@ -132,7 +132,7 @@
 def down_kernel(chunk, hidden_ref, down_ref, *outs):
     part, width = outs[0].shape
 
-    @pl.loop(0, width // DOWN_TILE)
+    @pl.loop(0, width // DOWN_TILE, unroll=True)
     def _(step):
         at = pl.ds(pl.multiple_of(step * DOWN_TILE, DOWN_TILE), DOWN_TILE)
         there = pl.ds(pl.multiple_of(chunk * width + step * DOWN_TILE, DOWN_TILE), DOWN_TILE)

time: 52.1 us -> 50.4 us (0.967)
  Pallas kernels: 9.24 us -> 7.65 us
  starting transfers between devices: 24 us -> 23.2 us
  waiting for transfers between devices: 17.8 us -> 18.4 us
    pallas_call x1, Pallas kernels: 5.04 us -> 4.05 us  [hidden_units(): pl.pallas_call(functools.partial(hidden_kernel, experts), out_shape=jax.S...]
    ppermute x6 -> x4, starting transfers between devices: 1.29 us -> 0.47 us  [to_core(): return lax.ppermute(value, 'node', [(i, i ^ 1) for i in range(2 * CHIPS)])]
    pallas_call x2 -> x1, Pallas kernels: 2.68 us -> 2.08 us  [down(): pl.pallas_call(functools.partial(down_kernel, chunk), out_shape=[jax.Shap...]
    ppermute x6 -> x4, waiting for transfers between devices: 2.93 us -> 3.5 us  [to_core(): return lax.ppermute(value, 'node', [(i, i ^ 1) for i in range(2 * CHIPS)])]
  transfers between devices with their start and end apart: 20 -> 18, of which waited for: 12 -> 12; matrix products, arithmetic and copies ran while one was open for 0% -> 0% of each run, Pallas kernels for 3% -> 1%
where the time goes in v14:
time: 50.4 us; the launch traced here: 50.2 us
  starting transfers between devices  23.2 us (46%)
  waiting for transfers between devices  18.4 us (37%)
  Pallas kernels  7.65 us (15%)
  other arithmetic  0.8 us (2%)
    ppermute x6, starting transfers between devices, to_place(): return lax.ppermute(value, 'local', [(i, i ^ bits) for i in range(PLACES)])  11.3 us
    ppermute x6, waiting for transfers between devices, to_place(): return lax.ppermute(value, 'local', [(i, i ^ bits) for i in range(PLACES)])  9.23 us
    ppermute x6, starting transfers between devices, to_chip(): return lax.ppermute(value, 'node', [(i, i ^ 2) for i in range(2 * CHIPS)])  8.5 us
    pallas_call x1, Pallas kernels, hidden_units(): pl.pallas_call(functools.partial(hidden_kernel, experts), out_shape=jax.S...  4.05 us
    ppermute x4, waiting for transfers between devices, to_core(): return lax.ppermute(value, 'node', [(i, i ^ 1) for i in range(2 * CHIPS)])  3.5 us
    ppermute x2, waiting for transfers between devices, to_both(): return lax.ppermute(value, ('node', 'local'), perm)  3.12 us
    ppermute x2, starting transfers between devices, to_both(): return lax.ppermute(value, ('node', 'local'), perm)  2.89 us
    ppermute x6, waiting for transfers between devices, to_chip(): return lax.ppermute(value, 'node', [(i, i ^ 2) for i in range(2 * CHIPS)])  2.54 us
  transfers between devices with their start and end apart: 18, of which 12 were waited for; matrix products, arithmetic and copies ran while one was open for 0% of the time, Pallas kernels for 1%

profile of v14, /device:TPU:0, one launch (start us, length us, event | category | flops | bytes accessed | tf_op | source)
XLA Modules:
  0.0 50.2 jit_solution(15384373485137995992)
XLA Ops:
  0.0 0.0 copy-start
  0.0 0.0 copy-start.1
  0.0 1.2 %pack.1.refs_0_ = bf16[8,7296]{1,0:T(8,128)(2,1)S(1)} custom-call(bf16[8,7168]{1,0:T(8,128)(2,1)} %refs_0_.1, s32[4,8]{1,0:T(4,128)} %bitcast.6, f32[4,8]{1,0:T(4,128)} %bitcast.7, s32[8]{0:T(128)} %refs_3_.1, bf16[2,7168,512]{2,1,0:T(8,128)(2,1)} %refs_4_.3, bf16[2,7168,512]{2,1,0:T(8,128)(2,1)} %refs_5_.3, bf16[2,512,7168]{2,1,0:T(8,128)(2,1)} %refs_6_.1), custom_call_target="tpu_custom_call" | custom-call | tf_op jit(solution)/shard_map/pack/pallas_call | solution.py:50
  1.2 3.1 %collective-permute-start.1 = (bf16[8,7296]{1,0:T(8,128)(2,1)S(1)}, bf16[8,7296]{1,0:T(8,128)(2,1)S(1)}, u32[]{:S(2)}, u32[]{:S(2)}) collective-permute-start(bf16[8,7296]{1,0:T(8,128)(2,1)S(1)} %pack.1.refs_0_), channel_id=1, source_target_pairs={{0,1},{1,0},{2,3},{3,2},{4,5},{5,4},{6,7},{7,6},{8,9},{9,8},{10,11... | collective-permute-start | bytes 350216 | tf_op jit(solution)/shard_map/ppermute | solution.py:177
  4.3 2.6 %collective-permute-start.3 = (bf16[8,7296]{1,0:T(8,128)(2,1)S(1)}, bf16[8,7296]{1,0:T(8,128)(2,1)S(1)}, u32[]{:S(2)}, u32[]{:S(2)}) collective-permute-start(bf16[8,7296]{1,0:T(8,128)(2,1)S(1)} %pack.1.refs_0_), channel_id=1, source_target_pairs={{0,2},{1,3},{2,0},{3,1},{4,6},{5,7},{6,4},{7,5},{8,10},{9,11},{10,... | collective-permute-start | bytes 350216 | tf_op jit(solution)/shard_map/ppermute | solution.py:177
  6.8 1.5 %collective-permute-start = (bf16[8,7296]{1,0:T(8,128)(2,1)S(1)}, bf16[8,7296]{1,0:T(8,128)(2,1)S(1)}, u32[]{:S(2)}, u32[]{:S(2)}) collective-permute-start(bf16[8,7296]{1,0:T(8,128)(2,1)S(1)} %pack.1.refs_0_), channel_id=1, source_target_pairs={{0,8},{4,12},{8,0},{12,4},{1,9},{5,13},{9,1},{13,5},{2,10},{6,14},... | collective-permute-start | bytes 350216 | tf_op jit(solution)/shard_map/ppermute | solution.py:173
  8.3 0.3 collective-permute-done.1.refs_2_
  8.7 1.8 %collective-permute-start.2 = (bf16[8,7296]{1,0:T(8,128)(2,1)S(1)}, bf16[8,7296]{1,0:T(8,128)(2,1)S(1)}, u32[]{:S(2)}, u32[]{:S(2)}) collective-permute-start(bf16[8,7296]{1,0:T(8,128)(2,1)S(1)} %collective-permute-done.1.refs_2_), channel_id=1, source_target_pairs={{0,8},{4,12},{8,0},{12,4},{1,9},{5,13},{9,1},{13,5},{2,10},{6,14},... | collective-permute-start | bytes 350216 | tf_op jit(solution)/shard_map/ppermute | solution.py:173
  10.5 1.9 %collective-permute-done.3.refs_0_ = bf16[8,7296]{1,0:T(8,128)(2,1)S(1)} collective-permute-done((bf16[8,7296]{1,0:T(8,128)(2,1)S(1)}, bf16[8,7296]{1,0:T(8,128)(2,1)S(1)}, u32[]{:S(2)}, u32[]{:S(2)}) %collective-permute-start.3) | collective-permute-done | bytes 116768 | tf_op jit(solution)/shard_map/ppermute | solution.py:177
  12.4 0.1 collective-permute-done.refs_1_
  12.5 1.5 %collective-permute-start.5 = (bf16[8,7296]{1,0:T(8,128)(2,1)S(1)}, bf16[8,7296]{1,0:T(8,128)(2,1)S(1)}, u32[]{:S(2)}, u32[]{:S(2)}) collective-permute-start(bf16[8,7296]{1,0:T(8,128)(2,1)S(1)} %collective-permute-done.3.refs_0_), channel_id=1, source_target_pairs={{0,8},{4,12},{8,0},{12,4},{1,9},{5,13},{9,1},{13,5},{2,10},{6,14},... | collective-permute-start | bytes 350216 | tf_op jit(solution)/shard_map/ppermute | solution.py:173
  14.0 0.8 %collective-permute-start.4 = (bf16[8,7296]{1,0:T(8,128)(2,1)S(1)}, bf16[8,7296]{1,0:T(8,128)(2,1)S(1)}, u32[]{:S(2)}, u32[]{:S(2)}) collective-permute-start(bf16[8,7296]{1,0:T(8,128)(2,1)S(1)} %collective-permute-done.3.refs_0_), channel_id=1, source_target_pairs={{0,1},{1,0},{2,3},{3,2},{4,5},{5,4},{6,7},{7,6},{8,9},{9,8},{10,11... | collective-permute-start | bytes 350216 | tf_op jit(solution)/shard_map/ppermute | solution.py:177
  14.7 0.0 collective-permute-done.2.refs_3_
  14.7 1.2 %collective-permute-start.6 = (bf16[8,7296]{1,0:T(8,128)(2,1)S(1)}, bf16[8,7296]{1,0:T(8,128)(2,1)S(1)}, u32[]{:S(2)}, u32[]{:S(2)}) collective-permute-start(bf16[8,7296]{1,0:T(8,128)(2,1)S(1)} %collective-permute-done.3.refs_0_), channel_id=1, source_target_pairs={{0,9},{1,8},{2,11},{3,10},{4,13},{5,12},{6,15},{7,14},{8,1},{9,0},... | collective-permute-start | bytes 350216 | tf_op jit(solution)/shard_map/ppermute | solution.py:183
  16.0 0.1 stack.2.refs_0_
  16.0 0.1 collective-permute-start.7
  16.1 2.4 %collective-permute-done.5.refs_2_ = bf16[8,7296]{1,0:T(8,128)(2,1)S(1)} collective-permute-done((bf16[8,7296]{1,0:T(8,128)(2,1)S(1)}, bf16[8,7296]{1,0:T(8,128)(2,1)S(1)}, u32[]{:S(2)}, u32[]{:S(2)}) %collective-permute-start.5) | collective-permute-done | bytes 116768 | tf_op jit(solution)/shard_map/ppermute | solution.py:173
  18.5 0.2 collective-permute-done.4.refs_1_
  18.8 1.7 %collective-permute-done.6.refs_3_ = bf16[8,7296]{1,0:T(8,128)(2,1)S(1)} collective-permute-done((bf16[8,7296]{1,0:T(8,128)(2,1)S(1)}, bf16[8,7296]{1,0:T(8,128)(2,1)S(1)}, u32[]{:S(2)}, u32[]{:S(2)}) %collective-permute-start.6) | collective-permute-done | bytes 116768 | tf_op jit(solution)/shard_map/ppermute | solution.py:183
  20.5 0.0 slice-start
  20.5 0.1 stack.3.refs_1_
  20.5 0.0 slice-start.1
  20.5 0.0 slice-start.2
  20.6 0.0 slice-start.3
  20.6 0.1 collective-permute-start.8
  20.6 0.0 collective-permute-done.7.refs_2_
  20.7 1.8 %collective-permute-done.8.refs_3_ = bf16[32,7296]{1,0:T(8,128)(2,1)S(1)} collective-permute-done((bf16[32,7296]{1,0:T(8,128)(2,1)S(1)}, bf16[32,7296]{1,0:T(8,128)(2,1)S(1)}, u32[]{:S(2)}, u32[]{:S(2)}) %collective-permute-start.8) | collective-permute-done | bytes 466976 | tf_op jit(solution)/shard_map/ppermute | solution.py:169
  22.5 0.0 copy-done
  22.5 0.0 copy-done.1
  22.5 4.0 %hidden.1.hidden_ref = bf16[128,1024]{1,0:T(8,128)(2,1)S(1)} custom-call(bf16[32,7296]{1,0:T(8,128)(2,1)S(1)} %stack.2.refs_0_, bf16[32,7296]{1,0:T(8,128)(2,1)S(1)} %stack.3.refs_1_, bf16[32,7296]{1,0:T(8,128)(2,1)S(1)} %collective-permute-done.7.refs_2_, bf16[32,7296]{1,0:T(8,128)(2,1)S(1)} %collective-permute-done.8.refs_3_, ...), custom_call_target="tpu_custom_call" | custom-call | flops 3758096384 | bytes 29360128 | tf_op jit(solution)/shard_map/hidden/pallas_call | solution.py:113
  26.5 0.0 slice-done
  26.5 0.0 slice-done.1
  26.5 0.0 slice-done.2
  26.6 0.0 slice-done.3
  26.6 2.1 %down.1 = (bf16[32,7168]{1,0:T(8,128)(2,1)S(1)}, bf16[32,7168]{1,0:T(8,128)(2,1)S(1)}, bf16[32,7168]{1,0:T(8,128)(2,1)S(1)}, bf16[32,7168]{1,0:T(8,128)(2,1)S(1)}) custom-call(bf16[128,1024]{1,0:T(8,128)(2,1)S(1)} %hidden.1.hidden_ref, bf16[1024,7168]{1,0:T(8,128)(2,1)S(1)} %bitcast.5), custom_call_target="tpu_custom_call" | custom-call | flops 1879048192 | bytes 14680064 | tf_op jit(solution)/shard_map/down/pallas_call | solution.py:150
  28.7 0.2 collective-permute-start.9
  28.9 1.7 %collective-permute-done.9.refs_1_ = bf16[32,7168]{1,0:T(8,128)(2,1)S(1)} collective-permute-done((bf16[32,7168]{1,0:T(8,128)(2,1)S(1)}, bf16[32,7168]{1,0:T(8,128)(2,1)S(1)}, u32[]{:S(2)}, u32[]{:S(2)}) %collective-permute-start.9) | collective-permute-done | bytes 458784 | tf_op jit(solution)/shard_map/ppermute | solution.py:169
  30.5 0.1 collective-permute-start.10
  30.7 0.1 sums.3
  30.8 1.3 %collective-permute-start.13 = (bf16[8,7168]{1,0:T(8,128)(2,1)S(1)}, bf16[8,7168]{1,0:T(8,128)(2,1)S(1)}, u32[]{:S(2)}, u32[]{:S(2)}) collective-permute-start(bf16[8,7168]{1,0:T(8,128)(2,1)S(1)} %get-tuple-element.34), channel_id=1, source_target_pairs={{0,1},{1,0},{2,3},{3,2},{4,5},{5,4},{6,7},{7,6},{8,9},{9,8},{10,11... | collective-permute-start | bytes 344072 | tf_op jit(solution)/shard_map/ppermute | solution.py:177
  32.1 0.6 %collective-permute-start.11 = (bf16[8,7168]{1,0:T(8,128)(2,1)S(1)}, bf16[8,7168]{1,0:T(8,128)(2,1)S(1)}, u32[]{:S(2)}, u32[]{:S(2)}) collective-permute-start(bf16[8,7168]{1,0:T(8,128)(2,1)S(1)} %get-tuple-element.32), channel_id=1, source_target_pairs={{0,8},{4,12},{8,0},{12,4},{1,9},{5,13},{9,1},{13,5},{2,10},{6,14},... | collective-permute-start | bytes 344072 | tf_op jit(solution)/shard_map/ppermute | solution.py:173
  32.7 1.7 %collective-permute-start.12 = (bf16[8,7168]{1,0:T(8,128)(2,1)S(1)}, bf16[8,7168]{1,0:T(8,128)(2,1)S(1)}, u32[]{:S(2)}, u32[]{:S(2)}) collective-permute-start(bf16[8,7168]{1,0:T(8,128)(2,1)S(1)} %get-tuple-element.33), channel_id=1, source_target_pairs={{0,9},{1,8},{2,11},{3,10},{4,13},{5,12},{6,15},{7,14},{8,1},{9,0},... | collective-permute-start | bytes 344072 | tf_op jit(solution)/shard_map/ppermute | solution.py:183
  34.4 0.0 collective-permute-done.10.refs_1_
  34.4 0.1 sums.2
  34.5 2.0 %collective-permute-done.13 = bf16[8,7168]{1,0:T(8,128)(2,1)S(1)} collective-permute-done((bf16[8,7168]{1,0:T(8,128)(2,1)S(1)}, bf16[8,7168]{1,0:T(8,128)(2,1)S(1)}, u32[]{:S(2)}, u32[]{:S(2)}) %collective-permute-start.13) | collective-permute-done | bytes 114720 | tf_op jit(solution)/shard_map/ppermute | solution.py:177
  36.5 2.0 %collective-permute-start.15 = (bf16[8,7168]{1,0:T(8,128)(2,1)S(1)}, bf16[8,7168]{1,0:T(8,128)(2,1)S(1)}, u32[]{:S(2)}, u32[]{:S(2)}) collective-permute-start(bf16[8,7168]{1,0:T(8,128)(2,1)S(1)} %get-tuple-element.37), channel_id=1, source_target_pairs={{0,8},{4,12},{8,0},{12,4},{1,9},{5,13},{9,1},{13,5},{2,10},{6,14},... | collective-permute-start | bytes 344072 | tf_op jit(solution)/shard_map/ppermute | solution.py:173
  38.5 0.0 collective-permute-done.11
  38.5 1.4 %collective-permute-done.12 = bf16[8,7168]{1,0:T(8,128)(2,1)S(1)} collective-permute-done((bf16[8,7168]{1,0:T(8,128)(2,1)S(1)}, bf16[8,7168]{1,0:T(8,128)(2,1)S(1)}, u32[]{:S(2)}, u32[]{:S(2)}) %collective-permute-start.12) | collective-permute-done | bytes 114720 | tf_op jit(solution)/shard_map/ppermute | solution.py:183
  40.0 0.1 add_convert_fusion.2
  40.0 2.3 %collective-permute-start.14 = (bf16[8,7168]{1,0:T(8,128)(2,1)S(1)}, bf16[8,7168]{1,0:T(8,128)(2,1)S(1)}, u32[]{:S(2)}, u32[]{:S(2)}) collective-permute-start(bf16[8,7168]{1,0:T(8,128)(2,1)S(1)} %add_convert_fusion.2), channel_id=1, source_target_pairs={{0,2},{1,3},{2,0},{3,1},{4,6},{5,7},{6,4},{7,5},{8,10},{9,11},{10,... | collective-permute-start | bytes 344072 | tf_op jit(solution)/shard_map/ppermute | solution.py:177
  42.4 0.0 collective-permute-done.15
  42.4 1.2 %collective-permute-start.16 = (bf16[8,7168]{1,0:T(8,128)(2,1)S(1)}, bf16[8,7168]{1,0:T(8,128)(2,1)S(1)}, u32[]{:S(2)}, u32[]{:S(2)}) collective-permute-start(bf16[8,7168]{1,0:T(8,128)(2,1)S(1)} %add_convert_fusion.1), channel_id=1, source_target_pairs={{0,1},{1,0},{2,3},{3,2},{4,5},{5,4},{6,7},{7,6},{8,9},{9,8},{10,11... | collective-permute-start | bytes 344072 | tf_op jit(solution)/shard_map/ppermute | solution.py:177
  43.6 1.1 %collective-permute-start.17 = (bf16[8,7168]{1,0:T(8,128)(2,1)S(1)}, bf16[8,7168]{1,0:T(8,128)(2,1)S(1)}, u32[]{:S(2)}, u32[]{:S(2)}) collective-permute-start(bf16[8,7168]{1,0:T(8,128)(2,1)S(1)} %get-tuple-element.40), channel_id=1, source_target_pairs={{0,8},{4,12},{8,0},{12,4},{1,9},{5,13},{9,1},{13,5},{2,10},{6,14},... | collective-permute-start | bytes 344072 | tf_op jit(solution)/shard_map/ppermute | solution.py:173
  44.8 3.3 %collective-permute-done.14 = bf16[8,7168]{1,0:T(8,128)(2,1)S(1)} collective-permute-done((bf16[8,7168]{1,0:T(8,128)(2,1)S(1)}, bf16[8,7168]{1,0:T(8,128)(2,1)S(1)}, u32[]{:S(2)}, u32[]{:S(2)}) %collective-permute-start.14) | collective-permute-done | bytes 114720 | tf_op jit(solution)/shard_map/ppermute | solution.py:177
  48.1 1.4 %collective-permute-done.16 = bf16[8,7168]{1,0:T(8,128)(2,1)S(1)} collective-permute-done((bf16[8,7168]{1,0:T(8,128)(2,1)S(1)}, bf16[8,7168]{1,0:T(8,128)(2,1)S(1)}, u32[]{:S(2)}, u32[]{:S(2)}) %collective-permute-start.16) | collective-permute-done | bytes 114720 | tf_op jit(solution)/shard_map/ppermute | solution.py:177
  49.5 0.0 collective-permute-done.17
  49.5 0.7 %add_convert_fusion = bf16[8,7168]{1,0:T(8,128)(2,1)} fusion(bf16[8,7168]{1,0:T(8,128)(2,1)S(1)} %collective-permute-done.17, bf16[8,7168]{1,0:T(8,128)(2,1)S(1)} %collective-permute-done.16, bf16[8,7168]{1,0:T(8,128)(2,1)S(1)} %collective-permute-done.14, bf16[8,7168]{1,0:T(8,128)(2,1)S(1)} %get-tuple-element.29), kind=kLoop, calls=%fused_computation | loop fusion | flops 458752 | bytes 573440 | tf_op jit(solution)/shard_map/convert_element_type | solution.py:243
  (2 shorter events, 0.0 us)
Async XLA Ops:
  0.0 22.5 %copy-start = (bf16[2,7168,512]{2,1,0:T(8,128)(2,1)S(1)}, bf16[2,7168,512]{2,1,0:T(8,128)(2,1)}, u32[]{:S(2)}) copy-start(bf16[2,7168,512]{2,1,0:T(8,128)(2,1)} %refs_4_.3) | copy-start | bytes 44040196
  0.0 22.5 %copy-start.1 = (bf16[2,7168,512]{2,1,0:T(8,128)(2,1)S(1)}, bf16[2,7168,512]{2,1,0:T(8,128)(2,1)}, u32[]{:S(2)}) copy-start(bf16[2,7168,512]{2,1,0:T(8,128)(2,1)} %refs_5_.3) | copy-start | bytes 44040196
  1.2 7.5 %collective-permute-start.1 = (bf16[8,7296]{1,0:T(8,128)(2,1)S(1)}, bf16[8,7296]{1,0:T(8,128)(2,1)S(1)}, u32[]{:S(2)}, u32[]{:S(2)}) collective-permute-start(bf16[8,7296]{1,0:T(8,128)(2,1)S(1)} %pack.1.refs_0_), channel_id=1, source_target_pairs={{0,1},{1,0},{2,3},{3,2},{4,5},{5,4},{6,7},{7,6},{8,9},{9,8},{10,11... | collective-permute-start | bytes 350216 | tf_op jit(solution)/shard_map/ppermute | solution.py:177
  4.3 8.1 %collective-permute-start.3 = (bf16[8,7296]{1,0:T(8,128)(2,1)S(1)}, bf16[8,7296]{1,0:T(8,128)(2,1)S(1)}, u32[]{:S(2)}, u32[]{:S(2)}) collective-permute-start(bf16[8,7296]{1,0:T(8,128)(2,1)S(1)} %pack.1.refs_0_), channel_id=1, source_target_pairs={{0,2},{1,3},{2,0},{3,1},{4,6},{5,7},{6,4},{7,5},{8,10},{9,11},{10,... | collective-permute-start | bytes 350216 | tf_op jit(solution)/shard_map/ppermute | solution.py:177
  6.8 5.6 %collective-permute-start = (bf16[8,7296]{1,0:T(8,128)(2,1)S(1)}, bf16[8,7296]{1,0:T(8,128)(2,1)S(1)}, u32[]{:S(2)}, u32[]{:S(2)}) collective-permute-start(bf16[8,7296]{1,0:T(8,128)(2,1)S(1)} %pack.1.refs_0_), channel_id=1, source_target_pairs={{0,8},{4,12},{8,0},{12,4},{1,9},{5,13},{9,1},{13,5},{2,10},{6,14},... | collective-permute-start | bytes 350216 | tf_op jit(solution)/shard_map/ppermute | solution.py:173
  8.7 6.1 %collective-permute-start.2 = (bf16[8,7296]{1,0:T(8,128)(2,1)S(1)}, bf16[8,7296]{1,0:T(8,128)(2,1)S(1)}, u32[]{:S(2)}, u32[]{:S(2)}) collective-permute-start(bf16[8,7296]{1,0:T(8,128)(2,1)S(1)} %collective-permute-done.1.refs_2_), channel_id=1, source_target_pairs={{0,8},{4,12},{8,0},{12,4},{1,9},{5,13},{9,1},{13,5},{2,10},{6,14},... | collective-permute-start | bytes 350216 | tf_op jit(solution)/shard_map/ppermute | solution.py:173
  12.5 6.1 %collective-permute-start.5 = (bf16[8,7296]{1,0:T(8,128)(2,1)S(1)}, bf16[8,7296]{1,0:T(8,128)(2,1)S(1)}, u32[]{:S(2)}, u32[]{:S(2)}) collective-permute-start(bf16[8,7296]{1,0:T(8,128)(2,1)S(1)} %collective-permute-done.3.refs_0_), channel_id=1, source_target_pairs={{0,8},{4,12},{8,0},{12,4},{1,9},{5,13},{9,1},{13,5},{2,10},{6,14},... | collective-permute-start | bytes 350216 | tf_op jit(solution)/shard_map/ppermute | solution.py:173
  14.0 4.8 %collective-permute-start.4 = (bf16[8,7296]{1,0:T(8,128)(2,1)S(1)}, bf16[8,7296]{1,0:T(8,128)(2,1)S(1)}, u32[]{:S(2)}, u32[]{:S(2)}) collective-permute-start(bf16[8,7296]{1,0:T(8,128)(2,1)S(1)} %collective-permute-done.3.refs_0_), channel_id=1, source_target_pairs={{0,1},{1,0},{2,3},{3,2},{4,5},{5,4},{6,7},{7,6},{8,9},{9,8},{10,11... | collective-permute-start | bytes 350216 | tf_op jit(solution)/shard_map/ppermute | solution.py:177
  14.7 5.7 %collective-permute-start.6 = (bf16[8,7296]{1,0:T(8,128)(2,1)S(1)}, bf16[8,7296]{1,0:T(8,128)(2,1)S(1)}, u32[]{:S(2)}, u32[]{:S(2)}) collective-permute-start(bf16[8,7296]{1,0:T(8,128)(2,1)S(1)} %collective-permute-done.3.refs_0_), channel_id=1, source_target_pairs={{0,9},{1,8},{2,11},{3,10},{4,13},{5,12},{6,15},{7,14},{8,1},{9,0},... | collective-permute-start | bytes 350216 | tf_op jit(solution)/shard_map/ppermute | solution.py:183
  16.0 4.6 %collective-permute-start.7 = (bf16[32,7296]{1,0:T(8,128)(2,1)S(1)}, bf16[32,7296]{1,0:T(8,128)(2,1)S(1)}, u32[]{:S(2)}, u32[]{:S(2)}) collective-permute-start(bf16[32,7296]{1,0:T(8,128)(2,1)S(1)} %stack.2.refs_0_), channel_id=1, source_target_pairs={{0,4},{4,0},{8,12},{12,8},{1,5},{5,1},{9,13},{13,9},{2,6},{6,2},{1... | collective-permute-start | bytes 1400840 | tf_op jit(solution)/shard_map/ppermute | solution.py:169
  20.5 6.1 %slice-start = ((s8[14680064]{0:T(1024)(128)(4,1)}), s8[4194304]{0:T(1024)(128)(4,1)S(1)}, s32[]{:S(2)}) async-start(s8[14680064]{0:T(1024)(128)(4,1)} %bitcast.3), calls=%async_computation | async-start | bytes 8388608
  20.5 6.0 %slice-start.1 = ((s8[14680064]{0:T(1024)(128)(4,1)}), s8[4194304]{0:T(1024)(128)(4,1)S(1)}, s32[]{:S(2)}) async-start(s8[14680064]{0:T(1024)(128)(4,1)} %bitcast.3), calls=%async_computation.1 | async-start | bytes 8388608
  20.5 6.0 %slice-start.2 = ((s8[14680064]{0:T(1024)(128)(4,1)}), s8[4194304]{0:T(1024)(128)(4,1)S(1)}, s32[]{:S(2)}) async-start(s8[14680064]{0:T(1024)(128)(4,1)} %bitcast.3), calls=%async_computation.2 | async-start | bytes 8388608
  20.6 6.0 %slice-start.3 = ((s8[14680064]{0:T(1024)(128)(4,1)}), s8[2097152]{0:T(1024)(128)(4,1)S(1)}, s32[]{:S(2)}) async-start(s8[14680064]{0:T(1024)(128)(4,1)} %bitcast.3), calls=%async_computation.3 | async-start | bytes 4194304
  20.6 1.9 %collective-permute-start.8 = (bf16[32,7296]{1,0:T(8,128)(2,1)S(1)}, bf16[32,7296]{1,0:T(8,128)(2,1)S(1)}, u32[]{:S(2)}, u32[]{:S(2)}) collective-permute-start(bf16[32,7296]{1,0:T(8,128)(2,1)S(1)} %stack.3.refs_1_), channel_id=1, source_target_pairs={{0,4},{4,0},{8,12},{12,8},{1,5},{5,1},{9,13},{13,9},{2,6},{6,2},{1... | collective-permute-start | bytes 1400840 | tf_op jit(solution)/shard_map/ppermute | solution.py:169
  28.7 1.9 %collective-permute-start.9 = (bf16[32,7168]{1,0:T(8,128)(2,1)S(1)}, bf16[32,7168]{1,0:T(8,128)(2,1)S(1)}, u32[]{:S(2)}, u32[]{:S(2)}) collective-permute-start(bf16[32,7168]{1,0:T(8,128)(2,1)S(1)} %get-tuple-element.27), channel_id=1, source_target_pairs={{0,4},{4,0},{8,12},{12,8},{1,5},{5,1},{9,13},{13,9},{2,6},{6,2},{1... | collective-permute-start | bytes 1376264 | tf_op jit(solution)/shard_map/ppermute | solution.py:169
  30.5 3.8 %collective-permute-start.10 = (bf16[32,7168]{1,0:T(8,128)(2,1)S(1)}, bf16[32,7168]{1,0:T(8,128)(2,1)S(1)}, u32[]{:S(2)}, u32[]{:S(2)}) collective-permute-start(bf16[32,7168]{1,0:T(8,128)(2,1)S(1)} %get-tuple-element.28), channel_id=1, source_target_pairs={{0,4},{4,0},{8,12},{12,8},{1,5},{5,1},{9,13},{13,9},{2,6},{6,2},{1... | collective-permute-start | bytes 1376264 | tf_op jit(solution)/shard_map/ppermute | solution.py:169
  30.8 5.7 %collective-permute-start.13 = (bf16[8,7168]{1,0:T(8,128)(2,1)S(1)}, bf16[8,7168]{1,0:T(8,128)(2,1)S(1)}, u32[]{:S(2)}, u32[]{:S(2)}) collective-permute-start(bf16[8,7168]{1,0:T(8,128)(2,1)S(1)} %get-tuple-element.34), channel_id=1, source_target_pairs={{0,1},{1,0},{2,3},{3,2},{4,5},{5,4},{6,7},{7,6},{8,9},{9,8},{10,11... | collective-permute-start | bytes 344072 | tf_op jit(solution)/shard_map/ppermute | solution.py:177
  32.1 6.4 %collective-permute-start.11 = (bf16[8,7168]{1,0:T(8,128)(2,1)S(1)}, bf16[8,7168]{1,0:T(8,128)(2,1)S(1)}, u32[]{:S(2)}, u32[]{:S(2)}) collective-permute-start(bf16[8,7168]{1,0:T(8,128)(2,1)S(1)} %get-tuple-element.32), channel_id=1, source_target_pairs={{0,8},{4,12},{8,0},{12,4},{1,9},{5,13},{9,1},{13,5},{2,10},{6,14},... | collective-permute-start | bytes 344072 | tf_op jit(solution)/shard_map/ppermute | solution.py:173
  32.7 7.3 %collective-permute-start.12 = (bf16[8,7168]{1,0:T(8,128)(2,1)S(1)}, bf16[8,7168]{1,0:T(8,128)(2,1)S(1)}, u32[]{:S(2)}, u32[]{:S(2)}) collective-permute-start(bf16[8,7168]{1,0:T(8,128)(2,1)S(1)} %get-tuple-element.33), channel_id=1, source_target_pairs={{0,9},{1,8},{2,11},{3,10},{4,13},{5,12},{6,15},{7,14},{8,1},{9,0},... | collective-permute-start | bytes 344072 | tf_op jit(solution)/shard_map/ppermute | solution.py:183
  36.5 5.9 %collective-permute-start.15 = (bf16[8,7168]{1,0:T(8,128)(2,1)S(1)}, bf16[8,7168]{1,0:T(8,128)(2,1)S(1)}, u32[]{:S(2)}, u32[]{:S(2)}) collective-permute-start(bf16[8,7168]{1,0:T(8,128)(2,1)S(1)} %get-tuple-element.37), channel_id=1, source_target_pairs={{0,8},{4,12},{8,0},{12,4},{1,9},{5,13},{9,1},{13,5},{2,10},{6,14},... | collective-permute-start | bytes 344072 | tf_op jit(solution)/shard_map/ppermute | solution.py:173
  40.0 8.0 %collective-permute-start.14 = (bf16[8,7168]{1,0:T(8,128)(2,1)S(1)}, bf16[8,7168]{1,0:T(8,128)(2,1)S(1)}, u32[]{:S(2)}, u32[]{:S(2)}) collective-permute-start(bf16[8,7168]{1,0:T(8,128)(2,1)S(1)} %add_convert_fusion.2), channel_id=1, source_target_pairs={{0,2},{1,3},{2,0},{3,1},{4,6},{5,7},{6,4},{7,5},{8,10},{9,11},{10,... | collective-permute-start | bytes 344072 | tf_op jit(solution)/shard_map/ppermute | solution.py:177
  42.4 7.1 %collective-permute-start.16 = (bf16[8,7168]{1,0:T(8,128)(2,1)S(1)}, bf16[8,7168]{1,0:T(8,128)(2,1)S(1)}, u32[]{:S(2)}, u32[]{:S(2)}) collective-permute-start(bf16[8,7168]{1,0:T(8,128)(2,1)S(1)} %add_convert_fusion.1), channel_id=1, source_target_pairs={{0,1},{1,0},{2,3},{3,2},{4,5},{5,4},{6,7},{7,6},{8,9},{9,8},{10,11... | collective-permute-start | bytes 344072 | tf_op jit(solution)/shard_map/ppermute | solution.py:177
  43.6 5.9 %collective-permute-start.17 = (bf16[8,7168]{1,0:T(8,128)(2,1)S(1)}, bf16[8,7168]{1,0:T(8,128)(2,1)S(1)}, u32[]{:S(2)}, u32[]{:S(2)}) collective-permute-start(bf16[8,7168]{1,0:T(8,128)(2,1)S(1)} %get-tuple-element.40), channel_id=1, source_target_pairs={{0,8},{4,12},{8,0},{12,4},{1,9},{5,13},{9,1},{13,5},{2,10},{6,14},... | collective-permute-start | bytes 344072 | tf_op jit(solution)/shard_map/ppermute | solution.py:173

commit v15 on v14

--- a/solution.py
+++ b/solution.py
@@ -193,8 +193,8 @@
     ready = after(second, far_own)
     far_second, third = to_chip(ready), to_place(ready, 1)
     far_third = to_both(after(ready, far_first), 1)
-    early = stack(own, far_own, first, far_first)
-    late = stack(second, third, far_second, far_third)
+    early = stack(own, far_own, first, second)
+    late = stack(far_first, third, far_second, far_third)
     return [early, late, to_core(early), to_core(late)]
 
 
@@ -231,15 +231,14 @@
     early, late, other_early, other_late = zip(*chunks)
     other_late = [to_core(each) for each in other_late]
     other_early = [to_core(after(each, *other_late)) for each in other_early]
-    second, third, far_second, far_third = sums(late, other_late)
-    far_second = to_chip(far_second)
-    far_third = to_both(far_third, 1)
-    third = to_place(third, 1)
-    second = total(second, far_second, far_third, third).astype(jnp.bfloat16)
-    own, far_own, first, far_first = sums(early, other_early)
-    first = total(first, to_chip(after(far_first, third))).astype(jnp.bfloat16)
+    far_first, third, far_second, far_third = sums(late, other_late)
+    third, far_second = to_place(third, 1), to_chip(far_second)
+    far_third, far_first = to_both(far_third, 1), to_chip(far_first)
+    own, far_own, first, second = sums(early, other_early)
+    first = total(first, far_first).astype(jnp.bfloat16)
+    second = total(second, third, far_second, far_third).astype(jnp.bfloat16)
     first, far_own = lax.optimization_barrier((first, far_own))
-    second_here, first_here, far_own = to_place(second, 2), to_place(first, 1), to_chip(far_own)
+    first_here, second_here, far_own = to_place(first, 1), to_place(second, 2), to_chip(far_own)
     return total(own, second_here, first_here, far_own).astype(jnp.bfloat16)
 
 

time: 50.4 us -> 50.1 us (level)
    ppermute x6, waiting for transfers between devices: 2.54 us -> 6.01 us  [to_chip(): return lax.ppermute(value, 'node', [(i, i ^ 2) for i in range(2 * CHIPS)])]
    ppermute x6, waiting for transfers between devices: 9.23 us -> 7.5 us  [to_place(): return lax.ppermute(value, 'local', [(i, i ^ bits) for i in range(PLACES)])]
    ppermute x2, waiting for transfers between devices: 3.12 us -> 1.68 us  [to_both(): return lax.ppermute(value, ('node', 'local'), perm)]
    ppermute x6, starting transfers between devices: 11.3 us -> 10.3 us  [to_place(): return lax.ppermute(value, 'local', [(i, i ^ bits) for i in range(PLACES)])]
  transfers between devices with their start and end apart: 18 -> 18, of which waited for: 12 -> 11; matrix products, arithmetic and copies ran while one was open for 0% -> 0% of each run, Pallas kernels for 1% -> 1%
where the time goes in v15:
time: 50.1 us; the launch traced here: 50 us
  starting transfers between devices  22.7 us (45%)
  waiting for transfers between devices  18.7 us (37%)
  Pallas kernels  7.65 us (15%)
  other arithmetic  0.8 us (2%)
    ppermute x6, starting transfers between devices, to_place(): return lax.ppermute(value, 'local', [(i, i ^ bits) for i in range(PLACES)])  10.3 us
    ppermute x6, starting transfers between devices, to_chip(): return lax.ppermute(value, 'node', [(i, i ^ 2) for i in range(2 * CHIPS)])  8.8 us
    ppermute x6, waiting for transfers between devices, to_place(): return lax.ppermute(value, 'local', [(i, i ^ bits) for i in range(PLACES)])  7.5 us
    ppermute x6, waiting for transfers between devices, to_chip(): return lax.ppermute(value, 'node', [(i, i ^ 2) for i in range(2 * CHIPS)])  6.01 us
    pallas_call x1, Pallas kernels, hidden_units(): pl.pallas_call(functools.partial(hidden_kernel, experts), out_shape=jax.S...  4.05 us
    ppermute x4, waiting for transfers between devices, to_core(): return lax.ppermute(value, 'node', [(i, i ^ 1) for i in range(2 * CHIPS)])  3.5 us
    ppermute x2, starting transfers between devices, to_both(): return lax.ppermute(value, ('node', 'local'), perm)  3.11 us
    pallas_call x1, Pallas kernels, down(): pl.pallas_call(functools.partial(down_kernel, chunk), out_shape=[jax.Shap...  2.08 us
  transfers between devices with their start and end apart: 18, of which 11 were waited for; matrix products, arithmetic and copies ran while one was open for 0% of the time, Pallas kernels for 1%

profile of v15, /device:TPU:0, one launch (start us, length us, event | category | flops | bytes accessed | tf_op | source)
XLA Modules:
  0.0 50.0 jit_solution(7054308267171299162)
XLA Ops:
  0.0 0.0 copy-start
  0.0 0.0 copy-start.1
  0.0 1.2 %pack.1.refs_0_ = bf16[8,7296]{1,0:T(8,128)(2,1)S(1)} custom-call(bf16[8,7168]{1,0:T(8,128)(2,1)} %refs_0_.1, s32[4,8]{1,0:T(4,128)} %bitcast.6, f32[4,8]{1,0:T(4,128)} %bitcast.7, s32[8]{0:T(128)} %refs_3_.1, bf16[2,7168,512]{2,1,0:T(8,128)(2,1)} %refs_4_.3, bf16[2,7168,512]{2,1,0:T(8,128)(2,1)} %refs_5_.3, bf16[2,512,7168]{2,1,0:T(8,128)(2,1)} %refs_6_.1), custom_call_target="tpu_custom_call" | custom-call | tf_op jit(solution)/shard_map/pack/pallas_call | solution.py:50
  1.2 3.1 %collective-permute-start.1 = (bf16[8,7296]{1,0:T(8,128)(2,1)S(1)}, bf16[8,7296]{1,0:T(8,128)(2,1)S(1)}, u32[]{:S(2)}, u32[]{:S(2)}) collective-permute-start(bf16[8,7296]{1,0:T(8,128)(2,1)S(1)} %pack.1.refs_0_), channel_id=1, source_target_pairs={{0,1},{1,0},{2,3},{3,2},{4,5},{5,4},{6,7},{7,6},{8,9},{9,8},{10,11... | collective-permute-start | bytes 350216 | tf_op jit(solution)/shard_map/ppermute | solution.py:177
  4.3 2.6 %collective-permute-start.2 = (bf16[8,7296]{1,0:T(8,128)(2,1)S(1)}, bf16[8,7296]{1,0:T(8,128)(2,1)S(1)}, u32[]{:S(2)}, u32[]{:S(2)}) collective-permute-start(bf16[8,7296]{1,0:T(8,128)(2,1)S(1)} %pack.1.refs_0_), channel_id=1, source_target_pairs={{0,2},{1,3},{2,0},{3,1},{4,6},{5,7},{6,4},{7,5},{8,10},{9,11},{10,... | collective-permute-start | bytes 350216 | tf_op jit(solution)/shard_map/ppermute | solution.py:177
  6.8 1.5 %collective-permute-start = (bf16[8,7296]{1,0:T(8,128)(2,1)S(1)}, bf16[8,7296]{1,0:T(8,128)(2,1)S(1)}, u32[]{:S(2)}, u32[]{:S(2)}) collective-permute-start(bf16[8,7296]{1,0:T(8,128)(2,1)S(1)} %pack.1.refs_0_), channel_id=1, source_target_pairs={{0,8},{4,12},{8,0},{12,4},{1,9},{5,13},{9,1},{13,5},{2,10},{6,14},... | collective-permute-start | bytes 350216 | tf_op jit(solution)/shard_map/ppermute | solution.py:173
  8.3 0.3 collective-permute-done.1.refs_2_
  8.7 1.8 %collective-permute-start.3 = (bf16[8,7296]{1,0:T(8,128)(2,1)S(1)}, bf16[8,7296]{1,0:T(8,128)(2,1)S(1)}, u32[]{:S(2)}, u32[]{:S(2)}) collective-permute-start(bf16[8,7296]{1,0:T(8,128)(2,1)S(1)} %collective-permute-done.1.refs_2_), channel_id=1, source_target_pairs={{0,8},{4,12},{8,0},{12,4},{1,9},{5,13},{9,1},{13,5},{2,10},{6,14},... | collective-permute-start | bytes 350216 | tf_op jit(solution)/shard_map/ppermute | solution.py:173
  10.5 1.9 %collective-permute-done.2.refs_3_ = bf16[8,7296]{1,0:T(8,128)(2,1)S(1)} collective-permute-done((bf16[8,7296]{1,0:T(8,128)(2,1)S(1)}, bf16[8,7296]{1,0:T(8,128)(2,1)S(1)}, u32[]{:S(2)}, u32[]{:S(2)}) %collective-permute-start.2) | collective-permute-done | bytes 116768 | tf_op jit(solution)/shard_map/ppermute | solution.py:177
  12.4 0.1 collective-permute-done.refs_1_
  12.5 1.5 %collective-permute-start.5 = (bf16[8,7296]{1,0:T(8,128)(2,1)S(1)}, bf16[8,7296]{1,0:T(8,128)(2,1)S(1)}, u32[]{:S(2)}, u32[]{:S(2)}) collective-permute-start(bf16[8,7296]{1,0:T(8,128)(2,1)S(1)} %collective-permute-done.2.refs_3_), channel_id=1, source_target_pairs={{0,8},{4,12},{8,0},{12,4},{1,9},{5,13},{9,1},{13,5},{2,10},{6,14},... | collective-permute-start | bytes 350216 | tf_op jit(solution)/shard_map/ppermute | solution.py:173
  14.0 0.8 %collective-permute-start.4 = (bf16[8,7296]{1,0:T(8,128)(2,1)S(1)}, bf16[8,7296]{1,0:T(8,128)(2,1)S(1)}, u32[]{:S(2)}, u32[]{:S(2)}) collective-permute-start(bf16[8,7296]{1,0:T(8,128)(2,1)S(1)} %collective-permute-done.2.refs_3_), channel_id=1, source_target_pairs={{0,1},{1,0},{2,3},{3,2},{4,5},{5,4},{6,7},{7,6},{8,9},{9,8},{10,11... | collective-permute-start | bytes 350216 | tf_op jit(solution)/shard_map/ppermute | solution.py:177
  14.7 0.0 collective-permute-done.3.refs_0_
  14.7 1.2 %collective-permute-start.6 = (bf16[8,7296]{1,0:T(8,128)(2,1)S(1)}, bf16[8,7296]{1,0:T(8,128)(2,1)S(1)}, u32[]{:S(2)}, u32[]{:S(2)}) collective-permute-start(bf16[8,7296]{1,0:T(8,128)(2,1)S(1)} %collective-permute-done.2.refs_3_), channel_id=1, source_target_pairs={{0,9},{1,8},{2,11},{3,10},{4,13},{5,12},{6,15},{7,14},{8,1},{9,0},... | collective-permute-start | bytes 350216 | tf_op jit(solution)/shard_map/ppermute | solution.py:183
  16.0 0.1 stack.2.refs_0_
  16.0 0.1 collective-permute-start.7
  16.1 2.4 %collective-permute-done.5.refs_2_ = bf16[8,7296]{1,0:T(8,128)(2,1)S(1)} collective-permute-done((bf16[8,7296]{1,0:T(8,128)(2,1)S(1)}, bf16[8,7296]{1,0:T(8,128)(2,1)S(1)}, u32[]{:S(2)}, u32[]{:S(2)}) %collective-permute-start.5) | collective-permute-done | bytes 116768 | tf_op jit(solution)/shard_map/ppermute | solution.py:173
  18.5 0.2 collective-permute-done.4.refs_1_
  18.8 1.7 %collective-permute-done.6.refs_3_ = bf16[8,7296]{1,0:T(8,128)(2,1)S(1)} collective-permute-done((bf16[8,7296]{1,0:T(8,128)(2,1)S(1)}, bf16[8,7296]{1,0:T(8,128)(2,1)S(1)}, u32[]{:S(2)}, u32[]{:S(2)}) %collective-permute-start.6) | collective-permute-done | bytes 116768 | tf_op jit(solution)/shard_map/ppermute | solution.py:183
  20.5 0.0 slice-start
  20.5 0.1 stack.3.refs_1_
  20.5 0.0 slice-start.1
  20.5 0.0 slice-start.2
  20.6 0.0 slice-start.3
  20.6 0.1 collective-permute-start.8
  20.6 0.0 collective-permute-done.7.refs_2_
  20.7 1.8 %collective-permute-done.8.refs_3_ = bf16[32,7296]{1,0:T(8,128)(2,1)S(1)} collective-permute-done((bf16[32,7296]{1,0:T(8,128)(2,1)S(1)}, bf16[32,7296]{1,0:T(8,128)(2,1)S(1)}, u32[]{:S(2)}, u32[]{:S(2)}) %collective-permute-start.8) | collective-permute-done | bytes 466976 | tf_op jit(solution)/shard_map/ppermute | solution.py:169
  22.5 0.0 copy-done
  22.5 0.0 copy-done.1
  22.5 4.0 %hidden.1.hidden_ref = bf16[128,1024]{1,0:T(8,128)(2,1)S(1)} custom-call(bf16[32,7296]{1,0:T(8,128)(2,1)S(1)} %stack.2.refs_0_, bf16[32,7296]{1,0:T(8,128)(2,1)S(1)} %stack.3.refs_1_, bf16[32,7296]{1,0:T(8,128)(2,1)S(1)} %collective-permute-done.7.refs_2_, bf16[32,7296]{1,0:T(8,128)(2,1)S(1)} %collective-permute-done.8.refs_3_, ...), custom_call_target="tpu_custom_call" | custom-call | flops 3758096384 | bytes 29360128 | tf_op jit(solution)/shard_map/hidden/pallas_call | solution.py:113
  26.5 0.0 slice-done
  26.5 0.0 slice-done.1
  26.5 0.0 slice-done.2
  26.6 0.0 slice-done.3
  26.6 2.1 %down.1 = (bf16[32,7168]{1,0:T(8,128)(2,1)S(1)}, bf16[32,7168]{1,0:T(8,128)(2,1)S(1)}, bf16[32,7168]{1,0:T(8,128)(2,1)S(1)}, bf16[32,7168]{1,0:T(8,128)(2,1)S(1)}) custom-call(bf16[128,1024]{1,0:T(8,128)(2,1)S(1)} %hidden.1.hidden_ref, bf16[1024,7168]{1,0:T(8,128)(2,1)S(1)} %bitcast.5), custom_call_target="tpu_custom_call" | custom-call | flops 1879048192 | bytes 14680064 | tf_op jit(solution)/shard_map/down/pallas_call | solution.py:150
  28.7 0.2 collective-permute-start.9
  28.9 1.7 %collective-permute-done.9.refs_1_ = bf16[32,7168]{1,0:T(8,128)(2,1)S(1)} collective-permute-done((bf16[32,7168]{1,0:T(8,128)(2,1)S(1)}, bf16[32,7168]{1,0:T(8,128)(2,1)S(1)}, u32[]{:S(2)}, u32[]{:S(2)}) %collective-permute-start.9) | collective-permute-done | bytes 458784 | tf_op jit(solution)/shard_map/ppermute | solution.py:169
  30.5 0.1 collective-permute-start.10
  30.7 0.1 sums.3
  30.8 1.8 %collective-permute-start.15 = (bf16[8,7168]{1,0:T(8,128)(2,1)S(1)}, bf16[8,7168]{1,0:T(8,128)(2,1)S(1)}, u32[]{:S(2)}, u32[]{:S(2)}) collective-permute-start(bf16[8,7168]{1,0:T(8,128)(2,1)S(1)} %get-tuple-element.35), channel_id=1, source_target_pairs={{0,8},{4,12},{8,0},{12,4},{1,9},{5,13},{9,1},{13,5},{2,10},{6,14},... | collective-permute-start | bytes 344072 | tf_op jit(solution)/shard_map/ppermute | solution.py:173
  32.6 0.1 collective-permute-start.11
  32.7 1.5 %collective-permute-start.12 = (bf16[8,7168]{1,0:T(8,128)(2,1)S(1)}, bf16[8,7168]{1,0:T(8,128)(2,1)S(1)}, u32[]{:S(2)}, u32[]{:S(2)}) collective-permute-start(bf16[8,7168]{1,0:T(8,128)(2,1)S(1)} %get-tuple-element.32), channel_id=1, source_target_pairs={{0,8},{4,12},{8,0},{12,4},{1,9},{5,13},{9,1},{13,5},{2,10},{6,14},... | collective-permute-start | bytes 344072 | tf_op jit(solution)/shard_map/ppermute | solution.py:173
  34.2 1.9 %collective-permute-start.13 = (bf16[8,7168]{1,0:T(8,128)(2,1)S(1)}, bf16[8,7168]{1,0:T(8,128)(2,1)S(1)}, u32[]{:S(2)}, u32[]{:S(2)}) collective-permute-start(bf16[8,7168]{1,0:T(8,128)(2,1)S(1)} %get-tuple-element.33), channel_id=1, source_target_pairs={{0,9},{1,8},{2,11},{3,10},{4,13},{5,12},{6,15},{7,14},{8,1},{9,0},... | collective-permute-start | bytes 344072 | tf_op jit(solution)/shard_map/ppermute | solution.py:183
  36.0 0.0 collective-permute-done.10.refs_1_
  36.1 0.1 sums.2
  36.2 0.7 %collective-permute-done.15 = bf16[8,7168]{1,0:T(8,128)(2,1)S(1)} collective-permute-done((bf16[8,7168]{1,0:T(8,128)(2,1)S(1)}, bf16[8,7168]{1,0:T(8,128)(2,1)S(1)}, u32[]{:S(2)}, u32[]{:S(2)}) %collective-permute-start.15) | collective-permute-done | bytes 114720 | tf_op jit(solution)/shard_map/ppermute | solution.py:173
  36.9 1.3 %collective-permute-start.16 = (bf16[8,7168]{1,0:T(8,128)(2,1)S(1)}, bf16[8,7168]{1,0:T(8,128)(2,1)S(1)}, u32[]{:S(2)}, u32[]{:S(2)}) collective-permute-start(bf16[8,7168]{1,0:T(8,128)(2,1)S(1)} %add_convert_fusion.1), channel_id=1, source_target_pairs={{0,1},{1,0},{2,3},{3,2},{4,5},{5,4},{6,7},{7,6},{8,9},{9,8},{10,11... | collective-permute-start | bytes 344072 | tf_op jit(solution)/shard_map/ppermute | solution.py:177
  38.2 0.8 %collective-permute-start.17 = (bf16[8,7168]{1,0:T(8,128)(2,1)S(1)}, bf16[8,7168]{1,0:T(8,128)(2,1)S(1)}, u32[]{:S(2)}, u32[]{:S(2)}) collective-permute-start(bf16[8,7168]{1,0:T(8,128)(2,1)S(1)} %get-tuple-element.38), channel_id=1, source_target_pairs={{0,8},{4,12},{8,0},{12,4},{1,9},{5,13},{9,1},{13,5},{2,10},{6,14},... | collective-permute-start | bytes 344072 | tf_op jit(solution)/shard_map/ppermute | solution.py:173
  38.9 0.0 collective-permute-done.11
  38.9 2.8 %collective-permute-done.12 = bf16[8,7168]{1,0:T(8,128)(2,1)S(1)} collective-permute-done((bf16[8,7168]{1,0:T(8,128)(2,1)S(1)}, bf16[8,7168]{1,0:T(8,128)(2,1)S(1)}, u32[]{:S(2)}, u32[]{:S(2)}) %collective-permute-start.12) | collective-permute-done | bytes 114720 | tf_op jit(solution)/shard_map/ppermute | solution.py:173
  41.8 0.0 collective-permute-done.13
  41.8 0.1 add_convert_fusion.2
  41.8 2.4 %collective-permute-start.14 = (bf16[8,7168]{1,0:T(8,128)(2,1)S(1)}, bf16[8,7168]{1,0:T(8,128)(2,1)S(1)}, u32[]{:S(2)}, u32[]{:S(2)}) collective-permute-start(bf16[8,7168]{1,0:T(8,128)(2,1)S(1)} %add_convert_fusion.2), channel_id=1, source_target_pairs={{0,2},{1,3},{2,0},{3,1},{4,6},{5,7},{6,4},{7,5},{8,10},{9,11},{10,... | collective-permute-start | bytes 344072 | tf_op jit(solution)/shard_map/ppermute | solution.py:177
  44.2 0.0 collective-permute-done.16
  44.2 0.0 collective-permute-done.17
  44.2 5.0 %collective-permute-done.14 = bf16[8,7168]{1,0:T(8,128)(2,1)S(1)} collective-permute-done((bf16[8,7168]{1,0:T(8,128)(2,1)S(1)}, bf16[8,7168]{1,0:T(8,128)(2,1)S(1)}, u32[]{:S(2)}, u32[]{:S(2)}) %collective-permute-start.14) | collective-permute-done | bytes 114720 | tf_op jit(solution)/shard_map/ppermute | solution.py:177
  49.3 0.7 %add_convert_fusion = bf16[8,7168]{1,0:T(8,128)(2,1)} fusion(bf16[8,7168]{1,0:T(8,128)(2,1)S(1)} %collective-permute-done.17, bf16[8,7168]{1,0:T(8,128)(2,1)S(1)} %collective-permute-done.16, bf16[8,7168]{1,0:T(8,128)(2,1)S(1)} %collective-permute-done.14, bf16[8,7168]{1,0:T(8,128)(2,1)S(1)} %get-tuple-element.28), kind=kLoop, calls=%fused_computation | loop fusion | flops 458752 | bytes 573440 | tf_op jit(solution)/shard_map/convert_element_type | solution.py:242
  (2 shorter events, 0.0 us)
Async XLA Ops:
  0.0 22.5 %copy-start = (bf16[2,7168,512]{2,1,0:T(8,128)(2,1)S(1)}, bf16[2,7168,512]{2,1,0:T(8,128)(2,1)}, u32[]{:S(2)}) copy-start(bf16[2,7168,512]{2,1,0:T(8,128)(2,1)} %refs_4_.3) | copy-start | bytes 44040196
  0.0 22.5 %copy-start.1 = (bf16[2,7168,512]{2,1,0:T(8,128)(2,1)S(1)}, bf16[2,7168,512]{2,1,0:T(8,128)(2,1)}, u32[]{:S(2)}) copy-start(bf16[2,7168,512]{2,1,0:T(8,128)(2,1)} %refs_5_.3) | copy-start | bytes 44040196
  1.2 7.5 %collective-permute-start.1 = (bf16[8,7296]{1,0:T(8,128)(2,1)S(1)}, bf16[8,7296]{1,0:T(8,128)(2,1)S(1)}, u32[]{:S(2)}, u32[]{:S(2)}) collective-permute-start(bf16[8,7296]{1,0:T(8,128)(2,1)S(1)} %pack.1.refs_0_), channel_id=1, source_target_pairs={{0,1},{1,0},{2,3},{3,2},{4,5},{5,4},{6,7},{7,6},{8,9},{9,8},{10,11... | collective-permute-start | bytes 350216 | tf_op jit(solution)/shard_map/ppermute | solution.py:177
  4.3 8.1 %collective-permute-start.2 = (bf16[8,7296]{1,0:T(8,128)(2,1)S(1)}, bf16[8,7296]{1,0:T(8,128)(2,1)S(1)}, u32[]{:S(2)}, u32[]{:S(2)}) collective-permute-start(bf16[8,7296]{1,0:T(8,128)(2,1)S(1)} %pack.1.refs_0_), channel_id=1, source_target_pairs={{0,2},{1,3},{2,0},{3,1},{4,6},{5,7},{6,4},{7,5},{8,10},{9,11},{10,... | collective-permute-start | bytes 350216 | tf_op jit(solution)/shard_map/ppermute | solution.py:177
  6.8 5.6 %collective-permute-start = (bf16[8,7296]{1,0:T(8,128)(2,1)S(1)}, bf16[8,7296]{1,0:T(8,128)(2,1)S(1)}, u32[]{:S(2)}, u32[]{:S(2)}) collective-permute-start(bf16[8,7296]{1,0:T(8,128)(2,1)S(1)} %pack.1.refs_0_), channel_id=1, source_target_pairs={{0,8},{4,12},{8,0},{12,4},{1,9},{5,13},{9,1},{13,5},{2,10},{6,14},... | collective-permute-start | bytes 350216 | tf_op jit(solution)/shard_map/ppermute | solution.py:173
  8.7 6.1 %collective-permute-start.3 = (bf16[8,7296]{1,0:T(8,128)(2,1)S(1)}, bf16[8,7296]{1,0:T(8,128)(2,1)S(1)}, u32[]{:S(2)}, u32[]{:S(2)}) collective-permute-start(bf16[8,7296]{1,0:T(8,128)(2,1)S(1)} %collective-permute-done.1.refs_2_), channel_id=1, source_target_pairs={{0,8},{4,12},{8,0},{12,4},{1,9},{5,13},{9,1},{13,5},{2,10},{6,14},... | collective-permute-start | bytes 350216 | tf_op jit(solution)/shard_map/ppermute | solution.py:173
  12.5 6.1 %collective-permute-start.5 = (bf16[8,7296]{1,0:T(8,128)(2,1)S(1)}, bf16[8,7296]{1,0:T(8,128)(2,1)S(1)}, u32[]{:S(2)}, u32[]{:S(2)}) collective-permute-start(bf16[8,7296]{1,0:T(8,128)(2,1)S(1)} %collective-permute-done.2.refs_3_), channel_id=1, source_target_pairs={{0,8},{4,12},{8,0},{12,4},{1,9},{5,13},{9,1},{13,5},{2,10},{6,14},... | collective-permute-start | bytes 350216 | tf_op jit(solution)/shard_map/ppermute | solution.py:173
  14.0 4.8 %collective-permute-start.4 = (bf16[8,7296]{1,0:T(8,128)(2,1)S(1)}, bf16[8,7296]{1,0:T(8,128)(2,1)S(1)}, u32[]{:S(2)}, u32[]{:S(2)}) collective-permute-start(bf16[8,7296]{1,0:T(8,128)(2,1)S(1)} %collective-permute-done.2.refs_3_), channel_id=1, source_target_pairs={{0,1},{1,0},{2,3},{3,2},{4,5},{5,4},{6,7},{7,6},{8,9},{9,8},{10,11... | collective-permute-start | bytes 350216 | tf_op jit(solution)/shard_map/ppermute | solution.py:177
  14.7 5.7 %collective-permute-start.6 = (bf16[8,7296]{1,0:T(8,128)(2,1)S(1)}, bf16[8,7296]{1,0:T(8,128)(2,1)S(1)}, u32[]{:S(2)}, u32[]{:S(2)}) collective-permute-start(bf16[8,7296]{1,0:T(8,128)(2,1)S(1)} %collective-permute-done.2.refs_3_), channel_id=1, source_target_pairs={{0,9},{1,8},{2,11},{3,10},{4,13},{5,12},{6,15},{7,14},{8,1},{9,0},... | collective-permute-start | bytes 350216 | tf_op jit(solution)/shard_map/ppermute | solution.py:183
  16.0 4.6 %collective-permute-start.7 = (bf16[32,7296]{1,0:T(8,128)(2,1)S(1)}, bf16[32,7296]{1,0:T(8,128)(2,1)S(1)}, u32[]{:S(2)}, u32[]{:S(2)}) collective-permute-start(bf16[32,7296]{1,0:T(8,128)(2,1)S(1)} %stack.2.refs_0_), channel_id=1, source_target_pairs={{0,4},{4,0},{8,12},{12,8},{1,5},{5,1},{9,13},{13,9},{2,6},{6,2},{1... | collective-permute-start | bytes 1400840 | tf_op jit(solution)/shard_map/ppermute | solution.py:169
  20.5 6.1 %slice-start = ((s8[14680064]{0:T(1024)(128)(4,1)}), s8[4194304]{0:T(1024)(128)(4,1)S(1)}, s32[]{:S(2)}) async-start(s8[14680064]{0:T(1024)(128)(4,1)} %bitcast.3), calls=%async_computation | async-start | bytes 8388608
  20.5 6.0 %slice-start.1 = ((s8[14680064]{0:T(1024)(128)(4,1)}), s8[4194304]{0:T(1024)(128)(4,1)S(1)}, s32[]{:S(2)}) async-start(s8[14680064]{0:T(1024)(128)(4,1)} %bitcast.3), calls=%async_computation.1 | async-start | bytes 8388608
  20.5 6.0 %slice-start.2 = ((s8[14680064]{0:T(1024)(128)(4,1)}), s8[4194304]{0:T(1024)(128)(4,1)S(1)}, s32[]{:S(2)}) async-start(s8[14680064]{0:T(1024)(128)(4,1)} %bitcast.3), calls=%async_computation.2 | async-start | bytes 8388608
  20.6 6.0 %slice-start.3 = ((s8[14680064]{0:T(1024)(128)(4,1)}), s8[2097152]{0:T(1024)(128)(4,1)S(1)}, s32[]{:S(2)}) async-start(s8[14680064]{0:T(1024)(128)(4,1)} %bitcast.3), calls=%async_computation.3 | async-start | bytes 4194304
  20.6 1.9 %collective-permute-start.8 = (bf16[32,7296]{1,0:T(8,128)(2,1)S(1)}, bf16[32,7296]{1,0:T(8,128)(2,1)S(1)}, u32[]{:S(2)}, u32[]{:S(2)}) collective-permute-start(bf16[32,7296]{1,0:T(8,128)(2,1)S(1)} %stack.3.refs_1_), channel_id=1, source_target_pairs={{0,4},{4,0},{8,12},{12,8},{1,5},{5,1},{9,13},{13,9},{2,6},{6,2},{1... | collective-permute-start | bytes 1400840 | tf_op jit(solution)/shard_map/ppermute | solution.py:169
  28.7 1.9 %collective-permute-start.9 = (bf16[32,7168]{1,0:T(8,128)(2,1)S(1)}, bf16[32,7168]{1,0:T(8,128)(2,1)S(1)}, u32[]{:S(2)}, u32[]{:S(2)}) collective-permute-start(bf16[32,7168]{1,0:T(8,128)(2,1)S(1)} %get-tuple-element.26), channel_id=1, source_target_pairs={{0,4},{4,0},{8,12},{12,8},{1,5},{5,1},{9,13},{13,9},{2,6},{6,2},{1... | collective-permute-start | bytes 1376264 | tf_op jit(solution)/shard_map/ppermute | solution.py:169
  30.5 5.5 %collective-permute-start.10 = (bf16[32,7168]{1,0:T(8,128)(2,1)S(1)}, bf16[32,7168]{1,0:T(8,128)(2,1)S(1)}, u32[]{:S(2)}, u32[]{:S(2)}) collective-permute-start(bf16[32,7168]{1,0:T(8,128)(2,1)S(1)} %get-tuple-element.27), channel_id=1, source_target_pairs={{0,4},{4,0},{8,12},{12,8},{1,5},{5,1},{9,13},{13,9},{2,6},{6,2},{1... | collective-permute-start | bytes 1376264 | tf_op jit(solution)/shard_map/ppermute | solution.py:169
  30.8 6.0 %collective-permute-start.15 = (bf16[8,7168]{1,0:T(8,128)(2,1)S(1)}, bf16[8,7168]{1,0:T(8,128)(2,1)S(1)}, u32[]{:S(2)}, u32[]{:S(2)}) collective-permute-start(bf16[8,7168]{1,0:T(8,128)(2,1)S(1)} %get-tuple-element.35), channel_id=1, source_target_pairs={{0,8},{4,12},{8,0},{12,4},{1,9},{5,13},{9,1},{13,5},{2,10},{6,14},... | collective-permute-start | bytes 344072 | tf_op jit(solution)/shard_map/ppermute | solution.py:173
  32.6 6.4 %collective-permute-start.11 = (bf16[8,7168]{1,0:T(8,128)(2,1)S(1)}, bf16[8,7168]{1,0:T(8,128)(2,1)S(1)}, u32[]{:S(2)}, u32[]{:S(2)}) collective-permute-start(bf16[8,7168]{1,0:T(8,128)(2,1)S(1)} %get-tuple-element.31), channel_id=1, source_target_pairs={{0,1},{1,0},{2,3},{3,2},{4,5},{5,4},{6,7},{7,6},{8,9},{9,8},{10,11... | collective-permute-start | bytes 344072 | tf_op jit(solution)/shard_map/ppermute | solution.py:177
  32.7 9.1 %collective-permute-start.12 = (bf16[8,7168]{1,0:T(8,128)(2,1)S(1)}, bf16[8,7168]{1,0:T(8,128)(2,1)S(1)}, u32[]{:S(2)}, u32[]{:S(2)}) collective-permute-start(bf16[8,7168]{1,0:T(8,128)(2,1)S(1)} %get-tuple-element.32), channel_id=1, source_target_pairs={{0,8},{4,12},{8,0},{12,4},{1,9},{5,13},{9,1},{13,5},{2,10},{6,14},... | collective-permute-start | bytes 344072 | tf_op jit(solution)/shard_map/ppermute | solution.py:173
  34.2 7.6 %collective-permute-start.13 = (bf16[8,7168]{1,0:T(8,128)(2,1)S(1)}, bf16[8,7168]{1,0:T(8,128)(2,1)S(1)}, u32[]{:S(2)}, u32[]{:S(2)}) collective-permute-start(bf16[8,7168]{1,0:T(8,128)(2,1)S(1)} %get-tuple-element.33), channel_id=1, source_target_pairs={{0,9},{1,8},{2,11},{3,10},{4,13},{5,12},{6,15},{7,14},{8,1},{9,0},... | collective-permute-start | bytes 344072 | tf_op jit(solution)/shard_map/ppermute | solution.py:183
  36.9 7.4 %collective-permute-start.16 = (bf16[8,7168]{1,0:T(8,128)(2,1)S(1)}, bf16[8,7168]{1,0:T(8,128)(2,1)S(1)}, u32[]{:S(2)}, u32[]{:S(2)}) collective-permute-start(bf16[8,7168]{1,0:T(8,128)(2,1)S(1)} %add_convert_fusion.1), channel_id=1, source_target_pairs={{0,1},{1,0},{2,3},{3,2},{4,5},{5,4},{6,7},{7,6},{8,9},{9,8},{10,11... | collective-permute-start | bytes 344072 | tf_op jit(solution)/shard_map/ppermute | solution.py:177
  38.2 6.1 %collective-permute-start.17 = (bf16[8,7168]{1,0:T(8,128)(2,1)S(1)}, bf16[8,7168]{1,0:T(8,128)(2,1)S(1)}, u32[]{:S(2)}, u32[]{:S(2)}) collective-permute-start(bf16[8,7168]{1,0:T(8,128)(2,1)S(1)} %get-tuple-element.38), channel_id=1, source_target_pairs={{0,8},{4,12},{8,0},{12,4},{1,9},{5,13},{9,1},{13,5},{2,10},{6,14},... | collective-permute-start | bytes 344072 | tf_op jit(solution)/shard_map/ppermute | solution.py:173
  41.8 7.5 %collective-permute-start.14 = (bf16[8,7168]{1,0:T(8,128)(2,1)S(1)}, bf16[8,7168]{1,0:T(8,128)(2,1)S(1)}, u32[]{:S(2)}, u32[]{:S(2)}) collective-permute-start(bf16[8,7168]{1,0:T(8,128)(2,1)S(1)} %add_convert_fusion.2), channel_id=1, source_target_pairs={{0,2},{1,3},{2,0},{3,1},{4,6},{5,7},{6,4},{7,5},{8,10},{9,11},{10,... | collective-permute-start | bytes 344072 | tf_op jit(solution)/shard_map/ppermute | solution.py:177

commit v16 on v15

--- a/solution.py
+++ b/solution.py
@@ -236,10 +236,10 @@
     far_third, far_first = to_both(far_third, 1), to_chip(far_first)
     own, far_own, first, second = sums(early, other_early)
     first = total(first, far_first).astype(jnp.bfloat16)
+    first_here = to_place(first, 1)
+    far_own = to_chip(after(far_own, first_here))
     second = total(second, third, far_second, far_third).astype(jnp.bfloat16)
-    first, far_own = lax.optimization_barrier((first, far_own))
-    first_here, second_here, far_own = to_place(first, 1), to_place(second, 2), to_chip(far_own)
-    return total(own, second_here, first_here, far_own).astype(jnp.bfloat16)
+    return total(own, to_place(second, 2), first_here, far_own).astype(jnp.bfloat16)
 
 
 def by_permutes(tokens, expert_ids, route_weights, expert_slot, w_gate, w_up, w_down):

time: 50.1 us -> 50.1 us (level)
    ppermute x6, starting transfers between devices: 8.8 us -> 9.43 us  [to_chip(): return lax.ppermute(value, 'node', [(i, i ^ 2) for i in range(2 * CHIPS)])]
  transfers between devices with their start and end apart: 18 -> 18, of which waited for: 11 -> 12; matrix products, arithmetic and copies ran while one was open for 0% -> 0% of each run, Pallas kernels for 1% -> 1%
where the time goes in v16:
time: 50.1 us; the launch traced here: 50 us
  starting transfers between devices  23.1 us (46%)
  waiting for transfers between devices  18.3 us (37%)
  Pallas kernels  7.65 us (15%)
  other arithmetic  0.8 us (2%)
    ppermute x6, starting transfers between devices, to_place(): return lax.ppermute(value, 'local', [(i, i ^ bits) for i in range(PLACES)])  10.1 us
    ppermute x6, starting transfers between devices, to_chip(): return lax.ppermute(value, 'node', [(i, i ^ 2) for i in range(2 * CHIPS)])  9.43 us
    ppermute x6, waiting for transfers between devices, to_place(): return lax.ppermute(value, 'local', [(i, i ^ bits) for i in range(PLACES)])  7.26 us
    ppermute x6, waiting for transfers between devices, to_chip(): return lax.ppermute(value, 'node', [(i, i ^ 2) for i in range(2 * CHIPS)])  5.84 us
    pallas_call x1, Pallas kernels, hidden_units(): pl.pallas_call(functools.partial(hidden_kernel, experts), out_shape=jax.S...  4.05 us
    ppermute x4, waiting for transfers between devices, to_core(): return lax.ppermute(value, 'node', [(i, i ^ 1) for i in range(2 * CHIPS)])  3.5 us
    ppermute x2, starting transfers between devices, to_both(): return lax.ppermute(value, ('node', 'local'), perm)  3.11 us
    pallas_call x1, Pallas kernels, down(): pl.pallas_call(functools.partial(down_kernel, chunk), out_shape=[jax.Shap...  2.08 us
  transfers between devices with their start and end apart: 18, of which 12 were waited for; matrix products, arithmetic and copies ran while one was open for 0% of the time, Pallas kernels for 1%

profile of v16, /device:TPU:0, one launch (start us, length us, event | category | flops | bytes accessed | tf_op | source)
XLA Modules:
  0.0 50.0 jit_solution(14761081312798707131)
XLA Ops:
  0.0 0.0 copy-start
  0.0 0.0 copy-start.1
  0.0 1.2 %pack.1.refs_0_ = bf16[8,7296]{1,0:T(8,128)(2,1)S(1)} custom-call(bf16[8,7168]{1,0:T(8,128)(2,1)} %refs_0_.1, s32[4,8]{1,0:T(4,128)} %bitcast.6, f32[4,8]{1,0:T(4,128)} %bitcast.7, s32[8]{0:T(128)} %refs_3_.1, bf16[2,7168,512]{2,1,0:T(8,128)(2,1)} %refs_4_.3, bf16[2,7168,512]{2,1,0:T(8,128)(2,1)} %refs_5_.3, bf16[2,512,7168]{2,1,0:T(8,128)(2,1)} %refs_6_.1), custom_call_target="tpu_custom_call" | custom-call | tf_op jit(solution)/shard_map/pack/pallas_call | solution.py:50
  1.2 3.1 %collective-permute-start.1 = (bf16[8,7296]{1,0:T(8,128)(2,1)S(1)}, bf16[8,7296]{1,0:T(8,128)(2,1)S(1)}, u32[]{:S(2)}, u32[]{:S(2)}) collective-permute-start(bf16[8,7296]{1,0:T(8,128)(2,1)S(1)} %pack.1.refs_0_), channel_id=1, source_target_pairs={{0,1},{1,0},{2,3},{3,2},{4,5},{5,4},{6,7},{7,6},{8,9},{9,8},{10,11... | collective-permute-start | bytes 350216 | tf_op jit(solution)/shard_map/ppermute | solution.py:177
  4.3 2.6 %collective-permute-start.2 = (bf16[8,7296]{1,0:T(8,128)(2,1)S(1)}, bf16[8,7296]{1,0:T(8,128)(2,1)S(1)}, u32[]{:S(2)}, u32[]{:S(2)}) collective-permute-start(bf16[8,7296]{1,0:T(8,128)(2,1)S(1)} %pack.1.refs_0_), channel_id=1, source_target_pairs={{0,2},{1,3},{2,0},{3,1},{4,6},{5,7},{6,4},{7,5},{8,10},{9,11},{10,... | collective-permute-start | bytes 350216 | tf_op jit(solution)/shard_map/ppermute | solution.py:177
  6.8 1.5 %collective-permute-start = (bf16[8,7296]{1,0:T(8,128)(2,1)S(1)}, bf16[8,7296]{1,0:T(8,128)(2,1)S(1)}, u32[]{:S(2)}, u32[]{:S(2)}) collective-permute-start(bf16[8,7296]{1,0:T(8,128)(2,1)S(1)} %pack.1.refs_0_), channel_id=1, source_target_pairs={{0,8},{4,12},{8,0},{12,4},{1,9},{5,13},{9,1},{13,5},{2,10},{6,14},... | collective-permute-start | bytes 350216 | tf_op jit(solution)/shard_map/ppermute | solution.py:173
  8.3 0.3 collective-permute-done.1.refs_2_
  8.7 1.8 %collective-permute-start.3 = (bf16[8,7296]{1,0:T(8,128)(2,1)S(1)}, bf16[8,7296]{1,0:T(8,128)(2,1)S(1)}, u32[]{:S(2)}, u32[]{:S(2)}) collective-permute-start(bf16[8,7296]{1,0:T(8,128)(2,1)S(1)} %collective-permute-done.1.refs_2_), channel_id=1, source_target_pairs={{0,8},{4,12},{8,0},{12,4},{1,9},{5,13},{9,1},{13,5},{2,10},{6,14},... | collective-permute-start | bytes 350216 | tf_op jit(solution)/shard_map/ppermute | solution.py:173
  10.5 1.9 %collective-permute-done.2.refs_3_ = bf16[8,7296]{1,0:T(8,128)(2,1)S(1)} collective-permute-done((bf16[8,7296]{1,0:T(8,128)(2,1)S(1)}, bf16[8,7296]{1,0:T(8,128)(2,1)S(1)}, u32[]{:S(2)}, u32[]{:S(2)}) %collective-permute-start.2) | collective-permute-done | bytes 116768 | tf_op jit(solution)/shard_map/ppermute | solution.py:177
  12.4 0.1 collective-permute-done.refs_1_
  12.5 1.5 %collective-permute-start.5 = (bf16[8,7296]{1,0:T(8,128)(2,1)S(1)}, bf16[8,7296]{1,0:T(8,128)(2,1)S(1)}, u32[]{:S(2)}, u32[]{:S(2)}) collective-permute-start(bf16[8,7296]{1,0:T(8,128)(2,1)S(1)} %collective-permute-done.2.refs_3_), channel_id=1, source_target_pairs={{0,8},{4,12},{8,0},{12,4},{1,9},{5,13},{9,1},{13,5},{2,10},{6,14},... | collective-permute-start | bytes 350216 | tf_op jit(solution)/shard_map/ppermute | solution.py:173
  14.0 0.8 %collective-permute-start.4 = (bf16[8,7296]{1,0:T(8,128)(2,1)S(1)}, bf16[8,7296]{1,0:T(8,128)(2,1)S(1)}, u32[]{:S(2)}, u32[]{:S(2)}) collective-permute-start(bf16[8,7296]{1,0:T(8,128)(2,1)S(1)} %collective-permute-done.2.refs_3_), channel_id=1, source_target_pairs={{0,1},{1,0},{2,3},{3,2},{4,5},{5,4},{6,7},{7,6},{8,9},{9,8},{10,11... | collective-permute-start | bytes 350216 | tf_op jit(solution)/shard_map/ppermute | solution.py:177
  14.7 0.0 collective-permute-done.3.refs_0_
  14.7 1.2 %collective-permute-start.6 = (bf16[8,7296]{1,0:T(8,128)(2,1)S(1)}, bf16[8,7296]{1,0:T(8,128)(2,1)S(1)}, u32[]{:S(2)}, u32[]{:S(2)}) collective-permute-start(bf16[8,7296]{1,0:T(8,128)(2,1)S(1)} %collective-permute-done.2.refs_3_), channel_id=1, source_target_pairs={{0,9},{1,8},{2,11},{3,10},{4,13},{5,12},{6,15},{7,14},{8,1},{9,0},... | collective-permute-start | bytes 350216 | tf_op jit(solution)/shard_map/ppermute | solution.py:183
  16.0 0.1 stack.2.refs_0_
  16.0 0.1 collective-permute-start.7
  16.1 2.4 %collective-permute-done.5.refs_2_ = bf16[8,7296]{1,0:T(8,128)(2,1)S(1)} collective-permute-done((bf16[8,7296]{1,0:T(8,128)(2,1)S(1)}, bf16[8,7296]{1,0:T(8,128)(2,1)S(1)}, u32[]{:S(2)}, u32[]{:S(2)}) %collective-permute-start.5) | collective-permute-done | bytes 116768 | tf_op jit(solution)/shard_map/ppermute | solution.py:173
  18.5 0.2 collective-permute-done.4.refs_1_
  18.8 1.7 %collective-permute-done.6.refs_3_ = bf16[8,7296]{1,0:T(8,128)(2,1)S(1)} collective-permute-done((bf16[8,7296]{1,0:T(8,128)(2,1)S(1)}, bf16[8,7296]{1,0:T(8,128)(2,1)S(1)}, u32[]{:S(2)}, u32[]{:S(2)}) %collective-permute-start.6) | collective-permute-done | bytes 116768 | tf_op jit(solution)/shard_map/ppermute | solution.py:183
  20.5 0.0 slice-start
  20.5 0.1 stack.3.refs_1_
  20.5 0.0 slice-start.1
  20.5 0.0 slice-start.2
  20.6 0.0 slice-start.3
  20.6 0.1 collective-permute-start.8
  20.6 0.0 collective-permute-done.7.refs_2_
  20.7 1.8 %collective-permute-done.8.refs_3_ = bf16[32,7296]{1,0:T(8,128)(2,1)S(1)} collective-permute-done((bf16[32,7296]{1,0:T(8,128)(2,1)S(1)}, bf16[32,7296]{1,0:T(8,128)(2,1)S(1)}, u32[]{:S(2)}, u32[]{:S(2)}) %collective-permute-start.8) | collective-permute-done | bytes 466976 | tf_op jit(solution)/shard_map/ppermute | solution.py:169
  22.5 0.0 copy-done
  22.5 0.0 copy-done.1
  22.5 4.0 %hidden.1.hidden_ref = bf16[128,1024]{1,0:T(8,128)(2,1)S(1)} custom-call(bf16[32,7296]{1,0:T(8,128)(2,1)S(1)} %stack.2.refs_0_, bf16[32,7296]{1,0:T(8,128)(2,1)S(1)} %stack.3.refs_1_, bf16[32,7296]{1,0:T(8,128)(2,1)S(1)} %collective-permute-done.7.refs_2_, bf16[32,7296]{1,0:T(8,128)(2,1)S(1)} %collective-permute-done.8.refs_3_, ...), custom_call_target="tpu_custom_call" | custom-call | flops 3758096384 | bytes 29360128 | tf_op jit(solution)/shard_map/hidden/pallas_call | solution.py:113
  26.5 0.0 slice-done
  26.5 0.0 slice-done.1
  26.5 0.0 slice-done.2
  26.6 0.0 slice-done.3
  26.6 2.1 %down.1 = (bf16[32,7168]{1,0:T(8,128)(2,1)S(1)}, bf16[32,7168]{1,0:T(8,128)(2,1)S(1)}, bf16[32,7168]{1,0:T(8,128)(2,1)S(1)}, bf16[32,7168]{1,0:T(8,128)(2,1)S(1)}) custom-call(bf16[128,1024]{1,0:T(8,128)(2,1)S(1)} %hidden.1.hidden_ref, bf16[1024,7168]{1,0:T(8,128)(2,1)S(1)} %bitcast.5), custom_call_target="tpu_custom_call" | custom-call | flops 1879048192 | bytes 14680064 | tf_op jit(solution)/shard_map/down/pallas_call | solution.py:150
  28.7 0.2 collective-permute-start.9
  28.9 1.7 %collective-permute-done.9.refs_1_ = bf16[32,7168]{1,0:T(8,128)(2,1)S(1)} collective-permute-done((bf16[32,7168]{1,0:T(8,128)(2,1)S(1)}, bf16[32,7168]{1,0:T(8,128)(2,1)S(1)}, u32[]{:S(2)}, u32[]{:S(2)}) %collective-permute-start.9) | collective-permute-done | bytes 458784 | tf_op jit(solution)/shard_map/ppermute | solution.py:169
  30.5 0.1 collective-permute-start.10
  30.7 0.1 sums.3
  30.8 1.8 %collective-permute-start.15 = (bf16[8,7168]{1,0:T(8,128)(2,1)S(1)}, bf16[8,7168]{1,0:T(8,128)(2,1)S(1)}, u32[]{:S(2)}, u32[]{:S(2)}) collective-permute-start(bf16[8,7168]{1,0:T(8,128)(2,1)S(1)} %get-tuple-element.34), channel_id=1, source_target_pairs={{0,8},{4,12},{8,0},{12,4},{1,9},{5,13},{9,1},{13,5},{2,10},{6,14},... | collective-permute-start | bytes 344072 | tf_op jit(solution)/shard_map/ppermute | solution.py:173
  32.6 0.1 collective-permute-start.11
  32.7 1.5 %collective-permute-start.12 = (bf16[8,7168]{1,0:T(8,128)(2,1)S(1)}, bf16[8,7168]{1,0:T(8,128)(2,1)S(1)}, u32[]{:S(2)}, u32[]{:S(2)}) collective-permute-start(bf16[8,7168]{1,0:T(8,128)(2,1)S(1)} %get-tuple-element.31), channel_id=1, source_target_pairs={{0,8},{4,12},{8,0},{12,4},{1,9},{5,13},{9,1},{13,5},{2,10},{6,14},... | collective-permute-start | bytes 344072 | tf_op jit(solution)/shard_map/ppermute | solution.py:173
  34.2 1.9 %collective-permute-start.13 = (bf16[8,7168]{1,0:T(8,128)(2,1)S(1)}, bf16[8,7168]{1,0:T(8,128)(2,1)S(1)}, u32[]{:S(2)}, u32[]{:S(2)}) collective-permute-start(bf16[8,7168]{1,0:T(8,128)(2,1)S(1)} %get-tuple-element.32), channel_id=1, source_target_pairs={{0,9},{1,8},{2,11},{3,10},{4,13},{5,12},{6,15},{7,14},{8,1},{9,0},... | collective-permute-start | bytes 344072 | tf_op jit(solution)/shard_map/ppermute | solution.py:183
  36.0 0.0 collective-permute-done.10.refs_1_
  36.1 0.1 sums.2
  36.2 0.7 %collective-permute-done.15 = bf16[8,7168]{1,0:T(8,128)(2,1)S(1)} collective-permute-done((bf16[8,7168]{1,0:T(8,128)(2,1)S(1)}, bf16[8,7168]{1,0:T(8,128)(2,1)S(1)}, u32[]{:S(2)}, u32[]{:S(2)}) %collective-permute-start.15) | collective-permute-done | bytes 114720 | tf_op jit(solution)/shard_map/ppermute | solution.py:173
  36.9 1.3 %collective-permute-start.16 = (bf16[8,7168]{1,0:T(8,128)(2,1)S(1)}, bf16[8,7168]{1,0:T(8,128)(2,1)S(1)}, u32[]{:S(2)}, u32[]{:S(2)}) collective-permute-start(bf16[8,7168]{1,0:T(8,128)(2,1)S(1)} %add_convert_fusion.1), channel_id=1, source_target_pairs={{0,1},{1,0},{2,3},{3,2},{4,5},{5,4},{6,7},{7,6},{8,9},{9,8},{10,11... | collective-permute-start | bytes 344072 | tf_op jit(solution)/shard_map/ppermute | solution.py:177
  38.2 0.4 collective-permute-done.11
  38.6 2.6 %collective-permute-done.12 = bf16[8,7168]{1,0:T(8,128)(2,1)S(1)} collective-permute-done((bf16[8,7168]{1,0:T(8,128)(2,1)S(1)}, bf16[8,7168]{1,0:T(8,128)(2,1)S(1)}, u32[]{:S(2)}, u32[]{:S(2)}) %collective-permute-start.12) | collective-permute-done | bytes 114720 | tf_op jit(solution)/shard_map/ppermute | solution.py:173
  41.2 0.0 collective-permute-done.13
  41.2 0.1 add_convert_fusion.2
  41.3 2.2 %collective-permute-start.14 = (bf16[8,7168]{1,0:T(8,128)(2,1)S(1)}, bf16[8,7168]{1,0:T(8,128)(2,1)S(1)}, u32[]{:S(2)}, u32[]{:S(2)}) collective-permute-start(bf16[8,7168]{1,0:T(8,128)(2,1)S(1)} %add_convert_fusion.2), channel_id=1, source_target_pairs={{0,2},{1,3},{2,0},{3,1},{4,6},{5,7},{6,4},{7,5},{8,10},{9,11},{10,... | collective-permute-start | bytes 344072 | tf_op jit(solution)/shard_map/ppermute | solution.py:177
  43.5 0.0 collective-permute-done.16
  43.5 1.4 %collective-permute-start.17 = (bf16[8,7168]{1,0:T(8,128)(2,1)S(1)}, bf16[8,7168]{1,0:T(8,128)(2,1)S(1)}, u32[]{:S(2)}, u32[]{:S(2)}) collective-permute-start(bf16[8,7168]{1,0:T(8,128)(2,1)S(1)} %get-tuple-element.36), channel_id=1, source_target_pairs={{0,8},{4,12},{8,0},{12,4},{1,9},{5,13},{9,1},{13,5},{2,10},{6,14},... | collective-permute-start | bytes 344072 | tf_op jit(solution)/shard_map/ppermute | solution.py:173
  44.9 4.4 %collective-permute-done.14 = bf16[8,7168]{1,0:T(8,128)(2,1)S(1)} collective-permute-done((bf16[8,7168]{1,0:T(8,128)(2,1)S(1)}, bf16[8,7168]{1,0:T(8,128)(2,1)S(1)}, u32[]{:S(2)}, u32[]{:S(2)}) %collective-permute-start.14) | collective-permute-done | bytes 114720 | tf_op jit(solution)/shard_map/ppermute | solution.py:177
  49.3 0.0 collective-permute-done.17
  49.3 0.7 %add_convert_fusion = bf16[8,7168]{1,0:T(8,128)(2,1)} fusion(bf16[8,7168]{1,0:T(8,128)(2,1)S(1)} %collective-permute-done.17, bf16[8,7168]{1,0:T(8,128)(2,1)S(1)} %collective-permute-done.16, bf16[8,7168]{1,0:T(8,128)(2,1)S(1)} %collective-permute-done.14, bf16[8,7168]{1,0:T(8,128)(2,1)S(1)} %get-tuple-element.27), kind=kLoop, calls=%fused_computation | loop fusion | flops 458752 | bytes 573440 | tf_op jit(solution)/shard_map/convert_element_type | solution.py:242
  (2 shorter events, 0.0 us)
Async XLA Ops:
  0.0 22.5 %copy-start = (bf16[2,7168,512]{2,1,0:T(8,128)(2,1)S(1)}, bf16[2,7168,512]{2,1,0:T(8,128)(2,1)}, u32[]{:S(2)}) copy-start(bf16[2,7168,512]{2,1,0:T(8,128)(2,1)} %refs_4_.3) | copy-start | bytes 44040196
  0.0 22.5 %copy-start.1 = (bf16[2,7168,512]{2,1,0:T(8,128)(2,1)S(1)}, bf16[2,7168,512]{2,1,0:T(8,128)(2,1)}, u32[]{:S(2)}) copy-start(bf16[2,7168,512]{2,1,0:T(8,128)(2,1)} %refs_5_.3) | copy-start | bytes 44040196
  1.2 7.5 %collective-permute-start.1 = (bf16[8,7296]{1,0:T(8,128)(2,1)S(1)}, bf16[8,7296]{1,0:T(8,128)(2,1)S(1)}, u32[]{:S(2)}, u32[]{:S(2)}) collective-permute-start(bf16[8,7296]{1,0:T(8,128)(2,1)S(1)} %pack.1.refs_0_), channel_id=1, source_target_pairs={{0,1},{1,0},{2,3},{3,2},{4,5},{5,4},{6,7},{7,6},{8,9},{9,8},{10,11... | collective-permute-start | bytes 350216 | tf_op jit(solution)/shard_map/ppermute | solution.py:177
  4.3 8.1 %collective-permute-start.2 = (bf16[8,7296]{1,0:T(8,128)(2,1)S(1)}, bf16[8,7296]{1,0:T(8,128)(2,1)S(1)}, u32[]{:S(2)}, u32[]{:S(2)}) collective-permute-start(bf16[8,7296]{1,0:T(8,128)(2,1)S(1)} %pack.1.refs_0_), channel_id=1, source_target_pairs={{0,2},{1,3},{2,0},{3,1},{4,6},{5,7},{6,4},{7,5},{8,10},{9,11},{10,... | collective-permute-start | bytes 350216 | tf_op jit(solution)/shard_map/ppermute | solution.py:177
  6.8 5.6 %collective-permute-start = (bf16[8,7296]{1,0:T(8,128)(2,1)S(1)}, bf16[8,7296]{1,0:T(8,128)(2,1)S(1)}, u32[]{:S(2)}, u32[]{:S(2)}) collective-permute-start(bf16[8,7296]{1,0:T(8,128)(2,1)S(1)} %pack.1.refs_0_), channel_id=1, source_target_pairs={{0,8},{4,12},{8,0},{12,4},{1,9},{5,13},{9,1},{13,5},{2,10},{6,14},... | collective-permute-start | bytes 350216 | tf_op jit(solution)/shard_map/ppermute | solution.py:173
  8.7 6.1 %collective-permute-start.3 = (bf16[8,7296]{1,0:T(8,128)(2,1)S(1)}, bf16[8,7296]{1,0:T(8,128)(2,1)S(1)}, u32[]{:S(2)}, u32[]{:S(2)}) collective-permute-start(bf16[8,7296]{1,0:T(8,128)(2,1)S(1)} %collective-permute-done.1.refs_2_), channel_id=1, source_target_pairs={{0,8},{4,12},{8,0},{12,4},{1,9},{5,13},{9,1},{13,5},{2,10},{6,14},... | collective-permute-start | bytes 350216 | tf_op jit(solution)/shard_map/ppermute | solution.py:173
  12.5 6.1 %collective-permute-start.5 = (bf16[8,7296]{1,0:T(8,128)(2,1)S(1)}, bf16[8,7296]{1,0:T(8,128)(2,1)S(1)}, u32[]{:S(2)}, u32[]{:S(2)}) collective-permute-start(bf16[8,7296]{1,0:T(8,128)(2,1)S(1)} %collective-permute-done.2.refs_3_), channel_id=1, source_target_pairs={{0,8},{4,12},{8,0},{12,4},{1,9},{5,13},{9,1},{13,5},{2,10},{6,14},... | collective-permute-start | bytes 350216 | tf_op jit(solution)/shard_map/ppermute | solution.py:173
  14.0 4.8 %collective-permute-start.4 = (bf16[8,7296]{1,0:T(8,128)(2,1)S(1)}, bf16[8,7296]{1,0:T(8,128)(2,1)S(1)}, u32[]{:S(2)}, u32[]{:S(2)}) collective-permute-start(bf16[8,7296]{1,0:T(8,128)(2,1)S(1)} %collective-permute-done.2.refs_3_), channel_id=1, source_target_pairs={{0,1},{1,0},{2,3},{3,2},{4,5},{5,4},{6,7},{7,6},{8,9},{9,8},{10,11... | collective-permute-start | bytes 350216 | tf_op jit(solution)/shard_map/ppermute | solution.py:177
  14.7 5.7 %collective-permute-start.6 = (bf16[8,7296]{1,0:T(8,128)(2,1)S(1)}, bf16[8,7296]{1,0:T(8,128)(2,1)S(1)}, u32[]{:S(2)}, u32[]{:S(2)}) collective-permute-start(bf16[8,7296]{1,0:T(8,128)(2,1)S(1)} %collective-permute-done.2.refs_3_), channel_id=1, source_target_pairs={{0,9},{1,8},{2,11},{3,10},{4,13},{5,12},{6,15},{7,14},{8,1},{9,0},... | collective-permute-start | bytes 350216 | tf_op jit(solution)/shard_map/ppermute | solution.py:183
  16.0 4.6 %collective-permute-start.7 = (bf16[32,7296]{1,0:T(8,128)(2,1)S(1)}, bf16[32,7296]{1,0:T(8,128)(2,1)S(1)}, u32[]{:S(2)}, u32[]{:S(2)}) collective-permute-start(bf16[32,7296]{1,0:T(8,128)(2,1)S(1)} %stack.2.refs_0_), channel_id=1, source_target_pairs={{0,4},{4,0},{8,12},{12,8},{1,5},{5,1},{9,13},{13,9},{2,6},{6,2},{1... | collective-permute-start | bytes 1400840 | tf_op jit(solution)/shard_map/ppermute | solution.py:169
  20.5 6.1 %slice-start = ((s8[14680064]{0:T(1024)(128)(4,1)}), s8[4194304]{0:T(1024)(128)(4,1)S(1)}, s32[]{:S(2)}) async-start(s8[14680064]{0:T(1024)(128)(4,1)} %bitcast.3), calls=%async_computation | async-start | bytes 8388608
  20.5 6.0 %slice-start.1 = ((s8[14680064]{0:T(1024)(128)(4,1)}), s8[4194304]{0:T(1024)(128)(4,1)S(1)}, s32[]{:S(2)}) async-start(s8[14680064]{0:T(1024)(128)(4,1)} %bitcast.3), calls=%async_computation.1 | async-start | bytes 8388608
  20.5 6.0 %slice-start.2 = ((s8[14680064]{0:T(1024)(128)(4,1)}), s8[4194304]{0:T(1024)(128)(4,1)S(1)}, s32[]{:S(2)}) async-start(s8[14680064]{0:T(1024)(128)(4,1)} %bitcast.3), calls=%async_computation.2 | async-start | bytes 8388608
  20.6 6.0 %slice-start.3 = ((s8[14680064]{0:T(1024)(128)(4,1)}), s8[2097152]{0:T(1024)(128)(4,1)S(1)}, s32[]{:S(2)}) async-start(s8[14680064]{0:T(1024)(128)(4,1)} %bitcast.3), calls=%async_computation.3 | async-start | bytes 4194304
  20.6 1.9 %collective-permute-start.8 = (bf16[32,7296]{1,0:T(8,128)(2,1)S(1)}, bf16[32,7296]{1,0:T(8,128)(2,1)S(1)}, u32[]{:S(2)}, u32[]{:S(2)}) collective-permute-start(bf16[32,7296]{1,0:T(8,128)(2,1)S(1)} %stack.3.refs_1_), channel_id=1, source_target_pairs={{0,4},{4,0},{8,12},{12,8},{1,5},{5,1},{9,13},{13,9},{2,6},{6,2},{1... | collective-permute-start | bytes 1400840 | tf_op jit(solution)/shard_map/ppermute | solution.py:169
  28.7 1.9 %collective-permute-start.9 = (bf16[32,7168]{1,0:T(8,128)(2,1)S(1)}, bf16[32,7168]{1,0:T(8,128)(2,1)S(1)}, u32[]{:S(2)}, u32[]{:S(2)}) collective-permute-start(bf16[32,7168]{1,0:T(8,128)(2,1)S(1)} %get-tuple-element.25), channel_id=1, source_target_pairs={{0,4},{4,0},{8,12},{12,8},{1,5},{5,1},{9,13},{13,9},{2,6},{6,2},{1... | collective-permute-start | bytes 1376264 | tf_op jit(solution)/shard_map/ppermute | solution.py:169
  30.5 5.5 %collective-permute-start.10 = (bf16[32,7168]{1,0:T(8,128)(2,1)S(1)}, bf16[32,7168]{1,0:T(8,128)(2,1)S(1)}, u32[]{:S(2)}, u32[]{:S(2)}) collective-permute-start(bf16[32,7168]{1,0:T(8,128)(2,1)S(1)} %get-tuple-element.26), channel_id=1, source_target_pairs={{0,4},{4,0},{8,12},{12,8},{1,5},{5,1},{9,13},{13,9},{2,6},{6,2},{1... | collective-permute-start | bytes 1376264 | tf_op jit(solution)/shard_map/ppermute | solution.py:169
  30.8 6.0 %collective-permute-start.15 = (bf16[8,7168]{1,0:T(8,128)(2,1)S(1)}, bf16[8,7168]{1,0:T(8,128)(2,1)S(1)}, u32[]{:S(2)}, u32[]{:S(2)}) collective-permute-start(bf16[8,7168]{1,0:T(8,128)(2,1)S(1)} %get-tuple-element.34), channel_id=1, source_target_pairs={{0,8},{4,12},{8,0},{12,4},{1,9},{5,13},{9,1},{13,5},{2,10},{6,14},... | collective-permute-start | bytes 344072 | tf_op jit(solution)/shard_map/ppermute | solution.py:173
  32.6 6.0 %collective-permute-start.11 = (bf16[8,7168]{1,0:T(8,128)(2,1)S(1)}, bf16[8,7168]{1,0:T(8,128)(2,1)S(1)}, u32[]{:S(2)}, u32[]{:S(2)}) collective-permute-start(bf16[8,7168]{1,0:T(8,128)(2,1)S(1)} %get-tuple-element.30), channel_id=1, source_target_pairs={{0,1},{1,0},{2,3},{3,2},{4,5},{5,4},{6,7},{7,6},{8,9},{9,8},{10,11... | collective-permute-start | bytes 344072 | tf_op jit(solution)/shard_map/ppermute | solution.py:177
  32.7 8.5 %collective-permute-start.12 = (bf16[8,7168]{1,0:T(8,128)(2,1)S(1)}, bf16[8,7168]{1,0:T(8,128)(2,1)S(1)}, u32[]{:S(2)}, u32[]{:S(2)}) collective-permute-start(bf16[8,7168]{1,0:T(8,128)(2,1)S(1)} %get-tuple-element.31), channel_id=1, source_target_pairs={{0,8},{4,12},{8,0},{12,4},{1,9},{5,13},{9,1},{13,5},{2,10},{6,14},... | collective-permute-start | bytes 344072 | tf_op jit(solution)/shard_map/ppermute | solution.py:173
  34.2 7.0 %collective-permute-start.13 = (bf16[8,7168]{1,0:T(8,128)(2,1)S(1)}, bf16[8,7168]{1,0:T(8,128)(2,1)S(1)}, u32[]{:S(2)}, u32[]{:S(2)}) collective-permute-start(bf16[8,7168]{1,0:T(8,128)(2,1)S(1)} %get-tuple-element.32), channel_id=1, source_target_pairs={{0,9},{1,8},{2,11},{3,10},{4,13},{5,12},{6,15},{7,14},{8,1},{9,0},... | collective-permute-start | bytes 344072 | tf_op jit(solution)/shard_map/ppermute | solution.py:183
  36.9 6.6 %collective-permute-start.16 = (bf16[8,7168]{1,0:T(8,128)(2,1)S(1)}, bf16[8,7168]{1,0:T(8,128)(2,1)S(1)}, u32[]{:S(2)}, u32[]{:S(2)}) collective-permute-start(bf16[8,7168]{1,0:T(8,128)(2,1)S(1)} %add_convert_fusion.1), channel_id=1, source_target_pairs={{0,1},{1,0},{2,3},{3,2},{4,5},{5,4},{6,7},{7,6},{8,9},{9,8},{10,11... | collective-permute-start | bytes 344072 | tf_op jit(solution)/shard_map/ppermute | solution.py:177
  41.3 8.0 %collective-permute-start.14 = (bf16[8,7168]{1,0:T(8,128)(2,1)S(1)}, bf16[8,7168]{1,0:T(8,128)(2,1)S(1)}, u32[]{:S(2)}, u32[]{:S(2)}) collective-permute-start(bf16[8,7168]{1,0:T(8,128)(2,1)S(1)} %add_convert_fusion.2), channel_id=1, source_target_pairs={{0,2},{1,3},{2,0},{3,1},{4,6},{5,7},{6,4},{7,5},{8,10},{9,11},{10,... | collective-permute-start | bytes 344072 | tf_op jit(solution)/shard_map/ppermute | solution.py:177
  43.5 5.8 %collective-permute-start.17 = (bf16[8,7168]{1,0:T(8,128)(2,1)S(1)}, bf16[8,7168]{1,0:T(8,128)(2,1)S(1)}, u32[]{:S(2)}, u32[]{:S(2)}) collective-permute-start(bf16[8,7168]{1,0:T(8,128)(2,1)S(1)} %get-tuple-element.36), channel_id=1, source_target_pairs={{0,8},{4,12},{8,0},{12,4},{1,9},{5,13},{9,1},{13,5},{2,10},{6,14},... | collective-permute-start | bytes 344072 | tf_op jit(solution)/shard_map/ppermute | solution.py:173

commit v17 on v16

--- a/solution.py
+++ b/solution.py
@@ -189,10 +189,9 @@
 
 def gather_blocks(own):
     second, first, far_own = to_place(own, 2), to_place(own, 1), to_chip(own)
-    far_first = to_chip(first)
-    ready = after(second, far_own)
-    far_second, third = to_chip(ready), to_place(ready, 1)
-    far_third = to_both(after(ready, far_first), 1)
+    far_first = to_both(own, 1)
+    far_second, third = to_chip(second), to_place(second, 1)
+    far_third = to_both(after(second, first), 1)
     early = stack(own, far_own, first, second)
     late = stack(far_first, third, far_second, far_third)
     return [early, late, to_core(early), to_core(late)]

time: 50.1 us -> 50.6 us (level)
  waiting for transfers between devices: 18.3 us -> 22.6 us
  starting transfers between devices: 23.1 us -> 19.2 us
    ppermute x6 -> x5, starting transfers between devices: 9.43 us -> 5.17 us  [to_chip(): return lax.ppermute(value, 'node', [(i, i ^ 2) for i in range(2 * CHIPS)])]
    ppermute x6 -> x5, waiting for transfers between devices: 5.84 us -> 8.46 us  [to_chip(): return lax.ppermute(value, 'node', [(i, i ^ 2) for i in range(2 * CHIPS)])]
    ppermute x6, waiting for transfers between devices: 7.26 us -> 8.43 us  [to_place(): return lax.ppermute(value, 'local', [(i, i ^ bits) for i in range(PLACES)])]
    ppermute x6, starting transfers between devices: 10.1 us -> 10.6 us  [to_place(): return lax.ppermute(value, 'local', [(i, i ^ bits) for i in range(PLACES)])]
    ppermute x2 -> x3, waiting for transfers between devices: 1.68 us -> 2.19 us  [to_both(): return lax.ppermute(value, ('node', 'local'), perm)]
    ppermute x2 -> x3, starting transfers between devices: 3.11 us -> 2.97 us  [to_both(): return lax.ppermute(value, ('node', 'local'), perm)]
  transfers between devices with their start and end apart: 18 -> 18, of which waited for: 12 -> 11; matrix products, arithmetic and copies ran while one was open for 0% -> 0% of each run, Pallas kernels for 1% -> 1%
where the time goes in v17:
time: 50.6 us; the launch traced here: 50.5 us
  waiting for transfers between devices  22.6 us (45%)
  starting transfers between devices  19.2 us (38%)
  Pallas kernels  7.65 us (15%)
  other arithmetic  0.8 us (2%)
    ppermute x6, starting transfers between devices, to_place(): return lax.ppermute(value, 'local', [(i, i ^ bits) for i in range(PLACES)])  10.6 us
    ppermute x5, waiting for transfers between devices, to_chip(): return lax.ppermute(value, 'node', [(i, i ^ 2) for i in range(2 * CHIPS)])  8.46 us
    ppermute x6, waiting for transfers between devices, to_place(): return lax.ppermute(value, 'local', [(i, i ^ bits) for i in range(PLACES)])  8.43 us
    ppermute x5, starting transfers between devices, to_chip(): return lax.ppermute(value, 'node', [(i, i ^ 2) for i in range(2 * CHIPS)])  5.17 us
    pallas_call x1, Pallas kernels, hidden_units(): pl.pallas_call(functools.partial(hidden_kernel, experts), out_shape=jax.S...  4.05 us
    ppermute x4, waiting for transfers between devices, to_core(): return lax.ppermute(value, 'node', [(i, i ^ 1) for i in range(2 * CHIPS)])  3.5 us
    ppermute x3, starting transfers between devices, to_both(): return lax.ppermute(value, ('node', 'local'), perm)  2.97 us
    ppermute x3, waiting for transfers between devices, to_both(): return lax.ppermute(value, ('node', 'local'), perm)  2.19 us
  transfers between devices with their start and end apart: 18, of which 11 were waited for; matrix products, arithmetic and copies ran while one was open for 0% of the time, Pallas kernels for 1%

profile of v17, /device:TPU:0, one launch (start us, length us, event | category | flops | bytes accessed | tf_op | source)
XLA Modules:
  0.0 50.5 jit_solution(8792706210703860110)
XLA Ops:
  0.0 0.0 copy-start
  0.0 0.0 copy-start.1
  0.0 1.2 %pack.1.refs_0_ = bf16[8,7296]{1,0:T(8,128)(2,1)S(1)} custom-call(bf16[8,7168]{1,0:T(8,128)(2,1)} %refs_0_.1, s32[4,8]{1,0:T(4,128)} %bitcast.6, f32[4,8]{1,0:T(4,128)} %bitcast.7, s32[8]{0:T(128)} %refs_3_.1, bf16[2,7168,512]{2,1,0:T(8,128)(2,1)} %refs_4_.3, bf16[2,7168,512]{2,1,0:T(8,128)(2,1)} %refs_5_.3, bf16[2,512,7168]{2,1,0:T(8,128)(2,1)} %refs_6_.1), custom_call_target="tpu_custom_call" | custom-call | tf_op jit(solution)/shard_map/pack/pallas_call | solution.py:50
  1.2 4.1 %collective-permute-start.2 = (bf16[8,7296]{1,0:T(8,128)(2,1)S(1)}, bf16[8,7296]{1,0:T(8,128)(2,1)S(1)}, u32[]{:S(2)}, u32[]{:S(2)}) collective-permute-start(bf16[8,7296]{1,0:T(8,128)(2,1)S(1)} %pack.1.refs_0_), channel_id=1, source_target_pairs={{0,2},{1,3},{2,0},{3,1},{4,6},{5,7},{6,4},{7,5},{8,10},{9,11},{10,... | collective-permute-start | bytes 350216 | tf_op jit(solution)/shard_map/ppermute | solution.py:177
  5.3 1.6 %collective-permute-start.1 = (bf16[8,7296]{1,0:T(8,128)(2,1)S(1)}, bf16[8,7296]{1,0:T(8,128)(2,1)S(1)}, u32[]{:S(2)}, u32[]{:S(2)}) collective-permute-start(bf16[8,7296]{1,0:T(8,128)(2,1)S(1)} %pack.1.refs_0_), channel_id=1, source_target_pairs={{0,1},{1,0},{2,3},{3,2},{4,5},{5,4},{6,7},{7,6},{8,9},{9,8},{10,11... | collective-permute-start | bytes 350216 | tf_op jit(solution)/shard_map/ppermute | solution.py:177
  6.8 1.4 %collective-permute-start.3 = (bf16[8,7296]{1,0:T(8,128)(2,1)S(1)}, bf16[8,7296]{1,0:T(8,128)(2,1)S(1)}, u32[]{:S(2)}, u32[]{:S(2)}) collective-permute-start(bf16[8,7296]{1,0:T(8,128)(2,1)S(1)} %pack.1.refs_0_), channel_id=1, source_target_pairs={{0,9},{1,8},{2,11},{3,10},{4,13},{5,12},{6,15},{7,14},{8,1},{9,0},... | collective-permute-start | bytes 350216 | tf_op jit(solution)/shard_map/ppermute | solution.py:183
  8.2 0.5 %collective-permute-start = (bf16[8,7296]{1,0:T(8,128)(2,1)S(1)}, bf16[8,7296]{1,0:T(8,128)(2,1)S(1)}, u32[]{:S(2)}, u32[]{:S(2)}) collective-permute-start(bf16[8,7296]{1,0:T(8,128)(2,1)S(1)} %pack.1.refs_0_), channel_id=1, source_target_pairs={{0,8},{4,12},{8,0},{12,4},{1,9},{5,13},{9,1},{13,5},{2,10},{6,14},... | collective-permute-start | bytes 350216 | tf_op jit(solution)/shard_map/ppermute | solution.py:173
  8.8 2.3 %collective-permute-done.2.refs_3_ = bf16[8,7296]{1,0:T(8,128)(2,1)S(1)} collective-permute-done((bf16[8,7296]{1,0:T(8,128)(2,1)S(1)}, bf16[8,7296]{1,0:T(8,128)(2,1)S(1)}, u32[]{:S(2)}, u32[]{:S(2)}) %collective-permute-start.2) | collective-permute-done | bytes 116768 | tf_op jit(solution)/shard_map/ppermute | solution.py:177
  11.1 1.1 %collective-permute-done.1.refs_2_ = bf16[8,7296]{1,0:T(8,128)(2,1)S(1)} collective-permute-done((bf16[8,7296]{1,0:T(8,128)(2,1)S(1)}, bf16[8,7296]{1,0:T(8,128)(2,1)S(1)}, u32[]{:S(2)}, u32[]{:S(2)}) %collective-permute-start.1) | collective-permute-done | bytes 116768 | tf_op jit(solution)/shard_map/ppermute | solution.py:177
  12.2 1.9 %collective-permute-start.5 = (bf16[8,7296]{1,0:T(8,128)(2,1)S(1)}, bf16[8,7296]{1,0:T(8,128)(2,1)S(1)}, u32[]{:S(2)}, u32[]{:S(2)}) collective-permute-start(bf16[8,7296]{1,0:T(8,128)(2,1)S(1)} %collective-permute-done.2.refs_3_), channel_id=1, source_target_pairs={{0,8},{4,12},{8,0},{12,4},{1,9},{5,13},{9,1},{13,5},{2,10},{6,14},... | collective-permute-start | bytes 350216 | tf_op jit(solution)/shard_map/ppermute | solution.py:173
  14.1 1.3 %collective-permute-start.4 = (bf16[8,7296]{1,0:T(8,128)(2,1)S(1)}, bf16[8,7296]{1,0:T(8,128)(2,1)S(1)}, u32[]{:S(2)}, u32[]{:S(2)}) collective-permute-start(bf16[8,7296]{1,0:T(8,128)(2,1)S(1)} %collective-permute-done.2.refs_3_), channel_id=1, source_target_pairs={{0,1},{1,0},{2,3},{3,2},{4,5},{5,4},{6,7},{7,6},{8,9},{9,8},{10,11... | collective-permute-start | bytes 350216 | tf_op jit(solution)/shard_map/ppermute | solution.py:177
  15.3 0.3 collective-permute-start.6
  15.7 0.3 collective-permute-done.refs_1_
  15.9 0.1 stack.2.refs_0_
  16.0 0.1 collective-permute-start.7
  16.1 0.0 collective-permute-done.3.refs_0_
  16.1 2.6 %collective-permute-done.5.refs_2_ = bf16[8,7296]{1,0:T(8,128)(2,1)S(1)} collective-permute-done((bf16[8,7296]{1,0:T(8,128)(2,1)S(1)}, bf16[8,7296]{1,0:T(8,128)(2,1)S(1)}, u32[]{:S(2)}, u32[]{:S(2)}) %collective-permute-start.5) | collective-permute-done | bytes 116768 | tf_op jit(solution)/shard_map/ppermute | solution.py:173
  18.7 0.1 collective-permute-done.4.refs_1_
  18.9 2.2 %collective-permute-done.6.refs_3_ = bf16[8,7296]{1,0:T(8,128)(2,1)S(1)} collective-permute-done((bf16[8,7296]{1,0:T(8,128)(2,1)S(1)}, bf16[8,7296]{1,0:T(8,128)(2,1)S(1)}, u32[]{:S(2)}, u32[]{:S(2)}) %collective-permute-start.6) | collective-permute-done | bytes 116768 | tf_op jit(solution)/shard_map/ppermute | solution.py:183
  21.1 0.0 slice-start
  21.1 0.1 stack.3.refs_1_
  21.1 0.0 slice-start.1
  21.1 0.0 slice-start.2
  21.2 0.0 slice-start.3
  21.2 0.1 collective-permute-start.8
  21.2 0.0 collective-permute-done.7.refs_2_
  21.3 1.8 %collective-permute-done.8.refs_3_ = bf16[32,7296]{1,0:T(8,128)(2,1)S(1)} collective-permute-done((bf16[32,7296]{1,0:T(8,128)(2,1)S(1)}, bf16[32,7296]{1,0:T(8,128)(2,1)S(1)}, u32[]{:S(2)}, u32[]{:S(2)}) %collective-permute-start.8) | collective-permute-done | bytes 466976 | tf_op jit(solution)/shard_map/ppermute | solution.py:169
  23.1 0.0 copy-done
  23.1 0.0 copy-done.1
  23.1 4.0 %hidden.1.hidden_ref = bf16[128,1024]{1,0:T(8,128)(2,1)S(1)} custom-call(bf16[32,7296]{1,0:T(8,128)(2,1)S(1)} %stack.2.refs_0_, bf16[32,7296]{1,0:T(8,128)(2,1)S(1)} %stack.3.refs_1_, bf16[32,7296]{1,0:T(8,128)(2,1)S(1)} %collective-permute-done.7.refs_2_, bf16[32,7296]{1,0:T(8,128)(2,1)S(1)} %collective-permute-done.8.refs_3_, ...), custom_call_target="tpu_custom_call" | custom-call | flops 3758096384 | bytes 29360128 | tf_op jit(solution)/shard_map/hidden/pallas_call | solution.py:113
  27.1 0.0 slice-done
  27.1 0.0 slice-done.1
  27.1 0.0 slice-done.2
  27.2 0.0 slice-done.3
  27.2 2.1 %down.1 = (bf16[32,7168]{1,0:T(8,128)(2,1)S(1)}, bf16[32,7168]{1,0:T(8,128)(2,1)S(1)}, bf16[32,7168]{1,0:T(8,128)(2,1)S(1)}, bf16[32,7168]{1,0:T(8,128)(2,1)S(1)}) custom-call(bf16[128,1024]{1,0:T(8,128)(2,1)S(1)} %hidden.1.hidden_ref, bf16[1024,7168]{1,0:T(8,128)(2,1)S(1)} %bitcast.5), custom_call_target="tpu_custom_call" | custom-call | flops 1879048192 | bytes 14680064 | tf_op jit(solution)/shard_map/down/pallas_call | solution.py:150
  29.3 0.2 collective-permute-start.9
  29.5 1.7 %collective-permute-done.9.refs_1_ = bf16[32,7168]{1,0:T(8,128)(2,1)S(1)} collective-permute-done((bf16[32,7168]{1,0:T(8,128)(2,1)S(1)}, bf16[32,7168]{1,0:T(8,128)(2,1)S(1)}, u32[]{:S(2)}, u32[]{:S(2)}) %collective-permute-start.9) | collective-permute-done | bytes 458784 | tf_op jit(solution)/shard_map/ppermute | solution.py:169
  31.1 0.1 collective-permute-start.10
  31.3 0.1 sums.3
  31.4 0.6 %collective-permute-start.15 = (bf16[8,7168]{1,0:T(8,128)(2,1)S(1)}, bf16[8,7168]{1,0:T(8,128)(2,1)S(1)}, u32[]{:S(2)}, u32[]{:S(2)}) collective-permute-start(bf16[8,7168]{1,0:T(8,128)(2,1)S(1)} %get-tuple-element.32), channel_id=1, source_target_pairs={{0,8},{4,12},{8,0},{12,4},{1,9},{5,13},{9,1},{13,5},{2,10},{6,14},... | collective-permute-start | bytes 344072 | tf_op jit(solution)/shard_map/ppermute | solution.py:173
  32.0 1.3 %collective-permute-start.11 = (bf16[8,7168]{1,0:T(8,128)(2,1)S(1)}, bf16[8,7168]{1,0:T(8,128)(2,1)S(1)}, u32[]{:S(2)}, u32[]{:S(2)}) collective-permute-start(bf16[8,7168]{1,0:T(8,128)(2,1)S(1)} %get-tuple-element.28), channel_id=1, source_target_pairs={{0,1},{1,0},{2,3},{3,2},{4,5},{5,4},{6,7},{7,6},{8,9},{9,8},{10,11... | collective-permute-start | bytes 344072 | tf_op jit(solution)/shard_map/ppermute | solution.py:177
  33.3 0.9 %collective-permute-start.12 = (bf16[8,7168]{1,0:T(8,128)(2,1)S(1)}, bf16[8,7168]{1,0:T(8,128)(2,1)S(1)}, u32[]{:S(2)}, u32[]{:S(2)}) collective-permute-start(bf16[8,7168]{1,0:T(8,128)(2,1)S(1)} %get-tuple-element.29), channel_id=1, source_target_pairs={{0,8},{4,12},{8,0},{12,4},{1,9},{5,13},{9,1},{13,5},{2,10},{6,14},... | collective-permute-start | bytes 344072 | tf_op jit(solution)/shard_map/ppermute | solution.py:173
  34.2 1.3 %collective-permute-start.13 = (bf16[8,7168]{1,0:T(8,128)(2,1)S(1)}, bf16[8,7168]{1,0:T(8,128)(2,1)S(1)}, u32[]{:S(2)}, u32[]{:S(2)}) collective-permute-start(bf16[8,7168]{1,0:T(8,128)(2,1)S(1)} %get-tuple-element.30), channel_id=1, source_target_pairs={{0,9},{1,8},{2,11},{3,10},{4,13},{5,12},{6,15},{7,14},{8,1},{9,0},... | collective-permute-start | bytes 344072 | tf_op jit(solution)/shard_map/ppermute | solution.py:183
  35.5 0.0 collective-permute-done.10.refs_1_
  35.5 0.1 sums.2
  35.6 2.0 %collective-permute-done.15 = bf16[8,7168]{1,0:T(8,128)(2,1)S(1)} collective-permute-done((bf16[8,7168]{1,0:T(8,128)(2,1)S(1)}, bf16[8,7168]{1,0:T(8,128)(2,1)S(1)}, u32[]{:S(2)}, u32[]{:S(2)}) %collective-permute-start.15) | collective-permute-done | bytes 114720 | tf_op jit(solution)/shard_map/ppermute | solution.py:173
  37.7 0.6 %collective-permute-start.16 = (bf16[8,7168]{1,0:T(8,128)(2,1)S(1)}, bf16[8,7168]{1,0:T(8,128)(2,1)S(1)}, u32[]{:S(2)}, u32[]{:S(2)}) collective-permute-start(bf16[8,7168]{1,0:T(8,128)(2,1)S(1)} %add_convert_fusion.1), channel_id=1, source_target_pairs={{0,1},{1,0},{2,3},{3,2},{4,5},{5,4},{6,7},{7,6},{8,9},{9,8},{10,11... | collective-permute-start | bytes 344072 | tf_op jit(solution)/shard_map/ppermute | solution.py:177
  38.3 0.0 collective-permute-done.11
  38.3 3.5 %collective-permute-done.12 = bf16[8,7168]{1,0:T(8,128)(2,1)S(1)} collective-permute-done((bf16[8,7168]{1,0:T(8,128)(2,1)S(1)}, bf16[8,7168]{1,0:T(8,128)(2,1)S(1)}, u32[]{:S(2)}, u32[]{:S(2)}) %collective-permute-start.12) | collective-permute-done | bytes 114720 | tf_op jit(solution)/shard_map/ppermute | solution.py:173
  41.8 0.0 collective-permute-done.13
  41.8 0.1 add_convert_fusion.2
  41.9 1.8 %collective-permute-start.14 = (bf16[8,7168]{1,0:T(8,128)(2,1)S(1)}, bf16[8,7168]{1,0:T(8,128)(2,1)S(1)}, u32[]{:S(2)}, u32[]{:S(2)}) collective-permute-start(bf16[8,7168]{1,0:T(8,128)(2,1)S(1)} %add_convert_fusion.2), channel_id=1, source_target_pairs={{0,2},{1,3},{2,0},{3,1},{4,6},{5,7},{6,4},{7,5},{8,10},{9,11},{10,... | collective-permute-start | bytes 344072 | tf_op jit(solution)/shard_map/ppermute | solution.py:177
  43.7 0.0 collective-permute-done.16
  43.7 1.2 %collective-permute-start.17 = (bf16[8,7168]{1,0:T(8,128)(2,1)S(1)}, bf16[8,7168]{1,0:T(8,128)(2,1)S(1)}, u32[]{:S(2)}, u32[]{:S(2)}) collective-permute-start(bf16[8,7168]{1,0:T(8,128)(2,1)S(1)} %get-tuple-element.34), channel_id=1, source_target_pairs={{0,8},{4,12},{8,0},{12,4},{1,9},{5,13},{9,1},{13,5},{2,10},{6,14},... | collective-permute-start | bytes 344072 | tf_op jit(solution)/shard_map/ppermute | solution.py:173
  44.9 4.9 %collective-permute-done.14 = bf16[8,7168]{1,0:T(8,128)(2,1)S(1)} collective-permute-done((bf16[8,7168]{1,0:T(8,128)(2,1)S(1)}, bf16[8,7168]{1,0:T(8,128)(2,1)S(1)}, u32[]{:S(2)}, u32[]{:S(2)}) %collective-permute-start.14) | collective-permute-done | bytes 114720 | tf_op jit(solution)/shard_map/ppermute | solution.py:177
  49.7 0.0 collective-permute-done.17
  49.7 0.7 %add_convert_fusion = bf16[8,7168]{1,0:T(8,128)(2,1)} fusion(bf16[8,7168]{1,0:T(8,128)(2,1)S(1)} %collective-permute-done.17, bf16[8,7168]{1,0:T(8,128)(2,1)S(1)} %collective-permute-done.16, bf16[8,7168]{1,0:T(8,128)(2,1)S(1)} %collective-permute-done.14, bf16[8,7168]{1,0:T(8,128)(2,1)S(1)} %get-tuple-element.25), kind=kLoop, calls=%fused_computation | loop fusion | flops 458752 | bytes 573440 | tf_op jit(solution)/shard_map/convert_element_type | solution.py:241
  (2 shorter events, 0.0 us)
Async XLA Ops:
  0.0 23.1 %copy-start = (bf16[2,7168,512]{2,1,0:T(8,128)(2,1)S(1)}, bf16[2,7168,512]{2,1,0:T(8,128)(2,1)}, u32[]{:S(2)}) copy-start(bf16[2,7168,512]{2,1,0:T(8,128)(2,1)} %refs_4_.3) | copy-start | bytes 44040196
  0.0 23.1 %copy-start.1 = (bf16[2,7168,512]{2,1,0:T(8,128)(2,1)S(1)}, bf16[2,7168,512]{2,1,0:T(8,128)(2,1)}, u32[]{:S(2)}) copy-start(bf16[2,7168,512]{2,1,0:T(8,128)(2,1)} %refs_5_.3) | copy-start | bytes 44040196
  1.2 9.9 %collective-permute-start.2 = (bf16[8,7296]{1,0:T(8,128)(2,1)S(1)}, bf16[8,7296]{1,0:T(8,128)(2,1)S(1)}, u32[]{:S(2)}, u32[]{:S(2)}) collective-permute-start(bf16[8,7296]{1,0:T(8,128)(2,1)S(1)} %pack.1.refs_0_), channel_id=1, source_target_pairs={{0,2},{1,3},{2,0},{3,1},{4,6},{5,7},{6,4},{7,5},{8,10},{9,11},{10,... | collective-permute-start | bytes 350216 | tf_op jit(solution)/shard_map/ppermute | solution.py:177
  5.3 6.9 %collective-permute-start.1 = (bf16[8,7296]{1,0:T(8,128)(2,1)S(1)}, bf16[8,7296]{1,0:T(8,128)(2,1)S(1)}, u32[]{:S(2)}, u32[]{:S(2)}) collective-permute-start(bf16[8,7296]{1,0:T(8,128)(2,1)S(1)} %pack.1.refs_0_), channel_id=1, source_target_pairs={{0,1},{1,0},{2,3},{3,2},{4,5},{5,4},{6,7},{7,6},{8,9},{9,8},{10,11... | collective-permute-start | bytes 350216 | tf_op jit(solution)/shard_map/ppermute | solution.py:177
  6.8 9.2 %collective-permute-start.3 = (bf16[8,7296]{1,0:T(8,128)(2,1)S(1)}, bf16[8,7296]{1,0:T(8,128)(2,1)S(1)}, u32[]{:S(2)}, u32[]{:S(2)}) collective-permute-start(bf16[8,7296]{1,0:T(8,128)(2,1)S(1)} %pack.1.refs_0_), channel_id=1, source_target_pairs={{0,9},{1,8},{2,11},{3,10},{4,13},{5,12},{6,15},{7,14},{8,1},{9,0},... | collective-permute-start | bytes 350216 | tf_op jit(solution)/shard_map/ppermute | solution.py:183
  8.2 7.7 %collective-permute-start = (bf16[8,7296]{1,0:T(8,128)(2,1)S(1)}, bf16[8,7296]{1,0:T(8,128)(2,1)S(1)}, u32[]{:S(2)}, u32[]{:S(2)}) collective-permute-start(bf16[8,7296]{1,0:T(8,128)(2,1)S(1)} %pack.1.refs_0_), channel_id=1, source_target_pairs={{0,8},{4,12},{8,0},{12,4},{1,9},{5,13},{9,1},{13,5},{2,10},{6,14},... | collective-permute-start | bytes 350216 | tf_op jit(solution)/shard_map/ppermute | solution.py:173
  12.2 6.6 %collective-permute-start.5 = (bf16[8,7296]{1,0:T(8,128)(2,1)S(1)}, bf16[8,7296]{1,0:T(8,128)(2,1)S(1)}, u32[]{:S(2)}, u32[]{:S(2)}) collective-permute-start(bf16[8,7296]{1,0:T(8,128)(2,1)S(1)} %collective-permute-done.2.refs_3_), channel_id=1, source_target_pairs={{0,8},{4,12},{8,0},{12,4},{1,9},{5,13},{9,1},{13,5},{2,10},{6,14},... | collective-permute-start | bytes 350216 | tf_op jit(solution)/shard_map/ppermute | solution.py:173
  14.1 4.8 %collective-permute-start.4 = (bf16[8,7296]{1,0:T(8,128)(2,1)S(1)}, bf16[8,7296]{1,0:T(8,128)(2,1)S(1)}, u32[]{:S(2)}, u32[]{:S(2)}) collective-permute-start(bf16[8,7296]{1,0:T(8,128)(2,1)S(1)} %collective-permute-done.2.refs_3_), channel_id=1, source_target_pairs={{0,1},{1,0},{2,3},{3,2},{4,5},{5,4},{6,7},{7,6},{8,9},{9,8},{10,11... | collective-permute-start | bytes 350216 | tf_op jit(solution)/shard_map/ppermute | solution.py:177
  15.3 5.7 %collective-permute-start.6 = (bf16[8,7296]{1,0:T(8,128)(2,1)S(1)}, bf16[8,7296]{1,0:T(8,128)(2,1)S(1)}, u32[]{:S(2)}, u32[]{:S(2)}) collective-permute-start(bf16[8,7296]{1,0:T(8,128)(2,1)S(1)} %collective-permute-done.2.refs_3_), channel_id=1, source_target_pairs={{0,9},{1,8},{2,11},{3,10},{4,13},{5,12},{6,15},{7,14},{8,1},{9,0},... | collective-permute-start | bytes 350216 | tf_op jit(solution)/shard_map/ppermute | solution.py:183
  16.0 5.3 %collective-permute-start.7 = (bf16[32,7296]{1,0:T(8,128)(2,1)S(1)}, bf16[32,7296]{1,0:T(8,128)(2,1)S(1)}, u32[]{:S(2)}, u32[]{:S(2)}) collective-permute-start(bf16[32,7296]{1,0:T(8,128)(2,1)S(1)} %stack.2.refs_0_), channel_id=1, source_target_pairs={{0,4},{4,0},{8,12},{12,8},{1,5},{5,1},{9,13},{13,9},{2,6},{6,2},{1... | collective-permute-start | bytes 1400840 | tf_op jit(solution)/shard_map/ppermute | solution.py:169
  21.1 6.1 %slice-start = ((s8[14680064]{0:T(1024)(128)(4,1)}), s8[4194304]{0:T(1024)(128)(4,1)S(1)}, s32[]{:S(2)}) async-start(s8[14680064]{0:T(1024)(128)(4,1)} %bitcast.3), calls=%async_computation | async-start | bytes 8388608
  21.1 6.0 %slice-start.1 = ((s8[14680064]{0:T(1024)(128)(4,1)}), s8[4194304]{0:T(1024)(128)(4,1)S(1)}, s32[]{:S(2)}) async-start(s8[14680064]{0:T(1024)(128)(4,1)} %bitcast.3), calls=%async_computation.1 | async-start | bytes 8388608
  21.1 6.0 %slice-start.2 = ((s8[14680064]{0:T(1024)(128)(4,1)}), s8[4194304]{0:T(1024)(128)(4,1)S(1)}, s32[]{:S(2)}) async-start(s8[14680064]{0:T(1024)(128)(4,1)} %bitcast.3), calls=%async_computation.2 | async-start | bytes 8388608
  21.2 6.0 %slice-start.3 = ((s8[14680064]{0:T(1024)(128)(4,1)}), s8[2097152]{0:T(1024)(128)(4,1)S(1)}, s32[]{:S(2)}) async-start(s8[14680064]{0:T(1024)(128)(4,1)} %bitcast.3), calls=%async_computation.3 | async-start | bytes 4194304
  21.2 1.9 %collective-permute-start.8 = (bf16[32,7296]{1,0:T(8,128)(2,1)S(1)}, bf16[32,7296]{1,0:T(8,128)(2,1)S(1)}, u32[]{:S(2)}, u32[]{:S(2)}) collective-permute-start(bf16[32,7296]{1,0:T(8,128)(2,1)S(1)} %stack.3.refs_1_), channel_id=1, source_target_pairs={{0,4},{4,0},{8,12},{12,8},{1,5},{5,1},{9,13},{13,9},{2,6},{6,2},{1... | collective-permute-start | bytes 1400840 | tf_op jit(solution)/shard_map/ppermute | solution.py:169
  29.3 1.9 %collective-permute-start.9 = (bf16[32,7168]{1,0:T(8,128)(2,1)S(1)}, bf16[32,7168]{1,0:T(8,128)(2,1)S(1)}, u32[]{:S(2)}, u32[]{:S(2)}) collective-permute-start(bf16[32,7168]{1,0:T(8,128)(2,1)S(1)} %get-tuple-element.23), channel_id=1, source_target_pairs={{0,4},{4,0},{8,12},{12,8},{1,5},{5,1},{9,13},{13,9},{2,6},{6,2},{1... | collective-permute-start | bytes 1376264 | tf_op jit(solution)/shard_map/ppermute | solution.py:169
  31.1 4.4 %collective-permute-start.10 = (bf16[32,7168]{1,0:T(8,128)(2,1)S(1)}, bf16[32,7168]{1,0:T(8,128)(2,1)S(1)}, u32[]{:S(2)}, u32[]{:S(2)}) collective-permute-start(bf16[32,7168]{1,0:T(8,128)(2,1)S(1)} %get-tuple-element.24), channel_id=1, source_target_pairs={{0,4},{4,0},{8,12},{12,8},{1,5},{5,1},{9,13},{13,9},{2,6},{6,2},{1... | collective-permute-start | bytes 1376264 | tf_op jit(solution)/shard_map/ppermute | solution.py:169
  31.4 6.3 %collective-permute-start.15 = (bf16[8,7168]{1,0:T(8,128)(2,1)S(1)}, bf16[8,7168]{1,0:T(8,128)(2,1)S(1)}, u32[]{:S(2)}, u32[]{:S(2)}) collective-permute-start(bf16[8,7168]{1,0:T(8,128)(2,1)S(1)} %get-tuple-element.32), channel_id=1, source_target_pairs={{0,8},{4,12},{8,0},{12,4},{1,9},{5,13},{9,1},{13,5},{2,10},{6,14},... | collective-permute-start | bytes 344072 | tf_op jit(solution)/shard_map/ppermute | solution.py:173
  32.0 6.2 %collective-permute-start.11 = (bf16[8,7168]{1,0:T(8,128)(2,1)S(1)}, bf16[8,7168]{1,0:T(8,128)(2,1)S(1)}, u32[]{:S(2)}, u32[]{:S(2)}) collective-permute-start(bf16[8,7168]{1,0:T(8,128)(2,1)S(1)} %get-tuple-element.28), channel_id=1, source_target_pairs={{0,1},{1,0},{2,3},{3,2},{4,5},{5,4},{6,7},{7,6},{8,9},{9,8},{10,11... | collective-permute-start | bytes 344072 | tf_op jit(solution)/shard_map/ppermute | solution.py:177
  33.3 8.5 %collective-permute-start.12 = (bf16[8,7168]{1,0:T(8,128)(2,1)S(1)}, bf16[8,7168]{1,0:T(8,128)(2,1)S(1)}, u32[]{:S(2)}, u32[]{:S(2)}) collective-permute-start(bf16[8,7168]{1,0:T(8,128)(2,1)S(1)} %get-tuple-element.29), channel_id=1, source_target_pairs={{0,8},{4,12},{8,0},{12,4},{1,9},{5,13},{9,1},{13,5},{2,10},{6,14},... | collective-permute-start | bytes 344072 | tf_op jit(solution)/shard_map/ppermute | solution.py:173
  34.2 7.6 %collective-permute-start.13 = (bf16[8,7168]{1,0:T(8,128)(2,1)S(1)}, bf16[8,7168]{1,0:T(8,128)(2,1)S(1)}, u32[]{:S(2)}, u32[]{:S(2)}) collective-permute-start(bf16[8,7168]{1,0:T(8,128)(2,1)S(1)} %get-tuple-element.30), channel_id=1, source_target_pairs={{0,9},{1,8},{2,11},{3,10},{4,13},{5,12},{6,15},{7,14},{8,1},{9,0},... | collective-permute-start | bytes 344072 | tf_op jit(solution)/shard_map/ppermute | solution.py:183
  37.7 6.0 %collective-permute-start.16 = (bf16[8,7168]{1,0:T(8,128)(2,1)S(1)}, bf16[8,7168]{1,0:T(8,128)(2,1)S(1)}, u32[]{:S(2)}, u32[]{:S(2)}) collective-permute-start(bf16[8,7168]{1,0:T(8,128)(2,1)S(1)} %add_convert_fusion.1), channel_id=1, source_target_pairs={{0,1},{1,0},{2,3},{3,2},{4,5},{5,4},{6,7},{7,6},{8,9},{9,8},{10,11... | collective-permute-start | bytes 344072 | tf_op jit(solution)/shard_map/ppermute | solution.py:177
  41.9 7.9 %collective-permute-start.14 = (bf16[8,7168]{1,0:T(8,128)(2,1)S(1)}, bf16[8,7168]{1,0:T(8,128)(2,1)S(1)}, u32[]{:S(2)}, u32[]{:S(2)}) collective-permute-start(bf16[8,7168]{1,0:T(8,128)(2,1)S(1)} %add_convert_fusion.2), channel_id=1, source_target_pairs={{0,2},{1,3},{2,0},{3,1},{4,6},{5,7},{6,4},{7,5},{8,10},{9,11},{10,... | collective-permute-start | bytes 344072 | tf_op jit(solution)/shard_map/ppermute | solution.py:177
  43.7 6.1 %collective-permute-start.17 = (bf16[8,7168]{1,0:T(8,128)(2,1)S(1)}, bf16[8,7168]{1,0:T(8,128)(2,1)S(1)}, u32[]{:S(2)}, u32[]{:S(2)}) collective-permute-start(bf16[8,7168]{1,0:T(8,128)(2,1)S(1)} %get-tuple-element.34), channel_id=1, source_target_pairs={{0,8},{4,12},{8,0},{12,4},{1,9},{5,13},{9,1},{13,5},{2,10},{6,14},... | collective-permute-start | bytes 344072 | tf_op jit(solution)/shard_map/ppermute | solution.py:173

commit v18 on v14

--- a/solution.py
+++ b/solution.py
@@ -22,7 +22,7 @@
     ]
     for copy in copies:
         copy.start()
-    for copy in copies:
+    for copy in copies[1:]:
         copy.wait()
     tokens_ref, ids_ref, route_ref, slot_ref = local
     rows, width = tokens_ref.shape
@@ -39,6 +39,7 @@
     second = (weights - first).astype(jnp.bfloat16).astype(jnp.float32)
     third = weights - first - second
     tail = jnp.where(column < experts, first, jnp.where(column < 2 * experts, second, third))
+    copies[0].wait()
     out_ref[:, :width] = tokens_ref[...]
     out_ref[:, width:] = jnp.where(column < 3 * experts, tail, 0.0).astype(jnp.bfloat16)
 
@@ -237,7 +238,7 @@
     third = to_place(third, 1)
     second = total(second, far_second, far_third, third).astype(jnp.bfloat16)
     own, far_own, first, far_first = sums(early, other_early)
-    first = total(first, to_chip(after(far_first, third))).astype(jnp.bfloat16)
+    first = total(first, to_chip(after(far_first, far_second))).astype(jnp.bfloat16)
     first, far_own = lax.optimization_barrier((first, far_own))
     second_here, first_here, far_own = to_place(second, 2), to_place(first, 1), to_chip(far_own)
     return total(own, second_here, first_here, far_own).astype(jnp.bfloat16)

time: 50.4 us -> 50.5 us (level)
  waiting for transfers between devices: 18.4 us -> 19 us
    ppermute x6, waiting for transfers between devices: 2.54 us -> 7.27 us  [to_chip(): return lax.ppermute(value, 'node', [(i, i ^ 2) for i in range(2 * CHIPS)])]
    ppermute x6, waiting for transfers between devices: 9.23 us -> 6.53 us  [to_place(): return lax.ppermute(value, 'local', [(i, i ^ bits) for i in range(PLACES)])]
    ppermute x2, waiting for transfers between devices: 3.12 us -> 1.68 us  [to_both(): return lax.ppermute(value, ('node', 'local'), perm)]
    ppermute x6, starting transfers between devices: 8.5 us -> 9.51 us  [to_chip(): return lax.ppermute(value, 'node', [(i, i ^ 2) for i in range(2 * CHIPS)])]
    ppermute x6, starting transfers between devices: 11.3 us -> 10.5 us  [to_place(): return lax.ppermute(value, 'local', [(i, i ^ bits) for i in range(PLACES)])]
    ppermute x2, starting transfers between devices: 2.89 us -> 2.25 us  [to_both(): return lax.ppermute(value, ('node', 'local'), perm)]
  transfers between devices with their start and end apart: 18 -> 18, of which waited for: 12 -> 13; matrix products, arithmetic and copies ran while one was open for 0% -> 0% of each run, Pallas kernels for 1% -> 1%
where the time goes in v18:
time: 50.5 us; the launch traced here: 50.3 us
  starting transfers between devices  22.8 us (45%)
  waiting for transfers between devices  19 us (38%)
  Pallas kernels  7.58 us (15%)
  other arithmetic  0.8 us (2%)
    ppermute x6, starting transfers between devices, to_place(): return lax.ppermute(value, 'local', [(i, i ^ bits) for i in range(PLACES)])  10.5 us
    ppermute x6, starting transfers between devices, to_chip(): return lax.ppermute(value, 'node', [(i, i ^ 2) for i in range(2 * CHIPS)])  9.51 us
    ppermute x6, waiting for transfers between devices, to_chip(): return lax.ppermute(value, 'node', [(i, i ^ 2) for i in range(2 * CHIPS)])  7.27 us
    ppermute x6, waiting for transfers between devices, to_place(): return lax.ppermute(value, 'local', [(i, i ^ bits) for i in range(PLACES)])  6.53 us
    pallas_call x1, Pallas kernels, hidden_units(): pl.pallas_call(functools.partial(hidden_kernel, experts), out_shape=jax.S...  4.05 us
    ppermute x4, waiting for transfers between devices, to_core(): return lax.ppermute(value, 'node', [(i, i ^ 1) for i in range(2 * CHIPS)])  3.5 us
    ppermute x2, starting transfers between devices, to_both(): return lax.ppermute(value, ('node', 'local'), perm)  2.25 us
    pallas_call x1, Pallas kernels, down(): pl.pallas_call(functools.partial(down_kernel, chunk), out_shape=[jax.Shap...  2.08 us
  transfers between devices with their start and end apart: 18, of which 13 were waited for; matrix products, arithmetic and copies ran while one was open for 0% of the time, Pallas kernels for 1%

profile of v18, /device:TPU:0, one launch (start us, length us, event | category | flops | bytes accessed | tf_op | source)
XLA Modules:
  0.0 50.3 jit_solution(15502100083360393512)
XLA Ops:
  0.0 0.0 copy-start
  0.0 0.0 copy-start.1
  0.0 1.1 %pack.1.refs_0_ = bf16[8,7296]{1,0:T(8,128)(2,1)S(1)} custom-call(bf16[8,7168]{1,0:T(8,128)(2,1)} %refs_0_.1, s32[4,8]{1,0:T(4,128)} %bitcast.6, f32[4,8]{1,0:T(4,128)} %bitcast.7, s32[8]{0:T(128)} %refs_3_.1, bf16[2,7168,512]{2,1,0:T(8,128)(2,1)} %refs_4_.3, bf16[2,7168,512]{2,1,0:T(8,128)(2,1)} %refs_5_.3, bf16[2,512,7168]{2,1,0:T(8,128)(2,1)} %refs_6_.1), custom_call_target="tpu_custom_call" | custom-call | tf_op jit(solution)/shard_map/pack/pallas_call | solution.py:51
  1.1 3.1 %collective-permute-start.1 = (bf16[8,7296]{1,0:T(8,128)(2,1)S(1)}, bf16[8,7296]{1,0:T(8,128)(2,1)S(1)}, u32[]{:S(2)}, u32[]{:S(2)}) collective-permute-start(bf16[8,7296]{1,0:T(8,128)(2,1)S(1)} %pack.1.refs_0_), channel_id=1, source_target_pairs={{0,1},{1,0},{2,3},{3,2},{4,5},{5,4},{6,7},{7,6},{8,9},{9,8},{10,11... | collective-permute-start | bytes 350216 | tf_op jit(solution)/shard_map/ppermute | solution.py:178
  4.2 2.6 %collective-permute-start.3 = (bf16[8,7296]{1,0:T(8,128)(2,1)S(1)}, bf16[8,7296]{1,0:T(8,128)(2,1)S(1)}, u32[]{:S(2)}, u32[]{:S(2)}) collective-permute-start(bf16[8,7296]{1,0:T(8,128)(2,1)S(1)} %pack.1.refs_0_), channel_id=1, source_target_pairs={{0,2},{1,3},{2,0},{3,1},{4,6},{5,7},{6,4},{7,5},{8,10},{9,11},{10,... | collective-permute-start | bytes 350216 | tf_op jit(solution)/shard_map/ppermute | solution.py:178
  6.8 1.5 %collective-permute-start = (bf16[8,7296]{1,0:T(8,128)(2,1)S(1)}, bf16[8,7296]{1,0:T(8,128)(2,1)S(1)}, u32[]{:S(2)}, u32[]{:S(2)}) collective-permute-start(bf16[8,7296]{1,0:T(8,128)(2,1)S(1)} %pack.1.refs_0_), channel_id=1, source_target_pairs={{0,8},{4,12},{8,0},{12,4},{1,9},{5,13},{9,1},{13,5},{2,10},{6,14},... | collective-permute-start | bytes 350216 | tf_op jit(solution)/shard_map/ppermute | solution.py:174
  8.3 0.3 collective-permute-done.1.refs_2_
  8.6 1.8 %collective-permute-start.2 = (bf16[8,7296]{1,0:T(8,128)(2,1)S(1)}, bf16[8,7296]{1,0:T(8,128)(2,1)S(1)}, u32[]{:S(2)}, u32[]{:S(2)}) collective-permute-start(bf16[8,7296]{1,0:T(8,128)(2,1)S(1)} %collective-permute-done.1.refs_2_), channel_id=1, source_target_pairs={{0,8},{4,12},{8,0},{12,4},{1,9},{5,13},{9,1},{13,5},{2,10},{6,14},... | collective-permute-start | bytes 350216 | tf_op jit(solution)/shard_map/ppermute | solution.py:174
  10.4 1.9 %collective-permute-done.3.refs_0_ = bf16[8,7296]{1,0:T(8,128)(2,1)S(1)} collective-permute-done((bf16[8,7296]{1,0:T(8,128)(2,1)S(1)}, bf16[8,7296]{1,0:T(8,128)(2,1)S(1)}, u32[]{:S(2)}, u32[]{:S(2)}) %collective-permute-start.3) | collective-permute-done | bytes 116768 | tf_op jit(solution)/shard_map/ppermute | solution.py:178
  12.3 0.1 collective-permute-done.refs_1_
  12.4 1.5 %collective-permute-start.5 = (bf16[8,7296]{1,0:T(8,128)(2,1)S(1)}, bf16[8,7296]{1,0:T(8,128)(2,1)S(1)}, u32[]{:S(2)}, u32[]{:S(2)}) collective-permute-start(bf16[8,7296]{1,0:T(8,128)(2,1)S(1)} %collective-permute-done.3.refs_0_), channel_id=1, source_target_pairs={{0,8},{4,12},{8,0},{12,4},{1,9},{5,13},{9,1},{13,5},{2,10},{6,14},... | collective-permute-start | bytes 350216 | tf_op jit(solution)/shard_map/ppermute | solution.py:174
  13.9 0.8 %collective-permute-start.4 = (bf16[8,7296]{1,0:T(8,128)(2,1)S(1)}, bf16[8,7296]{1,0:T(8,128)(2,1)S(1)}, u32[]{:S(2)}, u32[]{:S(2)}) collective-permute-start(bf16[8,7296]{1,0:T(8,128)(2,1)S(1)} %collective-permute-done.3.refs_0_), channel_id=1, source_target_pairs={{0,1},{1,0},{2,3},{3,2},{4,5},{5,4},{6,7},{7,6},{8,9},{9,8},{10,11... | collective-permute-start | bytes 350216 | tf_op jit(solution)/shard_map/ppermute | solution.py:178
  14.7 0.0 collective-permute-done.2.refs_3_
  14.7 1.2 %collective-permute-start.6 = (bf16[8,7296]{1,0:T(8,128)(2,1)S(1)}, bf16[8,7296]{1,0:T(8,128)(2,1)S(1)}, u32[]{:S(2)}, u32[]{:S(2)}) collective-permute-start(bf16[8,7296]{1,0:T(8,128)(2,1)S(1)} %collective-permute-done.3.refs_0_), channel_id=1, source_target_pairs={{0,9},{1,8},{2,11},{3,10},{4,13},{5,12},{6,15},{7,14},{8,1},{9,0},... | collective-permute-start | bytes 350216 | tf_op jit(solution)/shard_map/ppermute | solution.py:184
  15.9 0.1 stack.2.refs_0_
  16.0 0.1 collective-permute-start.7
  16.1 2.4 %collective-permute-done.5.refs_2_ = bf16[8,7296]{1,0:T(8,128)(2,1)S(1)} collective-permute-done((bf16[8,7296]{1,0:T(8,128)(2,1)S(1)}, bf16[8,7296]{1,0:T(8,128)(2,1)S(1)}, u32[]{:S(2)}, u32[]{:S(2)}) %collective-permute-start.5) | collective-permute-done | bytes 116768 | tf_op jit(solution)/shard_map/ppermute | solution.py:174
  18.5 0.2 collective-permute-done.4.refs_1_
  18.7 1.7 %collective-permute-done.6.refs_3_ = bf16[8,7296]{1,0:T(8,128)(2,1)S(1)} collective-permute-done((bf16[8,7296]{1,0:T(8,128)(2,1)S(1)}, bf16[8,7296]{1,0:T(8,128)(2,1)S(1)}, u32[]{:S(2)}, u32[]{:S(2)}) %collective-permute-start.6) | collective-permute-done | bytes 116768 | tf_op jit(solution)/shard_map/ppermute | solution.py:184
  20.4 0.0 slice-start
  20.4 0.1 stack.3.refs_1_
  20.5 0.0 slice-start.1
  20.5 0.0 slice-start.2
  20.5 0.0 slice-start.3
  20.5 0.1 collective-permute-start.8
  20.6 0.0 collective-permute-done.7.refs_2_
  20.6 1.8 %collective-permute-done.8.refs_3_ = bf16[32,7296]{1,0:T(8,128)(2,1)S(1)} collective-permute-done((bf16[32,7296]{1,0:T(8,128)(2,1)S(1)}, bf16[32,7296]{1,0:T(8,128)(2,1)S(1)}, u32[]{:S(2)}, u32[]{:S(2)}) %collective-permute-start.8) | collective-permute-done | bytes 466976 | tf_op jit(solution)/shard_map/ppermute | solution.py:170
  22.4 0.0 copy-done
  22.4 0.0 copy-done.1
  22.4 4.1 %hidden.1.hidden_ref = bf16[128,1024]{1,0:T(8,128)(2,1)S(1)} custom-call(bf16[32,7296]{1,0:T(8,128)(2,1)S(1)} %stack.2.refs_0_, bf16[32,7296]{1,0:T(8,128)(2,1)S(1)} %stack.3.refs_1_, bf16[32,7296]{1,0:T(8,128)(2,1)S(1)} %collective-permute-done.7.refs_2_, bf16[32,7296]{1,0:T(8,128)(2,1)S(1)} %collective-permute-done.8.refs_3_, ...), custom_call_target="tpu_custom_call" | custom-call | flops 3758096384 | bytes 29360128 | tf_op jit(solution)/shard_map/hidden/pallas_call | solution.py:114
  26.5 0.0 slice-done
  26.5 0.0 slice-done.1
  26.5 0.0 slice-done.2
  26.5 0.0 slice-done.3
  26.5 2.1 %down.1 = (bf16[32,7168]{1,0:T(8,128)(2,1)S(1)}, bf16[32,7168]{1,0:T(8,128)(2,1)S(1)}, bf16[32,7168]{1,0:T(8,128)(2,1)S(1)}, bf16[32,7168]{1,0:T(8,128)(2,1)S(1)}) custom-call(bf16[128,1024]{1,0:T(8,128)(2,1)S(1)} %hidden.1.hidden_ref, bf16[1024,7168]{1,0:T(8,128)(2,1)S(1)} %bitcast.5), custom_call_target="tpu_custom_call" | custom-call | flops 1879048192 | bytes 14680064 | tf_op jit(solution)/shard_map/down/pallas_call | solution.py:151
  28.6 0.2 collective-permute-start.9
  28.8 1.7 %collective-permute-done.9.refs_1_ = bf16[32,7168]{1,0:T(8,128)(2,1)S(1)} collective-permute-done((bf16[32,7168]{1,0:T(8,128)(2,1)S(1)}, bf16[32,7168]{1,0:T(8,128)(2,1)S(1)}, u32[]{:S(2)}, u32[]{:S(2)}) %collective-permute-start.9) | collective-permute-done | bytes 458784 | tf_op jit(solution)/shard_map/ppermute | solution.py:170
  30.5 0.1 collective-permute-start.10
  30.6 0.1 sums.3
  30.7 1.8 %collective-permute-start.11 = (bf16[8,7168]{1,0:T(8,128)(2,1)S(1)}, bf16[8,7168]{1,0:T(8,128)(2,1)S(1)}, u32[]{:S(2)}, u32[]{:S(2)}) collective-permute-start(bf16[8,7168]{1,0:T(8,128)(2,1)S(1)} %get-tuple-element.32), channel_id=1, source_target_pairs={{0,8},{4,12},{8,0},{12,4},{1,9},{5,13},{9,1},{13,5},{2,10},{6,14},... | collective-permute-start | bytes 344072 | tf_op jit(solution)/shard_map/ppermute | solution.py:174
  32.5 1.0 %collective-permute-start.12 = (bf16[8,7168]{1,0:T(8,128)(2,1)S(1)}, bf16[8,7168]{1,0:T(8,128)(2,1)S(1)}, u32[]{:S(2)}, u32[]{:S(2)}) collective-permute-start(bf16[8,7168]{1,0:T(8,128)(2,1)S(1)} %get-tuple-element.33), channel_id=1, source_target_pairs={{0,9},{1,8},{2,11},{3,10},{4,13},{5,12},{6,15},{7,14},{8,1},{9,0},... | collective-permute-start | bytes 344072 | tf_op jit(solution)/shard_map/ppermute | solution.py:184
  33.5 0.8 %collective-permute-start.13 = (bf16[8,7168]{1,0:T(8,128)(2,1)S(1)}, bf16[8,7168]{1,0:T(8,128)(2,1)S(1)}, u32[]{:S(2)}, u32[]{:S(2)}) collective-permute-start(bf16[8,7168]{1,0:T(8,128)(2,1)S(1)} %get-tuple-element.34), channel_id=1, source_target_pairs={{0,1},{1,0},{2,3},{3,2},{4,5},{5,4},{6,7},{7,6},{8,9},{9,8},{10,11... | collective-permute-start | bytes 344072 | tf_op jit(solution)/shard_map/ppermute | solution.py:178
  34.3 0.0 collective-permute-done.10.refs_1_
  34.3 0.1 sums.2
  34.4 3.5 %collective-permute-done.11 = bf16[8,7168]{1,0:T(8,128)(2,1)S(1)} collective-permute-done((bf16[8,7168]{1,0:T(8,128)(2,1)S(1)}, bf16[8,7168]{1,0:T(8,128)(2,1)S(1)}, u32[]{:S(2)}, u32[]{:S(2)}) %collective-permute-start.11) | collective-permute-done | bytes 114720 | tf_op jit(solution)/shard_map/ppermute | solution.py:174
  37.9 2.4 %collective-permute-start.15 = (bf16[8,7168]{1,0:T(8,128)(2,1)S(1)}, bf16[8,7168]{1,0:T(8,128)(2,1)S(1)}, u32[]{:S(2)}, u32[]{:S(2)}) collective-permute-start(bf16[8,7168]{1,0:T(8,128)(2,1)S(1)} %get-tuple-element.37), channel_id=1, source_target_pairs={{0,8},{4,12},{8,0},{12,4},{1,9},{5,13},{9,1},{13,5},{2,10},{6,14},... | collective-permute-start | bytes 344072 | tf_op jit(solution)/shard_map/ppermute | solution.py:174
  40.4 0.0 collective-permute-done.12
  40.4 0.0 collective-permute-done.13
  40.4 0.1 add_convert_fusion.2
  40.4 1.7 %collective-permute-start.14 = (bf16[8,7168]{1,0:T(8,128)(2,1)S(1)}, bf16[8,7168]{1,0:T(8,128)(2,1)S(1)}, u32[]{:S(2)}, u32[]{:S(2)}) collective-permute-start(bf16[8,7168]{1,0:T(8,128)(2,1)S(1)} %add_convert_fusion.2), channel_id=1, source_target_pairs={{0,2},{1,3},{2,0},{3,1},{4,6},{5,7},{6,4},{7,5},{8,10},{9,11},{10,... | collective-permute-start | bytes 344072 | tf_op jit(solution)/shard_map/ppermute | solution.py:178
  42.2 1.0 %collective-permute-done.15 = bf16[8,7168]{1,0:T(8,128)(2,1)S(1)} collective-permute-done((bf16[8,7168]{1,0:T(8,128)(2,1)S(1)}, bf16[8,7168]{1,0:T(8,128)(2,1)S(1)}, u32[]{:S(2)}, u32[]{:S(2)}) %collective-permute-start.15) | collective-permute-done | bytes 114720 | tf_op jit(solution)/shard_map/ppermute | solution.py:174
  43.3 1.6 %collective-permute-start.16 = (bf16[8,7168]{1,0:T(8,128)(2,1)S(1)}, bf16[8,7168]{1,0:T(8,128)(2,1)S(1)}, u32[]{:S(2)}, u32[]{:S(2)}) collective-permute-start(bf16[8,7168]{1,0:T(8,128)(2,1)S(1)} %add_convert_fusion.1), channel_id=1, source_target_pairs={{0,1},{1,0},{2,3},{3,2},{4,5},{5,4},{6,7},{7,6},{8,9},{9,8},{10,11... | collective-permute-start | bytes 344072 | tf_op jit(solution)/shard_map/ppermute | solution.py:178
  44.8 0.5 %collective-permute-start.17 = (bf16[8,7168]{1,0:T(8,128)(2,1)S(1)}, bf16[8,7168]{1,0:T(8,128)(2,1)S(1)}, u32[]{:S(2)}, u32[]{:S(2)}) collective-permute-start(bf16[8,7168]{1,0:T(8,128)(2,1)S(1)} %get-tuple-element.40), channel_id=1, source_target_pairs={{0,8},{4,12},{8,0},{12,4},{1,9},{5,13},{9,1},{13,5},{2,10},{6,14},... | collective-permute-start | bytes 344072 | tf_op jit(solution)/shard_map/ppermute | solution.py:174
  45.3 2.9 %collective-permute-done.14 = bf16[8,7168]{1,0:T(8,128)(2,1)S(1)} collective-permute-done((bf16[8,7168]{1,0:T(8,128)(2,1)S(1)}, bf16[8,7168]{1,0:T(8,128)(2,1)S(1)}, u32[]{:S(2)}, u32[]{:S(2)}) %collective-permute-start.14) | collective-permute-done | bytes 114720 | tf_op jit(solution)/shard_map/ppermute | solution.py:178
  48.2 1.2 %collective-permute-done.16 = bf16[8,7168]{1,0:T(8,128)(2,1)S(1)} collective-permute-done((bf16[8,7168]{1,0:T(8,128)(2,1)S(1)}, bf16[8,7168]{1,0:T(8,128)(2,1)S(1)}, u32[]{:S(2)}, u32[]{:S(2)}) %collective-permute-start.16) | collective-permute-done | bytes 114720 | tf_op jit(solution)/shard_map/ppermute | solution.py:178
  49.4 0.2 collective-permute-done.17
  49.6 0.7 %add_convert_fusion = bf16[8,7168]{1,0:T(8,128)(2,1)} fusion(bf16[8,7168]{1,0:T(8,128)(2,1)S(1)} %collective-permute-done.17, bf16[8,7168]{1,0:T(8,128)(2,1)S(1)} %collective-permute-done.16, bf16[8,7168]{1,0:T(8,128)(2,1)S(1)} %collective-permute-done.14, bf16[8,7168]{1,0:T(8,128)(2,1)S(1)} %get-tuple-element.29), kind=kLoop, calls=%fused_computation | loop fusion | flops 458752 | bytes 573440 | tf_op jit(solution)/shard_map/convert_element_type | solution.py:244
  (2 shorter events, 0.0 us)
Async XLA Ops:
  0.0 22.4 %copy-start = (bf16[2,7168,512]{2,1,0:T(8,128)(2,1)S(1)}, bf16[2,7168,512]{2,1,0:T(8,128)(2,1)}, u32[]{:S(2)}) copy-start(bf16[2,7168,512]{2,1,0:T(8,128)(2,1)} %refs_4_.3) | copy-start | bytes 44040196
  0.0 22.4 %copy-start.1 = (bf16[2,7168,512]{2,1,0:T(8,128)(2,1)S(1)}, bf16[2,7168,512]{2,1,0:T(8,128)(2,1)}, u32[]{:S(2)}) copy-start(bf16[2,7168,512]{2,1,0:T(8,128)(2,1)} %refs_5_.3) | copy-start | bytes 44040196
  1.1 7.5 %collective-permute-start.1 = (bf16[8,7296]{1,0:T(8,128)(2,1)S(1)}, bf16[8,7296]{1,0:T(8,128)(2,1)S(1)}, u32[]{:S(2)}, u32[]{:S(2)}) collective-permute-start(bf16[8,7296]{1,0:T(8,128)(2,1)S(1)} %pack.1.refs_0_), channel_id=1, source_target_pairs={{0,1},{1,0},{2,3},{3,2},{4,5},{5,4},{6,7},{7,6},{8,9},{9,8},{10,11... | collective-permute-start | bytes 350216 | tf_op jit(solution)/shard_map/ppermute | solution.py:178
  4.2 8.1 %collective-permute-start.3 = (bf16[8,7296]{1,0:T(8,128)(2,1)S(1)}, bf16[8,7296]{1,0:T(8,128)(2,1)S(1)}, u32[]{:S(2)}, u32[]{:S(2)}) collective-permute-start(bf16[8,7296]{1,0:T(8,128)(2,1)S(1)} %pack.1.refs_0_), channel_id=1, source_target_pairs={{0,2},{1,3},{2,0},{3,1},{4,6},{5,7},{6,4},{7,5},{8,10},{9,11},{10,... | collective-permute-start | bytes 350216 | tf_op jit(solution)/shard_map/ppermute | solution.py:178
  6.8 5.6 %collective-permute-start = (bf16[8,7296]{1,0:T(8,128)(2,1)S(1)}, bf16[8,7296]{1,0:T(8,128)(2,1)S(1)}, u32[]{:S(2)}, u32[]{:S(2)}) collective-permute-start(bf16[8,7296]{1,0:T(8,128)(2,1)S(1)} %pack.1.refs_0_), channel_id=1, source_target_pairs={{0,8},{4,12},{8,0},{12,4},{1,9},{5,13},{9,1},{13,5},{2,10},{6,14},... | collective-permute-start | bytes 350216 | tf_op jit(solution)/shard_map/ppermute | solution.py:174
  8.6 6.1 %collective-permute-start.2 = (bf16[8,7296]{1,0:T(8,128)(2,1)S(1)}, bf16[8,7296]{1,0:T(8,128)(2,1)S(1)}, u32[]{:S(2)}, u32[]{:S(2)}) collective-permute-start(bf16[8,7296]{1,0:T(8,128)(2,1)S(1)} %collective-permute-done.1.refs_2_), channel_id=1, source_target_pairs={{0,8},{4,12},{8,0},{12,4},{1,9},{5,13},{9,1},{13,5},{2,10},{6,14},... | collective-permute-start | bytes 350216 | tf_op jit(solution)/shard_map/ppermute | solution.py:174
  12.4 6.1 %collective-permute-start.5 = (bf16[8,7296]{1,0:T(8,128)(2,1)S(1)}, bf16[8,7296]{1,0:T(8,128)(2,1)S(1)}, u32[]{:S(2)}, u32[]{:S(2)}) collective-permute-start(bf16[8,7296]{1,0:T(8,128)(2,1)S(1)} %collective-permute-done.3.refs_0_), channel_id=1, source_target_pairs={{0,8},{4,12},{8,0},{12,4},{1,9},{5,13},{9,1},{13,5},{2,10},{6,14},... | collective-permute-start | bytes 350216 | tf_op jit(solution)/shard_map/ppermute | solution.py:174
  13.9 4.8 %collective-permute-start.4 = (bf16[8,7296]{1,0:T(8,128)(2,1)S(1)}, bf16[8,7296]{1,0:T(8,128)(2,1)S(1)}, u32[]{:S(2)}, u32[]{:S(2)}) collective-permute-start(bf16[8,7296]{1,0:T(8,128)(2,1)S(1)} %collective-permute-done.3.refs_0_), channel_id=1, source_target_pairs={{0,1},{1,0},{2,3},{3,2},{4,5},{5,4},{6,7},{7,6},{8,9},{9,8},{10,11... | collective-permute-start | bytes 350216 | tf_op jit(solution)/shard_map/ppermute | solution.py:178
  14.7 5.7 %collective-permute-start.6 = (bf16[8,7296]{1,0:T(8,128)(2,1)S(1)}, bf16[8,7296]{1,0:T(8,128)(2,1)S(1)}, u32[]{:S(2)}, u32[]{:S(2)}) collective-permute-start(bf16[8,7296]{1,0:T(8,128)(2,1)S(1)} %collective-permute-done.3.refs_0_), channel_id=1, source_target_pairs={{0,9},{1,8},{2,11},{3,10},{4,13},{5,12},{6,15},{7,14},{8,1},{9,0},... | collective-permute-start | bytes 350216 | tf_op jit(solution)/shard_map/ppermute | solution.py:184
  16.0 4.6 %collective-permute-start.7 = (bf16[32,7296]{1,0:T(8,128)(2,1)S(1)}, bf16[32,7296]{1,0:T(8,128)(2,1)S(1)}, u32[]{:S(2)}, u32[]{:S(2)}) collective-permute-start(bf16[32,7296]{1,0:T(8,128)(2,1)S(1)} %stack.2.refs_0_), channel_id=1, source_target_pairs={{0,4},{4,0},{8,12},{12,8},{1,5},{5,1},{9,13},{13,9},{2,6},{6,2},{1... | collective-permute-start | bytes 1400840 | tf_op jit(solution)/shard_map/ppermute | solution.py:170
  20.4 6.1 %slice-start = ((s8[14680064]{0:T(1024)(128)(4,1)}), s8[4194304]{0:T(1024)(128)(4,1)S(1)}, s32[]{:S(2)}) async-start(s8[14680064]{0:T(1024)(128)(4,1)} %bitcast.3), calls=%async_computation | async-start | bytes 8388608
  20.5 6.0 %slice-start.1 = ((s8[14680064]{0:T(1024)(128)(4,1)}), s8[4194304]{0:T(1024)(128)(4,1)S(1)}, s32[]{:S(2)}) async-start(s8[14680064]{0:T(1024)(128)(4,1)} %bitcast.3), calls=%async_computation.1 | async-start | bytes 8388608
  20.5 6.0 %slice-start.2 = ((s8[14680064]{0:T(1024)(128)(4,1)}), s8[4194304]{0:T(1024)(128)(4,1)S(1)}, s32[]{:S(2)}) async-start(s8[14680064]{0:T(1024)(128)(4,1)} %bitcast.3), calls=%async_computation.2 | async-start | bytes 8388608
  20.5 6.0 %slice-start.3 = ((s8[14680064]{0:T(1024)(128)(4,1)}), s8[2097152]{0:T(1024)(128)(4,1)S(1)}, s32[]{:S(2)}) async-start(s8[14680064]{0:T(1024)(128)(4,1)} %bitcast.3), calls=%async_computation.3 | async-start | bytes 4194304
  20.5 1.9 %collective-permute-start.8 = (bf16[32,7296]{1,0:T(8,128)(2,1)S(1)}, bf16[32,7296]{1,0:T(8,128)(2,1)S(1)}, u32[]{:S(2)}, u32[]{:S(2)}) collective-permute-start(bf16[32,7296]{1,0:T(8,128)(2,1)S(1)} %stack.3.refs_1_), channel_id=1, source_target_pairs={{0,4},{4,0},{8,12},{12,8},{1,5},{5,1},{9,13},{13,9},{2,6},{6,2},{1... | collective-permute-start | bytes 1400840 | tf_op jit(solution)/shard_map/ppermute | solution.py:170
  28.6 1.9 %collective-permute-start.9 = (bf16[32,7168]{1,0:T(8,128)(2,1)S(1)}, bf16[32,7168]{1,0:T(8,128)(2,1)S(1)}, u32[]{:S(2)}, u32[]{:S(2)}) collective-permute-start(bf16[32,7168]{1,0:T(8,128)(2,1)S(1)} %get-tuple-element.27), channel_id=1, source_target_pairs={{0,4},{4,0},{8,12},{12,8},{1,5},{5,1},{9,13},{13,9},{2,6},{6,2},{1... | collective-permute-start | bytes 1376264 | tf_op jit(solution)/shard_map/ppermute | solution.py:170
  30.5 3.8 %collective-permute-start.10 = (bf16[32,7168]{1,0:T(8,128)(2,1)S(1)}, bf16[32,7168]{1,0:T(8,128)(2,1)S(1)}, u32[]{:S(2)}, u32[]{:S(2)}) collective-permute-start(bf16[32,7168]{1,0:T(8,128)(2,1)S(1)} %get-tuple-element.28), channel_id=1, source_target_pairs={{0,4},{4,0},{8,12},{12,8},{1,5},{5,1},{9,13},{13,9},{2,6},{6,2},{1... | collective-permute-start | bytes 1376264 | tf_op jit(solution)/shard_map/ppermute | solution.py:170
  30.7 7.2 %collective-permute-start.11 = (bf16[8,7168]{1,0:T(8,128)(2,1)S(1)}, bf16[8,7168]{1,0:T(8,128)(2,1)S(1)}, u32[]{:S(2)}, u32[]{:S(2)}) collective-permute-start(bf16[8,7168]{1,0:T(8,128)(2,1)S(1)} %get-tuple-element.32), channel_id=1, source_target_pairs={{0,8},{4,12},{8,0},{12,4},{1,9},{5,13},{9,1},{13,5},{2,10},{6,14},... | collective-permute-start | bytes 344072 | tf_op jit(solution)/shard_map/ppermute | solution.py:174
  32.5 7.9 %collective-permute-start.12 = (bf16[8,7168]{1,0:T(8,128)(2,1)S(1)}, bf16[8,7168]{1,0:T(8,128)(2,1)S(1)}, u32[]{:S(2)}, u32[]{:S(2)}) collective-permute-start(bf16[8,7168]{1,0:T(8,128)(2,1)S(1)} %get-tuple-element.33), channel_id=1, source_target_pairs={{0,9},{1,8},{2,11},{3,10},{4,13},{5,12},{6,15},{7,14},{8,1},{9,0},... | collective-permute-start | bytes 344072 | tf_op jit(solution)/shard_map/ppermute | solution.py:184
  33.5 6.8 %collective-permute-start.13 = (bf16[8,7168]{1,0:T(8,128)(2,1)S(1)}, bf16[8,7168]{1,0:T(8,128)(2,1)S(1)}, u32[]{:S(2)}, u32[]{:S(2)}) collective-permute-start(bf16[8,7168]{1,0:T(8,128)(2,1)S(1)} %get-tuple-element.34), channel_id=1, source_target_pairs={{0,1},{1,0},{2,3},{3,2},{4,5},{5,4},{6,7},{7,6},{8,9},{9,8},{10,11... | collective-permute-start | bytes 344072 | tf_op jit(solution)/shard_map/ppermute | solution.py:178
  37.9 5.3 %collective-permute-start.15 = (bf16[8,7168]{1,0:T(8,128)(2,1)S(1)}, bf16[8,7168]{1,0:T(8,128)(2,1)S(1)}, u32[]{:S(2)}, u32[]{:S(2)}) collective-permute-start(bf16[8,7168]{1,0:T(8,128)(2,1)S(1)} %get-tuple-element.37), channel_id=1, source_target_pairs={{0,8},{4,12},{8,0},{12,4},{1,9},{5,13},{9,1},{13,5},{2,10},{6,14},... | collective-permute-start | bytes 344072 | tf_op jit(solution)/shard_map/ppermute | solution.py:174
  40.4 7.8 %collective-permute-start.14 = (bf16[8,7168]{1,0:T(8,128)(2,1)S(1)}, bf16[8,7168]{1,0:T(8,128)(2,1)S(1)}, u32[]{:S(2)}, u32[]{:S(2)}) collective-permute-start(bf16[8,7168]{1,0:T(8,128)(2,1)S(1)} %add_convert_fusion.2), channel_id=1, source_target_pairs={{0,2},{1,3},{2,0},{3,1},{4,6},{5,7},{6,4},{7,5},{8,10},{9,11},{10,... | collective-permute-start | bytes 344072 | tf_op jit(solution)/shard_map/ppermute | solution.py:178
  43.3 6.2 %collective-permute-start.16 = (bf16[8,7168]{1,0:T(8,128)(2,1)S(1)}, bf16[8,7168]{1,0:T(8,128)(2,1)S(1)}, u32[]{:S(2)}, u32[]{:S(2)}) collective-permute-start(bf16[8,7168]{1,0:T(8,128)(2,1)S(1)} %add_convert_fusion.1), channel_id=1, source_target_pairs={{0,1},{1,0},{2,3},{3,2},{4,5},{5,4},{6,7},{7,6},{8,9},{9,8},{10,11... | collective-permute-start | bytes 344072 | tf_op jit(solution)/shard_map/ppermute | solution.py:178
  44.8 4.8 %collective-permute-start.17 = (bf16[8,7168]{1,0:T(8,128)(2,1)S(1)}, bf16[8,7168]{1,0:T(8,128)(2,1)S(1)}, u32[]{:S(2)}, u32[]{:S(2)}) collective-permute-start(bf16[8,7168]{1,0:T(8,128)(2,1)S(1)} %get-tuple-element.40), channel_id=1, source_target_pairs={{0,8},{4,12},{8,0},{12,4},{1,9},{5,13},{9,1},{13,5},{2,10},{6,14},... | collective-permute-start | bytes 344072 | tf_op jit(solution)/shard_map/ppermute | solution.py:174

commit v19 on v12

--- a/solution.py
+++ b/solution.py
@@ -10,7 +10,6 @@
 LANES = 128
 N_TILE = 256
 DOWN_TILE = 1792
-OUT_CHUNKS = 1
 VMEM_LIMIT = 4 * 2**20
 
 
@@ -22,7 +21,7 @@
     ]
     for copy in copies:
         copy.start()
-    for copy in copies:
+    for copy in copies[1:]:
         copy.wait()
     tokens_ref, ids_ref, route_ref, slot_ref = local
     rows, width = tokens_ref.shape
@@ -39,6 +38,7 @@
     second = (weights - first).astype(jnp.bfloat16).astype(jnp.float32)
     third = weights - first - second
     tail = jnp.where(column < experts, first, jnp.where(column < 2 * experts, second, third))
+    copies[0].wait()
     out_ref[:, :width] = tokens_ref[...]
     out_ref[:, width:] = jnp.where(column < 3 * experts, tail, 0.0).astype(jnp.bfloat16)
 
@@ -93,7 +93,7 @@
         weight_ref[member] = jnp.sum(jnp.where(mine, tail, 0.0), axis=1, keepdims=True)
     tiles = hid // N_TILE
 
-    @pl.loop(0, members * tiles)
+    @pl.loop(0, members * tiles, unroll=True)
     def _(step):
         member = step // tiles
         at = pl.ds(pl.multiple_of(lax.rem(step, tiles) * N_TILE, N_TILE), N_TILE)
@@ -129,33 +129,32 @@
     )(*pieces, w_gate, w_up)
 
 
-def down_kernel(chunk, hidden_ref, down_ref, *outs):
-    part, width = outs[0].shape
-
-    @pl.loop(0, width // DOWN_TILE)
+def down_kernel(hidden_ref, down_ref, *outs):
+    width = down_ref.shape[1]
+
+    @pl.loop(0, width // DOWN_TILE, unroll=True)
     def _(step):
         at = pl.ds(pl.multiple_of(step * DOWN_TILE, DOWN_TILE), DOWN_TILE)
-        there = pl.ds(pl.multiple_of(chunk * width + step * DOWN_TILE, DOWN_TILE), DOWN_TILE)
-        total = jnp.dot(
-            hidden_ref[...], down_ref[:, there], preferred_element_type=jnp.float32
-        ).astype(jnp.bfloat16)
-        for i, ref in enumerate(outs):
-            ref[:, at] = total[i * part : (i + 1) * part]
-
-
-def down(hidden, w_down, chunk, chunks):
+        total = jnp.dot(hidden_ref[...], down_ref[:, at], preferred_element_type=jnp.float32)
+        start = 0
+        for ref in outs:
+            ref[:, at] = total[start : start + ref.shape[0]].astype(ref.dtype)
+            start += ref.shape[0]
+
+
+def down(hidden, w_down, groups):
     units, width = w_down.shape
     rows = hidden.shape[0]
     vmem = pl.BlockSpec(memory_space=pltpu.VMEM)
     return pl.pallas_call(
-        functools.partial(down_kernel, chunk),
-        out_shape=[jax.ShapeDtypeStruct((rows // 4, width // chunks), jnp.bfloat16)] * 4,
+        down_kernel,
+        out_shape=[jax.ShapeDtypeStruct((size, width), jnp.bfloat16) for size in groups],
         in_specs=[vmem, vmem],
-        out_specs=[vmem] * 4,
+        out_specs=[vmem] * len(groups),
         compiler_params=pltpu.CompilerParams(vmem_limit_bytes=VMEM_LIMIT),
         cost_estimate=pl.CostEstimate(
-            flops=2 * rows * units * width // chunks,
-            bytes_accessed=2 * units * width // chunks,
+            flops=2 * rows * units * width,
+            bytes_accessed=2 * units * width,
             transcendentals=0,
         ),
         name="down",
@@ -163,6 +162,7 @@
 
 
 CHIPS, PLACES = 2, 4
+EARLY, LATE = 5, 3
 
 
 def to_core(value):
@@ -198,22 +198,39 @@
     return [early, late, to_core(early), to_core(late)]
 
 
+def sums_kernel(here_ref, other_ref, *outs):
+    total = here_ref[...].astype(jnp.float32) + other_ref[...].astype(jnp.float32)
+    rows = outs[0].shape[0]
+    for i, ref in enumerate(outs):
+        ref[...] = total[i * rows : (i + 1) * rows].astype(ref.dtype)
+
+
+def sums(here, other, blocks):
+    vmem = pl.BlockSpec(memory_space=pltpu.VMEM)
+    block = jax.ShapeDtypeStruct((here.shape[0] // blocks, here.shape[1]), here.dtype)
+    return pl.pallas_call(
+        sums_kernel,
+        out_shape=[block] * blocks,
+        in_specs=[vmem, vmem],
+        out_specs=[vmem] * blocks,
+        compiler_params=pltpu.CompilerParams(vmem_limit_bytes=VMEM_LIMIT),
+        name="sums",
+    )(here, other)
+
+
 def total(*terms):
     return sum(term.astype(jnp.float32) for term in terms)
 
 
-def reduce_blocks(early, late, other_early, other_late, rows):
-    def blocks(here, other):
-        return total(here, other).astype(jnp.bfloat16).reshape(PLACES, rows, -1)
-
+def reduce_blocks(early, late, other_early, other_late):
     other_late = to_core(other_late)
     other_early = to_core(after(other_early, other_late))
-    second, third, far_second, far_third = blocks(late, other_late)
+    third, far_second, far_third = sums(late, other_late, LATE)
     far_second = to_chip(far_second)
     far_third = to_both(far_third, 1)
     third = to_place(third, 1)
+    own, far_own, first, far_first, second = sums(early, other_early, EARLY)
     second = total(second, far_second, far_third, third).astype(jnp.bfloat16)
-    own, far_own, first, far_first = blocks(early, other_early)
     first = total(first, to_chip(after(far_first, third))).astype(jnp.bfloat16)
     first, far_own = lax.optimization_barrier((first, far_own))
     second_here, first_here, far_own = to_place(second, 2), to_place(first, 1), to_chip(far_own)
@@ -221,14 +238,12 @@
 
 
 def by_permutes(tokens, expert_ids, route_weights, expert_slot, w_gate, w_up, w_down):
-    rows = tokens.shape[0]
     own = pack(tokens, expert_ids, route_weights, expert_slot, w_gate, w_up, w_down)
     hidden = hidden_units(gather_blocks(own), w_gate, w_up, expert_slot.shape[0])
     matrix = w_down.reshape(-1, w_down.shape[-1])
-    outs = []
-    for chunk in range(OUT_CHUNKS):
-        outs.append(reduce_blocks(*down(hidden, matrix, chunk, OUT_CHUNKS), rows))
-    return jnp.concatenate(outs, axis=1)
+    rows = tokens.shape[0]
+    groups = (EARLY * rows, LATE * rows) * 2
+    return reduce_blocks(*down(hidden, matrix, groups))
 
 
 def by_collectives(tokens, expert_ids, route_weights, expert_slot, w_gate, w_up, w_down):

time: 51.1 us -> 50.1 us (0.980)
  starting transfers between devices: 21.1 us -> 23.2 us
  Pallas kernels: 9.03 us -> 7.58 us
  waiting for transfers between devices: 19.6 us -> 18.2 us
    ppermute x6, starting transfers between devices: 9.27 us -> 11.3 us  [to_place(): return lax.ppermute(value, 'local', [(i, i ^ bits) for i in range(PLACES)])]
    ppermute x6, waiting for transfers between devices: 3.64 us -> 2.54 us  [to_chip(): return lax.ppermute(value, 'node', [(i, i ^ 2) for i in range(2 * CHIPS)])]
    pallas_call x1, Pallas kernels: 5.04 us -> 4.05 us  [hidden_units(): pl.pallas_call(functools.partial(hidden_kernel, experts), out_shape=jax.S...]
    pallas_call x1 -> x3, Pallas kernels: 2.69 us -> 2.3 us  [the longest x1 2.08 us: down(): pl.pallas_call(down_kernel, out_shape=[jax.ShapeDtypeStruct((size, width)...]
  transfers between devices with their start and end apart: 18 -> 18, of which waited for: 13 -> 12; matrix products, arithmetic and copies ran while one was open for 1% -> 0% of each run, Pallas kernels for 0% -> 1%
where the time goes in v19:
time: 50.1 us; the launch traced here: 50 us
  starting transfers between devices  23.2 us (46%)
  waiting for transfers between devices  18.2 us (36%)
  Pallas kernels  7.58 us (15%)
  other arithmetic  0.8 us (2%)
    ppermute x6, starting transfers between devices, to_place(): return lax.ppermute(value, 'local', [(i, i ^ bits) for i in range(PLACES)])  11.3 us
    ppermute x6, waiting for transfers between devices, to_place(): return lax.ppermute(value, 'local', [(i, i ^ bits) for i in range(PLACES)])  9.21 us
    ppermute x6, starting transfers between devices, to_chip(): return lax.ppermute(value, 'node', [(i, i ^ 2) for i in range(2 * CHIPS)])  8.49 us
    pallas_call x1, Pallas kernels, hidden_units(): pl.pallas_call(functools.partial(hidden_kernel, experts), out_shape=jax.S...  4.05 us
    ppermute x4, waiting for transfers between devices, to_core(): return lax.ppermute(value, 'node', [(i, i ^ 1) for i in range(2 * CHIPS)])  3.34 us
    ppermute x2, waiting for transfers between devices, to_both(): return lax.ppermute(value, ('node', 'local'), perm)  3.12 us
    ppermute x2, starting transfers between devices, to_both(): return lax.ppermute(value, ('node', 'local'), perm)  2.89 us
    ppermute x6, waiting for transfers between devices, to_chip(): return lax.ppermute(value, 'node', [(i, i ^ 2) for i in range(2 * CHIPS)])  2.54 us
  transfers between devices with their start and end apart: 18, of which 12 were waited for; matrix products, arithmetic and copies ran while one was open for 0% of the time, Pallas kernels for 1%

profile of v19, /device:TPU:0, one launch (start us, length us, event | category | flops | bytes accessed | tf_op | source)
XLA Modules:
  0.0 50.0 jit_solution(1762867549845122738)
XLA Ops:
  0.0 0.0 copy-start
  0.0 0.0 copy-start.1
  0.0 1.1 %pack.1.refs_0_ = bf16[8,7296]{1,0:T(8,128)(2,1)S(1)} custom-call(bf16[8,7168]{1,0:T(8,128)(2,1)} %refs_0_.1, s32[4,8]{1,0:T(4,128)} %bitcast.6, f32[4,8]{1,0:T(4,128)} %bitcast.7, s32[8]{0:T(128)} %refs_3_.1, bf16[2,7168,512]{2,1,0:T(8,128)(2,1)} %refs_4_.3, bf16[2,7168,512]{2,1,0:T(8,128)(2,1)} %refs_5_.3, bf16[2,512,7168]{2,1,0:T(8,128)(2,1)} %refs_6_.1), custom_call_target="tpu_custom_call" | custom-call | tf_op jit(solution)/shard_map/pack/pallas_call | solution.py:50
  1.1 3.1 %collective-permute-start.1 = (bf16[8,7296]{1,0:T(8,128)(2,1)S(1)}, bf16[8,7296]{1,0:T(8,128)(2,1)S(1)}, u32[]{:S(2)}, u32[]{:S(2)}) collective-permute-start(bf16[8,7296]{1,0:T(8,128)(2,1)S(1)} %pack.1.refs_0_), channel_id=1, source_target_pairs={{0,1},{1,0},{2,3},{3,2},{4,5},{5,4},{6,7},{7,6},{8,9},{9,8},{10,11... | collective-permute-start | bytes 350216 | tf_op jit(solution)/shard_map/ppermute | solution.py:177
  4.2 2.6 %collective-permute-start.3 = (bf16[8,7296]{1,0:T(8,128)(2,1)S(1)}, bf16[8,7296]{1,0:T(8,128)(2,1)S(1)}, u32[]{:S(2)}, u32[]{:S(2)}) collective-permute-start(bf16[8,7296]{1,0:T(8,128)(2,1)S(1)} %pack.1.refs_0_), channel_id=1, source_target_pairs={{0,2},{1,3},{2,0},{3,1},{4,6},{5,7},{6,4},{7,5},{8,10},{9,11},{10,... | collective-permute-start | bytes 350216 | tf_op jit(solution)/shard_map/ppermute | solution.py:177
  6.8 1.5 %collective-permute-start = (bf16[8,7296]{1,0:T(8,128)(2,1)S(1)}, bf16[8,7296]{1,0:T(8,128)(2,1)S(1)}, u32[]{:S(2)}, u32[]{:S(2)}) collective-permute-start(bf16[8,7296]{1,0:T(8,128)(2,1)S(1)} %pack.1.refs_0_), channel_id=1, source_target_pairs={{0,8},{4,12},{8,0},{12,4},{1,9},{5,13},{9,1},{13,5},{2,10},{6,14},... | collective-permute-start | bytes 350216 | tf_op jit(solution)/shard_map/ppermute | solution.py:173
  8.3 0.3 collective-permute-done.1.refs_2_
  8.6 1.8 %collective-permute-start.2 = (bf16[8,7296]{1,0:T(8,128)(2,1)S(1)}, bf16[8,7296]{1,0:T(8,128)(2,1)S(1)}, u32[]{:S(2)}, u32[]{:S(2)}) collective-permute-start(bf16[8,7296]{1,0:T(8,128)(2,1)S(1)} %collective-permute-done.1.refs_2_), channel_id=1, source_target_pairs={{0,8},{4,12},{8,0},{12,4},{1,9},{5,13},{9,1},{13,5},{2,10},{6,14},... | collective-permute-start | bytes 350216 | tf_op jit(solution)/shard_map/ppermute | solution.py:173
  10.4 1.9 %collective-permute-done.3.refs_0_ = bf16[8,7296]{1,0:T(8,128)(2,1)S(1)} collective-permute-done((bf16[8,7296]{1,0:T(8,128)(2,1)S(1)}, bf16[8,7296]{1,0:T(8,128)(2,1)S(1)}, u32[]{:S(2)}, u32[]{:S(2)}) %collective-permute-start.3) | collective-permute-done | bytes 116768 | tf_op jit(solution)/shard_map/ppermute | solution.py:177
  12.3 0.1 collective-permute-done.refs_1_
  12.4 1.5 %collective-permute-start.5 = (bf16[8,7296]{1,0:T(8,128)(2,1)S(1)}, bf16[8,7296]{1,0:T(8,128)(2,1)S(1)}, u32[]{:S(2)}, u32[]{:S(2)}) collective-permute-start(bf16[8,7296]{1,0:T(8,128)(2,1)S(1)} %collective-permute-done.3.refs_0_), channel_id=1, source_target_pairs={{0,8},{4,12},{8,0},{12,4},{1,9},{5,13},{9,1},{13,5},{2,10},{6,14},... | collective-permute-start | bytes 350216 | tf_op jit(solution)/shard_map/ppermute | solution.py:173
  13.9 0.8 %collective-permute-start.4 = (bf16[8,7296]{1,0:T(8,128)(2,1)S(1)}, bf16[8,7296]{1,0:T(8,128)(2,1)S(1)}, u32[]{:S(2)}, u32[]{:S(2)}) collective-permute-start(bf16[8,7296]{1,0:T(8,128)(2,1)S(1)} %collective-permute-done.3.refs_0_), channel_id=1, source_target_pairs={{0,1},{1,0},{2,3},{3,2},{4,5},{5,4},{6,7},{7,6},{8,9},{9,8},{10,11... | collective-permute-start | bytes 350216 | tf_op jit(solution)/shard_map/ppermute | solution.py:177
  14.7 0.0 collective-permute-done.2.refs_3_
  14.7 1.2 %collective-permute-start.6 = (bf16[8,7296]{1,0:T(8,128)(2,1)S(1)}, bf16[8,7296]{1,0:T(8,128)(2,1)S(1)}, u32[]{:S(2)}, u32[]{:S(2)}) collective-permute-start(bf16[8,7296]{1,0:T(8,128)(2,1)S(1)} %collective-permute-done.3.refs_0_), channel_id=1, source_target_pairs={{0,9},{1,8},{2,11},{3,10},{4,13},{5,12},{6,15},{7,14},{8,1},{9,0},... | collective-permute-start | bytes 350216 | tf_op jit(solution)/shard_map/ppermute | solution.py:183
  15.9 0.1 stack.2.refs_0_
  16.0 0.1 collective-permute-start.7
  16.1 2.4 %collective-permute-done.5.refs_2_ = bf16[8,7296]{1,0:T(8,128)(2,1)S(1)} collective-permute-done((bf16[8,7296]{1,0:T(8,128)(2,1)S(1)}, bf16[8,7296]{1,0:T(8,128)(2,1)S(1)}, u32[]{:S(2)}, u32[]{:S(2)}) %collective-permute-start.5) | collective-permute-done | bytes 116768 | tf_op jit(solution)/shard_map/ppermute | solution.py:173
  18.5 0.2 collective-permute-done.4.refs_1_
  18.7 1.7 %collective-permute-done.6.refs_3_ = bf16[8,7296]{1,0:T(8,128)(2,1)S(1)} collective-permute-done((bf16[8,7296]{1,0:T(8,128)(2,1)S(1)}, bf16[8,7296]{1,0:T(8,128)(2,1)S(1)}, u32[]{:S(2)}, u32[]{:S(2)}) %collective-permute-start.6) | collective-permute-done | bytes 116768 | tf_op jit(solution)/shard_map/ppermute | solution.py:183
  20.4 0.0 slice-start
  20.4 0.1 stack.3.refs_1_
  20.5 0.0 slice-start.1
  20.5 0.0 slice-start.2
  20.5 0.0 slice-start.3
  20.5 0.1 collective-permute-start.8
  20.6 0.0 collective-permute-done.7.refs_2_
  20.6 1.8 %collective-permute-done.8.refs_3_ = bf16[32,7296]{1,0:T(8,128)(2,1)S(1)} collective-permute-done((bf16[32,7296]{1,0:T(8,128)(2,1)S(1)}, bf16[32,7296]{1,0:T(8,128)(2,1)S(1)}, u32[]{:S(2)}, u32[]{:S(2)}) %collective-permute-start.8) | collective-permute-done | bytes 466976 | tf_op jit(solution)/shard_map/ppermute | solution.py:169
  22.4 0.0 copy-done
  22.4 0.0 copy-done.1
  22.4 4.1 %hidden.1.hidden_ref = bf16[128,1024]{1,0:T(8,128)(2,1)S(1)} custom-call(bf16[32,7296]{1,0:T(8,128)(2,1)S(1)} %stack.2.refs_0_, bf16[32,7296]{1,0:T(8,128)(2,1)S(1)} %stack.3.refs_1_, bf16[32,7296]{1,0:T(8,128)(2,1)S(1)} %collective-permute-done.7.refs_2_, bf16[32,7296]{1,0:T(8,128)(2,1)S(1)} %collective-permute-done.8.refs_3_, ...), custom_call_target="tpu_custom_call" | custom-call | flops 3758096384 | bytes 29360128 | tf_op jit(solution)/shard_map/hidden/pallas_call | solution.py:113
  26.5 0.0 slice-done
  26.5 0.0 slice-done.1
  26.5 0.0 slice-done.2
  26.5 0.0 slice-done.3
  26.5 2.1 %down.1 = (bf16[40,7168]{1,0:T(8,128)(2,1)S(1)}, bf16[24,7168]{1,0:T(8,128)(2,1)S(1)}, bf16[40,7168]{1,0:T(8,128)(2,1)S(1)}, bf16[24,7168]{1,0:T(8,128)(2,1)S(1)}) custom-call(bf16[128,1024]{1,0:T(8,128)(2,1)S(1)} %hidden.1.hidden_ref, bf16[1024,7168]{1,0:T(8,128)(2,1)S(1)} %bitcast.5), custom_call_target="tpu_custom_call" | custom-call | flops 1879048192 | bytes 14680064 | tf_op jit(solution)/shard_map/down/pallas_call | solution.py:149
  28.6 0.2 collective-permute-start.9
  28.8 1.5 %collective-permute-done.9.other_ref = bf16[24,7168]{1,0:T(8,128)(2,1)S(1)} collective-permute-done((bf16[24,7168]{1,0:T(8,128)(2,1)S(1)}, bf16[24,7168]{1,0:T(8,128)(2,1)S(1)}, u32[]{:S(2)}, u32[]{:S(2)}) %collective-permute-start.9) | collective-permute-done | bytes 344096 | tf_op jit(solution)/shard_map/ppermute | solution.py:169
  30.3 0.1 collective-permute-start.10
  30.5 0.1 sums.3
  30.5 1.3 %collective-permute-start.13 = (bf16[8,7168]{1,0:T(8,128)(2,1)S(1)}, bf16[8,7168]{1,0:T(8,128)(2,1)S(1)}, u32[]{:S(2)}, u32[]{:S(2)}) collective-permute-start(bf16[8,7168]{1,0:T(8,128)(2,1)S(1)} %get-tuple-element.34), channel_id=1, source_target_pairs={{0,1},{1,0},{2,3},{3,2},{4,5},{5,4},{6,7},{7,6},{8,9},{9,8},{10,11... | collective-permute-start | bytes 344072 | tf_op jit(solution)/shard_map/ppermute | solution.py:177
  31.9 0.6 %collective-permute-start.11 = (bf16[8,7168]{1,0:T(8,128)(2,1)S(1)}, bf16[8,7168]{1,0:T(8,128)(2,1)S(1)}, u32[]{:S(2)}, u32[]{:S(2)}) collective-permute-start(bf16[8,7168]{1,0:T(8,128)(2,1)S(1)} %get-tuple-element.32), channel_id=1, source_target_pairs={{0,8},{4,12},{8,0},{12,4},{1,9},{5,13},{9,1},{13,5},{2,10},{6,14},... | collective-permute-start | bytes 344072 | tf_op jit(solution)/shard_map/ppermute | solution.py:173
  32.4 1.7 %collective-permute-start.12 = (bf16[8,7168]{1,0:T(8,128)(2,1)S(1)}, bf16[8,7168]{1,0:T(8,128)(2,1)S(1)}, u32[]{:S(2)}, u32[]{:S(2)}) collective-permute-start(bf16[8,7168]{1,0:T(8,128)(2,1)S(1)} %get-tuple-element.33), channel_id=1, source_target_pairs={{0,9},{1,8},{2,11},{3,10},{4,13},{5,12},{6,15},{7,14},{8,1},{9,0},... | collective-permute-start | bytes 344072 | tf_op jit(solution)/shard_map/ppermute | solution.py:183
  34.1 0.0 collective-permute-done.10.other_ref
  34.1 0.1 sums.2
  34.2 2.0 %collective-permute-done.13 = bf16[8,7168]{1,0:T(8,128)(2,1)S(1)} collective-permute-done((bf16[8,7168]{1,0:T(8,128)(2,1)S(1)}, bf16[8,7168]{1,0:T(8,128)(2,1)S(1)}, u32[]{:S(2)}, u32[]{:S(2)}) %collective-permute-start.13) | collective-permute-done | bytes 114720 | tf_op jit(solution)/shard_map/ppermute | solution.py:177
  36.3 2.0 %collective-permute-start.15 = (bf16[8,7168]{1,0:T(8,128)(2,1)S(1)}, bf16[8,7168]{1,0:T(8,128)(2,1)S(1)}, u32[]{:S(2)}, u32[]{:S(2)}) collective-permute-start(bf16[8,7168]{1,0:T(8,128)(2,1)S(1)} %get-tuple-element.37), channel_id=1, source_target_pairs={{0,8},{4,12},{8,0},{12,4},{1,9},{5,13},{9,1},{13,5},{2,10},{6,14},... | collective-permute-start | bytes 344072 | tf_op jit(solution)/shard_map/ppermute | solution.py:173
  38.3 0.0 collective-permute-done.11
  38.3 1.4 %collective-permute-done.12 = bf16[8,7168]{1,0:T(8,128)(2,1)S(1)} collective-permute-done((bf16[8,7168]{1,0:T(8,128)(2,1)S(1)}, bf16[8,7168]{1,0:T(8,128)(2,1)S(1)}, u32[]{:S(2)}, u32[]{:S(2)}) %collective-permute-start.12) | collective-permute-done | bytes 114720 | tf_op jit(solution)/shard_map/ppermute | solution.py:183
  39.7 0.1 add_convert_fusion.2
  39.8 2.4 %collective-permute-start.14 = (bf16[8,7168]{1,0:T(8,128)(2,1)S(1)}, bf16[8,7168]{1,0:T(8,128)(2,1)S(1)}, u32[]{:S(2)}, u32[]{:S(2)}) collective-permute-start(bf16[8,7168]{1,0:T(8,128)(2,1)S(1)} %add_convert_fusion.2), channel_id=1, source_target_pairs={{0,2},{1,3},{2,0},{3,1},{4,6},{5,7},{6,4},{7,5},{8,10},{9,11},{10,... | collective-permute-start | bytes 344072 | tf_op jit(solution)/shard_map/ppermute | solution.py:177
  42.1 0.0 collective-permute-done.15
  42.2 1.2 %collective-permute-start.16 = (bf16[8,7168]{1,0:T(8,128)(2,1)S(1)}, bf16[8,7168]{1,0:T(8,128)(2,1)S(1)}, u32[]{:S(2)}, u32[]{:S(2)}) collective-permute-start(bf16[8,7168]{1,0:T(8,128)(2,1)S(1)} %add_convert_fusion.1), channel_id=1, source_target_pairs={{0,1},{1,0},{2,3},{3,2},{4,5},{5,4},{6,7},{7,6},{8,9},{9,8},{10,11... | collective-permute-start | bytes 344072 | tf_op jit(solution)/shard_map/ppermute | solution.py:177
  43.4 1.1 %collective-permute-start.17 = (bf16[8,7168]{1,0:T(8,128)(2,1)S(1)}, bf16[8,7168]{1,0:T(8,128)(2,1)S(1)}, u32[]{:S(2)}, u32[]{:S(2)}) collective-permute-start(bf16[8,7168]{1,0:T(8,128)(2,1)S(1)} %get-tuple-element.40), channel_id=1, source_target_pairs={{0,8},{4,12},{8,0},{12,4},{1,9},{5,13},{9,1},{13,5},{2,10},{6,14},... | collective-permute-start | bytes 344072 | tf_op jit(solution)/shard_map/ppermute | solution.py:173
  44.5 3.3 %collective-permute-done.14 = bf16[8,7168]{1,0:T(8,128)(2,1)S(1)} collective-permute-done((bf16[8,7168]{1,0:T(8,128)(2,1)S(1)}, bf16[8,7168]{1,0:T(8,128)(2,1)S(1)}, u32[]{:S(2)}, u32[]{:S(2)}) %collective-permute-start.14) | collective-permute-done | bytes 114720 | tf_op jit(solution)/shard_map/ppermute | solution.py:177
  47.8 1.4 %collective-permute-done.16 = bf16[8,7168]{1,0:T(8,128)(2,1)S(1)} collective-permute-done((bf16[8,7168]{1,0:T(8,128)(2,1)S(1)}, bf16[8,7168]{1,0:T(8,128)(2,1)S(1)}, u32[]{:S(2)}, u32[]{:S(2)}) %collective-permute-start.16) | collective-permute-done | bytes 114720 | tf_op jit(solution)/shard_map/ppermute | solution.py:177
  49.2 0.0 collective-permute-done.17
  49.2 0.7 %add_convert_fusion = bf16[8,7168]{1,0:T(8,128)(2,1)} fusion(bf16[8,7168]{1,0:T(8,128)(2,1)S(1)} %collective-permute-done.17, bf16[8,7168]{1,0:T(8,128)(2,1)S(1)} %collective-permute-done.16, bf16[8,7168]{1,0:T(8,128)(2,1)S(1)} %collective-permute-done.14, bf16[8,7168]{1,0:T(8,128)(2,1)S(1)} %get-tuple-element.29), kind=kLoop, calls=%fused_computation | loop fusion | flops 458752 | bytes 573440 | tf_op jit(solution)/shard_map/convert_element_type | solution.py:237
  (2 shorter events, 0.0 us)
Async XLA Ops:
  0.0 22.4 %copy-start = (bf16[2,7168,512]{2,1,0:T(8,128)(2,1)S(1)}, bf16[2,7168,512]{2,1,0:T(8,128)(2,1)}, u32[]{:S(2)}) copy-start(bf16[2,7168,512]{2,1,0:T(8,128)(2,1)} %refs_4_.3) | copy-start | bytes 44040196
  0.0 22.4 %copy-start.1 = (bf16[2,7168,512]{2,1,0:T(8,128)(2,1)S(1)}, bf16[2,7168,512]{2,1,0:T(8,128)(2,1)}, u32[]{:S(2)}) copy-start(bf16[2,7168,512]{2,1,0:T(8,128)(2,1)} %refs_5_.3) | copy-start | bytes 44040196
  1.1 7.5 %collective-permute-start.1 = (bf16[8,7296]{1,0:T(8,128)(2,1)S(1)}, bf16[8,7296]{1,0:T(8,128)(2,1)S(1)}, u32[]{:S(2)}, u32[]{:S(2)}) collective-permute-start(bf16[8,7296]{1,0:T(8,128)(2,1)S(1)} %pack.1.refs_0_), channel_id=1, source_target_pairs={{0,1},{1,0},{2,3},{3,2},{4,5},{5,4},{6,7},{7,6},{8,9},{9,8},{10,11... | collective-permute-start | bytes 350216 | tf_op jit(solution)/shard_map/ppermute | solution.py:177
  4.2 8.1 %collective-permute-start.3 = (bf16[8,7296]{1,0:T(8,128)(2,1)S(1)}, bf16[8,7296]{1,0:T(8,128)(2,1)S(1)}, u32[]{:S(2)}, u32[]{:S(2)}) collective-permute-start(bf16[8,7296]{1,0:T(8,128)(2,1)S(1)} %pack.1.refs_0_), channel_id=1, source_target_pairs={{0,2},{1,3},{2,0},{3,1},{4,6},{5,7},{6,4},{7,5},{8,10},{9,11},{10,... | collective-permute-start | bytes 350216 | tf_op jit(solution)/shard_map/ppermute | solution.py:177
  6.8 5.6 %collective-permute-start = (bf16[8,7296]{1,0:T(8,128)(2,1)S(1)}, bf16[8,7296]{1,0:T(8,128)(2,1)S(1)}, u32[]{:S(2)}, u32[]{:S(2)}) collective-permute-start(bf16[8,7296]{1,0:T(8,128)(2,1)S(1)} %pack.1.refs_0_), channel_id=1, source_target_pairs={{0,8},{4,12},{8,0},{12,4},{1,9},{5,13},{9,1},{13,5},{2,10},{6,14},... | collective-permute-start | bytes 350216 | tf_op jit(solution)/shard_map/ppermute | solution.py:173
  8.6 6.1 %collective-permute-start.2 = (bf16[8,7296]{1,0:T(8,128)(2,1)S(1)}, bf16[8,7296]{1,0:T(8,128)(2,1)S(1)}, u32[]{:S(2)}, u32[]{:S(2)}) collective-permute-start(bf16[8,7296]{1,0:T(8,128)(2,1)S(1)} %collective-permute-done.1.refs_2_), channel_id=1, source_target_pairs={{0,8},{4,12},{8,0},{12,4},{1,9},{5,13},{9,1},{13,5},{2,10},{6,14},... | collective-permute-start | bytes 350216 | tf_op jit(solution)/shard_map/ppermute | solution.py:173
  12.4 6.1 %collective-permute-start.5 = (bf16[8,7296]{1,0:T(8,128)(2,1)S(1)}, bf16[8,7296]{1,0:T(8,128)(2,1)S(1)}, u32[]{:S(2)}, u32[]{:S(2)}) collective-permute-start(bf16[8,7296]{1,0:T(8,128)(2,1)S(1)} %collective-permute-done.3.refs_0_), channel_id=1, source_target_pairs={{0,8},{4,12},{8,0},{12,4},{1,9},{5,13},{9,1},{13,5},{2,10},{6,14},... | collective-permute-start | bytes 350216 | tf_op jit(solution)/shard_map/ppermute | solution.py:173
  13.9 4.8 %collective-permute-start.4 = (bf16[8,7296]{1,0:T(8,128)(2,1)S(1)}, bf16[8,7296]{1,0:T(8,128)(2,1)S(1)}, u32[]{:S(2)}, u32[]{:S(2)}) collective-permute-start(bf16[8,7296]{1,0:T(8,128)(2,1)S(1)} %collective-permute-done.3.refs_0_), channel_id=1, source_target_pairs={{0,1},{1,0},{2,3},{3,2},{4,5},{5,4},{6,7},{7,6},{8,9},{9,8},{10,11... | collective-permute-start | bytes 350216 | tf_op jit(solution)/shard_map/ppermute | solution.py:177
  14.7 5.7 %collective-permute-start.6 = (bf16[8,7296]{1,0:T(8,128)(2,1)S(1)}, bf16[8,7296]{1,0:T(8,128)(2,1)S(1)}, u32[]{:S(2)}, u32[]{:S(2)}) collective-permute-start(bf16[8,7296]{1,0:T(8,128)(2,1)S(1)} %collective-permute-done.3.refs_0_), channel_id=1, source_target_pairs={{0,9},{1,8},{2,11},{3,10},{4,13},{5,12},{6,15},{7,14},{8,1},{9,0},... | collective-permute-start | bytes 350216 | tf_op jit(solution)/shard_map/ppermute | solution.py:183
  16.0 4.6 %collective-permute-start.7 = (bf16[32,7296]{1,0:T(8,128)(2,1)S(1)}, bf16[32,7296]{1,0:T(8,128)(2,1)S(1)}, u32[]{:S(2)}, u32[]{:S(2)}) collective-permute-start(bf16[32,7296]{1,0:T(8,128)(2,1)S(1)} %stack.2.refs_0_), channel_id=1, source_target_pairs={{0,4},{4,0},{8,12},{12,8},{1,5},{5,1},{9,13},{13,9},{2,6},{6,2},{1... | collective-permute-start | bytes 1400840 | tf_op jit(solution)/shard_map/ppermute | solution.py:169
  20.4 6.1 %slice-start = ((s8[14680064]{0:T(1024)(128)(4,1)}), s8[4194304]{0:T(1024)(128)(4,1)S(1)}, s32[]{:S(2)}) async-start(s8[14680064]{0:T(1024)(128)(4,1)} %bitcast.3), calls=%async_computation | async-start | bytes 8388608
  20.5 6.0 %slice-start.1 = ((s8[14680064]{0:T(1024)(128)(4,1)}), s8[4194304]{0:T(1024)(128)(4,1)S(1)}, s32[]{:S(2)}) async-start(s8[14680064]{0:T(1024)(128)(4,1)} %bitcast.3), calls=%async_computation.1 | async-start | bytes 8388608
  20.5 6.0 %slice-start.2 = ((s8[14680064]{0:T(1024)(128)(4,1)}), s8[4194304]{0:T(1024)(128)(4,1)S(1)}, s32[]{:S(2)}) async-start(s8[14680064]{0:T(1024)(128)(4,1)} %bitcast.3), calls=%async_computation.2 | async-start | bytes 8388608
  20.5 6.0 %slice-start.3 = ((s8[14680064]{0:T(1024)(128)(4,1)}), s8[2097152]{0:T(1024)(128)(4,1)S(1)}, s32[]{:S(2)}) async-start(s8[14680064]{0:T(1024)(128)(4,1)} %bitcast.3), calls=%async_computation.3 | async-start | bytes 4194304
  20.5 1.9 %collective-permute-start.8 = (bf16[32,7296]{1,0:T(8,128)(2,1)S(1)}, bf16[32,7296]{1,0:T(8,128)(2,1)S(1)}, u32[]{:S(2)}, u32[]{:S(2)}) collective-permute-start(bf16[32,7296]{1,0:T(8,128)(2,1)S(1)} %stack.3.refs_1_), channel_id=1, source_target_pairs={{0,4},{4,0},{8,12},{12,8},{1,5},{5,1},{9,13},{13,9},{2,6},{6,2},{1... | collective-permute-start | bytes 1400840 | tf_op jit(solution)/shard_map/ppermute | solution.py:169
  28.6 1.7 %collective-permute-start.9 = (bf16[24,7168]{1,0:T(8,128)(2,1)S(1)}, bf16[24,7168]{1,0:T(8,128)(2,1)S(1)}, u32[]{:S(2)}, u32[]{:S(2)}) collective-permute-start(bf16[24,7168]{1,0:T(8,128)(2,1)S(1)} %get-tuple-element.27), channel_id=1, source_target_pairs={{0,4},{4,0},{8,12},{12,8},{1,5},{5,1},{9,13},{13,9},{2,6},{6,2},{1... | collective-permute-start | bytes 1032200 | tf_op jit(solution)/shard_map/ppermute | solution.py:169
  30.3 3.8 %collective-permute-start.10 = (bf16[40,7168]{1,0:T(8,128)(2,1)S(1)}, bf16[40,7168]{1,0:T(8,128)(2,1)S(1)}, u32[]{:S(2)}, u32[]{:S(2)}) collective-permute-start(bf16[40,7168]{1,0:T(8,128)(2,1)S(1)} %get-tuple-element.28), channel_id=1, source_target_pairs={{0,4},{4,0},{8,12},{12,8},{1,5},{5,1},{9,13},{13,9},{2,6},{6,2},{1... | collective-permute-start | bytes 1720328 | tf_op jit(solution)/shard_map/ppermute | solution.py:169
  30.5 5.7 %collective-permute-start.13 = (bf16[8,7168]{1,0:T(8,128)(2,1)S(1)}, bf16[8,7168]{1,0:T(8,128)(2,1)S(1)}, u32[]{:S(2)}, u32[]{:S(2)}) collective-permute-start(bf16[8,7168]{1,0:T(8,128)(2,1)S(1)} %get-tuple-element.34), channel_id=1, source_target_pairs={{0,1},{1,0},{2,3},{3,2},{4,5},{5,4},{6,7},{7,6},{8,9},{9,8},{10,11... | collective-permute-start | bytes 344072 | tf_op jit(solution)/shard_map/ppermute | solution.py:177
  31.9 6.4 %collective-permute-start.11 = (bf16[8,7168]{1,0:T(8,128)(2,1)S(1)}, bf16[8,7168]{1,0:T(8,128)(2,1)S(1)}, u32[]{:S(2)}, u32[]{:S(2)}) collective-permute-start(bf16[8,7168]{1,0:T(8,128)(2,1)S(1)} %get-tuple-element.32), channel_id=1, source_target_pairs={{0,8},{4,12},{8,0},{12,4},{1,9},{5,13},{9,1},{13,5},{2,10},{6,14},... | collective-permute-start | bytes 344072 | tf_op jit(solution)/shard_map/ppermute | solution.py:173
  32.4 7.3 %collective-permute-start.12 = (bf16[8,7168]{1,0:T(8,128)(2,1)S(1)}, bf16[8,7168]{1,0:T(8,128)(2,1)S(1)}, u32[]{:S(2)}, u32[]{:S(2)}) collective-permute-start(bf16[8,7168]{1,0:T(8,128)(2,1)S(1)} %get-tuple-element.33), channel_id=1, source_target_pairs={{0,9},{1,8},{2,11},{3,10},{4,13},{5,12},{6,15},{7,14},{8,1},{9,0},... | collective-permute-start | bytes 344072 | tf_op jit(solution)/shard_map/ppermute | solution.py:183
  36.3 5.9 %collective-permute-start.15 = (bf16[8,7168]{1,0:T(8,128)(2,1)S(1)}, bf16[8,7168]{1,0:T(8,128)(2,1)S(1)}, u32[]{:S(2)}, u32[]{:S(2)}) collective-permute-start(bf16[8,7168]{1,0:T(8,128)(2,1)S(1)} %get-tuple-element.37), channel_id=1, source_target_pairs={{0,8},{4,12},{8,0},{12,4},{1,9},{5,13},{9,1},{13,5},{2,10},{6,14},... | collective-permute-start | bytes 344072 | tf_op jit(solution)/shard_map/ppermute | solution.py:173
  39.8 8.0 %collective-permute-start.14 = (bf16[8,7168]{1,0:T(8,128)(2,1)S(1)}, bf16[8,7168]{1,0:T(8,128)(2,1)S(1)}, u32[]{:S(2)}, u32[]{:S(2)}) collective-permute-start(bf16[8,7168]{1,0:T(8,128)(2,1)S(1)} %add_convert_fusion.2), channel_id=1, source_target_pairs={{0,2},{1,3},{2,0},{3,1},{4,6},{5,7},{6,4},{7,5},{8,10},{9,11},{10,... | collective-permute-start | bytes 344072 | tf_op jit(solution)/shard_map/ppermute | solution.py:177
  42.2 7.1 %collective-permute-start.16 = (bf16[8,7168]{1,0:T(8,128)(2,1)S(1)}, bf16[8,7168]{1,0:T(8,128)(2,1)S(1)}, u32[]{:S(2)}, u32[]{:S(2)}) collective-permute-start(bf16[8,7168]{1,0:T(8,128)(2,1)S(1)} %add_convert_fusion.1), channel_id=1, source_target_pairs={{0,1},{1,0},{2,3},{3,2},{4,5},{5,4},{6,7},{7,6},{8,9},{9,8},{10,11... | collective-permute-start | bytes 344072 | tf_op jit(solution)/shard_map/ppermute | solution.py:177
  43.4 5.9 %collective-permute-start.17 = (bf16[8,7168]{1,0:T(8,128)(2,1)S(1)}, bf16[8,7168]{1,0:T(8,128)(2,1)S(1)}, u32[]{:S(2)}, u32[]{:S(2)}) collective-permute-start(bf16[8,7168]{1,0:T(8,128)(2,1)S(1)} %get-tuple-element.40), channel_id=1, source_target_pairs={{0,8},{4,12},{8,0},{12,4},{1,9},{5,13},{9,1},{13,5},{2,10},{6,14},... | collective-permute-start | bytes 344072 | tf_op jit(solution)/shard_map/ppermute | solution.py:173

commit v20 on v16

--- a/solution.py
+++ b/solution.py
@@ -22,7 +22,7 @@
     ]
     for copy in copies:
         copy.start()
-    for copy in copies:
+    for copy in copies[1:]:
         copy.wait()
     tokens_ref, ids_ref, route_ref, slot_ref = local
     rows, width = tokens_ref.shape
@@ -39,6 +39,7 @@
     second = (weights - first).astype(jnp.bfloat16).astype(jnp.float32)
     third = weights - first - second
     tail = jnp.where(column < experts, first, jnp.where(column < 2 * experts, second, third))
+    copies[0].wait()
     out_ref[:, :width] = tokens_ref[...]
     out_ref[:, width:] = jnp.where(column < 3 * experts, tail, 0.0).astype(jnp.bfloat16)
 

time: 50.1 us -> 50.1 us (level)
  no operation moved by 1% of the time
where the time goes in v20:
time: 50.1 us; the launch traced here: 49.9 us
  starting transfers between devices  23.1 us (46%)
  waiting for transfers between devices  18.3 us (37%)
  Pallas kernels  7.58 us (15%)
  other arithmetic  0.8 us (2%)
    ppermute x6, starting transfers between devices, to_place(): return lax.ppermute(value, 'local', [(i, i ^ bits) for i in range(PLACES)])  10.1 us
    ppermute x6, starting transfers between devices, to_chip(): return lax.ppermute(value, 'node', [(i, i ^ 2) for i in range(2 * CHIPS)])  9.41 us
    ppermute x6, waiting for transfers between devices, to_place(): return lax.ppermute(value, 'local', [(i, i ^ bits) for i in range(PLACES)])  7.27 us
    ppermute x6, waiting for transfers between devices, to_chip(): return lax.ppermute(value, 'node', [(i, i ^ 2) for i in range(2 * CHIPS)])  5.85 us
    pallas_call x1, Pallas kernels, hidden_units(): pl.pallas_call(functools.partial(hidden_kernel, experts), out_shape=jax.S...  4.05 us
    ppermute x4, waiting for transfers between devices, to_core(): return lax.ppermute(value, 'node', [(i, i ^ 1) for i in range(2 * CHIPS)])  3.5 us
    ppermute x2, starting transfers between devices, to_both(): return lax.ppermute(value, ('node', 'local'), perm)  3.11 us
    pallas_call x1, Pallas kernels, down(): pl.pallas_call(functools.partial(down_kernel, chunk), out_shape=[jax.Shap...  2.08 us
  transfers between devices with their start and end apart: 18, of which 12 were waited for; matrix products, arithmetic and copies ran while one was open for 0% of the time, Pallas kernels for 1%

profile of v20, /device:TPU:0, one launch (start us, length us, event | category | flops | bytes accessed | tf_op | source)
XLA Modules:
  0.0 49.9 jit_solution(8227516528570039569)
XLA Ops:
  0.0 0.0 copy-start
  0.0 0.0 copy-start.1
  0.0 1.1 %pack.1.refs_0_ = bf16[8,7296]{1,0:T(8,128)(2,1)S(1)} custom-call(bf16[8,7168]{1,0:T(8,128)(2,1)} %refs_0_.1, s32[4,8]{1,0:T(4,128)} %bitcast.6, f32[4,8]{1,0:T(4,128)} %bitcast.7, s32[8]{0:T(128)} %refs_3_.1, bf16[2,7168,512]{2,1,0:T(8,128)(2,1)} %refs_4_.3, bf16[2,7168,512]{2,1,0:T(8,128)(2,1)} %refs_5_.3, bf16[2,512,7168]{2,1,0:T(8,128)(2,1)} %refs_6_.1), custom_call_target="tpu_custom_call" | custom-call | tf_op jit(solution)/shard_map/pack/pallas_call | solution.py:51
  1.1 3.1 %collective-permute-start.1 = (bf16[8,7296]{1,0:T(8,128)(2,1)S(1)}, bf16[8,7296]{1,0:T(8,128)(2,1)S(1)}, u32[]{:S(2)}, u32[]{:S(2)}) collective-permute-start(bf16[8,7296]{1,0:T(8,128)(2,1)S(1)} %pack.1.refs_0_), channel_id=1, source_target_pairs={{0,1},{1,0},{2,3},{3,2},{4,5},{5,4},{6,7},{7,6},{8,9},{9,8},{10,11... | collective-permute-start | bytes 350216 | tf_op jit(solution)/shard_map/ppermute | solution.py:178
  4.2 2.6 %collective-permute-start.2 = (bf16[8,7296]{1,0:T(8,128)(2,1)S(1)}, bf16[8,7296]{1,0:T(8,128)(2,1)S(1)}, u32[]{:S(2)}, u32[]{:S(2)}) collective-permute-start(bf16[8,7296]{1,0:T(8,128)(2,1)S(1)} %pack.1.refs_0_), channel_id=1, source_target_pairs={{0,2},{1,3},{2,0},{3,1},{4,6},{5,7},{6,4},{7,5},{8,10},{9,11},{10,... | collective-permute-start | bytes 350216 | tf_op jit(solution)/shard_map/ppermute | solution.py:178
  6.8 1.5 %collective-permute-start = (bf16[8,7296]{1,0:T(8,128)(2,1)S(1)}, bf16[8,7296]{1,0:T(8,128)(2,1)S(1)}, u32[]{:S(2)}, u32[]{:S(2)}) collective-permute-start(bf16[8,7296]{1,0:T(8,128)(2,1)S(1)} %pack.1.refs_0_), channel_id=1, source_target_pairs={{0,8},{4,12},{8,0},{12,4},{1,9},{5,13},{9,1},{13,5},{2,10},{6,14},... | collective-permute-start | bytes 350216 | tf_op jit(solution)/shard_map/ppermute | solution.py:174
  8.3 0.3 collective-permute-done.1.refs_2_
  8.6 1.8 %collective-permute-start.3 = (bf16[8,7296]{1,0:T(8,128)(2,1)S(1)}, bf16[8,7296]{1,0:T(8,128)(2,1)S(1)}, u32[]{:S(2)}, u32[]{:S(2)}) collective-permute-start(bf16[8,7296]{1,0:T(8,128)(2,1)S(1)} %collective-permute-done.1.refs_2_), channel_id=1, source_target_pairs={{0,8},{4,12},{8,0},{12,4},{1,9},{5,13},{9,1},{13,5},{2,10},{6,14},... | collective-permute-start | bytes 350216 | tf_op jit(solution)/shard_map/ppermute | solution.py:174
  10.4 1.9 %collective-permute-done.2.refs_3_ = bf16[8,7296]{1,0:T(8,128)(2,1)S(1)} collective-permute-done((bf16[8,7296]{1,0:T(8,128)(2,1)S(1)}, bf16[8,7296]{1,0:T(8,128)(2,1)S(1)}, u32[]{:S(2)}, u32[]{:S(2)}) %collective-permute-start.2) | collective-permute-done | bytes 116768 | tf_op jit(solution)/shard_map/ppermute | solution.py:178
  12.3 0.1 collective-permute-done.refs_1_
  12.4 1.5 %collective-permute-start.5 = (bf16[8,7296]{1,0:T(8,128)(2,1)S(1)}, bf16[8,7296]{1,0:T(8,128)(2,1)S(1)}, u32[]{:S(2)}, u32[]{:S(2)}) collective-permute-start(bf16[8,7296]{1,0:T(8,128)(2,1)S(1)} %collective-permute-done.2.refs_3_), channel_id=1, source_target_pairs={{0,8},{4,12},{8,0},{12,4},{1,9},{5,13},{9,1},{13,5},{2,10},{6,14},... | collective-permute-start | bytes 350216 | tf_op jit(solution)/shard_map/ppermute | solution.py:174
  13.9 0.8 %collective-permute-start.4 = (bf16[8,7296]{1,0:T(8,128)(2,1)S(1)}, bf16[8,7296]{1,0:T(8,128)(2,1)S(1)}, u32[]{:S(2)}, u32[]{:S(2)}) collective-permute-start(bf16[8,7296]{1,0:T(8,128)(2,1)S(1)} %collective-permute-done.2.refs_3_), channel_id=1, source_target_pairs={{0,1},{1,0},{2,3},{3,2},{4,5},{5,4},{6,7},{7,6},{8,9},{9,8},{10,11... | collective-permute-start | bytes 350216 | tf_op jit(solution)/shard_map/ppermute | solution.py:178
  14.7 0.0 collective-permute-done.3.refs_0_
  14.7 1.2 %collective-permute-start.6 = (bf16[8,7296]{1,0:T(8,128)(2,1)S(1)}, bf16[8,7296]{1,0:T(8,128)(2,1)S(1)}, u32[]{:S(2)}, u32[]{:S(2)}) collective-permute-start(bf16[8,7296]{1,0:T(8,128)(2,1)S(1)} %collective-permute-done.2.refs_3_), channel_id=1, source_target_pairs={{0,9},{1,8},{2,11},{3,10},{4,13},{5,12},{6,15},{7,14},{8,1},{9,0},... | collective-permute-start | bytes 350216 | tf_op jit(solution)/shard_map/ppermute | solution.py:184
  15.9 0.1 stack.2.refs_0_
  16.0 0.1 collective-permute-start.7
  16.1 2.4 %collective-permute-done.5.refs_2_ = bf16[8,7296]{1,0:T(8,128)(2,1)S(1)} collective-permute-done((bf16[8,7296]{1,0:T(8,128)(2,1)S(1)}, bf16[8,7296]{1,0:T(8,128)(2,1)S(1)}, u32[]{:S(2)}, u32[]{:S(2)}) %collective-permute-start.5) | collective-permute-done | bytes 116768 | tf_op jit(solution)/shard_map/ppermute | solution.py:174
  18.5 0.2 collective-permute-done.4.refs_1_
  18.7 1.7 %collective-permute-done.6.refs_3_ = bf16[8,7296]{1,0:T(8,128)(2,1)S(1)} collective-permute-done((bf16[8,7296]{1,0:T(8,128)(2,1)S(1)}, bf16[8,7296]{1,0:T(8,128)(2,1)S(1)}, u32[]{:S(2)}, u32[]{:S(2)}) %collective-permute-start.6) | collective-permute-done | bytes 116768 | tf_op jit(solution)/shard_map/ppermute | solution.py:184
  20.4 0.0 slice-start
  20.4 0.1 stack.3.refs_1_
  20.5 0.0 slice-start.1
  20.5 0.0 slice-start.2
  20.5 0.0 slice-start.3
  20.5 0.1 collective-permute-start.8
  20.6 0.0 collective-permute-done.7.refs_2_
  20.6 1.8 %collective-permute-done.8.refs_3_ = bf16[32,7296]{1,0:T(8,128)(2,1)S(1)} collective-permute-done((bf16[32,7296]{1,0:T(8,128)(2,1)S(1)}, bf16[32,7296]{1,0:T(8,128)(2,1)S(1)}, u32[]{:S(2)}, u32[]{:S(2)}) %collective-permute-start.8) | collective-permute-done | bytes 466976 | tf_op jit(solution)/shard_map/ppermute | solution.py:170
  22.4 0.0 copy-done
  22.4 0.0 copy-done.1
  22.4 4.1 %hidden.1.hidden_ref = bf16[128,1024]{1,0:T(8,128)(2,1)S(1)} custom-call(bf16[32,7296]{1,0:T(8,128)(2,1)S(1)} %stack.2.refs_0_, bf16[32,7296]{1,0:T(8,128)(2,1)S(1)} %stack.3.refs_1_, bf16[32,7296]{1,0:T(8,128)(2,1)S(1)} %collective-permute-done.7.refs_2_, bf16[32,7296]{1,0:T(8,128)(2,1)S(1)} %collective-permute-done.8.refs_3_, ...), custom_call_target="tpu_custom_call" | custom-call | flops 3758096384 | bytes 29360128 | tf_op jit(solution)/shard_map/hidden/pallas_call | solution.py:114
  26.5 0.0 slice-done
  26.5 0.0 slice-done.1
  26.5 0.0 slice-done.2
  26.5 0.0 slice-done.3
  26.5 2.1 %down.1 = (bf16[32,7168]{1,0:T(8,128)(2,1)S(1)}, bf16[32,7168]{1,0:T(8,128)(2,1)S(1)}, bf16[32,7168]{1,0:T(8,128)(2,1)S(1)}, bf16[32,7168]{1,0:T(8,128)(2,1)S(1)}) custom-call(bf16[128,1024]{1,0:T(8,128)(2,1)S(1)} %hidden.1.hidden_ref, bf16[1024,7168]{1,0:T(8,128)(2,1)S(1)} %bitcast.5), custom_call_target="tpu_custom_call" | custom-call | flops 1879048192 | bytes 14680064 | tf_op jit(solution)/shard_map/down/pallas_call | solution.py:151
  28.6 0.2 collective-permute-start.9
  28.8 1.7 %collective-permute-done.9.refs_1_ = bf16[32,7168]{1,0:T(8,128)(2,1)S(1)} collective-permute-done((bf16[32,7168]{1,0:T(8,128)(2,1)S(1)}, bf16[32,7168]{1,0:T(8,128)(2,1)S(1)}, u32[]{:S(2)}, u32[]{:S(2)}) %collective-permute-start.9) | collective-permute-done | bytes 458784 | tf_op jit(solution)/shard_map/ppermute | solution.py:170
  30.5 0.1 collective-permute-start.10
  30.6 0.1 sums.3
  30.7 1.8 %collective-permute-start.15 = (bf16[8,7168]{1,0:T(8,128)(2,1)S(1)}, bf16[8,7168]{1,0:T(8,128)(2,1)S(1)}, u32[]{:S(2)}, u32[]{:S(2)}) collective-permute-start(bf16[8,7168]{1,0:T(8,128)(2,1)S(1)} %get-tuple-element.34), channel_id=1, source_target_pairs={{0,8},{4,12},{8,0},{12,4},{1,9},{5,13},{9,1},{13,5},{2,10},{6,14},... | collective-permute-start | bytes 344072 | tf_op jit(solution)/shard_map/ppermute | solution.py:174
  32.5 0.1 collective-permute-start.11
  32.6 1.5 %collective-permute-start.12 = (bf16[8,7168]{1,0:T(8,128)(2,1)S(1)}, bf16[8,7168]{1,0:T(8,128)(2,1)S(1)}, u32[]{:S(2)}, u32[]{:S(2)}) collective-permute-start(bf16[8,7168]{1,0:T(8,128)(2,1)S(1)} %get-tuple-element.31), channel_id=1, source_target_pairs={{0,8},{4,12},{8,0},{12,4},{1,9},{5,13},{9,1},{13,5},{2,10},{6,14},... | collective-permute-start | bytes 344072 | tf_op jit(solution)/shard_map/ppermute | solution.py:174
  34.1 1.9 %collective-permute-start.13 = (bf16[8,7168]{1,0:T(8,128)(2,1)S(1)}, bf16[8,7168]{1,0:T(8,128)(2,1)S(1)}, u32[]{:S(2)}, u32[]{:S(2)}) collective-permute-start(bf16[8,7168]{1,0:T(8,128)(2,1)S(1)} %get-tuple-element.32), channel_id=1, source_target_pairs={{0,9},{1,8},{2,11},{3,10},{4,13},{5,12},{6,15},{7,14},{8,1},{9,0},... | collective-permute-start | bytes 344072 | tf_op jit(solution)/shard_map/ppermute | solution.py:184
  36.0 0.0 collective-permute-done.10.refs_1_
  36.0 0.1 sums.2
  36.1 0.7 %collective-permute-done.15 = bf16[8,7168]{1,0:T(8,128)(2,1)S(1)} collective-permute-done((bf16[8,7168]{1,0:T(8,128)(2,1)S(1)}, bf16[8,7168]{1,0:T(8,128)(2,1)S(1)}, u32[]{:S(2)}, u32[]{:S(2)}) %collective-permute-start.15) | collective-permute-done | bytes 114720 | tf_op jit(solution)/shard_map/ppermute | solution.py:174
  36.8 1.3 %collective-permute-start.16 = (bf16[8,7168]{1,0:T(8,128)(2,1)S(1)}, bf16[8,7168]{1,0:T(8,128)(2,1)S(1)}, u32[]{:S(2)}, u32[]{:S(2)}) collective-permute-start(bf16[8,7168]{1,0:T(8,128)(2,1)S(1)} %add_convert_fusion.1), channel_id=1, source_target_pairs={{0,1},{1,0},{2,3},{3,2},{4,5},{5,4},{6,7},{7,6},{8,9},{9,8},{10,11... | collective-permute-start | bytes 344072 | tf_op jit(solution)/shard_map/ppermute | solution.py:178
  38.1 0.4 collective-permute-done.11
  38.5 2.6 %collective-permute-done.12 = bf16[8,7168]{1,0:T(8,128)(2,1)S(1)} collective-permute-done((bf16[8,7168]{1,0:T(8,128)(2,1)S(1)}, bf16[8,7168]{1,0:T(8,128)(2,1)S(1)}, u32[]{:S(2)}, u32[]{:S(2)}) %collective-permute-start.12) | collective-permute-done | bytes 114720 | tf_op jit(solution)/shard_map/ppermute | solution.py:174
  41.1 0.0 collective-permute-done.13
  41.1 0.1 add_convert_fusion.2
  41.2 2.2 %collective-permute-start.14 = (bf16[8,7168]{1,0:T(8,128)(2,1)S(1)}, bf16[8,7168]{1,0:T(8,128)(2,1)S(1)}, u32[]{:S(2)}, u32[]{:S(2)}) collective-permute-start(bf16[8,7168]{1,0:T(8,128)(2,1)S(1)} %add_convert_fusion.2), channel_id=1, source_target_pairs={{0,2},{1,3},{2,0},{3,1},{4,6},{5,7},{6,4},{7,5},{8,10},{9,11},{10,... | collective-permute-start | bytes 344072 | tf_op jit(solution)/shard_map/ppermute | solution.py:178
  43.4 0.0 collective-permute-done.16
  43.4 1.4 %collective-permute-start.17 = (bf16[8,7168]{1,0:T(8,128)(2,1)S(1)}, bf16[8,7168]{1,0:T(8,128)(2,1)S(1)}, u32[]{:S(2)}, u32[]{:S(2)}) collective-permute-start(bf16[8,7168]{1,0:T(8,128)(2,1)S(1)} %get-tuple-element.36), channel_id=1, source_target_pairs={{0,8},{4,12},{8,0},{12,4},{1,9},{5,13},{9,1},{13,5},{2,10},{6,14},... | collective-permute-start | bytes 344072 | tf_op jit(solution)/shard_map/ppermute | solution.py:174
  44.8 4.4 %collective-permute-done.14 = bf16[8,7168]{1,0:T(8,128)(2,1)S(1)} collective-permute-done((bf16[8,7168]{1,0:T(8,128)(2,1)S(1)}, bf16[8,7168]{1,0:T(8,128)(2,1)S(1)}, u32[]{:S(2)}, u32[]{:S(2)}) %collective-permute-start.14) | collective-permute-done | bytes 114720 | tf_op jit(solution)/shard_map/ppermute | solution.py:178
  49.2 0.0 collective-permute-done.17
  49.2 0.7 %add_convert_fusion = bf16[8,7168]{1,0:T(8,128)(2,1)} fusion(bf16[8,7168]{1,0:T(8,128)(2,1)S(1)} %collective-permute-done.17, bf16[8,7168]{1,0:T(8,128)(2,1)S(1)} %collective-permute-done.16, bf16[8,7168]{1,0:T(8,128)(2,1)S(1)} %collective-permute-done.14, bf16[8,7168]{1,0:T(8,128)(2,1)S(1)} %get-tuple-element.27), kind=kLoop, calls=%fused_computation | loop fusion | flops 458752 | bytes 573440 | tf_op jit(solution)/shard_map/convert_element_type | solution.py:243
  (2 shorter events, 0.0 us)
Async XLA Ops:
  0.0 22.4 %copy-start = (bf16[2,7168,512]{2,1,0:T(8,128)(2,1)S(1)}, bf16[2,7168,512]{2,1,0:T(8,128)(2,1)}, u32[]{:S(2)}) copy-start(bf16[2,7168,512]{2,1,0:T(8,128)(2,1)} %refs_4_.3) | copy-start | bytes 44040196
  0.0 22.4 %copy-start.1 = (bf16[2,7168,512]{2,1,0:T(8,128)(2,1)S(1)}, bf16[2,7168,512]{2,1,0:T(8,128)(2,1)}, u32[]{:S(2)}) copy-start(bf16[2,7168,512]{2,1,0:T(8,128)(2,1)} %refs_5_.3) | copy-start | bytes 44040196
  1.1 7.5 %collective-permute-start.1 = (bf16[8,7296]{1,0:T(8,128)(2,1)S(1)}, bf16[8,7296]{1,0:T(8,128)(2,1)S(1)}, u32[]{:S(2)}, u32[]{:S(2)}) collective-permute-start(bf16[8,7296]{1,0:T(8,128)(2,1)S(1)} %pack.1.refs_0_), channel_id=1, source_target_pairs={{0,1},{1,0},{2,3},{3,2},{4,5},{5,4},{6,7},{7,6},{8,9},{9,8},{10,11... | collective-permute-start | bytes 350216 | tf_op jit(solution)/shard_map/ppermute | solution.py:178
  4.2 8.1 %collective-permute-start.2 = (bf16[8,7296]{1,0:T(8,128)(2,1)S(1)}, bf16[8,7296]{1,0:T(8,128)(2,1)S(1)}, u32[]{:S(2)}, u32[]{:S(2)}) collective-permute-start(bf16[8,7296]{1,0:T(8,128)(2,1)S(1)} %pack.1.refs_0_), channel_id=1, source_target_pairs={{0,2},{1,3},{2,0},{3,1},{4,6},{5,7},{6,4},{7,5},{8,10},{9,11},{10,... | collective-permute-start | bytes 350216 | tf_op jit(solution)/shard_map/ppermute | solution.py:178
  6.8 5.6 %collective-permute-start = (bf16[8,7296]{1,0:T(8,128)(2,1)S(1)}, bf16[8,7296]{1,0:T(8,128)(2,1)S(1)}, u32[]{:S(2)}, u32[]{:S(2)}) collective-permute-start(bf16[8,7296]{1,0:T(8,128)(2,1)S(1)} %pack.1.refs_0_), channel_id=1, source_target_pairs={{0,8},{4,12},{8,0},{12,4},{1,9},{5,13},{9,1},{13,5},{2,10},{6,14},... | collective-permute-start | bytes 350216 | tf_op jit(solution)/shard_map/ppermute | solution.py:174
  8.6 6.1 %collective-permute-start.3 = (bf16[8,7296]{1,0:T(8,128)(2,1)S(1)}, bf16[8,7296]{1,0:T(8,128)(2,1)S(1)}, u32[]{:S(2)}, u32[]{:S(2)}) collective-permute-start(bf16[8,7296]{1,0:T(8,128)(2,1)S(1)} %collective-permute-done.1.refs_2_), channel_id=1, source_target_pairs={{0,8},{4,12},{8,0},{12,4},{1,9},{5,13},{9,1},{13,5},{2,10},{6,14},... | collective-permute-start | bytes 350216 | tf_op jit(solution)/shard_map/ppermute | solution.py:174
  12.4 6.1 %collective-permute-start.5 = (bf16[8,7296]{1,0:T(8,128)(2,1)S(1)}, bf16[8,7296]{1,0:T(8,128)(2,1)S(1)}, u32[]{:S(2)}, u32[]{:S(2)}) collective-permute-start(bf16[8,7296]{1,0:T(8,128)(2,1)S(1)} %collective-permute-done.2.refs_3_), channel_id=1, source_target_pairs={{0,8},{4,12},{8,0},{12,4},{1,9},{5,13},{9,1},{13,5},{2,10},{6,14},... | collective-permute-start | bytes 350216 | tf_op jit(solution)/shard_map/ppermute | solution.py:174
  13.9 4.8 %collective-permute-start.4 = (bf16[8,7296]{1,0:T(8,128)(2,1)S(1)}, bf16[8,7296]{1,0:T(8,128)(2,1)S(1)}, u32[]{:S(2)}, u32[]{:S(2)}) collective-permute-start(bf16[8,7296]{1,0:T(8,128)(2,1)S(1)} %collective-permute-done.2.refs_3_), channel_id=1, source_target_pairs={{0,1},{1,0},{2,3},{3,2},{4,5},{5,4},{6,7},{7,6},{8,9},{9,8},{10,11... | collective-permute-start | bytes 350216 | tf_op jit(solution)/shard_map/ppermute | solution.py:178
  14.7 5.7 %collective-permute-start.6 = (bf16[8,7296]{1,0:T(8,128)(2,1)S(1)}, bf16[8,7296]{1,0:T(8,128)(2,1)S(1)}, u32[]{:S(2)}, u32[]{:S(2)}) collective-permute-start(bf16[8,7296]{1,0:T(8,128)(2,1)S(1)} %collective-permute-done.2.refs_3_), channel_id=1, source_target_pairs={{0,9},{1,8},{2,11},{3,10},{4,13},{5,12},{6,15},{7,14},{8,1},{9,0},... | collective-permute-start | bytes 350216 | tf_op jit(solution)/shard_map/ppermute | solution.py:184
  16.0 4.6 %collective-permute-start.7 = (bf16[32,7296]{1,0:T(8,128)(2,1)S(1)}, bf16[32,7296]{1,0:T(8,128)(2,1)S(1)}, u32[]{:S(2)}, u32[]{:S(2)}) collective-permute-start(bf16[32,7296]{1,0:T(8,128)(2,1)S(1)} %stack.2.refs_0_), channel_id=1, source_target_pairs={{0,4},{4,0},{8,12},{12,8},{1,5},{5,1},{9,13},{13,9},{2,6},{6,2},{1... | collective-permute-start | bytes 1400840 | tf_op jit(solution)/shard_map/ppermute | solution.py:170
  20.4 6.1 %slice-start = ((s8[14680064]{0:T(1024)(128)(4,1)}), s8[4194304]{0:T(1024)(128)(4,1)S(1)}, s32[]{:S(2)}) async-start(s8[14680064]{0:T(1024)(128)(4,1)} %bitcast.3), calls=%async_computation | async-start | bytes 8388608
  20.5 6.0 %slice-start.1 = ((s8[14680064]{0:T(1024)(128)(4,1)}), s8[4194304]{0:T(1024)(128)(4,1)S(1)}, s32[]{:S(2)}) async-start(s8[14680064]{0:T(1024)(128)(4,1)} %bitcast.3), calls=%async_computation.1 | async-start | bytes 8388608
  20.5 6.0 %slice-start.2 = ((s8[14680064]{0:T(1024)(128)(4,1)}), s8[4194304]{0:T(1024)(128)(4,1)S(1)}, s32[]{:S(2)}) async-start(s8[14680064]{0:T(1024)(128)(4,1)} %bitcast.3), calls=%async_computation.2 | async-start | bytes 8388608
  20.5 6.0 %slice-start.3 = ((s8[14680064]{0:T(1024)(128)(4,1)}), s8[2097152]{0:T(1024)(128)(4,1)S(1)}, s32[]{:S(2)}) async-start(s8[14680064]{0:T(1024)(128)(4,1)} %bitcast.3), calls=%async_computation.3 | async-start | bytes 4194304
  20.5 1.9 %collective-permute-start.8 = (bf16[32,7296]{1,0:T(8,128)(2,1)S(1)}, bf16[32,7296]{1,0:T(8,128)(2,1)S(1)}, u32[]{:S(2)}, u32[]{:S(2)}) collective-permute-start(bf16[32,7296]{1,0:T(8,128)(2,1)S(1)} %stack.3.refs_1_), channel_id=1, source_target_pairs={{0,4},{4,0},{8,12},{12,8},{1,5},{5,1},{9,13},{13,9},{2,6},{6,2},{1... | collective-permute-start | bytes 1400840 | tf_op jit(solution)/shard_map/ppermute | solution.py:170
  28.6 1.9 %collective-permute-start.9 = (bf16[32,7168]{1,0:T(8,128)(2,1)S(1)}, bf16[32,7168]{1,0:T(8,128)(2,1)S(1)}, u32[]{:S(2)}, u32[]{:S(2)}) collective-permute-start(bf16[32,7168]{1,0:T(8,128)(2,1)S(1)} %get-tuple-element.25), channel_id=1, source_target_pairs={{0,4},{4,0},{8,12},{12,8},{1,5},{5,1},{9,13},{13,9},{2,6},{6,2},{1... | collective-permute-start | bytes 1376264 | tf_op jit(solution)/shard_map/ppermute | solution.py:170
  30.5 5.5 %collective-permute-start.10 = (bf16[32,7168]{1,0:T(8,128)(2,1)S(1)}, bf16[32,7168]{1,0:T(8,128)(2,1)S(1)}, u32[]{:S(2)}, u32[]{:S(2)}) collective-permute-start(bf16[32,7168]{1,0:T(8,128)(2,1)S(1)} %get-tuple-element.26), channel_id=1, source_target_pairs={{0,4},{4,0},{8,12},{12,8},{1,5},{5,1},{9,13},{13,9},{2,6},{6,2},{1... | collective-permute-start | bytes 1376264 | tf_op jit(solution)/shard_map/ppermute | solution.py:170
  30.7 6.0 %collective-permute-start.15 = (bf16[8,7168]{1,0:T(8,128)(2,1)S(1)}, bf16[8,7168]{1,0:T(8,128)(2,1)S(1)}, u32[]{:S(2)}, u32[]{:S(2)}) collective-permute-start(bf16[8,7168]{1,0:T(8,128)(2,1)S(1)} %get-tuple-element.34), channel_id=1, source_target_pairs={{0,8},{4,12},{8,0},{12,4},{1,9},{5,13},{9,1},{13,5},{2,10},{6,14},... | collective-permute-start | bytes 344072 | tf_op jit(solution)/shard_map/ppermute | solution.py:174
  32.5 6.0 %collective-permute-start.11 = (bf16[8,7168]{1,0:T(8,128)(2,1)S(1)}, bf16[8,7168]{1,0:T(8,128)(2,1)S(1)}, u32[]{:S(2)}, u32[]{:S(2)}) collective-permute-start(bf16[8,7168]{1,0:T(8,128)(2,1)S(1)} %get-tuple-element.30), channel_id=1, source_target_pairs={{0,1},{1,0},{2,3},{3,2},{4,5},{5,4},{6,7},{7,6},{8,9},{9,8},{10,11... | collective-permute-start | bytes 344072 | tf_op jit(solution)/shard_map/ppermute | solution.py:178
  32.6 8.5 %collective-permute-start.12 = (bf16[8,7168]{1,0:T(8,128)(2,1)S(1)}, bf16[8,7168]{1,0:T(8,128)(2,1)S(1)}, u32[]{:S(2)}, u32[]{:S(2)}) collective-permute-start(bf16[8,7168]{1,0:T(8,128)(2,1)S(1)} %get-tuple-element.31), channel_id=1, source_target_pairs={{0,8},{4,12},{8,0},{12,4},{1,9},{5,13},{9,1},{13,5},{2,10},{6,14},... | collective-permute-start | bytes 344072 | tf_op jit(solution)/shard_map/ppermute | solution.py:174
  34.1 7.1 %collective-permute-start.13 = (bf16[8,7168]{1,0:T(8,128)(2,1)S(1)}, bf16[8,7168]{1,0:T(8,128)(2,1)S(1)}, u32[]{:S(2)}, u32[]{:S(2)}) collective-permute-start(bf16[8,7168]{1,0:T(8,128)(2,1)S(1)} %get-tuple-element.32), channel_id=1, source_target_pairs={{0,9},{1,8},{2,11},{3,10},{4,13},{5,12},{6,15},{7,14},{8,1},{9,0},... | collective-permute-start | bytes 344072 | tf_op jit(solution)/shard_map/ppermute | solution.py:184
  36.8 6.6 %collective-permute-start.16 = (bf16[8,7168]{1,0:T(8,128)(2,1)S(1)}, bf16[8,7168]{1,0:T(8,128)(2,1)S(1)}, u32[]{:S(2)}, u32[]{:S(2)}) collective-permute-start(bf16[8,7168]{1,0:T(8,128)(2,1)S(1)} %add_convert_fusion.1), channel_id=1, source_target_pairs={{0,1},{1,0},{2,3},{3,2},{4,5},{5,4},{6,7},{7,6},{8,9},{9,8},{10,11... | collective-permute-start | bytes 344072 | tf_op jit(solution)/shard_map/ppermute | solution.py:178
  41.2 8.0 %collective-permute-start.14 = (bf16[8,7168]{1,0:T(8,128)(2,1)S(1)}, bf16[8,7168]{1,0:T(8,128)(2,1)S(1)}, u32[]{:S(2)}, u32[]{:S(2)}) collective-permute-start(bf16[8,7168]{1,0:T(8,128)(2,1)S(1)} %add_convert_fusion.2), channel_id=1, source_target_pairs={{0,2},{1,3},{2,0},{3,1},{4,6},{5,7},{6,4},{7,5},{8,10},{9,11},{10,... | collective-permute-start | bytes 344072 | tf_op jit(solution)/shard_map/ppermute | solution.py:178
  43.4 5.8 %collective-permute-start.17 = (bf16[8,7168]{1,0:T(8,128)(2,1)S(1)}, bf16[8,7168]{1,0:T(8,128)(2,1)S(1)}, u32[]{:S(2)}, u32[]{:S(2)}) collective-permute-start(bf16[8,7168]{1,0:T(8,128)(2,1)S(1)} %get-tuple-element.36), channel_id=1, source_target_pairs={{0,8},{4,12},{8,0},{12,4},{1,9},{5,13},{9,1},{13,5},{2,10},{6,14},... | collective-permute-start | bytes 344072 | tf_op jit(solution)/shard_map/ppermute | solution.py:174

commit v21 on v18

--- a/solution.py
+++ b/solution.py
@@ -238,7 +238,7 @@
     third = to_place(third, 1)
     second = total(second, far_second, far_third, third).astype(jnp.bfloat16)
     own, far_own, first, far_first = sums(early, other_early)
-    first = total(first, to_chip(after(far_first, far_second))).astype(jnp.bfloat16)
+    first = total(first, to_chip(after(far_first, far_second, third))).astype(jnp.bfloat16)
     first, far_own = lax.optimization_barrier((first, far_own))
     second_here, first_here, far_own = to_place(second, 2), to_place(first, 1), to_chip(far_own)
     return total(own, second_here, first_here, far_own).astype(jnp.bfloat16)

time: 50.5 us -> 49.4 us (0.978)
  starting transfers between devices: 22.8 us -> 21.1 us
  waiting for transfers between devices: 19 us -> 19.6 us
    ppermute x6, waiting for transfers between devices: 7.27 us -> 5.43 us  [to_chip(): return lax.ppermute(value, 'node', [(i, i ^ 2) for i in range(2 * CHIPS)])]
    ppermute x6, waiting for transfers between devices: 6.53 us -> 7.95 us  [to_place(): return lax.ppermute(value, 'local', [(i, i ^ bits) for i in range(PLACES)])]
    ppermute x6, starting transfers between devices: 10.5 us -> 9.28 us  [to_place(): return lax.ppermute(value, 'local', [(i, i ^ bits) for i in range(PLACES)])]
    ppermute x6, starting transfers between devices: 9.51 us -> 8.42 us  [to_chip(): return lax.ppermute(value, 'node', [(i, i ^ 2) for i in range(2 * CHIPS)])]
    ppermute x2, waiting for transfers between devices: 1.68 us -> 2.77 us  [to_both(): return lax.ppermute(value, ('node', 'local'), perm)]
    ppermute x2, starting transfers between devices: 2.25 us -> 2.89 us  [to_both(): return lax.ppermute(value, ('node', 'local'), perm)]
  transfers between devices with their start and end apart: 18 -> 18, of which waited for: 13 -> 14; matrix products, arithmetic and copies ran while one was open for 0% -> 0% of each run, Pallas kernels for 1% -> 1%
where the time goes in v21:
time: 49.4 us; the launch traced here: 49.3 us
  starting transfers between devices  21.1 us (43%)
  waiting for transfers between devices  19.6 us (40%)
  Pallas kernels  7.58 us (15%)
  other arithmetic  0.8 us (2%)
    ppermute x6, starting transfers between devices, to_place(): return lax.ppermute(value, 'local', [(i, i ^ bits) for i in range(PLACES)])  9.28 us
    ppermute x6, starting transfers between devices, to_chip(): return lax.ppermute(value, 'node', [(i, i ^ 2) for i in range(2 * CHIPS)])  8.42 us
    ppermute x6, waiting for transfers between devices, to_place(): return lax.ppermute(value, 'local', [(i, i ^ bits) for i in range(PLACES)])  7.95 us
    ppermute x6, waiting for transfers between devices, to_chip(): return lax.ppermute(value, 'node', [(i, i ^ 2) for i in range(2 * CHIPS)])  5.43 us
    pallas_call x1, Pallas kernels, hidden_units(): pl.pallas_call(functools.partial(hidden_kernel, experts), out_shape=jax.S...  4.05 us
    ppermute x4, waiting for transfers between devices, to_core(): return lax.ppermute(value, 'node', [(i, i ^ 1) for i in range(2 * CHIPS)])  3.5 us
    ppermute x2, starting transfers between devices, to_both(): return lax.ppermute(value, ('node', 'local'), perm)  2.89 us
    ppermute x2, waiting for transfers between devices, to_both(): return lax.ppermute(value, ('node', 'local'), perm)  2.77 us
  transfers between devices with their start and end apart: 18, of which 14 were waited for; matrix products, arithmetic and copies ran while one was open for 0% of the time, Pallas kernels for 1%

profile of v21, /device:TPU:0, one launch (start us, length us, event | category | flops | bytes accessed | tf_op | source)
XLA Modules:
  0.0 49.3 jit_solution(10877952995340386919)
XLA Ops:
  0.0 0.0 copy-start
  0.0 0.0 copy-start.1
  0.0 1.1 %pack.1.refs_0_ = bf16[8,7296]{1,0:T(8,128)(2,1)S(1)} custom-call(bf16[8,7168]{1,0:T(8,128)(2,1)} %refs_0_.1, s32[4,8]{1,0:T(4,128)} %bitcast.6, f32[4,8]{1,0:T(4,128)} %bitcast.7, s32[8]{0:T(128)} %refs_3_.1, bf16[2,7168,512]{2,1,0:T(8,128)(2,1)} %refs_4_.3, bf16[2,7168,512]{2,1,0:T(8,128)(2,1)} %refs_5_.3, bf16[2,512,7168]{2,1,0:T(8,128)(2,1)} %refs_6_.1), custom_call_target="tpu_custom_call" | custom-call | tf_op jit(solution)/shard_map/pack/pallas_call | solution.py:51
  1.1 3.1 %collective-permute-start.1 = (bf16[8,7296]{1,0:T(8,128)(2,1)S(1)}, bf16[8,7296]{1,0:T(8,128)(2,1)S(1)}, u32[]{:S(2)}, u32[]{:S(2)}) collective-permute-start(bf16[8,7296]{1,0:T(8,128)(2,1)S(1)} %pack.1.refs_0_), channel_id=1, source_target_pairs={{0,1},{1,0},{2,3},{3,2},{4,5},{5,4},{6,7},{7,6},{8,9},{9,8},{10,11... | collective-permute-start | bytes 350216 | tf_op jit(solution)/shard_map/ppermute | solution.py:178
  4.2 2.6 %collective-permute-start.3 = (bf16[8,7296]{1,0:T(8,128)(2,1)S(1)}, bf16[8,7296]{1,0:T(8,128)(2,1)S(1)}, u32[]{:S(2)}, u32[]{:S(2)}) collective-permute-start(bf16[8,7296]{1,0:T(8,128)(2,1)S(1)} %pack.1.refs_0_), channel_id=1, source_target_pairs={{0,2},{1,3},{2,0},{3,1},{4,6},{5,7},{6,4},{7,5},{8,10},{9,11},{10,... | collective-permute-start | bytes 350216 | tf_op jit(solution)/shard_map/ppermute | solution.py:178
  6.8 1.5 %collective-permute-start = (bf16[8,7296]{1,0:T(8,128)(2,1)S(1)}, bf16[8,7296]{1,0:T(8,128)(2,1)S(1)}, u32[]{:S(2)}, u32[]{:S(2)}) collective-permute-start(bf16[8,7296]{1,0:T(8,128)(2,1)S(1)} %pack.1.refs_0_), channel_id=1, source_target_pairs={{0,8},{4,12},{8,0},{12,4},{1,9},{5,13},{9,1},{13,5},{2,10},{6,14},... | collective-permute-start | bytes 350216 | tf_op jit(solution)/shard_map/ppermute | solution.py:174
  8.3 0.3 collective-permute-done.1.refs_2_
  8.6 1.8 %collective-permute-start.2 = (bf16[8,7296]{1,0:T(8,128)(2,1)S(1)}, bf16[8,7296]{1,0:T(8,128)(2,1)S(1)}, u32[]{:S(2)}, u32[]{:S(2)}) collective-permute-start(bf16[8,7296]{1,0:T(8,128)(2,1)S(1)} %collective-permute-done.1.refs_2_), channel_id=1, source_target_pairs={{0,8},{4,12},{8,0},{12,4},{1,9},{5,13},{9,1},{13,5},{2,10},{6,14},... | collective-permute-start | bytes 350216 | tf_op jit(solution)/shard_map/ppermute | solution.py:174
  10.4 1.9 %collective-permute-done.3.refs_0_ = bf16[8,7296]{1,0:T(8,128)(2,1)S(1)} collective-permute-done((bf16[8,7296]{1,0:T(8,128)(2,1)S(1)}, bf16[8,7296]{1,0:T(8,128)(2,1)S(1)}, u32[]{:S(2)}, u32[]{:S(2)}) %collective-permute-start.3) | collective-permute-done | bytes 116768 | tf_op jit(solution)/shard_map/ppermute | solution.py:178
  12.3 0.1 collective-permute-done.refs_1_
  12.4 1.5 %collective-permute-start.5 = (bf16[8,7296]{1,0:T(8,128)(2,1)S(1)}, bf16[8,7296]{1,0:T(8,128)(2,1)S(1)}, u32[]{:S(2)}, u32[]{:S(2)}) collective-permute-start(bf16[8,7296]{1,0:T(8,128)(2,1)S(1)} %collective-permute-done.3.refs_0_), channel_id=1, source_target_pairs={{0,8},{4,12},{8,0},{12,4},{1,9},{5,13},{9,1},{13,5},{2,10},{6,14},... | collective-permute-start | bytes 350216 | tf_op jit(solution)/shard_map/ppermute | solution.py:174
  13.9 0.8 %collective-permute-start.4 = (bf16[8,7296]{1,0:T(8,128)(2,1)S(1)}, bf16[8,7296]{1,0:T(8,128)(2,1)S(1)}, u32[]{:S(2)}, u32[]{:S(2)}) collective-permute-start(bf16[8,7296]{1,0:T(8,128)(2,1)S(1)} %collective-permute-done.3.refs_0_), channel_id=1, source_target_pairs={{0,1},{1,0},{2,3},{3,2},{4,5},{5,4},{6,7},{7,6},{8,9},{9,8},{10,11... | collective-permute-start | bytes 350216 | tf_op jit(solution)/shard_map/ppermute | solution.py:178
  14.7 0.0 collective-permute-done.2.refs_3_
  14.7 1.2 %collective-permute-start.6 = (bf16[8,7296]{1,0:T(8,128)(2,1)S(1)}, bf16[8,7296]{1,0:T(8,128)(2,1)S(1)}, u32[]{:S(2)}, u32[]{:S(2)}) collective-permute-start(bf16[8,7296]{1,0:T(8,128)(2,1)S(1)} %collective-permute-done.3.refs_0_), channel_id=1, source_target_pairs={{0,9},{1,8},{2,11},{3,10},{4,13},{5,12},{6,15},{7,14},{8,1},{9,0},... | collective-permute-start | bytes 350216 | tf_op jit(solution)/shard_map/ppermute | solution.py:184
  15.9 0.1 stack.2.refs_0_
  16.0 0.1 collective-permute-start.7
  16.1 2.4 %collective-permute-done.5.refs_2_ = bf16[8,7296]{1,0:T(8,128)(2,1)S(1)} collective-permute-done((bf16[8,7296]{1,0:T(8,128)(2,1)S(1)}, bf16[8,7296]{1,0:T(8,128)(2,1)S(1)}, u32[]{:S(2)}, u32[]{:S(2)}) %collective-permute-start.5) | collective-permute-done | bytes 116768 | tf_op jit(solution)/shard_map/ppermute | solution.py:174
  18.5 0.2 collective-permute-done.4.refs_1_
  18.7 1.7 %collective-permute-done.6.refs_3_ = bf16[8,7296]{1,0:T(8,128)(2,1)S(1)} collective-permute-done((bf16[8,7296]{1,0:T(8,128)(2,1)S(1)}, bf16[8,7296]{1,0:T(8,128)(2,1)S(1)}, u32[]{:S(2)}, u32[]{:S(2)}) %collective-permute-start.6) | collective-permute-done | bytes 116768 | tf_op jit(solution)/shard_map/ppermute | solution.py:184
  20.4 0.0 slice-start
  20.4 0.1 stack.3.refs_1_
  20.5 0.0 slice-start.1
  20.5 0.0 slice-start.2
  20.5 0.0 slice-start.3
  20.5 0.1 collective-permute-start.8
  20.6 0.0 collective-permute-done.7.refs_2_
  20.6 1.8 %collective-permute-done.8.refs_3_ = bf16[32,7296]{1,0:T(8,128)(2,1)S(1)} collective-permute-done((bf16[32,7296]{1,0:T(8,128)(2,1)S(1)}, bf16[32,7296]{1,0:T(8,128)(2,1)S(1)}, u32[]{:S(2)}, u32[]{:S(2)}) %collective-permute-start.8) | collective-permute-done | bytes 466976 | tf_op jit(solution)/shard_map/ppermute | solution.py:170
  22.4 0.0 copy-done
  22.4 0.0 copy-done.1
  22.4 4.1 %hidden.1.hidden_ref = bf16[128,1024]{1,0:T(8,128)(2,1)S(1)} custom-call(bf16[32,7296]{1,0:T(8,128)(2,1)S(1)} %stack.2.refs_0_, bf16[32,7296]{1,0:T(8,128)(2,1)S(1)} %stack.3.refs_1_, bf16[32,7296]{1,0:T(8,128)(2,1)S(1)} %collective-permute-done.7.refs_2_, bf16[32,7296]{1,0:T(8,128)(2,1)S(1)} %collective-permute-done.8.refs_3_, ...), custom_call_target="tpu_custom_call" | custom-call | flops 3758096384 | bytes 29360128 | tf_op jit(solution)/shard_map/hidden/pallas_call | solution.py:114
  26.5 0.0 slice-done
  26.5 0.0 slice-done.1
  26.5 0.0 slice-done.2
  26.5 0.0 slice-done.3
  26.5 2.1 %down.1 = (bf16[32,7168]{1,0:T(8,128)(2,1)S(1)}, bf16[32,7168]{1,0:T(8,128)(2,1)S(1)}, bf16[32,7168]{1,0:T(8,128)(2,1)S(1)}, bf16[32,7168]{1,0:T(8,128)(2,1)S(1)}) custom-call(bf16[128,1024]{1,0:T(8,128)(2,1)S(1)} %hidden.1.hidden_ref, bf16[1024,7168]{1,0:T(8,128)(2,1)S(1)} %bitcast.5), custom_call_target="tpu_custom_call" | custom-call | flops 1879048192 | bytes 14680064 | tf_op jit(solution)/shard_map/down/pallas_call | solution.py:151
  28.6 0.2 collective-permute-start.9
  28.8 1.7 %collective-permute-done.9.refs_1_ = bf16[32,7168]{1,0:T(8,128)(2,1)S(1)} collective-permute-done((bf16[32,7168]{1,0:T(8,128)(2,1)S(1)}, bf16[32,7168]{1,0:T(8,128)(2,1)S(1)}, u32[]{:S(2)}, u32[]{:S(2)}) %collective-permute-start.9) | collective-permute-done | bytes 458784 | tf_op jit(solution)/shard_map/ppermute | solution.py:170
  30.5 0.1 collective-permute-start.10
  30.6 0.1 sums.3
  30.7 1.8 %collective-permute-start.11 = (bf16[8,7168]{1,0:T(8,128)(2,1)S(1)}, bf16[8,7168]{1,0:T(8,128)(2,1)S(1)}, u32[]{:S(2)}, u32[]{:S(2)}) collective-permute-start(bf16[8,7168]{1,0:T(8,128)(2,1)S(1)} %get-tuple-element.32), channel_id=1, source_target_pairs={{0,8},{4,12},{8,0},{12,4},{1,9},{5,13},{9,1},{13,5},{2,10},{6,14},... | collective-permute-start | bytes 344072 | tf_op jit(solution)/shard_map/ppermute | solution.py:174
  32.5 0.1 collective-permute-start.13
  32.6 1.7 %collective-permute-start.12 = (bf16[8,7168]{1,0:T(8,128)(2,1)S(1)}, bf16[8,7168]{1,0:T(8,128)(2,1)S(1)}, u32[]{:S(2)}, u32[]{:S(2)}) collective-permute-start(bf16[8,7168]{1,0:T(8,128)(2,1)S(1)} %get-tuple-element.33), channel_id=1, source_target_pairs={{0,9},{1,8},{2,11},{3,10},{4,13},{5,12},{6,15},{7,14},{8,1},{9,0},... | collective-permute-start | bytes 344072 | tf_op jit(solution)/shard_map/ppermute | solution.py:184
  34.3 0.0 collective-permute-done.10.refs_1_
  34.3 0.1 sums.2
  34.4 1.8 %collective-permute-done.11 = bf16[8,7168]{1,0:T(8,128)(2,1)S(1)} collective-permute-done((bf16[8,7168]{1,0:T(8,128)(2,1)S(1)}, bf16[8,7168]{1,0:T(8,128)(2,1)S(1)}, u32[]{:S(2)}, u32[]{:S(2)}) %collective-permute-start.11) | collective-permute-done | bytes 114720 | tf_op jit(solution)/shard_map/ppermute | solution.py:174
  36.2 2.3 %collective-permute-done.13 = bf16[8,7168]{1,0:T(8,128)(2,1)S(1)} collective-permute-done((bf16[8,7168]{1,0:T(8,128)(2,1)S(1)}, bf16[8,7168]{1,0:T(8,128)(2,1)S(1)}, u32[]{:S(2)}, u32[]{:S(2)}) %collective-permute-start.13) | collective-permute-done | bytes 114720 | tf_op jit(solution)/shard_map/ppermute | solution.py:178
  38.5 0.3 collective-permute-start.15
  38.8 1.1 %collective-permute-done.12 = bf16[8,7168]{1,0:T(8,128)(2,1)S(1)} collective-permute-done((bf16[8,7168]{1,0:T(8,128)(2,1)S(1)}, bf16[8,7168]{1,0:T(8,128)(2,1)S(1)}, u32[]{:S(2)}, u32[]{:S(2)}) %collective-permute-start.12) | collective-permute-done | bytes 114720 | tf_op jit(solution)/shard_map/ppermute | solution.py:184
  39.9 0.1 add_convert_fusion.2
  40.0 2.2 %collective-permute-start.14 = (bf16[8,7168]{1,0:T(8,128)(2,1)S(1)}, bf16[8,7168]{1,0:T(8,128)(2,1)S(1)}, u32[]{:S(2)}, u32[]{:S(2)}) collective-permute-start(bf16[8,7168]{1,0:T(8,128)(2,1)S(1)} %add_convert_fusion.2), channel_id=1, source_target_pairs={{0,2},{1,3},{2,0},{3,1},{4,6},{5,7},{6,4},{7,5},{8,10},{9,11},{10,... | collective-permute-start | bytes 344072 | tf_op jit(solution)/shard_map/ppermute | solution.py:178
  42.2 1.1 %collective-permute-done.15 = bf16[8,7168]{1,0:T(8,128)(2,1)S(1)} collective-permute-done((bf16[8,7168]{1,0:T(8,128)(2,1)S(1)}, bf16[8,7168]{1,0:T(8,128)(2,1)S(1)}, u32[]{:S(2)}, u32[]{:S(2)}) %collective-permute-start.15) | collective-permute-done | bytes 114720 | tf_op jit(solution)/shard_map/ppermute | solution.py:174
  43.3 0.4 collective-permute-start.16
  43.8 1.5 %collective-permute-start.17 = (bf16[8,7168]{1,0:T(8,128)(2,1)S(1)}, bf16[8,7168]{1,0:T(8,128)(2,1)S(1)}, u32[]{:S(2)}, u32[]{:S(2)}) collective-permute-start(bf16[8,7168]{1,0:T(8,128)(2,1)S(1)} %get-tuple-element.40), channel_id=1, source_target_pairs={{0,8},{4,12},{8,0},{12,4},{1,9},{5,13},{9,1},{13,5},{2,10},{6,14},... | collective-permute-start | bytes 344072 | tf_op jit(solution)/shard_map/ppermute | solution.py:174
  45.3 2.3 %collective-permute-done.14 = bf16[8,7168]{1,0:T(8,128)(2,1)S(1)} collective-permute-done((bf16[8,7168]{1,0:T(8,128)(2,1)S(1)}, bf16[8,7168]{1,0:T(8,128)(2,1)S(1)}, u32[]{:S(2)}, u32[]{:S(2)}) %collective-permute-start.14) | collective-permute-done | bytes 114720 | tf_op jit(solution)/shard_map/ppermute | solution.py:178
  47.6 0.9 %collective-permute-done.16 = bf16[8,7168]{1,0:T(8,128)(2,1)S(1)} collective-permute-done((bf16[8,7168]{1,0:T(8,128)(2,1)S(1)}, bf16[8,7168]{1,0:T(8,128)(2,1)S(1)}, u32[]{:S(2)}, u32[]{:S(2)}) %collective-permute-start.16) | collective-permute-done | bytes 114720 | tf_op jit(solution)/shard_map/ppermute | solution.py:178
  48.5 0.0 collective-permute-done.17
  48.6 0.7 %add_convert_fusion = bf16[8,7168]{1,0:T(8,128)(2,1)} fusion(bf16[8,7168]{1,0:T(8,128)(2,1)S(1)} %collective-permute-done.17, bf16[8,7168]{1,0:T(8,128)(2,1)S(1)} %collective-permute-done.16, bf16[8,7168]{1,0:T(8,128)(2,1)S(1)} %collective-permute-done.14, bf16[8,7168]{1,0:T(8,128)(2,1)S(1)} %get-tuple-element.29), kind=kLoop, calls=%fused_computation | loop fusion | flops 458752 | bytes 573440 | tf_op jit(solution)/shard_map/convert_element_type | solution.py:244
  (2 shorter events, 0.0 us)
Async XLA Ops:
  0.0 22.4 %copy-start = (bf16[2,7168,512]{2,1,0:T(8,128)(2,1)S(1)}, bf16[2,7168,512]{2,1,0:T(8,128)(2,1)}, u32[]{:S(2)}) copy-start(bf16[2,7168,512]{2,1,0:T(8,128)(2,1)} %refs_4_.3) | copy-start | bytes 44040196
  0.0 22.4 %copy-start.1 = (bf16[2,7168,512]{2,1,0:T(8,128)(2,1)S(1)}, bf16[2,7168,512]{2,1,0:T(8,128)(2,1)}, u32[]{:S(2)}) copy-start(bf16[2,7168,512]{2,1,0:T(8,128)(2,1)} %refs_5_.3) | copy-start | bytes 44040196
  1.1 7.5 %collective-permute-start.1 = (bf16[8,7296]{1,0:T(8,128)(2,1)S(1)}, bf16[8,7296]{1,0:T(8,128)(2,1)S(1)}, u32[]{:S(2)}, u32[]{:S(2)}) collective-permute-start(bf16[8,7296]{1,0:T(8,128)(2,1)S(1)} %pack.1.refs_0_), channel_id=1, source_target_pairs={{0,1},{1,0},{2,3},{3,2},{4,5},{5,4},{6,7},{7,6},{8,9},{9,8},{10,11... | collective-permute-start | bytes 350216 | tf_op jit(solution)/shard_map/ppermute | solution.py:178
  4.2 8.1 %collective-permute-start.3 = (bf16[8,7296]{1,0:T(8,128)(2,1)S(1)}, bf16[8,7296]{1,0:T(8,128)(2,1)S(1)}, u32[]{:S(2)}, u32[]{:S(2)}) collective-permute-start(bf16[8,7296]{1,0:T(8,128)(2,1)S(1)} %pack.1.refs_0_), channel_id=1, source_target_pairs={{0,2},{1,3},{2,0},{3,1},{4,6},{5,7},{6,4},{7,5},{8,10},{9,11},{10,... | collective-permute-start | bytes 350216 | tf_op jit(solution)/shard_map/ppermute | solution.py:178
  6.8 5.6 %collective-permute-start = (bf16[8,7296]{1,0:T(8,128)(2,1)S(1)}, bf16[8,7296]{1,0:T(8,128)(2,1)S(1)}, u32[]{:S(2)}, u32[]{:S(2)}) collective-permute-start(bf16[8,7296]{1,0:T(8,128)(2,1)S(1)} %pack.1.refs_0_), channel_id=1, source_target_pairs={{0,8},{4,12},{8,0},{12,4},{1,9},{5,13},{9,1},{13,5},{2,10},{6,14},... | collective-permute-start | bytes 350216 | tf_op jit(solution)/shard_map/ppermute | solution.py:174
  8.6 6.1 %collective-permute-start.2 = (bf16[8,7296]{1,0:T(8,128)(2,1)S(1)}, bf16[8,7296]{1,0:T(8,128)(2,1)S(1)}, u32[]{:S(2)}, u32[]{:S(2)}) collective-permute-start(bf16[8,7296]{1,0:T(8,128)(2,1)S(1)} %collective-permute-done.1.refs_2_), channel_id=1, source_target_pairs={{0,8},{4,12},{8,0},{12,4},{1,9},{5,13},{9,1},{13,5},{2,10},{6,14},... | collective-permute-start | bytes 350216 | tf_op jit(solution)/shard_map/ppermute | solution.py:174
  12.4 6.1 %collective-permute-start.5 = (bf16[8,7296]{1,0:T(8,128)(2,1)S(1)}, bf16[8,7296]{1,0:T(8,128)(2,1)S(1)}, u32[]{:S(2)}, u32[]{:S(2)}) collective-permute-start(bf16[8,7296]{1,0:T(8,128)(2,1)S(1)} %collective-permute-done.3.refs_0_), channel_id=1, source_target_pairs={{0,8},{4,12},{8,0},{12,4},{1,9},{5,13},{9,1},{13,5},{2,10},{6,14},... | collective-permute-start | bytes 350216 | tf_op jit(solution)/shard_map/ppermute | solution.py:174
  13.9 4.8 %collective-permute-start.4 = (bf16[8,7296]{1,0:T(8,128)(2,1)S(1)}, bf16[8,7296]{1,0:T(8,128)(2,1)S(1)}, u32[]{:S(2)}, u32[]{:S(2)}) collective-permute-start(bf16[8,7296]{1,0:T(8,128)(2,1)S(1)} %collective-permute-done.3.refs_0_), channel_id=1, source_target_pairs={{0,1},{1,0},{2,3},{3,2},{4,5},{5,4},{6,7},{7,6},{8,9},{9,8},{10,11... | collective-permute-start | bytes 350216 | tf_op jit(solution)/shard_map/ppermute | solution.py:178
  14.7 5.7 %collective-permute-start.6 = (bf16[8,7296]{1,0:T(8,128)(2,1)S(1)}, bf16[8,7296]{1,0:T(8,128)(2,1)S(1)}, u32[]{:S(2)}, u32[]{:S(2)}) collective-permute-start(bf16[8,7296]{1,0:T(8,128)(2,1)S(1)} %collective-permute-done.3.refs_0_), channel_id=1, source_target_pairs={{0,9},{1,8},{2,11},{3,10},{4,13},{5,12},{6,15},{7,14},{8,1},{9,0},... | collective-permute-start | bytes 350216 | tf_op jit(solution)/shard_map/ppermute | solution.py:184
  16.0 4.6 %collective-permute-start.7 = (bf16[32,7296]{1,0:T(8,128)(2,1)S(1)}, bf16[32,7296]{1,0:T(8,128)(2,1)S(1)}, u32[]{:S(2)}, u32[]{:S(2)}) collective-permute-start(bf16[32,7296]{1,0:T(8,128)(2,1)S(1)} %stack.2.refs_0_), channel_id=1, source_target_pairs={{0,4},{4,0},{8,12},{12,8},{1,5},{5,1},{9,13},{13,9},{2,6},{6,2},{1... | collective-permute-start | bytes 1400840 | tf_op jit(solution)/shard_map/ppermute | solution.py:170
  20.4 6.1 %slice-start = ((s8[14680064]{0:T(1024)(128)(4,1)}), s8[4194304]{0:T(1024)(128)(4,1)S(1)}, s32[]{:S(2)}) async-start(s8[14680064]{0:T(1024)(128)(4,1)} %bitcast.3), calls=%async_computation | async-start | bytes 8388608
  20.5 6.0 %slice-start.1 = ((s8[14680064]{0:T(1024)(128)(4,1)}), s8[4194304]{0:T(1024)(128)(4,1)S(1)}, s32[]{:S(2)}) async-start(s8[14680064]{0:T(1024)(128)(4,1)} %bitcast.3), calls=%async_computation.1 | async-start | bytes 8388608
  20.5 6.0 %slice-start.2 = ((s8[14680064]{0:T(1024)(128)(4,1)}), s8[4194304]{0:T(1024)(128)(4,1)S(1)}, s32[]{:S(2)}) async-start(s8[14680064]{0:T(1024)(128)(4,1)} %bitcast.3), calls=%async_computation.2 | async-start | bytes 8388608
  20.5 6.0 %slice-start.3 = ((s8[14680064]{0:T(1024)(128)(4,1)}), s8[2097152]{0:T(1024)(128)(4,1)S(1)}, s32[]{:S(2)}) async-start(s8[14680064]{0:T(1024)(128)(4,1)} %bitcast.3), calls=%async_computation.3 | async-start | bytes 4194304
  20.5 1.9 %collective-permute-start.8 = (bf16[32,7296]{1,0:T(8,128)(2,1)S(1)}, bf16[32,7296]{1,0:T(8,128)(2,1)S(1)}, u32[]{:S(2)}, u32[]{:S(2)}) collective-permute-start(bf16[32,7296]{1,0:T(8,128)(2,1)S(1)} %stack.3.refs_1_), channel_id=1, source_target_pairs={{0,4},{4,0},{8,12},{12,8},{1,5},{5,1},{9,13},{13,9},{2,6},{6,2},{1... | collective-permute-start | bytes 1400840 | tf_op jit(solution)/shard_map/ppermute | solution.py:170
  28.6 1.9 %collective-permute-start.9 = (bf16[32,7168]{1,0:T(8,128)(2,1)S(1)}, bf16[32,7168]{1,0:T(8,128)(2,1)S(1)}, u32[]{:S(2)}, u32[]{:S(2)}) collective-permute-start(bf16[32,7168]{1,0:T(8,128)(2,1)S(1)} %get-tuple-element.27), channel_id=1, source_target_pairs={{0,4},{4,0},{8,12},{12,8},{1,5},{5,1},{9,13},{13,9},{2,6},{6,2},{1... | collective-permute-start | bytes 1376264 | tf_op jit(solution)/shard_map/ppermute | solution.py:170
  30.5 3.8 %collective-permute-start.10 = (bf16[32,7168]{1,0:T(8,128)(2,1)S(1)}, bf16[32,7168]{1,0:T(8,128)(2,1)S(1)}, u32[]{:S(2)}, u32[]{:S(2)}) collective-permute-start(bf16[32,7168]{1,0:T(8,128)(2,1)S(1)} %get-tuple-element.28), channel_id=1, source_target_pairs={{0,4},{4,0},{8,12},{12,8},{1,5},{5,1},{9,13},{13,9},{2,6},{6,2},{1... | collective-permute-start | bytes 1376264 | tf_op jit(solution)/shard_map/ppermute | solution.py:170
  30.7 5.5 %collective-permute-start.11 = (bf16[8,7168]{1,0:T(8,128)(2,1)S(1)}, bf16[8,7168]{1,0:T(8,128)(2,1)S(1)}, u32[]{:S(2)}, u32[]{:S(2)}) collective-permute-start(bf16[8,7168]{1,0:T(8,128)(2,1)S(1)} %get-tuple-element.32), channel_id=1, source_target_pairs={{0,8},{4,12},{8,0},{12,4},{1,9},{5,13},{9,1},{13,5},{2,10},{6,14},... | collective-permute-start | bytes 344072 | tf_op jit(solution)/shard_map/ppermute | solution.py:174
  32.5 6.0 %collective-permute-start.13 = (bf16[8,7168]{1,0:T(8,128)(2,1)S(1)}, bf16[8,7168]{1,0:T(8,128)(2,1)S(1)}, u32[]{:S(2)}, u32[]{:S(2)}) collective-permute-start(bf16[8,7168]{1,0:T(8,128)(2,1)S(1)} %get-tuple-element.34), channel_id=1, source_target_pairs={{0,1},{1,0},{2,3},{3,2},{4,5},{5,4},{6,7},{7,6},{8,9},{9,8},{10,11... | collective-permute-start | bytes 344072 | tf_op jit(solution)/shard_map/ppermute | solution.py:178
  32.6 7.3 %collective-permute-start.12 = (bf16[8,7168]{1,0:T(8,128)(2,1)S(1)}, bf16[8,7168]{1,0:T(8,128)(2,1)S(1)}, u32[]{:S(2)}, u32[]{:S(2)}) collective-permute-start(bf16[8,7168]{1,0:T(8,128)(2,1)S(1)} %get-tuple-element.33), channel_id=1, source_target_pairs={{0,9},{1,8},{2,11},{3,10},{4,13},{5,12},{6,15},{7,14},{8,1},{9,0},... | collective-permute-start | bytes 344072 | tf_op jit(solution)/shard_map/ppermute | solution.py:184
  38.5 4.8 %collective-permute-start.15 = (bf16[8,7168]{1,0:T(8,128)(2,1)S(1)}, bf16[8,7168]{1,0:T(8,128)(2,1)S(1)}, u32[]{:S(2)}, u32[]{:S(2)}) collective-permute-start(bf16[8,7168]{1,0:T(8,128)(2,1)S(1)} %get-tuple-element.37), channel_id=1, source_target_pairs={{0,8},{4,12},{8,0},{12,4},{1,9},{5,13},{9,1},{13,5},{2,10},{6,14},... | collective-permute-start | bytes 344072 | tf_op jit(solution)/shard_map/ppermute | solution.py:174
  40.0 7.6 %collective-permute-start.14 = (bf16[8,7168]{1,0:T(8,128)(2,1)S(1)}, bf16[8,7168]{1,0:T(8,128)(2,1)S(1)}, u32[]{:S(2)}, u32[]{:S(2)}) collective-permute-start(bf16[8,7168]{1,0:T(8,128)(2,1)S(1)} %add_convert_fusion.2), channel_id=1, source_target_pairs={{0,2},{1,3},{2,0},{3,1},{4,6},{5,7},{6,4},{7,5},{8,10},{9,11},{10,... | collective-permute-start | bytes 344072 | tf_op jit(solution)/shard_map/ppermute | solution.py:178
  43.3 5.2 %collective-permute-start.16 = (bf16[8,7168]{1,0:T(8,128)(2,1)S(1)}, bf16[8,7168]{1,0:T(8,128)(2,1)S(1)}, u32[]{:S(2)}, u32[]{:S(2)}) collective-permute-start(bf16[8,7168]{1,0:T(8,128)(2,1)S(1)} %add_convert_fusion.1), channel_id=1, source_target_pairs={{0,1},{1,0},{2,3},{3,2},{4,5},{5,4},{6,7},{7,6},{8,9},{9,8},{10,11... | collective-permute-start | bytes 344072 | tf_op jit(solution)/shard_map/ppermute | solution.py:178
  43.8 4.8 %collective-permute-start.17 = (bf16[8,7168]{1,0:T(8,128)(2,1)S(1)}, bf16[8,7168]{1,0:T(8,128)(2,1)S(1)}, u32[]{:S(2)}, u32[]{:S(2)}) collective-permute-start(bf16[8,7168]{1,0:T(8,128)(2,1)S(1)} %get-tuple-element.40), channel_id=1, source_target_pairs={{0,8},{4,12},{8,0},{12,4},{1,9},{5,13},{9,1},{13,5},{2,10},{6,14},... | collective-permute-start | bytes 344072 | tf_op jit(solution)/shard_map/ppermute | solution.py:174

commit v22 on v19

--- a/solution.py
+++ b/solution.py
@@ -231,7 +231,7 @@
     third = to_place(third, 1)
     own, far_own, first, far_first, second = sums(early, other_early, EARLY)
     second = total(second, far_second, far_third, third).astype(jnp.bfloat16)
-    first = total(first, to_chip(after(far_first, third))).astype(jnp.bfloat16)
+    first = total(first, to_chip(after(far_first, far_second, third))).astype(jnp.bfloat16)
     first, far_own = lax.optimization_barrier((first, far_own))
     second_here, first_here, far_own = to_place(second, 2), to_place(first, 1), to_chip(far_own)
     return total(own, second_here, first_here, far_own).astype(jnp.bfloat16)

time: 50.1 us -> 49.2 us (0.982)
  starting transfers between devices: 23.2 us -> 21.1 us
  waiting for transfers between devices: 18.2 us -> 19.5 us
    ppermute x6, waiting for transfers between devices: 2.54 us -> 5.4 us  [to_chip(): return lax.ppermute(value, 'node', [(i, i ^ 2) for i in range(2 * CHIPS)])]
    ppermute x6, starting transfers between devices: 11.3 us -> 9.28 us  [to_place(): return lax.ppermute(value, 'local', [(i, i ^ bits) for i in range(PLACES)])]
    ppermute x6, waiting for transfers between devices: 9.21 us -> 7.95 us  [to_place(): return lax.ppermute(value, 'local', [(i, i ^ bits) for i in range(PLACES)])]
  transfers between devices with their start and end apart: 18 -> 18, of which waited for: 12 -> 14; matrix products, arithmetic and copies ran while one was open for 0% -> 0% of each run, Pallas kernels for 1% -> 1%
where the time goes in v22:
time: 49.2 us; the launch traced here: 49.1 us
  starting transfers between devices  21.1 us (43%)
  waiting for transfers between devices  19.5 us (40%)
  Pallas kernels  7.58 us (15%)
  other arithmetic  0.8 us (2%)
    ppermute x6, starting transfers between devices, to_place(): return lax.ppermute(value, 'local', [(i, i ^ bits) for i in range(PLACES)])  9.28 us
    ppermute x6, starting transfers between devices, to_chip(): return lax.ppermute(value, 'node', [(i, i ^ 2) for i in range(2 * CHIPS)])  8.42 us
    ppermute x6, waiting for transfers between devices, to_place(): return lax.ppermute(value, 'local', [(i, i ^ bits) for i in range(PLACES)])  7.95 us
    ppermute x6, waiting for transfers between devices, to_chip(): return lax.ppermute(value, 'node', [(i, i ^ 2) for i in range(2 * CHIPS)])  5.4 us
    pallas_call x1, Pallas kernels, hidden_units(): pl.pallas_call(functools.partial(hidden_kernel, experts), out_shape=jax.S...  4.05 us
    ppermute x4, waiting for transfers between devices, to_core(): return lax.ppermute(value, 'node', [(i, i ^ 1) for i in range(2 * CHIPS)])  3.34 us
    ppermute x2, starting transfers between devices, to_both(): return lax.ppermute(value, ('node', 'local'), perm)  2.89 us
    ppermute x2, waiting for transfers between devices, to_both(): return lax.ppermute(value, ('node', 'local'), perm)  2.77 us
  transfers between devices with their start and end apart: 18, of which 14 were waited for; matrix products, arithmetic and copies ran while one was open for 0% of the time, Pallas kernels for 1%

profile of v22, /device:TPU:0, one launch (start us, length us, event | category | flops | bytes accessed | tf_op | source)
XLA Modules:
  0.0 49.1 jit_solution(8474709602177852680)
XLA Ops:
  0.0 0.0 copy-start
  0.0 0.0 copy-start.1
  0.0 1.1 %pack.1.refs_0_ = bf16[8,7296]{1,0:T(8,128)(2,1)S(1)} custom-call(bf16[8,7168]{1,0:T(8,128)(2,1)} %refs_0_.1, s32[4,8]{1,0:T(4,128)} %bitcast.6, f32[4,8]{1,0:T(4,128)} %bitcast.7, s32[8]{0:T(128)} %refs_3_.1, bf16[2,7168,512]{2,1,0:T(8,128)(2,1)} %refs_4_.3, bf16[2,7168,512]{2,1,0:T(8,128)(2,1)} %refs_5_.3, bf16[2,512,7168]{2,1,0:T(8,128)(2,1)} %refs_6_.1), custom_call_target="tpu_custom_call" | custom-call | tf_op jit(solution)/shard_map/pack/pallas_call | solution.py:50
  1.1 3.1 %collective-permute-start.1 = (bf16[8,7296]{1,0:T(8,128)(2,1)S(1)}, bf16[8,7296]{1,0:T(8,128)(2,1)S(1)}, u32[]{:S(2)}, u32[]{:S(2)}) collective-permute-start(bf16[8,7296]{1,0:T(8,128)(2,1)S(1)} %pack.1.refs_0_), channel_id=1, source_target_pairs={{0,1},{1,0},{2,3},{3,2},{4,5},{5,4},{6,7},{7,6},{8,9},{9,8},{10,11... | collective-permute-start | bytes 350216 | tf_op jit(solution)/shard_map/ppermute | solution.py:177
  4.2 2.6 %collective-permute-start.3 = (bf16[8,7296]{1,0:T(8,128)(2,1)S(1)}, bf16[8,7296]{1,0:T(8,128)(2,1)S(1)}, u32[]{:S(2)}, u32[]{:S(2)}) collective-permute-start(bf16[8,7296]{1,0:T(8,128)(2,1)S(1)} %pack.1.refs_0_), channel_id=1, source_target_pairs={{0,2},{1,3},{2,0},{3,1},{4,6},{5,7},{6,4},{7,5},{8,10},{9,11},{10,... | collective-permute-start | bytes 350216 | tf_op jit(solution)/shard_map/ppermute | solution.py:177
  6.8 1.5 %collective-permute-start = (bf16[8,7296]{1,0:T(8,128)(2,1)S(1)}, bf16[8,7296]{1,0:T(8,128)(2,1)S(1)}, u32[]{:S(2)}, u32[]{:S(2)}) collective-permute-start(bf16[8,7296]{1,0:T(8,128)(2,1)S(1)} %pack.1.refs_0_), channel_id=1, source_target_pairs={{0,8},{4,12},{8,0},{12,4},{1,9},{5,13},{9,1},{13,5},{2,10},{6,14},... | collective-permute-start | bytes 350216 | tf_op jit(solution)/shard_map/ppermute | solution.py:173
  8.3 0.3 collective-permute-done.1.refs_2_
  8.6 1.8 %collective-permute-start.2 = (bf16[8,7296]{1,0:T(8,128)(2,1)S(1)}, bf16[8,7296]{1,0:T(8,128)(2,1)S(1)}, u32[]{:S(2)}, u32[]{:S(2)}) collective-permute-start(bf16[8,7296]{1,0:T(8,128)(2,1)S(1)} %collective-permute-done.1.refs_2_), channel_id=1, source_target_pairs={{0,8},{4,12},{8,0},{12,4},{1,9},{5,13},{9,1},{13,5},{2,10},{6,14},... | collective-permute-start | bytes 350216 | tf_op jit(solution)/shard_map/ppermute | solution.py:173
  10.4 1.9 %collective-permute-done.3.refs_0_ = bf16[8,7296]{1,0:T(8,128)(2,1)S(1)} collective-permute-done((bf16[8,7296]{1,0:T(8,128)(2,1)S(1)}, bf16[8,7296]{1,0:T(8,128)(2,1)S(1)}, u32[]{:S(2)}, u32[]{:S(2)}) %collective-permute-start.3) | collective-permute-done | bytes 116768 | tf_op jit(solution)/shard_map/ppermute | solution.py:177
  12.3 0.1 collective-permute-done.refs_1_
  12.4 1.5 %collective-permute-start.5 = (bf16[8,7296]{1,0:T(8,128)(2,1)S(1)}, bf16[8,7296]{1,0:T(8,128)(2,1)S(1)}, u32[]{:S(2)}, u32[]{:S(2)}) collective-permute-start(bf16[8,7296]{1,0:T(8,128)(2,1)S(1)} %collective-permute-done.3.refs_0_), channel_id=1, source_target_pairs={{0,8},{4,12},{8,0},{12,4},{1,9},{5,13},{9,1},{13,5},{2,10},{6,14},... | collective-permute-start | bytes 350216 | tf_op jit(solution)/shard_map/ppermute | solution.py:173
  13.9 0.8 %collective-permute-start.4 = (bf16[8,7296]{1,0:T(8,128)(2,1)S(1)}, bf16[8,7296]{1,0:T(8,128)(2,1)S(1)}, u32[]{:S(2)}, u32[]{:S(2)}) collective-permute-start(bf16[8,7296]{1,0:T(8,128)(2,1)S(1)} %collective-permute-done.3.refs_0_), channel_id=1, source_target_pairs={{0,1},{1,0},{2,3},{3,2},{4,5},{5,4},{6,7},{7,6},{8,9},{9,8},{10,11... | collective-permute-start | bytes 350216 | tf_op jit(solution)/shard_map/ppermute | solution.py:177
  14.7 0.0 collective-permute-done.2.refs_3_
  14.7 1.2 %collective-permute-start.6 = (bf16[8,7296]{1,0:T(8,128)(2,1)S(1)}, bf16[8,7296]{1,0:T(8,128)(2,1)S(1)}, u32[]{:S(2)}, u32[]{:S(2)}) collective-permute-start(bf16[8,7296]{1,0:T(8,128)(2,1)S(1)} %collective-permute-done.3.refs_0_), channel_id=1, source_target_pairs={{0,9},{1,8},{2,11},{3,10},{4,13},{5,12},{6,15},{7,14},{8,1},{9,0},... | collective-permute-start | bytes 350216 | tf_op jit(solution)/shard_map/ppermute | solution.py:183
  15.9 0.1 stack.2.refs_0_
  16.0 0.1 collective-permute-start.7
  16.1 2.4 %collective-permute-done.5.refs_2_ = bf16[8,7296]{1,0:T(8,128)(2,1)S(1)} collective-permute-done((bf16[8,7296]{1,0:T(8,128)(2,1)S(1)}, bf16[8,7296]{1,0:T(8,128)(2,1)S(1)}, u32[]{:S(2)}, u32[]{:S(2)}) %collective-permute-start.5) | collective-permute-done | bytes 116768 | tf_op jit(solution)/shard_map/ppermute | solution.py:173
  18.5 0.2 collective-permute-done.4.refs_1_
  18.7 1.7 %collective-permute-done.6.refs_3_ = bf16[8,7296]{1,0:T(8,128)(2,1)S(1)} collective-permute-done((bf16[8,7296]{1,0:T(8,128)(2,1)S(1)}, bf16[8,7296]{1,0:T(8,128)(2,1)S(1)}, u32[]{:S(2)}, u32[]{:S(2)}) %collective-permute-start.6) | collective-permute-done | bytes 116768 | tf_op jit(solution)/shard_map/ppermute | solution.py:183
  20.4 0.0 slice-start
  20.4 0.1 stack.3.refs_1_
  20.5 0.0 slice-start.1
  20.5 0.0 slice-start.2
  20.5 0.0 slice-start.3
  20.5 0.1 collective-permute-start.8
  20.6 0.0 collective-permute-done.7.refs_2_
  20.6 1.8 %collective-permute-done.8.refs_3_ = bf16[32,7296]{1,0:T(8,128)(2,1)S(1)} collective-permute-done((bf16[32,7296]{1,0:T(8,128)(2,1)S(1)}, bf16[32,7296]{1,0:T(8,128)(2,1)S(1)}, u32[]{:S(2)}, u32[]{:S(2)}) %collective-permute-start.8) | collective-permute-done | bytes 466976 | tf_op jit(solution)/shard_map/ppermute | solution.py:169
  22.4 0.0 copy-done
  22.4 0.0 copy-done.1
  22.4 4.1 %hidden.1.hidden_ref = bf16[128,1024]{1,0:T(8,128)(2,1)S(1)} custom-call(bf16[32,7296]{1,0:T(8,128)(2,1)S(1)} %stack.2.refs_0_, bf16[32,7296]{1,0:T(8,128)(2,1)S(1)} %stack.3.refs_1_, bf16[32,7296]{1,0:T(8,128)(2,1)S(1)} %collective-permute-done.7.refs_2_, bf16[32,7296]{1,0:T(8,128)(2,1)S(1)} %collective-permute-done.8.refs_3_, ...), custom_call_target="tpu_custom_call" | custom-call | flops 3758096384 | bytes 29360128 | tf_op jit(solution)/shard_map/hidden/pallas_call | solution.py:113
  26.5 0.0 slice-done
  26.5 0.0 slice-done.1
  26.5 0.0 slice-done.2
  26.5 0.0 slice-done.3
  26.5 2.1 %down.1 = (bf16[40,7168]{1,0:T(8,128)(2,1)S(1)}, bf16[24,7168]{1,0:T(8,128)(2,1)S(1)}, bf16[40,7168]{1,0:T(8,128)(2,1)S(1)}, bf16[24,7168]{1,0:T(8,128)(2,1)S(1)}) custom-call(bf16[128,1024]{1,0:T(8,128)(2,1)S(1)} %hidden.1.hidden_ref, bf16[1024,7168]{1,0:T(8,128)(2,1)S(1)} %bitcast.5), custom_call_target="tpu_custom_call" | custom-call | flops 1879048192 | bytes 14680064 | tf_op jit(solution)/shard_map/down/pallas_call | solution.py:149
  28.6 0.2 collective-permute-start.9
  28.8 1.5 %collective-permute-done.9.other_ref = bf16[24,7168]{1,0:T(8,128)(2,1)S(1)} collective-permute-done((bf16[24,7168]{1,0:T(8,128)(2,1)S(1)}, bf16[24,7168]{1,0:T(8,128)(2,1)S(1)}, u32[]{:S(2)}, u32[]{:S(2)}) %collective-permute-start.9) | collective-permute-done | bytes 344096 | tf_op jit(solution)/shard_map/ppermute | solution.py:169
  30.3 0.1 collective-permute-start.10
  30.5 0.1 sums.3
  30.5 1.8 %collective-permute-start.11 = (bf16[8,7168]{1,0:T(8,128)(2,1)S(1)}, bf16[8,7168]{1,0:T(8,128)(2,1)S(1)}, u32[]{:S(2)}, u32[]{:S(2)}) collective-permute-start(bf16[8,7168]{1,0:T(8,128)(2,1)S(1)} %get-tuple-element.32), channel_id=1, source_target_pairs={{0,8},{4,12},{8,0},{12,4},{1,9},{5,13},{9,1},{13,5},{2,10},{6,14},... | collective-permute-start | bytes 344072 | tf_op jit(solution)/shard_map/ppermute | solution.py:173
  32.3 0.1 collective-permute-start.13
  32.4 1.7 %collective-permute-start.12 = (bf16[8,7168]{1,0:T(8,128)(2,1)S(1)}, bf16[8,7168]{1,0:T(8,128)(2,1)S(1)}, u32[]{:S(2)}, u32[]{:S(2)}) collective-permute-start(bf16[8,7168]{1,0:T(8,128)(2,1)S(1)} %get-tuple-element.33), channel_id=1, source_target_pairs={{0,9},{1,8},{2,11},{3,10},{4,13},{5,12},{6,15},{7,14},{8,1},{9,0},... | collective-permute-start | bytes 344072 | tf_op jit(solution)/shard_map/ppermute | solution.py:183
  34.1 0.0 collective-permute-done.10.other_ref
  34.1 0.1 sums.2
  34.2 1.8 %collective-permute-done.11 = bf16[8,7168]{1,0:T(8,128)(2,1)S(1)} collective-permute-done((bf16[8,7168]{1,0:T(8,128)(2,1)S(1)}, bf16[8,7168]{1,0:T(8,128)(2,1)S(1)}, u32[]{:S(2)}, u32[]{:S(2)}) %collective-permute-start.11) | collective-permute-done | bytes 114720 | tf_op jit(solution)/shard_map/ppermute | solution.py:173
  36.0 2.3 %collective-permute-done.13 = bf16[8,7168]{1,0:T(8,128)(2,1)S(1)} collective-permute-done((bf16[8,7168]{1,0:T(8,128)(2,1)S(1)}, bf16[8,7168]{1,0:T(8,128)(2,1)S(1)}, u32[]{:S(2)}, u32[]{:S(2)}) %collective-permute-start.13) | collective-permute-done | bytes 114720 | tf_op jit(solution)/shard_map/ppermute | solution.py:177
  38.3 0.3 collective-permute-start.15
  38.6 1.1 %collective-permute-done.12 = bf16[8,7168]{1,0:T(8,128)(2,1)S(1)} collective-permute-done((bf16[8,7168]{1,0:T(8,128)(2,1)S(1)}, bf16[8,7168]{1,0:T(8,128)(2,1)S(1)}, u32[]{:S(2)}, u32[]{:S(2)}) %collective-permute-start.12) | collective-permute-done | bytes 114720 | tf_op jit(solution)/shard_map/ppermute | solution.py:183
  39.7 0.1 add_convert_fusion.2
  39.8 2.2 %collective-permute-start.14 = (bf16[8,7168]{1,0:T(8,128)(2,1)S(1)}, bf16[8,7168]{1,0:T(8,128)(2,1)S(1)}, u32[]{:S(2)}, u32[]{:S(2)}) collective-permute-start(bf16[8,7168]{1,0:T(8,128)(2,1)S(1)} %add_convert_fusion.2), channel_id=1, source_target_pairs={{0,2},{1,3},{2,0},{3,1},{4,6},{5,7},{6,4},{7,5},{8,10},{9,11},{10,... | collective-permute-start | bytes 344072 | tf_op jit(solution)/shard_map/ppermute | solution.py:177
  42.0 1.1 %collective-permute-done.15 = bf16[8,7168]{1,0:T(8,128)(2,1)S(1)} collective-permute-done((bf16[8,7168]{1,0:T(8,128)(2,1)S(1)}, bf16[8,7168]{1,0:T(8,128)(2,1)S(1)}, u32[]{:S(2)}, u32[]{:S(2)}) %collective-permute-start.15) | collective-permute-done | bytes 114720 | tf_op jit(solution)/shard_map/ppermute | solution.py:173
  43.1 0.4 collective-permute-start.16
  43.6 1.5 %collective-permute-start.17 = (bf16[8,7168]{1,0:T(8,128)(2,1)S(1)}, bf16[8,7168]{1,0:T(8,128)(2,1)S(1)}, u32[]{:S(2)}, u32[]{:S(2)}) collective-permute-start(bf16[8,7168]{1,0:T(8,128)(2,1)S(1)} %get-tuple-element.40), channel_id=1, source_target_pairs={{0,8},{4,12},{8,0},{12,4},{1,9},{5,13},{9,1},{13,5},{2,10},{6,14},... | collective-permute-start | bytes 344072 | tf_op jit(solution)/shard_map/ppermute | solution.py:173
  45.1 2.3 %collective-permute-done.14 = bf16[8,7168]{1,0:T(8,128)(2,1)S(1)} collective-permute-done((bf16[8,7168]{1,0:T(8,128)(2,1)S(1)}, bf16[8,7168]{1,0:T(8,128)(2,1)S(1)}, u32[]{:S(2)}, u32[]{:S(2)}) %collective-permute-start.14) | collective-permute-done | bytes 114720 | tf_op jit(solution)/shard_map/ppermute | solution.py:177
  47.4 0.9 %collective-permute-done.16 = bf16[8,7168]{1,0:T(8,128)(2,1)S(1)} collective-permute-done((bf16[8,7168]{1,0:T(8,128)(2,1)S(1)}, bf16[8,7168]{1,0:T(8,128)(2,1)S(1)}, u32[]{:S(2)}, u32[]{:S(2)}) %collective-permute-start.16) | collective-permute-done | bytes 114720 | tf_op jit(solution)/shard_map/ppermute | solution.py:177
  48.3 0.0 collective-permute-done.17
  48.4 0.7 %add_convert_fusion = bf16[8,7168]{1,0:T(8,128)(2,1)} fusion(bf16[8,7168]{1,0:T(8,128)(2,1)S(1)} %collective-permute-done.17, bf16[8,7168]{1,0:T(8,128)(2,1)S(1)} %collective-permute-done.16, bf16[8,7168]{1,0:T(8,128)(2,1)S(1)} %collective-permute-done.14, bf16[8,7168]{1,0:T(8,128)(2,1)S(1)} %get-tuple-element.29), kind=kLoop, calls=%fused_computation | loop fusion | flops 458752 | bytes 573440 | tf_op jit(solution)/shard_map/convert_element_type | solution.py:237
  (2 shorter events, 0.0 us)
Async XLA Ops:
  0.0 22.4 %copy-start = (bf16[2,7168,512]{2,1,0:T(8,128)(2,1)S(1)}, bf16[2,7168,512]{2,1,0:T(8,128)(2,1)}, u32[]{:S(2)}) copy-start(bf16[2,7168,512]{2,1,0:T(8,128)(2,1)} %refs_4_.3) | copy-start | bytes 44040196
  0.0 22.4 %copy-start.1 = (bf16[2,7168,512]{2,1,0:T(8,128)(2,1)S(1)}, bf16[2,7168,512]{2,1,0:T(8,128)(2,1)}, u32[]{:S(2)}) copy-start(bf16[2,7168,512]{2,1,0:T(8,128)(2,1)} %refs_5_.3) | copy-start | bytes 44040196
  1.1 7.5 %collective-permute-start.1 = (bf16[8,7296]{1,0:T(8,128)(2,1)S(1)}, bf16[8,7296]{1,0:T(8,128)(2,1)S(1)}, u32[]{:S(2)}, u32[]{:S(2)}) collective-permute-start(bf16[8,7296]{1,0:T(8,128)(2,1)S(1)} %pack.1.refs_0_), channel_id=1, source_target_pairs={{0,1},{1,0},{2,3},{3,2},{4,5},{5,4},{6,7},{7,6},{8,9},{9,8},{10,11... | collective-permute-start | bytes 350216 | tf_op jit(solution)/shard_map/ppermute | solution.py:177
  4.2 8.1 %collective-permute-start.3 = (bf16[8,7296]{1,0:T(8,128)(2,1)S(1)}, bf16[8,7296]{1,0:T(8,128)(2,1)S(1)}, u32[]{:S(2)}, u32[]{:S(2)}) collective-permute-start(bf16[8,7296]{1,0:T(8,128)(2,1)S(1)} %pack.1.refs_0_), channel_id=1, source_target_pairs={{0,2},{1,3},{2,0},{3,1},{4,6},{5,7},{6,4},{7,5},{8,10},{9,11},{10,... | collective-permute-start | bytes 350216 | tf_op jit(solution)/shard_map/ppermute | solution.py:177
  6.8 5.6 %collective-permute-start = (bf16[8,7296]{1,0:T(8,128)(2,1)S(1)}, bf16[8,7296]{1,0:T(8,128)(2,1)S(1)}, u32[]{:S(2)}, u32[]{:S(2)}) collective-permute-start(bf16[8,7296]{1,0:T(8,128)(2,1)S(1)} %pack.1.refs_0_), channel_id=1, source_target_pairs={{0,8},{4,12},{8,0},{12,4},{1,9},{5,13},{9,1},{13,5},{2,10},{6,14},... | collective-permute-start | bytes 350216 | tf_op jit(solution)/shard_map/ppermute | solution.py:173
  8.6 6.1 %collective-permute-start.2 = (bf16[8,7296]{1,0:T(8,128)(2,1)S(1)}, bf16[8,7296]{1,0:T(8,128)(2,1)S(1)}, u32[]{:S(2)}, u32[]{:S(2)}) collective-permute-start(bf16[8,7296]{1,0:T(8,128)(2,1)S(1)} %collective-permute-done.1.refs_2_), channel_id=1, source_target_pairs={{0,8},{4,12},{8,0},{12,4},{1,9},{5,13},{9,1},{13,5},{2,10},{6,14},... | collective-permute-start | bytes 350216 | tf_op jit(solution)/shard_map/ppermute | solution.py:173
  12.4 6.1 %collective-permute-start.5 = (bf16[8,7296]{1,0:T(8,128)(2,1)S(1)}, bf16[8,7296]{1,0:T(8,128)(2,1)S(1)}, u32[]{:S(2)}, u32[]{:S(2)}) collective-permute-start(bf16[8,7296]{1,0:T(8,128)(2,1)S(1)} %collective-permute-done.3.refs_0_), channel_id=1, source_target_pairs={{0,8},{4,12},{8,0},{12,4},{1,9},{5,13},{9,1},{13,5},{2,10},{6,14},... | collective-permute-start | bytes 350216 | tf_op jit(solution)/shard_map/ppermute | solution.py:173
  13.9 4.8 %collective-permute-start.4 = (bf16[8,7296]{1,0:T(8,128)(2,1)S(1)}, bf16[8,7296]{1,0:T(8,128)(2,1)S(1)}, u32[]{:S(2)}, u32[]{:S(2)}) collective-permute-start(bf16[8,7296]{1,0:T(8,128)(2,1)S(1)} %collective-permute-done.3.refs_0_), channel_id=1, source_target_pairs={{0,1},{1,0},{2,3},{3,2},{4,5},{5,4},{6,7},{7,6},{8,9},{9,8},{10,11... | collective-permute-start | bytes 350216 | tf_op jit(solution)/shard_map/ppermute | solution.py:177
  14.7 5.7 %collective-permute-start.6 = (bf16[8,7296]{1,0:T(8,128)(2,1)S(1)}, bf16[8,7296]{1,0:T(8,128)(2,1)S(1)}, u32[]{:S(2)}, u32[]{:S(2)}) collective-permute-start(bf16[8,7296]{1,0:T(8,128)(2,1)S(1)} %collective-permute-done.3.refs_0_), channel_id=1, source_target_pairs={{0,9},{1,8},{2,11},{3,10},{4,13},{5,12},{6,15},{7,14},{8,1},{9,0},... | collective-permute-start | bytes 350216 | tf_op jit(solution)/shard_map/ppermute | solution.py:183
  16.0 4.6 %collective-permute-start.7 = (bf16[32,7296]{1,0:T(8,128)(2,1)S(1)}, bf16[32,7296]{1,0:T(8,128)(2,1)S(1)}, u32[]{:S(2)}, u32[]{:S(2)}) collective-permute-start(bf16[32,7296]{1,0:T(8,128)(2,1)S(1)} %stack.2.refs_0_), channel_id=1, source_target_pairs={{0,4},{4,0},{8,12},{12,8},{1,5},{5,1},{9,13},{13,9},{2,6},{6,2},{1... | collective-permute-start | bytes 1400840 | tf_op jit(solution)/shard_map/ppermute | solution.py:169
  20.4 6.1 %slice-start = ((s8[14680064]{0:T(1024)(128)(4,1)}), s8[4194304]{0:T(1024)(128)(4,1)S(1)}, s32[]{:S(2)}) async-start(s8[14680064]{0:T(1024)(128)(4,1)} %bitcast.3), calls=%async_computation | async-start | bytes 8388608
  20.5 6.0 %slice-start.1 = ((s8[14680064]{0:T(1024)(128)(4,1)}), s8[4194304]{0:T(1024)(128)(4,1)S(1)}, s32[]{:S(2)}) async-start(s8[14680064]{0:T(1024)(128)(4,1)} %bitcast.3), calls=%async_computation.1 | async-start | bytes 8388608
  20.5 6.0 %slice-start.2 = ((s8[14680064]{0:T(1024)(128)(4,1)}), s8[4194304]{0:T(1024)(128)(4,1)S(1)}, s32[]{:S(2)}) async-start(s8[14680064]{0:T(1024)(128)(4,1)} %bitcast.3), calls=%async_computation.2 | async-start | bytes 8388608
  20.5 6.0 %slice-start.3 = ((s8[14680064]{0:T(1024)(128)(4,1)}), s8[2097152]{0:T(1024)(128)(4,1)S(1)}, s32[]{:S(2)}) async-start(s8[14680064]{0:T(1024)(128)(4,1)} %bitcast.3), calls=%async_computation.3 | async-start | bytes 4194304
  20.5 1.9 %collective-permute-start.8 = (bf16[32,7296]{1,0:T(8,128)(2,1)S(1)}, bf16[32,7296]{1,0:T(8,128)(2,1)S(1)}, u32[]{:S(2)}, u32[]{:S(2)}) collective-permute-start(bf16[32,7296]{1,0:T(8,128)(2,1)S(1)} %stack.3.refs_1_), channel_id=1, source_target_pairs={{0,4},{4,0},{8,12},{12,8},{1,5},{5,1},{9,13},{13,9},{2,6},{6,2},{1... | collective-permute-start | bytes 1400840 | tf_op jit(solution)/shard_map/ppermute | solution.py:169
  28.6 1.7 %collective-permute-start.9 = (bf16[24,7168]{1,0:T(8,128)(2,1)S(1)}, bf16[24,7168]{1,0:T(8,128)(2,1)S(1)}, u32[]{:S(2)}, u32[]{:S(2)}) collective-permute-start(bf16[24,7168]{1,0:T(8,128)(2,1)S(1)} %get-tuple-element.27), channel_id=1, source_target_pairs={{0,4},{4,0},{8,12},{12,8},{1,5},{5,1},{9,13},{13,9},{2,6},{6,2},{1... | collective-permute-start | bytes 1032200 | tf_op jit(solution)/shard_map/ppermute | solution.py:169
  30.3 3.8 %collective-permute-start.10 = (bf16[40,7168]{1,0:T(8,128)(2,1)S(1)}, bf16[40,7168]{1,0:T(8,128)(2,1)S(1)}, u32[]{:S(2)}, u32[]{:S(2)}) collective-permute-start(bf16[40,7168]{1,0:T(8,128)(2,1)S(1)} %get-tuple-element.28), channel_id=1, source_target_pairs={{0,4},{4,0},{8,12},{12,8},{1,5},{5,1},{9,13},{13,9},{2,6},{6,2},{1... | collective-permute-start | bytes 1720328 | tf_op jit(solution)/shard_map/ppermute | solution.py:169
  30.5 5.5 %collective-permute-start.11 = (bf16[8,7168]{1,0:T(8,128)(2,1)S(1)}, bf16[8,7168]{1,0:T(8,128)(2,1)S(1)}, u32[]{:S(2)}, u32[]{:S(2)}) collective-permute-start(bf16[8,7168]{1,0:T(8,128)(2,1)S(1)} %get-tuple-element.32), channel_id=1, source_target_pairs={{0,8},{4,12},{8,0},{12,4},{1,9},{5,13},{9,1},{13,5},{2,10},{6,14},... | collective-permute-start | bytes 344072 | tf_op jit(solution)/shard_map/ppermute | solution.py:173
  32.3 6.0 %collective-permute-start.13 = (bf16[8,7168]{1,0:T(8,128)(2,1)S(1)}, bf16[8,7168]{1,0:T(8,128)(2,1)S(1)}, u32[]{:S(2)}, u32[]{:S(2)}) collective-permute-start(bf16[8,7168]{1,0:T(8,128)(2,1)S(1)} %get-tuple-element.34), channel_id=1, source_target_pairs={{0,1},{1,0},{2,3},{3,2},{4,5},{5,4},{6,7},{7,6},{8,9},{9,8},{10,11... | collective-permute-start | bytes 344072 | tf_op jit(solution)/shard_map/ppermute | solution.py:177
  32.4 7.3 %collective-permute-start.12 = (bf16[8,7168]{1,0:T(8,128)(2,1)S(1)}, bf16[8,7168]{1,0:T(8,128)(2,1)S(1)}, u32[]{:S(2)}, u32[]{:S(2)}) collective-permute-start(bf16[8,7168]{1,0:T(8,128)(2,1)S(1)} %get-tuple-element.33), channel_id=1, source_target_pairs={{0,9},{1,8},{2,11},{3,10},{4,13},{5,12},{6,15},{7,14},{8,1},{9,0},... | collective-permute-start | bytes 344072 | tf_op jit(solution)/shard_map/ppermute | solution.py:183
  38.3 4.8 %collective-permute-start.15 = (bf16[8,7168]{1,0:T(8,128)(2,1)S(1)}, bf16[8,7168]{1,0:T(8,128)(2,1)S(1)}, u32[]{:S(2)}, u32[]{:S(2)}) collective-permute-start(bf16[8,7168]{1,0:T(8,128)(2,1)S(1)} %get-tuple-element.37), channel_id=1, source_target_pairs={{0,8},{4,12},{8,0},{12,4},{1,9},{5,13},{9,1},{13,5},{2,10},{6,14},... | collective-permute-start | bytes 344072 | tf_op jit(solution)/shard_map/ppermute | solution.py:173
  39.8 7.6 %collective-permute-start.14 = (bf16[8,7168]{1,0:T(8,128)(2,1)S(1)}, bf16[8,7168]{1,0:T(8,128)(2,1)S(1)}, u32[]{:S(2)}, u32[]{:S(2)}) collective-permute-start(bf16[8,7168]{1,0:T(8,128)(2,1)S(1)} %add_convert_fusion.2), channel_id=1, source_target_pairs={{0,2},{1,3},{2,0},{3,1},{4,6},{5,7},{6,4},{7,5},{8,10},{9,11},{10,... | collective-permute-start | bytes 344072 | tf_op jit(solution)/shard_map/ppermute | solution.py:177
  43.1 5.2 %collective-permute-start.16 = (bf16[8,7168]{1,0:T(8,128)(2,1)S(1)}, bf16[8,7168]{1,0:T(8,128)(2,1)S(1)}, u32[]{:S(2)}, u32[]{:S(2)}) collective-permute-start(bf16[8,7168]{1,0:T(8,128)(2,1)S(1)} %add_convert_fusion.1), channel_id=1, source_target_pairs={{0,1},{1,0},{2,3},{3,2},{4,5},{5,4},{6,7},{7,6},{8,9},{9,8},{10,11... | collective-permute-start | bytes 344072 | tf_op jit(solution)/shard_map/ppermute | solution.py:177
  43.6 4.8 %collective-permute-start.17 = (bf16[8,7168]{1,0:T(8,128)(2,1)S(1)}, bf16[8,7168]{1,0:T(8,128)(2,1)S(1)}, u32[]{:S(2)}, u32[]{:S(2)}) collective-permute-start(bf16[8,7168]{1,0:T(8,128)(2,1)S(1)} %get-tuple-element.40), channel_id=1, source_target_pairs={{0,8},{4,12},{8,0},{12,4},{1,9},{5,13},{9,1},{13,5},{2,10},{6,14},... | collective-permute-start | bytes 344072 | tf_op jit(solution)/shard_map/ppermute | solution.py:173

commit v23 on v22

--- a/solution.py
+++ b/solution.py
@@ -8,7 +8,7 @@
 from jax.sharding import PartitionSpec as P
 
 LANES = 128
-N_TILE = 256
+N_TILE = 512
 DOWN_TILE = 1792
 VMEM_LIMIT = 4 * 2**20
 

time: 49.2 us -> 49.2 us (level)
  no operation moved by 1% of the time
where the time goes in v23:
time: 49.2 us; the launch traced here: 49.1 us
  starting transfers between devices  21 us (43%)
  waiting for transfers between devices  19.5 us (40%)
  Pallas kernels  7.56 us (15%)
  other arithmetic  0.8 us (2%)
    ppermute x6, starting transfers between devices, to_place(): return lax.ppermute(value, 'local', [(i, i ^ bits) for i in range(PLACES)])  9.25 us
    ppermute x6, starting transfers between devices, to_chip(): return lax.ppermute(value, 'node', [(i, i ^ 2) for i in range(2 * CHIPS)])  8.43 us
    ppermute x6, waiting for transfers between devices, to_place(): return lax.ppermute(value, 'local', [(i, i ^ bits) for i in range(PLACES)])  7.99 us
    ppermute x6, waiting for transfers between devices, to_chip(): return lax.ppermute(value, 'node', [(i, i ^ 2) for i in range(2 * CHIPS)])  5.39 us
    pallas_call x1, Pallas kernels, hidden_units(): pl.pallas_call(functools.partial(hidden_kernel, experts), out_shape=jax.S...  4.02 us
    ppermute x4, waiting for transfers between devices, to_core(): return lax.ppermute(value, 'node', [(i, i ^ 1) for i in range(2 * CHIPS)])  3.33 us
    ppermute x2, starting transfers between devices, to_both(): return lax.ppermute(value, ('node', 'local'), perm)  2.88 us
    ppermute x2, waiting for transfers between devices, to_both(): return lax.ppermute(value, ('node', 'local'), perm)  2.78 us
  transfers between devices with their start and end apart: 18, of which 14 were waited for; matrix products, arithmetic and copies ran while one was open for 0% of the time, Pallas kernels for 1%

profile of v23, /device:TPU:0, one launch (start us, length us, event | category | flops | bytes accessed | tf_op | source)
XLA Modules:
  0.0 49.1 jit_solution(18242371225980918879)
XLA Ops:
  0.0 0.0 copy-start
  0.0 0.0 copy-start.1
  0.0 1.1 %pack.1.refs_0_ = bf16[8,7296]{1,0:T(8,128)(2,1)S(1)} custom-call(bf16[8,7168]{1,0:T(8,128)(2,1)} %refs_0_.1, s32[4,8]{1,0:T(4,128)} %bitcast.6, f32[4,8]{1,0:T(4,128)} %bitcast.7, s32[8]{0:T(128)} %refs_3_.1, bf16[2,7168,512]{2,1,0:T(8,128)(2,1)} %refs_4_.3, bf16[2,7168,512]{2,1,0:T(8,128)(2,1)} %refs_5_.3, bf16[2,512,7168]{2,1,0:T(8,128)(2,1)} %refs_6_.1), custom_call_target="tpu_custom_call" | custom-call | tf_op jit(solution)/shard_map/pack/pallas_call | solution.py:50
  1.1 3.1 %collective-permute-start.1 = (bf16[8,7296]{1,0:T(8,128)(2,1)S(1)}, bf16[8,7296]{1,0:T(8,128)(2,1)S(1)}, u32[]{:S(2)}, u32[]{:S(2)}) collective-permute-start(bf16[8,7296]{1,0:T(8,128)(2,1)S(1)} %pack.1.refs_0_), channel_id=1, source_target_pairs={{0,1},{1,0},{2,3},{3,2},{4,5},{5,4},{6,7},{7,6},{8,9},{9,8},{10,11... | collective-permute-start | bytes 350216 | tf_op jit(solution)/shard_map/ppermute | solution.py:177
  4.2 2.6 %collective-permute-start.3 = (bf16[8,7296]{1,0:T(8,128)(2,1)S(1)}, bf16[8,7296]{1,0:T(8,128)(2,1)S(1)}, u32[]{:S(2)}, u32[]{:S(2)}) collective-permute-start(bf16[8,7296]{1,0:T(8,128)(2,1)S(1)} %pack.1.refs_0_), channel_id=1, source_target_pairs={{0,2},{1,3},{2,0},{3,1},{4,6},{5,7},{6,4},{7,5},{8,10},{9,11},{10,... | collective-permute-start | bytes 350216 | tf_op jit(solution)/shard_map/ppermute | solution.py:177
  6.8 1.5 %collective-permute-start = (bf16[8,7296]{1,0:T(8,128)(2,1)S(1)}, bf16[8,7296]{1,0:T(8,128)(2,1)S(1)}, u32[]{:S(2)}, u32[]{:S(2)}) collective-permute-start(bf16[8,7296]{1,0:T(8,128)(2,1)S(1)} %pack.1.refs_0_), channel_id=1, source_target_pairs={{0,8},{4,12},{8,0},{12,4},{1,9},{5,13},{9,1},{13,5},{2,10},{6,14},... | collective-permute-start | bytes 350216 | tf_op jit(solution)/shard_map/ppermute | solution.py:173
  8.3 0.3 collective-permute-done.1.refs_2_
  8.6 1.8 %collective-permute-start.2 = (bf16[8,7296]{1,0:T(8,128)(2,1)S(1)}, bf16[8,7296]{1,0:T(8,128)(2,1)S(1)}, u32[]{:S(2)}, u32[]{:S(2)}) collective-permute-start(bf16[8,7296]{1,0:T(8,128)(2,1)S(1)} %collective-permute-done.1.refs_2_), channel_id=1, source_target_pairs={{0,8},{4,12},{8,0},{12,4},{1,9},{5,13},{9,1},{13,5},{2,10},{6,14},... | collective-permute-start | bytes 350216 | tf_op jit(solution)/shard_map/ppermute | solution.py:173
  10.4 1.9 %collective-permute-done.3.refs_0_ = bf16[8,7296]{1,0:T(8,128)(2,1)S(1)} collective-permute-done((bf16[8,7296]{1,0:T(8,128)(2,1)S(1)}, bf16[8,7296]{1,0:T(8,128)(2,1)S(1)}, u32[]{:S(2)}, u32[]{:S(2)}) %collective-permute-start.3) | collective-permute-done | bytes 116768 | tf_op jit(solution)/shard_map/ppermute | solution.py:177
  12.3 0.1 collective-permute-done.refs_1_
  12.4 1.5 %collective-permute-start.5 = (bf16[8,7296]{1,0:T(8,128)(2,1)S(1)}, bf16[8,7296]{1,0:T(8,128)(2,1)S(1)}, u32[]{:S(2)}, u32[]{:S(2)}) collective-permute-start(bf16[8,7296]{1,0:T(8,128)(2,1)S(1)} %collective-permute-done.3.refs_0_), channel_id=1, source_target_pairs={{0,8},{4,12},{8,0},{12,4},{1,9},{5,13},{9,1},{13,5},{2,10},{6,14},... | collective-permute-start | bytes 350216 | tf_op jit(solution)/shard_map/ppermute | solution.py:173
  13.9 0.8 %collective-permute-start.4 = (bf16[8,7296]{1,0:T(8,128)(2,1)S(1)}, bf16[8,7296]{1,0:T(8,128)(2,1)S(1)}, u32[]{:S(2)}, u32[]{:S(2)}) collective-permute-start(bf16[8,7296]{1,0:T(8,128)(2,1)S(1)} %collective-permute-done.3.refs_0_), channel_id=1, source_target_pairs={{0,1},{1,0},{2,3},{3,2},{4,5},{5,4},{6,7},{7,6},{8,9},{9,8},{10,11... | collective-permute-start | bytes 350216 | tf_op jit(solution)/shard_map/ppermute | solution.py:177
  14.7 0.0 collective-permute-done.2.refs_3_
  14.7 1.2 %collective-permute-start.6 = (bf16[8,7296]{1,0:T(8,128)(2,1)S(1)}, bf16[8,7296]{1,0:T(8,128)(2,1)S(1)}, u32[]{:S(2)}, u32[]{:S(2)}) collective-permute-start(bf16[8,7296]{1,0:T(8,128)(2,1)S(1)} %collective-permute-done.3.refs_0_), channel_id=1, source_target_pairs={{0,9},{1,8},{2,11},{3,10},{4,13},{5,12},{6,15},{7,14},{8,1},{9,0},... | collective-permute-start | bytes 350216 | tf_op jit(solution)/shard_map/ppermute | solution.py:183
  15.9 0.1 stack.2.refs_0_
  16.0 0.1 collective-permute-start.7
  16.1 2.4 %collective-permute-done.5.refs_2_ = bf16[8,7296]{1,0:T(8,128)(2,1)S(1)} collective-permute-done((bf16[8,7296]{1,0:T(8,128)(2,1)S(1)}, bf16[8,7296]{1,0:T(8,128)(2,1)S(1)}, u32[]{:S(2)}, u32[]{:S(2)}) %collective-permute-start.5) | collective-permute-done | bytes 116768 | tf_op jit(solution)/shard_map/ppermute | solution.py:173
  18.5 0.2 collective-permute-done.4.refs_1_
  18.7 1.7 %collective-permute-done.6.refs_3_ = bf16[8,7296]{1,0:T(8,128)(2,1)S(1)} collective-permute-done((bf16[8,7296]{1,0:T(8,128)(2,1)S(1)}, bf16[8,7296]{1,0:T(8,128)(2,1)S(1)}, u32[]{:S(2)}, u32[]{:S(2)}) %collective-permute-start.6) | collective-permute-done | bytes 116768 | tf_op jit(solution)/shard_map/ppermute | solution.py:183
  20.4 0.0 slice-start
  20.4 0.1 stack.3.refs_1_
  20.5 0.0 slice-start.1
  20.5 0.0 slice-start.2
  20.5 0.0 slice-start.3
  20.5 0.1 collective-permute-start.8
  20.6 0.0 collective-permute-done.7.refs_2_
  20.6 1.8 %collective-permute-done.8.refs_3_ = bf16[32,7296]{1,0:T(8,128)(2,1)S(1)} collective-permute-done((bf16[32,7296]{1,0:T(8,128)(2,1)S(1)}, bf16[32,7296]{1,0:T(8,128)(2,1)S(1)}, u32[]{:S(2)}, u32[]{:S(2)}) %collective-permute-start.8) | collective-permute-done | bytes 466976 | tf_op jit(solution)/shard_map/ppermute | solution.py:169
  22.4 0.0 copy-done
  22.4 0.0 copy-done.1
  22.4 4.0 %hidden.1.hidden_ref = bf16[128,1024]{1,0:T(8,128)(2,1)S(1)} custom-call(bf16[32,7296]{1,0:T(8,128)(2,1)S(1)} %stack.2.refs_0_, bf16[32,7296]{1,0:T(8,128)(2,1)S(1)} %stack.3.refs_1_, bf16[32,7296]{1,0:T(8,128)(2,1)S(1)} %collective-permute-done.7.refs_2_, bf16[32,7296]{1,0:T(8,128)(2,1)S(1)} %collective-permute-done.8.refs_3_, ...), custom_call_target="tpu_custom_call" | custom-call | flops 3758096384 | bytes 29360128 | tf_op jit(solution)/shard_map/hidden/pallas_call | solution.py:113
  26.4 0.0 slice-done
  26.4 0.0 slice-done.1
  26.5 0.0 slice-done.2
  26.5 0.0 slice-done.3
  26.5 2.1 %down.1 = (bf16[40,7168]{1,0:T(8,128)(2,1)S(1)}, bf16[24,7168]{1,0:T(8,128)(2,1)S(1)}, bf16[40,7168]{1,0:T(8,128)(2,1)S(1)}, bf16[24,7168]{1,0:T(8,128)(2,1)S(1)}) custom-call(bf16[128,1024]{1,0:T(8,128)(2,1)S(1)} %hidden.1.hidden_ref, bf16[1024,7168]{1,0:T(8,128)(2,1)S(1)} %bitcast.5), custom_call_target="tpu_custom_call" | custom-call | flops 1879048192 | bytes 14680064 | tf_op jit(solution)/shard_map/down/pallas_call | solution.py:149
  28.6 0.2 collective-permute-start.9
  28.8 1.5 %collective-permute-done.9.other_ref = bf16[24,7168]{1,0:T(8,128)(2,1)S(1)} collective-permute-done((bf16[24,7168]{1,0:T(8,128)(2,1)S(1)}, bf16[24,7168]{1,0:T(8,128)(2,1)S(1)}, u32[]{:S(2)}, u32[]{:S(2)}) %collective-permute-start.9) | collective-permute-done | bytes 344096 | tf_op jit(solution)/shard_map/ppermute | solution.py:169
  30.3 0.1 collective-permute-start.10
  30.4 0.1 sums.3
  30.5 1.8 %collective-permute-start.11 = (bf16[8,7168]{1,0:T(8,128)(2,1)S(1)}, bf16[8,7168]{1,0:T(8,128)(2,1)S(1)}, u32[]{:S(2)}, u32[]{:S(2)}) collective-permute-start(bf16[8,7168]{1,0:T(8,128)(2,1)S(1)} %get-tuple-element.32), channel_id=1, source_target_pairs={{0,8},{4,12},{8,0},{12,4},{1,9},{5,13},{9,1},{13,5},{2,10},{6,14},... | collective-permute-start | bytes 344072 | tf_op jit(solution)/shard_map/ppermute | solution.py:173
  32.3 0.1 collective-permute-start.13
  32.4 1.7 %collective-permute-start.12 = (bf16[8,7168]{1,0:T(8,128)(2,1)S(1)}, bf16[8,7168]{1,0:T(8,128)(2,1)S(1)}, u32[]{:S(2)}, u32[]{:S(2)}) collective-permute-start(bf16[8,7168]{1,0:T(8,128)(2,1)S(1)} %get-tuple-element.33), channel_id=1, source_target_pairs={{0,9},{1,8},{2,11},{3,10},{4,13},{5,12},{6,15},{7,14},{8,1},{9,0},... | collective-permute-start | bytes 344072 | tf_op jit(solution)/shard_map/ppermute | solution.py:183
  34.1 0.0 collective-permute-done.10.other_ref
  34.1 0.1 sums.2
  34.2 1.8 %collective-permute-done.11 = bf16[8,7168]{1,0:T(8,128)(2,1)S(1)} collective-permute-done((bf16[8,7168]{1,0:T(8,128)(2,1)S(1)}, bf16[8,7168]{1,0:T(8,128)(2,1)S(1)}, u32[]{:S(2)}, u32[]{:S(2)}) %collective-permute-start.11) | collective-permute-done | bytes 114720 | tf_op jit(solution)/shard_map/ppermute | solution.py:173
  36.0 2.3 %collective-permute-done.13 = bf16[8,7168]{1,0:T(8,128)(2,1)S(1)} collective-permute-done((bf16[8,7168]{1,0:T(8,128)(2,1)S(1)}, bf16[8,7168]{1,0:T(8,128)(2,1)S(1)}, u32[]{:S(2)}, u32[]{:S(2)}) %collective-permute-start.13) | collective-permute-done | bytes 114720 | tf_op jit(solution)/shard_map/ppermute | solution.py:177
  38.3 0.3 collective-permute-start.15
  38.6 1.1 %collective-permute-done.12 = bf16[8,7168]{1,0:T(8,128)(2,1)S(1)} collective-permute-done((bf16[8,7168]{1,0:T(8,128)(2,1)S(1)}, bf16[8,7168]{1,0:T(8,128)(2,1)S(1)}, u32[]{:S(2)}, u32[]{:S(2)}) %collective-permute-start.12) | collective-permute-done | bytes 114720 | tf_op jit(solution)/shard_map/ppermute | solution.py:183
  39.7 0.1 add_convert_fusion.2
  39.8 2.2 %collective-permute-start.14 = (bf16[8,7168]{1,0:T(8,128)(2,1)S(1)}, bf16[8,7168]{1,0:T(8,128)(2,1)S(1)}, u32[]{:S(2)}, u32[]{:S(2)}) collective-permute-start(bf16[8,7168]{1,0:T(8,128)(2,1)S(1)} %add_convert_fusion.2), channel_id=1, source_target_pairs={{0,2},{1,3},{2,0},{3,1},{4,6},{5,7},{6,4},{7,5},{8,10},{9,11},{10,... | collective-permute-start | bytes 344072 | tf_op jit(solution)/shard_map/ppermute | solution.py:177
  42.0 1.1 %collective-permute-done.15 = bf16[8,7168]{1,0:T(8,128)(2,1)S(1)} collective-permute-done((bf16[8,7168]{1,0:T(8,128)(2,1)S(1)}, bf16[8,7168]{1,0:T(8,128)(2,1)S(1)}, u32[]{:S(2)}, u32[]{:S(2)}) %collective-permute-start.15) | collective-permute-done | bytes 114720 | tf_op jit(solution)/shard_map/ppermute | solution.py:173
  43.1 0.4 collective-permute-start.16
  43.5 1.5 %collective-permute-start.17 = (bf16[8,7168]{1,0:T(8,128)(2,1)S(1)}, bf16[8,7168]{1,0:T(8,128)(2,1)S(1)}, u32[]{:S(2)}, u32[]{:S(2)}) collective-permute-start(bf16[8,7168]{1,0:T(8,128)(2,1)S(1)} %get-tuple-element.40), channel_id=1, source_target_pairs={{0,8},{4,12},{8,0},{12,4},{1,9},{5,13},{9,1},{13,5},{2,10},{6,14},... | collective-permute-start | bytes 344072 | tf_op jit(solution)/shard_map/ppermute | solution.py:173
  45.1 2.4 %collective-permute-done.14 = bf16[8,7168]{1,0:T(8,128)(2,1)S(1)} collective-permute-done((bf16[8,7168]{1,0:T(8,128)(2,1)S(1)}, bf16[8,7168]{1,0:T(8,128)(2,1)S(1)}, u32[]{:S(2)}, u32[]{:S(2)}) %collective-permute-start.14) | collective-permute-done | bytes 114720 | tf_op jit(solution)/shard_map/ppermute | solution.py:177
  47.4 0.9 %collective-permute-done.16 = bf16[8,7168]{1,0:T(8,128)(2,1)S(1)} collective-permute-done((bf16[8,7168]{1,0:T(8,128)(2,1)S(1)}, bf16[8,7168]{1,0:T(8,128)(2,1)S(1)}, u32[]{:S(2)}, u32[]{:S(2)}) %collective-permute-start.16) | collective-permute-done | bytes 114720 | tf_op jit(solution)/shard_map/ppermute | solution.py:177
  48.3 0.0 collective-permute-done.17
  48.3 0.7 %add_convert_fusion = bf16[8,7168]{1,0:T(8,128)(2,1)} fusion(bf16[8,7168]{1,0:T(8,128)(2,1)S(1)} %collective-permute-done.17, bf16[8,7168]{1,0:T(8,128)(2,1)S(1)} %collective-permute-done.16, bf16[8,7168]{1,0:T(8,128)(2,1)S(1)} %collective-permute-done.14, bf16[8,7168]{1,0:T(8,128)(2,1)S(1)} %get-tuple-element.29), kind=kLoop, calls=%fused_computation | loop fusion | flops 458752 | bytes 573440 | tf_op jit(solution)/shard_map/convert_element_type | solution.py:237
  (2 shorter events, 0.0 us)
Async XLA Ops:
  0.0 22.4 %copy-start = (bf16[2,7168,512]{2,1,0:T(8,128)(2,1)S(1)}, bf16[2,7168,512]{2,1,0:T(8,128)(2,1)}, u32[]{:S(2)}) copy-start(bf16[2,7168,512]{2,1,0:T(8,128)(2,1)} %refs_4_.3) | copy-start | bytes 44040196
  0.0 22.4 %copy-start.1 = (bf16[2,7168,512]{2,1,0:T(8,128)(2,1)S(1)}, bf16[2,7168,512]{2,1,0:T(8,128)(2,1)}, u32[]{:S(2)}) copy-start(bf16[2,7168,512]{2,1,0:T(8,128)(2,1)} %refs_5_.3) | copy-start | bytes 44040196
  1.1 7.5 %collective-permute-start.1 = (bf16[8,7296]{1,0:T(8,128)(2,1)S(1)}, bf16[8,7296]{1,0:T(8,128)(2,1)S(1)}, u32[]{:S(2)}, u32[]{:S(2)}) collective-permute-start(bf16[8,7296]{1,0:T(8,128)(2,1)S(1)} %pack.1.refs_0_), channel_id=1, source_target_pairs={{0,1},{1,0},{2,3},{3,2},{4,5},{5,4},{6,7},{7,6},{8,9},{9,8},{10,11... | collective-permute-start | bytes 350216 | tf_op jit(solution)/shard_map/ppermute | solution.py:177
  4.2 8.1 %collective-permute-start.3 = (bf16[8,7296]{1,0:T(8,128)(2,1)S(1)}, bf16[8,7296]{1,0:T(8,128)(2,1)S(1)}, u32[]{:S(2)}, u32[]{:S(2)}) collective-permute-start(bf16[8,7296]{1,0:T(8,128)(2,1)S(1)} %pack.1.refs_0_), channel_id=1, source_target_pairs={{0,2},{1,3},{2,0},{3,1},{4,6},{5,7},{6,4},{7,5},{8,10},{9,11},{10,... | collective-permute-start | bytes 350216 | tf_op jit(solution)/shard_map/ppermute | solution.py:177
  6.8 5.6 %collective-permute-start = (bf16[8,7296]{1,0:T(8,128)(2,1)S(1)}, bf16[8,7296]{1,0:T(8,128)(2,1)S(1)}, u32[]{:S(2)}, u32[]{:S(2)}) collective-permute-start(bf16[8,7296]{1,0:T(8,128)(2,1)S(1)} %pack.1.refs_0_), channel_id=1, source_target_pairs={{0,8},{4,12},{8,0},{12,4},{1,9},{5,13},{9,1},{13,5},{2,10},{6,14},... | collective-permute-start | bytes 350216 | tf_op jit(solution)/shard_map/ppermute | solution.py:173
  8.6 6.1 %collective-permute-start.2 = (bf16[8,7296]{1,0:T(8,128)(2,1)S(1)}, bf16[8,7296]{1,0:T(8,128)(2,1)S(1)}, u32[]{:S(2)}, u32[]{:S(2)}) collective-permute-start(bf16[8,7296]{1,0:T(8,128)(2,1)S(1)} %collective-permute-done.1.refs_2_), channel_id=1, source_target_pairs={{0,8},{4,12},{8,0},{12,4},{1,9},{5,13},{9,1},{13,5},{2,10},{6,14},... | collective-permute-start | bytes 350216 | tf_op jit(solution)/shard_map/ppermute | solution.py:173
  12.4 6.1 %collective-permute-start.5 = (bf16[8,7296]{1,0:T(8,128)(2,1)S(1)}, bf16[8,7296]{1,0:T(8,128)(2,1)S(1)}, u32[]{:S(2)}, u32[]{:S(2)}) collective-permute-start(bf16[8,7296]{1,0:T(8,128)(2,1)S(1)} %collective-permute-done.3.refs_0_), channel_id=1, source_target_pairs={{0,8},{4,12},{8,0},{12,4},{1,9},{5,13},{9,1},{13,5},{2,10},{6,14},... | collective-permute-start | bytes 350216 | tf_op jit(solution)/shard_map/ppermute | solution.py:173
  13.9 4.8 %collective-permute-start.4 = (bf16[8,7296]{1,0:T(8,128)(2,1)S(1)}, bf16[8,7296]{1,0:T(8,128)(2,1)S(1)}, u32[]{:S(2)}, u32[]{:S(2)}) collective-permute-start(bf16[8,7296]{1,0:T(8,128)(2,1)S(1)} %collective-permute-done.3.refs_0_), channel_id=1, source_target_pairs={{0,1},{1,0},{2,3},{3,2},{4,5},{5,4},{6,7},{7,6},{8,9},{9,8},{10,11... | collective-permute-start | bytes 350216 | tf_op jit(solution)/shard_map/ppermute | solution.py:177
  14.7 5.7 %collective-permute-start.6 = (bf16[8,7296]{1,0:T(8,128)(2,1)S(1)}, bf16[8,7296]{1,0:T(8,128)(2,1)S(1)}, u32[]{:S(2)}, u32[]{:S(2)}) collective-permute-start(bf16[8,7296]{1,0:T(8,128)(2,1)S(1)} %collective-permute-done.3.refs_0_), channel_id=1, source_target_pairs={{0,9},{1,8},{2,11},{3,10},{4,13},{5,12},{6,15},{7,14},{8,1},{9,0},... | collective-permute-start | bytes 350216 | tf_op jit(solution)/shard_map/ppermute | solution.py:183
  16.0 4.6 %collective-permute-start.7 = (bf16[32,7296]{1,0:T(8,128)(2,1)S(1)}, bf16[32,7296]{1,0:T(8,128)(2,1)S(1)}, u32[]{:S(2)}, u32[]{:S(2)}) collective-permute-start(bf16[32,7296]{1,0:T(8,128)(2,1)S(1)} %stack.2.refs_0_), channel_id=1, source_target_pairs={{0,4},{4,0},{8,12},{12,8},{1,5},{5,1},{9,13},{13,9},{2,6},{6,2},{1... | collective-permute-start | bytes 1400840 | tf_op jit(solution)/shard_map/ppermute | solution.py:169
  20.4 6.0 %slice-start = ((s8[14680064]{0:T(1024)(128)(4,1)}), s8[4194304]{0:T(1024)(128)(4,1)S(1)}, s32[]{:S(2)}) async-start(s8[14680064]{0:T(1024)(128)(4,1)} %bitcast.3), calls=%async_computation | async-start | bytes 8388608
  20.5 6.0 %slice-start.1 = ((s8[14680064]{0:T(1024)(128)(4,1)}), s8[4194304]{0:T(1024)(128)(4,1)S(1)}, s32[]{:S(2)}) async-start(s8[14680064]{0:T(1024)(128)(4,1)} %bitcast.3), calls=%async_computation.1 | async-start | bytes 8388608
  20.5 6.0 %slice-start.2 = ((s8[14680064]{0:T(1024)(128)(4,1)}), s8[4194304]{0:T(1024)(128)(4,1)S(1)}, s32[]{:S(2)}) async-start(s8[14680064]{0:T(1024)(128)(4,1)} %bitcast.3), calls=%async_computation.2 | async-start | bytes 8388608
  20.5 6.0 %slice-start.3 = ((s8[14680064]{0:T(1024)(128)(4,1)}), s8[2097152]{0:T(1024)(128)(4,1)S(1)}, s32[]{:S(2)}) async-start(s8[14680064]{0:T(1024)(128)(4,1)} %bitcast.3), calls=%async_computation.3 | async-start | bytes 4194304
  20.5 1.9 %collective-permute-start.8 = (bf16[32,7296]{1,0:T(8,128)(2,1)S(1)}, bf16[32,7296]{1,0:T(8,128)(2,1)S(1)}, u32[]{:S(2)}, u32[]{:S(2)}) collective-permute-start(bf16[32,7296]{1,0:T(8,128)(2,1)S(1)} %stack.3.refs_1_), channel_id=1, source_target_pairs={{0,4},{4,0},{8,12},{12,8},{1,5},{5,1},{9,13},{13,9},{2,6},{6,2},{1... | collective-permute-start | bytes 1400840 | tf_op jit(solution)/shard_map/ppermute | solution.py:169
  28.6 1.7 %collective-permute-start.9 = (bf16[24,7168]{1,0:T(8,128)(2,1)S(1)}, bf16[24,7168]{1,0:T(8,128)(2,1)S(1)}, u32[]{:S(2)}, u32[]{:S(2)}) collective-permute-start(bf16[24,7168]{1,0:T(8,128)(2,1)S(1)} %get-tuple-element.27), channel_id=1, source_target_pairs={{0,4},{4,0},{8,12},{12,8},{1,5},{5,1},{9,13},{13,9},{2,6},{6,2},{1... | collective-permute-start | bytes 1032200 | tf_op jit(solution)/shard_map/ppermute | solution.py:169
  30.3 3.8 %collective-permute-start.10 = (bf16[40,7168]{1,0:T(8,128)(2,1)S(1)}, bf16[40,7168]{1,0:T(8,128)(2,1)S(1)}, u32[]{:S(2)}, u32[]{:S(2)}) collective-permute-start(bf16[40,7168]{1,0:T(8,128)(2,1)S(1)} %get-tuple-element.28), channel_id=1, source_target_pairs={{0,4},{4,0},{8,12},{12,8},{1,5},{5,1},{9,13},{13,9},{2,6},{6,2},{1... | collective-permute-start | bytes 1720328 | tf_op jit(solution)/shard_map/ppermute | solution.py:169
  30.5 5.5 %collective-permute-start.11 = (bf16[8,7168]{1,0:T(8,128)(2,1)S(1)}, bf16[8,7168]{1,0:T(8,128)(2,1)S(1)}, u32[]{:S(2)}, u32[]{:S(2)}) collective-permute-start(bf16[8,7168]{1,0:T(8,128)(2,1)S(1)} %get-tuple-element.32), channel_id=1, source_target_pairs={{0,8},{4,12},{8,0},{12,4},{1,9},{5,13},{9,1},{13,5},{2,10},{6,14},... | collective-permute-start | bytes 344072 | tf_op jit(solution)/shard_map/ppermute | solution.py:173
  32.3 6.0 %collective-permute-start.13 = (bf16[8,7168]{1,0:T(8,128)(2,1)S(1)}, bf16[8,7168]{1,0:T(8,128)(2,1)S(1)}, u32[]{:S(2)}, u32[]{:S(2)}) collective-permute-start(bf16[8,7168]{1,0:T(8,128)(2,1)S(1)} %get-tuple-element.34), channel_id=1, source_target_pairs={{0,1},{1,0},{2,3},{3,2},{4,5},{5,4},{6,7},{7,6},{8,9},{9,8},{10,11... | collective-permute-start | bytes 344072 | tf_op jit(solution)/shard_map/ppermute | solution.py:177
  32.4 7.3 %collective-permute-start.12 = (bf16[8,7168]{1,0:T(8,128)(2,1)S(1)}, bf16[8,7168]{1,0:T(8,128)(2,1)S(1)}, u32[]{:S(2)}, u32[]{:S(2)}) collective-permute-start(bf16[8,7168]{1,0:T(8,128)(2,1)S(1)} %get-tuple-element.33), channel_id=1, source_target_pairs={{0,9},{1,8},{2,11},{3,10},{4,13},{5,12},{6,15},{7,14},{8,1},{9,0},... | collective-permute-start | bytes 344072 | tf_op jit(solution)/shard_map/ppermute | solution.py:183
  38.3 4.8 %collective-permute-start.15 = (bf16[8,7168]{1,0:T(8,128)(2,1)S(1)}, bf16[8,7168]{1,0:T(8,128)(2,1)S(1)}, u32[]{:S(2)}, u32[]{:S(2)}) collective-permute-start(bf16[8,7168]{1,0:T(8,128)(2,1)S(1)} %get-tuple-element.37), channel_id=1, source_target_pairs={{0,8},{4,12},{8,0},{12,4},{1,9},{5,13},{9,1},{13,5},{2,10},{6,14},... | collective-permute-start | bytes 344072 | tf_op jit(solution)/shard_map/ppermute | solution.py:173
  39.8 7.7 %collective-permute-start.14 = (bf16[8,7168]{1,0:T(8,128)(2,1)S(1)}, bf16[8,7168]{1,0:T(8,128)(2,1)S(1)}, u32[]{:S(2)}, u32[]{:S(2)}) collective-permute-start(bf16[8,7168]{1,0:T(8,128)(2,1)S(1)} %add_convert_fusion.2), channel_id=1, source_target_pairs={{0,2},{1,3},{2,0},{3,1},{4,6},{5,7},{6,4},{7,5},{8,10},{9,11},{10,... | collective-permute-start | bytes 344072 | tf_op jit(solution)/shard_map/ppermute | solution.py:177
  43.1 5.2 %collective-permute-start.16 = (bf16[8,7168]{1,0:T(8,128)(2,1)S(1)}, bf16[8,7168]{1,0:T(8,128)(2,1)S(1)}, u32[]{:S(2)}, u32[]{:S(2)}) collective-permute-start(bf16[8,7168]{1,0:T(8,128)(2,1)S(1)} %add_convert_fusion.1), channel_id=1, source_target_pairs={{0,1},{1,0},{2,3},{3,2},{4,5},{5,4},{6,7},{7,6},{8,9},{9,8},{10,11... | collective-permute-start | bytes 344072 | tf_op jit(solution)/shard_map/ppermute | solution.py:177
  43.5 4.8 %collective-permute-start.17 = (bf16[8,7168]{1,0:T(8,128)(2,1)S(1)}, bf16[8,7168]{1,0:T(8,128)(2,1)S(1)}, u32[]{:S(2)}, u32[]{:S(2)}) collective-permute-start(bf16[8,7168]{1,0:T(8,128)(2,1)S(1)} %get-tuple-element.40), channel_id=1, source_target_pairs={{0,8},{4,12},{8,0},{12,4},{1,9},{5,13},{9,1},{13,5},{2,10},{6,14},... | collective-permute-start | bytes 344072 | tf_op jit(solution)/shard_map/ppermute | solution.py:173
